TPU v7x, 32 devices: a whole 2x2x4 slice. The times are simulated.
32 devices in a mesh: groups: 2 (over y), dp: 4 (over x, core), tensor: 4 (over z).
Axes of the slice: x: 2, y: 2, z: 4, core: 2. Of those that a mesh axis runs over, the one named last changes fastest.
Arguments:
- tokens: bfloat16 [4096, 4096], P(('groups', 'dp'), 'tensor'), parts along dimension 0, may hold values from -96 to 96
- query_key_value_weight: bfloat16 [4096, 6, 512], P(None, None, 'tensor'), may hold values from -0.09375 to 0.09375
- output_weight: bfloat16 [512, 4, 4096], P('tensor'), may hold values from -0.125 to 0.125
- adapter_down_maps: bfloat16 [8, 192, 4096], P(('groups', 'dp'), None, 'tensor'), parts along dimension 0, may hold values from -0.09375 to 0.09375
- adapter_up_maps: bfloat16 [8, 64, 6, 512], P(('groups', 'dp'), None, None, 'tensor'), parts along dimension 0, may hold values from -0.75 to 0.75
- output_down_maps: bfloat16 [8, 64, 4, 512], P(('groups', 'dp'), None, None, 'tensor'), parts along dimension 0, may hold values from -0.125 to 0.125
- output_up_maps: bfloat16 [8, 64, 4096], P(('groups', 'dp'), None, 'tensor'), parts along dimension 0, may hold values from -0.75 to 0.75
- request_adapter: int32 [8, 4], P(('groups', 'dp')), parts along dimension 0, may hold values from 0 to 3
- lengths: int32 [8, 4], P(('groups', 'dp')), parts along dimension 0, may hold values from 1 to 256, 512 in all within a row
Outputs:
- layer_out: bfloat16 [4096, 4096], P(('groups', 'dp'), 'tensor'), parts along dimension 0
There are 2 independent parts, one for each index of `groups`. A program takes and returns all parts, laid end to end along the dimension named above; an argument that names none is the same for every part. Nothing has to cross between parts.
Inputs may be any that keep to these rules, and one draw needn't show every extreme that they name: `lengths`: each row sums to 512; its largest entry is 256.
All inputs are finite; a program needn't handle non-finite values.
Results may differ from a plain program's by a relative error of at most 0.01225.
The roundings to bfloat16 on the way count: a program that leaves them out, or rounds other values in their place, can miss the bound.
Values may be sent and summed in bfloat16 or wider, within the bound.
No kernel may reach another device: no remote copies, remote signals or barrier semaphores. Data moves between devices by JAX's collectives and lax.ppermute only.
A program may use at most 128 MiB of HBM per device.

v0:
```python
import math

import jax
import jax.numpy as jnp
from jax import lax
from jax.sharding import PartitionSpec as P


def layout(lengths_row, tok_count):
    req_ends = jnp.cumsum(lengths_row)
    starts = req_ends - lengths_row
    tok_index = jnp.arange(tok_count, dtype=jnp.int32)
    member = (tok_index[None, :] >= starts[:, None]) & (tok_index[None, :] < req_ends[:, None])
    weight_matrix = member.astype(jnp.float32)
    position = tok_index - jnp.sum(jnp.where(member, starts[:, None], 0), axis=0)
    order = jnp.arange(lengths_row.shape[0], dtype=jnp.int32)
    segment = jnp.sum(jnp.where(member, order[:, None], 0), axis=0)
    return (weight_matrix, position, segment)


def rotate(vectors, position):
    half_size = vectors.shape[-1] // 2
    inv_freq = 10000.0 ** (-2.0 * jnp.arange(half_size, dtype=jnp.float32) / vectors.shape[-1])
    angles = position.astype(jnp.float32)[:, None] * inv_freq[None, :]
    angles = angles.reshape((angles.shape[0],) + (1,) * (vectors.ndim - 2) + (half_size,))
    cosine = jnp.cos(angles)
    sine = jnp.sin(angles)
    first = vectors[..., :half_size]
    second = vectors[..., half_size:]
    return jnp.concatenate(
        [first * cosine - second * sine, second * cosine + first * sine], axis=-1
    )


def attend(queries, keys_rot, values, position, segment):
    scores = jnp.einsum("tpc,uc->ptu", queries, keys_rot, preferred_element_type=jnp.float32)
    scores = scores / math.sqrt(queries.shape[2])
    allowed = (segment[:, None] == segment[None, :]) & (position[None, :] <= position[:, None])
    scores = jnp.where(allowed[None], scores, -1e30)
    row_max = jnp.max(scores, axis=-1, keepdims=True)
    weights_exp = jnp.exp(scores - row_max)
    probabilities = (weights_exp / jnp.sum(weights_exp, axis=-1, keepdims=True)).astype(
        jnp.bfloat16
    )
    return jnp.einsum(
        "ptu,uc->tpc", probabilities, values, preferred_element_type=jnp.float32
    ).astype(jnp.bfloat16)


def local(
    tokens,
    query_key_value_weight,
    output_weight,
    adapter_down_maps,
    adapter_up_maps,
    output_down_maps,
    output_up_maps,
    request_adapter,
    lengths,
):
    token_rows = tokens.shape[0]
    slot_count = query_key_value_weight.shape[1]
    group_count = slot_count - 2
    head_size = query_key_value_weight.shape[2]
    adapter_rank_size = adapter_up_maps.shape[1]
    weight_matrix, position, segment = layout(lengths[0], token_rows)
    requests = request_adapter[0]
    gathered = (
        lax.all_gather(adapter_down_maps, "dp", axis=0, tiled=True),
        lax.all_gather(adapter_up_maps, "dp", axis=0, tiled=True),
        lax.all_gather(output_down_maps, "dp", axis=0, tiled=True),
        lax.all_gather(output_up_maps, "dp", axis=0, tiled=True),
    )
    chosen = tuple((jnp.take(member, requests, axis=0) for member in gathered))
    chosen_down, chosen_up, odown_sel, chosen_output_up = chosen
    shard_piece = lax.all_gather(tokens, "tensor", axis=1, tiled=True)
    flat_rows = query_key_value_weight.reshape(shard_piece.shape[1], slot_count * head_size)
    base_proj = jnp.dot(shard_piece, flat_rows, preferred_element_type=jnp.float32)
    partial_shrink = jnp.einsum(
        "td,qkd->qtk", tokens, chosen_down, preferred_element_type=jnp.float32
    )
    local_shrink = jnp.einsum("qt,qtk->tk", weight_matrix, partial_shrink)
    reduced_rows = lax.psum(local_shrink, "tensor").astype(jnp.bfloat16)
    masked = (
        weight_matrix[:, :, None, None]
        * reduced_rows.reshape(token_rows, 3, adapter_rank_size).astype(jnp.float32)[None]
    ).astype(jnp.bfloat16)
    query_extra = jnp.einsum(
        "qtr,qrsc->tsc",
        masked[:, :, 0],
        chosen_up[:, :, :group_count],
        preferred_element_type=jnp.float32,
    )
    key_extra = jnp.einsum(
        "qtr,qrc->tc",
        masked[:, :, 1],
        chosen_up[:, :, group_count],
        preferred_element_type=jnp.float32,
    )
    value_extra = jnp.einsum(
        "qtr,qrc->tc",
        masked[:, :, 2],
        chosen_up[:, :, group_count + 1],
        preferred_element_type=jnp.float32,
    )
    expanded = jnp.concatenate([query_extra, key_extra[:, None], value_extra[:, None]], axis=1)
    projected = base_proj.reshape(token_rows, slot_count, head_size) + expanded
    queries = rotate(projected[:, :group_count], position).astype(jnp.bfloat16)
    keys_rot = rotate(projected[:, group_count], position).astype(jnp.bfloat16)
    values = projected[:, group_count + 1].astype(jnp.bfloat16)
    attended = attend(queries, keys_rot, values, position, segment)
    partial_value = jnp.einsum(
        "tpc,cpd->td", attended, output_weight, preferred_element_type=jnp.float32
    )
    added_total = lax.psum_scatter(
        partial_value.astype(jnp.bfloat16), "tensor", scatter_dimension=1, tiled=True
    ).astype(jnp.float32)
    out_partial = jnp.einsum(
        "tpc,qrpc->qtr", attended, odown_sel, preferred_element_type=jnp.float32
    )
    local_out = jnp.einsum("qt,qtr->tr", weight_matrix, out_partial)
    out_shrink = lax.psum(local_out.astype(jnp.bfloat16), "tensor")
    output_masked_rows = (weight_matrix[:, :, None] * out_shrink.astype(jnp.float32)[None]).astype(
        jnp.bfloat16
    )
    adapter_output = jnp.einsum(
        "aei,aiu->eu", output_masked_rows, chosen_output_up, preferred_element_type=jnp.float32
    )
    return (added_total + adapter_output).astype(jnp.bfloat16)


def solution(mesh):
    in_specs = (
        P(("groups", "dp"), "tensor"),
        P(None, None, "tensor"),
        P("tensor", None, None),
        P(("groups", "dp"), None, "tensor"),
        P(("groups", "dp"), None, None, "tensor"),
        P(("groups", "dp"), None, None, "tensor"),
        P(("groups", "dp"), None, "tensor"),
        P(("groups", "dp"), None),
        P(("groups", "dp"), None),
    )
    out_specs = P(("groups", "dp"), "tensor")
    return jax.shard_map(local, mesh=mesh, in_specs=in_specs, out_specs=out_specs, check_vma=False)
```

profile of v0, /device:TPU:0, one launch (start us, length us, event | category | flops | bytes accessed | tf_op | source)
XLA Modules:
  0.0 260.8 jit_solution(3097719417786938723)
XLA Ops:
  6.5 0.7 all-gather.5.cloned.1.call-update
  7.3 0.7 all-gather.3.cloned.1.call-update
  8.1 8.8 %copy.22 = bf16[4096,6,128]{0,2,1:T(8,128)(2,1)} copy(bf16[4096,6,128]{2,0,1:T(8,128)(2,1)} %param.10) | data formatting | bytes 12582912 | tf_op args[1]
  16.9 9.8 %all_gather.17 = bf16[4,64,6,128]{3,1,2,0:T(8,128)(2,1)S(1)} all-gather(bf16[1,64,6,128]{3,1,2,0:T(8,128)(2,1)S(1)} %copy-done.4), channel_id=1, replica_groups=mesh['groups'=2,'dp'=4,'tensor'=4] {'dp'}, dimensions={0}, use_global_device_ids=true | all-gather | bytes 491520 | tf_op jit(solution)/shard_map/all_gather | solution.py:70
  26.7 0.6 gather_fusion.1
  27.4 6.8 %all_gather.18 = bf16[4,64,4,128]{3,1,2,0:T(8,128)(2,1)S(1)} all-gather(bf16[1,64,4,128]{3,1,2,0:T(8,128)(2,1)S(1)} %copy.29), channel_id=1, replica_groups=mesh['groups'=2,'dp'=4,'tensor'=4] {'dp'}, dimensions={0}, use_global_device_ids=true | all-gather | bytes 327680 | tf_op jit(solution)/shard_map/all_gather | solution.py:71
  34.1 1.3 gather_fusion.2
  35.8 1.0 compare_and_fusion
  36.9 2.1 gather_fusion
  39.0 1.0 fusion.11
  40.0 39.0 %all-reduce.4 = bf16[512,192]{0,1:T(8,128)(2,1)S(1)} all-reduce(f32[512,192]{0,1:T(8,128)S(1)} %fusion.11), channel_id=1, replica_groups=mesh['groups'=2,'dp'=4,'tensor'=4] {'tensor'}, use_global_device_ids=true, to_apply=%region_1.2 | all-reduce | flops 98304 | bytes 589824 | tf_op jit(solution)/shard_map/psum | solution.py:83
  79.3 0.3 convolution_bitcast_fusion
  79.6 0.2 convolution_bitcast_fusion.3
  79.8 0.2 convolution_bitcast_fusion.2
  80.1 47.2 %all-gather.3.cloned.1.call-done = bf16[512,4096]{1,0:T(8,128)(2,1)} async-done(((bf16[512,1024]{1,0:T(8,128)(2,1)}), bf16[512,4096]{1,0:T(8,128)(2,1)}) %all-gather.3.cloned.1.call-update) | async-done | bytes 4194320 | tf_op jit(solution)/shard_map/all_gather | solution.py:76
  127.2 6.8 %maximum_add_fusion = f32[512,6,128]{0,2,1:T(8,128)S(1)} fusion(f32[512,1,128]{0,2,1:T(8,128)S(1)} %convolution_bitcast_fusion.2, f32[512,1,128]{0,2,1:T(8,128)S(1)} %convolution_bitcast_fusion.3, f32[512,4,128]{0,2,1:T(8,128)S(1)} %convolution_bitcast_fusion, bf16[4096,6,128]{0,2,1:T(8,128)(2,1)} %copy.22, bf16[512,4096]{1,0:T(8,128)(2,1)} %all-gather.3.cloned.1.call-done), kind=kOutput, calls=%fused_computation.20 | convolution fusion | flops 3222405120 | bytes 13631488 | tf_op jit(solution)/shard_map/dot_general | solution.py:78
  134.1 0.6 subtract_convert_fusion.1
  134.7 0.2 subtract_convert_fusion
  134.9 0.7 fusion.28
  135.6 2.1 fusion.57
  137.7 0.5 fusion.19
  138.2 0.5 copy-done.1
  138.7 1.0 fusion.21
  139.7 0.2 reduce-scatter.2.cloned.1.call-start
  139.9 9.8 %bitcast_convert_fusion = bf16[512,4096]{1,0:T(8,128)(2,1)} fusion(bf16[128,4,4096]{2,1,0:T(4,128)(2,1)} %param.11, bf16[128,4,512]{2,0,1:T(8,128)(2,1)S(1)} %fusion.19), kind=kOutput, calls=%fused_computation.5 | convolution fusion | flops 2149580800 | bytes 8912896 | tf_op jit(solution)/shard_map/tpc,cpd->td/dot_general | solution.py:112
  149.8 0.9 copy-done.3
  150.6 7.0 %all_gather.19 = bf16[4,64,1024]{2,1,0:T(8,128)(2,1)S(1)} all-gather(bf16[1,64,1024]{2,1,0:T(8,128)(2,1)S(1)} %copy-done.3), channel_id=1, replica_groups=mesh['groups'=2,'dp'=4,'tensor'=4] {'dp'}, dimensions={0}, use_global_device_ids=true | all-gather | bytes 655360 | tf_op jit(solution)/shard_map/all_gather | solution.py:72
  157.7 0.6 gather_fusion.3
  158.3 14.5 %all-reduce.3.cloned.1.call-done = bf16[512,64]{0,1:T(8,128)(2,1)} async-done(((bf16[512,64]{0,1:T(8,128)(2,1)}), bf16[512,64]{0,1:T(8,128)(2,1)}) %all-reduce.3.cloned.1.call-update) | async-done | bytes 65552 | tf_op jit(solution)/shard_map/psum | solution.py:122
  172.8 0.8 convert_element_type.81
  173.7 77.9 %reduce-scatter.2.cloned.1.call-done = bf16[512,1024]{1,0:T(8,128)(2,1)} async-done(((bf16[512,4096]{1,0:T(8,128)(2,1)}), bf16[512,1024]{1,0:T(8,128)(2,1)}) %reduce-scatter.2.cloned.1.call-update) | async-done | bytes 1048592 | tf_op jit(solution)/shard_map/reduce_scatter | solution.py:115
  251.6 2.7 %fusion.6 = bf16[512,1024]{1,0:T(8,128)(2,1)} fusion(bf16[512,1024]{1,0:T(8,128)(2,1)} %reduce-scatter.2.cloned.1.call-done, bf16[4,64,1024]{2,1,0:T(8,128)(2,1)S(1)} %gather_fusion.3, pred[4]{0:T(512)(128)(4,1)S(1)} %compare_and_fusion.1, f32[512,64]{0,1:T(8,128)S(1)} %convert_element_type.81, f32[4,512]{1,0:T(4,128)S(1)} %get-tuple-element.15), kind=kOutput, calls=%fused_computation.15 | convolution fusion | flops 270532608 | bytes 2760708 | tf_op jit(solution)/shard_map/aei,aiu->eu/dot_general | solution.py:126
  (34 shorter events, 0.8 us)
Async XLA Ops:
  6.5 30.4 %all-gather.5.cloned.1.call-start = ((), (), s32[]{:S(2)}) async-start(), calls=%async_computation.2 | async-start | bytes 1966080 | tf_op jit(solution)/shard_map/all_gather | solution.py:69
  7.3 120.0 %all-gather.3.cloned.1.call-start = ((), (), s32[]{:S(2)}) async-start(), calls=%async_computation.1 | async-start | bytes 5242880 | tf_op jit(solution)/shard_map/all_gather | solution.py:76
  8.0 8.9 %copy-start.5 = (bf16[1,64,4,128]{3,2,1,0:T(4,128)(2,1)S(1)}, bf16[1,64,4,128]{3,2,1,0:T(4,128)(2,1)}, u32[]{:S(2)}) copy-start(bf16[1,64,4,128]{3,2,1,0:T(4,128)(2,1)} %param.14) | copy-start | bytes 196612
  8.0 8.9 %copy-start.7 = (s32[1,4]{1,0:T(1,128)S(1)}, s32[1,4]{1,0:T(1,128)}, u32[]{:S(2)}) copy-start(s32[1,4]{1,0:T(1,128)} %param.16) | copy-start | bytes 52
  8.0 8.9 %copy-start.4 = (bf16[1,64,6,128]{3,1,2,0:T(8,128)(2,1)S(1)}, bf16[1,64,6,128]{3,1,2,0:T(8,128)(2,1)}, u32[]{:S(2)}) copy-start(bf16[1,64,6,128]{3,1,2,0:T(8,128)(2,1)} %param.13) | copy-start | bytes 294916
  8.0 27.4 %copy-start.6 = (s32[1,4]{1,0:T(1,128)S(1)}, s32[1,4]{1,0:T(1,128)}, u32[]{:S(2)}) copy-start(s32[1,4]{1,0:T(1,128)} %param.17) | copy-start | bytes 52
  8.0 164.8 %all-reduce.3.cloned.1.call-start = ((), (), s32[]{:S(2)}) async-start(), calls=%async_computation.4 | async-start | bytes 131072 | tf_op jit(solution)/shard_map/psum | solution.py:122
  16.9 22.1 %copy-start = (bf16[512,1024]{1,0:T(8,128)(2,1)S(1)}, bf16[512,1024]{1,0:T(8,128)(2,1)}, u32[]{:S(2)}) copy-start(bf16[512,1024]{1,0:T(8,128)(2,1)} %param.9) | copy-start | bytes 3145732
  134.1 1.5 copy-start.2
  137.7 1.0 copy-start.1
  139.7 111.9 %reduce-scatter.2.cloned.1.call-start = ((), (), s32[]{:S(2)}) async-start(), calls=%async_computation.3 | async-start | bytes 5242880 | tf_op jit(solution)/shard_map/reduce_scatter | solution.py:115
  149.7 0.9 copy-start.3
Sparse Core Ops, SparseCore 0:
  8.9 24.8 all-gather.4
  35.4 91.7 all-gather.2
  139.8 32.9 all-reduce.2
  175.1 76.4 reduce-scatter.1
where the time goes:
time: 261 us
  waiting for transfers between devices  141 us (54%)
  blocking collectives  62.6 us (24%)
  matrix products  23.3 us (9%)
  local copies, waits for them, and re-layouts  14.7 us (6%)
  between operations  13.4 us (5%)
  other arithmetic  5.35 us (2%)
    reduce_scatter x1, waiting for transfers between devices, local(): lax.psum_scatter(partial_value.astype(jnp.bfloat16), 'tensor', scatter_di...  77.9 us
    all_gather x1, waiting for transfers between devices, local(): shard_piece = lax.all_gather(tokens, 'tensor', axis=1, tiled=True)  47.2 us
    psum x1, blocking collectives, local(): reduced_rows = lax.psum(local_shrink, 'tensor').astype(jnp.bfloat16)  39 us
    psum x1, waiting for transfers between devices, local(): out_shrink = lax.psum(local_out.astype(jnp.bfloat16), 'tensor')  14.5 us
    unnamed x18, local copies, waits for them, and re-layouts  10.2 us
    dot_general x1, matrix products, local(): jnp.einsum('tpc,cpd->td', attended, output_weight, preferred_element_type...  9.82 us
    all_gather x1, blocking collectives, local(): lax.all_gather(adapter_up_maps, 'dp', axis=0, tiled=True)  9.79 us
    all_gather x1, blocking collectives, local(): lax.all_gather(output_up_maps, 'dp', axis=0, tiled=True)  7.05 us
  transfers between devices with their start and end apart: 4, of which 3 were waited for; matrix products, arithmetic and copies ran while one was open for 11% of the time, Pallas kernels for 0%

commit v1 on v0

v1 whole, which is shorter than its diff:
```python
import functools
import math

import jax
import jax.numpy as jnp
from jax import lax
from jax.experimental import pallas as pl
from jax.experimental.pallas import tpu as pltpu
from jax.sharding import PartitionSpec as P

CHUNKS = 2
VMEM_BYTES = 48 * 1024 * 1024
PLANE = ("groups", "dp")


def attend_kernel(
    shards, first_row, outer, head_size, slots, ids_ref, start_ref, cos_ref, sin_ref, low_ref,
    up_ref, *refs
):
    token_refs, w_ref = refs[:shards], refs[shards]
    rest = refs[shards + 1 :]
    prior = rest[:2] if first_row else ()
    attended_ref, keys_ref, values_ref, acc_ref = rest[len(prior) :]
    step = pl.program_id(0)
    rows = acc_ref.shape[0]
    queries = slots - 2

    def wide(left, right):
        return jnp.concatenate([left, right], axis=1)

    def accumulate(token_ref, first):
        for pair in range(slots // 2):
            columns = slice(2 * pair * head_size, (2 * pair + 2) * head_size)
            if outer:
                depth = w_ref.shape[2]
                total = None
                for piece in range(w_ref.shape[0]):
                    part = jnp.dot(
                        token_ref[:, piece * depth : (piece + 1) * depth],
                        wide(w_ref[piece, 2 * pair], w_ref[piece, 2 * pair + 1]),
                        preferred_element_type=jnp.float32,
                    )
                    total = part if total is None else total + part
            else:
                total = jnp.dot(
                    token_ref[...],
                    wide(w_ref[2 * pair], w_ref[2 * pair + 1]),
                    preferred_element_type=jnp.float32,
                )
            if first:
                acc_ref[:, columns] = total
            else:
                acc_ref[:, columns] += total

    for number in range(shards):
        pl.when(step == number)(
            functools.partial(accumulate, token_refs[number], number == 0)
        )

    @pl.when(step == shards - 1)
    def _():
        cos, sin = cos_ref[...], sin_ref[...]

        def slot(index):
            which = 0 if index < queries else index - queries + 1
            extra = jnp.dot(low_ref[which], up_ref[index], preferred_element_type=jnp.float32)
            return acc_ref[:, index * head_size : (index + 1) * head_size] + extra

        def rotated(index):
            value = slot(index)
            turned = pltpu.roll(value, head_size // 2, 1)
            return (value * cos + turned * sin).astype(jnp.bfloat16)

        keys = rotated(queries)
        values = slot(queries + 1).astype(jnp.bfloat16)
        keys_ref[...] = keys
        values_ref[...] = values
        if first_row:
            keys = jnp.concatenate([prior[0][...], keys], axis=0)
            values = jnp.concatenate([prior[1][...], values], axis=0)
        key_rows = keys.shape[0]
        key_at = lax.broadcasted_iota(jnp.int32, (rows, key_rows), 1)
        row_at = lax.broadcasted_iota(jnp.int32, (rows, key_rows), 0) + first_row
        allowed = (key_at >= start_ref[...]) & (key_at <= row_at)
        for index in range(queries):
            scores = lax.dot_general(
                rotated(index), keys, (((1,), (1,)), ((), ())), preferred_element_type=jnp.float32
            )
            scores = jnp.where(allowed, scores * (1.0 / math.sqrt(head_size)), -1e30)
            weights = jnp.exp(scores - jnp.max(scores, axis=1, keepdims=True))
            scale = 1.0 / jnp.sum(weights, axis=1, keepdims=True)
            attended = jnp.dot(
                (weights * scale).astype(jnp.bfloat16), values, preferred_element_type=jnp.float32
            )
            attended_ref[:, index * head_size : (index + 1) * head_size] = attended.astype(
                jnp.bfloat16
            )


def attend_chunk(ids, start, cos, sin, low, up, tokens, weight, outer, prior):
    shards = len(tokens)
    rows, depth = tokens[0].shape
    slots, _, head_size = up.shape
    first_row = prior[0].shape[0] if prior else 0
    whole = pl.BlockSpec(memory_space=pltpu.VMEM)
    if outer:
        pieces = weight.shape[0] // shards
        w_spec = pl.BlockSpec(
            (pieces,) + weight.shape[1:], lambda step, ids_ref: (ids_ref[step], 0, 0, 0)
        )
    else:
        w_spec = pl.BlockSpec(
            (slots, depth, head_size), lambda step, ids_ref: (0, ids_ref[step], 0)
        )
    width = slots * head_size
    out = (
        jax.ShapeDtypeStruct((rows, width - 2 * head_size), jnp.bfloat16),
        jax.ShapeDtypeStruct((rows, head_size), jnp.bfloat16),
        jax.ShapeDtypeStruct((rows, head_size), jnp.bfloat16),
    )
    flops = 2 * rows * depth * shards * width
    return pl.pallas_call(
        functools.partial(attend_kernel, shards, first_row, outer, head_size, slots),
        out_shape=out,
        grid_spec=pltpu.PrefetchScalarGridSpec(
            num_scalar_prefetch=1,
            grid=(shards,),
            in_specs=[whole] * (5 + shards) + [w_spec] + [whole] * len(prior),
            out_specs=[whole] * 3,
            scratch_shapes=[pltpu.VMEM((rows, width), jnp.float32)],
        ),
        compiler_params=pltpu.CompilerParams(vmem_limit_bytes=VMEM_BYTES),
        cost_estimate=pl.CostEstimate(
            flops=2 * flops, bytes_accessed=2 * shards * depth * (width + rows), transcendentals=0
        ),
        name="attend",
    )(ids, start, cos, sin, low, up, *tokens, weight, *prior)


def output_kernel(groups, ids_ref, mask_ref, up_ref, *refs):
    attended_refs = refs[:groups]
    w_ref, down_ref, out_ref, acc_ref, low_ref = refs[groups:]
    step = pl.program_id(0)

    def accumulate(attended_ref, first):
        attended = attended_ref[...]
        part = jnp.dot(attended, w_ref[0], preferred_element_type=jnp.float32)
        low = lax.dot_general(
            attended, down_ref[0], (((1,), (1,)), ((), ())), preferred_element_type=jnp.float32
        )
        if first:
            acc_ref[...] = part
            low_ref[...] = low
        else:
            acc_ref[...] += part
            low_ref[...] += low

    for number in range(groups):
        pl.when(step == number)(
            functools.partial(accumulate, attended_refs[number], number == 0)
        )

    @pl.when(step == groups - 1)
    def _():
        low = low_ref[...].astype(jnp.bfloat16) * mask_ref[...]
        extra = jnp.dot(low, up_ref[...], preferred_element_type=jnp.float32)
        out_ref[...] = (acc_ref[...] + extra).astype(jnp.bfloat16)


def output_chunk(ids, mask, up, attended, weight, down):
    groups = len(attended)
    rows = attended[0].shape[0]
    features, columns = weight.shape[1:]
    ranks = down.shape[1]
    whole = pl.BlockSpec(memory_space=pltpu.VMEM)
    return pl.pallas_call(
        functools.partial(output_kernel, groups),
        out_shape=jax.ShapeDtypeStruct((rows, columns), jnp.bfloat16),
        grid_spec=pltpu.PrefetchScalarGridSpec(
            num_scalar_prefetch=1,
            grid=(groups,),
            in_specs=[whole] * (2 + groups)
            + [
                pl.BlockSpec((1, features, columns), lambda step, ids_ref: (ids_ref[step], 0, 0)),
                pl.BlockSpec((1, ranks, features), lambda step, ids_ref: (ids_ref[step], 0, 0)),
            ],
            out_specs=whole,
            scratch_shapes=[
                pltpu.VMEM((rows, columns), jnp.float32),
                pltpu.VMEM((rows, ranks), jnp.float32),
            ],
        ),
        compiler_params=pltpu.CompilerParams(vmem_limit_bytes=VMEM_BYTES),
        cost_estimate=pl.CostEstimate(
            flops=2 * rows * groups * features * (columns + ranks),
            bytes_accessed=2 * groups * features * (columns + ranks + rows),
            transcendentals=0,
        ),
        name="project_out",
    )(ids, mask, up, *attended, weight, down)


def local(
    plane_size,
    planes,
    tokens,
    query_key_value_weight,
    output_weight,
    adapter_down_maps,
    adapter_up_maps,
    output_down_maps,
    output_up_maps,
    request_adapter,
    lengths,
):
    token_rows, depth = tokens.shape
    _, slots, head_size = query_key_value_weight.shape
    queries = slots - 2
    rank = adapter_up_maps.shape[1]
    features = queries * head_size
    model_width = output_weight.shape[2]
    columns = model_width // planes
    pairs = planes // 2

    def worker(pair):
        return 2 * pair + 1 - pair % 2

    def outer(pair):
        return 2 * pair + pair % 2

    to_worker = [(outer(p), worker(p)) for p in range(pairs)]
    from_worker = [(worker(p), outer(p)) for p in range(pairs)]
    ring = [(worker(p), worker((p + 1) % pairs)) for p in range(pairs)]
    here = lax.axis_index("tensor")
    pair = here // 2
    is_worker = here == worker(pair)
    ids = []
    for step in range(pairs):
        source = (pair - step + pairs) % pairs
        ids += [worker(source), outer(source)]
    ids = jnp.stack(ids).astype(jnp.int32)
    place = lax.axis_index(PLANE)

    chunk_rows = token_rows // CHUNKS
    token_bundles = []
    for chunk in range(CHUNKS):
        own = tokens[chunk * chunk_rows : (chunk + 1) * chunk_rows]
        other = lax.ppermute(own, "tensor", to_worker)
        bundle = [own, other]
        for _ in range(pairs - 1):
            own = lax.ppermute(own, "tensor", ring)
            other = lax.ppermute(other, "tensor", ring)
            bundle += [own, other]
        token_bundles.append(bundle)

    weight = jnp.transpose(query_key_value_weight, (1, 0, 2))
    share = weight.shape[1] // plane_size
    piece = lax.dynamic_slice_in_dim(weight, place * share, share, axis=1)
    piece = lax.ppermute(piece, "tensor", to_worker)
    outer_weight = lax.all_gather(piece, PLANE, axis=0)

    request_ends = jnp.cumsum(lengths[0])
    request_starts = request_ends - lengths[0]
    at = jnp.arange(token_rows, dtype=jnp.int32)
    member = (at[:, None] >= request_starts[None, :]) & (at[:, None] < request_ends[None, :])
    start = jnp.sum(jnp.where(member, request_starts[None, :], 0), axis=1).astype(jnp.int32)
    position = at - start
    half = head_size // 2
    inv_freq = 10000.0 ** (-2.0 * jnp.arange(half, dtype=jnp.float32) / head_size)
    angles = position.astype(jnp.float32)[:, None] * inv_freq[None, :]
    cosine, sine = jnp.cos(angles), jnp.sin(angles)
    cos = jnp.concatenate([cosine, cosine], axis=1)
    sin = jnp.concatenate([-sine, sine], axis=1)

    down_all = lax.all_gather(adapter_down_maps, "dp", axis=0, tiled=True)
    up_own = jnp.transpose(adapter_up_maps[0], (1, 0, 2))
    up_pair = jnp.stack([up_own, lax.ppermute(up_own, "tensor", to_worker)])
    up_all = lax.all_gather(up_pair, "dp", axis=0)
    out_down_all = lax.all_gather(
        output_down_maps.reshape(rank, features), ("dp", "tensor"), axis=0
    ).reshape(-1, planes, rank, features)
    out_up_all = lax.all_gather(output_up_maps, "dp", axis=0, tiled=True)
    pool = up_all.shape[0]
    requests = request_adapter.shape[1]
    if pool <= requests:
        chosen = member @ jax.nn.one_hot(request_adapter[0], pool, dtype=jnp.float32) > 0.5
    else:
        chosen = member
        down_all, up_all, out_down_all, out_up_all = (
            jnp.take(maps, request_adapter[0], axis=0)
            for maps in (down_all, up_all, out_down_all, out_up_all)
        )
    count = chosen.shape[1]
    partial = jnp.einsum("td,akd->tak", tokens, down_all, preferred_element_type=jnp.float32)
    shrink = jnp.sum(jnp.where(chosen[:, :, None], partial, 0.0), axis=1)
    shrink = shrink + lax.ppermute(shrink, "tensor", to_worker)
    moving = shrink
    for _ in range(pairs - 1):
        moving = lax.ppermute(moving, "tensor", ring)
        shrink = shrink + moving
    shrink = shrink.astype(jnp.bfloat16).reshape(token_rows, 3, 1, rank)
    low = jnp.where(chosen[:, None, :, None], shrink, jnp.zeros((), jnp.bfloat16))
    low = jnp.transpose(low.reshape(token_rows, 3, count * rank), (1, 0, 2))
    ups = jnp.transpose(up_all, (1, 2, 0, 3, 4)).reshape(2, slots, count * rank, head_size)
    out_downs = jnp.transpose(out_down_all, (1, 0, 2, 3)).reshape(planes, count * rank, features)
    out_ups = out_up_all.reshape(count * rank, columns)
    out_mask = jnp.repeat(chosen.astype(jnp.bfloat16), rank, axis=1)

    lines = head_size // plane_size
    piece = lax.dynamic_slice_in_dim(output_weight, place * lines, lines, axis=0)
    piece = jnp.transpose(piece.reshape(lines, queries, planes, columns), (2, 1, 0, 3))
    piece = lax.all_to_all(piece, "tensor", 0, 0)
    gathered = lax.all_gather(piece, PLANE, axis=0)
    out_weight = jnp.transpose(gathered, (1, 2, 0, 3, 4)).reshape(planes, features, columns)

    outs = []
    prior = ((), ())
    for chunk in range(CHUNKS):
        rows = slice(chunk * chunk_rows, (chunk + 1) * chunk_rows)
        results = [
            attend_chunk(
                ids, start[rows, None], cos[rows], sin[rows], low[:, rows], ups[which],
                token_bundles[chunk], (weight, outer_weight)[which], which == 1, prior[which],
            )
            for which in range(2)
        ]
        prior = tuple(
            tuple(
                jnp.concatenate([old, new], axis=0) for old, new in zip(prior[which], result[1:])
            ) if prior[which] else result[1:]
            for which, result in enumerate(results)
        )
        bundle = [result[0] for result in results]
        attended = list(bundle)
        for _ in range(pairs - 1):
            bundle = [lax.ppermute(part, "tensor", ring) for part in bundle]
            attended += bundle
        attended = [
            jnp.where(is_worker, part, lax.ppermute(part, "tensor", from_worker))
            for part in attended
        ]
        outs.append(
            output_chunk(ids, out_mask[rows], out_ups, attended, out_weight, out_downs)
        )
    return jnp.concatenate(outs, axis=0)


def solution(mesh):
    in_specs = (
        P(PLANE, "tensor"),
        P(None, None, "tensor"),
        P("tensor", None, None),
        P(PLANE, None, "tensor"),
        P(PLANE, None, None, "tensor"),
        P(PLANE, None, None, "tensor"),
        P(PLANE, None, "tensor"),
        P(PLANE, None),
        P(PLANE, None),
    )
    function = functools.partial(
        local, mesh.shape["groups"] * mesh.shape["dp"], mesh.shape["tensor"]
    )
    return jax.shard_map(
        function, mesh=mesh, in_specs=in_specs, out_specs=P(PLANE, "tensor"), check_vma=False
    )
```

time: 261 us -> 249 us (0.954)
  waiting for transfers between devices: 141 us -> 74.1 us
  Pallas kernels: 0 us -> 43.8 us
  starting transfers between devices: 0.3 us -> 37 us
  blocking collectives: 62.6 us -> 37.7 us
  matrix products: 23.3 us -> 3.45 us
  local copies, waits for them, and re-layouts: 14.7 us -> 24.1 us
  other arithmetic: 5.35 us -> 13.2 us
    reduce_scatter x1 -> x0, waiting for transfers between devices: 77.9 us -> none  [local(): lax.psum_scatter(partial_value.astype(jnp.bfloat16), 'tensor', scatter_di...]
    ppermute x0 -> x22, waiting for transfers between devices: none -> 73.3 us  [the longest x8 40.6 us: local(): lax.ppermute(part, 'tensor', from_worker)]
    all_gather x2 -> x4, waiting for transfers between devices: 47.2 us -> 0.06 us  [the longest x1 0.02 us: local(): lax.all_gather(output_down_maps.reshape(rank, features), ('dp', 'tensor')...]
    pallas_call x0 -> x6, Pallas kernels: none -> 43.8 us  [the longest x4 33.7 us: attend_chunk(): pl.pallas_call(functools.partial(attend_kernel, shards, first_row, outer,...]
    psum x1 -> x0, blocking collectives: 39 us -> none  [local(): reduced_rows = lax.psum(local_shrink, 'tensor').astype(jnp.bfloat16)]
    ppermute x0 -> x22, starting transfers between devices: none -> 36.9 us  [the longest x8 10.8 us: local(): lax.ppermute(part, 'tensor', from_worker)]
    all_to_all x0 -> x1, blocking collectives: none -> 20.4 us  [local(): piece = lax.all_to_all(piece, 'tensor', 0, 0)]
    dot_general x10 -> x2, matrix products: 23.3 us -> 3.45 us  [the longest x1 3.2 us: local(): jnp.einsum('td,akd->tak', tokens, down_all, preferred_element_type=jnp.fl...]
  transfers between devices with their start and end apart: 4 -> 26, of which waited for: 3 -> 8; matrix products, arithmetic and copies ran while one was open for 11% -> 13% of each run, Pallas kernels for 0% -> 16%
where the time goes in v1:
time: 249 us; the launch traced here: 247 us
  waiting for transfers between devices  74.1 us (30%)
  Pallas kernels  43.8 us (18%)
  blocking collectives  37.7 us (15%)
  starting transfers between devices  37 us (15%)
  local copies, waits for them, and re-layouts  24.1 us (10%)
  between operations  13.8 us (6%)
  other arithmetic  13.2 us (5%)
  matrix products  3.45 us (1%)
    ppermute x8, waiting for transfers between devices, local(): lax.ppermute(part, 'tensor', from_worker)  40.6 us
    pallas_call x4, Pallas kernels, attend_chunk(): pl.pallas_call(functools.partial(attend_kernel, shards, first_row, outer,...  33.7 us
    all_to_all x1, blocking collectives, local(): piece = lax.all_to_all(piece, 'tensor', 0, 0)  20.4 us
    ppermute x1, waiting for transfers between devices, local(): piece = lax.ppermute(piece, 'tensor', to_worker)  16.7 us
    ppermute x1, waiting for transfers between devices, local(): shrink = shrink + lax.ppermute(shrink, 'tensor', to_worker)  14.1 us
    ppermute x8, starting transfers between devices, local(): lax.ppermute(part, 'tensor', from_worker)  10.8 us
    pallas_call x2, Pallas kernels, output_chunk(): pl.pallas_call(functools.partial(output_kernel, groups), out_shape=jax.Sh...  10.1 us
    all_gather x1, blocking collectives, local(): up_all = lax.all_gather(up_pair, 'dp', axis=0)  9.94 us
  transfers between devices with their start and end apart: 26, of which 8 were waited for; matrix products, arithmetic and copies ran while one was open for 13% of the time, Pallas kernels for 16%

profile of v1, /device:TPU:0, one launch (start us, length us, event | category | flops | bytes accessed | tf_op | source)
XLA Modules:
  0.0 247.2 jit_solution(9652528310683069813)
XLA Ops:
  7.3 1.5 all_gather_reshape.3
  10.1 5.0 %collective-permute-start.7 = (bf16[6,512,128]{2,1,0:T(8,128)(2,1)S(1)}, bf16[6,512,128]{2,1,0:T(8,128)(2,1)S(1)}, u32[]{:S(2)}, u32[]{:S(2)}) collective-permute-start(bf16[6,512,128]{2,1,0:T(8,128)(2,1)S(1)} %dynamic-slice_bitcast_fusion), channel_id=1, source_target_pairs={{0,1},{3,2},{4,5},{7,6},{8,9},{11,10},{12,13},{15,14},{16,17},{19,... | collective-permute-start | bytes 2359304 | tf_op jit(solution)/shard_map/ppermute | solution.py:259
  15.1 16.7 %collective-permute-done.7 = bf16[6,512,128]{2,1,0:T(8,128)(2,1)S(1)} collective-permute-done((bf16[6,512,128]{2,1,0:T(8,128)(2,1)S(1)}, bf16[6,512,128]{2,1,0:T(8,128)(2,1)S(1)}, u32[]{:S(2)}, u32[]{:S(2)}) %collective-permute-start.7) | collective-permute-done | bytes 786464 | tf_op jit(solution)/shard_map/ppermute | solution.py:259
  34.7 20.4 %all_to_all.5 = bf16[4,4,16,1024]{3,2,1,0:T(8,128)(2,1)} all-to-all(bf16[4,4,16,1024]{3,2,1,0:T(8,128)(2,1)S(1)} %copy.57), channel_id=1, replica_groups=mesh['groups'=2,'dp'=4,'tensor'=4] {'tensor'}, dimensions={0} | all-to-all | bytes 1048576 | tf_op jit(solution)/shard_map/all_to_all | solution.py:312
  55.2 2.1 collective-permute-start.13
  58.1 3.6 %collective-permute-start.2 = (bf16[6,64,128]{2,1,0:T(8,128)(2,1)}, bf16[6,64,128]{2,1,0:T(8,128)(2,1)}, u32[]{:S(2)}, u32[]{:S(2)}) collective-permute-start(bf16[6,64,128]{2,1,0:T(8,128)(2,1)} %bitcast.18), channel_id=1, source_target_pairs={{0,1},{3,2},{4,5},{7,6},{8,9},{11,10},{12,13},{15,14},{16,17},{19,... | collective-permute-start | bytes 294920 | tf_op jit(solution)/shard_map/ppermute | solution.py:277
  61.7 2.1 collective-permute-start.3
  64.4 1.9 fusion.3
  66.2 3.2 %select_reduce_fusion = f32[512,192]{0,1:T(8,128)} fusion(bf16[4,192,1024]{2,1,0:T(8,128)(2,1)} %all-gather.8.cloned.1.call-done, bf16[512,1024]{1,0:T(8,128)(2,1)S(1)} %copy-done.23, pred[512,4]{0,1:T(4,128)(4,1)S(1)} %get-tuple-element.39), kind=kOutput, calls=%fused_computation | convolution fusion | flops 805994496 | bytes 3016704 | tf_op jit(solution)/shard_map/td,akd->tak/dot_general | solution.py:294
  69.4 2.0 collective-permute-start
  72.7 1.5 fusion.1
  74.4 1.8 collective-permute-done.2
  76.2 1.5 collective-permute-start.4
  78.6 14.1 %collective-permute-done = f32[512,192]{0,1:T(8,128)} collective-permute-done((f32[512,192]{0,1:T(8,128)}, f32[512,192]{0,1:T(8,128)}, u32[]{:S(2)}, u32[]{:S(2)}) %collective-permute-start) | collective-permute-done | bytes 393248 | tf_op jit(solution)/shard_map/ppermute | solution.py:296
  94.6 9.9 %all-gather = bf16[8,6,64,128]{3,2,1,0:T(8,128)(2,1)S(1)} all-gather(bf16[2,6,64,128]{3,2,1,0:T(8,128)(2,1)S(1)} %pad_maximum_fusion.1), channel_id=2, replica_groups=mesh['groups'=2,'dp'=4,'tensor'=4] {'dp'}, dimensions={0}, use_global_device_ids=true | all-gather | bytes 983040 | tf_op jit(solution)/shard_map/all_gather | solution.py:278
  106.9 1.5 collective-permute-start.5
  109.3 2.3 copy.52
  113.0 7.7 %attend.4 = (bf16[256,512]{1,0:T(8,128)(2,1)S(1)}, bf16[256,128]{1,0:T(8,128)(2,1)S(1)}, bf16[256,128]{1,0:T(8,128)(2,1)S(1)}) custom-call(s32[4]{0:T(128)S(1)} %pad_add_fusion.ids_ref, s32[256,1]{1,0:T(8,128)S(1)} %copy.54.start_ref, f32[256,128]{1,0:T(8,128)S(1)} %get-tuple-element.41.cos_ref, f32[256,128]{1,0:T(8,128)S(1)} %get-tuple-element.27.sin_ref, ...), custom_call_target="tpu_custom_call" | custom-call | flops 3221225472 | bytes 8388608 | tf_op jit(solution)/shard_map/attend/pallas_call | solution.py:122
  122.7 8.8 %attend.6 = (bf16[256,512]{1,0:T(8,128)(2,1)S(1)}, bf16[256,128]{1,0:T(8,128)(2,1)}, bf16[256,128]{1,0:T(8,128)(2,1)}) custom-call(s32[4]{0:T(128)S(1)} %pad_add_fusion.ids_ref, s32[256,1]{1,0:T(8,128)S(1)} %copy.61.start_ref, f32[256,128]{1,0:T(8,128)S(1)} %get-tuple-element.40.cos_ref, f32[256,128]{1,0:T(8,128)S(1)} %get-tuple-element.28.sin_ref, ...), custom_call_target="tpu_custom_call" | custom-call | flops 3221225472 | bytes 8388608 | tf_op jit(solution)/shard_map/attend/pallas_call | solution.py:122
  136.8 7.3 %all_gather.27 = bf16[4,64,1024]{2,1,0:T(8,128)(2,1)S(1)} all-gather(bf16[1,64,1024]{2,1,0:T(8,128)(2,1)S(1)} %copy-done.25), channel_id=1, replica_groups=mesh['groups'=2,'dp'=4,'tensor'=4] {'dp'}, dimensions={0}, use_global_device_ids=true | all-gather | bytes 655360 | tf_op jit(solution)/shard_map/all_gather | solution.py:282
  147.1 1.5 collective-permute-start.10
  148.6 17.8 %collective-permute-done.16 = bf16[256,512]{1,0:T(8,128)(2,1)} collective-permute-done((bf16[256,512]{1,0:T(8,128)(2,1)S(1)}, bf16[256,512]{1,0:T(8,128)(2,1)}, u32[]{:S(2)}, u32[]{:S(2)}) %collective-permute-start.16) | collective-permute-done | bytes 262176 | tf_op jit(solution)/shard_map/ppermute | solution.py:339
  167.4 6.3 %collective-permute-done.6 = bf16[256,512]{1,0:T(8,128)(2,1)} collective-permute-done((bf16[256,512]{1,0:T(8,128)(2,1)S(1)}, bf16[256,512]{1,0:T(8,128)(2,1)}, u32[]{:S(2)}, u32[]{:S(2)}) %collective-permute-start.6) | collective-permute-done | bytes 262176 | tf_op jit(solution)/shard_map/ppermute | solution.py:339
  179.4 8.4 %attend.5 = (bf16[256,512]{1,0:T(8,128)(2,1)}, bf16[256,128]{1,0:T(8,128)(2,1)S(1)}, bf16[256,128]{1,0:T(8,128)(2,1)S(1)}) custom-call(s32[4]{0:T(128)S(1)} %pad_add_fusion.ids_ref, s32[256,1]{1,0:T(8,128)S(1)} %copy-done.17, f32[256,128]{1,0:T(8,128)S(1)} %copy-done.13, f32[256,128]{1,0:T(8,128)S(1)} %copy-done.11, bf16[3,256,256]{2,1,0:T(8,128)(2,1)S(1)} %copy-done.4, ...), custom_call_target="tpu_custom_call" | custom-call | flops 3221225472 | bytes 8388608 | tf_op jit(solution)/shard_map/attend/pallas_call | solution.py:122
  187.9 8.9 %attend.7 = (bf16[256,512]{1,0:T(8,128)(2,1)}, bf16[256,128]{1,0:T(8,128)(2,1)}, bf16[256,128]{1,0:T(8,128)(2,1)}) custom-call(s32[4]{0:T(128)S(1)} %pad_add_fusion.ids_ref, s32[256,1]{1,0:T(8,128)S(1)} %copy-done.15, f32[256,128]{1,0:T(8,128)S(1)} %copy-done.9, f32[256,128]{1,0:T(8,128)S(1)} %get-tuple-element.28.sin_ref, ...), custom_call_target="tpu_custom_call" | custom-call | flops 3221225472 | bytes 8388608 | tf_op jit(solution)/shard_map/attend/pallas_call | solution.py:122
  204.0 5.0 %copy.58 = bf16[4,4,8,16,1024]{4,3,2,1,0:T(8,128)(2,1)} copy(bf16[4,4,8,16,1024]{4,3,1,0,2:T(8,128)(2,1)} %bitcast.63) | data formatting | bytes 8388608 | tf_op jit(solution)/shard_map/transpose | solution.py:314
  210.3 2.9 %collective-permute-done.17 = bf16[256,512]{1,0:T(8,128)(2,1)S(1)} collective-permute-done((bf16[256,512]{1,0:T(8,128)(2,1)}, bf16[256,512]{1,0:T(8,128)(2,1)S(1)}, u32[]{:S(2)}, u32[]{:S(2)}) %collective-permute-start.17) | collective-permute-done | bytes 262176 | tf_op jit(solution)/shard_map/ppermute | solution.py:339
  213.3 1.6 collective-permute-start.12
  214.8 3.8 %collective-permute-done.8 = bf16[256,512]{1,0:T(8,128)(2,1)} collective-permute-done((bf16[256,512]{1,0:T(8,128)(2,1)}, bf16[256,512]{1,0:T(8,128)(2,1)}, u32[]{:S(2)}, u32[]{:S(2)}) %collective-permute-start.8) | collective-permute-done | bytes 262176 | tf_op jit(solution)/shard_map/ppermute | solution.py:339
  219.6 9.8 %collective-permute-done.21 = bf16[256,512]{1,0:T(8,128)(2,1)S(1)} collective-permute-done((bf16[256,512]{1,0:T(8,128)(2,1)}, bf16[256,512]{1,0:T(8,128)(2,1)S(1)}, u32[]{:S(2)}, u32[]{:S(2)}) %collective-permute-start.21) | collective-permute-done | bytes 262176 | tf_op jit(solution)/shard_map/ppermute | solution.py:339
  229.5 5.0 %project_out.3 = bf16[256,1024]{1,0:T(8,128)(2,1)S(1)} custom-call(s32[4]{0:T(128)S(1)} %pad_add_fusion.ids_ref, bf16[256,256]{1,0:T(8,128)(2,1)S(1)} %copy.63.mask_ref, bf16[256,1024]{1,0:T(8,128)(2,1)S(1)} %bitcast.55, bf16[256,512]{1,0:T(8,128)(2,1)S(1)} %broadcast_select_fusion.3.refs_0_, bf16[256,512]{1,0:T(8,128)(2,1)S(1)} %broadcast_select_fusion.2.refs_1_, ...), custom_call_target="tpu_custom_call" | custom-call | flops 1342177280 | bytes 6291456 | tf_op jit(solution)/shard_map/project_out/pallas_call | solution.py:176
  234.6 5.0 %project_out.2 = bf16[256,1024]{1,0:T(8,128)(2,1)S(1)} custom-call(s32[4]{0:T(128)S(1)} %pad_add_fusion.ids_ref, bf16[256,256]{1,0:T(8,128)(2,1)S(1)} %copy.60.mask_ref, bf16[256,1024]{1,0:T(8,128)(2,1)S(1)} %bitcast.56, bf16[256,512]{1,0:T(8,128)(2,1)S(1)} %broadcast_select_fusion.7.refs_0_, bf16[256,512]{1,0:T(8,128)(2,1)S(1)} %broadcast_select_fusion.6.refs_1_, ...), custom_call_target="tpu_custom_call" | custom-call | flops 1342177280 | bytes 6291456 | tf_op jit(solution)/shard_map/project_out/pallas_call | solution.py:176
  (135 shorter events, 42.4 us)
Async XLA Ops:
  6.5 59.7 %all-gather.8.cloned.1.call-start = ((), (), s32[]{:S(2)}) async-start(), calls=%async_computation.1 | async-start | bytes 1966080 | tf_op jit(solution)/shard_map/all_gather | solution.py:275
  7.3 137.1 %all-gather.10.cloned.1.call-start = ((), (), s32[]{:S(2)}) async-start(), calls=%async_computation.2 | async-start | bytes 1114112 | tf_op jit(solution)/shard_map/all_gather | solution.py:279
  8.8 165.9 %all-gather.12.cloned.1.call-start = ((), (), s32[]{:S(2)}) async-start(), calls=%async_computation.3 | async-start | bytes 7077888 | tf_op jit(solution)/shard_map/all_gather | solution.py:260
  10.1 21.7 %collective-permute-start.7 = (bf16[6,512,128]{2,1,0:T(8,128)(2,1)S(1)}, bf16[6,512,128]{2,1,0:T(8,128)(2,1)S(1)}, u32[]{:S(2)}, u32[]{:S(2)}) collective-permute-start(bf16[6,512,128]{2,1,0:T(8,128)(2,1)S(1)} %dynamic-slice_bitcast_fusion), channel_id=1, source_target_pairs={{0,1},{3,2},{4,5},{7,6},{8,9},{11,10},{12,13},{15,14},{16,17},{19,... | collective-permute-start | bytes 2359304 | tf_op jit(solution)/shard_map/ppermute | solution.py:259
  32.7 171.3 %all-gather.14.cloned.1.call-start = ((), (), s32[]{:S(2)}) async-start(), calls=%async_computation.4 | async-start | bytes 4718592 | tf_op jit(solution)/shard_map/all_gather | solution.py:313
  34.7 29.4 %copy-start.27 = (s32[1,4]{1,0:T(1,128)S(1)}, s32[1,4]{1,0:T(1,128)}, u32[]{:S(2)}) copy-start(s32[1,4]{1,0:T(1,128)} %param.16) | copy-start | bytes 52
  55.2 50.2 %collective-permute-start.13 = (bf16[256,1024]{1,0:T(8,128)(2,1)S(1)}, bf16[256,1024]{1,0:T(8,128)(2,1)S(1)}, u32[]{:S(2)}, u32[]{:S(2)}) collective-permute-start(bf16[256,1024]{1,0:T(8,128)(2,1)S(1)} %get-tuple-element.22.refs_0_), channel_id=1, source_target_pairs={{0,1},{3,2},{4,5},{7,6},{8,9},{11,10},{12,13},{15,14},{16,17},{19,... | collective-permute-start | bytes 1572872 | tf_op jit(solution)/shard_map/ppermute | solution.py:248
  57.4 63.4 %collective-permute-start.14 = (bf16[256,1024]{1,0:T(8,128)(2,1)S(1)}, bf16[256,1024]{1,0:T(8,128)(2,1)S(1)}, u32[]{:S(2)}, u32[]{:S(2)}) collective-permute-start(bf16[256,1024]{1,0:T(8,128)(2,1)S(1)} %get-tuple-element.22.refs_0_), channel_id=1, source_target_pairs={{1,2},{2,1},{5,6},{6,5},{9,10},{10,9},{13,14},{14,13},{17,18},{18,... | collective-permute-start | bytes 1572872 | tf_op jit(solution)/shard_map/ppermute | solution.py:251
  58.1 18.1 %collective-permute-start.2 = (bf16[6,64,128]{2,1,0:T(8,128)(2,1)}, bf16[6,64,128]{2,1,0:T(8,128)(2,1)}, u32[]{:S(2)}, u32[]{:S(2)}) collective-permute-start(bf16[6,64,128]{2,1,0:T(8,128)(2,1)} %bitcast.18), channel_id=1, source_target_pairs={{0,1},{3,2},{4,5},{7,6},{8,9},{11,10},{12,13},{15,14},{16,17},{19,... | collective-permute-start | bytes 294920 | tf_op jit(solution)/shard_map/ppermute | solution.py:277
  61.7 45.2 %collective-permute-start.3 = (bf16[256,1024]{1,0:T(8,128)(2,1)S(1)}, bf16[256,1024]{1,0:T(8,128)(2,1)}, u32[]{:S(2)}, u32[]{:S(2)}) collective-permute-start(bf16[256,1024]{1,0:T(8,128)(2,1)S(1)} %get-tuple-element.21.refs_0_), channel_id=1, source_target_pairs={{0,1},{3,2},{4,5},{7,6},{8,9},{11,10},{12,13},{15,14},{16,17},{19,... | collective-permute-start | bytes 1572872 | tf_op jit(solution)/shard_map/ppermute | solution.py:248
  69.4 23.3 %collective-permute-start = (f32[512,192]{0,1:T(8,128)}, f32[512,192]{0,1:T(8,128)}, u32[]{:S(2)}, u32[]{:S(2)}) collective-permute-start(f32[512,192]{0,1:T(8,128)} %select_reduce_fusion), channel_id=1, source_target_pairs={{0,1},{3,2},{4,5},{7,6},{8,9},{11,10},{12,13},{15,14},{16,17},{19,... | collective-permute-start | bytes 1179656 | tf_op jit(solution)/shard_map/ppermute | solution.py:296
  71.6 50.0 %copy-start.14 = (s32[256,1]{1,0:T(8,128)}, s32[256,1]{1,0:T(8,128)S(1)}, u32[]{:S(2)}) copy-start(s32[256,1]{1,0:T(8,128)S(1)} %copy.61.start_ref) | copy-start | bytes 3076
  72.7 40.3 %copy-start.16 = (s32[256,1]{1,0:T(8,128)}, s32[256,1]{1,0:T(8,128)S(1)}, u32[]{:S(2)}) copy-start(s32[256,1]{1,0:T(8,128)S(1)} %copy.54.start_ref) | copy-start | bytes 3076
  74.2 38.7 %copy-start.10 = (f32[256,128]{1,0:T(8,128)}, f32[256,128]{1,0:T(8,128)S(1)}, u32[]{:S(2)}) copy-start(f32[256,128]{1,0:T(8,128)S(1)} %get-tuple-element.27.sin_ref) | copy-start | bytes 393220
  74.3 38.7 %copy-start.12 = (f32[256,128]{1,0:T(8,128)}, f32[256,128]{1,0:T(8,128)S(1)}, u32[]{:S(2)}) copy-start(f32[256,128]{1,0:T(8,128)S(1)} %get-tuple-element.41.cos_ref) | copy-start | bytes 393220
  74.3 47.3 %copy-start.8 = (f32[256,128]{1,0:T(8,128)}, f32[256,128]{1,0:T(8,128)S(1)}, u32[]{:S(2)}) copy-start(f32[256,128]{1,0:T(8,128)S(1)} %get-tuple-element.40.cos_ref) | copy-start | bytes 393220
  76.2 36.8 %collective-permute-start.4 = (bf16[256,1024]{1,0:T(8,128)(2,1)S(1)}, bf16[256,1024]{1,0:T(8,128)(2,1)}, u32[]{:S(2)}, u32[]{:S(2)}) collective-permute-start(bf16[256,1024]{1,0:T(8,128)(2,1)S(1)} %get-tuple-element.21.refs_0_), channel_id=1, source_target_pairs={{1,2},{2,1},{5,6},{6,5},{9,10},{10,9},{13,14},{14,13},{17,18},{18,... | collective-permute-start | bytes 1572872 | tf_op jit(solution)/shard_map/ppermute | solution.py:251
  93.9 14.4 %collective-permute-start.1 = (f32[512,192]{0,1:T(8,128)S(1)}, f32[512,192]{0,1:T(8,128)S(1)}, u32[]{:S(2)}, u32[]{:S(2)}) collective-permute-start(f32[512,192]{0,1:T(8,128)S(1)} %add.70), channel_id=1, source_target_pairs={{1,2},{2,1},{5,6},{6,5},{9,10},{10,9},{13,14},{14,13},{17,18},{18,... | collective-permute-start | bytes 1179656 | tf_op jit(solution)/shard_map/ppermute | solution.py:299
  105.4 16.2 %collective-permute-start.15 = (bf16[256,1024]{1,0:T(8,128)(2,1)S(1)}, bf16[256,1024]{1,0:T(8,128)(2,1)}, u32[]{:S(2)}, u32[]{:S(2)}) collective-permute-start(bf16[256,1024]{1,0:T(8,128)(2,1)S(1)} %collective-permute-done.13.refs_1_), channel_id=1, source_target_pairs={{1,2},{2,1},{5,6},{6,5},{9,10},{10,9},{13,14},{14,13},{17,18},{18,... | collective-permute-start | bytes 1572872 | tf_op jit(solution)/shard_map/ppermute | solution.py:252
  106.9 6.1 %collective-permute-start.5 = (bf16[256,1024]{1,0:T(8,128)(2,1)}, bf16[256,1024]{1,0:T(8,128)(2,1)}, u32[]{:S(2)}, u32[]{:S(2)}) collective-permute-start(bf16[256,1024]{1,0:T(8,128)(2,1)} %collective-permute-done.3.refs_1_), channel_id=1, source_target_pairs={{1,2},{2,1},{5,6},{6,5},{9,10},{10,9},{13,14},{14,13},{17,18},{18,... | collective-permute-start | bytes 1572872 | tf_op jit(solution)/shard_map/ppermute | solution.py:252
  131.4 35.0 %collective-permute-start.16 = (bf16[256,512]{1,0:T(8,128)(2,1)S(1)}, bf16[256,512]{1,0:T(8,128)(2,1)}, u32[]{:S(2)}, u32[]{:S(2)}) collective-permute-start(bf16[256,512]{1,0:T(8,128)(2,1)S(1)} %get-tuple-element.17), channel_id=1, source_target_pairs={{1,0},{2,3},{5,4},{6,7},{9,8},{10,11},{13,12},{14,15},{17,16},{18,... | collective-permute-start | bytes 786440 | tf_op jit(solution)/shard_map/ppermute | solution.py:339
  132.7 13.1 %collective-permute-start.18 = (bf16[256,512]{1,0:T(8,128)(2,1)S(1)}, bf16[256,512]{1,0:T(8,128)(2,1)}, u32[]{:S(2)}, u32[]{:S(2)}) collective-permute-start(bf16[256,512]{1,0:T(8,128)(2,1)S(1)} %get-tuple-element.17), channel_id=1, source_target_pairs={{1,2},{2,1},{5,6},{6,5},{9,10},{10,9},{13,14},{14,13},{17,18},{18,... | collective-permute-start | bytes 786440 | tf_op jit(solution)/shard_map/ppermute | solution.py:336
  134.1 13.0 %collective-permute-start.9 = (bf16[256,512]{1,0:T(8,128)(2,1)S(1)}, bf16[256,512]{1,0:T(8,128)(2,1)}, u32[]{:S(2)}, u32[]{:S(2)}) collective-permute-start(bf16[256,512]{1,0:T(8,128)(2,1)S(1)} %get-tuple-element.13), channel_id=1, source_target_pairs={{1,2},{2,1},{5,6},{6,5},{9,10},{10,9},{13,14},{14,13},{17,18},{18,... | collective-permute-start | bytes 786440 | tf_op jit(solution)/shard_map/ppermute | solution.py:336
  135.5 38.2 %collective-permute-start.6 = (bf16[256,512]{1,0:T(8,128)(2,1)S(1)}, bf16[256,512]{1,0:T(8,128)(2,1)}, u32[]{:S(2)}, u32[]{:S(2)}) collective-permute-start(bf16[256,512]{1,0:T(8,128)(2,1)S(1)} %get-tuple-element.13), channel_id=1, source_target_pairs={{1,0},{2,3},{5,4},{6,7},{9,8},{10,11},{13,12},{14,15},{17,16},{18,... | collective-permute-start | bytes 786440 | tf_op jit(solution)/shard_map/ppermute | solution.py:339
  145.8 53.6 %collective-permute-start.19 = (bf16[256,512]{1,0:T(8,128)(2,1)}, bf16[256,512]{1,0:T(8,128)(2,1)}, u32[]{:S(2)}, u32[]{:S(2)}) collective-permute-start(bf16[256,512]{1,0:T(8,128)(2,1)} %collective-permute-done.18), channel_id=1, source_target_pairs={{1,0},{2,3},{5,4},{6,7},{9,8},{10,11},{13,12},{14,15},{17,16},{18,... | collective-permute-start | bytes 786440 | tf_op jit(solution)/shard_map/ppermute | solution.py:339
  147.1 55.9 %collective-permute-start.10 = (bf16[256,512]{1,0:T(8,128)(2,1)}, bf16[256,512]{1,0:T(8,128)(2,1)}, u32[]{:S(2)}, u32[]{:S(2)}) collective-permute-start(bf16[256,512]{1,0:T(8,128)(2,1)} %collective-permute-done.9), channel_id=1, source_target_pairs={{1,0},{2,3},{5,4},{6,7},{9,8},{10,11},{13,12},{14,15},{17,16},{18,... | collective-permute-start | bytes 786440 | tf_op jit(solution)/shard_map/ppermute | solution.py:339
  196.7 16.5 %collective-permute-start.17 = (bf16[256,512]{1,0:T(8,128)(2,1)}, bf16[256,512]{1,0:T(8,128)(2,1)S(1)}, u32[]{:S(2)}, u32[]{:S(2)}) collective-permute-start(bf16[256,512]{1,0:T(8,128)(2,1)} %get-tuple-element.20), channel_id=1, source_target_pairs={{1,0},{2,3},{5,4},{6,7},{9,8},{10,11},{13,12},{14,15},{17,16},{18,... | collective-permute-start | bytes 786440 | tf_op jit(solution)/shard_map/ppermute | solution.py:339
  198.0 11.0 %collective-permute-start.20 = (bf16[256,512]{1,0:T(8,128)(2,1)}, bf16[256,512]{1,0:T(8,128)(2,1)}, u32[]{:S(2)}, u32[]{:S(2)}) collective-permute-start(bf16[256,512]{1,0:T(8,128)(2,1)} %get-tuple-element.20), channel_id=1, source_target_pairs={{1,2},{2,1},{5,6},{6,5},{9,10},{10,9},{13,14},{14,13},{17,18},{18,... | collective-permute-start | bytes 786440 | tf_op jit(solution)/shard_map/ppermute | solution.py:336
  200.3 18.3 %collective-permute-start.8 = (bf16[256,512]{1,0:T(8,128)(2,1)}, bf16[256,512]{1,0:T(8,128)(2,1)}, u32[]{:S(2)}, u32[]{:S(2)}) collective-permute-start(bf16[256,512]{1,0:T(8,128)(2,1)} %get-tuple-element.14), channel_id=1, source_target_pairs={{1,0},{2,3},{5,4},{6,7},{9,8},{10,11},{13,12},{14,15},{17,16},{18,... | collective-permute-start | bytes 786440 | tf_op jit(solution)/shard_map/ppermute | solution.py:339
  201.6 11.6 %collective-permute-start.11 = (bf16[256,512]{1,0:T(8,128)(2,1)}, bf16[256,512]{1,0:T(8,128)(2,1)}, u32[]{:S(2)}, u32[]{:S(2)}) collective-permute-start(bf16[256,512]{1,0:T(8,128)(2,1)} %get-tuple-element.14), channel_id=1, source_target_pairs={{1,2},{2,1},{5,6},{6,5},{9,10},{10,9},{13,14},{14,13},{17,18},{18,... | collective-permute-start | bytes 786440 | tf_op jit(solution)/shard_map/ppermute | solution.py:336
  209.0 20.4 %collective-permute-start.21 = (bf16[256,512]{1,0:T(8,128)(2,1)}, bf16[256,512]{1,0:T(8,128)(2,1)S(1)}, u32[]{:S(2)}, u32[]{:S(2)}) collective-permute-start(bf16[256,512]{1,0:T(8,128)(2,1)} %collective-permute-done.20), channel_id=1, source_target_pairs={{1,0},{2,3},{5,4},{6,7},{9,8},{10,11},{13,12},{14,15},{17,16},{18,... | collective-permute-start | bytes 786440 | tf_op jit(solution)/shard_map/ppermute | solution.py:339
  213.3 21.2 %collective-permute-start.12 = (bf16[256,512]{1,0:T(8,128)(2,1)}, bf16[256,512]{1,0:T(8,128)(2,1)S(1)}, u32[]{:S(2)}, u32[]{:S(2)}) collective-permute-start(bf16[256,512]{1,0:T(8,128)(2,1)} %collective-permute-done.11), channel_id=1, source_target_pairs={{1,0},{2,3},{5,4},{6,7},{9,8},{10,11},{13,12},{14,15},{17,16},{18,... | collective-permute-start | bytes 786440 | tf_op jit(solution)/shard_map/ppermute | solution.py:339
  (22 other events, 207.8 us)
Sparse Core Ops, SparseCore 0:
  8.9 22.3 all-gather.7
  33.5 40.0 all-gather.9
  75.5 45.2 all-gather.11
  122.5 40.7 all-gather.13

commit v2 on v0

v2 whole, which is shorter than its diff:
```python
import functools
import math

import jax
import jax.numpy as jnp
from jax import lax
from jax.experimental import pallas as pl
from jax.experimental.pallas import tpu as pltpu
from jax.sharding import PartitionSpec as P

CHUNKS = 2
VMEM_BYTES = 48 * 1024 * 1024
PLANE = ("groups", "dp")
WHOLE = pl.BlockSpec(memory_space=pltpu.VMEM)


def after(value, *earlier):
    return lax.optimization_barrier((value,) + earlier)[0]


def wide_slots(w_refs, pair):
    if len(w_refs[0].shape) == 3:
        parts = [w_ref[...] for w_ref in w_refs]
    else:
        parts = [
            w_ref[piece] for piece in range(w_refs[0].shape[0]) for w_ref in w_refs
        ]
    wide = [jnp.concatenate([part[2 * pair], part[2 * pair + 1]], axis=1) for part in parts]
    return wide[0] if len(wide) == 1 else jnp.concatenate(wide, axis=0)


def accumulate(acc_ref, token_refs, w_refs, first):
    slots, _, head_size = w_refs[0].shape[-3:]
    for pair in range(slots // 2):
        columns = slice(2 * pair * head_size, (2 * pair + 2) * head_size)
        weight = wide_slots(w_refs, pair)
        row = 0
        for token_ref in token_refs:
            rows = slice(row, row + token_ref.shape[0])
            row = rows.stop
            total = jnp.dot(token_ref[...], weight, preferred_element_type=jnp.float32)
            if first is None:
                acc_ref[rows, columns] = total
            else:
                acc_ref[rows, columns] = first[rows, columns] + total


def split_refs(refs, layout):
    groups, at = [], 0
    for count in layout:
        groups.append(refs[at : at + count])
        at += count
    return groups, refs[at:]


def project_kernel(layout, weights, ids_ref, *refs):
    tokens, rest = split_refs(refs, layout)
    w_refs, acc_ref = rest[:weights], rest[weights]
    step = pl.program_id(0)
    for number, token_refs in enumerate(tokens):
        pl.when(step == number)(
            functools.partial(
                accumulate, acc_ref, token_refs, w_refs, acc_ref if number else None
            )
        )


def attend_kernel(layout, weights, started, first_row, ids_ref, *refs):
    start_ref, cos_ref, sin_ref, low_ref, up_ref = refs[:5]
    tokens, rest = split_refs(refs[5:], layout)
    w_refs, rest = rest[:weights], rest[weights:]
    begun, rest = rest[:started], rest[started:]
    prior = rest[:2] if first_row else ()
    attended_ref, keys_ref, values_ref, acc_ref = rest[len(prior) :]
    slots, _, head_size = w_refs[0].shape[-3:]
    step = pl.program_id(0)
    rows = acc_ref.shape[0]
    block = min(rows, 256)
    queries = slots - 2

    for number, token_refs in enumerate(tokens):
        first = acc_ref if number else (begun[0] if begun else None)
        pl.when(step == number)(
            functools.partial(accumulate, acc_ref, token_refs, w_refs, first)
        )

    @pl.when(step == len(layout) - 1)
    def _():
        def slot(index, at):
            which = 0 if index < queries else index - queries + 1
            extra = jnp.dot(
                low_ref[which, at], up_ref[index], preferred_element_type=jnp.float32
            )
            return acc_ref[at, index * head_size : (index + 1) * head_size] + extra

        def rotated(index, at):
            value = slot(index, at)
            turned = pltpu.roll(value, head_size // 2, 1)
            return (value * cos_ref[at, :] + turned * sin_ref[at, :]).astype(jnp.bfloat16)

        for row in range(0, rows, block):
            at = slice(row, row + block)
            keys_ref[at, :] = rotated(queries, at)
            values_ref[at, :] = slot(queries + 1, at).astype(jnp.bfloat16)
            keys, values = keys_ref[: row + block], values_ref[: row + block]
            if first_row:
                keys = jnp.concatenate([prior[0][...], keys], axis=0)
                values = jnp.concatenate([prior[1][...], values], axis=0)
            key_rows = keys.shape[0]
            key_at = lax.broadcasted_iota(jnp.int32, (block, key_rows), 1)
            row_at = lax.broadcasted_iota(jnp.int32, (block, key_rows), 0) + (first_row + row)
            allowed = (key_at >= start_ref[at, :]) & (key_at <= row_at)
            for index in range(queries):
                scores = lax.dot_general(
                    rotated(index, at), keys, (((1,), (1,)), ((), ())),
                    preferred_element_type=jnp.float32,
                )
                scores = jnp.where(allowed, scores * (1.0 / math.sqrt(head_size)), -1e30)
                weights_exp = jnp.exp(scores - jnp.max(scores, axis=1, keepdims=True))
                scale = 1.0 / jnp.sum(weights_exp, axis=1, keepdims=True)
                attended = jnp.dot(
                    (weights_exp * scale).astype(jnp.bfloat16), values,
                    preferred_element_type=jnp.float32,
                )
                attended_ref[at, index * head_size : (index + 1) * head_size] = (
                    attended.astype(jnp.bfloat16)
                )


def weight_spec(weight, depth):
    if len(weight.shape) == 3:
        slots, _, head_size = weight.shape
        return pl.BlockSpec((slots, depth, head_size), lambda step, ids: (0, ids[step], 0))
    pieces = depth // (weight.shape[2] * weight.shape[0] // weight.shape[0])
    return pl.BlockSpec((pieces,) + weight.shape[1:], lambda step, ids: (ids[step], 0, 0, 0))


def weight_specs(weights, depth):
    if len(weights) == 1 and len(weights[0].shape) == 3:
        return [weight_spec(weights[0], depth)]
    pieces = depth // sum(weight.shape[2] for weight in weights)
    return [
        pl.BlockSpec((pieces,) + weight.shape[1:], lambda step, ids: (ids[step], 0, 0, 0))
        for weight in weights
    ]


PARAMS = pltpu.CompilerParams(vmem_limit_bytes=VMEM_BYTES)
COST = pl.CostEstimate(flops=1000, bytes_accessed=1000, transcendentals=0)


def project(ids, tokens, weights):
    depth = tokens[0][0].shape[1]
    rows = sum(part.shape[0] for part in tokens[0])
    slots, _, head_size = weights[0].shape[-3:]
    return pl.pallas_call(
        functools.partial(project_kernel, [len(parts) for parts in tokens], len(weights)),
        out_shape=jax.ShapeDtypeStruct((rows, slots * head_size), jnp.float32),
        grid_spec=pltpu.PrefetchScalarGridSpec(
            num_scalar_prefetch=1,
            grid=(len(tokens),),
            in_specs=[WHOLE] * sum(len(parts) for parts in tokens)
            + weight_specs(weights, depth),
            out_specs=WHOLE,
        ),
        compiler_params=PARAMS,
        cost_estimate=COST,
        name="project",
    )(ids, *[part for parts in tokens for part in parts], *weights)


def attend(ids, tables, up, tokens, weights, begun, prior):
    depth = tokens[0][0].shape[1]
    rows = sum(part.shape[0] for part in tokens[0])
    slots, _, head_size = weights[0].shape[-3:]
    first_row = prior[0].shape[0] if prior else 0
    out = (
        jax.ShapeDtypeStruct((rows, (slots - 2) * head_size), jnp.bfloat16),
        jax.ShapeDtypeStruct((rows, head_size), jnp.bfloat16),
        jax.ShapeDtypeStruct((rows, head_size), jnp.bfloat16),
    )
    parts = [part for parts in tokens for part in parts]
    return pl.pallas_call(
        functools.partial(
            attend_kernel, [len(item) for item in tokens], len(weights), len(begun), first_row
        ),
        out_shape=out,
        grid_spec=pltpu.PrefetchScalarGridSpec(
            num_scalar_prefetch=1,
            grid=(len(tokens),),
            in_specs=[WHOLE] * (5 + len(parts))
            + weight_specs(weights, depth)
            + [WHOLE] * (len(begun) + len(prior)),
            out_specs=[WHOLE] * 3,
            scratch_shapes=[pltpu.VMEM((rows, slots * head_size), jnp.float32)],
        ),
        compiler_params=PARAMS,
        cost_estimate=COST,
        name="attend",
    )(ids, *tables, up, *parts, *weights, *begun, *prior)


def output_kernel(groups, parts, begun, last, ids_ref, *refs):
    attended_refs, rest = refs[: groups * parts * 2], refs[groups * parts * 2 :]
    w_ref, down_ref = rest[:2]
    rest = rest[2:]
    begun_refs, rest = rest[: 2 * begun], rest[2 * begun :]
    if last:
        mask_ref, up_ref, out_ref, acc_ref, low_ref = rest
    else:
        acc_ref, low_ref = rest
    step = pl.program_id(0)

    def accumulate_group(number, side):
        row = 0
        for part in range(parts):
            attended = attended_refs[(number * parts + part) * 2 + side][...]
            at = slice(row, row + attended.shape[0])
            row = at.stop
            total = jnp.dot(attended, w_ref[0], preferred_element_type=jnp.float32)
            low = lax.dot_general(
                attended, down_ref[0], (((1,), (1,)), ((), ())),
                preferred_element_type=jnp.float32,
            )
            if number:
                total, low = acc_ref[at, :] + total, low_ref[at, :] + low
            elif begun:
                total, low = begun_refs[0][at, :] + total, begun_refs[1][at, :] + low
            acc_ref[at, :] = total
            low_ref[at, :] = low

    for number in range(groups):
        for side in range(2):
            pl.when((step == number) & (ids_ref[groups] == side))(
                functools.partial(accumulate_group, number, side)
            )

    if last:
        @pl.when(step == groups - 1)
        def _():
            low = low_ref[...].astype(jnp.bfloat16) * mask_ref[...]
            extra = jnp.dot(low, up_ref[...], preferred_element_type=jnp.float32)
            out_ref[...] = (acc_ref[...] + extra).astype(jnp.bfloat16)


def project_out(ids, is_worker, attended, weight, down, begun, final):
    groups, parts = len(attended), len(attended[0])
    rows = sum(part[0].shape[0] for part in attended[0])
    features, columns = weight.shape[1:]
    ranks = down.shape[1]
    ids = jnp.concatenate([ids, is_worker.astype(jnp.int32)[None]])
    flat = [array for group in attended for part in group for array in part]
    sums = [
        jax.ShapeDtypeStruct((rows, columns), jnp.float32),
        jax.ShapeDtypeStruct((rows, ranks), jnp.float32),
    ]
    return pl.pallas_call(
        functools.partial(output_kernel, groups, parts, len(begun) // 2, bool(final)),
        out_shape=jax.ShapeDtypeStruct((rows, columns), jnp.bfloat16) if final else sums,
        grid_spec=pltpu.PrefetchScalarGridSpec(
            num_scalar_prefetch=1,
            grid=(groups,),
            in_specs=[WHOLE] * len(flat)
            + [
                pl.BlockSpec((1, features, columns), lambda step, ids: (ids[step], 0, 0)),
                pl.BlockSpec((1, ranks, features), lambda step, ids: (ids[step], 0, 0)),
            ]
            + [WHOLE] * (len(begun) + len(final)),
            out_specs=WHOLE if final else [WHOLE] * 2,
            scratch_shapes=[pltpu.VMEM(item.shape, jnp.float32) for item in sums]
            if final else [],
        ),
        compiler_params=PARAMS,
        cost_estimate=COST,
        name="project_out",
    )(ids, *flat, weight, down, *begun, *final)


def gather_over(value, axis, size):
    here = lax.axis_index(axis)
    value = value[None]
    distance = size // 2
    while distance:
        moved = lax.ppermute(value, axis, [(i, i ^ distance) for i in range(size)])
        upper = (here // distance) % 2 == 1
        value = jnp.concatenate(
            [jnp.where(upper, moved, value), jnp.where(upper, value, moved)], axis=0
        )
        distance //= 2
    return value


def bit_order(size):
    order = [0]
    distance = size // 2
    while distance:
        order = order + [place + distance for place in order]
        distance //= 2
    return order


def local(
    dp_size,
    plane_size,
    planes,
    tokens,
    query_key_value_weight,
    output_weight,
    adapter_down_maps,
    adapter_up_maps,
    output_down_maps,
    output_up_maps,
    request_adapter,
    lengths,
):
    token_rows, depth = tokens.shape
    _, slots, head_size = query_key_value_weight.shape
    queries = slots - 2
    rank = adapter_up_maps.shape[1]
    features = queries * head_size
    columns = output_weight.shape[2] // planes
    pairs = planes // 2

    def worker(pair):
        return 2 * pair + 1 - pair % 2

    def outer(pair):
        return 2 * pair + pair % 2

    to_worker = [(outer(p), worker(p)) for p in range(pairs)]
    from_worker = [(worker(p), outer(p)) for p in range(pairs)]
    ring = [(worker(p), worker((p + 1) % pairs)) for p in range(pairs)]
    here = lax.axis_index("tensor")
    pair = here // 2
    is_worker = here == worker(pair)
    sources = [(pair - step + pairs) % pairs for step in range(pairs)]
    worker_ids = jnp.stack([worker(source) for source in sources]).astype(jnp.int32)
    outer_ids = jnp.stack([outer(source) for source in sources]).astype(jnp.int32)
    place = lax.axis_index(PLANE)

    own_tokens = [tokens]
    for _ in range(pairs - 1):
        own_tokens.append(lax.ppermute(own_tokens[-1], "tensor", ring))

    weight = jnp.transpose(query_key_value_weight, (1, 0, 2))
    share = weight.shape[1] // plane_size
    up_own = jnp.transpose(adapter_up_maps[0], (1, 0, 2))
    up_outer = lax.ppermute(up_own, "tensor", to_worker)
    shares = []
    for half in range(2):
        piece = lax.dynamic_slice_in_dim(
            weight, place * share + half * (share // 2), share // 2, axis=1
        )
        shares.append(lax.ppermute(piece, "tensor", to_worker))
    outer_weights = [lax.all_gather(piece, PLANE, axis=0) for piece in shares]

    chunk_rows = token_rows // CHUNKS
    outer_tokens = []
    previous = shares[1]
    for chunk in range(CHUNKS):
        part = after(tokens[chunk * chunk_rows : (chunk + 1) * chunk_rows], previous)
        previous = lax.ppermute(part, "tensor", to_worker)
        moving = [previous]
        for _ in range(pairs - 1):
            moving.append(lax.ppermute(moving[-1], "tensor", ring))
        outer_tokens.append(moving)

    request_ends = jnp.cumsum(lengths[0])
    request_starts = request_ends - lengths[0]
    at = jnp.arange(token_rows, dtype=jnp.int32)
    member = (at[:, None] >= request_starts[None, :]) & (at[:, None] < request_ends[None, :])
    start = jnp.sum(jnp.where(member, request_starts[None, :], 0), axis=1).astype(jnp.int32)
    position = at - start
    half = head_size // 2
    inv_freq = 10000.0 ** (-2.0 * jnp.arange(half, dtype=jnp.float32) / head_size)
    angles = position.astype(jnp.float32)[:, None] * inv_freq[None, :]
    cosine, sine = jnp.cos(angles), jnp.sin(angles)
    cos = jnp.concatenate([cosine, cosine], axis=1)
    sin = jnp.concatenate([-sine, sine], axis=1)

    down = adapter_down_maps[0].reshape(-1, head_size)
    pack = jnp.concatenate(
        [
            down,
            up_own.reshape(-1, head_size),
            up_outer.reshape(-1, head_size),
            output_up_maps[0].reshape(-1, head_size),
        ],
        axis=0,
    )
    sizes = [down.shape[0], slots * rank, slots * rank]
    order = jnp.array(bit_order(dp_size))
    pack = gather_over(pack, "dp", dp_size)
    down_all, up_all, up_other, out_up_all = jnp.split(
        pack, [sizes[0], sizes[0] + sizes[1], sum(sizes)], axis=1
    )
    down_all = down_all.reshape(dp_size, 3 * rank, depth)
    up_all = jnp.stack([up_all, up_other], axis=1).reshape(
        dp_size, 2, slots, rank, head_size
    )
    out_up_all = out_up_all.reshape(dp_size, rank, columns)
    pool = dp_size
    requests = request_adapter.shape[1]
    chosen_id = jnp.sum(jnp.where(member, request_adapter, 0), axis=1)
    if pool <= requests:
        chosen = chosen_id[:, None] == order[None, :]
    else:
        chosen = member
        spots = jnp.argmax(request_adapter[0][:, None] == order[None, :], axis=1)
        down_all, up_all, out_up_all = (
            jnp.take(maps, spots, axis=0) for maps in (down_all, up_all, out_up_all)
        )
    count = chosen.shape[1]
    partial = jnp.einsum("td,akd->tak", tokens, down_all, preferred_element_type=jnp.float32)
    shrink = jnp.sum(jnp.where(chosen[:, :, None], partial, 0.0), axis=1)
    shrink = shrink + lax.ppermute(shrink, "tensor", to_worker)
    moving = shrink
    for _ in range(pairs - 1):
        moving = lax.ppermute(moving, "tensor", ring)
        shrink = shrink + moving
    shrink = shrink.astype(jnp.bfloat16).reshape(token_rows, 3, 1, rank)
    low = jnp.where(chosen[:, None, :, None], shrink, jnp.zeros((), jnp.bfloat16))
    low = jnp.transpose(low.reshape(token_rows, 3, count * rank), (1, 0, 2))
    ups = jnp.transpose(up_all, (1, 2, 0, 3, 4)).reshape(2, slots, count * rank, head_size)
    out_ups = out_up_all.reshape(count * rank, columns)
    out_mask = jnp.repeat(chosen.astype(jnp.bfloat16), rank, axis=1)

    lines = head_size // plane_size
    piece = lax.dynamic_slice_in_dim(output_weight, place * lines, lines, axis=0)
    piece = jnp.transpose(piece.reshape(lines, queries, planes, columns), (2, 1, 0, 3))
    out_down = output_down_maps[0].reshape(rank, features)
    ready = own_tokens[-1]
    got, got_down = [lax.dynamic_index_in_dim(piece, here, 0, False)], [out_down]
    for turn in range(1, planes):
        send = lax.dynamic_index_in_dim(piece, (here + turn) % planes, 0, False)
        send = jnp.concatenate(
            [send.reshape(-1, columns), out_down.reshape(-1, columns)], axis=0
        )
        got_one = lax.ppermute(
            after(send, ready), "tensor", [(i, (i + turn) % planes) for i in range(planes)]
        )
        lines_got = queries * lines
        got.append(got_one[:lines_got].reshape(queries, lines, columns))
        got_down.append(got_one[lines_got:].reshape(rank, features))
    turned = gather_over(jnp.stack(got), "groups", plane_size // dp_size)
    turned = gather_over(turned, "dp", dp_size)
    turned_down = gather_over(jnp.stack(got_down), "dp", dp_size)
    turned = turned[jnp.argsort(order)]
    out_weight = jnp.transpose(turned, (2, 3, 1, 0, 4, 5)).reshape(planes, features, columns)
    if pool > requests:
        turned_down = jnp.take(turned_down, spots, axis=0)
    out_downs = jnp.transpose(turned_down, (1, 0, 2, 3)).reshape(planes, count * rank, features)

    tables = (start[:, None], cos, sin, low)
    begun = project(worker_ids, [(array,) for array in own_tokens], [weight])
    own_parts, prior = [], ()
    for chunk in range(CHUNKS):
        rows = slice(chunk * chunk_rows, (chunk + 1) * chunk_rows)
        attended, keys, values = attend(
            outer_ids,
            (start[rows, None], cos[rows], sin[rows], low[:, rows]),
            ups[0],
            [(array,) for array in outer_tokens[chunk]],
            [weight],
            [begun[rows]],
            prior,
        )
        prior = (keys, values)
        own_parts.append(attended)
    all_ids = jnp.concatenate([worker_ids, outer_ids])
    outer_part, _, _ = attend(
        all_ids,
        tables,
        ups[1],
        [(array,) for array in own_tokens]
        + [
            tuple(outer_tokens[chunk][step] for chunk in range(CHUNKS)) for step in range(pairs)
        ],
        outer_weights,
        [],
        (),
    )

    def spread(parts):
        result, moving = [], parts
        for step in range(pairs):
            if step:
                moving = [lax.ppermute(part, "tensor", ring) for part in moving]
            result.append(
                [(lax.ppermute(part, "tensor", from_worker), part) for part in moving]
            )
        return result

    def turns(ids):
        return (here - ids + planes) % planes

    begun = project_out(
        turns(worker_ids), is_worker, spread(own_parts), out_weight, out_downs, [], []
    )
    return project_out(
        turns(outer_ids), is_worker, spread([outer_part]), out_weight, out_downs,
        list(begun), [out_mask, out_ups],
    )


def solution(mesh):
    in_specs = (
        P(PLANE, "tensor"),
        P(None, None, "tensor"),
        P("tensor", None, None),
        P(PLANE, None, "tensor"),
        P(PLANE, None, None, "tensor"),
        P(PLANE, None, None, "tensor"),
        P(PLANE, None, "tensor"),
        P(PLANE, None),
        P(PLANE, None),
    )
    function = functools.partial(
        local,
        mesh.shape["dp"],
        mesh.shape["groups"] * mesh.shape["dp"],
        mesh.shape["tensor"],
    )
    return jax.shard_map(
        function, mesh=mesh, in_specs=in_specs, out_specs=P(PLANE, "tensor"), check_vma=False
    )
```

time: 261 us -> 278 us (1.065)
  blocking collectives: 62.6 us -> 0 us
  waiting for transfers between devices: 141 us -> 79.7 us
  starting transfers between devices: 0.3 us -> 50.4 us
  local copies, waits for them, and re-layouts: 14.7 us -> 59.1 us
  Pallas kernels: 0 us -> 38.5 us
  other arithmetic: 5.35 us -> 31.6 us
  matrix products: 23.3 us -> 2.53 us
    ppermute x0 -> x29, waiting for transfers between devices: none -> 79.6 us  [the longest x6 34.9 us: spread(): lax.ppermute(part, 'tensor', from_worker)]
    reduce_scatter x1 -> x0, waiting for transfers between devices: 77.9 us -> none  [local(): lax.psum_scatter(partial_value.astype(jnp.bfloat16), 'tensor', scatter_di...]
    ppermute x0 -> x29, starting transfers between devices: none -> 50.3 us  [the longest x2 9.74 us: local(): shares.append(lax.ppermute(piece, 'tensor', to_worker))]
    all_gather x2, waiting for transfers between devices: 47.2 us -> 0.04 us  [local(): outer_weights = [lax.all_gather(piece, PLANE, axis=0) for piece in shares]]
    psum x1 -> x0, blocking collectives: 39 us -> none  [local(): reduced_rows = lax.psum(local_shrink, 'tensor').astype(jnp.bfloat16)]
    pallas_call x0 -> x6, Pallas kernels: none -> 38.5 us  [the longest x3 24.6 us: attend(): pl.pallas_call(functools.partial(attend_kernel, [len(item) for item in to...]
    all_gather x3 -> x0, blocking collectives: 23.6 us -> none  [the longest x1 9.79 us: local(): lax.all_gather(adapter_up_maps, 'dp', axis=0, tiled=True)]
    dot_general x10 -> x1, matrix products: 23.3 us -> 2.53 us  [local(): jnp.einsum('td,akd->tak', tokens, down_all, preferred_element_type=jnp.fl...]
  transfers between devices with their start and end apart: 4 -> 31, of which waited for: 3 -> 9; matrix products, arithmetic and copies ran while one was open for 11% -> 30% of each run, Pallas kernels for 0% -> 12%
where the time goes in v2:
time: 278 us; the launch traced here: 276 us
  waiting for transfers between devices  79.7 us (29%)
  local copies, waits for them, and re-layouts  59.1 us (21%)
  starting transfers between devices  50.4 us (18%)
  Pallas kernels  38.5 us (14%)
  other arithmetic  31.6 us (11%)
  between operations  14.4 us (5%)
    ppermute x6, waiting for transfers between devices, spread(): lax.ppermute(part, 'tensor', from_worker)  34.9 us
    ppermute x7, waiting for transfers between devices, gather_over(): moved = lax.ppermute(value, axis, [(i, i ^ distance) for i in range(size)])  27.7 us
    pallas_call x3, Pallas kernels, attend(): pl.pallas_call(functools.partial(attend_kernel, [len(item) for item in to...  24.6 us
    unnamed x141, local copies, waits for them, and re-layouts  15 us
    pallas_call x2, Pallas kernels, project_out(): pl.pallas_call(functools.partial(output_kernel, groups, parts, len(begun)...  9.93 us
    ppermute x2, starting transfers between devices, local(): shares.append(lax.ppermute(piece, 'tensor', to_worker))  9.74 us
    select_n x6, other arithmetic, gather_over(): jnp.where(upper, moved, value)  8.82 us
    ppermute x3, waiting for transfers between devices, local(): lax.ppermute(after(send, ready), 'tensor', [(i, (i + turn) % planes) for...  8.57 us
  transfers between devices with their start and end apart: 31, of which 9 were waited for; matrix products, arithmetic and copies ran while one was open for 30% of the time, Pallas kernels for 12%

profile of v2, /device:TPU:0, one launch (start us, length us, event | category | flops | bytes accessed | tf_op | source)
XLA Modules:
  0.0 276.3 jit_solution(2416783629588244905)
XLA Ops:
  6.6 2.1 dynamic-slice_bitcast_fusion
  8.7 4.9 %collective-permute-start.11 = (bf16[6,256,128]{2,1,0:T(8,128)(2,1)S(1)}, bf16[6,256,128]{2,1,0:T(8,128)(2,1)S(1)}, u32[]{:S(2)}, u32[]{:S(2)}) collective-permute-start(bf16[6,256,128]{2,1,0:T(8,128)(2,1)S(1)} %get-tuple-element.37), channel_id=1, source_target_pairs={{0,1},{3,2},{4,5},{7,6},{8,9},{11,10},{12,13},{15,14},{16,17},{19,... | collective-permute-start | bytes 1179656 | tf_op jit(solution)/shard_map/ppermute | solution.py:354
  13.6 8.3 %collective-permute-done.11 = bf16[6,256,128]{2,1,0:T(8,128)(2,1)S(1)} collective-permute-done((bf16[6,256,128]{2,1,0:T(8,128)(2,1)S(1)}, bf16[6,256,128]{2,1,0:T(8,128)(2,1)S(1)}, u32[]{:S(2)}, u32[]{:S(2)}) %collective-permute-start.11) | collective-permute-done | bytes 393248 | tf_op jit(solution)/shard_map/ppermute | solution.py:354
  22.8 4.4 %collective-permute-start = (bf16[6,64,128]{2,1,0:T(8,128)(2,1)S(1)}, bf16[6,64,128]{2,1,0:T(8,128)(2,1)S(1)}, u32[]{:S(2)}, u32[]{:S(2)}) collective-permute-start(bf16[6,64,128]{2,1,0:T(8,128)(2,1)S(1)} %bitcast.126), channel_id=1, source_target_pairs={{0,1},{3,2},{4,5},{7,6},{8,9},{11,10},{12,13},{15,14},{16,17},{19,... | collective-permute-start | bytes 294920 | tf_op jit(solution)/shard_map/ppermute | solution.py:348
  27.9 4.8 %collective-permute-start.6 = (bf16[6,256,128]{2,1,0:T(8,128)(2,1)}, bf16[6,256,128]{2,1,0:T(8,128)(2,1)}, u32[]{:S(2)}, u32[]{:S(2)}) collective-permute-start(bf16[6,256,128]{2,1,0:T(8,128)(2,1)} %get-tuple-element.38), channel_id=1, source_target_pairs={{0,1},{3,2},{4,5},{7,6},{8,9},{11,10},{12,13},{15,14},{16,17},{19,... | collective-permute-start | bytes 1179656 | tf_op jit(solution)/shard_map/ppermute | solution.py:354
  33.2 2.2 constant_dynamic-slice_fusion.4
  37.0 1.9 constant_dynamic-slice_fusion.3
  39.5 1.8 fusion.9
  48.4 20.4 %collective-permute-done.1 = bf16[1,2816,128]{2,1,0:T(8,128)(2,1)} collective-permute-done((bf16[1,2816,128]{2,1,0:T(8,128)(2,1)}, bf16[1,2816,128]{2,1,0:T(8,128)(2,1)}, u32[]{:S(2)}, u32[]{:S(2)}) %collective-permute-start.1) | collective-permute-done | bytes 720928 | tf_op jit(solution)/shard_map/ppermute | solution.py:284
  74.1 1.8 copy.52
  84.2 1.8 copy.62.refs_8_
  89.5 2.2 pad_maximum_fusion.10
  91.8 5.3 %collective-permute-start.8 = (bf16[256,1024]{1,0:T(8,128)(2,1)}, bf16[256,1024]{1,0:T(8,128)(2,1)}, u32[]{:S(2)}, u32[]{:S(2)}) collective-permute-start(bf16[256,1024]{1,0:T(8,128)(2,1)} %get-tuple-element.19), channel_id=1, source_target_pairs={{0,1},{3,2},{4,5},{7,6},{8,9},{11,10},{12,13},{15,14},{16,17},{19,... | collective-permute-start | bytes 1572872 | tf_op jit(solution)/shard_map/ppermute | solution.py:362
  97.2 8.6 %collective-permute-done.16 = bf16[96,1024]{1,0:T(8,128)(2,1)S(1)} collective-permute-done((bf16[96,1024]{1,0:T(8,128)(2,1)S(1)}, bf16[96,1024]{1,0:T(8,128)(2,1)S(1)}, u32[]{:S(2)}, u32[]{:S(2)}) %collective-permute-start.16) | collective-permute-done | bytes 196640 | tf_op jit(solution)/shard_map/ppermute | solution.py:439
  110.8 4.0 %project.1 = f32[512,768]{1,0:T(8,128)S(1)} custom-call(s32[2]{0:T(128)S(1)} %get-tuple-element.34.ids_ref, bf16[512,1024]{1,0:T(8,128)(2,1)S(1)} %copy-done, bf16[512,1024]{1,0:T(8,128)(2,1)S(1)} %collective-permute-done.5.refs_6_.refs_1_, bf16[6,4096,128]{2,1,0:T(8,128)(2,1)} %bitcast.100), custom_call_target="tpu_custom_call" | custom-call | flops 1000 | bytes 1000 | tf_op jit(solution)/shard_map/project/pallas_call | solution.py:156
  135.7 3.7 %reshape.123 = bf16[4,192,1024]{2,1,0:T(8,128)(2,1)} reshape(bf16[4,1536,128]{2,1,0:T(8,128)(2,1)} %fusion) | data formatting | bytes 3145728 | tf_op jit(solution)/shard_map/reshape | solution.py:397
  139.4 2.5 fusion.1
  141.9 6.7 %collective-permute-start.3 = (f32[512,192]{0,1:T(8,128)S(1)}, f32[512,192]{0,1:T(8,128)S(1)}, u32[]{:S(2)}, u32[]{:S(2)}) collective-permute-start(f32[512,192]{0,1:T(8,128)S(1)} %fusion.1), channel_id=1, source_target_pairs={{0,1},{3,2},{4,5},{7,6},{8,9},{11,10},{12,13},{15,14},{16,17},{19,... | collective-permute-start | bytes 1179656 | tf_op jit(solution)/shard_map/ppermute | solution.py:416
  148.6 7.3 %collective-permute-done.19 = bf16[1,2,4,4,16,1024]{5,4,3,2,1,0:T(8,128)(2,1)} collective-permute-done((bf16[1,2,4,4,16,1024]{5,4,3,2,1,0:T(8,128)(2,1)}, bf16[1,2,4,4,16,1024]{5,4,3,2,1,0:T(8,128)(2,1)}, u32[]{:S(2)}, u32[]{:S(2)}) %collective-permute-start.19) | collective-permute-done | bytes 1048608 | tf_op jit(solution)/shard_map/ppermute | solution.py:284
  170.3 12.5 %attend.3 = (bf16[512,512]{1,0:T(8,128)(2,1)}, bf16[512,128]{1,0:T(8,128)(2,1)}, bf16[512,128]{1,0:T(8,128)(2,1)}) custom-call(s32[4]{0:T(128)S(1)} %pad_add_fusion.2.ids_ref, s32[512,1]{1,0:T(8,128)S(1)} %copy-done.8, f32[512,128]{1,0:T(8,128)S(1)} %copy-done.5, f32[512,128]{1,0:T(8,128)S(1)} %copy-done.6, ...), custom_call_target="tpu_custom_call" | custom-call | flops 1000 | bytes 1000 | tf_op jit(solution)/shard_map/attend/pallas_call | solution.py:183
  185.7 5.3 %attend.4 = (bf16[256,512]{1,0:T(8,128)(2,1)S(1)}, bf16[256,128]{1,0:T(8,128)(2,1)S(1)}, bf16[256,128]{1,0:T(8,128)(2,1)S(1)}) custom-call(s32[2]{0:T(128)S(1)} %get-tuple-element.36.ids_ref, s32[256,1]{1,0:T(8,128)S(1)} %copy-done.14, f32[256,128]{1,0:T(8,128)S(1)} %copy-done.12, f32[256,128]{1,0:T(8,128)S(1)} %copy-done.11, ...), custom_call_target="tpu_custom_call" | custom-call | flops 1000 | bytes 1000 | tf_op jit(solution)/shard_map/attend/pallas_call | solution.py:183
  193.2 6.9 %attend.5 = (bf16[256,512]{1,0:T(8,128)(2,1)}, bf16[256,128]{1,0:T(8,128)(2,1)}, bf16[256,128]{1,0:T(8,128)(2,1)}) custom-call(s32[2]{0:T(128)S(1)} %get-tuple-element.36.ids_ref, s32[256,1]{1,0:T(8,128)S(1)} %copy-done.13, f32[256,128]{1,0:T(8,128)S(1)} %copy-done.10, f32[256,128]{1,0:T(8,128)S(1)} %copy-done.9, ...), custom_call_target="tpu_custom_call" | custom-call | flops 1000 | bytes 1000 | tf_op jit(solution)/shard_map/attend/pallas_call | solution.py:183
  201.7 13.5 %collective-permute-done.23.refs_0_ = bf16[256,512]{1,0:T(8,128)(2,1)S(1)} collective-permute-done((bf16[256,512]{1,0:T(8,128)(2,1)S(1)}, bf16[256,512]{1,0:T(8,128)(2,1)S(1)}, u32[]{:S(2)}, u32[]{:S(2)}) %collective-permute-start.23) | collective-permute-done | bytes 262176 | tf_op jit(solution)/shard_map/ppermute | solution.py:490
  221.8 2.4 broadcast_select_fusion.1
  224.2 2.4 pad_maximum_fusion
  226.6 5.1 %gather_fusion = bf16[4,2,4,4,16,1024]{5,4,3,2,1,0:T(8,128)(2,1)} fusion(bf16[4,2,4,4,16,1024]{5,4,3,2,1,0:T(8,128)(2,1)} %pad_maximum_fusion, s32[1024]{0:T(1024)} %pad_clamp_fusion), kind=kCustom, calls=%fused_computation | custom fusion | bytes 8388624 | tf_op jit(solution)/shard_map/gather | solution.py:448
  231.7 5.1 %copy.59 = bf16[4,4,2,4,16,1024]{5,4,3,2,1,0:T(8,128)(2,1)} copy(bf16[4,4,2,4,16,1024]{5,4,1,0,2,3:T(8,128)(2,1)} %bitcast.105) | data formatting | bytes 8388608 | tf_op jit(solution)/shard_map/transpose | solution.py:449
  237.7 5.6 %collective-permute-done.28.refs_6_ = bf16[256,512]{1,0:T(8,128)(2,1)} collective-permute-done((bf16[256,512]{1,0:T(8,128)(2,1)S(1)}, bf16[256,512]{1,0:T(8,128)(2,1)}, u32[]{:S(2)}, u32[]{:S(2)}) %collective-permute-start.28) | collective-permute-done | bytes 262176 | tf_op jit(solution)/shard_map/ppermute | solution.py:490
  243.3 3.9 %project_out.2 = (f32[512,1024]{1,0:T(8,128)S(1)}, f32[512,256]{1,0:T(8,128)S(1)}) custom-call(s32[3]{0:T(128)S(1)} %pad_add_fusion.4.ids_ref, bf16[256,512]{1,0:T(8,128)(2,1)S(1)} %collective-permute-done.23.refs_0_, bf16[256,512]{1,0:T(8,128)(2,1)S(1)} %copy-done.16, bf16[256,512]{1,0:T(8,128)(2,1)} %collective-permute-done.24.refs_2_, ...), custom_call_target="tpu_custom_call" | custom-call | flops 1000 | bytes 1000 | tf_op jit(solution)/shard_map/project_out/pallas_call | solution.py:257
  248.5 5.9 %collective-permute-done.12.refs_0_ = bf16[512,512]{1,0:T(8,128)(2,1)S(1)} collective-permute-done((bf16[512,512]{1,0:T(8,128)(2,1)}, bf16[512,512]{1,0:T(8,128)(2,1)S(1)}, u32[]{:S(2)}, u32[]{:S(2)}) %collective-permute-start.12) | collective-permute-done | bytes 524320 | tf_op jit(solution)/shard_map/ppermute | solution.py:490
  254.5 9.0 %collective-permute-done.14.refs_2_ = bf16[512,512]{1,0:T(8,128)(2,1)S(1)} collective-permute-done((bf16[512,512]{1,0:T(8,128)(2,1)}, bf16[512,512]{1,0:T(8,128)(2,1)S(1)}, u32[]{:S(2)}, u32[]{:S(2)}) %collective-permute-start.14) | collective-permute-done | bytes 524320 | tf_op jit(solution)/shard_map/ppermute | solution.py:490
  263.4 6.0 %project_out.3 = bf16[512,1024]{1,0:T(8,128)(2,1)} custom-call(s32[3]{0:T(128)S(1)} %pad_add_fusion.1.ids_ref, bf16[512,512]{1,0:T(8,128)(2,1)S(1)} %collective-permute-done.12.refs_0_, bf16[512,512]{1,0:T(8,128)(2,1)} %get-tuple-element.20.refs_1_, bf16[512,512]{1,0:T(8,128)(2,1)S(1)} %collective-permute-done.14.refs_2_, ...), custom_call_target="tpu_custom_call" | custom-call | flops 1000 | bytes 1000 | tf_op jit(solution)/shard_map/project_out/pallas_call | solution.py:257
  (255 shorter events, 83.7 us)
Async XLA Ops:
  6.5 159.9 %all-gather.5.cloned.1.call-start = ((), (), s32[]{:S(2)}) async-start(), calls=%async_computation | async-start | bytes 3538944 | tf_op jit(solution)/shard_map/all_gather | solution.py:355
  8.7 13.3 %collective-permute-start.11 = (bf16[6,256,128]{2,1,0:T(8,128)(2,1)S(1)}, bf16[6,256,128]{2,1,0:T(8,128)(2,1)S(1)}, u32[]{:S(2)}, u32[]{:S(2)}) collective-permute-start(bf16[6,256,128]{2,1,0:T(8,128)(2,1)S(1)} %get-tuple-element.37), channel_id=1, source_target_pairs={{0,1},{3,2},{4,5},{7,6},{8,9},{11,10},{12,13},{15,14},{16,17},{19,... | collective-permute-start | bytes 1179656 | tf_op jit(solution)/shard_map/ppermute | solution.py:354
  22.7 143.7 %all-gather.7.cloned.1.call-start = ((), (), s32[]{:S(2)}) async-start(), calls=%async_computation.1 | async-start | bytes 3538944 | tf_op jit(solution)/shard_map/all_gather | solution.py:355
  22.8 19.9 %collective-permute-start = (bf16[6,64,128]{2,1,0:T(8,128)(2,1)S(1)}, bf16[6,64,128]{2,1,0:T(8,128)(2,1)S(1)}, u32[]{:S(2)}, u32[]{:S(2)}) collective-permute-start(bf16[6,64,128]{2,1,0:T(8,128)(2,1)S(1)} %bitcast.126), channel_id=1, source_target_pairs={{0,1},{3,2},{4,5},{7,6},{8,9},{11,10},{12,13},{15,14},{16,17},{19,... | collective-permute-start | bytes 294920 | tf_op jit(solution)/shard_map/ppermute | solution.py:348
  27.2 60.2 %collective-permute-start.5 = (bf16[512,1024]{1,0:T(8,128)(2,1)S(1)}, bf16[512,1024]{1,0:T(8,128)(2,1)S(1)}, u32[]{:S(2)}, u32[]{:S(2)}) collective-permute-start(bf16[512,1024]{1,0:T(8,128)(2,1)S(1)} %copy-done), channel_id=1, source_target_pairs={{1,2},{2,1},{5,6},{6,5},{9,10},{10,9},{13,14},{14,13},{17,18},{18,... | collective-permute-start | bytes 3145736 | tf_op jit(solution)/shard_map/ppermute | solution.py:343
  27.9 19.1 %collective-permute-start.6 = (bf16[6,256,128]{2,1,0:T(8,128)(2,1)}, bf16[6,256,128]{2,1,0:T(8,128)(2,1)}, u32[]{:S(2)}, u32[]{:S(2)}) collective-permute-start(bf16[6,256,128]{2,1,0:T(8,128)(2,1)} %get-tuple-element.38), channel_id=1, source_target_pairs={{0,1},{3,2},{4,5},{7,6},{8,9},{11,10},{12,13},{15,14},{16,17},{19,... | collective-permute-start | bytes 1179656 | tf_op jit(solution)/shard_map/ppermute | solution.py:354
  43.7 25.2 %collective-permute-start.1 = (bf16[1,2816,128]{2,1,0:T(8,128)(2,1)}, bf16[1,2816,128]{2,1,0:T(8,128)(2,1)}, u32[]{:S(2)}, u32[]{:S(2)}) collective-permute-start(bf16[1,2816,128]{2,1,0:T(8,128)(2,1)} %maximum_bitcast_fusion.1), channel_id=1, source_target_pairs={{0,8},{4,12},{8,0},{12,4},{1,9},{5,13},{9,1},{13,5},{2,10},{6,14},... | collective-permute-start | bytes 2162696 | tf_op jit(solution)/shard_map/ppermute | solution.py:284
  45.3 28.1 %copy-start.61 = (pred[512,4]{0,1:T(4,128)(4,1)}, pred[512,4]{0,1:T(4,128)(4,1)S(1)}, u32[]{:S(2)}) copy-start(pred[512,4]{0,1:T(4,128)(4,1)S(1)} %get-tuple-element.75) | copy-start | bytes 6148
  47.1 44.7 %collective-permute-start.7 = (bf16[256,1024]{1,0:T(8,128)(2,1)}, bf16[256,1024]{1,0:T(8,128)(2,1)S(1)}, u32[]{:S(2)}, u32[]{:S(2)}) collective-permute-start(bf16[256,1024]{1,0:T(8,128)(2,1)} %get-tuple-element.18), channel_id=1, source_target_pairs={{0,1},{3,2},{4,5},{7,6},{8,9},{11,10},{12,13},{15,14},{16,17},{19,... | collective-permute-start | bytes 1572872 | tf_op jit(solution)/shard_map/ppermute | solution.py:362
  71.8 59.5 %collective-permute-start.2 = (bf16[2,2816,128]{2,1,0:T(8,128)(2,1)}, bf16[2,2816,128]{2,1,0:T(8,128)(2,1)}, u32[]{:S(2)}, u32[]{:S(2)}) collective-permute-start(bf16[2,2816,128]{2,1,0:T(8,128)(2,1)} %pad_maximum_fusion.2), channel_id=1, source_target_pairs={{0,4},{4,0},{8,12},{12,8},{1,5},{5,1},{9,13},{13,9},{2,6},{6,2},{1... | collective-permute-start | bytes 4325384 | tf_op jit(solution)/shard_map/ppermute | solution.py:284
  87.4 9.7 %collective-permute-start.17 = (bf16[96,1024]{1,0:T(8,128)(2,1)S(1)}, bf16[96,1024]{1,0:T(8,128)(2,1)S(1)}, u32[]{:S(2)}, u32[]{:S(2)}) collective-permute-start(bf16[96,1024]{1,0:T(8,128)(2,1)S(1)} %get-tuple-element.23), channel_id=1, source_target_pairs={{0,3},{1,0},{2,1},{3,2},{4,7},{5,4},{6,5},{7,6},{8,11},{9,8},{10,9... | collective-permute-start | bytes 589832 | tf_op jit(solution)/shard_map/ppermute | solution.py:439
  88.6 17.1 %collective-permute-start.16 = (bf16[96,1024]{1,0:T(8,128)(2,1)S(1)}, bf16[96,1024]{1,0:T(8,128)(2,1)S(1)}, u32[]{:S(2)}, u32[]{:S(2)}) collective-permute-start(bf16[96,1024]{1,0:T(8,128)(2,1)S(1)} %get-tuple-element.22), channel_id=1, source_target_pairs={{0,2},{1,3},{2,0},{3,1},{4,6},{5,7},{6,4},{7,5},{8,10},{9,11},{10,... | collective-permute-start | bytes 589832 | tf_op jit(solution)/shard_map/ppermute | solution.py:439
  88.6 17.1 %collective-permute-start.15 = (bf16[96,1024]{1,0:T(8,128)(2,1)S(1)}, bf16[96,1024]{1,0:T(8,128)(2,1)S(1)}, u32[]{:S(2)}, u32[]{:S(2)}) collective-permute-start(bf16[96,1024]{1,0:T(8,128)(2,1)S(1)} %get-tuple-element.21), channel_id=1, source_target_pairs={{0,1},{1,2},{2,3},{3,0},{4,5},{5,6},{6,7},{7,4},{8,9},{9,10},{10,1... | collective-permute-start | bytes 589832 | tf_op jit(solution)/shard_map/ppermute | solution.py:439
  91.8 35.2 %collective-permute-start.8 = (bf16[256,1024]{1,0:T(8,128)(2,1)}, bf16[256,1024]{1,0:T(8,128)(2,1)}, u32[]{:S(2)}, u32[]{:S(2)}) collective-permute-start(bf16[256,1024]{1,0:T(8,128)(2,1)} %get-tuple-element.19), channel_id=1, source_target_pairs={{0,1},{3,2},{4,5},{7,6},{8,9},{11,10},{12,13},{15,14},{16,17},{19,... | collective-permute-start | bytes 1572872 | tf_op jit(solution)/shard_map/ppermute | solution.py:362
  106.8 21.7 %collective-permute-start.18 = (bf16[1,4,4,16,1024]{4,3,2,1,0:T(8,128)(2,1)}, bf16[1,4,4,16,1024]{4,3,2,1,0:T(8,128)(2,1)}, u32[]{:S(2)}, u32[]{:S(2)}) collective-permute-start(bf16[1,4,4,16,1024]{4,3,2,1,0:T(8,128)(2,1)} %maximum_bitcast_fusion.2), channel_id=1, source_target_pairs={{0,16},{16,0},{1,17},{17,1},{2,18},{18,2},{3,19},{19,3},{4,20},{20... | collective-permute-start | bytes 1572872 | tf_op jit(solution)/shard_map/ppermute | solution.py:284
  109.3 57.1 %collective-permute-start.9 = (bf16[256,1024]{1,0:T(8,128)(2,1)S(1)}, bf16[256,1024]{1,0:T(8,128)(2,1)}, u32[]{:S(2)}, u32[]{:S(2)}) collective-permute-start(bf16[256,1024]{1,0:T(8,128)(2,1)S(1)} %collective-permute-done.7.refs_7_.refs_5_), channel_id=1, source_target_pairs={{1,2},{2,1},{5,6},{6,5},{9,10},{10,9},{13,14},{14,13},{17,18},{18,... | collective-permute-start | bytes 1572872 | tf_op jit(solution)/shard_map/ppermute | solution.py:365
  125.5 33.5 %collective-permute-start.21 = (bf16[1,4,64,512]{3,2,0,1:T(8,128)(2,1)}, bf16[1,4,64,512]{3,2,0,1:T(8,128)(2,1)}, u32[]{:S(2)}, u32[]{:S(2)}) collective-permute-start(bf16[1,4,64,512]{3,2,0,1:T(8,128)(2,1)} %maximum_bitcast_fusion.3), channel_id=1, source_target_pairs={{0,8},{4,12},{8,0},{12,4},{1,9},{5,13},{9,1},{13,5},{2,10},{6,14},... | collective-permute-start | bytes 786440 | tf_op jit(solution)/shard_map/ppermute | solution.py:284
  127.0 39.4 %collective-permute-start.10 = (bf16[256,1024]{1,0:T(8,128)(2,1)}, bf16[256,1024]{1,0:T(8,128)(2,1)}, u32[]{:S(2)}, u32[]{:S(2)}) collective-permute-start(bf16[256,1024]{1,0:T(8,128)(2,1)} %collective-permute-done.8.refs_8_.refs_5_), channel_id=1, source_target_pairs={{1,2},{2,1},{5,6},{6,5},{9,10},{10,9},{13,14},{14,13},{17,18},{18,... | collective-permute-start | bytes 1572872 | tf_op jit(solution)/shard_map/ppermute | solution.py:365
  130.7 25.2 %collective-permute-start.19 = (bf16[1,2,4,4,16,1024]{5,4,3,2,1,0:T(8,128)(2,1)}, bf16[1,2,4,4,16,1024]{5,4,3,2,1,0:T(8,128)(2,1)}, u32[]{:S(2)}, u32[]{:S(2)}) collective-permute-start(bf16[1,2,4,4,16,1024]{5,4,3,2,1,0:T(8,128)(2,1)} %maximum_bitcast_fusion), channel_id=1, source_target_pairs={{0,8},{4,12},{8,0},{12,4},{1,9},{5,13},{9,1},{13,5},{2,10},{6,14},... | collective-permute-start | bytes 3145736 | tf_op jit(solution)/shard_map/ppermute | solution.py:284
  141.9 20.1 %collective-permute-start.3 = (f32[512,192]{0,1:T(8,128)S(1)}, f32[512,192]{0,1:T(8,128)S(1)}, u32[]{:S(2)}, u32[]{:S(2)}) collective-permute-start(f32[512,192]{0,1:T(8,128)S(1)} %fusion.1), channel_id=1, source_target_pairs={{0,1},{3,2},{4,5},{7,6},{8,9},{11,10},{12,13},{15,14},{16,17},{19,... | collective-permute-start | bytes 1179656 | tf_op jit(solution)/shard_map/ppermute | solution.py:416
  159.0 60.2 %collective-permute-start.20 = (bf16[2,2,4,4,16,1024]{5,4,3,2,1,0:T(8,128)(2,1)}, bf16[2,2,4,4,16,1024]{5,4,3,2,1,0:T(8,128)(2,1)}, u32[]{:S(2)}, u32[]{:S(2)}) collective-permute-start(bf16[2,2,4,4,16,1024]{5,4,3,2,1,0:T(8,128)(2,1)} %pad_maximum_fusion.1), channel_id=1, source_target_pairs={{0,4},{4,0},{8,12},{12,8},{1,5},{5,1},{9,13},{13,9},{2,6},{6,2},{1... | collective-permute-start | bytes 6291464 | tf_op jit(solution)/shard_map/ppermute | solution.py:284
  161.7 22.7 %collective-permute-start.22 = (bf16[2,4,64,512]{3,2,0,1:T(8,128)(2,1)}, bf16[2,4,64,512]{3,2,0,1:T(8,128)(2,1)}, u32[]{:S(2)}, u32[]{:S(2)}) collective-permute-start(bf16[2,4,64,512]{3,2,0,1:T(8,128)(2,1)} %pad_maximum_fusion.6), channel_id=1, source_target_pairs={{0,4},{4,0},{8,12},{12,8},{1,5},{5,1},{9,13},{13,9},{2,6},{6,2},{1... | collective-permute-start | bytes 1572872 | tf_op jit(solution)/shard_map/ppermute | solution.py:284
  162.1 1.7 collective-permute-start.4
  182.8 37.6 %collective-permute-start.13 = (bf16[512,512]{1,0:T(8,128)(2,1)}, bf16[512,512]{1,0:T(8,128)(2,1)}, u32[]{:S(2)}, u32[]{:S(2)}) collective-permute-start(bf16[512,512]{1,0:T(8,128)(2,1)} %get-tuple-element.20.refs_1_), channel_id=1, source_target_pairs={{1,2},{2,1},{5,6},{6,5},{9,10},{10,9},{13,14},{14,13},{17,18},{18,... | collective-permute-start | bytes 1572872 | tf_op jit(solution)/shard_map/ppermute | solution.py:488
  191.0 24.2 %collective-permute-start.23 = (bf16[256,512]{1,0:T(8,128)(2,1)S(1)}, bf16[256,512]{1,0:T(8,128)(2,1)S(1)}, u32[]{:S(2)}, u32[]{:S(2)}) collective-permute-start(bf16[256,512]{1,0:T(8,128)(2,1)S(1)} %get-tuple-element.25.refs_1_), channel_id=1, source_target_pairs={{1,0},{2,3},{5,4},{6,7},{9,8},{10,11},{13,12},{14,15},{17,16},{18,... | collective-permute-start | bytes 786440 | tf_op jit(solution)/shard_map/ppermute | solution.py:490
  192.3 24.2 %collective-permute-start.25 = (bf16[256,512]{1,0:T(8,128)(2,1)S(1)}, bf16[256,512]{1,0:T(8,128)(2,1)S(1)}, u32[]{:S(2)}, u32[]{:S(2)}) collective-permute-start(bf16[256,512]{1,0:T(8,128)(2,1)S(1)} %get-tuple-element.25.refs_1_), channel_id=1, source_target_pairs={{1,2},{2,1},{5,6},{6,5},{9,10},{10,9},{13,14},{14,13},{17,18},{18,... | collective-permute-start | bytes 786440 | tf_op jit(solution)/shard_map/ppermute | solution.py:488
  200.1 17.7 %collective-permute-start.27 = (bf16[256,512]{1,0:T(8,128)(2,1)}, bf16[256,512]{1,0:T(8,128)(2,1)S(1)}, u32[]{:S(2)}, u32[]{:S(2)}) collective-permute-start(bf16[256,512]{1,0:T(8,128)(2,1)} %get-tuple-element.28.refs_3_), channel_id=1, source_target_pairs={{1,2},{2,1},{5,6},{6,5},{9,10},{10,9},{13,14},{14,13},{17,18},{18,... | collective-permute-start | bytes 786440 | tf_op jit(solution)/shard_map/ppermute | solution.py:488
  215.2 21.5 %collective-permute-start.24 = (bf16[256,512]{1,0:T(8,128)(2,1)}, bf16[256,512]{1,0:T(8,128)(2,1)}, u32[]{:S(2)}, u32[]{:S(2)}) collective-permute-start(bf16[256,512]{1,0:T(8,128)(2,1)} %get-tuple-element.28.refs_3_), channel_id=1, source_target_pairs={{1,0},{2,3},{5,4},{6,7},{9,8},{10,11},{13,12},{14,15},{17,16},{18,... | collective-permute-start | bytes 786440 | tf_op jit(solution)/shard_map/ppermute | solution.py:490
  216.5 21.2 %collective-permute-start.26 = (bf16[256,512]{1,0:T(8,128)(2,1)S(1)}, bf16[256,512]{1,0:T(8,128)(2,1)}, u32[]{:S(2)}, u32[]{:S(2)}) collective-permute-start(bf16[256,512]{1,0:T(8,128)(2,1)S(1)} %collective-permute-done.25.refs_5_), channel_id=1, source_target_pairs={{1,0},{2,3},{5,4},{6,7},{9,8},{10,11},{13,12},{14,15},{17,16},{18,... | collective-permute-start | bytes 786440 | tf_op jit(solution)/shard_map/ppermute | solution.py:490
  217.8 25.5 %collective-permute-start.28 = (bf16[256,512]{1,0:T(8,128)(2,1)S(1)}, bf16[256,512]{1,0:T(8,128)(2,1)}, u32[]{:S(2)}, u32[]{:S(2)}) collective-permute-start(bf16[256,512]{1,0:T(8,128)(2,1)S(1)} %collective-permute-done.27.refs_7_), channel_id=1, source_target_pairs={{1,0},{2,3},{5,4},{6,7},{9,8},{10,11},{13,12},{14,15},{17,16},{18,... | collective-permute-start | bytes 786440 | tf_op jit(solution)/shard_map/ppermute | solution.py:490
  219.2 35.3 %collective-permute-start.12 = (bf16[512,512]{1,0:T(8,128)(2,1)}, bf16[512,512]{1,0:T(8,128)(2,1)S(1)}, u32[]{:S(2)}, u32[]{:S(2)}) collective-permute-start(bf16[512,512]{1,0:T(8,128)(2,1)} %get-tuple-element.20.refs_1_), channel_id=1, source_target_pairs={{1,0},{2,3},{5,4},{6,7},{9,8},{10,11},{13,12},{14,15},{17,16},{18,... | collective-permute-start | bytes 1572872 | tf_op jit(solution)/shard_map/ppermute | solution.py:490
  220.5 43.0 %collective-permute-start.14 = (bf16[512,512]{1,0:T(8,128)(2,1)}, bf16[512,512]{1,0:T(8,128)(2,1)S(1)}, u32[]{:S(2)}, u32[]{:S(2)}) collective-permute-start(bf16[512,512]{1,0:T(8,128)(2,1)} %collective-permute-done.13.refs_3_), channel_id=1, source_target_pairs={{1,0},{2,3},{5,4},{6,7},{9,8},{10,11},{13,12},{14,15},{17,16},{18,... | collective-permute-start | bytes 1572872 | tf_op jit(solution)/shard_map/ppermute | solution.py:490
  (67 other events, 579.4 us)
Sparse Core Ops, SparseCore 0:
  22.8 41.5 all-gather.4
  66.3 32.5 all-gather.6

commit v3 on v2

v3 whole, which is shorter than its diff:
```python
import functools
import math

import jax
import jax.numpy as jnp
from jax import lax
from jax.experimental import pallas as pl
from jax.experimental.pallas import tpu as pltpu
from jax.sharding import PartitionSpec as P

CHUNKS = 2
VMEM_BYTES = 48 * 1024 * 1024
PLANE = ("groups", "dp")


def after(value, *earlier):
    return lax.optimization_barrier((value,) + earlier)[0]


def wide_slots(w_refs, pair):
    if len(w_refs[0].shape) == 3:
        parts = [w_ref[...] for w_ref in w_refs]
    else:
        parts = [
            w_ref[piece] for piece in range(w_refs[0].shape[0]) for w_ref in w_refs
        ]
    wide = [jnp.concatenate([part[2 * pair], part[2 * pair + 1]], axis=1) for part in parts]
    return wide[0] if len(wide) == 1 else jnp.concatenate(wide, axis=0)


def accumulate(acc_ref, token_refs, w_refs, first):
    slots, _, head_size = w_refs[0].shape[-3:]
    for pair in range(slots // 2):
        columns = slice(2 * pair * head_size, (2 * pair + 2) * head_size)
        weight = wide_slots(w_refs, pair)
        row = 0
        for token_ref in token_refs:
            rows = slice(row, row + token_ref.shape[0])
            row = rows.stop
            total = jnp.dot(token_ref[...], weight, preferred_element_type=jnp.float32)
            if first is None:
                acc_ref[rows, columns] = total
            else:
                acc_ref[rows, columns] = first[rows, columns] + total


def split_refs(refs, layout):
    groups, at = [], 0
    for count in layout:
        groups.append(refs[at : at + count])
        at += count
    return groups, refs[at:]


def project_kernel(layout, weights, ids_ref, *refs):
    tokens, rest = split_refs(refs, layout)
    w_refs, acc_ref = rest[:weights], rest[weights]
    step = pl.program_id(0)
    for number, token_refs in enumerate(tokens):
        pl.when(step == number)(
            functools.partial(
                accumulate, acc_ref, token_refs, w_refs, acc_ref if number else None
            )
        )


def attend_kernel(layout, weights, sums, started, which, ids_ref, table_ref, turn_ref, up_ref, *refs):
    sum_refs, refs = refs[:sums], refs[sums:]
    tokens, rest = split_refs(refs, layout)
    w_refs, rest = rest[:weights], rest[weights:]
    begun, prior, rest = rest[:started[0]], rest[started[0] : started[0] + started[1]], rest[sum(started) :]
    attended_ref, keys_ref, values_ref, acc_ref = rest
    first_row = prior[0].shape[0] if prior else 0
    slots, _, head_size = w_refs[0].shape[-3:]
    rank = up_ref.shape[3]
    count = ids_ref.shape[0] - len(layout)
    step = pl.program_id(0)
    rows = acc_ref.shape[0]
    block = min(rows, 256)
    queries = slots - 2

    for number, token_refs in enumerate(tokens):
        first = acc_ref if number else (begun[0] if begun else None)
        pl.when(step == number)(
            functools.partial(accumulate, acc_ref, token_refs, w_refs, first)
        )

    @pl.when(step == len(layout) - 1)
    def _():
        ups = [
            jnp.concatenate(
                [up_ref[ids_ref[len(layout) + j], which, index] for j in range(count)], axis=0
            )
            for index in range(slots)
        ]
        for row in range(0, rows, block):
            at = slice(row, row + block)
            shrink = sum(sum_ref[at, :] for sum_ref in sum_refs).astype(jnp.bfloat16)
            lane = lax.broadcasted_iota(jnp.int32, (block, count * rank), 1)
            kept = (lane >= table_ref[at, 1:2]) & (lane < table_ref[at, 1:2] + rank)
            lows = []
            for part in range(3):
                piece = shrink[:, part * rank : (part + 1) * rank].astype(jnp.float32)
                piece = jnp.concatenate([piece] * count, axis=1)
                lows.append(jnp.where(kept, piece, 0.0).astype(jnp.bfloat16))

            def slot(index):
                low = lows[0 if index < queries else index - queries + 1]
                extra = jnp.dot(low, ups[index], preferred_element_type=jnp.float32)
                return acc_ref[at, index * head_size : (index + 1) * head_size] + extra

            def rotated(index):
                value = slot(index)
                turned = pltpu.roll(value, head_size // 2, 1)
                cos, sin = turn_ref[at, :head_size], turn_ref[at, head_size:]
                return (value * cos + turned * sin).astype(jnp.bfloat16)

            keys_ref[at, :] = rotated(queries)
            values_ref[at, :] = slot(queries + 1).astype(jnp.bfloat16)
            keys, values = keys_ref[: row + block], values_ref[: row + block]
            if prior:
                keys = jnp.concatenate([prior[0][...], keys], axis=0)
                values = jnp.concatenate([prior[1][...], values], axis=0)
            key_rows = keys.shape[0]
            key_at = lax.broadcasted_iota(jnp.int32, (block, key_rows), 1)
            row_at = lax.broadcasted_iota(jnp.int32, (block, key_rows), 0) + (first_row + row)
            allowed = (key_at >= table_ref[at, 0:1]) & (key_at <= row_at)
            for index in range(queries):
                scores = lax.dot_general(
                    rotated(index), keys, (((1,), (1,)), ((), ())),
                    preferred_element_type=jnp.float32,
                )
                scores = jnp.where(allowed, scores * (1.0 / math.sqrt(head_size)), -1e30)
                weights_exp = jnp.exp(scores - jnp.max(scores, axis=1, keepdims=True))
                scale = 1.0 / jnp.sum(weights_exp, axis=1, keepdims=True)
                attended = jnp.dot(
                    (weights_exp * scale).astype(jnp.bfloat16), values,
                    preferred_element_type=jnp.float32,
                )
                attended_ref[at, index * head_size : (index + 1) * head_size] = (
                    attended.astype(jnp.bfloat16)
                )


def weight_specs(weights, depth):
    if len(weights[0].shape) == 3:
        slots, _, head_size = weights[0].shape
        return [pl.BlockSpec((slots, depth, head_size), lambda step, ids: (0, ids[step], 0))]
    pieces = depth // sum(weight.shape[2] for weight in weights)
    return [
        pl.BlockSpec((pieces,) + weight.shape[1:], lambda step, ids: (ids[step], 0, 0, 0))
        for weight in weights
    ]


def fixed(array):
    shape = array.shape
    return pl.BlockSpec(shape, lambda step, ids: (0,) * len(shape))


PARAMS = pltpu.CompilerParams(vmem_limit_bytes=VMEM_BYTES)
COST = pl.CostEstimate(flops=1000, bytes_accessed=1000, transcendentals=0)


def call(kernel, name, ids, grid, specs, arrays, out, scratch=()):
    return pl.pallas_call(
        kernel,
        out_shape=out,
        grid_spec=pltpu.PrefetchScalarGridSpec(
            num_scalar_prefetch=1,
            grid=(grid,),
            in_specs=[fixed(array) if spec is None else spec for spec, array in zip(specs, arrays)],
            out_specs=[fixed(item) for item in out] if isinstance(out, tuple) else fixed(out),
            scratch_shapes=list(scratch),
        ),
        compiler_params=PARAMS,
        cost_estimate=COST,
        name=name,
    )(ids, *arrays)


def project(ids, tokens, weights):
    depth = tokens[0][0].shape[1]
    rows = sum(part.shape[0] for part in tokens[0])
    slots, _, head_size = weights[0].shape[-3:]
    parts = [part for item in tokens for part in item]
    return call(
        functools.partial(project_kernel, [len(item) for item in tokens], len(weights)),
        "project",
        ids,
        len(tokens),
        [None] * len(parts) + weight_specs(weights, depth),
        parts + weights,
        jax.ShapeDtypeStruct((rows, slots * head_size), jnp.float32),
    )


def attend(ids, adapters, row, table, turn, up, which, sums, tokens, weights, begun, prior):
    depth = tokens[0][0].shape[1]
    rows = sum(part.shape[0] for part in tokens[0])
    slots, _, head_size = weights[0].shape[-3:]
    out = (
        jax.ShapeDtypeStruct((rows, (slots - 2) * head_size), jnp.bfloat16),
        jax.ShapeDtypeStruct((rows, head_size), jnp.bfloat16),
        jax.ShapeDtypeStruct((rows, head_size), jnp.bfloat16),
    )
    parts = [part for item in tokens for part in item]

    def rows_of(array):
        return pl.BlockSpec((rows, array.shape[1]), lambda step, ids: (row // rows, 0))

    tables = [table, turn]
    started = (len(begun), len(prior))
    arrays = tables + [up] + sums + parts + weights + begun + list(prior)
    specs = (
        [rows_of(array) for array in tables]
        + [None]
        + [rows_of(array) for array in sums]
        + [None] * len(parts)
        + weight_specs(weights, depth)
        + [rows_of(array) for array in begun]
        + [None] * len(prior)
    )
    return call(
        functools.partial(
            attend_kernel, [len(item) for item in tokens], len(weights), len(sums), started, which
        ),
        "attend",
        jnp.concatenate([ids, adapters]),
        len(tokens),
        specs,
        arrays,
        out,
        [pltpu.VMEM((rows, slots * head_size), jnp.float32)],
    )


def shrink_kernel(ids_ref, table_ref, token_ref, down_ref, out_ref):
    step = pl.program_id(0)
    part = lax.dot_general(
        token_ref[...], down_ref[0], (((1,), (1,)), ((), ())), preferred_element_type=jnp.float32
    )
    rank = part.shape[1] // 3
    part = jnp.where(table_ref[:, 1:2] == step * rank, part, 0.0)

    @pl.when(step == 0)
    def _():
        out_ref[...] = part

    @pl.when(step > 0)
    def _():
        out_ref[...] += part


def shrink_partial(adapters, table, tokens, down):
    _, width, depth = down.shape
    return call(
        shrink_kernel,
        "shrink",
        adapters,
        adapters.shape[0],
        [None, None, pl.BlockSpec((1, width, depth), lambda step, ids: (ids[step], 0, 0))],
        [table, tokens, down],
        jax.ShapeDtypeStruct((tokens.shape[0], width), jnp.float32),
    )


def output_kernel(
    groups, parts, begun, last, dp_size, group_size, planes, count, ids_ref, *refs
):
    attended_refs, rest = refs[: groups * parts * 2], refs[groups * parts * 2 :]
    own_ref, half_refs, rest = rest[0], rest[1:3], rest[3:]
    begun_refs, rest = rest[: 2 * begun], rest[2 * begun :]
    if last:
        table_ref, up_ref, out_ref, acc_ref, low_ref, w_ref, down_ref = rest
    else:
        acc_ref, low_ref, w_ref, down_ref = rest
    step = pl.program_id(0)
    turn = ids_ref[step]
    at_worker, at_group = groups, groups + 1
    at_dp = groups + 2
    at_adapter = at_dp + dp_size
    at_pool = at_adapter + count
    features, columns = own_ref.shape
    share = features // (dp_size * group_size)
    rank = down_ref.shape[0] // count
    lot = (planes - 1) * share
    split = columns // features
    down_share = rank // split
    half_count = dp_size // 2

    def blocks(index, start, size):
        start = pl.multiple_of(start, 16)
        near = half_refs[0][jnp.minimum(index, half_count - 1), pl.ds(start, size), :]
        far = half_refs[1][jnp.maximum(index - half_count, 0), pl.ds(start, size), :]
        return jnp.where(index < half_count, near, far)

    @pl.when(turn == 0)
    def _():
        w_ref[...] = own_ref[...]

    @pl.when(turn > 0)
    def _():
        for group in range(group_size):
            base = (ids_ref[at_group] ^ group) * lot + (turn - 1) * share
            for place in range(dp_size):
                row = (group * dp_size + place) * share
                w_ref[row : row + share, :] = blocks(ids_ref[at_dp + place], base, share)

    for number in range(count):
        block = blocks(
            ids_ref[at_adapter + number], group_size * lot + turn * down_share, down_share
        )
        for piece in range(split):
            row = number * rank + piece * down_share
            down_ref[row : row + down_share, :] = block[
                :, piece * features : (piece + 1) * features
            ]

    def accumulate_group(number, side):
        row = 0
        for part in range(parts):
            attended = attended_refs[(number * parts + part) * 2 + side][...]
            at = slice(row, row + attended.shape[0])
            row = at.stop
            total = jnp.dot(attended, w_ref[...], preferred_element_type=jnp.float32)
            low = lax.dot_general(
                attended, down_ref[...], (((1,), (1,)), ((), ())),
                preferred_element_type=jnp.float32,
            )
            if number:
                total, low = acc_ref[at, :] + total, low_ref[at, :] + low
            elif begun:
                total, low = begun_refs[0][at, :] + total, begun_refs[1][at, :] + low
            acc_ref[at, :] = total
            low_ref[at, :] = low

    for number in range(groups):
        for side in range(2):
            pl.when((step == number) & (ids_ref[at_worker] == side))(
                functools.partial(accumulate_group, number, side)
            )

    if last:
        @pl.when(step == groups - 1)
        def _():
            low = low_ref[...].astype(jnp.bfloat16).astype(jnp.float32)
            lane = lax.broadcasted_iota(jnp.int32, low.shape, 1)
            kept = (lane >= table_ref[:, 1:2]) & (lane < table_ref[:, 1:2] + rank)
            low = jnp.where(kept, low, 0.0).astype(jnp.bfloat16)
            up = jnp.concatenate([up_ref[ids_ref[at_pool + j]] for j in range(count)], axis=0)
            extra = jnp.dot(low, up, preferred_element_type=jnp.float32)
            out_ref[...] = (acc_ref[...] + extra).astype(jnp.bfloat16)


def project_out(ids, attended, weights, sizes, begun, final):
    dp_size, group_size, planes, count, rank = sizes
    groups, parts = len(attended), len(attended[0])
    rows = sum(part[0].shape[0] for part in attended[0])
    features, columns = weights[0].shape
    flat = [array for group in attended for part in group for array in part]
    sums = (
        jax.ShapeDtypeStruct((rows, columns), jnp.float32),
        jax.ShapeDtypeStruct((rows, count * rank), jnp.float32),
    )
    arrays = flat + weights + begun + final
    scratch = [
        pltpu.VMEM((features, columns), jnp.bfloat16),
        pltpu.VMEM((count * rank, features), jnp.bfloat16),
    ]
    if final:
        scratch = [pltpu.VMEM(item.shape, jnp.float32) for item in sums] + scratch
    return call(
        functools.partial(
            output_kernel, groups, parts, len(begun) // 2, bool(final), dp_size, group_size,
            planes, count,
        ),
        "project_out",
        ids,
        groups,
        [None] * len(arrays),
        arrays,
        jax.ShapeDtypeStruct((rows, columns), jnp.bfloat16) if final else sums,
        scratch,
    )


def doubled(value, axis, size):
    distance = size // 2
    moved = lax.ppermute(value, axis, [(i, i ^ distance) for i in range(size)])
    while distance > 1:
        distance //= 2
        value = jnp.concatenate([value, moved], axis=0)
        moved = lax.ppermute(value, axis, [(i, i ^ distance) for i in range(size)])
    return value, moved


def block_of(relative, size):
    block, bit, distance = 0, 1, size // 2
    while distance:
        block = block + jnp.where(relative & distance, bit, 0)
        bit, distance = bit * 2, distance // 2
    return block


def local(
    dp_size,
    group_size,
    planes,
    tokens,
    query_key_value_weight,
    output_weight,
    adapter_down_maps,
    adapter_up_maps,
    output_down_maps,
    output_up_maps,
    request_adapter,
    lengths,
):
    token_rows, depth = tokens.shape
    _, slots, head_size = query_key_value_weight.shape
    queries = slots - 2
    rank = adapter_up_maps.shape[1]
    features = queries * head_size
    columns = output_weight.shape[2] // planes
    pairs = planes // 2
    plane_size = dp_size * group_size

    def worker(pair):
        return 2 * pair + 1 - pair % 2

    def outer(pair):
        return 2 * pair + pair % 2

    to_worker = [(outer(p), worker(p)) for p in range(pairs)]
    from_worker = [(worker(p), outer(p)) for p in range(pairs)]
    ring = [(worker(p), worker((p + 1) % pairs)) for p in range(pairs)]
    here = lax.axis_index("tensor")
    pair = here // 2
    is_worker = here == worker(pair)
    sources = [(pair - step + pairs) % pairs for step in range(pairs)]
    worker_ids = jnp.stack([worker(source) for source in sources]).astype(jnp.int32)
    outer_ids = jnp.stack([outer(source) for source in sources]).astype(jnp.int32)
    dp_here, group_here = lax.axis_index("dp"), lax.axis_index("groups")
    place = group_here * dp_size + dp_here

    own_tokens = [tokens]
    for _ in range(pairs - 1):
        own_tokens.append(lax.ppermute(own_tokens[-1], "tensor", ring))

    weight = jnp.transpose(query_key_value_weight, (1, 0, 2))
    share = weight.shape[1] // plane_size
    piece = lax.dynamic_slice_in_dim(weight, place * share, share, axis=1)
    piece = lax.ppermute(piece, "tensor", to_worker)
    outer_weight = lax.all_gather(piece, PLANE, axis=0)

    chunk_rows = token_rows // CHUNKS
    outer_tokens = []
    previous = piece
    for chunk in range(CHUNKS):
        part = after(tokens[chunk * chunk_rows : (chunk + 1) * chunk_rows], previous)
        previous = lax.ppermute(part, "tensor", to_worker)
        moving = [previous]
        for _ in range(pairs - 1):
            moving.append(lax.ppermute(moving[-1], "tensor", ring))
        outer_tokens.append(moving)

    down_all = lax.all_gather(adapter_down_maps, "dp", axis=0, tiled=True)
    up_own = jnp.transpose(adapter_up_maps[0], (1, 0, 2))
    up_pair = jnp.stack([up_own, lax.ppermute(up_own, "tensor", to_worker)])
    up_all = lax.all_gather(up_pair, "dp", axis=0)
    out_up_all = lax.all_gather(output_up_maps, "dp", axis=0, tiled=True)

    requests = request_adapter.shape[1]
    request_ends = jnp.cumsum(lengths[0])
    request_starts = request_ends - lengths[0]
    at = jnp.arange(token_rows, dtype=jnp.int32)
    member = (at[:, None] >= request_starts[None, :]) & (at[:, None] < request_ends[None, :])
    if dp_size <= requests:
        count, adapters, label = dp_size, jnp.arange(dp_size), request_adapter[0]
    else:
        count, adapters, label = requests, request_adapter[0], jnp.arange(requests)
    adapters = adapters.astype(jnp.int32)
    wanted = jnp.stack([request_starts, label * rank], axis=0)
    table = jnp.sum(jnp.where(member[:, None, :], wanted[None], 0), axis=2).astype(jnp.int32)
    position = at - table[:, 0]
    half = head_size // 2
    inv_freq = 10000.0 ** (-2.0 * jnp.arange(half, dtype=jnp.float32) / head_size)
    angles = position.astype(jnp.float32)[:, None] * inv_freq[None, :]
    cosine, sine = jnp.cos(angles), jnp.sin(angles)
    turn = jnp.concatenate([cosine, cosine, -sine, sine], axis=1)

    shrink = shrink_partial(adapters, table, tokens, down_all)
    shrink = shrink + lax.ppermute(shrink, "tensor", to_worker)
    sums = [shrink]
    for _ in range(pairs - 1):
        sums.append(lax.ppermute(sums[-1], "tensor", ring))

    out_share = features // plane_size
    first = place * out_share
    piece = lax.dynamic_slice(
        output_weight, (first % head_size, first // head_size, 0),
        (out_share, 1, output_weight.shape[2]),
    )[:, 0]
    own_weight = jnp.transpose(
        lax.dynamic_slice_in_dim(output_weight, here * columns, columns, axis=2), (1, 0, 2)
    ).reshape(features, columns)
    out_down = output_down_maps[0].reshape(rank, features)
    split = columns // features
    out_down = jnp.concatenate(jnp.split(out_down, split, axis=0), axis=1)
    received = []
    for turn_by in range(1, planes):
        send = lax.dynamic_slice_in_dim(
            piece, (here + turn_by) % planes * columns, columns, axis=1
        )
        send = jnp.concatenate([send, out_down], axis=0)
        received.append(
            lax.ppermute(
                after(send, own_tokens[-1]), "tensor",
                [(i, (i + turn_by) % planes) for i in range(planes)],
            )
        )
    lot = jnp.concatenate([item[:out_share] for item in received], axis=0)
    lots = jnp.concatenate(doubled(lot, "groups", group_size), axis=0)
    lots = jnp.concatenate(
        [lots, out_down] + [item[out_share:] for item in received], axis=0
    )
    halves = list(doubled(lots[None], "dp", dp_size))

    begun = project(worker_ids, [(array,) for array in own_tokens], [weight])
    own_parts, prior = [], ()
    for chunk in range(CHUNKS):
        attended, keys, values = attend(
            outer_ids, adapters, chunk * chunk_rows, table, turn, up_all, 0, sums,
            [(array,) for array in outer_tokens[chunk]], [weight], [begun], prior,
        )
        prior = (keys, values)
        own_parts.append(attended)
    outer_part, _, _ = attend(
        jnp.concatenate([worker_ids, outer_ids]), adapters, 0, table, turn, up_all, 1, sums,
        [(array,) for array in own_tokens]
        + [
            tuple(outer_tokens[chunk][step] for chunk in range(CHUNKS)) for step in range(pairs)
        ],
        [outer_weight], [], (),
    )

    def spread(parts):
        result, moving = [], parts
        for step in range(pairs):
            if step:
                moving = [lax.ppermute(part, "tensor", ring) for part in moving]
            result.append(
                [(lax.ppermute(part, "tensor", from_worker), part) for part in moving]
            )
        return result

    def lookups(ids):
        return jnp.concatenate(
            [
                (here - ids + planes) % planes,
                jnp.stack([is_worker.astype(jnp.int32), group_here]),
                block_of(dp_here ^ jnp.arange(dp_size), dp_size),
                block_of(dp_here ^ adapters, dp_size),
                adapters,
            ]
        ).astype(jnp.int32)

    weights = [own_weight] + halves
    sizes = (dp_size, group_size, planes, count, rank)
    begun = project_out(lookups(worker_ids), spread(own_parts), weights, sizes, [], [])
    return project_out(
        lookups(outer_ids), spread([outer_part]), weights, sizes, list(begun),
        [table, out_up_all],
    )


def solution(mesh):
    in_specs = (
        P(PLANE, "tensor"),
        P(None, None, "tensor"),
        P("tensor", None, None),
        P(PLANE, None, "tensor"),
        P(PLANE, None, None, "tensor"),
        P(PLANE, None, None, "tensor"),
        P(PLANE, None, "tensor"),
        P(PLANE, None),
        P(PLANE, None),
    )
    function = functools.partial(
        local, mesh.shape["dp"], mesh.shape["groups"], mesh.shape["tensor"]
    )
    return jax.shard_map(
        function, mesh=mesh, in_specs=in_specs, out_specs=P(PLANE, "tensor"), check_vma=False
    )
```

time: 278 us -> 265 us (0.953)
  local copies, waits for them, and re-layouts: 59.1 us -> 22.9 us
  other arithmetic: 31.6 us -> 6.12 us
  starting transfers between devices: 50.4 us -> 72.3 us
  blocking collectives: 0 us -> 16.4 us
  waiting for transfers between devices: 79.7 us -> 87.8 us
  Pallas kernels: 38.5 us -> 44.5 us
    ppermute x14 -> x9, starting transfers between devices: 22.3 us -> 44.2 us  [the longest x3 30.1 us: local(): lax.ppermute(after(send, own_tokens[-1]), 'tensor', [(i, (i + turn_by) %...]
    all_gather x0 -> x2, blocking collectives: none -> 16.4 us  [the longest x1 9.02 us: local(): up_all = lax.all_gather(up_pair, 'dp', axis=0)]
    ppermute x14 -> x9, waiting for transfers between devices: 44.7 us -> 30.5 us  [the longest x1 16.7 us: local(): piece = lax.ppermute(piece, 'tensor', to_worker)]
    select_n x9 -> x2, other arithmetic: 10.5 us -> 0.17 us  [lookups(): (here - ids + planes) % planes]
    ppermute x1, waiting for transfers between devices: 0.01 us -> 8.9 us  [local(): shrink = shrink + lax.ppermute(shrink, 'tensor', to_worker)]
    concatenate x14 -> x5, other arithmetic: 12.3 us -> 3.55 us  [the longest x1 3.13 us: doubled(): value = jnp.concatenate([value, moved], axis=0)]
    another operation x9 -> x0, local copies, waits for them, and re-layouts: 7.51 us -> none  [the longest x4 5.11 us: local(): turned_down = gather_over(jnp.stack(got_down), 'dp', dp_size)]
    ppermute x2, waiting for transfers between devices: 0.01 us -> 7.1 us  [local(): previous = lax.ppermute(part, 'tensor', to_worker)]
  transfers between devices with their start and end apart: 31 -> 26, of which waited for: 9 -> 11; matrix products, arithmetic and copies ran while one was open for 30% -> 8% of each run, Pallas kernels for 12% -> 14%
where the time goes in v3:
time: 265 us; the launch traced here: 264 us
  waiting for transfers between devices  87.8 us (33%)
  starting transfers between devices  72.3 us (27%)
  Pallas kernels  44.5 us (17%)
  local copies, waits for them, and re-layouts  22.9 us (9%)
  blocking collectives  16.4 us (6%)
  between operations  14 us (5%)
  other arithmetic  6.12 us (2%)
    pallas_call x7, Pallas kernels, call(): pl.pallas_call(kernel, out_shape=out, grid_spec=pltpu.PrefetchScalarGridS...  44.5 us
    ppermute x6, waiting for transfers between devices, spread(): lax.ppermute(part, 'tensor', from_worker)  40.5 us
    ppermute x3, starting transfers between devices, local(): lax.ppermute(after(send, own_tokens[-1]), 'tensor', [(i, (i + turn_by) %...  30.1 us
    ppermute x1, waiting for transfers between devices, local(): piece = lax.ppermute(piece, 'tensor', to_worker)  16.7 us
    unnamed x37, local copies, waits for them, and re-layouts  10.7 us
    ppermute x3, waiting for transfers between devices, local(): lax.ppermute(after(send, own_tokens[-1]), 'tensor', [(i, (i + turn_by) %...  10.6 us
    ppermute x2, starting transfers between devices, local(): previous = lax.ppermute(part, 'tensor', to_worker)  9.79 us
    all_gather x1, blocking collectives, local(): up_all = lax.all_gather(up_pair, 'dp', axis=0)  9.02 us
  transfers between devices with their start and end apart: 26, of which 11 were waited for; matrix products, arithmetic and copies ran while one was open for 8% of the time, Pallas kernels for 14%

profile of v3, /device:TPU:0, one launch (start us, length us, event | category | flops | bytes accessed | tf_op | source)
XLA Modules:
  0.0 263.9 jit_solution(13364704631503335233)
XLA Ops:
  8.6 5.0 %collective-permute-start.4 = (bf16[6,512,128]{2,1,0:T(8,128)(2,1)S(1)}, bf16[6,512,128]{2,1,0:T(8,128)(2,1)S(1)}, u32[]{:S(2)}, u32[]{:S(2)}) collective-permute-start(bf16[6,512,128]{2,1,0:T(8,128)(2,1)S(1)} %dynamic-slice_bitcast_fusion.1), channel_id=1, source_target_pairs={{0,1},{3,2},{4,5},{7,6},{8,9},{11,10},{12,13},{15,14},{16,17},{19,... | collective-permute-start | bytes 2359304 | tf_op jit(solution)/shard_map/ppermute | solution.py:454
  13.5 16.7 %collective-permute-done.4 = bf16[6,512,128]{2,1,0:T(8,128)(2,1)S(1)} collective-permute-done((bf16[6,512,128]{2,1,0:T(8,128)(2,1)S(1)}, bf16[6,512,128]{2,1,0:T(8,128)(2,1)S(1)}, u32[]{:S(2)}, u32[]{:S(2)}) %collective-permute-start.4) | collective-permute-done | bytes 786464 | tf_op jit(solution)/shard_map/ppermute | solution.py:454
  32.1 2.8 %fusion.7 = (bf16[64,1,1024]{2,1,0:T(2,128)(2,1)S(1)}, bf16[64,1,1024]{2,1,0:T(2,128)(2,1)S(1)}, bf16[64,1,1024]{2,1,0:T(2,128)(2,1)S(1)}) fusion(bf16[128,4,4096]{2,1,0:T(4,128)(2,1)} %param.11, s32[]{:T(128)S(6)} %select_n.122, s32[]{:T(128)S(6)} %select_n.125, s32[]{:T(128)S(6)} %select_n.134, s32[]{:T(128)S(6)} %select_n.131, s32[]{:T(128)S(6)} %select_n.128), kind=kLoop, calls=%fused_computation.51 | loop fusion | bytes 786452 | tf_op jit(solution)/shard_map/dynamic_slice | solution.py:513
  35.2 28.6 %collective-permute-start.12 = (bf16[96,1024]{1,0:T(8,128)(2,1)S(1)}, bf16[96,1024]{1,0:T(8,128)(2,1)S(1)}, u32[]{:S(2)}, u32[]{:S(2)}) collective-permute-start(bf16[96,1024]{1,0:T(8,128)(2,1)S(1)} %get-tuple-element.20), channel_id=1, source_target_pairs={{0,1},{1,2},{2,3},{3,0},{4,5},{5,6},{6,7},{7,4},{8,9},{9,10},{10,1... | collective-permute-start | bytes 589832 | tf_op jit(solution)/shard_map/ppermute | solution.py:518
  63.9 1.5 collective-permute-start.13
  65.3 3.9 %collective-permute-done.12 = bf16[96,1024]{1,0:T(8,128)(2,1)S(1)} collective-permute-done((bf16[96,1024]{1,0:T(8,128)(2,1)S(1)}, bf16[96,1024]{1,0:T(8,128)(2,1)S(1)}, u32[]{:S(2)}, u32[]{:S(2)}) %collective-permute-start.12) | collective-permute-done | bytes 196640 | tf_op jit(solution)/shard_map/ppermute | solution.py:518
  69.9 6.7 %collective-permute-done.13 = bf16[96,1024]{1,0:T(8,128)(2,1)S(1)} collective-permute-done((bf16[96,1024]{1,0:T(8,128)(2,1)S(1)}, bf16[96,1024]{1,0:T(8,128)(2,1)S(1)}, u32[]{:S(2)}, u32[]{:S(2)}) %collective-permute-start.13) | collective-permute-done | bytes 196640 | tf_op jit(solution)/shard_map/ppermute | solution.py:518
  77.9 1.7 collective-permute-start.15
  79.6 5.1 %collective-permute-start = (bf16[6,64,128]{2,1,0:T(8,128)(2,1)}, bf16[6,64,128]{2,1,0:T(8,128)(2,1)}, u32[]{:S(2)}, u32[]{:S(2)}) collective-permute-start(bf16[6,64,128]{2,1,0:T(8,128)(2,1)} %bitcast.12), channel_id=1, source_target_pairs={{0,1},{3,2},{4,5},{7,6},{8,9},{11,10},{12,13},{15,14},{16,17},{19,... | collective-permute-start | bytes 294920 | tf_op jit(solution)/shard_map/ppermute | solution.py:470
  90.1 1.6 collective-permute-start.16
  92.6 4.6 %collective-permute-start.5 = (bf16[256,1024]{1,0:T(8,128)(2,1)S(1)}, bf16[256,1024]{1,0:T(8,128)(2,1)S(1)}, u32[]{:S(2)}, u32[]{:S(2)}) collective-permute-start(bf16[256,1024]{1,0:T(8,128)(2,1)S(1)} %get-tuple-element.17), channel_id=1, source_target_pairs={{0,1},{3,2},{4,5},{7,6},{8,9},{11,10},{12,13},{15,14},{16,17},{19,... | collective-permute-start | bytes 1572872 | tf_op jit(solution)/shard_map/ppermute | solution.py:462
  97.6 7.1 %collective-permute-done.5.refs_4_.refs_2_ = bf16[256,1024]{1,0:T(8,128)(2,1)S(1)} collective-permute-done((bf16[256,1024]{1,0:T(8,128)(2,1)S(1)}, bf16[256,1024]{1,0:T(8,128)(2,1)S(1)}, u32[]{:S(2)}, u32[]{:S(2)}) %collective-permute-start.5) | collective-permute-done | bytes 524320 | tf_op jit(solution)/shard_map/ppermute | solution.py:462
  104.7 5.2 %collective-permute-start.6 = (bf16[256,1024]{1,0:T(8,128)(2,1)}, bf16[256,1024]{1,0:T(8,128)(2,1)}, u32[]{:S(2)}, u32[]{:S(2)}) collective-permute-start(bf16[256,1024]{1,0:T(8,128)(2,1)} %get-tuple-element.18), channel_id=1, source_target_pairs={{0,1},{3,2},{4,5},{7,6},{8,9},{11,10},{12,13},{15,14},{16,17},{19,... | collective-permute-start | bytes 1572872 | tf_op jit(solution)/shard_map/ppermute | solution.py:462
  109.9 1.9 collective-permute-done.16
  111.8 3.1 %pad_maximum_fusion.refs_9_.refs_5_ = bf16[2,512,1024]{2,1,0:T(8,128)(2,1)} fusion(bf16[1,512,1024]{2,1,0:T(8,128)(2,1)} %collective-permute-done.16, bf16[1,512,1024]{2,1,0:T(8,128)(2,1)} %bitcast.24), kind=kLoop, calls=%fused_computation | loop fusion | flops 1048576 | bytes 4194304 | tf_op jit(solution)/shard_map/concatenate | solution.py:393
  116.4 2.6 shrink.1
  119.0 4.7 %collective-permute-start.1 = (f32[512,192]{1,0:T(8,128)S(1)}, f32[512,192]{1,0:T(8,128)S(1)}, u32[]{:S(2)}, u32[]{:S(2)}) collective-permute-start(f32[512,192]{1,0:T(8,128)S(1)} %shrink.1), channel_id=1, source_target_pairs={{0,1},{3,2},{4,5},{7,6},{8,9},{11,10},{12,13},{15,14},{16,17},{19,... | collective-permute-start | bytes 1179656 | tf_op jit(solution)/shard_map/ppermute | solution.py:494
  126.6 8.9 %collective-permute-done.1 = f32[512,192]{1,0:T(8,128)S(1)} collective-permute-done((f32[512,192]{1,0:T(8,128)S(1)}, f32[512,192]{1,0:T(8,128)S(1)}, u32[]{:S(2)}, u32[]{:S(2)}) %collective-permute-start.1) | collective-permute-done | bytes 393248 | tf_op jit(solution)/shard_map/ppermute | solution.py:494
  137.2 9.0 %all-gather = bf16[8,6,64,128]{3,2,1,0:T(8,128)(2,1)S(1)} all-gather(bf16[2,6,64,128]{3,2,1,0:T(8,128)(2,1)S(1)} %pad_maximum_fusion.6), channel_id=2, replica_groups=mesh['groups'=2,'dp'=4,'tensor'=4] {'dp'}, dimensions={0}, use_global_device_ids=true | all-gather | bytes 983040 | tf_op jit(solution)/shard_map/all_gather | solution.py:471
  149.9 12.8 %attend.3 = (bf16[512,512]{1,0:T(8,128)(2,1)}, bf16[512,128]{1,0:T(8,128)(2,1)}, bf16[512,128]{1,0:T(8,128)(2,1)}) custom-call(s32[8]{0:T(128)S(1)} %concatenate.42.ids_ref, s32[512,2]{1,0:T(8,128)S(1)} %copy.30.table_ref.refs_9_, f32[512,256]{1,0:T(8,128)S(1)} %pad_maximum_fusion.1.turn_ref, bf16[4,2,6,64,128]{4,3,2,1,0:T(8,128)(2,1)S(1)} %bitcast.44, ...), custom_call_target="tpu_custom_call" | custom-call | flops 1000 | bytes 1000 | tf_op jit(solution)/shard_map/attend/pallas_call | solution.py:166
  164.3 4.0 %project.1.refs_5_ = f32[512,768]{1,0:T(8,128)S(1)} custom-call(s32[2]{0:T(128)S(1)} %get-tuple-element.30.ids_ref, bf16[512,1024]{1,0:T(8,128)(2,1)S(1)} %copy-done.1, bf16[512,1024]{1,0:T(8,128)(2,1)S(1)} %copy-done.3, bf16[6,4096,128]{2,1,0:T(8,128)(2,1)} %bitcast.49), custom_call_target="tpu_custom_call" | custom-call | flops 1000 | bytes 1000 | tf_op jit(solution)/shard_map/project/pallas_call | solution.py:166
  168.3 5.9 %attend.4 = (bf16[256,512]{1,0:T(8,128)(2,1)}, bf16[256,128]{1,0:T(8,128)(2,1)S(1)}, bf16[256,128]{1,0:T(8,128)(2,1)S(1)}) custom-call(s32[6]{0:T(128)S(1)} %pad_add_fusion.2.ids_ref, s32[512,2]{1,0:T(8,128)S(1)} %copy.30.table_ref.refs_9_, f32[512,256]{1,0:T(8,128)S(1)} %pad_maximum_fusion.1.turn_ref, bf16[4,2,6,64,128]{4,3,2,1,0:T(8,128)(2,1)S(1)} %bitcast.45, ...), custom_call_target="tpu_custom_call" | custom-call | flops 1000 | bytes 1000 | tf_op jit(solution)/shard_map/attend/pallas_call | solution.py:166
  174.2 1.5 collective-permute-start.18
  175.7 6.6 %attend.5 = (bf16[256,512]{1,0:T(8,128)(2,1)S(1)}, bf16[256,128]{1,0:T(8,128)(2,1)}, bf16[256,128]{1,0:T(8,128)(2,1)}) custom-call(s32[6]{0:T(128)S(1)} %pad_add_fusion.2.ids_ref, s32[512,2]{1,0:T(8,128)S(1)} %copy.30.table_ref.refs_9_, f32[512,256]{1,0:T(8,128)S(1)} %pad_maximum_fusion.1.turn_ref, bf16[4,2,6,64,128]{4,3,2,1,0:T(8,128)(2,1)S(1)} %bitcast.46, ...), custom_call_target="tpu_custom_call" | custom-call | flops 1000 | bytes 1000 | tf_op jit(solution)/shard_map/attend/pallas_call | solution.py:166
  184.4 13.3 %collective-permute-done.18.refs_0_ = bf16[256,512]{1,0:T(8,128)(2,1)S(1)} collective-permute-done((bf16[256,512]{1,0:T(8,128)(2,1)}, bf16[256,512]{1,0:T(8,128)(2,1)S(1)}, u32[]{:S(2)}, u32[]{:S(2)}) %collective-permute-start.18) | collective-permute-done | bytes 262176 | tf_op jit(solution)/shard_map/ppermute | solution.py:554
  199.1 6.6 %collective-permute-done.19.refs_2_ = bf16[256,512]{1,0:T(8,128)(2,1)S(1)} collective-permute-done((bf16[256,512]{1,0:T(8,128)(2,1)S(1)}, bf16[256,512]{1,0:T(8,128)(2,1)S(1)}, u32[]{:S(2)}, u32[]{:S(2)}) %collective-permute-start.19) | collective-permute-done | bytes 262176 | tf_op jit(solution)/shard_map/ppermute | solution.py:554
  208.2 1.6 dynamic-slice_bitcast_fusion
  215.2 7.4 %all_gather.23.refs_10_ = bf16[4,64,1024]{2,1,0:T(8,128)(2,1)S(1)} all-gather(bf16[1,64,1024]{2,1,0:T(8,128)(2,1)S(1)} %copy-done.11), channel_id=1, replica_groups=mesh['groups'=2,'dp'=4,'tensor'=4] {'dp'}, dimensions={0}, use_global_device_ids=true | all-gather | bytes 655360 | tf_op jit(solution)/shard_map/all_gather | solution.py:472
  222.6 16.9 %collective-permute-done.21.refs_4_ = bf16[256,512]{1,0:T(8,128)(2,1)} collective-permute-done((bf16[256,512]{1,0:T(8,128)(2,1)S(1)}, bf16[256,512]{1,0:T(8,128)(2,1)}, u32[]{:S(2)}, u32[]{:S(2)}) %collective-permute-start.21) | collective-permute-done | bytes 262176 | tf_op jit(solution)/shard_map/ppermute | solution.py:554
  239.6 3.6 %collective-permute-done.23.refs_6_ = bf16[256,512]{1,0:T(8,128)(2,1)} collective-permute-done((bf16[256,512]{1,0:T(8,128)(2,1)}, bf16[256,512]{1,0:T(8,128)(2,1)}, u32[]{:S(2)}, u32[]{:S(2)}) %collective-permute-start.23) | collective-permute-done | bytes 262176 | tf_op jit(solution)/shard_map/ppermute | solution.py:554
  243.2 5.3 %project_out.2 = (f32[512,1024]{1,0:T(8,128)S(1)}, f32[512,256]{1,0:T(8,128)S(1)}) custom-call(s32[16]{0:T(128)S(1)} %concatenate.51.ids_ref, bf16[256,512]{1,0:T(8,128)(2,1)S(1)} %collective-permute-done.18.refs_0_, bf16[256,512]{1,0:T(8,128)(2,1)} %get-tuple-element.23.refs_1_, bf16[256,512]{1,0:T(8,128)(2,1)S(1)} %collective-permute-done.19.refs_2_, ...), custom_call_target="tpu_custom_call" | custom-call | flops 1000 | bytes 1000 | tf_op jit(solution)/shard_map/project_out/pallas_call | solution.py:166
  249.8 7.3 %project_out.3 = bf16[512,1024]{1,0:T(8,128)(2,1)} custom-call(s32[16]{0:T(128)S(1)} %concatenate.41.ids_ref, bf16[512,512]{1,0:T(8,128)(2,1)S(1)} %collective-permute-done.9.refs_0_, bf16[512,512]{1,0:T(8,128)(2,1)} %get-tuple-element.19.refs_1_, bf16[512,512]{1,0:T(8,128)(2,1)S(1)} %collective-permute-done.11.refs_2_, ...), custom_call_target="tpu_custom_call" | custom-call | flops 1000 | bytes 1000 | tf_op jit(solution)/shard_map/project_out/pallas_call | solution.py:166
  (108 shorter events, 36.2 us)
Async XLA Ops:
  6.5 24.7 %copy-start = (bf16[512,1024]{1,0:T(8,128)(2,1)S(1)}, bf16[512,1024]{1,0:T(8,128)(2,1)}, u32[]{:S(2)}) copy-start(bf16[512,1024]{1,0:T(8,128)(2,1)} %refs_0_.1) | copy-start | bytes 3145732
  6.5 108.4 %all-gather.5.cloned.1.call-start = ((), (), s32[]{:S(2)}) async-start(), calls=%async_computation | async-start | bytes 1966080 | tf_op jit(solution)/shard_map/all_gather | solution.py:468
  7.3 140.6 %all-gather.7.cloned.1.call-start = ((), (), s32[]{:S(2)}) async-start(), calls=%async_computation.1 | async-start | bytes 7077888 | tf_op jit(solution)/shard_map/all_gather | solution.py:455
  7.3 27.6 %copy-start.12 = (bf16[1,64,4,128]{3,2,1,0:T(4,128)(2,1)S(1)}, bf16[1,64,4,128]{3,2,1,0:T(4,128)(2,1)}, u32[]{:S(2)}) copy-start(bf16[1,64,4,128]{3,2,1,0:T(4,128)(2,1)} %param.14) | copy-start | bytes 196612
  8.6 21.7 %collective-permute-start.4 = (bf16[6,512,128]{2,1,0:T(8,128)(2,1)S(1)}, bf16[6,512,128]{2,1,0:T(8,128)(2,1)S(1)}, u32[]{:S(2)}, u32[]{:S(2)}) collective-permute-start(bf16[6,512,128]{2,1,0:T(8,128)(2,1)S(1)} %dynamic-slice_bitcast_fusion.1), channel_id=1, source_target_pairs={{0,1},{3,2},{4,5},{7,6},{8,9},{11,10},{12,13},{15,14},{16,17},{19,... | collective-permute-start | bytes 2359304 | tf_op jit(solution)/shard_map/ppermute | solution.py:454
  31.2 4.0 %collective-permute-start.3 = (bf16[512,1024]{1,0:T(8,128)(2,1)S(1)}, bf16[512,1024]{1,0:T(8,128)(2,1)S(1)}, u32[]{:S(2)}, u32[]{:S(2)}) collective-permute-start(bf16[512,1024]{1,0:T(8,128)(2,1)S(1)} %copy-done), channel_id=1, source_target_pairs={{1,2},{2,1},{5,6},{6,5},{9,10},{10,9},{13,14},{14,13},{17,18},{18,... | collective-permute-start | bytes 3145736 | tf_op jit(solution)/shard_map/ppermute | solution.py:449
  35.0 49.8 %copy-start.13 = (s32[1,4]{1,0:T(1,128)S(1)}, s32[1,4]{1,0:T(1,128)}, u32[]{:S(2)}) copy-start(s32[1,4]{1,0:T(1,128)} %param.17) | copy-start | bytes 52
  35.2 57.4 %copy-start.2 = (bf16[512,1024]{1,0:T(8,128)(2,1)}, bf16[512,1024]{1,0:T(8,128)(2,1)S(1)}, u32[]{:S(2)}) copy-start(bf16[512,1024]{1,0:T(8,128)(2,1)S(1)} %collective-permute-done.3.refs_3_.refs_1_) | copy-start | bytes 3145732
  35.2 34.0 %collective-permute-start.12 = (bf16[96,1024]{1,0:T(8,128)(2,1)S(1)}, bf16[96,1024]{1,0:T(8,128)(2,1)S(1)}, u32[]{:S(2)}, u32[]{:S(2)}) collective-permute-start(bf16[96,1024]{1,0:T(8,128)(2,1)S(1)} %get-tuple-element.20), channel_id=1, source_target_pairs={{0,1},{1,2},{2,3},{3,0},{4,5},{5,6},{6,7},{7,4},{8,9},{9,10},{10,1... | collective-permute-start | bytes 589832 | tf_op jit(solution)/shard_map/ppermute | solution.py:518
  63.9 13.4 %collective-permute-start.14 = (bf16[96,1024]{1,0:T(8,128)(2,1)S(1)}, bf16[96,1024]{1,0:T(8,128)(2,1)S(1)}, u32[]{:S(2)}, u32[]{:S(2)}) collective-permute-start(bf16[96,1024]{1,0:T(8,128)(2,1)S(1)} %get-tuple-element.22), channel_id=1, source_target_pairs={{0,3},{1,0},{2,1},{3,2},{4,7},{5,4},{6,5},{7,6},{8,11},{9,8},{10,9... | collective-permute-start | bytes 589832 | tf_op jit(solution)/shard_map/ppermute | solution.py:518
  63.9 12.7 %collective-permute-start.13 = (bf16[96,1024]{1,0:T(8,128)(2,1)S(1)}, bf16[96,1024]{1,0:T(8,128)(2,1)S(1)}, u32[]{:S(2)}, u32[]{:S(2)}) collective-permute-start(bf16[96,1024]{1,0:T(8,128)(2,1)S(1)} %get-tuple-element.21), channel_id=1, source_target_pairs={{0,2},{1,3},{2,0},{3,1},{4,6},{5,7},{6,4},{7,5},{8,10},{9,11},{10,... | collective-permute-start | bytes 589832 | tf_op jit(solution)/shard_map/ppermute | solution.py:518
  77.9 19.4 %copy-start.14 = (s32[1,4]{1,0:T(1,128)S(1)}, s32[1,4]{1,0:T(1,128)}, u32[]{:S(2)}) copy-start(s32[1,4]{1,0:T(1,128)} %param.16) | copy-start | bytes 52
  77.9 8.3 %collective-permute-start.15 = (bf16[192,1024]{1,0:T(8,128)(2,1)S(1)}, bf16[192,1024]{1,0:T(8,128)(2,1)S(1)}, u32[]{:S(2)}, u32[]{:S(2)}) collective-permute-start(bf16[192,1024]{1,0:T(8,128)(2,1)S(1)} %pad_maximum_fusion.2), channel_id=1, source_target_pairs={{0,16},{16,0},{1,17},{17,1},{2,18},{18,2},{3,19},{19,3},{4,20},{20... | collective-permute-start | bytes 1179656 | tf_op jit(solution)/shard_map/ppermute | solution.py:390
  79.6 56.6 %collective-permute-start = (bf16[6,64,128]{2,1,0:T(8,128)(2,1)}, bf16[6,64,128]{2,1,0:T(8,128)(2,1)}, u32[]{:S(2)}, u32[]{:S(2)}) collective-permute-start(bf16[6,64,128]{2,1,0:T(8,128)(2,1)} %bitcast.12), channel_id=1, source_target_pairs={{0,1},{3,2},{4,5},{7,6},{8,9},{11,10},{12,13},{15,14},{16,17},{19,... | collective-permute-start | bytes 294920 | tf_op jit(solution)/shard_map/ppermute | solution.py:470
  90.1 21.6 %collective-permute-start.16 = (bf16[1,512,1024]{2,1,0:T(8,128)(2,1)}, bf16[1,512,1024]{2,1,0:T(8,128)(2,1)}, u32[]{:S(2)}, u32[]{:S(2)}) collective-permute-start(bf16[1,512,1024]{2,1,0:T(8,128)(2,1)} %bitcast.24), channel_id=1, source_target_pairs={{0,8},{4,12},{8,0},{12,4},{1,9},{5,13},{9,1},{13,5},{2,10},{6,14},... | collective-permute-start | bytes 3145736 | tf_op jit(solution)/shard_map/ppermute | solution.py:390
  92.6 12.1 %collective-permute-start.5 = (bf16[256,1024]{1,0:T(8,128)(2,1)S(1)}, bf16[256,1024]{1,0:T(8,128)(2,1)S(1)}, u32[]{:S(2)}, u32[]{:S(2)}) collective-permute-start(bf16[256,1024]{1,0:T(8,128)(2,1)S(1)} %get-tuple-element.17), channel_id=1, source_target_pairs={{0,1},{3,2},{4,5},{7,6},{8,9},{11,10},{12,13},{15,14},{16,17},{19,... | collective-permute-start | bytes 1572872 | tf_op jit(solution)/shard_map/ppermute | solution.py:462
  104.7 20.8 %collective-permute-start.6 = (bf16[256,1024]{1,0:T(8,128)(2,1)}, bf16[256,1024]{1,0:T(8,128)(2,1)}, u32[]{:S(2)}, u32[]{:S(2)}) collective-permute-start(bf16[256,1024]{1,0:T(8,128)(2,1)} %get-tuple-element.18), channel_id=1, source_target_pairs={{0,1},{3,2},{4,5},{7,6},{8,9},{11,10},{12,13},{15,14},{16,17},{19,... | collective-permute-start | bytes 1572872 | tf_op jit(solution)/shard_map/ppermute | solution.py:462
  114.9 128.3 %collective-permute-start.17 = (bf16[2,512,1024]{2,1,0:T(8,128)(2,1)}, bf16[2,512,1024]{2,1,0:T(8,128)(2,1)}, u32[]{:S(2)}, u32[]{:S(2)}) collective-permute-start(bf16[2,512,1024]{2,1,0:T(8,128)(2,1)} %pad_maximum_fusion.refs_9_.refs_5_), channel_id=1, source_target_pairs={{0,4},{4,0},{8,12},{12,8},{1,5},{5,1},{9,13},{13,9},{2,6},{6,2},{1... | collective-permute-start | bytes 6291464 | tf_op jit(solution)/shard_map/ppermute | solution.py:394
  119.0 16.5 %collective-permute-start.1 = (f32[512,192]{1,0:T(8,128)S(1)}, f32[512,192]{1,0:T(8,128)S(1)}, u32[]{:S(2)}, u32[]{:S(2)}) collective-permute-start(f32[512,192]{1,0:T(8,128)S(1)} %shrink.1), channel_id=1, source_target_pairs={{0,1},{3,2},{4,5},{7,6},{8,9},{11,10},{12,13},{15,14},{16,17},{19,... | collective-permute-start | bytes 1179656 | tf_op jit(solution)/shard_map/ppermute | solution.py:494
  124.9 21.4 %collective-permute-start.7 = (bf16[256,1024]{1,0:T(8,128)(2,1)S(1)}, bf16[256,1024]{1,0:T(8,128)(2,1)S(1)}, u32[]{:S(2)}, u32[]{:S(2)}) collective-permute-start(bf16[256,1024]{1,0:T(8,128)(2,1)S(1)} %collective-permute-done.5.refs_4_.refs_2_), channel_id=1, source_target_pairs={{1,2},{2,1},{5,6},{6,5},{9,10},{10,9},{13,14},{14,13},{17,18},{18,... | collective-permute-start | bytes 1572872 | tf_op jit(solution)/shard_map/ppermute | solution.py:465
  125.6 21.4 %collective-permute-start.8 = (bf16[256,1024]{1,0:T(8,128)(2,1)}, bf16[256,1024]{1,0:T(8,128)(2,1)S(1)}, u32[]{:S(2)}, u32[]{:S(2)}) collective-permute-start(bf16[256,1024]{1,0:T(8,128)(2,1)} %collective-permute-done.6.refs_5_.refs_2_), channel_id=1, source_target_pairs={{1,2},{2,1},{5,6},{6,5},{9,10},{10,9},{13,14},{14,13},{17,18},{18,... | collective-permute-start | bytes 1572872 | tf_op jit(solution)/shard_map/ppermute | solution.py:465
  135.5 12.3 %collective-permute-start.2 = (f32[512,192]{1,0:T(8,128)S(1)}, f32[512,192]{1,0:T(8,128)S(1)}, u32[]{:S(2)}, u32[]{:S(2)}) collective-permute-start(f32[512,192]{1,0:T(8,128)S(1)} %add.138.refs_0_), channel_id=1, source_target_pairs={{1,2},{2,1},{5,6},{6,5},{9,10},{10,9},{13,14},{14,13},{17,18},{18,... | collective-permute-start | bytes 1179656 | tf_op jit(solution)/shard_map/ppermute | solution.py:497
  162.7 44.2 %collective-permute-start.10 = (bf16[512,512]{1,0:T(8,128)(2,1)}, bf16[512,512]{1,0:T(8,128)(2,1)}, u32[]{:S(2)}, u32[]{:S(2)}) collective-permute-start(bf16[512,512]{1,0:T(8,128)(2,1)} %get-tuple-element.19.refs_1_), channel_id=1, source_target_pairs={{1,2},{2,1},{5,6},{6,5},{9,10},{10,9},{13,14},{14,13},{17,18},{18,... | collective-permute-start | bytes 1572872 | tf_op jit(solution)/shard_map/ppermute | solution.py:552
  174.2 23.5 %collective-permute-start.18 = (bf16[256,512]{1,0:T(8,128)(2,1)}, bf16[256,512]{1,0:T(8,128)(2,1)S(1)}, u32[]{:S(2)}, u32[]{:S(2)}) collective-permute-start(bf16[256,512]{1,0:T(8,128)(2,1)} %get-tuple-element.23.refs_1_), channel_id=1, source_target_pairs={{1,0},{2,3},{5,4},{6,7},{9,8},{10,11},{13,12},{14,15},{17,16},{18,... | collective-permute-start | bytes 786440 | tf_op jit(solution)/shard_map/ppermute | solution.py:554
  182.4 23.3 %collective-permute-start.19 = (bf16[256,512]{1,0:T(8,128)(2,1)S(1)}, bf16[256,512]{1,0:T(8,128)(2,1)S(1)}, u32[]{:S(2)}, u32[]{:S(2)}) collective-permute-start(bf16[256,512]{1,0:T(8,128)(2,1)S(1)} %get-tuple-element.26.refs_3_), channel_id=1, source_target_pairs={{1,0},{2,3},{5,4},{6,7},{9,8},{10,11},{13,12},{14,15},{17,16},{18,... | collective-permute-start | bytes 786440 | tf_op jit(solution)/shard_map/ppermute | solution.py:554
  183.7 26.6 %collective-permute-start.20 = (bf16[256,512]{1,0:T(8,128)(2,1)}, bf16[256,512]{1,0:T(8,128)(2,1)S(1)}, u32[]{:S(2)}, u32[]{:S(2)}) collective-permute-start(bf16[256,512]{1,0:T(8,128)(2,1)} %get-tuple-element.23.refs_1_), channel_id=1, source_target_pairs={{1,2},{2,1},{5,6},{6,5},{9,10},{10,9},{13,14},{14,13},{17,18},{18,... | collective-permute-start | bytes 786440 | tf_op jit(solution)/shard_map/ppermute | solution.py:552
  197.7 13.9 %collective-permute-start.22 = (bf16[256,512]{1,0:T(8,128)(2,1)S(1)}, bf16[256,512]{1,0:T(8,128)(2,1)}, u32[]{:S(2)}, u32[]{:S(2)}) collective-permute-start(bf16[256,512]{1,0:T(8,128)(2,1)S(1)} %get-tuple-element.26.refs_3_), channel_id=1, source_target_pairs={{1,2},{2,1},{5,6},{6,5},{9,10},{10,9},{13,14},{14,13},{17,18},{18,... | collective-permute-start | bytes 786440 | tf_op jit(solution)/shard_map/ppermute | solution.py:552
  199.1 16.2 %copy-start.11 = (bf16[1,64,1024]{2,1,0:T(8,128)(2,1)S(1)}, bf16[1,64,1024]{2,1,0:T(8,128)(2,1)}, u32[]{:S(2)}) copy-start(bf16[1,64,1024]{2,1,0:T(8,128)(2,1)} %param.15) | copy-start | bytes 393220
  205.6 44.2 %collective-permute-start.9 = (bf16[512,512]{1,0:T(8,128)(2,1)}, bf16[512,512]{1,0:T(8,128)(2,1)S(1)}, u32[]{:S(2)}, u32[]{:S(2)}) collective-permute-start(bf16[512,512]{1,0:T(8,128)(2,1)} %get-tuple-element.19.refs_1_), channel_id=1, source_target_pairs={{1,0},{2,3},{5,4},{6,7},{9,8},{10,11},{13,12},{14,15},{17,16},{18,... | collective-permute-start | bytes 1572872 | tf_op jit(solution)/shard_map/ppermute | solution.py:554
  206.9 42.9 %collective-permute-start.11 = (bf16[512,512]{1,0:T(8,128)(2,1)}, bf16[512,512]{1,0:T(8,128)(2,1)S(1)}, u32[]{:S(2)}, u32[]{:S(2)}) collective-permute-start(bf16[512,512]{1,0:T(8,128)(2,1)} %collective-permute-done.10.refs_3_), channel_id=1, source_target_pairs={{1,0},{2,3},{5,4},{6,7},{9,8},{10,11},{13,12},{14,15},{17,16},{18,... | collective-permute-start | bytes 1572872 | tf_op jit(solution)/shard_map/ppermute | solution.py:554
  210.3 29.3 %collective-permute-start.21 = (bf16[256,512]{1,0:T(8,128)(2,1)S(1)}, bf16[256,512]{1,0:T(8,128)(2,1)}, u32[]{:S(2)}, u32[]{:S(2)}) collective-permute-start(bf16[256,512]{1,0:T(8,128)(2,1)S(1)} %collective-permute-done.20.refs_5_), channel_id=1, source_target_pairs={{1,0},{2,3},{5,4},{6,7},{9,8},{10,11},{13,12},{14,15},{17,16},{18,... | collective-permute-start | bytes 786440 | tf_op jit(solution)/shard_map/ppermute | solution.py:554
  211.6 31.6 %collective-permute-start.23 = (bf16[256,512]{1,0:T(8,128)(2,1)}, bf16[256,512]{1,0:T(8,128)(2,1)}, u32[]{:S(2)}, u32[]{:S(2)}) collective-permute-start(bf16[256,512]{1,0:T(8,128)(2,1)} %collective-permute-done.22.refs_7_), channel_id=1, source_target_pairs={{1,0},{2,3},{5,4},{6,7},{9,8},{10,11},{13,12},{14,15},{17,16},{18,... | collective-permute-start | bytes 786440 | tf_op jit(solution)/shard_map/ppermute | solution.py:554
  (9 other events, 36.2 us)
Sparse Core Ops, SparseCore 0:
  8.9 22.3 all-gather.4
  33.2 45.5 all-gather.6

commit v4 on v3

--- a/solution.py
+++ b/solution.py
@@ -9,7 +9,7 @@
 from jax.sharding import PartitionSpec as P
 
 CHUNKS = 2
-VMEM_BYTES = 48 * 1024 * 1024
+VMEM_BYTES = 60 * 1024 * 1024
 PLANE = ("groups", "dp")
 
 
@@ -447,28 +447,16 @@
     own_tokens = [tokens]
     for _ in range(pairs - 1):
         own_tokens.append(lax.ppermute(own_tokens[-1], "tensor", ring))
-
     weight = jnp.transpose(query_key_value_weight, (1, 0, 2))
     share = weight.shape[1] // plane_size
     piece = lax.dynamic_slice_in_dim(weight, place * share, share, axis=1)
     piece = lax.ppermute(piece, "tensor", to_worker)
-    outer_weight = lax.all_gather(piece, PLANE, axis=0)
-
-    chunk_rows = token_rows // CHUNKS
-    outer_tokens = []
-    previous = piece
-    for chunk in range(CHUNKS):
-        part = after(tokens[chunk * chunk_rows : (chunk + 1) * chunk_rows], previous)
-        previous = lax.ppermute(part, "tensor", to_worker)
-        moving = [previous]
-        for _ in range(pairs - 1):
-            moving.append(lax.ppermute(moving[-1], "tensor", ring))
-        outer_tokens.append(moving)
-
+    up_own = jnp.transpose(adapter_up_maps[0], (1, 0, 2))
+    up_outer = lax.ppermute(up_own, "tensor", to_worker)
+    first = (own_tokens[-1], piece)
+    outer_weight = lax.all_gather(after(piece, own_tokens[-1]), PLANE, axis=0)
     down_all = lax.all_gather(adapter_down_maps, "dp", axis=0, tiled=True)
-    up_own = jnp.transpose(adapter_up_maps[0], (1, 0, 2))
-    up_pair = jnp.stack([up_own, lax.ppermute(up_own, "tensor", to_worker)])
-    up_all = lax.all_gather(up_pair, "dp", axis=0)
+    up_all = lax.all_gather(jnp.stack([up_own, up_outer]), "dp", axis=0)
     out_up_all = lax.all_gather(output_up_maps, "dp", axis=0, tiled=True)
 
     requests = request_adapter.shape[1]
@@ -490,16 +478,16 @@
     cosine, sine = jnp.cos(angles), jnp.sin(angles)
     turn = jnp.concatenate([cosine, cosine, -sine, sine], axis=1)
 
-    shrink = shrink_partial(adapters, table, tokens, down_all)
-    shrink = shrink + lax.ppermute(shrink, "tensor", to_worker)
-    sums = [shrink]
-    for _ in range(pairs - 1):
-        sums.append(lax.ppermute(sums[-1], "tensor", ring))
+    chunk_rows = token_rows // CHUNKS
+    begun = project(worker_ids, [(array,) for array in own_tokens], [weight])
+    outer_first = lax.ppermute(after(tokens[:chunk_rows], *first), "tensor", to_worker)
+    shrink = shrink_partial(adapters, table, after(tokens, *first), down_all)
+    shrink_outer = lax.ppermute(shrink, "tensor", to_worker)
 
     out_share = features // plane_size
-    first = place * out_share
+    line = place * out_share
     piece = lax.dynamic_slice(
-        output_weight, (first % head_size, first // head_size, 0),
+        output_weight, (line % head_size, line // head_size, 0),
         (out_share, 1, output_weight.shape[2]),
     )[:, 0]
     own_weight = jnp.transpose(
@@ -516,44 +504,64 @@
         send = jnp.concatenate([send, out_down], axis=0)
         received.append(
             lax.ppermute(
-                after(send, own_tokens[-1]), "tensor",
+                after(send, *first), "tensor",
                 [(i, (i + turn_by) % planes) for i in range(planes)],
             )
         )
     lot = jnp.concatenate([item[:out_share] for item in received], axis=0)
-    lots = jnp.concatenate(doubled(lot, "groups", group_size), axis=0)
+
+    second = (outer_first, shrink_outer, lot, begun, up_all, out_up_all)
+    outer_tokens = [[outer_first]]
+    for _ in range(pairs - 1):
+        outer_tokens[0].append(lax.ppermute(outer_tokens[0][-1], "tensor", ring))
+    outer_tokens.append([lax.ppermute(after(tokens[chunk_rows:], *second), "tensor", to_worker)])
+    sums = [shrink + shrink_outer]
+    for _ in range(pairs - 1):
+        sums.append(lax.ppermute(sums[-1], "tensor", ring))
+    lots = jnp.concatenate(doubled(after(lot, *second), "groups", group_size), axis=0)
     lots = jnp.concatenate(
         [lots, out_down] + [item[out_share:] for item in received], axis=0
     )
-    halves = list(doubled(lots[None], "dp", dp_size))
-
-    begun = project(worker_ids, [(array,) for array in own_tokens], [weight])
-    own_parts, prior = [], ()
-    for chunk in range(CHUNKS):
-        attended, keys, values = attend(
+
+    third = (outer_tokens[0][-1], sums[-1], outer_tokens[1][0], lots)
+    outer_tokens[1][0] = after(outer_tokens[1][0], *third[:3])
+    for _ in range(pairs - 1):
+        outer_tokens[1].append(lax.ppermute(outer_tokens[1][-1], "tensor", ring))
+    halves = list(doubled(after(lots, *third)[None], "dp", dp_size))
+
+    def own_heads(chunk, prior):
+        return attend(
             outer_ids, adapters, chunk * chunk_rows, table, turn, up_all, 0, sums,
             [(array,) for array in outer_tokens[chunk]], [weight], [begun], prior,
         )
-        prior = (keys, values)
-        own_parts.append(attended)
+
+    def spread(parts, gates):
+        result, moving = [], parts
+        for step in range(pairs):
+            if step:
+                moving = [
+                    lax.ppermute(after(part, *gates), "tensor", ring) for part in moving
+                ]
+            result.append(
+                [(lax.ppermute(part, "tensor", from_worker), part) for part in moving]
+            )
+        return result
+
+    own_first, keys, values = own_heads(0, ())
+    spread_first = spread([own_first], ())
+    own_second, _, _ = own_heads(1, (keys, values))
+    spread_second = spread([own_second], ())
+    gates = (own_second, spread_first[-1][0][1], spread_first[0][0][0], halves[0])
     outer_part, _, _ = attend(
         jnp.concatenate([worker_ids, outer_ids]), adapters, 0, table, turn, up_all, 1, sums,
         [(array,) for array in own_tokens]
         + [
             tuple(outer_tokens[chunk][step] for chunk in range(CHUNKS)) for step in range(pairs)
         ],
-        [outer_weight], [], (),
-    )
-
-    def spread(parts):
-        result, moving = [], parts
-        for step in range(pairs):
-            if step:
-                moving = [lax.ppermute(part, "tensor", ring) for part in moving]
-            result.append(
-                [(lax.ppermute(part, "tensor", from_worker), part) for part in moving]
-            )
-        return result
+        [after(outer_weight, *gates)], [], (),
+    )
+    spread_own = [a + b for a, b in zip(spread_first, spread_second)]
+    spread_outer = spread([outer_part], (spread_second[-1][0][1],))
 
     def lookups(ids):
         return jnp.concatenate(
@@ -568,9 +576,9 @@
 
     weights = [own_weight] + halves
     sizes = (dp_size, group_size, planes, count, rank)
-    begun = project_out(lookups(worker_ids), spread(own_parts), weights, sizes, [], [])
+    begun = project_out(lookups(worker_ids), spread_own, weights, sizes, [], [])
     return project_out(
-        lookups(outer_ids), spread([outer_part]), weights, sizes, list(begun),
+        lookups(outer_ids), spread_outer, weights, sizes, list(begun),
         [table, out_up_all],
     )
 

time: 265 us -> 259 us (0.977)
  starting transfers between devices: 72.3 us -> 48.7 us
  Pallas kernels: 44.5 us -> 56.4 us
  blocking collectives: 16.4 us -> 24.5 us
  local copies, waits for them, and re-layouts: 22.9 us -> 17.3 us
  waiting for transfers between devices: 87.8 us -> 91.8 us
    ppermute x12, starting transfers between devices: 54.6 us -> 28.6 us  [the longest x1 9.54 us: local(): lax.ppermute(after(tokens[chunk_rows:], *second), 'tensor', to_worker)]
    ppermute x12, waiting for transfers between devices: 26.6 us -> 7.16 us  [the longest x1 6.8 us: local(): lax.ppermute(after(tokens[chunk_rows:], *second), 'tensor', to_worker)]
    ppermute x3, waiting for transfers between devices: 3.16 us -> 21.9 us  [doubled(): moved = lax.ppermute(value, axis, [(i, i ^ distance) for i in range(size)])]
    pallas_call x7, Pallas kernels: 44.5 us -> 56.4 us  [call(): pl.pallas_call(kernel, out_shape=out, grid_spec=pltpu.PrefetchScalarGridS...]
    unnamed x37 -> x50, local copies, waits for them, and re-layouts: 10.7 us -> 4.99 us
    ppermute x6, waiting for transfers between devices: 40.5 us -> 45.6 us  [spread(): lax.ppermute(part, 'tensor', from_worker)]
    all_gather x1, blocking collectives: 9.02 us -> 13.6 us  [local(): up_all = lax.all_gather(jnp.stack([up_own, up_outer]), 'dp', axis=0)]
    all_gather x1, blocking collectives: 7.4 us -> 10.8 us  [local(): out_up_all = lax.all_gather(output_up_maps, 'dp', axis=0, tiled=True)]
  transfers between devices with their start and end apart: 26 -> 26, of which waited for: 11 -> 8; matrix products, arithmetic and copies ran while one was open for 8% -> 8% of each run, Pallas kernels for 14% -> 19%
where the time goes in v4:
time: 259 us; the launch traced here: 258 us
  waiting for transfers between devices  91.8 us (35%)
  Pallas kernels  56.4 us (22%)
  starting transfers between devices  48.7 us (19%)
  blocking collectives  24.5 us (9%)
  local copies, waits for them, and re-layouts  17.3 us (7%)
  between operations  13.9 us (5%)
  other arithmetic  5.65 us (2%)
    pallas_call x7, Pallas kernels, call(): pl.pallas_call(kernel, out_shape=out, grid_spec=pltpu.PrefetchScalarGridS...  56.4 us
    ppermute x6, waiting for transfers between devices, spread(): lax.ppermute(part, 'tensor', from_worker)  45.6 us
    ppermute x3, waiting for transfers between devices, doubled(): moved = lax.ppermute(value, axis, [(i, i ^ distance) for i in range(size)])  21.9 us
    ppermute x1, waiting for transfers between devices, local(): piece = lax.ppermute(piece, 'tensor', to_worker)  16.5 us
    all_gather x1, blocking collectives, local(): up_all = lax.all_gather(jnp.stack([up_own, up_outer]), 'dp', axis=0)  13.6 us
    all_gather x1, blocking collectives, local(): out_up_all = lax.all_gather(output_up_maps, 'dp', axis=0, tiled=True)  10.8 us
    ppermute x1, starting transfers between devices, local(): lax.ppermute(after(tokens[chunk_rows:], *second), 'tensor', to_worker)  9.54 us
    ppermute x6, starting transfers between devices, spread(): lax.ppermute(part, 'tensor', from_worker)  8.13 us
  transfers between devices with their start and end apart: 26, of which 8 were waited for; matrix products, arithmetic and copies ran while one was open for 8% of the time, Pallas kernels for 19%

profile of v4, /device:TPU:0, one launch (start us, length us, event | category | flops | bytes accessed | tf_op | source)
XLA Modules:
  0.0 258.3 jit_solution(12610983903063901009)
XLA Ops:
  9.3 7.7 %collective-permute-start.2 = (bf16[6,512,128]{2,1,0:T(8,128)(2,1)S(1)}, bf16[6,512,128]{2,1,0:T(8,128)(2,1)S(1)}, u32[]{:S(2)}, u32[]{:S(2)}) collective-permute-start(bf16[6,512,128]{2,1,0:T(8,128)(2,1)S(1)} %dynamic-slice_bitcast_fusion.1), channel_id=1, source_target_pairs={{0,1},{3,2},{4,5},{7,6},{8,9},{11,10},{12,13},{15,14},{16,17},{19,... | collective-permute-start | bytes 2359304 | tf_op jit(solution)/shard_map/ppermute | solution.py:453
  17.0 16.5 %collective-permute-done.2 = bf16[6,512,128]{2,1,0:T(8,128)(2,1)S(1)} collective-permute-done((bf16[6,512,128]{2,1,0:T(8,128)(2,1)S(1)}, bf16[6,512,128]{2,1,0:T(8,128)(2,1)S(1)}, u32[]{:S(2)}, u32[]{:S(2)}) %collective-permute-start.2) | collective-permute-done | bytes 786464 | tf_op jit(solution)/shard_map/ppermute | solution.py:453
  34.5 5.5 %collective-permute-start = (bf16[6,64,128]{2,1,0:T(8,128)(2,1)S(1)}, bf16[6,64,128]{2,1,0:T(8,128)(2,1)}, u32[]{:S(2)}, u32[]{:S(2)}) collective-permute-start(bf16[6,64,128]{2,1,0:T(8,128)(2,1)S(1)} %bitcast.60), channel_id=1, source_target_pairs={{0,1},{3,2},{4,5},{7,6},{8,9},{11,10},{12,13},{15,14},{16,17},{19,... | collective-permute-start | bytes 294920 | tf_op jit(solution)/shard_map/ppermute | solution.py:455
  41.2 3.0 %fusion.7 = (bf16[64,1,1024]{2,1,0:T(2,128)(2,1)S(1)}, bf16[64,1,1024]{2,1,0:T(2,128)(2,1)S(1)}, bf16[64,1,1024]{2,1,0:T(2,128)(2,1)S(1)}) fusion(bf16[128,4,4096]{2,1,0:T(4,128)(2,1)} %param.11, s32[]{:T(128)S(6)} %select_n.121, s32[]{:T(128)S(6)} %select_n.124, s32[]{:T(128)S(6)} %select_n.127, s32[]{:T(128)S(6)} %select_n.130, s32[]{:T(128)S(6)} %select_n.133), kind=kLoop, calls=%fused_computation.49 | loop fusion | bytes 786452 | tf_op jit(solution)/shard_map/dynamic_slice | solution.py:501
  45.2 10.8 %all_gather.21.refs_10_ = bf16[4,64,1024]{2,1,0:T(8,128)(2,1)} all-gather(bf16[1,64,1024]{2,1,0:T(8,128)(2,1)S(1)} %copy-done.16), channel_id=1, replica_groups=mesh['groups'=2,'dp'=4,'tensor'=4] {'dp'}, dimensions={0}, use_global_device_ids=true | all-gather | bytes 655360 | tf_op jit(solution)/shard_map/all_gather | solution.py:460
  56.7 1.3 collective-permute-start.5
  58.9 2.4 collective-permute-start.8
  62.5 5.9 %shrink.1 = f32[512,192]{1,0:T(8,128)} custom-call(s32[4]{0:T(128)} %iota.39.ids_ref, s32[512,2]{1,0:T(8,128)} %copy.35.table_ref.refs_9_, bf16[512,1024]{1,0:T(8,128)(2,1)} %refs_2_.1, bf16[4,192,1024]{2,1,0:T(8,128)(2,1)} %all-gather.5.cloned.1.call-done.down_ref), custom_call_target="tpu_custom_call" | custom-call | flops 1000 | bytes 1000 | tf_op jit(solution)/shard_map/shrink/pallas_call | solution.py:166
  68.4 4.4 %collective-permute-start.3 = (f32[512,192]{1,0:T(8,128)}, f32[512,192]{1,0:T(8,128)S(1)}, u32[]{:S(2)}, u32[]{:S(2)}) collective-permute-start(f32[512,192]{1,0:T(8,128)} %shrink.1), channel_id=1, source_target_pairs={{0,1},{3,2},{4,5},{7,6},{8,9},{11,10},{12,13},{15,14},{16,17},{19,... | collective-permute-start | bytes 1179656 | tf_op jit(solution)/shard_map/ppermute | solution.py:485
  72.8 13.6 %all-gather = bf16[8,6,64,128]{3,2,1,0:T(8,128)(2,1)} all-gather(bf16[2,6,64,128]{3,2,1,0:T(8,128)(2,1)S(1)} %pad_maximum_fusion.6), channel_id=2, replica_groups=mesh['groups'=2,'dp'=4,'tensor'=4] {'dp'}, dimensions={0}, use_global_device_ids=true | all-gather | bytes 983040 | tf_op jit(solution)/shard_map/all_gather | solution.py:459
  86.4 6.0 %project.1.refs_5_ = f32[512,768]{1,0:T(8,128)} custom-call(s32[2]{0:T(128)} %get-tuple-element.44.ids_ref, bf16[512,1024]{1,0:T(8,128)(2,1)} %refs_2_.1, bf16[512,1024]{1,0:T(8,128)(2,1)} %copy-done.4, bf16[6,4096,128]{2,1,0:T(8,128)(2,1)} %bitcast.44), custom_call_target="tpu_custom_call" | custom-call | flops 1000 | bytes 1000 | tf_op jit(solution)/shard_map/project/pallas_call | solution.py:166
  93.9 1.5 collective-permute-start.14
  96.8 9.5 %collective-permute-start.9 = (bf16[256,1024]{1,0:T(8,128)(2,1)S(1)}, bf16[256,1024]{1,0:T(8,128)(2,1)}, u32[]{:S(2)}, u32[]{:S(2)}) collective-permute-start(bf16[256,1024]{1,0:T(8,128)(2,1)S(1)} %get-tuple-element.29), channel_id=1, source_target_pairs={{0,1},{3,2},{4,5},{7,6},{8,9},{11,10},{12,13},{15,14},{16,17},{19,... | collective-permute-start | bytes 1572872 | tf_op jit(solution)/shard_map/ppermute | solution.py:517
  109.0 6.8 %collective-permute-done.9.refs_2_.refs_5_ = bf16[256,1024]{1,0:T(8,128)(2,1)} collective-permute-done((bf16[256,1024]{1,0:T(8,128)(2,1)S(1)}, bf16[256,1024]{1,0:T(8,128)(2,1)}, u32[]{:S(2)}, u32[]{:S(2)}) %collective-permute-start.9) | collective-permute-done | bytes 524320 | tf_op jit(solution)/shard_map/ppermute | solution.py:517
  117.0 21.9 %collective-permute-done.15 = bf16[1,512,1024]{2,1,0:T(8,128)(2,1)S(1)} collective-permute-done((bf16[1,512,1024]{2,1,0:T(8,128)(2,1)S(1)}, bf16[1,512,1024]{2,1,0:T(8,128)(2,1)S(1)}, u32[]{:S(2)}, u32[]{:S(2)}) %collective-permute-start.15) | collective-permute-done | bytes 1048608 | tf_op jit(solution)/shard_map/ppermute | solution.py:390
  142.6 7.1 %attend.3 = (bf16[256,512]{1,0:T(8,128)(2,1)}, bf16[256,128]{1,0:T(8,128)(2,1)}, bf16[256,128]{1,0:T(8,128)(2,1)}) custom-call(s32[6]{0:T(128)} %pad_add_fusion.2.ids_ref, s32[512,2]{1,0:T(8,128)} %copy.35.table_ref.refs_9_, f32[512,256]{1,0:T(8,128)} %pad_maximum_fusion.1.turn_ref, bf16[4,2,6,64,128]{4,3,2,1,0:T(8,128)(2,1)} %bitcast.47, ...), custom_call_target="tpu_custom_call" | custom-call | flops 1000 | bytes 1000 | tf_op jit(solution)/shard_map/attend/pallas_call | solution.py:166
  150.4 1.5 collective-permute-start.13
  152.7 7.8 %attend.4 = (bf16[256,512]{1,0:T(8,128)(2,1)}, bf16[256,128]{1,0:T(8,128)(2,1)}, bf16[256,128]{1,0:T(8,128)(2,1)}) custom-call(s32[6]{0:T(128)} %pad_add_fusion.2.ids_ref, s32[512,2]{1,0:T(8,128)} %copy.35.table_ref.refs_9_, f32[512,256]{1,0:T(8,128)} %pad_maximum_fusion.1.turn_ref, bf16[4,2,6,64,128]{4,3,2,1,0:T(8,128)(2,1)} %bitcast.48, ...), custom_call_target="tpu_custom_call" | custom-call | flops 1000 | bytes 1000 | tf_op jit(solution)/shard_map/attend/pallas_call | solution.py:166
  160.5 1.4 collective-permute-start.17
  162.4 9.2 %collective-permute-done.13.refs_0_ = bf16[256,512]{1,0:T(8,128)(2,1)S(1)} collective-permute-done((bf16[256,512]{1,0:T(8,128)(2,1)}, bf16[256,512]{1,0:T(8,128)(2,1)S(1)}, u32[]{:S(2)}, u32[]{:S(2)}) %collective-permute-start.13) | collective-permute-done | bytes 262176 | tf_op jit(solution)/shard_map/ppermute | solution.py:546
  171.6 13.9 %attend.5 = (bf16[512,512]{1,0:T(8,128)(2,1)}, bf16[512,128]{1,0:T(8,128)(2,1)}, bf16[512,128]{1,0:T(8,128)(2,1)}) custom-call(s32[8]{0:T(128)} %concatenate.41.ids_ref, s32[512,2]{1,0:T(8,128)} %copy.35.table_ref.refs_9_, f32[512,256]{1,0:T(8,128)} %pad_maximum_fusion.1.turn_ref, bf16[4,2,6,64,128]{4,3,2,1,0:T(8,128)(2,1)} %bitcast.49, ...), custom_call_target="tpu_custom_call" | custom-call | flops 1000 | bytes 1000 | tf_op jit(solution)/shard_map/attend/pallas_call | solution.py:166
  185.5 1.5 collective-permute-start.18
  188.3 1.3 collective-permute-start.16
  189.6 1.3 collective-permute-start.19
  192.2 10.5 %collective-permute-done.22.refs_4_ = bf16[256,512]{1,0:T(8,128)(2,1)S(1)} collective-permute-done((bf16[256,512]{1,0:T(8,128)(2,1)S(1)}, bf16[256,512]{1,0:T(8,128)(2,1)S(1)}, u32[]{:S(2)}, u32[]{:S(2)}) %collective-permute-start.22) | collective-permute-done | bytes 262176 | tf_op jit(solution)/shard_map/ppermute | solution.py:546
  203.4 1.5 collective-permute-start.23
  204.9 1.6 dynamic-slice_bitcast_fusion
  206.5 1.3 copy.36
  209.1 21.8 %collective-permute-done.21.refs_2_ = bf16[256,512]{1,0:T(8,128)(2,1)} collective-permute-done((bf16[256,512]{1,0:T(8,128)(2,1)}, bf16[256,512]{1,0:T(8,128)(2,1)}, u32[]{:S(2)}, u32[]{:S(2)}) %collective-permute-start.21) | collective-permute-done | bytes 262176 | tf_op jit(solution)/shard_map/ppermute | solution.py:546
  230.9 4.1 %collective-permute-done.23.refs_6_ = bf16[256,512]{1,0:T(8,128)(2,1)S(1)} collective-permute-done((bf16[256,512]{1,0:T(8,128)(2,1)}, bf16[256,512]{1,0:T(8,128)(2,1)S(1)}, u32[]{:S(2)}, u32[]{:S(2)}) %collective-permute-start.23) | collective-permute-done | bytes 262176 | tf_op jit(solution)/shard_map/ppermute | solution.py:546
  235.7 7.5 %project_out.2 = (f32[512,1024]{1,0:T(8,128)}, f32[512,256]{1,0:T(8,128)}) custom-call(s32[16]{0:T(128)} %concatenate.51.ids_ref, bf16[256,512]{1,0:T(8,128)(2,1)} %copy-done.11, bf16[256,512]{1,0:T(8,128)(2,1)} %get-tuple-element.35.refs_1_, bf16[256,512]{1,0:T(8,128)(2,1)} %collective-permute-done.21.refs_2_, bf16[256,512]{1,0:T(8,128)(2,1)} %get-tuple-element.34.refs_3_, ...), custom_call_target="tpu_custom_call" | custom-call | flops 1000 | bytes 1000 | tf_op jit(solution)/shard_map/project_out/pallas_call | solution.py:166
  243.2 8.2 %project_out.3 = bf16[512,1024]{1,0:T(8,128)(2,1)} custom-call(s32[16]{0:T(128)} %concatenate.40.ids_ref, bf16[512,512]{1,0:T(8,128)(2,1)} %collective-permute-done.16.refs_0_, bf16[512,512]{1,0:T(8,128)(2,1)} %get-tuple-element.40.refs_1_, bf16[512,512]{1,0:T(8,128)(2,1)} %collective-permute-done.19.refs_2_, ...), custom_call_target="tpu_custom_call" | custom-call | flops 1000 | bytes 1000 | tf_op jit(solution)/shard_map/project_out/pallas_call | solution.py:166
  (121 shorter events, 26.2 us)
Async XLA Ops:
  6.5 27.9 %copy-start.17 = (bf16[1,64,6,128]{3,1,2,0:T(8,128)(2,1)S(1)}, bf16[1,64,6,128]{3,1,2,0:T(8,128)(2,1)}, u32[]{:S(2)}) copy-start(bf16[1,64,6,128]{3,1,2,0:T(8,128)(2,1)} %param.13) | copy-start | bytes 294916
  6.5 33.4 %copy-start.20 = (s32[1,4]{1,0:T(1,128)S(1)}, s32[1,4]{1,0:T(1,128)}, u32[]{:S(2)}) copy-start(s32[1,4]{1,0:T(1,128)} %param.17) | copy-start | bytes 52
  6.5 33.6 %copy-start.19 = (s32[1,4]{1,0:T(1,128)S(1)}, s32[1,4]{1,0:T(1,128)}, u32[]{:S(2)}) copy-start(s32[1,4]{1,0:T(1,128)} %param.16) | copy-start | bytes 52
  6.5 55.4 %all-gather.5.cloned.1.call-start = ((), (), s32[]{:S(2)}) async-start(), calls=%async_computation | async-start | bytes 1966080 | tf_op jit(solution)/shard_map/all_gather | solution.py:458
  7.3 164.4 %all-gather.7.cloned.1.call-start = ((), (), s32[]{:S(2)}) async-start(), calls=%async_computation.1 | async-start | bytes 7077888 | tf_op jit(solution)/shard_map/all_gather | solution.py:457
  7.3 26.2 %collective-permute-start.1 = (bf16[512,1024]{1,0:T(8,128)(2,1)}, bf16[512,1024]{1,0:T(8,128)(2,1)S(1)}, u32[]{:S(2)}, u32[]{:S(2)}) collective-permute-start(bf16[512,1024]{1,0:T(8,128)(2,1)} %refs_2_.1), channel_id=1, source_target_pairs={{1,2},{2,1},{5,6},{6,5},{9,10},{10,9},{13,14},{14,13},{17,18},{18,... | collective-permute-start | bytes 3145736 | tf_op jit(solution)/shard_map/ppermute | solution.py:449
  8.1 36.2 %copy-start.18 = (bf16[1,64,4,128]{3,2,1,0:T(4,128)(2,1)S(1)}, bf16[1,64,4,128]{3,2,1,0:T(4,128)(2,1)}, u32[]{:S(2)}) copy-start(bf16[1,64,4,128]{3,2,1,0:T(4,128)(2,1)} %param.14) | copy-start | bytes 196612
  9.3 24.2 %collective-permute-start.2 = (bf16[6,512,128]{2,1,0:T(8,128)(2,1)S(1)}, bf16[6,512,128]{2,1,0:T(8,128)(2,1)S(1)}, u32[]{:S(2)}, u32[]{:S(2)}) collective-permute-start(bf16[6,512,128]{2,1,0:T(8,128)(2,1)S(1)} %dynamic-slice_bitcast_fusion.1), channel_id=1, source_target_pairs={{0,1},{3,2},{4,5},{7,6},{8,9},{11,10},{12,13},{15,14},{16,17},{19,... | collective-permute-start | bytes 2359304 | tf_op jit(solution)/shard_map/ppermute | solution.py:453
  34.5 23.5 %collective-permute-start = (bf16[6,64,128]{2,1,0:T(8,128)(2,1)S(1)}, bf16[6,64,128]{2,1,0:T(8,128)(2,1)}, u32[]{:S(2)}, u32[]{:S(2)}) collective-permute-start(bf16[6,64,128]{2,1,0:T(8,128)(2,1)S(1)} %bitcast.60), channel_id=1, source_target_pairs={{0,1},{3,2},{4,5},{7,6},{8,9},{11,10},{12,13},{15,14},{16,17},{19,... | collective-permute-start | bytes 294920 | tf_op jit(solution)/shard_map/ppermute | solution.py:455
  56.7 36.9 %collective-permute-start.5 = (bf16[256,1024]{1,0:T(8,128)(2,1)S(1)}, bf16[256,1024]{1,0:T(8,128)(2,1)S(1)}, u32[]{:S(2)}, u32[]{:S(2)}) collective-permute-start(bf16[256,1024]{1,0:T(8,128)(2,1)S(1)} %get-tuple-element.25), channel_id=1, source_target_pairs={{0,1},{3,2},{4,5},{7,6},{8,9},{11,10},{12,13},{15,14},{16,17},{19,... | collective-permute-start | bytes 1572872 | tf_op jit(solution)/shard_map/ppermute | solution.py:483
  58.9 33.5 %collective-permute-start.8 = (bf16[96,1024]{1,0:T(8,128)(2,1)}, bf16[96,1024]{1,0:T(8,128)(2,1)S(1)}, u32[]{:S(2)}, u32[]{:S(2)}) collective-permute-start(bf16[96,1024]{1,0:T(8,128)(2,1)} %get-tuple-element.28), channel_id=1, source_target_pairs={{0,3},{1,0},{2,1},{3,2},{4,7},{5,4},{6,5},{7,6},{8,11},{9,8},{10,9... | collective-permute-start | bytes 589832 | tf_op jit(solution)/shard_map/ppermute | solution.py:506
  61.3 31.1 %collective-permute-start.7 = (bf16[96,1024]{1,0:T(8,128)(2,1)S(1)}, bf16[96,1024]{1,0:T(8,128)(2,1)S(1)}, u32[]{:S(2)}, u32[]{:S(2)}) collective-permute-start(bf16[96,1024]{1,0:T(8,128)(2,1)S(1)} %get-tuple-element.27), channel_id=1, source_target_pairs={{0,2},{1,3},{2,0},{3,1},{4,6},{5,7},{6,4},{7,5},{8,10},{9,11},{10,... | collective-permute-start | bytes 589832 | tf_op jit(solution)/shard_map/ppermute | solution.py:506
  61.3 31.2 %collective-permute-start.6 = (bf16[96,1024]{1,0:T(8,128)(2,1)S(1)}, bf16[96,1024]{1,0:T(8,128)(2,1)}, u32[]{:S(2)}, u32[]{:S(2)}) collective-permute-start(bf16[96,1024]{1,0:T(8,128)(2,1)S(1)} %get-tuple-element.26), channel_id=1, source_target_pairs={{0,1},{1,2},{2,3},{3,0},{4,5},{5,6},{6,7},{7,4},{8,9},{9,10},{10,1... | collective-permute-start | bytes 589832 | tf_op jit(solution)/shard_map/ppermute | solution.py:506
  68.4 25.5 %collective-permute-start.3 = (f32[512,192]{1,0:T(8,128)}, f32[512,192]{1,0:T(8,128)S(1)}, u32[]{:S(2)}, u32[]{:S(2)}) collective-permute-start(f32[512,192]{1,0:T(8,128)} %shrink.1), channel_id=1, source_target_pairs={{0,1},{3,2},{4,5},{7,6},{8,9},{11,10},{12,13},{15,14},{16,17},{19,... | collective-permute-start | bytes 1179656 | tf_op jit(solution)/shard_map/ppermute | solution.py:485
  93.9 12.5 %collective-permute-start.14 = (bf16[192,1024]{1,0:T(8,128)(2,1)S(1)}, bf16[192,1024]{1,0:T(8,128)(2,1)S(1)}, u32[]{:S(2)}, u32[]{:S(2)}) collective-permute-start(bf16[192,1024]{1,0:T(8,128)(2,1)S(1)} %pad_maximum_fusion.2), channel_id=1, source_target_pairs={{0,16},{16,0},{1,17},{17,1},{2,18},{18,2},{3,19},{19,3},{4,20},{20... | collective-permute-start | bytes 1179656 | tf_op jit(solution)/shard_map/ppermute | solution.py:390
  95.3 13.7 %collective-permute-start.10 = (bf16[256,1024]{1,0:T(8,128)(2,1)S(1)}, bf16[256,1024]{1,0:T(8,128)(2,1)S(1)}, u32[]{:S(2)}, u32[]{:S(2)}) collective-permute-start(bf16[256,1024]{1,0:T(8,128)(2,1)S(1)} %collective-permute-done.5.refs_2_.refs_4_), channel_id=1, source_target_pairs={{1,2},{2,1},{5,6},{6,5},{9,10},{10,9},{13,14},{14,13},{17,18},{18,... | collective-permute-start | bytes 1572872 | tf_op jit(solution)/shard_map/ppermute | solution.py:516
  96.1 43.0 %copy-start.2 = (f32[512,192]{1,0:T(8,128)}, f32[512,192]{1,0:T(8,128)S(1)}, u32[]{:S(2)}) copy-start(f32[512,192]{1,0:T(8,128)S(1)} %add.140.refs_0_) | copy-start | bytes 1179652
  96.1 12.9 %collective-permute-start.4 = (f32[512,192]{1,0:T(8,128)S(1)}, f32[512,192]{1,0:T(8,128)S(1)}, u32[]{:S(2)}, u32[]{:S(2)}) collective-permute-start(f32[512,192]{1,0:T(8,128)S(1)} %add.140.refs_0_), channel_id=1, source_target_pairs={{1,2},{2,1},{5,6},{6,5},{9,10},{10,9},{13,14},{14,13},{17,18},{18,... | collective-permute-start | bytes 1179656 | tf_op jit(solution)/shard_map/ppermute | solution.py:520
  96.8 19.0 %collective-permute-start.9 = (bf16[256,1024]{1,0:T(8,128)(2,1)S(1)}, bf16[256,1024]{1,0:T(8,128)(2,1)}, u32[]{:S(2)}, u32[]{:S(2)}) collective-permute-start(bf16[256,1024]{1,0:T(8,128)(2,1)S(1)} %get-tuple-element.29), channel_id=1, source_target_pairs={{0,1},{3,2},{4,5},{7,6},{8,9},{11,10},{12,13},{15,14},{16,17},{19,... | collective-permute-start | bytes 1572872 | tf_op jit(solution)/shard_map/ppermute | solution.py:517
  109.0 30.1 %copy-start.3 = (f32[512,192]{1,0:T(8,128)}, f32[512,192]{1,0:T(8,128)S(1)}, u32[]{:S(2)}) copy-start(f32[512,192]{1,0:T(8,128)S(1)} %collective-permute-done.4.refs_1_) | copy-start | bytes 1179652
  115.8 23.1 %collective-permute-start.15 = (bf16[1,512,1024]{2,1,0:T(8,128)(2,1)S(1)}, bf16[1,512,1024]{2,1,0:T(8,128)(2,1)S(1)}, u32[]{:S(2)}, u32[]{:S(2)}) collective-permute-start(bf16[1,512,1024]{2,1,0:T(8,128)(2,1)S(1)} %bitcast.53), channel_id=1, source_target_pairs={{0,8},{4,12},{8,0},{12,4},{1,9},{5,13},{9,1},{13,5},{2,10},{6,14},... | collective-permute-start | bytes 3145736 | tf_op jit(solution)/shard_map/ppermute | solution.py:390
  139.1 95.9 %collective-permute-start.20 = (bf16[2,512,1024]{2,1,0:T(8,128)(2,1)S(1)}, bf16[2,512,1024]{2,1,0:T(8,128)(2,1)}, u32[]{:S(2)}, u32[]{:S(2)}) collective-permute-start(bf16[2,512,1024]{2,1,0:T(8,128)(2,1)S(1)} %pad_maximum_fusion.refs_9_.refs_5_), channel_id=1, source_target_pairs={{0,4},{4,0},{8,12},{12,8},{1,5},{5,1},{9,13},{13,9},{2,6},{6,2},{1... | collective-permute-start | bytes 6291464 | tf_op jit(solution)/shard_map/ppermute | solution.py:394
  139.2 12.6 %collective-permute-start.11 = (bf16[256,1024]{1,0:T(8,128)(2,1)}, bf16[256,1024]{1,0:T(8,128)(2,1)S(1)}, u32[]{:S(2)}, u32[]{:S(2)}) collective-permute-start(bf16[256,1024]{1,0:T(8,128)(2,1)} %collective-permute-done.9.refs_2_.refs_5_), channel_id=1, source_target_pairs={{1,2},{2,1},{5,6},{6,5},{9,10},{10,9},{13,14},{14,13},{17,18},{18,... | collective-permute-start | bytes 1572872 | tf_op jit(solution)/shard_map/ppermute | solution.py:529
  149.7 12.7 %collective-permute-start.12 = (bf16[256,512]{1,0:T(8,128)(2,1)}, bf16[256,512]{1,0:T(8,128)(2,1)S(1)}, u32[]{:S(2)}, u32[]{:S(2)}) collective-permute-start(bf16[256,512]{1,0:T(8,128)(2,1)} %get-tuple-element.35.refs_1_), channel_id=1, source_target_pairs={{1,2},{2,1},{5,6},{6,5},{9,10},{10,9},{13,14},{14,13},{17,18},{18,... | collective-permute-start | bytes 786440 | tf_op jit(solution)/shard_map/ppermute | solution.py:543
  150.4 21.2 %collective-permute-start.13 = (bf16[256,512]{1,0:T(8,128)(2,1)}, bf16[256,512]{1,0:T(8,128)(2,1)S(1)}, u32[]{:S(2)}, u32[]{:S(2)}) collective-permute-start(bf16[256,512]{1,0:T(8,128)(2,1)} %get-tuple-element.35.refs_1_), channel_id=1, source_target_pairs={{1,0},{2,3},{5,4},{6,7},{9,8},{10,11},{13,12},{14,15},{17,16},{18,... | collective-permute-start | bytes 786440 | tf_op jit(solution)/shard_map/ppermute | solution.py:546
  160.5 25.1 %collective-permute-start.17 = (bf16[256,512]{1,0:T(8,128)(2,1)}, bf16[256,512]{1,0:T(8,128)(2,1)}, u32[]{:S(2)}, u32[]{:S(2)}) collective-permute-start(bf16[256,512]{1,0:T(8,128)(2,1)} %get-tuple-element.34.refs_3_), channel_id=1, source_target_pairs={{1,2},{2,1},{5,6},{6,5},{9,10},{10,9},{13,14},{14,13},{17,18},{18,... | collective-permute-start | bytes 786440 | tf_op jit(solution)/shard_map/ppermute | solution.py:543
  185.5 4.1 %collective-permute-start.18 = (bf16[512,512]{1,0:T(8,128)(2,1)}, bf16[512,512]{1,0:T(8,128)(2,1)}, u32[]{:S(2)}, u32[]{:S(2)}) collective-permute-start(bf16[512,512]{1,0:T(8,128)(2,1)} %get-tuple-element.40.refs_1_), channel_id=1, source_target_pairs={{1,2},{2,1},{5,6},{6,5},{9,10},{10,9},{13,14},{14,13},{17,18},{18,... | collective-permute-start | bytes 1572872 | tf_op jit(solution)/shard_map/ppermute | solution.py:543
  187.0 15.7 %collective-permute-start.22 = (bf16[256,512]{1,0:T(8,128)(2,1)S(1)}, bf16[256,512]{1,0:T(8,128)(2,1)S(1)}, u32[]{:S(2)}, u32[]{:S(2)}) collective-permute-start(bf16[256,512]{1,0:T(8,128)(2,1)S(1)} %collective-permute-done.12.refs_5_), channel_id=1, source_target_pairs={{1,0},{2,3},{5,4},{6,7},{9,8},{10,11},{13,12},{14,15},{17,16},{18,... | collective-permute-start | bytes 786440 | tf_op jit(solution)/shard_map/ppermute | solution.py:546
  188.3 55.0 %collective-permute-start.16 = (bf16[512,512]{1,0:T(8,128)(2,1)}, bf16[512,512]{1,0:T(8,128)(2,1)}, u32[]{:S(2)}, u32[]{:S(2)}) collective-permute-start(bf16[512,512]{1,0:T(8,128)(2,1)} %get-tuple-element.40.refs_1_), channel_id=1, source_target_pairs={{1,0},{2,3},{5,4},{6,7},{9,8},{10,11},{13,12},{14,15},{17,16},{18,... | collective-permute-start | bytes 1572872 | tf_op jit(solution)/shard_map/ppermute | solution.py:546
  189.6 53.6 %collective-permute-start.19 = (bf16[512,512]{1,0:T(8,128)(2,1)}, bf16[512,512]{1,0:T(8,128)(2,1)}, u32[]{:S(2)}, u32[]{:S(2)}) collective-permute-start(bf16[512,512]{1,0:T(8,128)(2,1)} %collective-permute-done.18.refs_3_), channel_id=1, source_target_pairs={{1,0},{2,3},{5,4},{6,7},{9,8},{10,11},{13,12},{14,15},{17,16},{18,... | collective-permute-start | bytes 1572872 | tf_op jit(solution)/shard_map/ppermute | solution.py:546
  190.9 40.0 %collective-permute-start.21 = (bf16[256,512]{1,0:T(8,128)(2,1)}, bf16[256,512]{1,0:T(8,128)(2,1)}, u32[]{:S(2)}, u32[]{:S(2)}) collective-permute-start(bf16[256,512]{1,0:T(8,128)(2,1)} %get-tuple-element.34.refs_3_), channel_id=1, source_target_pairs={{1,0},{2,3},{5,4},{6,7},{9,8},{10,11},{13,12},{14,15},{17,16},{18,... | collective-permute-start | bytes 786440 | tf_op jit(solution)/shard_map/ppermute | solution.py:546
  203.4 31.6 %collective-permute-start.23 = (bf16[256,512]{1,0:T(8,128)(2,1)}, bf16[256,512]{1,0:T(8,128)(2,1)S(1)}, u32[]{:S(2)}, u32[]{:S(2)}) collective-permute-start(bf16[256,512]{1,0:T(8,128)(2,1)} %collective-permute-done.17.refs_7_), channel_id=1, source_target_pairs={{1,0},{2,3},{5,4},{6,7},{9,8},{10,11},{13,12},{14,15},{17,16},{18,... | collective-permute-start | bytes 786440 | tf_op jit(solution)/shard_map/ppermute | solution.py:546
  (15 other events, 125.9 us)
Sparse Core Ops, SparseCore 0:
  8.9 22.3 all-gather.4
  34.6 53.4 all-gather.6

commit v5 on v4

--- a/solution.py
+++ b/solution.py
@@ -9,7 +9,7 @@
 from jax.sharding import PartitionSpec as P
 
 CHUNKS = 2
-VMEM_BYTES = 60 * 1024 * 1024
+VMEM_BYTES = 40 * 1024 * 1024
 PLANE = ("groups", "dp")
 
 
@@ -17,22 +17,21 @@
     return lax.optimization_barrier((value,) + earlier)[0]
 
 
-def wide_slots(w_refs, pair):
-    if len(w_refs[0].shape) == 3:
-        parts = [w_ref[...] for w_ref in w_refs]
+def wide_slots(w_ref, depth, pair):
+    if len(w_ref.shape) == 3:
+        parts = [w_ref]
     else:
-        parts = [
-            w_ref[piece] for piece in range(w_refs[0].shape[0]) for w_ref in w_refs
-        ]
+        parts = [w_ref.at[piece, :, : depth // w_ref.shape[0]] for piece in range(w_ref.shape[0])]
     wide = [jnp.concatenate([part[2 * pair], part[2 * pair + 1]], axis=1) for part in parts]
     return wide[0] if len(wide) == 1 else jnp.concatenate(wide, axis=0)
 
 
-def accumulate(acc_ref, token_refs, w_refs, first):
-    slots, _, head_size = w_refs[0].shape[-3:]
+def accumulate(acc_ref, token_refs, w_ref, first):
+    slots, _, head_size = w_ref.shape[-3:]
+    depth = token_refs[0].shape[1]
     for pair in range(slots // 2):
         columns = slice(2 * pair * head_size, (2 * pair + 2) * head_size)
-        weight = wide_slots(w_refs, pair)
+        weight = wide_slots(w_ref, depth, pair)
         row = 0
         for token_ref in token_refs:
             rows = slice(row, row + token_ref.shape[0])
@@ -52,28 +51,32 @@
     return groups, refs[at:]
 
 
-def project_kernel(layout, weights, ids_ref, *refs):
-    tokens, rest = split_refs(refs, layout)
-    w_refs, acc_ref = rest[:weights], rest[weights]
+def project_kernel(layout, ids_ref, *refs):
+    tokens, (w_ref, acc_ref) = split_refs(refs, layout)
     step = pl.program_id(0)
     for number, token_refs in enumerate(tokens):
         pl.when(step == number)(
             functools.partial(
-                accumulate, acc_ref, token_refs, w_refs, acc_ref if number else None
+                accumulate, acc_ref, token_refs, w_ref, acc_ref if number else None
             )
         )
 
 
-def attend_kernel(layout, weights, sums, started, which, ids_ref, table_ref, turn_ref, up_ref, *refs):
+def attend_kernel(
+    layout, sums, started, ids_ref, table_ref, turn_ref, up_ref, *refs
+):
     sum_refs, refs = refs[:sums], refs[sums:]
     tokens, rest = split_refs(refs, layout)
-    w_refs, rest = rest[:weights], rest[weights:]
-    begun, prior, rest = rest[:started[0]], rest[started[0] : started[0] + started[1]], rest[sum(started) :]
+    w_ref, rest = rest[0], rest[1:]
+    begun, prior, rest = (
+        rest[: started[0]], rest[started[0] : sum(started)], rest[sum(started) :]
+    )
     attended_ref, keys_ref, values_ref, acc_ref = rest
     first_row = prior[0].shape[0] if prior else 0
-    slots, _, head_size = w_refs[0].shape[-3:]
-    rank = up_ref.shape[3]
-    count = ids_ref.shape[0] - len(layout)
+    slots, _, head_size = w_ref.shape[-3:]
+    rank = up_ref.shape[2]
+    at_adapter = len(layout) + 1
+    count = ids_ref.shape[0] - at_adapter
     step = pl.program_id(0)
     rows = acc_ref.shape[0]
     block = min(rows, 256)
@@ -82,14 +85,14 @@
     for number, token_refs in enumerate(tokens):
         first = acc_ref if number else (begun[0] if begun else None)
         pl.when(step == number)(
-            functools.partial(accumulate, acc_ref, token_refs, w_refs, first)
+            functools.partial(accumulate, acc_ref, token_refs, w_ref, first)
         )
 
     @pl.when(step == len(layout) - 1)
     def _():
         ups = [
             jnp.concatenate(
-                [up_ref[ids_ref[len(layout) + j], which, index] for j in range(count)], axis=0
+                [up_ref[ids_ref[at_adapter + j], index] for j in range(count)], axis=0
             )
             for index in range(slots)
         ]
@@ -142,15 +145,13 @@
                 )
 
 
-def weight_specs(weights, depth):
-    if len(weights[0].shape) == 3:
-        slots, _, head_size = weights[0].shape
-        return [pl.BlockSpec((slots, depth, head_size), lambda step, ids: (0, ids[step], 0))]
-    pieces = depth // sum(weight.shape[2] for weight in weights)
-    return [
-        pl.BlockSpec((pieces,) + weight.shape[1:], lambda step, ids: (ids[step], 0, 0, 0))
-        for weight in weights
-    ]
+def weight_spec(weight, tokens):
+    depth = tokens[0][0].shape[1]
+    if len(weight.shape) == 3:
+        slots, _, head_size = weight.shape
+        return pl.BlockSpec((slots, depth, head_size), lambda step, ids: (0, ids[step], 0))
+    pieces = weight.shape[0] // len(tokens)
+    return pl.BlockSpec((pieces,) + weight.shape[1:], lambda step, ids: (ids[step], 0, 0, 0))
 
 
 def fixed(array):
@@ -159,10 +160,10 @@
 
 
 PARAMS = pltpu.CompilerParams(vmem_limit_bytes=VMEM_BYTES)
-COST = pl.CostEstimate(flops=1000, bytes_accessed=1000, transcendentals=0)
 
 
 def call(kernel, name, ids, grid, specs, arrays, out, scratch=()):
+    total = sum(array.size * array.dtype.itemsize for array in arrays)
     return pl.pallas_call(
         kernel,
         out_shape=out,
@@ -174,31 +175,29 @@
             scratch_shapes=list(scratch),
         ),
         compiler_params=PARAMS,
-        cost_estimate=COST,
+        cost_estimate=pl.CostEstimate(flops=0, bytes_accessed=3 * total, transcendentals=0),
         name=name,
     )(ids, *arrays)
 
 
-def project(ids, tokens, weights):
-    depth = tokens[0][0].shape[1]
+def project(ids, tokens, weight):
     rows = sum(part.shape[0] for part in tokens[0])
-    slots, _, head_size = weights[0].shape[-3:]
+    slots, _, head_size = weight.shape[-3:]
     parts = [part for item in tokens for part in item]
     return call(
-        functools.partial(project_kernel, [len(item) for item in tokens], len(weights)),
+        functools.partial(project_kernel, [len(item) for item in tokens]),
         "project",
         ids,
         len(tokens),
-        [None] * len(parts) + weight_specs(weights, depth),
-        parts + weights,
+        [None] * len(parts) + [weight_spec(weight, tokens)],
+        parts + [weight],
         jax.ShapeDtypeStruct((rows, slots * head_size), jnp.float32),
     )
 
 
-def attend(ids, adapters, row, table, turn, up, which, sums, tokens, weights, begun, prior):
-    depth = tokens[0][0].shape[1]
+def attend(ids, group, adapters, dp_size, row, table, turn, up, rank, sums, tokens, weight, begun, prior):
     rows = sum(part.shape[0] for part in tokens[0])
-    slots, _, head_size = weights[0].shape[-3:]
+    slots, _, head_size = weight.shape[-3:]
     out = (
         jax.ShapeDtypeStruct((rows, (slots - 2) * head_size), jnp.bfloat16),
         jax.ShapeDtypeStruct((rows, head_size), jnp.bfloat16),
@@ -209,24 +208,30 @@
     def rows_of(array):
         return pl.BlockSpec((rows, array.shape[1]), lambda step, ids: (row // rows, 0))
 
+    last = up.shape[2] // rank - 1
+    group_at = len(tokens)
+    up_spec = pl.BlockSpec(
+        (dp_size, slots, rank, head_size),
+        lambda step, ids: (ids[group_at] if up.shape[0] > dp_size else 0, 0, last, 0),
+    )
     tables = [table, turn]
     started = (len(begun), len(prior))
-    arrays = tables + [up] + sums + parts + weights + begun + list(prior)
+    arrays = tables + [up] + sums + parts + [weight] + begun + list(prior)
     specs = (
         [rows_of(array) for array in tables]
-        + [None]
+        + [up_spec]
         + [rows_of(array) for array in sums]
         + [None] * len(parts)
-        + weight_specs(weights, depth)
+        + [weight_spec(weight, tokens)]
         + [rows_of(array) for array in begun]
         + [None] * len(prior)
     )
     return call(
         functools.partial(
-            attend_kernel, [len(item) for item in tokens], len(weights), len(sums), started, which
+            attend_kernel, [len(item) for item in tokens], len(sums), started
         ),
         "attend",
-        jnp.concatenate([ids, adapters]),
+        jnp.concatenate([ids, group.astype(jnp.int32)[None], adapters]),
         len(tokens),
         specs,
         arrays,
@@ -385,9 +390,10 @@
     )
 
 
-def doubled(value, axis, size):
+def doubled(value, axis, size, moved=None):
     distance = size // 2
-    moved = lax.ppermute(value, axis, [(i, i ^ distance) for i in range(size)])
+    if moved is None:
+        moved = lax.ppermute(value, axis, [(i, i ^ distance) for i in range(size)])
     while distance > 1:
         distance //= 2
         value = jnp.concatenate([value, moved], axis=0)
@@ -449,14 +455,11 @@
         own_tokens.append(lax.ppermute(own_tokens[-1], "tensor", ring))
     weight = jnp.transpose(query_key_value_weight, (1, 0, 2))
     share = weight.shape[1] // plane_size
+    up_own = jnp.transpose(adapter_up_maps[0], (1, 0, 2))
     piece = lax.dynamic_slice_in_dim(weight, place * share, share, axis=1)
-    piece = lax.ppermute(piece, "tensor", to_worker)
-    up_own = jnp.transpose(adapter_up_maps[0], (1, 0, 2))
-    up_outer = lax.ppermute(up_own, "tensor", to_worker)
-    first = (own_tokens[-1], piece)
-    outer_weight = lax.all_gather(after(piece, own_tokens[-1]), PLANE, axis=0)
+    piece = lax.ppermute(jnp.concatenate([piece, up_own], axis=1), "tensor", to_worker)
     down_all = lax.all_gather(adapter_down_maps, "dp", axis=0, tiled=True)
-    up_all = lax.all_gather(jnp.stack([up_own, up_outer]), "dp", axis=0)
+    up_all = lax.all_gather(up_own, "dp", axis=0)
     out_up_all = lax.all_gather(output_up_maps, "dp", axis=0, tiled=True)
 
     requests = request_adapter.shape[1]
@@ -478,15 +481,9 @@
     cosine, sine = jnp.cos(angles), jnp.sin(angles)
     turn = jnp.concatenate([cosine, cosine, -sine, sine], axis=1)
 
-    chunk_rows = token_rows // CHUNKS
-    begun = project(worker_ids, [(array,) for array in own_tokens], [weight])
-    outer_first = lax.ppermute(after(tokens[:chunk_rows], *first), "tensor", to_worker)
-    shrink = shrink_partial(adapters, table, after(tokens, *first), down_all)
-    shrink_outer = lax.ppermute(shrink, "tensor", to_worker)
-
     out_share = features // plane_size
     line = place * out_share
-    piece = lax.dynamic_slice(
+    out_piece = lax.dynamic_slice(
         output_weight, (line % head_size, line // head_size, 0),
         (out_share, 1, output_weight.shape[2]),
     )[:, 0]
@@ -496,21 +493,39 @@
     out_down = output_down_maps[0].reshape(rank, features)
     split = columns // features
     out_down = jnp.concatenate(jnp.split(out_down, split, axis=0), axis=1)
-    received = []
-    for turn_by in range(1, planes):
-        send = lax.dynamic_slice_in_dim(
-            piece, (here + turn_by) % planes * columns, columns, axis=1
+    sends = [
+        jnp.concatenate(
+            [
+                lax.dynamic_slice_in_dim(
+                    out_piece, (here + turn_by) % planes * columns, columns, axis=1
+                ),
+                out_down,
+            ],
+            axis=0,
         )
-        send = jnp.concatenate([send, out_down], axis=0)
-        received.append(
-            lax.ppermute(
-                after(send, *first), "tensor",
-                [(i, (i + turn_by) % planes) for i in range(planes)],
-            )
+        for turn_by in range(1, planes)
+    ]
+
+    first = (own_tokens[-1], piece, up_all, table, turn, own_weight) + tuple(sends)
+    outer_weight = lax.all_gather(after(piece, *first), PLANE, axis=0)
+
+    chunk_rows = token_rows // CHUNKS
+    begun = project(
+        worker_ids, [(after(array, *first),) for array in own_tokens], weight
+    )
+    outer_first = lax.ppermute(after(tokens[:chunk_rows], *first), "tensor", to_worker)
+    shrink = shrink_partial(adapters, table, after(tokens, *first), down_all)
+    shrink_outer = lax.ppermute(shrink, "tensor", to_worker)
+
+    received = [
+        lax.ppermute(
+            after(send, shrink), "tensor", [(i, (i + turn_by) % planes) for i in range(planes)]
         )
+        for turn_by, send in enumerate(sends, 1)
+    ]
     lot = jnp.concatenate([item[:out_share] for item in received], axis=0)
 
-    second = (outer_first, shrink_outer, lot, begun, up_all, out_up_all)
+    second = (outer_first, shrink_outer, lot, begun)
     outer_tokens = [[outer_first]]
     for _ in range(pairs - 1):
         outer_tokens[0].append(lax.ppermute(outer_tokens[0][-1], "tensor", ring))
@@ -527,12 +542,12 @@
     outer_tokens[1][0] = after(outer_tokens[1][0], *third[:3])
     for _ in range(pairs - 1):
         outer_tokens[1].append(lax.ppermute(outer_tokens[1][-1], "tensor", ring))
-    halves = list(doubled(after(lots, *third)[None], "dp", dp_size))
 
     def own_heads(chunk, prior):
         return attend(
-            outer_ids, adapters, chunk * chunk_rows, table, turn, up_all, 0, sums,
-            [(array,) for array in outer_tokens[chunk]], [weight], [begun], prior,
+            outer_ids, group_here, adapters, dp_size, chunk * chunk_rows, table, turn, up_all,
+            rank, sums,
+            [(array,) for array in outer_tokens[chunk]], weight, [begun], prior,
         )
 
     def spread(parts, gates):
@@ -547,18 +562,23 @@
             )
         return result
 
+    halves = after(lots, *third)[None]
+    moved = lax.ppermute(halves, "dp", [(i, i ^ (dp_size // 2)) for i in range(dp_size)])
     own_first, keys, values = own_heads(0, ())
     spread_first = spread([own_first], ())
     own_second, _, _ = own_heads(1, (keys, values))
+    halves = doubled(halves, "dp", dp_size, after(moved, own_second))
     spread_second = spread([own_second], ())
     gates = (own_second, spread_first[-1][0][1], spread_first[0][0][0], halves[0])
+    outer_weight = after(outer_weight, *gates)
     outer_part, _, _ = attend(
-        jnp.concatenate([worker_ids, outer_ids]), adapters, 0, table, turn, up_all, 1, sums,
+        jnp.concatenate([worker_ids, outer_ids]), group_here, adapters, dp_size, 0, table, turn,
+        outer_weight, rank, sums,
         [(array,) for array in own_tokens]
         + [
             tuple(outer_tokens[chunk][step] for chunk in range(CHUNKS)) for step in range(pairs)
         ],
-        [after(outer_weight, *gates)], [], (),
+        outer_weight, [], (),
     )
     spread_own = [a + b for a, b in zip(spread_first, spread_second)]
     spread_outer = spread([outer_part], (spread_second[-1][0][1],))
@@ -574,7 +594,7 @@
             ]
         ).astype(jnp.int32)
 
-    weights = [own_weight] + halves
+    weights = [own_weight] + list(halves)
     sizes = (dp_size, group_size, planes, count, rank)
     begun = project_out(lookups(worker_ids), spread_own, weights, sizes, [], [])
     return project_out(

time: 259 us -> 231 us (0.89)
  waiting for transfers between devices: 91.8 us -> 60.8 us
  local copies, waits for them, and re-layouts: 17.3 us -> 45.4 us
  Pallas kernels: 56.4 us -> 40.4 us
  blocking collectives: 24.5 us -> 16.2 us
  starting transfers between devices: 48.7 us -> 43.8 us
  other arithmetic: 5.65 us -> 8.56 us
    unnamed x50 -> x66, local copies, waits for them, and re-layouts: 4.99 us -> 30.2 us
    ppermute x3 -> x2, waiting for transfers between devices: 21.9 us -> 0.7 us  [doubled(): moved = lax.ppermute(value, axis, [(i, i ^ distance) for i in range(size)])]
    pallas_call x7, Pallas kernels: 56.4 us -> 40.4 us  [call(): pl.pallas_call(kernel, out_shape=out, grid_spec=pltpu.PrefetchScalarGridS...]
    ppermute x1, starting transfers between devices: 1.31 us -> 8.18 us  [local(): lax.ppermute(after(tokens[:chunk_rows], *first), 'tensor', to_worker)]
    ppermute x1, waiting for transfers between devices: 6.8 us -> 0.01 us  [local(): lax.ppermute(after(tokens[chunk_rows:], *second), 'tensor', to_worker)]
    ppermute x5, starting transfers between devices: 16.3 us -> 10.3 us  [the longest x1 5.83 us: local(): lax.ppermute(jnp.concatenate([piece, up_own], axis=1), 'tensor', to_worker)]
    ppermute x6, waiting for transfers between devices: 45.6 us -> 39.8 us  [spread(): lax.ppermute(part, 'tensor', from_worker)]
    all_gather x1, blocking collectives: 13.6 us -> 9.46 us  [local(): up_all = lax.all_gather(up_own, 'dp', axis=0)]
  transfers between devices with their start and end apart: 26 -> 25, of which waited for: 8 -> 9; matrix products, arithmetic and copies ran while one was open for 8% -> 12% of each run, Pallas kernels for 19% -> 15%
where the time goes in v5:
time: 231 us; the launch traced here: 229 us
  waiting for transfers between devices  60.8 us (26%)
  local copies, waits for them, and re-layouts  45.4 us (20%)
  starting transfers between devices  43.8 us (19%)
  Pallas kernels  40.4 us (17%)
  blocking collectives  16.2 us (7%)
  between operations  13.9 us (6%)
  other arithmetic  8.56 us (4%)
    pallas_call x7, Pallas kernels, call(): pl.pallas_call(kernel, out_shape=out, grid_spec=pltpu.PrefetchScalarGridS...  40.4 us
    ppermute x6, waiting for transfers between devices, spread(): lax.ppermute(part, 'tensor', from_worker)  39.8 us
    unnamed x66, local copies, waits for them, and re-layouts  30.2 us
    ppermute x3, waiting for transfers between devices, local(): lax.ppermute(after(send, shrink), 'tensor', [(i, (i + turn_by) % planes)...  17.7 us
    all_gather x1, blocking collectives, local(): up_all = lax.all_gather(up_own, 'dp', axis=0)  9.46 us
    ppermute x1, starting transfers between devices, local(): lax.ppermute(after(tokens[:chunk_rows], *first), 'tensor', to_worker)  8.18 us
    ppermute x6, starting transfers between devices, spread(): lax.ppermute(part, 'tensor', from_worker)  7.72 us
    all_gather x1, blocking collectives, local(): out_up_all = lax.all_gather(output_up_maps, 'dp', axis=0, tiled=True)  6.76 us
  transfers between devices with their start and end apart: 25, of which 9 were waited for; matrix products, arithmetic and copies ran while one was open for 12% of the time, Pallas kernels for 15%

profile of v5, /device:TPU:0, one launch (start us, length us, event | category | flops | bytes accessed | tf_op | source)
XLA Modules:
  0.0 229.1 jit_solution(11044111545740215329)
XLA Ops:
  7.9 1.9 pad_maximum_fusion.1
  9.7 5.8 %collective-permute-start = (bf16[6,576,128]{2,1,0:T(8,128)(2,1)}, bf16[6,576,128]{2,1,0:T(8,128)(2,1)}, u32[]{:S(2)}, u32[]{:S(2)}) collective-permute-start(bf16[6,576,128]{2,1,0:T(8,128)(2,1)} %pad_maximum_fusion.1), channel_id=1, source_target_pairs={{0,1},{3,2},{4,5},{7,6},{8,9},{11,10},{12,13},{15,14},{16,17},{19,... | collective-permute-start | bytes 2654216 | tf_op jit(solution)/shard_map/ppermute | solution.py:460
  16.8 1.8 multiply_cosine_fusion
  18.7 1.6 dynamic-slice_bitcast_fusion
  20.4 2.9 %fusion.7 = (bf16[64,1,1024]{2,1,0:T(2,128)(2,1)S(1)}, bf16[64,1,1024]{2,1,0:T(2,128)(2,1)S(1)}, bf16[64,1,1024]{2,1,0:T(2,128)(2,1)S(1)}) fusion(bf16[128,4,4096]{2,1,0:T(4,128)(2,1)} %param.11, s32[]{:T(128)S(6)} %select_n.122, s32[]{:T(128)S(6)} %select_n.125, s32[]{:T(128)S(6)} %select_n.134, s32[]{:T(128)S(6)} %select_n.131, s32[]{:T(128)S(6)} %select_n.128), kind=kLoop, calls=%fused_computation.49 | loop fusion | bytes 786452 | tf_op jit(solution)/shard_map/dynamic_slice | solution.py:499
  25.9 9.5 %all-gather = bf16[24,64,128]{2,1,0:T(8,128)(2,1)} all-gather(bf16[6,64,128]{2,1,0:T(8,128)(2,1)S(1)} %bitcast.52), channel_id=2, replica_groups=mesh['groups'=2,'dp'=4,'tensor'=4] {'dp'}, dimensions={0}, use_global_device_ids=true | all-gather | bytes 491520 | tf_op jit(solution)/shard_map/all_gather | solution.py:462
  36.6 8.2 %collective-permute-start.4 = (bf16[256,1024]{1,0:T(8,128)(2,1)}, bf16[256,1024]{1,0:T(8,128)(2,1)}, u32[]{:S(2)}, u32[]{:S(2)}) collective-permute-start(bf16[256,1024]{1,0:T(8,128)(2,1)} %get-tuple-element.28), channel_id=1, source_target_pairs={{0,1},{3,2},{4,5},{7,6},{8,9},{11,10},{12,13},{15,14},{16,17},{19,... | collective-permute-start | bytes 1572872 | tf_op jit(solution)/shard_map/ppermute | solution.py:516
  46.4 3.4 %shrink.1 = f32[512,192]{1,0:T(8,128)} custom-call(s32[4]{0:T(128)S(1)} %iota.40.ids_ref, s32[512,2]{1,0:T(8,128)S(1)} %copy.36.table_ref.refs_9_, bf16[512,1024]{1,0:T(8,128)(2,1)S(1)} %copy-done.3, bf16[4,192,1024]{2,1,0:T(8,128)(2,1)S(1)} %copy-done.20), custom_call_target="tpu_custom_call" | custom-call | bytes 7876608 | tf_op jit(solution)/shard_map/shrink/pallas_call | solution.py:167
  49.8 2.1 collective-permute-start.2
  51.9 2.5 %collective-permute-start.7 = (bf16[96,1024]{1,0:T(8,128)(2,1)}, bf16[96,1024]{1,0:T(8,128)(2,1)}, u32[]{:S(2)}, u32[]{:S(2)}) collective-permute-start(bf16[96,1024]{1,0:T(8,128)(2,1)} %get-tuple-element.31), channel_id=1, source_target_pairs={{0,3},{1,0},{2,1},{3,2},{4,7},{5,4},{6,5},{7,6},{8,11},{9,8},{10,9... | collective-permute-start | bytes 589832 | tf_op jit(solution)/shard_map/ppermute | solution.py:521
  55.1 2.8 %copy-done = bf16[4096,6,128]{2,0,1:T(8,128)(2,1)S(1)} copy-done((bf16[4096,6,128]{2,0,1:T(8,128)(2,1)S(1)}, bf16[4096,6,128]{2,0,1:T(8,128)(2,1)}, u32[]{:S(2)}) %copy-start) | copy-done | bytes 6291480
  59.1 2.8 %project.1.refs_5_ = f32[512,768]{1,0:T(8,128)S(1)} custom-call(s32[2]{0:T(128)S(1)} %get-tuple-element.48.ids_ref, bf16[512,1024]{1,0:T(8,128)(2,1)S(1)} %copy-done.3, bf16[512,1024]{1,0:T(8,128)(2,1)S(1)} %copy-done.14, bf16[6,4096,128]{2,1,0:T(8,128)(2,1)S(1)} %bitcast.41), custom_call_target="tpu_custom_call" | custom-call | bytes 25165824 | tf_op jit(solution)/shard_map/project/pallas_call | solution.py:167
  61.9 10.2 %collective-permute-done.7 = bf16[96,1024]{1,0:T(8,128)(2,1)} collective-permute-done((bf16[96,1024]{1,0:T(8,128)(2,1)}, bf16[96,1024]{1,0:T(8,128)(2,1)}, u32[]{:S(2)}, u32[]{:S(2)}) %collective-permute-start.7) | collective-permute-done | bytes 196640 | tf_op jit(solution)/shard_map/ppermute | solution.py:521
  73.0 3.3 %collective-permute-done.6 = bf16[96,1024]{1,0:T(8,128)(2,1)} collective-permute-done((bf16[96,1024]{1,0:T(8,128)(2,1)}, bf16[96,1024]{1,0:T(8,128)(2,1)}, u32[]{:S(2)}, u32[]{:S(2)}) %collective-permute-start.6) | collective-permute-done | bytes 196640 | tf_op jit(solution)/shard_map/ppermute | solution.py:521
  77.2 4.2 %collective-permute-done.5 = bf16[96,1024]{1,0:T(8,128)(2,1)} collective-permute-done((bf16[96,1024]{1,0:T(8,128)(2,1)}, bf16[96,1024]{1,0:T(8,128)(2,1)}, u32[]{:S(2)}, u32[]{:S(2)}) %collective-permute-start.5) | collective-permute-done | bytes 196640 | tf_op jit(solution)/shard_map/ppermute | solution.py:521
  82.4 1.6 collective-permute-start.13
  87.4 6.7 %collective-permute-start.8 = (bf16[256,1024]{1,0:T(8,128)(2,1)S(1)}, bf16[256,1024]{1,0:T(8,128)(2,1)}, u32[]{:S(2)}, u32[]{:S(2)}) collective-permute-start(bf16[256,1024]{1,0:T(8,128)(2,1)S(1)} %copy-done.23), channel_id=1, source_target_pairs={{0,1},{3,2},{4,5},{7,6},{8,9},{11,10},{12,13},{15,14},{16,17},{19,... | collective-permute-start | bytes 1572872 | tf_op jit(solution)/shard_map/ppermute | solution.py:532
  103.7 1.5 collective-permute-start.14
  106.7 2.8 %copy-done.1 = bf16[4096,6,128]{2,0,1:T(8,128)(2,1)S(1)} copy-done((bf16[4096,6,128]{2,0,1:T(8,128)(2,1)S(1)}, bf16[4096,6,128]{2,0,1:T(8,128)(2,1)}, u32[]{:S(2)}) %copy-start.1) | copy-done | bytes 6291480
  113.6 5.6 %attend.3 = (bf16[256,512]{1,0:T(8,128)(2,1)}, bf16[256,128]{1,0:T(8,128)(2,1)S(1)}, bf16[256,128]{1,0:T(8,128)(2,1)S(1)}) custom-call(s32[7]{0:T(128)S(1)} %pad_add_fusion.1.ids_ref, s32[512,2]{1,0:T(8,128)S(1)} %copy.36.table_ref.refs_9_, f32[512,256]{1,0:T(8,128)S(1)} %pad_maximum_fusion.2.turn_ref, bf16[4,6,64,128]{3,2,1,0:T(8,128)(2,1)S(1)} %bitcast.48, ...), custom_call_target="tpu_custom_call" | custom-call | bytes 31862784 | tf_op jit(solution)/shard_map/attend/pallas_call | solution.py:167
  119.2 6.5 %attend.4 = (bf16[256,512]{1,0:T(8,128)(2,1)}, bf16[256,128]{1,0:T(8,128)(2,1)}, bf16[256,128]{1,0:T(8,128)(2,1)}) custom-call(s32[7]{0:T(128)S(1)} %pad_add_fusion.1.ids_ref, s32[512,2]{1,0:T(8,128)S(1)} %copy.36.table_ref.refs_9_, f32[512,256]{1,0:T(8,128)S(1)} %pad_maximum_fusion.2.turn_ref, bf16[4,6,64,128]{3,2,1,0:T(8,128)(2,1)S(1)} %bitcast.49, ...), custom_call_target="tpu_custom_call" | custom-call | bytes 32256000 | tf_op jit(solution)/shard_map/attend/pallas_call | solution.py:167
  125.7 2.5 %collective-permute-done.14 = bf16[1,512,1024]{2,1,0:T(8,128)(2,1)} collective-permute-done((bf16[1,512,1024]{2,1,0:T(8,128)(2,1)}, bf16[1,512,1024]{2,1,0:T(8,128)(2,1)}, u32[]{:S(2)}, u32[]{:S(2)}) %collective-permute-start.14) | collective-permute-done | bytes 1048608 | tf_op jit(solution)/shard_map/ppermute | solution.py:566
  128.2 1.7 pad_maximum_fusion.refs_9_.refs_5_
  134.2 11.8 %collective-permute-done.12.refs_0_ = bf16[256,512]{1,0:T(8,128)(2,1)} collective-permute-done((bf16[256,512]{1,0:T(8,128)(2,1)}, bf16[256,512]{1,0:T(8,128)(2,1)}, u32[]{:S(2)}, u32[]{:S(2)}) %collective-permute-start.12) | collective-permute-done | bytes 262176 | tf_op jit(solution)/shard_map/ppermute | solution.py:561
  145.9 3.0 %copy-done.2 = bf16[48,576,128]{2,1,0:T(8,128)(2,1)S(1)} copy-done((bf16[48,576,128]{2,1,0:T(8,128)(2,1)S(1)}, bf16[48,576,128]{2,1,0:T(8,128)(2,1)}, u32[]{:S(2)}) %copy-start.2) | copy-done | bytes 7077912
  154.4 11.2 %attend.5 = (bf16[512,512]{1,0:T(8,128)(2,1)}, bf16[512,128]{1,0:T(8,128)(2,1)}, bf16[512,128]{1,0:T(8,128)(2,1)}) custom-call(s32[9]{0:T(128)S(1)} %concatenate.44.ids_ref, s32[512,2]{1,0:T(8,128)S(1)} %copy.36.table_ref.refs_9_, f32[512,256]{1,0:T(8,128)S(1)} %copy-done.6, bf16[8,6,576,128]{3,2,1,0:T(8,128)(2,1)S(1)} %bitcast.44, ...), custom_call_target="tpu_custom_call" | custom-call | bytes 58994688 | tf_op jit(solution)/shard_map/attend/pallas_call | solution.py:167
  171.6 6.1 %collective-permute-done.21.refs_4_ = bf16[256,512]{1,0:T(8,128)(2,1)} collective-permute-done((bf16[256,512]{1,0:T(8,128)(2,1)}, bf16[256,512]{1,0:T(8,128)(2,1)}, u32[]{:S(2)}, u32[]{:S(2)}) %collective-permute-start.21) | collective-permute-done | bytes 262176 | tf_op jit(solution)/shard_map/ppermute | solution.py:561
  181.4 6.8 %all_gather.23.refs_10_ = bf16[4,64,1024]{2,1,0:T(8,128)(2,1)S(1)} all-gather(bf16[1,64,1024]{2,1,0:T(8,128)(2,1)S(1)} %copy-done.25), channel_id=1, replica_groups=mesh['groups'=2,'dp'=4,'tensor'=4] {'dp'}, dimensions={0}, use_global_device_ids=true | all-gather | bytes 655360 | tf_op jit(solution)/shard_map/all_gather | solution.py:463
  188.2 17.6 %collective-permute-done.20.refs_2_ = bf16[256,512]{1,0:T(8,128)(2,1)} collective-permute-done((bf16[256,512]{1,0:T(8,128)(2,1)}, bf16[256,512]{1,0:T(8,128)(2,1)}, u32[]{:S(2)}, u32[]{:S(2)}) %collective-permute-start.20) | collective-permute-done | bytes 262176 | tf_op jit(solution)/shard_map/ppermute | solution.py:561
  205.8 4.3 %collective-permute-done.22.refs_6_ = bf16[256,512]{1,0:T(8,128)(2,1)} collective-permute-done((bf16[256,512]{1,0:T(8,128)(2,1)}, bf16[256,512]{1,0:T(8,128)(2,1)}, u32[]{:S(2)}, u32[]{:S(2)}) %collective-permute-start.22) | collective-permute-done | bytes 262176 | tf_op jit(solution)/shard_map/ppermute | solution.py:561
  211.3 4.9 %project_out.2 = (f32[512,1024]{1,0:T(8,128)S(1)}, f32[512,256]{1,0:T(8,128)S(1)}) custom-call(s32[16]{0:T(128)S(1)} %concatenate.55.ids_ref, bf16[256,512]{1,0:T(8,128)(2,1)} %collective-permute-done.12.refs_0_, bf16[256,512]{1,0:T(8,128)(2,1)} %get-tuple-element.38.refs_1_, bf16[256,512]{1,0:T(8,128)(2,1)} %collective-permute-done.20.refs_2_, ...), custom_call_target="tpu_custom_call" | custom-call | bytes 22020096 | tf_op jit(solution)/shard_map/project_out/pallas_call | solution.py:167
  216.3 6.0 %project_out.3 = bf16[512,1024]{1,0:T(8,128)(2,1)} custom-call(s32[16]{0:T(128)S(1)} %concatenate.43.ids_ref, bf16[512,512]{1,0:T(8,128)(2,1)S(1)} %collective-permute-done.15.refs_0_, bf16[512,512]{1,0:T(8,128)(2,1)} %get-tuple-element.44.refs_1_, bf16[512,512]{1,0:T(8,128)(2,1)} %collective-permute-done.18.refs_2_, ...), custom_call_target="tpu_custom_call" | custom-call | bytes 31469568 | tf_op jit(solution)/shard_map/project_out/pallas_call | solution.py:167
  (134 shorter events, 51.6 us)
Async XLA Ops:
  6.5 9.9 %copy-start.27 = (s32[1,4]{1,0:T(1,128)S(1)}, s32[1,4]{1,0:T(1,128)}, u32[]{:S(2)}) copy-start(s32[1,4]{1,0:T(1,128)} %param.17) | copy-start | bytes 52
  6.5 10.0 %copy-start.28 = (s32[1,4]{1,0:T(1,128)S(1)}, s32[1,4]{1,0:T(1,128)}, u32[]{:S(2)}) copy-start(s32[1,4]{1,0:T(1,128)} %param.16) | copy-start | bytes 52
  6.5 10.2 %copy-start.26 = (bf16[1,64,4,128]{3,2,1,0:T(4,128)(2,1)S(1)}, bf16[1,64,4,128]{3,2,1,0:T(4,128)(2,1)}, u32[]{:S(2)}) copy-start(bf16[1,64,4,128]{3,2,1,0:T(4,128)(2,1)} %param.14) | copy-start | bytes 196612
  6.5 38.4 %all-gather.5.cloned.1.call-start = ((), (), s32[]{:S(2)}) async-start(), calls=%async_computation | async-start | bytes 1966080 | tf_op jit(solution)/shard_map/all_gather | solution.py:461
  9.7 25.6 %collective-permute-start = (bf16[6,576,128]{2,1,0:T(8,128)(2,1)}, bf16[6,576,128]{2,1,0:T(8,128)(2,1)}, u32[]{:S(2)}, u32[]{:S(2)}) collective-permute-start(bf16[6,576,128]{2,1,0:T(8,128)(2,1)} %pad_maximum_fusion.1), channel_id=1, source_target_pairs={{0,1},{3,2},{4,5},{7,6},{8,9},{11,10},{12,13},{15,14},{16,17},{19,... | collective-permute-start | bytes 2654216 | tf_op jit(solution)/shard_map/ppermute | solution.py:460
  15.6 19.8 %collective-permute-start.1 = (bf16[512,1024]{1,0:T(8,128)(2,1)S(1)}, bf16[512,1024]{1,0:T(8,128)(2,1)S(1)}, u32[]{:S(2)}, u32[]{:S(2)}) collective-permute-start(bf16[512,1024]{1,0:T(8,128)(2,1)S(1)} %copy-done.3), channel_id=1, source_target_pairs={{1,2},{2,1},{5,6},{6,5},{9,10},{10,9},{13,14},{14,13},{17,18},{18,... | collective-permute-start | bytes 3145736 | tf_op jit(solution)/shard_map/ppermute | solution.py:455
  16.3 129.6 %all-gather.7.cloned.1.call-start = ((), (), s32[]{:S(2)}) async-start(), calls=%async_computation.1 | async-start | bytes 7962624 | tf_op jit(solution)/shard_map/all_gather | solution.py:510
  24.9 94.3 %copy-start.5 = (f32[512,256]{1,0:T(8,128)}, f32[512,256]{1,0:T(8,128)S(1)}, u32[]{:S(2)}) copy-start(f32[512,256]{1,0:T(8,128)S(1)} %pad_maximum_fusion.2.turn_ref) | copy-start | bytes 1572868
  35.4 14.4 %copy-start.13 = (bf16[512,1024]{1,0:T(8,128)(2,1)}, bf16[512,1024]{1,0:T(8,128)(2,1)S(1)}, u32[]{:S(2)}) copy-start(bf16[512,1024]{1,0:T(8,128)(2,1)S(1)} %collective-permute-done.1.refs_1_.refs_3_) | copy-start | bytes 3145732
  36.6 45.7 %collective-permute-start.4 = (bf16[256,1024]{1,0:T(8,128)(2,1)}, bf16[256,1024]{1,0:T(8,128)(2,1)}, u32[]{:S(2)}, u32[]{:S(2)}) collective-permute-start(bf16[256,1024]{1,0:T(8,128)(2,1)} %get-tuple-element.28), channel_id=1, source_target_pairs={{0,1},{3,2},{4,5},{7,6},{8,9},{11,10},{12,13},{15,14},{16,17},{19,... | collective-permute-start | bytes 1572872 | tf_op jit(solution)/shard_map/ppermute | solution.py:516
  49.8 32.5 %collective-permute-start.2 = (f32[512,192]{1,0:T(8,128)}, f32[512,192]{1,0:T(8,128)}, u32[]{:S(2)}, u32[]{:S(2)}) collective-permute-start(f32[512,192]{1,0:T(8,128)} %shrink.1), channel_id=1, source_target_pairs={{0,1},{3,2},{4,5},{7,6},{8,9},{11,10},{12,13},{15,14},{16,17},{19,... | collective-permute-start | bytes 1179656 | tf_op jit(solution)/shard_map/ppermute | solution.py:518
  51.9 20.2 %collective-permute-start.7 = (bf16[96,1024]{1,0:T(8,128)(2,1)}, bf16[96,1024]{1,0:T(8,128)(2,1)}, u32[]{:S(2)}, u32[]{:S(2)}) collective-permute-start(bf16[96,1024]{1,0:T(8,128)(2,1)} %get-tuple-element.31), channel_id=1, source_target_pairs={{0,3},{1,0},{2,1},{3,2},{4,7},{5,4},{6,5},{7,6},{8,11},{9,8},{10,9... | collective-permute-start | bytes 589832 | tf_op jit(solution)/shard_map/ppermute | solution.py:521
  54.4 21.9 %collective-permute-start.6 = (bf16[96,1024]{1,0:T(8,128)(2,1)}, bf16[96,1024]{1,0:T(8,128)(2,1)}, u32[]{:S(2)}, u32[]{:S(2)}) collective-permute-start(bf16[96,1024]{1,0:T(8,128)(2,1)} %get-tuple-element.30), channel_id=1, source_target_pairs={{0,2},{1,3},{2,0},{3,1},{4,6},{5,7},{6,4},{7,5},{8,10},{9,11},{10,... | collective-permute-start | bytes 589832 | tf_op jit(solution)/shard_map/ppermute | solution.py:521
  54.4 27.0 %collective-permute-start.5 = (bf16[96,1024]{1,0:T(8,128)(2,1)}, bf16[96,1024]{1,0:T(8,128)(2,1)}, u32[]{:S(2)}, u32[]{:S(2)}) collective-permute-start(bf16[96,1024]{1,0:T(8,128)(2,1)} %get-tuple-element.29), channel_id=1, source_target_pairs={{0,1},{1,2},{2,3},{3,0},{4,5},{5,6},{6,7},{7,4},{8,9},{9,10},{10,1... | collective-permute-start | bytes 589832 | tf_op jit(solution)/shard_map/ppermute | solution.py:521
  61.9 25.5 %copy-start.23 = (bf16[256,1024]{1,0:T(8,128)(2,1)S(1)}, bf16[256,1024]{1,0:T(8,128)(2,1)}, u32[]{:S(2)}) copy-start(bf16[256,1024]{1,0:T(8,128)(2,1)} %get-tuple-element.33) | copy-start | bytes 1572868
  82.4 13.3 %collective-permute-start.13 = (bf16[192,1024]{1,0:T(8,128)(2,1)S(1)}, bf16[192,1024]{1,0:T(8,128)(2,1)S(1)}, u32[]{:S(2)}, u32[]{:S(2)}) collective-permute-start(bf16[192,1024]{1,0:T(8,128)(2,1)S(1)} %pad_maximum_fusion.3), channel_id=1, source_target_pairs={{0,16},{16,0},{1,17},{17,1},{2,18},{18,2},{3,19},{19,3},{4,20},{20... | collective-permute-start | bytes 1179656 | tf_op jit(solution)/shard_map/ppermute | solution.py:396
  84.0 18.1 %collective-permute-start.9 = (bf16[256,1024]{1,0:T(8,128)(2,1)}, bf16[256,1024]{1,0:T(8,128)(2,1)S(1)}, u32[]{:S(2)}, u32[]{:S(2)}) collective-permute-start(bf16[256,1024]{1,0:T(8,128)(2,1)} %collective-permute-done.4.refs_2_.refs_4_), channel_id=1, source_target_pairs={{1,2},{2,1},{5,6},{6,5},{9,10},{10,9},{13,14},{14,13},{17,18},{18,... | collective-permute-start | bytes 1572872 | tf_op jit(solution)/shard_map/ppermute | solution.py:531
  85.9 17.0 %collective-permute-start.3 = (f32[512,192]{1,0:T(8,128)S(1)}, f32[512,192]{1,0:T(8,128)S(1)}, u32[]{:S(2)}, u32[]{:S(2)}) collective-permute-start(f32[512,192]{1,0:T(8,128)S(1)} %add.153.refs_0_), channel_id=1, source_target_pairs={{1,2},{2,1},{5,6},{6,5},{9,10},{10,9},{13,14},{14,13},{17,18},{18,... | collective-permute-start | bytes 1179656 | tf_op jit(solution)/shard_map/ppermute | solution.py:535
  87.4 16.3 %collective-permute-start.8 = (bf16[256,1024]{1,0:T(8,128)(2,1)S(1)}, bf16[256,1024]{1,0:T(8,128)(2,1)}, u32[]{:S(2)}, u32[]{:S(2)}) collective-permute-start(bf16[256,1024]{1,0:T(8,128)(2,1)S(1)} %copy-done.23), channel_id=1, source_target_pairs={{0,1},{3,2},{4,5},{7,6},{8,9},{11,10},{12,13},{15,14},{16,17},{19,... | collective-permute-start | bytes 1572872 | tf_op jit(solution)/shard_map/ppermute | solution.py:532
  103.7 24.5 %collective-permute-start.14 = (bf16[1,512,1024]{2,1,0:T(8,128)(2,1)}, bf16[1,512,1024]{2,1,0:T(8,128)(2,1)}, u32[]{:S(2)}, u32[]{:S(2)}) collective-permute-start(bf16[1,512,1024]{2,1,0:T(8,128)(2,1)} %bitcast.23), channel_id=1, source_target_pairs={{0,8},{4,12},{8,0},{12,4},{1,9},{5,13},{9,1},{13,5},{2,10},{6,14},... | collective-permute-start | bytes 3145736 | tf_op jit(solution)/shard_map/ppermute | solution.py:566
  105.2 14.0 %collective-permute-start.10 = (bf16[256,1024]{1,0:T(8,128)(2,1)}, bf16[256,1024]{1,0:T(8,128)(2,1)}, u32[]{:S(2)}, u32[]{:S(2)}) collective-permute-start(bf16[256,1024]{1,0:T(8,128)(2,1)} %collective-permute-done.8.refs_2_.refs_5_), channel_id=1, source_target_pairs={{1,2},{2,1},{5,6},{6,5},{9,10},{10,9},{13,14},{14,13},{17,18},{18,... | collective-permute-start | bytes 1572872 | tf_op jit(solution)/shard_map/ppermute | solution.py:544
  129.9 80.2 %collective-permute-start.19 = (bf16[2,512,1024]{2,1,0:T(8,128)(2,1)S(1)}, bf16[2,512,1024]{2,1,0:T(8,128)(2,1)}, u32[]{:S(2)}, u32[]{:S(2)}) collective-permute-start(bf16[2,512,1024]{2,1,0:T(8,128)(2,1)S(1)} %pad_maximum_fusion.refs_9_.refs_5_), channel_id=1, source_target_pairs={{0,4},{4,0},{8,12},{12,8},{1,5},{5,1},{9,13},{13,9},{2,6},{6,2},{1... | collective-permute-start | bytes 6291464 | tf_op jit(solution)/shard_map/ppermute | solution.py:400
  130.0 4.2 %collective-permute-start.11 = (bf16[256,512]{1,0:T(8,128)(2,1)}, bf16[256,512]{1,0:T(8,128)(2,1)}, u32[]{:S(2)}, u32[]{:S(2)}) collective-permute-start(bf16[256,512]{1,0:T(8,128)(2,1)} %get-tuple-element.38.refs_1_), channel_id=1, source_target_pairs={{1,2},{2,1},{5,6},{6,5},{9,10},{10,9},{13,14},{14,13},{17,18},{18,... | collective-permute-start | bytes 786440 | tf_op jit(solution)/shard_map/ppermute | solution.py:558
  131.4 14.5 %collective-permute-start.12 = (bf16[256,512]{1,0:T(8,128)(2,1)}, bf16[256,512]{1,0:T(8,128)(2,1)}, u32[]{:S(2)}, u32[]{:S(2)}) collective-permute-start(bf16[256,512]{1,0:T(8,128)(2,1)} %get-tuple-element.38.refs_1_), channel_id=1, source_target_pairs={{1,0},{2,3},{5,4},{6,7},{9,8},{10,11},{13,12},{14,15},{17,16},{18,... | collective-permute-start | bytes 786440 | tf_op jit(solution)/shard_map/ppermute | solution.py:561
  132.7 32.9 %collective-permute-start.16 = (bf16[256,512]{1,0:T(8,128)(2,1)}, bf16[256,512]{1,0:T(8,128)(2,1)}, u32[]{:S(2)}, u32[]{:S(2)}) collective-permute-start(bf16[256,512]{1,0:T(8,128)(2,1)} %get-tuple-element.37.refs_3_), channel_id=1, source_target_pairs={{1,2},{2,1},{5,6},{6,5},{9,10},{10,9},{13,14},{14,13},{17,18},{18,... | collective-permute-start | bytes 786440 | tf_op jit(solution)/shard_map/ppermute | solution.py:558
  154.4 27.0 %copy-start.25 = (bf16[1,64,1024]{2,1,0:T(8,128)(2,1)S(1)}, bf16[1,64,1024]{2,1,0:T(8,128)(2,1)}, u32[]{:S(2)}) copy-start(bf16[1,64,1024]{2,1,0:T(8,128)(2,1)} %param.15) | copy-start | bytes 393220
  165.6 3.3 %collective-permute-start.17 = (bf16[512,512]{1,0:T(8,128)(2,1)}, bf16[512,512]{1,0:T(8,128)(2,1)S(1)}, u32[]{:S(2)}, u32[]{:S(2)}) collective-permute-start(bf16[512,512]{1,0:T(8,128)(2,1)} %get-tuple-element.44.refs_1_), channel_id=1, source_target_pairs={{1,2},{2,1},{5,6},{6,5},{9,10},{10,9},{13,14},{14,13},{17,18},{18,... | collective-permute-start | bytes 1572872 | tf_op jit(solution)/shard_map/ppermute | solution.py:558
  166.3 11.4 %collective-permute-start.21 = (bf16[256,512]{1,0:T(8,128)(2,1)}, bf16[256,512]{1,0:T(8,128)(2,1)}, u32[]{:S(2)}, u32[]{:S(2)}) collective-permute-start(bf16[256,512]{1,0:T(8,128)(2,1)} %collective-permute-done.11.refs_5_), channel_id=1, source_target_pairs={{1,0},{2,3},{5,4},{6,7},{9,8},{10,11},{13,12},{14,15},{17,16},{18,... | collective-permute-start | bytes 786440 | tf_op jit(solution)/shard_map/ppermute | solution.py:561
  167.6 48.7 %collective-permute-start.15 = (bf16[512,512]{1,0:T(8,128)(2,1)}, bf16[512,512]{1,0:T(8,128)(2,1)S(1)}, u32[]{:S(2)}, u32[]{:S(2)}) collective-permute-start(bf16[512,512]{1,0:T(8,128)(2,1)} %get-tuple-element.44.refs_1_), channel_id=1, source_target_pairs={{1,0},{2,3},{5,4},{6,7},{9,8},{10,11},{13,12},{14,15},{17,16},{18,... | collective-permute-start | bytes 1572872 | tf_op jit(solution)/shard_map/ppermute | solution.py:561
  168.9 47.4 %collective-permute-start.18 = (bf16[512,512]{1,0:T(8,128)(2,1)S(1)}, bf16[512,512]{1,0:T(8,128)(2,1)}, u32[]{:S(2)}, u32[]{:S(2)}) collective-permute-start(bf16[512,512]{1,0:T(8,128)(2,1)S(1)} %collective-permute-done.17.refs_3_), channel_id=1, source_target_pairs={{1,0},{2,3},{5,4},{6,7},{9,8},{10,11},{13,12},{14,15},{17,16},{18,... | collective-permute-start | bytes 1572872 | tf_op jit(solution)/shard_map/ppermute | solution.py:561
  170.3 35.5 %collective-permute-start.20 = (bf16[256,512]{1,0:T(8,128)(2,1)}, bf16[256,512]{1,0:T(8,128)(2,1)}, u32[]{:S(2)}, u32[]{:S(2)}) collective-permute-start(bf16[256,512]{1,0:T(8,128)(2,1)} %get-tuple-element.37.refs_3_), channel_id=1, source_target_pairs={{1,0},{2,3},{5,4},{6,7},{9,8},{10,11},{13,12},{14,15},{17,16},{18,... | collective-permute-start | bytes 786440 | tf_op jit(solution)/shard_map/ppermute | solution.py:561
  177.7 32.4 %collective-permute-start.22 = (bf16[256,512]{1,0:T(8,128)(2,1)}, bf16[256,512]{1,0:T(8,128)(2,1)}, u32[]{:S(2)}, u32[]{:S(2)}) collective-permute-start(bf16[256,512]{1,0:T(8,128)(2,1)} %collective-permute-done.16.refs_7_), channel_id=1, source_target_pairs={{1,0},{2,3},{5,4},{6,7},{9,8},{10,11},{13,12},{14,15},{17,16},{18,... | collective-permute-start | bytes 786440 | tf_op jit(solution)/shard_map/ppermute | solution.py:561
  (22 other events, 43.3 us)
Sparse Core Ops, SparseCore 0:
  16.4 21.8 all-gather.4
  40.2 52.2 all-gather.6

commit v6 on v0

v6 whole, which is shorter than its diff:
```python
import functools
import math

import jax
import jax.numpy as jnp
from jax import lax
from jax.experimental import pallas as pl
from jax.experimental.pallas import tpu as pltpu
from jax.sharding import PartitionSpec as P

VMEM_BYTES = 40 * 1024 * 1024
PLANE = ("groups", "dp")


def after(value, *earlier):
    return lax.optimization_barrier((value,) + earlier)[0]


def fixed(array):
    shape = array.shape
    return pl.BlockSpec(shape, lambda step, ids: (0,) * len(shape))


def call(kernel, name, ids, grid, specs, arrays, out, scratch=()):
    total = sum(array.size * array.dtype.itemsize for array in arrays)
    return pl.pallas_call(
        kernel,
        out_shape=out,
        grid_spec=pltpu.PrefetchScalarGridSpec(
            num_scalar_prefetch=1,
            grid=(grid,),
            in_specs=[fixed(array) if spec is None else spec for spec, array in zip(specs, arrays)],
            out_specs=[fixed(item) for item in out] if isinstance(out, tuple) else fixed(out),
            scratch_shapes=list(scratch),
        ),
        compiler_params=pltpu.CompilerParams(vmem_limit_bytes=VMEM_BYTES),
        cost_estimate=pl.CostEstimate(flops=0, bytes_accessed=3 * total, transcendentals=0),
        name=name,
    )(ids.astype(jnp.int32), *arrays)


def accumulate(acc_ref, token_ref, w_ref, first):
    slots, _, head_size = w_ref.shape
    for pair in range(slots // 2):
        columns = slice(2 * pair * head_size, (2 * pair + 2) * head_size)
        weight = jnp.concatenate([w_ref[2 * pair], w_ref[2 * pair + 1]], axis=1)
        total = jnp.dot(token_ref[...], weight, preferred_element_type=jnp.float32)
        acc_ref[:, columns] = total if first is None else first[:, columns] + total


def project_kernel(shards, begun, ids_ref, *refs):
    token_refs, w_ref, rest = refs[:shards], refs[shards], refs[shards + 1 :]
    acc_ref = rest[-1]
    step = pl.program_id(0)
    for number, token_ref in enumerate(token_refs):
        first = acc_ref if number else (rest[0] if begun else None)
        pl.when(step == number)(
            functools.partial(accumulate, acc_ref, token_ref, w_ref, first)
        )


def shard_spec(weight, depth):
    slots, _, head_size = weight.shape
    return pl.BlockSpec((slots, depth, head_size), lambda step, ids: (0, ids[step], 0))


def project(ids, tokens, weight, begun=()):
    rows, depth = tokens[0].shape
    slots, _, head_size = weight.shape
    return call(
        functools.partial(project_kernel, len(tokens), len(begun)),
        "project",
        ids,
        len(tokens),
        [None] * len(tokens) + [shard_spec(weight, depth)] + [None] * len(begun),
        [*tokens, weight, *begun],
        jax.ShapeDtypeStruct((rows, slots * head_size), jnp.float32),
    )


def attend_kernel(
    ids_ref, table_ref, turn_ref, up_ref, shrink_ref, token_ref, w_ref, begun_ref, out_ref,
    acc_ref, keys_ref, values_ref,
):
    accumulate(acc_ref, token_ref, w_ref, begun_ref)
    slots, _, head_size = w_ref.shape
    rank = up_ref.shape[2]
    count = ids_ref.shape[0] - 1
    rows = acc_ref.shape[0]
    block = min(rows, 256)
    queries = slots - 2
    ups = [
        jnp.concatenate([up_ref[ids_ref[1 + j], index] for j in range(count)], axis=0)
        for index in range(slots)
    ]
    for row in range(0, rows, block):
        at = slice(row, row + block)
        lane = lax.broadcasted_iota(jnp.int32, (block, count * rank), 1)
        kept = (lane >= table_ref[at, 1:2]) & (lane < table_ref[at, 1:2] + rank)
        lows = []
        for part in range(3):
            piece = shrink_ref[at, part * rank : (part + 1) * rank].astype(jnp.float32)
            piece = jnp.concatenate([piece] * count, axis=1)
            lows.append(jnp.where(kept, piece, 0.0).astype(jnp.bfloat16))

        def slot(index):
            low = lows[0 if index < queries else index - queries + 1]
            extra = jnp.dot(low, ups[index], preferred_element_type=jnp.float32)
            return acc_ref[at, index * head_size : (index + 1) * head_size] + extra

        def rotated(index):
            value = slot(index)
            turned = pltpu.roll(value, head_size // 2, 1)
            cos, sin = turn_ref[at, :head_size], turn_ref[at, head_size:]
            return (value * cos + turned * sin).astype(jnp.bfloat16)

        keys_ref[at, :] = rotated(queries)
        values_ref[at, :] = slot(queries + 1).astype(jnp.bfloat16)
        key_rows = row + block
        keys, values = keys_ref[:key_rows], values_ref[:key_rows]
        key_at = lax.broadcasted_iota(jnp.int32, (block, key_rows), 1)
        row_at = lax.broadcasted_iota(jnp.int32, (block, key_rows), 0) + row
        allowed = (key_at >= table_ref[at, 0:1]) & (key_at <= row_at)
        for index in range(queries):
            scores = lax.dot_general(
                rotated(index), keys, (((1,), (1,)), ((), ())),
                preferred_element_type=jnp.float32,
            )
            scores = jnp.where(allowed, scores * (1.0 / math.sqrt(head_size)), -1e30)
            weights = jnp.exp(scores - jnp.max(scores, axis=1, keepdims=True))
            scale = 1.0 / jnp.sum(weights, axis=1, keepdims=True)
            attended = jnp.dot(
                (weights * scale).astype(jnp.bfloat16), values, preferred_element_type=jnp.float32
            )
            out_ref[at, index * head_size : (index + 1) * head_size] = attended.astype(
                jnp.bfloat16
            )


def attend(shard, adapters, table, turn, up, shrink, tokens, weight, begun):
    rows, depth = tokens.shape
    slots, _, head_size = weight.shape
    return call(
        attend_kernel,
        "attend",
        jnp.concatenate([shard[None], adapters]),
        1,
        [None] * 5 + [shard_spec(weight, depth), None],
        [table, turn, up, shrink, tokens, weight, begun],
        jax.ShapeDtypeStruct((rows, (slots - 2) * head_size), jnp.bfloat16),
        [
            pltpu.VMEM((rows, slots * head_size), jnp.float32),
            pltpu.VMEM((rows, head_size), jnp.bfloat16),
            pltpu.VMEM((rows, head_size), jnp.bfloat16),
        ],
    )


def shrink_kernel(ids_ref, table_ref, token_ref, down_ref, out_ref):
    step = pl.program_id(0)
    part = lax.dot_general(
        token_ref[...], down_ref[0], (((1,), (1,)), ((), ())), preferred_element_type=jnp.float32
    )
    rank = part.shape[1] // 3
    part = jnp.where(table_ref[:, 1:2] == step * rank, part, 0.0)

    @pl.when(step == 0)
    def _():
        out_ref[...] = part

    @pl.when(step > 0)
    def _():
        out_ref[...] += part


def shrink_partial(adapters, table, tokens, down):
    _, width, depth = down.shape
    return call(
        shrink_kernel,
        "shrink",
        adapters,
        adapters.shape[0],
        [None, None, pl.BlockSpec((1, width, depth), lambda step, ids: (ids[step], 0, 0))],
        [table, tokens, down],
        jax.ShapeDtypeStruct((tokens.shape[0], width), jnp.float32),
    )


def output_kernel(groups, begun, last, ids_ref, *refs):
    attended_refs, w_refs, rest = refs[:groups], refs[groups : 2 * groups], refs[2 * groups :]
    down_ref, rest = rest[0], rest[1:]
    begun_refs, rest = rest[:begun], rest[begun:]
    if last:
        table_ref, up_ref, out_ref = rest
    else:
        acc_ref, low_ref = rest
    count = ids_ref.shape[0] - groups
    step = pl.program_id(0)
    down = jnp.concatenate([down_ref[ids_ref[groups + j], 0] for j in range(count)], axis=0)
    rank = down_ref.shape[2]

    def one(number):
        w_ref = w_refs[number]
        if len(w_ref.shape) == 2:
            weight = w_ref[...]
        else:
            weight = jnp.concatenate([w_ref[i, 0] for i in range(w_ref.shape[0])], axis=0)
        attended = attended_refs[number][...]
        total = jnp.dot(attended, weight, preferred_element_type=jnp.float32)
        low = lax.dot_general(
            attended, down, (((1,), (1,)), ((), ())), preferred_element_type=jnp.float32
        )
        if number:
            total, low = acc_ref[...] + total, low_ref[...] + low
        elif begun:
            total, low = begun_refs[0][...] + total, begun_refs[1][...] + low
        if last:
            low = low.astype(jnp.bfloat16).astype(jnp.float32)
            lane = lax.broadcasted_iota(jnp.int32, low.shape, 1)
            kept = (lane >= table_ref[:, 1:2]) & (lane < table_ref[:, 1:2] + rank)
            low = jnp.where(kept, low, 0.0).astype(jnp.bfloat16)
            up = jnp.concatenate([up_ref[ids_ref[groups + j]] for j in range(count)], axis=0)
            extra = jnp.dot(low, up, preferred_element_type=jnp.float32)
            out_ref[...] = (total + extra).astype(jnp.bfloat16)
        else:
            acc_ref[...] = total
            low_ref[...] = low

    for number in range(groups):
        pl.when(step == number)(functools.partial(one, number))


def project_out(planes_of, adapters, attended, weights, down, begun, final):
    groups = len(attended)
    rows, features = attended[0].shape
    rank = down.shape[2]
    columns = weights[0][0].shape[-1]
    w_arrays, w_specs = [], []
    for array, turn in weights:
        w_arrays.append(array)
        if turn is None:
            w_specs.append(None)
        else:
            w_specs.append(
                pl.BlockSpec(
                    (array.shape[0], 1) + array.shape[2:],
                    lambda step, ids, turn=turn: (0, turn, 0, 0),
                )
            )
    down_spec = pl.BlockSpec(
        (down.shape[0], 1) + down.shape[2:], lambda step, ids: (0, ids[step], 0, 0)
    )
    sums = (
        jax.ShapeDtypeStruct((rows, columns), jnp.float32),
        jax.ShapeDtypeStruct((rows, adapters.shape[0] * rank), jnp.float32),
    )
    return call(
        functools.partial(output_kernel, groups, len(begun), bool(final)),
        "project_out",
        jnp.concatenate([planes_of, adapters]),
        groups,
        [None] * groups + w_specs + [down_spec] + [None] * (len(begun) + len(final)),
        [*attended, *w_arrays, down, *begun, *final],
        jax.ShapeDtypeStruct((rows, columns), jnp.bfloat16) if final else sums,
    )


def local(
    plane_size,
    planes,
    tokens,
    query_key_value_weight,
    output_weight,
    adapter_down_maps,
    adapter_up_maps,
    output_down_maps,
    output_up_maps,
    request_adapter,
    lengths,
):
    token_rows, depth = tokens.shape
    _, slots, head_size = query_key_value_weight.shape
    queries = slots - 2
    pool, rank = plane_size // lax.axis_size("groups"), adapter_up_maps.shape[1]
    features = queries * head_size
    columns = output_weight.shape[2] // planes
    here = lax.axis_index("tensor")
    place = lax.axis_index(PLANE)
    planes_of = (here - jnp.arange(planes) + planes) % planes

    def turned(value, turn=1):
        return lax.ppermute(value, "tensor", [(i, (i + turn) % planes) for i in range(planes)])

    held = [tokens, turned(tokens)]
    weight = jnp.transpose(query_key_value_weight, (1, 0, 2))
    down_all = lax.all_gather(adapter_down_maps, "dp", axis=0, tiled=True)
    up_all = lax.all_gather(jnp.transpose(adapter_up_maps[0], (1, 0, 2)), "dp", axis=0)
    out_down = output_down_maps[0].reshape(rank, features)
    out_downs = lax.all_gather(after(out_down, down_all), ("dp", "tensor"), axis=0)
    out_downs = out_downs.reshape(pool, planes, rank, features)

    requests = request_adapter.shape[1]
    request_ends = jnp.cumsum(lengths[0])
    request_starts = request_ends - lengths[0]
    at = jnp.arange(token_rows, dtype=jnp.int32)
    member = (at[:, None] >= request_starts[None, :]) & (at[:, None] < request_ends[None, :])
    if pool <= requests:
        adapters, label = jnp.arange(pool), request_adapter[0]
    else:
        adapters, label = request_adapter[0], jnp.arange(requests)
    wanted = jnp.stack([request_starts, label * rank], axis=0)
    table = jnp.sum(jnp.where(member[:, None, :], wanted[None], 0), axis=2).astype(jnp.int32)
    position = at - table[:, 0]
    half = head_size // 2
    inv_freq = 10000.0 ** (-2.0 * jnp.arange(half, dtype=jnp.float32) / head_size)
    angles = position.astype(jnp.float32)[:, None] * inv_freq[None, :]
    cosine, sine = jnp.cos(angles), jnp.sin(angles)
    turn = jnp.concatenate([cosine, cosine, -sine, sine], axis=1)

    own_rows = jnp.transpose(
        lax.dynamic_slice_in_dim(output_weight, here * columns, columns, axis=2), (1, 0, 2)
    ).reshape(features, columns)
    share = features // plane_size
    line = place * share
    piece = lax.dynamic_slice(
        output_weight, (line % head_size, line // head_size, 0),
        (share, 1, output_weight.shape[2]),
    )[:, 0]
    sends = [
        lax.dynamic_slice_in_dim(piece, (here + k) % planes * columns, columns, axis=1)
        for k in range(1, planes)
    ]

    begun = project(planes_of[:1], held[:1], weight)
    held[1] = after(held[1], begun, up_all, table, turn, own_rows, *sends)
    lines = [turned(after(send, held[1]), k) for k, send in enumerate(sends, 1)]
    shrink = shrink_partial(adapters, table, after(tokens, held[1]), down_all)
    shrink = lax.psum_scatter(shrink, "tensor", scatter_dimension=0, tiled=True)
    done = (shrink, *lines)
    for step in range(2, planes):
        arrived = held[-1]
        held.append(turned(arrived))
        begun = project(planes_of[step - 1 : step], [arrived], weight, [begun])
        held[-1] = after(held[-1], begun, *done)
        done = ()
    lines = lax.all_gather(jnp.stack(lines), PLANE, axis=0)
    shrink = lax.all_gather(shrink.astype(jnp.bfloat16), "tensor", axis=0, tiled=True)
    out_up_all = lax.all_gather(
        after(output_up_maps, *held[2:3]), "dp", axis=0, tiled=True
    )
    attended = [
        attend(
            planes_of[planes - 1], adapters, table, turn, up_all, after(shrink, out_up_all),
            held[-1], weight, begun,
        )
    ]

    attended.append(turned(attended[0]))
    sums = project_out(
        planes_of[:1], adapters, attended[:1], [(own_rows, None)], out_downs, [], []
    )
    for step in range(2, planes + 1):
        arrived = after(attended[-1], *sums)
        if step < planes:
            attended.append(turned(arrived))
        sums = project_out(
            planes_of[step - 1 : step], adapters, [arrived], [(lines, step - 2)], out_downs,
            list(sums), [] if step < planes else [table, out_up_all],
        )
    return sums


def solution(mesh):
    in_specs = (
        P(PLANE, "tensor"),
        P(None, None, "tensor"),
        P("tensor", None, None),
        P(PLANE, None, "tensor"),
        P(PLANE, None, None, "tensor"),
        P(PLANE, None, None, "tensor"),
        P(PLANE, None, "tensor"),
        P(PLANE, None),
        P(PLANE, None),
    )
    function = functools.partial(
        local, mesh.shape["groups"] * mesh.shape["dp"], mesh.shape["tensor"]
    )
    return jax.shard_map(
        function, mesh=mesh, in_specs=in_specs, out_specs=P(PLANE, "tensor"), check_vma=False
    )
```

time: 261 us -> 212 us (0.81)
  waiting for transfers between devices: 141 us -> 69.2 us
  starting transfers between devices: 0.3 us -> 38.4 us
  blocking collectives: 62.6 us -> 28 us
  Pallas kernels: 0 us -> 26.8 us
  matrix products: 23.3 us -> 0 us
  local copies, waits for them, and re-layouts: 14.7 us -> 28.5 us
    reduce_scatter x1, waiting for transfers between devices: 77.9 us -> 0.01 us  [local(): shrink = lax.psum_scatter(shrink, 'tensor', scatter_dimension=0, tiled=True)]
    ppermute x0 -> x9, waiting for transfers between devices: none -> 68.4 us  [turned(): lax.ppermute(value, 'tensor', [(i, (i + turn) % planes) for i in range(pl...]
    all_gather x2 -> x3, waiting for transfers between devices: 47.2 us -> 0.01 us  [the longest x1 0.01 us: local(): down_all = lax.all_gather(adapter_down_maps, 'dp', axis=0, tiled=True)]
    psum x1 -> x0, blocking collectives: 39 us -> none  [local(): reduced_rows = lax.psum(local_shrink, 'tensor').astype(jnp.bfloat16)]
    ppermute x0 -> x9, starting transfers between devices: none -> 38.3 us  [turned(): lax.ppermute(value, 'tensor', [(i, (i + turn) % planes) for i in range(pl...]
    pallas_call x0 -> x9, Pallas kernels: none -> 26.8 us  [call(): pl.pallas_call(kernel, out_shape=out, grid_spec=pltpu.PrefetchScalarGridS...]
    dot_general x10 -> x0, matrix products: 23.3 us -> none  [the longest x1 9.82 us: local(): jnp.einsum('tpc,cpd->td', attended, output_weight, preferred_element_type...]
    psum x1 -> x0, waiting for transfers between devices: 14.5 us -> none  [local(): out_shrink = lax.psum(local_out.astype(jnp.bfloat16), 'tensor')]
  transfers between devices with their start and end apart: 4 -> 13, of which waited for: 3 -> 7; matrix products, arithmetic and copies ran while one was open for 11% -> 7% of each run, Pallas kernels for 0% -> 10%
where the time goes in v6:
time: 212 us
  waiting for transfers between devices  69.2 us (33%)
  starting transfers between devices  38.4 us (18%)
  local copies, waits for them, and re-layouts  28.5 us (13%)
  blocking collectives  28 us (13%)
  Pallas kernels  26.8 us (13%)
  between operations  13.4 us (6%)
  other arithmetic  7.23 us (3%)
    ppermute x9, waiting for transfers between devices, turned(): lax.ppermute(value, 'tensor', [(i, (i + turn) % planes) for i in range(pl...  68.4 us
    ppermute x9, starting transfers between devices, turned(): lax.ppermute(value, 'tensor', [(i, (i + turn) % planes) for i in range(pl...  38.3 us
    pallas_call x9, Pallas kernels, call(): pl.pallas_call(kernel, out_shape=out, grid_spec=pltpu.PrefetchScalarGridS...  26.8 us
    unnamed x54, local copies, waits for them, and re-layouts  21.9 us
    all_gather x1, blocking collectives, local(): lax.all_gather(shrink.astype(jnp.bfloat16), 'tensor', axis=0, tiled=True)  14 us
    all_gather x1, blocking collectives, local(): lax.all_gather(after(output_up_maps, *held[2:3]), 'dp', axis=0, tiled=True)  7.16 us
    all_gather x1, blocking collectives, local(): lax.all_gather(jnp.transpose(adapter_up_maps[0], (1, 0, 2)), 'dp', axis=0)  6.91 us
  transfers between devices with their start and end apart: 13, of which 7 were waited for; matrix products, arithmetic and copies ran while one was open for 7% of the time, Pallas kernels for 10%

profile of v6, /device:TPU:0, one launch (start us, length us, event | category | flops | bytes accessed | tf_op | source)
XLA Modules:
  0.0 211.5 jit_solution(4696790850610374467)
XLA Ops:
  7.3 3.1 %collective-permute-start = (bf16[512,1024]{1,0:T(8,128)(2,1)}, bf16[512,1024]{1,0:T(8,128)(2,1)}, u32[]{:S(2)}, u32[]{:S(2)}) collective-permute-start(bf16[512,1024]{1,0:T(8,128)(2,1)} %token_ref), channel_id=1, source_target_pairs={{0,1},{1,2},{2,3},{3,0},{4,5},{5,6},{6,7},{7,4},{8,9},{9,10},{10,1... | collective-permute-start | bytes 3145736 | tf_op jit(solution)/shard_map/ppermute | solution.py:292
  12.2 3.7 %fusion.4 = (bf16[64,1,1024]{2,1,0:T(2,128)(2,1)}, bf16[64,1,1024]{2,1,0:T(2,128)(2,1)}, bf16[64,1,1024]{2,1,0:T(2,128)(2,1)S(1)}) fusion(bf16[128,4,4096]{2,1,0:T(4,128)(2,1)} %param.11, s32[]{:T(128)S(6)} %select_n.66, s32[]{:T(128)S(6)} %select_n.69, s32[]{:T(128)S(6)} %select_n.78, s32[]{:T(128)S(6)} %select_n.75, s32[]{:T(128)S(6)} %select_n.72), kind=kLoop, calls=%fused_computation.28 | loop fusion | bytes 786452 | tf_op jit(solution)/shard_map/dynamic_slice | solution.py:330
  15.9 1.7 dynamic-slice_bitcast_fusion
  18.6 3.0 %copy-done = bf16[4096,6,128]{2,0,1:T(8,128)(2,1)S(1)} copy-done((bf16[4096,6,128]{2,0,1:T(8,128)(2,1)S(1)}, bf16[4096,6,128]{2,0,1:T(8,128)(2,1)}, u32[]{:S(2)}) %copy-start) | copy-done | bytes 6291480
  21.7 1.7 project.3.refs_2_
  26.6 6.9 %all-gather = bf16[24,64,128]{2,1,0:T(8,128)(2,1)} all-gather(bf16[6,64,128]{2,1,0:T(8,128)(2,1)S(1)} %bitcast.51), channel_id=2, replica_groups=mesh['groups'=2,'dp'=4,'tensor'=4] {'dp'}, dimensions={0}, use_global_device_ids=true | all-gather | bytes 491520 | tf_op jit(solution)/shard_map/all_gather | solution.py:297
  33.6 2.2 %collective-permute-done.refs_0_ = bf16[512,1024]{1,0:T(8,128)(2,1)} collective-permute-done((bf16[512,1024]{1,0:T(8,128)(2,1)}, bf16[512,1024]{1,0:T(8,128)(2,1)}, u32[]{:S(2)}, u32[]{:S(2)}) %collective-permute-start) | collective-permute-done | bytes 1048608 | tf_op jit(solution)/shard_map/ppermute | solution.py:292
  37.3 3.4 %shrink.1 = f32[512,192]{1,0:T(8,128)} custom-call(s32[4]{0:T(128)S(1)} %iota.37.ids_ref, s32[512,2]{1,0:T(8,128)S(1)} %copy.32.table_ref.refs_5_, bf16[512,1024]{1,0:T(8,128)(2,1)S(1)} %copy-done.11, bf16[4,192,1024]{2,1,0:T(8,128)(2,1)S(1)} %copy-done.17), custom_call_target="tpu_custom_call" | custom-call | bytes 7876608 | tf_op jit(solution)/shard_map/shrink/pallas_call | solution.py:26
  41.6 2.3 %collective-permute-start.3 = (bf16[64,1024]{1,0:T(8,128)(2,1)S(1)}, bf16[64,1024]{1,0:T(8,128)(2,1)S(1)}, u32[]{:S(2)}, u32[]{:S(2)}) collective-permute-start(bf16[64,1024]{1,0:T(8,128)(2,1)S(1)} %get-tuple-element.27), channel_id=1, source_target_pairs={{0,2},{1,3},{2,0},{3,1},{4,6},{5,7},{6,4},{7,5},{8,10},{9,11},{10,... | collective-permute-start | bytes 393224 | tf_op jit(solution)/shard_map/ppermute | solution.py:292
  43.9 1.5 collective-permute-start.4
  45.4 4.4 %collective-permute-done.2 = bf16[64,1024]{1,0:T(8,128)(2,1)S(1)} collective-permute-done((bf16[64,1024]{1,0:T(8,128)(2,1)S(1)}, bf16[64,1024]{1,0:T(8,128)(2,1)S(1)}, u32[]{:S(2)}, u32[]{:S(2)}) %collective-permute-start.2) | collective-permute-done | bytes 131104 | tf_op jit(solution)/shard_map/ppermute | solution.py:292
  49.8 8.6 %collective-permute-done.3 = bf16[64,1024]{1,0:T(8,128)(2,1)S(1)} collective-permute-done((bf16[64,1024]{1,0:T(8,128)(2,1)S(1)}, bf16[64,1024]{1,0:T(8,128)(2,1)S(1)}, u32[]{:S(2)}, u32[]{:S(2)}) %collective-permute-start.3) | collective-permute-done | bytes 131104 | tf_op jit(solution)/shard_map/ppermute | solution.py:292
  59.2 28.9 %collective-permute-start.1 = (bf16[512,1024]{1,0:T(8,128)(2,1)}, bf16[512,1024]{1,0:T(8,128)(2,1)}, u32[]{:S(2)}, u32[]{:S(2)}) collective-permute-start(bf16[512,1024]{1,0:T(8,128)(2,1)} %collective-permute-done.refs_0_), channel_id=1, source_target_pairs={{0,1},{1,2},{2,3},{3,0},{4,5},{5,6},{6,7},{7,4},{8,9},{9,10},{10,1... | collective-permute-start | bytes 3145736 | tf_op jit(solution)/shard_map/ppermute | solution.py:292
  88.1 2.8 %copy-done.1 = bf16[4096,6,128]{2,0,1:T(8,128)(2,1)S(1)} copy-done((bf16[4096,6,128]{2,0,1:T(8,128)(2,1)S(1)}, bf16[4096,6,128]{2,0,1:T(8,128)(2,1)}, u32[]{:S(2)}) %copy-start.1) | copy-done | bytes 6291480
  92.3 3.0 %project.4.refs_2_ = f32[512,768]{1,0:T(8,128)S(1)} custom-call(s32[1]{0:T(128)} %get-tuple-element.54.ids_ref, bf16[512,1024]{1,0:T(8,128)(2,1)} %collective-permute-done.refs_0_, bf16[6,4096,128]{2,1,0:T(8,128)(2,1)S(1)} %bitcast.32, f32[512,768]{1,0:T(8,128)S(1)} %copy-done.8), custom_call_target="tpu_custom_call" | custom-call | bytes 26738688 | tf_op jit(solution)/shard_map/project/pallas_call | solution.py:26
  96.5 19.0 %collective-permute-done.1.refs_0_ = bf16[512,1024]{1,0:T(8,128)(2,1)} collective-permute-done((bf16[512,1024]{1,0:T(8,128)(2,1)}, bf16[512,1024]{1,0:T(8,128)(2,1)}, u32[]{:S(2)}, u32[]{:S(2)}) %collective-permute-start.1) | collective-permute-done | bytes 1048608 | tf_op jit(solution)/shard_map/ppermute | solution.py:292
  115.5 2.5 %collective-permute-start.5 = (bf16[512,1024]{1,0:T(8,128)(2,1)}, bf16[512,1024]{1,0:T(8,128)(2,1)S(1)}, u32[]{:S(2)}, u32[]{:S(2)}) collective-permute-start(bf16[512,1024]{1,0:T(8,128)(2,1)} %collective-permute-done.1.refs_0_), channel_id=1, source_target_pairs={{0,1},{1,2},{2,3},{3,0},{4,5},{5,6},{6,7},{7,4},{8,9},{9,10},{10,1... | collective-permute-start | bytes 3145736 | tf_op jit(solution)/shard_map/ppermute | solution.py:292
  118.0 2.7 %pad_add_fusion.4 = (s32[5]{0:T(128)S(1)}, s32[5]{0:T(128)S(1)}, s32[5]{0:T(128)S(1)}, s32[5]{0:T(128)S(1)}) fusion(s32[1]{0:T(128)} %get-tuple-element.53.ids_ref, s32[4]{0:T(128)S(1)} %iota.34, s32[1]{0:T(128)} %get-tuple-element.55.ids_ref, s32[1]{0:T(128)} %get-tuple-element.54.ids_ref, s32[1]{0:T(128)} %get-tuple-element.56), kind=kLoop, calls=%fused_computation.24 | loop fusion | flops 20 | bytes 112 | tf_op jit(solution)/shard_map/concatenate | solution.py:260
  120.7 2.8 %copy-done.2 = bf16[4096,6,128]{2,0,1:T(8,128)(2,1)S(1)} copy-done((bf16[4096,6,128]{2,0,1:T(8,128)(2,1)S(1)}, bf16[4096,6,128]{2,0,1:T(8,128)(2,1)}, u32[]{:S(2)}) %copy-start.2) | copy-done | bytes 6291480
  124.9 3.5 %project.5.begun_ref = f32[512,768]{1,0:T(8,128)S(1)} custom-call(s32[1]{0:T(128)} %get-tuple-element.53.ids_ref, bf16[512,1024]{1,0:T(8,128)(2,1)} %collective-permute-done.1.refs_0_, bf16[6,4096,128]{2,1,0:T(8,128)(2,1)S(1)} %bitcast.33, f32[512,768]{1,0:T(8,128)S(1)} %copy-done.10), custom_call_target="tpu_custom_call" | custom-call | bytes 26738688 | tf_op jit(solution)/shard_map/project/pallas_call | solution.py:26
  128.4 14.0 %all_gather.30.shrink_ref = bf16[512,192]{1,0:T(8,128)(2,1)S(1)} all-gather(bf16[128,192]{1,0:T(8,128)(2,1)S(1)} %convert_element_type.8), channel_id=1, replica_groups=mesh['groups'=2,'dp'=4,'tensor'=4] {'tensor'}, dimensions={0}, use_global_device_ids=true | all-gather | bytes 245760 | tf_op jit(solution)/shard_map/all_gather | solution.py:347
  142.3 7.2 %all_gather.31.refs_6_ = bf16[4,64,1024]{2,1,0:T(8,128)(2,1)} all-gather(bf16[1,64,1024]{2,1,0:T(8,128)(2,1)S(1)} %copy-done.20), channel_id=1, replica_groups=mesh['groups'=2,'dp'=4,'tensor'=4] {'dp'}, dimensions={0}, use_global_device_ids=true | all-gather | bytes 655360 | tf_op jit(solution)/shard_map/all_gather | solution.py:348
  149.5 7.2 %attend.1.refs_0_ = bf16[512,512]{1,0:T(8,128)(2,1)} custom-call(s32[5]{0:T(128)S(1)} %get-tuple-element.52.ids_ref, s32[512,2]{1,0:T(8,128)S(1)} %copy.32.table_ref.refs_5_, f32[512,256]{1,0:T(8,128)S(1)} %copy-done.13, bf16[4,6,64,128]{3,2,1,0:T(8,128)(2,1)S(1)} %bitcast.45, bf16[512,192]{1,0:T(8,128)(2,1)S(1)} %all_gather.30.shrink_ref, ...), custom_call_target="tpu_custom_call" | custom-call | bytes 30093312 | tf_op jit(solution)/shard_map/attend/pallas_call | solution.py:26
  157.9 2.5 %project_out.4 = (f32[512,1024]{1,0:T(8,128)S(1)}, f32[512,256]{1,0:T(8,128)S(1)}) custom-call(s32[5]{0:T(128)S(1)} %get-tuple-element.50.ids_ref, bf16[512,512]{1,0:T(8,128)(2,1)} %attend.1.refs_0_, bf16[512,1024]{1,0:T(8,128)(2,1)S(1)} %bitcast.44, bf16[4,4,64,512]{3,2,1,0:T(8,128)(2,1)S(1)} %bitcast.40), custom_call_target="tpu_custom_call" | custom-call | bytes 7864320 | tf_op jit(solution)/shard_map/project_out/pallas_call | solution.py:26
  161.8 11.1 %collective-permute-done.6.refs_0_ = bf16[512,512]{1,0:T(8,128)(2,1)S(1)} collective-permute-done((bf16[512,512]{1,0:T(8,128)(2,1)}, bf16[512,512]{1,0:T(8,128)(2,1)S(1)}, u32[]{:S(2)}, u32[]{:S(2)}) %collective-permute-start.6) | collective-permute-done | bytes 524320 | tf_op jit(solution)/shard_map/ppermute | solution.py:292
  172.9 1.9 copy-done.3
  174.8 1.6 copy-done.15
  176.4 1.4 project_out.5
  177.8 10.2 %collective-permute-done.7.refs_0_ = bf16[512,512]{1,0:T(8,128)(2,1)S(1)} collective-permute-done((bf16[512,512]{1,0:T(8,128)(2,1)S(1)}, bf16[512,512]{1,0:T(8,128)(2,1)S(1)}, u32[]{:S(2)}, u32[]{:S(2)}) %collective-permute-start.7) | collective-permute-done | bytes 524320 | tf_op jit(solution)/shard_map/ppermute | solution.py:292
  188.1 1.4 project_out.6
  189.5 12.8 %collective-permute-done.8.refs_0_ = bf16[512,512]{1,0:T(8,128)(2,1)S(1)} collective-permute-done((bf16[512,512]{1,0:T(8,128)(2,1)S(1)}, bf16[512,512]{1,0:T(8,128)(2,1)S(1)}, u32[]{:S(2)}, u32[]{:S(2)}) %collective-permute-start.8) | collective-permute-done | bytes 524320 | tf_op jit(solution)/shard_map/ppermute | solution.py:292
  202.3 2.7 %project_out.7 = bf16[512,1024]{1,0:T(8,128)(2,1)} custom-call(s32[5]{0:T(128)S(1)} %get-tuple-element.52.ids_ref, bf16[512,512]{1,0:T(8,128)(2,1)S(1)} %collective-permute-done.8.refs_0_, bf16[8,3,64,1024]{3,2,1,0:T(8,128)(2,1)S(1)} %bitcast.39, bf16[4,4,64,512]{3,2,1,0:T(8,128)(2,1)S(1)} %bitcast.43, f32[512,1024]{1,0:T(8,128)S(1)} %get-tuple-element.40.refs_3_, ...), custom_call_target="tpu_custom_call" | custom-call | bytes 23605248 | tf_op jit(solution)/shard_map/project_out/pallas_call | solution.py:26
  (86 shorter events, 16.6 us)
Async XLA Ops:
  6.5 29.3 %all-gather.7.cloned.1.call-start = ((), (), s32[]{:S(2)}) async-start(), calls=%async_computation.1 | async-start | bytes 1966080 | tf_op jit(solution)/shard_map/all_gather | solution.py:296
  7.3 108.3 %reduce-scatter.2.cloned.1.call-start = ((), (), s32[]{:S(2)}) async-start(), calls=%async_computation.2 | async-start | bytes 655360 | tf_op jit(solution)/shard_map/reduce_scatter | solution.py:338
  7.3 28.6 %collective-permute-start = (bf16[512,1024]{1,0:T(8,128)(2,1)}, bf16[512,1024]{1,0:T(8,128)(2,1)}, u32[]{:S(2)}, u32[]{:S(2)}) collective-permute-start(bf16[512,1024]{1,0:T(8,128)(2,1)} %token_ref), channel_id=1, source_target_pairs={{0,1},{1,2},{2,3},{3,0},{4,5},{5,6},{6,7},{7,4},{8,9},{9,10},{10,1... | collective-permute-start | bytes 3145736 | tf_op jit(solution)/shard_map/ppermute | solution.py:292
  15.9 2.7 %copy-start.11 = (bf16[512,1024]{1,0:T(8,128)(2,1)S(1)}, bf16[512,1024]{1,0:T(8,128)(2,1)}, u32[]{:S(2)}) copy-start(bf16[512,1024]{1,0:T(8,128)(2,1)} %token_ref) | copy-start | bytes 3145732
  18.6 3.0 %copy-start = (bf16[4096,6,128]{2,0,1:T(8,128)(2,1)S(1)}, bf16[4096,6,128]{2,0,1:T(8,128)(2,1)}, u32[]{:S(2)}) copy-start(bf16[4096,6,128]{2,0,1:T(8,128)(2,1)} %param.10) | copy-start | bytes 18874372
  24.5 2.1 copy-start.22
  24.5 9.0 %copy-start.18 = (bf16[64,1,1024]{2,1,0:T(2,128)(2,1)S(1)}, bf16[64,1,1024]{2,1,0:T(2,128)(2,1)}, u32[]{:S(2)}) copy-start(bf16[64,1,1024]{2,1,0:T(2,128)(2,1)} %get-tuple-element.43) | copy-start | bytes 393220
  24.5 9.0 %copy-start.19 = (bf16[64,1,1024]{2,1,0:T(2,128)(2,1)S(1)}, bf16[64,1,1024]{2,1,0:T(2,128)(2,1)}, u32[]{:S(2)}) copy-start(bf16[64,1,1024]{2,1,0:T(2,128)(2,1)} %get-tuple-element.44) | copy-start | bytes 393220
  33.6 7.3 %copy-start.23 = (bf16[1,64,4,128]{3,2,1,0:T(4,128)(2,1)S(1)}, bf16[1,64,4,128]{3,2,1,0:T(4,128)(2,1)}, u32[]{:S(2)}) copy-start(bf16[1,64,4,128]{3,2,1,0:T(4,128)(2,1)} %param.14) | copy-start | bytes 196612
  40.8 116.0 %all-gather.9.cloned.1.call-start = ((), (), s32[]{:S(2)}) async-start(), calls=%async_computation.3 | async-start | bytes 1114112 | tf_op jit(solution)/shard_map/all_gather | solution.py:299
  41.5 131.4 %all-gather.11.cloned.1.call-start = ((), (), s32[]{:S(2)}) async-start(), calls=%async_computation.4 | async-start | bytes 3538944 | tf_op jit(solution)/shard_map/all_gather | solution.py:346
  41.5 8.3 %collective-permute-start.2 = (bf16[64,1024]{1,0:T(8,128)(2,1)S(1)}, bf16[64,1024]{1,0:T(8,128)(2,1)S(1)}, u32[]{:S(2)}, u32[]{:S(2)}) collective-permute-start(bf16[64,1024]{1,0:T(8,128)(2,1)S(1)} %bitcast.47), channel_id=1, source_target_pairs={{0,1},{1,2},{2,3},{3,0},{4,5},{5,6},{6,7},{7,4},{8,9},{9,10},{10,1... | collective-permute-start | bytes 393224 | tf_op jit(solution)/shard_map/ppermute | solution.py:292
  41.6 16.8 %collective-permute-start.3 = (bf16[64,1024]{1,0:T(8,128)(2,1)S(1)}, bf16[64,1024]{1,0:T(8,128)(2,1)S(1)}, u32[]{:S(2)}, u32[]{:S(2)}) collective-permute-start(bf16[64,1024]{1,0:T(8,128)(2,1)S(1)} %get-tuple-element.27), channel_id=1, source_target_pairs={{0,2},{1,3},{2,0},{3,1},{4,6},{5,7},{6,4},{7,5},{8,10},{9,11},{10,... | collective-permute-start | bytes 393224 | tf_op jit(solution)/shard_map/ppermute | solution.py:292
  43.9 14.5 %collective-permute-start.4 = (bf16[64,1024]{1,0:T(8,128)(2,1)S(1)}, bf16[64,1024]{1,0:T(8,128)(2,1)S(1)}, u32[]{:S(2)}, u32[]{:S(2)}) collective-permute-start(bf16[64,1024]{1,0:T(8,128)(2,1)S(1)} %get-tuple-element.28), channel_id=1, source_target_pairs={{0,3},{1,0},{2,1},{3,2},{4,7},{5,4},{6,5},{7,6},{8,11},{9,8},{10,9... | collective-permute-start | bytes 393224 | tf_op jit(solution)/shard_map/ppermute | solution.py:292
  59.2 56.3 %collective-permute-start.1 = (bf16[512,1024]{1,0:T(8,128)(2,1)}, bf16[512,1024]{1,0:T(8,128)(2,1)}, u32[]{:S(2)}, u32[]{:S(2)}) collective-permute-start(bf16[512,1024]{1,0:T(8,128)(2,1)} %collective-permute-done.refs_0_), channel_id=1, source_target_pairs={{0,1},{1,2},{2,3},{3,0},{4,5},{5,6},{6,7},{7,4},{8,9},{9,10},{10,1... | collective-permute-start | bytes 3145736 | tf_op jit(solution)/shard_map/ppermute | solution.py:292
  88.1 2.8 %copy-start.1 = (bf16[4096,6,128]{2,0,1:T(8,128)(2,1)S(1)}, bf16[4096,6,128]{2,0,1:T(8,128)(2,1)}, u32[]{:S(2)}) copy-start(bf16[4096,6,128]{2,0,1:T(8,128)(2,1)} %param.10) | copy-start | bytes 18874372
  92.3 57.2 %slice-start = ((s8[6291456]{0:T(1024)(128)(4,1)}), s8[2097152]{0:T(1024)(128)(4,1)S(1)}, s32[]{:S(2)}) async-start(s8[6291456]{0:T(1024)(128)(4,1)} %bitcast.34), calls=%async_computation.5 | async-start | bytes 4194304
  115.5 34.0 %collective-permute-start.5 = (bf16[512,1024]{1,0:T(8,128)(2,1)}, bf16[512,1024]{1,0:T(8,128)(2,1)S(1)}, u32[]{:S(2)}, u32[]{:S(2)}) collective-permute-start(bf16[512,1024]{1,0:T(8,128)(2,1)} %collective-permute-done.1.refs_0_), channel_id=1, source_target_pairs={{0,1},{1,2},{2,3},{3,0},{4,5},{5,6},{6,7},{7,4},{8,9},{9,10},{10,1... | collective-permute-start | bytes 3145736 | tf_op jit(solution)/shard_map/ppermute | solution.py:292
  120.7 2.8 %copy-start.2 = (bf16[4096,6,128]{2,0,1:T(8,128)(2,1)S(1)}, bf16[4096,6,128]{2,0,1:T(8,128)(2,1)}, u32[]{:S(2)}) copy-start(bf16[4096,6,128]{2,0,1:T(8,128)(2,1)} %param.10) | copy-start | bytes 18874372
  124.9 3.5 %copy-start.21 = (f32[128,192]{1,0:T(8,128)S(1)}, f32[128,192]{1,0:T(8,128)}, u32[]{:S(2)}) copy-start(f32[128,192]{1,0:T(8,128)} %reduce-scatter.2.cloned.1.call-done) | copy-start | bytes 294916
  124.9 17.5 %copy-start.20 = (bf16[1,64,1024]{2,1,0:T(8,128)(2,1)S(1)}, bf16[1,64,1024]{2,1,0:T(8,128)(2,1)}, u32[]{:S(2)}) copy-start(bf16[1,64,1024]{2,1,0:T(8,128)(2,1)} %param.15) | copy-start | bytes 393220
  124.9 24.6 %slice-start.1 = ((s8[6291456]{0:T(1024)(128)(4,1)}), s8[4194304]{0:T(1024)(128)(4,1)S(1)}, s32[]{:S(2)}) async-start(s8[6291456]{0:T(1024)(128)(4,1)} %bitcast.34), calls=%async_computation.6 | async-start | bytes 8388608
  124.9 24.6 %copy-start.13 = (f32[512,256]{1,0:T(8,128)S(1)}, f32[512,256]{1,0:T(8,128)}, u32[]{:S(2)}) copy-start(f32[512,256]{1,0:T(8,128)} %pad_maximum_fusion.turn_ref) | copy-start | bytes 1572868
  124.9 24.7 %copy-start.16 = (bf16[24,64,128]{2,1,0:T(8,128)(2,1)S(1)}, bf16[24,64,128]{2,1,0:T(8,128)(2,1)}, u32[]{:S(2)}) copy-start(bf16[24,64,128]{2,1,0:T(8,128)(2,1)} %all-gather) | copy-start | bytes 1179652
  156.7 16.2 %collective-permute-start.6 = (bf16[512,512]{1,0:T(8,128)(2,1)}, bf16[512,512]{1,0:T(8,128)(2,1)S(1)}, u32[]{:S(2)}, u32[]{:S(2)}) collective-permute-start(bf16[512,512]{1,0:T(8,128)(2,1)} %attend.1.refs_0_), channel_id=1, source_target_pairs={{0,1},{1,2},{2,3},{3,0},{4,5},{5,6},{6,7},{7,4},{8,9},{9,10},{10,1... | collective-permute-start | bytes 1572872 | tf_op jit(solution)/shard_map/ppermute | solution.py:292
  157.9 15.0 %copy-start.6 = (bf16[1024,512]{1,0:T(8,128)(2,1)S(1)}, bf16[1024,512]{1,0:T(8,128)(2,1)}, u32[]{:S(2)}) copy-start(bf16[1024,512]{1,0:T(8,128)(2,1)} %all-gather.9.cloned.1.call-done) | copy-start | bytes 3145732
  172.9 15.2 %collective-permute-start.7 = (bf16[512,512]{1,0:T(8,128)(2,1)S(1)}, bf16[512,512]{1,0:T(8,128)(2,1)S(1)}, u32[]{:S(2)}, u32[]{:S(2)}) collective-permute-start(bf16[512,512]{1,0:T(8,128)(2,1)S(1)} %collective-permute-done.6.refs_0_), channel_id=1, source_target_pairs={{0,1},{1,2},{2,3},{3,0},{4,5},{5,6},{6,7},{7,4},{8,9},{9,10},{10,1... | collective-permute-start | bytes 1572872 | tf_op jit(solution)/shard_map/ppermute | solution.py:292
  172.9 1.9 copy-start.3
  174.8 1.6 copy-start.15
  176.4 11.7 %copy-start.4 = (bf16[24,64,1024]{2,1,0:T(8,128)(2,1)S(1)}, bf16[24,64,1024]{2,1,0:T(8,128)(2,1)}, u32[]{:S(2)}) copy-start(bf16[24,64,1024]{2,1,0:T(8,128)(2,1)} %all-gather.11.cloned.1.call-done) | copy-start | bytes 9437188
  188.1 14.3 %collective-permute-start.8 = (bf16[512,512]{1,0:T(8,128)(2,1)S(1)}, bf16[512,512]{1,0:T(8,128)(2,1)S(1)}, u32[]{:S(2)}, u32[]{:S(2)}) collective-permute-start(bf16[512,512]{1,0:T(8,128)(2,1)S(1)} %collective-permute-done.7.refs_0_), channel_id=1, source_target_pairs={{0,1},{1,2},{2,3},{3,0},{4,5},{5,6},{6,7},{7,4},{8,9},{9,10},{10,1... | collective-permute-start | bytes 1572872 | tf_op jit(solution)/shard_map/ppermute | solution.py:292
  188.1 14.3 %copy-start.12 = (bf16[4,64,1024]{2,1,0:T(8,128)(2,1)S(1)}, bf16[4,64,1024]{2,1,0:T(8,128)(2,1)}, u32[]{:S(2)}) copy-start(bf16[4,64,1024]{2,1,0:T(8,128)(2,1)} %all_gather.31.refs_6_) | copy-start | bytes 1572868
  (7 other events, 9.1 us)
Sparse Core Ops, SparseCore 0:
  8.9 22.3 all-gather.6
  40.9 24.7 reduce-scatter.1
  67.9 58.9 all-gather.8
  128.7 30.9 all-gather.10

commit v7 on v6

--- a/solution.py
+++ b/solution.py
@@ -78,19 +78,21 @@
     )
 
 
-def attend_kernel(
-    ids_ref, table_ref, turn_ref, up_ref, shrink_ref, token_ref, w_ref, begun_ref, out_ref,
-    acc_ref, keys_ref, values_ref,
-):
+def attend_kernel(planes, ids_ref, table_ref, turn_ref, up_ref, *refs):
+    piece_refs, refs = refs[:planes], refs[planes:]
+    token_ref, w_ref, begun_ref, out_ref, acc_ref, keys_ref, values_ref, shrink_ref = refs
+    for number, piece_ref in enumerate(piece_refs):
+        size = piece_ref.shape[0]
+        shrink_ref[pl.ds(pl.multiple_of(ids_ref[number] * size, size), size), :] = piece_ref[...]
     accumulate(acc_ref, token_ref, w_ref, begun_ref)
     slots, _, head_size = w_ref.shape
     rank = up_ref.shape[2]
-    count = ids_ref.shape[0] - 1
+    count = ids_ref.shape[0] - planes
     rows = acc_ref.shape[0]
     block = min(rows, 256)
     queries = slots - 2
     ups = [
-        jnp.concatenate([up_ref[ids_ref[1 + j], index] for j in range(count)], axis=0)
+        jnp.concatenate([up_ref[ids_ref[planes + j], index] for j in range(count)], axis=0)
         for index in range(slots)
     ]
     for row in range(0, rows, block):
@@ -137,27 +139,35 @@
             )
 
 
-def attend(shard, adapters, table, turn, up, shrink, tokens, weight, begun):
+def attend(planes_of, adapters, table, turn, up, shrink, tokens, weight, begun):
     rows, depth = tokens.shape
     slots, _, head_size = weight.shape
+    planes = len(shrink)
     return call(
-        attend_kernel,
+        functools.partial(attend_kernel, planes),
         "attend",
-        jnp.concatenate([shard[None], adapters]),
+        jnp.concatenate([planes_of, adapters]),
         1,
-        [None] * 5 + [shard_spec(weight, depth), None],
-        [table, turn, up, shrink, tokens, weight, begun],
+        [None] * (4 + planes)
+        + [
+            pl.BlockSpec((slots, depth, head_size), lambda step, ids: (0, ids[planes - 1], 0)),
+            None,
+        ],
+        [table, turn, up, *shrink, tokens, weight, begun],
         jax.ShapeDtypeStruct((rows, (slots - 2) * head_size), jnp.bfloat16),
         [
             pltpu.VMEM((rows, slots * head_size), jnp.float32),
             pltpu.VMEM((rows, head_size), jnp.bfloat16),
             pltpu.VMEM((rows, head_size), jnp.bfloat16),
+            pltpu.VMEM((rows, shrink[0].shape[1]), jnp.bfloat16),
         ],
     )
 
 
-def shrink_kernel(ids_ref, table_ref, token_ref, down_ref, out_ref):
+def shrink_kernel(planes, ids_ref, table_ref, token_ref, down_ref, *refs):
+    out_refs, acc_ref = refs[:planes], refs[planes]
     step = pl.program_id(0)
+    count = ids_ref.shape[0] - 1
     part = lax.dot_general(
         token_ref[...], down_ref[0], (((1,), (1,)), ((), ())), preferred_element_type=jnp.float32
     )
@@ -166,23 +176,32 @@
 
     @pl.when(step == 0)
     def _():
-        out_ref[...] = part
+        acc_ref[...] = part
 
     @pl.when(step > 0)
     def _():
-        out_ref[...] += part
-
-
-def shrink_partial(adapters, table, tokens, down):
+        acc_ref[...] += part
+
+    @pl.when(step == count - 1)
+    def _():
+        for turn, out_ref in enumerate(out_refs):
+            rows = out_ref.shape[0]
+            plane = lax.rem(ids_ref[count] + turn, planes)
+            out_ref[...] = acc_ref[pl.ds(pl.multiple_of(plane * rows, rows), rows), :]
+
+
+def shrink_partial(adapters, here, planes, table, tokens, down):
     _, width, depth = down.shape
+    rows = tokens.shape[0]
     return call(
-        shrink_kernel,
+        functools.partial(shrink_kernel, planes),
         "shrink",
-        adapters,
+        jnp.concatenate([adapters, here[None]]),
         adapters.shape[0],
         [None, None, pl.BlockSpec((1, width, depth), lambda step, ids: (ids[step], 0, 0))],
         [table, tokens, down],
-        jax.ShapeDtypeStruct((tokens.shape[0], width), jnp.float32),
+        (jax.ShapeDtypeStruct((rows // planes, width), jnp.float32),) * planes,
+        [pltpu.VMEM((rows, width), jnp.float32)],
     )
 
 
@@ -334,27 +353,24 @@
     begun = project(planes_of[:1], held[:1], weight)
     held[1] = after(held[1], begun, up_all, table, turn, own_rows, *sends)
     lines = [turned(after(send, held[1]), k) for k, send in enumerate(sends, 1)]
-    shrink = shrink_partial(adapters, table, after(tokens, held[1]), down_all)
-    shrink = lax.psum_scatter(shrink, "tensor", scatter_dimension=0, tiled=True)
-    done = (shrink, *lines)
+    sums = shrink_partial(adapters, here, planes, table, after(tokens, held[1]), down_all)
+    sums = [sums[0]] + [turned(sums[k], k) for k in range(1, planes)]
+    shrink = sum(sums[1:], sums[0]).astype(jnp.bfloat16)
     for step in range(2, planes):
         arrived = held[-1]
         held.append(turned(arrived))
         begun = project(planes_of[step - 1 : step], [arrived], weight, [begun])
-        held[-1] = after(held[-1], begun, *done)
-        done = ()
-    lines = lax.all_gather(jnp.stack(lines), PLANE, axis=0)
-    shrink = lax.all_gather(shrink.astype(jnp.bfloat16), "tensor", axis=0, tiled=True)
+        held[-1] = after(held[-1], begun, *([shrink, *lines] if step == 2 else []))
+    lines = lax.all_gather(jnp.stack([after(line, held[2]) for line in lines]), PLANE, axis=0)
+    shrink = after(shrink, held[2])
+    shrink = [shrink] + [turned(shrink, k) for k in range(1, planes)]
+    attended = [
+        attend(planes_of, adapters, table, turn, up_all, shrink, held[-1], weight, begun)
+    ]
+
     out_up_all = lax.all_gather(
-        after(output_up_maps, *held[2:3]), "dp", axis=0, tiled=True
-    )
-    attended = [
-        attend(
-            planes_of[planes - 1], adapters, table, turn, up_all, after(shrink, out_up_all),
-            held[-1], weight, begun,
-        )
-    ]
-
+        after(output_up_maps, attended[0]), "dp", axis=0, tiled=True
+    )
     attended.append(turned(attended[0]))
     sums = project_out(
         planes_of[:1], adapters, attended[:1], [(own_rows, None)], out_downs, [], []

time: 212 us -> 198 us (0.934)
  blocking collectives: 28 us -> 14.1 us
  starting transfers between devices: 38.4 us -> 30 us
  waiting for transfers between devices: 69.2 us -> 76 us
    all_gather x2 -> x1, blocking collectives: 21.1 us -> 6.5 us  [local(): lax.all_gather(after(output_up_maps, attended[0]), 'dp', axis=0, tiled=True)]
    all_gather x1, waiting for transfers between devices: 0.01 us -> 13.4 us  [local(): down_all = lax.all_gather(adapter_down_maps, 'dp', axis=0, tiled=True)]
    ppermute x9 -> x15, starting transfers between devices: 38.3 us -> 29.9 us  [turned(): lax.ppermute(value, 'tensor', [(i, (i + turn) % planes) for i in range(pl...]
    ppermute x9 -> x15, waiting for transfers between devices: 68.4 us -> 61.9 us  [turned(): lax.ppermute(value, 'tensor', [(i, (i + turn) % planes) for i in range(pl...]
    unnamed x54 -> x46, local copies, waits for them, and re-layouts: 21.9 us -> 22.7 us
  transfers between devices with their start and end apart: 13 -> 18, of which waited for: 7 -> 9; matrix products, arithmetic and copies ran while one was open for 7% -> 8% of each run, Pallas kernels for 10% -> 12%
where the time goes in v7:
time: 198 us; the launch traced here: 197 us
  waiting for transfers between devices  76 us (38%)
  local copies, waits for them, and re-layouts  30.2 us (15%)
  starting transfers between devices  30 us (15%)
  Pallas kernels  25.7 us (13%)
  blocking collectives  14.1 us (7%)
  between operations  13.3 us (7%)
  other arithmetic  7.5 us (4%)
    ppermute x15, waiting for transfers between devices, turned(): lax.ppermute(value, 'tensor', [(i, (i + turn) % planes) for i in range(pl...  61.9 us
    ppermute x15, starting transfers between devices, turned(): lax.ppermute(value, 'tensor', [(i, (i + turn) % planes) for i in range(pl...  29.9 us
    pallas_call x9, Pallas kernels, call(): pl.pallas_call(kernel, out_shape=out, grid_spec=pltpu.PrefetchScalarGridS...  25.7 us
    unnamed x46, local copies, waits for them, and re-layouts  22.7 us
    all_gather x1, waiting for transfers between devices, local(): down_all = lax.all_gather(adapter_down_maps, 'dp', axis=0, tiled=True)  13.4 us
    all_gather x1, blocking collectives, local(): lax.all_gather(jnp.transpose(adapter_up_maps[0], (1, 0, 2)), 'dp', axis=0)  7.6 us
    all_gather x1, blocking collectives, local(): lax.all_gather(after(output_up_maps, attended[0]), 'dp', axis=0, tiled=True)  6.5 us
  transfers between devices with their start and end apart: 18, of which 9 were waited for; matrix products, arithmetic and copies ran while one was open for 8% of the time, Pallas kernels for 12%

profile of v7, /device:TPU:0, one launch (start us, length us, event | category | flops | bytes accessed | tf_op | source)
XLA Modules:
  0.0 196.8 jit_solution(15643193144447720746)
XLA Ops:
  7.3 3.1 %collective-permute-start = (bf16[512,1024]{1,0:T(8,128)(2,1)}, bf16[512,1024]{1,0:T(8,128)(2,1)}, u32[]{:S(2)}, u32[]{:S(2)}) collective-permute-start(bf16[512,1024]{1,0:T(8,128)(2,1)} %token_ref), channel_id=1, source_target_pairs={{0,1},{1,2},{2,3},{3,0},{4,5},{5,6},{6,7},{7,4},{8,9},{9,10},{10,1... | collective-permute-start | bytes 3145736 | tf_op jit(solution)/shard_map/ppermute | solution.py:311
  12.1 2.8 %fusion.4 = (bf16[64,1,1024]{2,1,0:T(2,128)(2,1)S(1)}, bf16[64,1,1024]{2,1,0:T(2,128)(2,1)S(1)}, bf16[64,1,1024]{2,1,0:T(2,128)(2,1)S(1)}) fusion(bf16[128,4,4096]{2,1,0:T(4,128)(2,1)} %param.11, s32[]{:T(128)S(6)} %select_n.66, s32[]{:T(128)S(6)} %select_n.69, s32[]{:T(128)S(6)} %select_n.78, s32[]{:T(128)S(6)} %select_n.75, s32[]{:T(128)S(6)} %select_n.72), kind=kLoop, calls=%fused_computation.31 | loop fusion | bytes 786452 | tf_op jit(solution)/shard_map/dynamic_slice | solution.py:349
  16.2 1.7 dynamic-slice_bitcast_fusion
  18.0 13.4 %all-gather.7.cloned.1.call-done.down_ref = bf16[4,192,1024]{2,1,0:T(8,128)(2,1)} async-done(((bf16[1,192,1024]{2,1,0:T(8,128)(2,1)}), bf16[4,192,1024]{2,1,0:T(8,128)(2,1)}) %all-gather.7.cloned.1.call-update) | async-done | bytes 1572880 | tf_op jit(solution)/shard_map/all_gather | solution.py:315
  32.7 2.8 %copy-done = bf16[4096,6,128]{2,0,1:T(8,128)(2,1)S(1)} copy-done((bf16[4096,6,128]{2,0,1:T(8,128)(2,1)S(1)}, bf16[4096,6,128]{2,0,1:T(8,128)(2,1)}, u32[]{:S(2)}) %copy-start) | copy-done | bytes 6291480
  35.5 1.7 project.3.refs_2_
  39.3 7.6 %all-gather = bf16[24,64,128]{2,1,0:T(8,128)(2,1)} all-gather(bf16[6,64,128]{2,1,0:T(8,128)(2,1)S(1)} %bitcast.50), channel_id=2, replica_groups=mesh['groups'=2,'dp'=4,'tensor'=4] {'dp'}, dimensions={0}, use_global_device_ids=true | all-gather | bytes 491520 | tf_op jit(solution)/shard_map/all_gather | solution.py:316
  50.8 2.7 %shrink.1 = (f32[128,192]{1,0:T(8,128)S(1)}, f32[128,192]{1,0:T(8,128)S(1)}, f32[128,192]{1,0:T(8,128)S(1)}, f32[128,192]{1,0:T(8,128)S(1)}) custom-call(s32[5]{0:T(128)S(1)} %pad_add_fusion.3.ids_ref, s32[512,2]{1,0:T(8,128)S(1)} %copy.32.table_ref.refs_5_, bf16[512,1024]{1,0:T(8,128)(2,1)S(1)} %copy-done.8, bf16[4,192,1024]{2,1,0:T(8,128)(2,1)S(1)} %copy-done.14), custom_call_target="tpu_custom_call" | custom-call | bytes 7876608 | tf_op jit(solution)/shard_map/shrink/pallas_call | solution.py:26
  56.4 2.4 %collective-permute-start.3 = (f32[128,192]{1,0:T(8,128)S(1)}, f32[128,192]{1,0:T(8,128)S(1)}, u32[]{:S(2)}, u32[]{:S(2)}) collective-permute-start(f32[128,192]{1,0:T(8,128)S(1)} %get-tuple-element.36), channel_id=1, source_target_pairs={{0,3},{1,0},{2,1},{3,2},{4,7},{5,4},{6,5},{7,6},{8,11},{9,8},{10,9... | collective-permute-start | bytes 294920 | tf_op jit(solution)/shard_map/ppermute | solution.py:311
  58.9 2.8 %copy-done.1 = bf16[4096,6,128]{2,0,1:T(8,128)(2,1)S(1)} copy-done((bf16[4096,6,128]{2,0,1:T(8,128)(2,1)S(1)}, bf16[4096,6,128]{2,0,1:T(8,128)(2,1)}, u32[]{:S(2)}) %copy-start.1) | copy-done | bytes 6291480
  61.6 2.9 %project.4.refs_2_ = f32[512,768]{1,0:T(8,128)S(1)} custom-call(s32[1]{0:T(128)} %get-tuple-element.68.ids_ref, bf16[512,1024]{1,0:T(8,128)(2,1)} %collective-permute-done.refs_0_, bf16[6,4096,128]{2,1,0:T(8,128)(2,1)S(1)} %bitcast.33, f32[512,768]{1,0:T(8,128)S(1)} %project.3.refs_2_), custom_call_target="tpu_custom_call" | custom-call | bytes 26738688 | tf_op jit(solution)/shard_map/project/pallas_call | solution.py:26
  64.7 18.2 %collective-permute-done.1 = f32[128,192]{1,0:T(8,128)S(1)} collective-permute-done((f32[128,192]{1,0:T(8,128)S(1)}, f32[128,192]{1,0:T(8,128)S(1)}, u32[]{:S(2)}, u32[]{:S(2)}) %collective-permute-start.1) | collective-permute-done | bytes 98336 | tf_op jit(solution)/shard_map/ppermute | solution.py:311
  82.9 6.0 %collective-permute-start.6 = (bf16[64,1024]{1,0:T(8,128)(2,1)S(1)}, bf16[64,1024]{1,0:T(8,128)(2,1)S(1)}, u32[]{:S(2)}, u32[]{:S(2)}) collective-permute-start(bf16[64,1024]{1,0:T(8,128)(2,1)S(1)} %copy-done.19), channel_id=1, source_target_pairs={{0,2},{1,3},{2,0},{3,1},{4,6},{5,7},{6,4},{7,5},{8,10},{9,11},{10,... | collective-permute-start | bytes 393224 | tf_op jit(solution)/shard_map/ppermute | solution.py:311
  88.8 6.9 %collective-permute-start.7 = (bf16[64,1024]{1,0:T(8,128)(2,1)S(1)}, bf16[64,1024]{1,0:T(8,128)(2,1)S(1)}, u32[]{:S(2)}, u32[]{:S(2)}) collective-permute-start(bf16[64,1024]{1,0:T(8,128)(2,1)S(1)} %copy-done.18), channel_id=1, source_target_pairs={{0,3},{1,0},{2,1},{3,2},{4,7},{5,4},{6,5},{7,6},{8,11},{9,8},{10,9... | collective-permute-start | bytes 393224 | tf_op jit(solution)/shard_map/ppermute | solution.py:311
  95.8 3.6 %collective-permute-done.6 = bf16[64,1024]{1,0:T(8,128)(2,1)S(1)} collective-permute-done((bf16[64,1024]{1,0:T(8,128)(2,1)S(1)}, bf16[64,1024]{1,0:T(8,128)(2,1)S(1)}, u32[]{:S(2)}, u32[]{:S(2)}) %collective-permute-start.6) | collective-permute-done | bytes 131104 | tf_op jit(solution)/shard_map/ppermute | solution.py:311
  100.2 3.4 %collective-permute-start.11 = (bf16[512,1024]{1,0:T(8,128)(2,1)}, bf16[512,1024]{1,0:T(8,128)(2,1)S(1)}, u32[]{:S(2)}, u32[]{:S(2)}) collective-permute-start(bf16[512,1024]{1,0:T(8,128)(2,1)} %collective-permute-done.4.refs_0_), channel_id=1, source_target_pairs={{0,1},{1,2},{2,3},{3,0},{4,5},{5,6},{6,7},{7,4},{8,9},{9,10},{10,1... | collective-permute-start | bytes 3145736 | tf_op jit(solution)/shard_map/ppermute | solution.py:311
  105.2 2.0 %collective-permute-start.8 = (bf16[128,192]{1,0:T(8,128)(2,1)S(1)}, bf16[128,192]{1,0:T(8,128)(2,1)S(1)}, u32[]{:S(2)}, u32[]{:S(2)}) collective-permute-start(bf16[128,192]{1,0:T(8,128)(2,1)S(1)} %add_convert_fusion.refs_0_), channel_id=1, source_target_pairs={{0,1},{1,2},{2,3},{3,0},{4,5},{5,6},{6,7},{7,4},{8,9},{9,10},{10,1... | collective-permute-start | bytes 147464 | tf_op jit(solution)/shard_map/ppermute | solution.py:311
  107.3 3.1 %copy-done.2 = bf16[4096,6,128]{2,0,1:T(8,128)(2,1)S(1)} copy-done((bf16[4096,6,128]{2,0,1:T(8,128)(2,1)S(1)}, bf16[4096,6,128]{2,0,1:T(8,128)(2,1)}, u32[]{:S(2)}) %copy-start.2) | copy-done | bytes 6291480
  110.4 3.0 %project.5.refs_6_ = f32[512,768]{1,0:T(8,128)S(1)} custom-call(s32[1]{0:T(128)} %get-tuple-element.67.ids_ref, bf16[512,1024]{1,0:T(8,128)(2,1)} %collective-permute-done.4.refs_0_, bf16[6,4096,128]{2,1,0:T(8,128)(2,1)S(1)} %bitcast.34, f32[512,768]{1,0:T(8,128)S(1)} %project.4.refs_2_), custom_call_target="tpu_custom_call" | custom-call | bytes 26738688 | tf_op jit(solution)/shard_map/project/pallas_call | solution.py:26
  113.4 15.5 %collective-permute-done.11.refs_4_ = bf16[512,1024]{1,0:T(8,128)(2,1)S(1)} collective-permute-done((bf16[512,1024]{1,0:T(8,128)(2,1)}, bf16[512,1024]{1,0:T(8,128)(2,1)S(1)}, u32[]{:S(2)}, u32[]{:S(2)}) %collective-permute-start.11) | collective-permute-done | bytes 1048608 | tf_op jit(solution)/shard_map/ppermute | solution.py:311
  129.2 4.2 %collective-permute-done.9.refs_2_ = bf16[128,192]{1,0:T(8,128)(2,1)S(1)} collective-permute-done((bf16[128,192]{1,0:T(8,128)(2,1)S(1)}, bf16[128,192]{1,0:T(8,128)(2,1)S(1)}, u32[]{:S(2)}, u32[]{:S(2)}) %collective-permute-start.9) | collective-permute-done | bytes 49184 | tf_op jit(solution)/shard_map/ppermute | solution.py:311
  133.4 2.8 %copy-done.3 = bf16[4096,6,128]{2,0,1:T(8,128)(2,1)S(1)} copy-done((bf16[4096,6,128]{2,0,1:T(8,128)(2,1)S(1)}, bf16[4096,6,128]{2,0,1:T(8,128)(2,1)}, u32[]{:S(2)}) %copy-start.3) | copy-done | bytes 6291480
  136.2 6.4 %attend.1.refs_0_ = bf16[512,512]{1,0:T(8,128)(2,1)S(1)} custom-call(s32[8]{0:T(128)S(1)} %pad_add_fusion.2.ids_ref, s32[512,2]{1,0:T(8,128)S(1)} %copy.32.table_ref.refs_5_, f32[512,256]{1,0:T(8,128)S(1)} %copy-done.10, bf16[4,6,64,128]{3,2,1,0:T(8,128)(2,1)S(1)} %bitcast.44, bf16[128,192]{1,0:T(8,128)(2,1)S(1)} %add_convert_fusion.refs_0_, ...), custom_call_target="tpu_custom_call" | custom-call | bytes 30093312 | tf_op jit(solution)/shard_map/attend/pallas_call | solution.py:26
  142.7 2.7 %pad_add_fusion.6 = (s32[5]{0:T(128)S(1)}, s32[5]{0:T(128)S(1)}, s32[5]{0:T(128)S(1)}, s32[5]{0:T(128)S(1)}) fusion(s32[1]{0:T(128)} %get-tuple-element.67.ids_ref, s32[4]{0:T(128)S(1)} %iota.36, s32[1]{0:T(128)} %get-tuple-element.69.ids_ref, s32[1]{0:T(128)} %get-tuple-element.68.ids_ref, s32[1]{0:T(128)} %get-tuple-element.70), kind=kLoop, calls=%fused_computation.27 | loop fusion | flops 20 | bytes 112 | tf_op jit(solution)/shard_map/concatenate | solution.py:279
  151.3 7.1 %collective-permute-done.12.refs_0_ = bf16[512,512]{1,0:T(8,128)(2,1)} collective-permute-done((bf16[512,512]{1,0:T(8,128)(2,1)S(1)}, bf16[512,512]{1,0:T(8,128)(2,1)}, u32[]{:S(2)}, u32[]{:S(2)}) %collective-permute-start.12) | collective-permute-done | bytes 524320 | tf_op jit(solution)/shard_map/ppermute | solution.py:311
  158.4 1.9 copy-done.4
  162.9 2.7 %project_out.5 = (f32[512,1024]{1,0:T(8,128)S(1)}, f32[512,256]{1,0:T(8,128)S(1)}) custom-call(s32[5]{0:T(128)S(1)} %get-tuple-element.65.ids_ref, bf16[512,512]{1,0:T(8,128)(2,1)} %collective-permute-done.12.refs_0_, bf16[8,3,64,1024]{3,2,1,0:T(8,128)(2,1)S(1)} %bitcast.36, bf16[4,4,64,512]{3,2,1,0:T(8,128)(2,1)S(1)} %bitcast.40, ...), custom_call_target="tpu_custom_call" | custom-call | bytes 22020096 | tf_op jit(solution)/shard_map/project_out/pallas_call | solution.py:26
  165.6 7.9 %collective-permute-done.13.refs_0_ = bf16[512,512]{1,0:T(8,128)(2,1)} collective-permute-done((bf16[512,512]{1,0:T(8,128)(2,1)}, bf16[512,512]{1,0:T(8,128)(2,1)}, u32[]{:S(2)}, u32[]{:S(2)}) %collective-permute-start.13) | collective-permute-done | bytes 524320 | tf_op jit(solution)/shard_map/ppermute | solution.py:311
  173.5 6.5 %all_gather.31.refs_6_ = bf16[4,64,1024]{2,1,0:T(8,128)(2,1)S(1)} all-gather(bf16[1,64,1024]{2,1,0:T(8,128)(2,1)S(1)} %copy-done.17), channel_id=1, replica_groups=mesh['groups'=2,'dp'=4,'tensor'=4] {'dp'}, dimensions={0}, use_global_device_ids=true | all-gather | bytes 655360 | tf_op jit(solution)/shard_map/all_gather | solution.py:371
  180.0 2.4 %project_out.6 = (f32[512,1024]{1,0:T(8,128)S(1)}, f32[512,256]{1,0:T(8,128)S(1)}) custom-call(s32[5]{0:T(128)S(1)} %get-tuple-element.63.ids_ref, bf16[512,512]{1,0:T(8,128)(2,1)} %collective-permute-done.13.refs_0_, bf16[8,3,64,1024]{3,2,1,0:T(8,128)(2,1)S(1)} %bitcast.37, bf16[4,4,64,512]{3,2,1,0:T(8,128)(2,1)S(1)} %bitcast.41, ...), custom_call_target="tpu_custom_call" | custom-call | bytes 22020096 | tf_op jit(solution)/shard_map/project_out/pallas_call | solution.py:26
  182.4 5.2 %collective-permute-done.14.refs_0_ = bf16[512,512]{1,0:T(8,128)(2,1)S(1)} collective-permute-done((bf16[512,512]{1,0:T(8,128)(2,1)}, bf16[512,512]{1,0:T(8,128)(2,1)S(1)}, u32[]{:S(2)}, u32[]{:S(2)}) %collective-permute-start.14) | collective-permute-done | bytes 524320 | tf_op jit(solution)/shard_map/ppermute | solution.py:311
  187.6 2.6 %project_out.7 = bf16[512,1024]{1,0:T(8,128)(2,1)} custom-call(s32[5]{0:T(128)S(1)} %get-tuple-element.66.ids_ref, bf16[512,512]{1,0:T(8,128)(2,1)S(1)} %collective-permute-done.14.refs_0_, bf16[8,3,64,1024]{3,2,1,0:T(8,128)(2,1)S(1)} %bitcast.38, bf16[4,4,64,512]{3,2,1,0:T(8,128)(2,1)S(1)} %bitcast.42, f32[512,1024]{1,0:T(8,128)S(1)} %get-tuple-element.53.refs_3_, ...), custom_call_target="tpu_custom_call" | custom-call | bytes 23605248 | tf_op jit(solution)/shard_map/project_out/pallas_call | solution.py:26
  (88 shorter events, 25.7 us)
Async XLA Ops:
  6.5 9.1 %copy-start.21 = (bf16[1,64,4,128]{3,2,1,0:T(4,128)(2,1)S(1)}, bf16[1,64,4,128]{3,2,1,0:T(4,128)(2,1)}, u32[]{:S(2)}) copy-start(bf16[1,64,4,128]{3,2,1,0:T(4,128)(2,1)} %param.14) | copy-start | bytes 196612
  6.5 24.8 %all-gather.7.cloned.1.call-start = ((), (), s32[]{:S(2)}) async-start(), calls=%async_computation | async-start | bytes 1966080 | tf_op jit(solution)/shard_map/all_gather | solution.py:315
  7.3 138.1 %all-gather.9.cloned.1.call-start = ((), (), s32[]{:S(2)}) async-start(), calls=%async_computation.1 | async-start | bytes 1114112 | tf_op jit(solution)/shard_map/all_gather | solution.py:318
  7.3 40.4 %collective-permute-start = (bf16[512,1024]{1,0:T(8,128)(2,1)}, bf16[512,1024]{1,0:T(8,128)(2,1)}, u32[]{:S(2)}, u32[]{:S(2)}) collective-permute-start(bf16[512,1024]{1,0:T(8,128)(2,1)} %token_ref), channel_id=1, source_target_pairs={{0,1},{1,2},{2,3},{3,0},{4,5},{5,6},{6,7},{7,4},{8,9},{9,10},{10,1... | collective-permute-start | bytes 3145736 | tf_op jit(solution)/shard_map/ppermute | solution.py:311
  16.2 16.5 %copy-start.8 = (bf16[512,1024]{1,0:T(8,128)(2,1)S(1)}, bf16[512,1024]{1,0:T(8,128)(2,1)}, u32[]{:S(2)}) copy-start(bf16[512,1024]{1,0:T(8,128)(2,1)} %token_ref) | copy-start | bytes 3145732
  31.3 127.1 %all-gather.11.cloned.1.call-start = ((), (), s32[]{:S(2)}) async-start(), calls=%async_computation.2 | async-start | bytes 3538944 | tf_op jit(solution)/shard_map/all_gather | solution.py:364
  32.7 2.8 %copy-start = (bf16[4096,6,128]{2,0,1:T(8,128)(2,1)S(1)}, bf16[4096,6,128]{2,0,1:T(8,128)(2,1)}, u32[]{:S(2)}) copy-start(bf16[4096,6,128]{2,0,1:T(8,128)(2,1)} %param.10) | copy-start | bytes 18874372
  37.2 2.1 %copy-start.20 = (bf16[1,64,6,128]{3,1,2,0:T(8,128)(2,1)S(1)}, bf16[1,64,6,128]{3,1,2,0:T(8,128)(2,1)}, u32[]{:S(2)}) copy-start(bf16[1,64,6,128]{3,1,2,0:T(8,128)(2,1)} %param.13) | copy-start | bytes 294916
  47.7 51.7 %collective-permute-start.4 = (bf16[512,1024]{1,0:T(8,128)(2,1)}, bf16[512,1024]{1,0:T(8,128)(2,1)}, u32[]{:S(2)}, u32[]{:S(2)}) collective-permute-start(bf16[512,1024]{1,0:T(8,128)(2,1)} %collective-permute-done.refs_0_), channel_id=1, source_target_pairs={{0,1},{1,2},{2,3},{3,0},{4,5},{5,6},{6,7},{7,4},{8,9},{9,10},{10,1... | collective-permute-start | bytes 3145736 | tf_op jit(solution)/shard_map/ppermute | solution.py:311
  53.5 29.4 %collective-permute-start.1 = (f32[128,192]{1,0:T(8,128)S(1)}, f32[128,192]{1,0:T(8,128)S(1)}, u32[]{:S(2)}, u32[]{:S(2)}) collective-permute-start(f32[128,192]{1,0:T(8,128)S(1)} %get-tuple-element.34), channel_id=1, source_target_pairs={{0,1},{1,2},{2,3},{3,0},{4,5},{5,6},{6,7},{7,4},{8,9},{9,10},{10,1... | collective-permute-start | bytes 294920 | tf_op jit(solution)/shard_map/ppermute | solution.py:311
  55.0 33.8 %collective-permute-start.2 = (f32[128,192]{1,0:T(8,128)S(1)}, f32[128,192]{1,0:T(8,128)S(1)}, u32[]{:S(2)}, u32[]{:S(2)}) collective-permute-start(f32[128,192]{1,0:T(8,128)S(1)} %get-tuple-element.35), channel_id=1, source_target_pairs={{0,2},{1,3},{2,0},{3,1},{4,6},{5,7},{6,4},{7,5},{8,10},{9,11},{10,... | collective-permute-start | bytes 294920 | tf_op jit(solution)/shard_map/ppermute | solution.py:311
  56.4 39.3 %collective-permute-start.3 = (f32[128,192]{1,0:T(8,128)S(1)}, f32[128,192]{1,0:T(8,128)S(1)}, u32[]{:S(2)}, u32[]{:S(2)}) collective-permute-start(f32[128,192]{1,0:T(8,128)S(1)} %get-tuple-element.36), channel_id=1, source_target_pairs={{0,3},{1,0},{2,1},{3,2},{4,7},{5,4},{6,5},{7,6},{8,11},{9,8},{10,9... | collective-permute-start | bytes 294920 | tf_op jit(solution)/shard_map/ppermute | solution.py:311
  58.9 2.8 %copy-start.1 = (bf16[4096,6,128]{2,0,1:T(8,128)(2,1)S(1)}, bf16[4096,6,128]{2,0,1:T(8,128)(2,1)}, u32[]{:S(2)}) copy-start(bf16[4096,6,128]{2,0,1:T(8,128)(2,1)} %param.10) | copy-start | bytes 18874372
  61.6 21.2 %copy-start.19 = (bf16[64,1024]{1,0:T(8,128)(2,1)S(1)}, bf16[64,1024]{1,0:T(8,128)(2,1)}, u32[]{:S(2)}) copy-start(bf16[64,1024]{1,0:T(8,128)(2,1)} %get-tuple-element.38) | copy-start | bytes 393220
  61.6 27.2 %copy-start.18 = (bf16[64,1024]{1,0:T(8,128)(2,1)S(1)}, bf16[64,1024]{1,0:T(8,128)(2,1)}, u32[]{:S(2)}) copy-start(bf16[64,1024]{1,0:T(8,128)(2,1)} %get-tuple-element.39) | copy-start | bytes 393220
  64.6 31.2 %collective-permute-start.5 = (bf16[64,1024]{1,0:T(8,128)(2,1)S(1)}, bf16[64,1024]{1,0:T(8,128)(2,1)S(1)}, u32[]{:S(2)}, u32[]{:S(2)}) collective-permute-start(bf16[64,1024]{1,0:T(8,128)(2,1)S(1)} %bitcast.46), channel_id=1, source_target_pairs={{0,1},{1,2},{2,3},{3,0},{4,5},{5,6},{6,7},{7,4},{8,9},{9,10},{10,1... | collective-permute-start | bytes 393224 | tf_op jit(solution)/shard_map/ppermute | solution.py:311
  82.9 16.4 %collective-permute-start.6 = (bf16[64,1024]{1,0:T(8,128)(2,1)S(1)}, bf16[64,1024]{1,0:T(8,128)(2,1)S(1)}, u32[]{:S(2)}, u32[]{:S(2)}) collective-permute-start(bf16[64,1024]{1,0:T(8,128)(2,1)S(1)} %copy-done.19), channel_id=1, source_target_pairs={{0,2},{1,3},{2,0},{3,1},{4,6},{5,7},{6,4},{7,5},{8,10},{9,11},{10,... | collective-permute-start | bytes 393224 | tf_op jit(solution)/shard_map/ppermute | solution.py:311
  88.8 10.5 %collective-permute-start.7 = (bf16[64,1024]{1,0:T(8,128)(2,1)S(1)}, bf16[64,1024]{1,0:T(8,128)(2,1)S(1)}, u32[]{:S(2)}, u32[]{:S(2)}) collective-permute-start(bf16[64,1024]{1,0:T(8,128)(2,1)S(1)} %copy-done.18), channel_id=1, source_target_pairs={{0,3},{1,0},{2,1},{3,2},{4,7},{5,4},{6,5},{7,6},{8,11},{9,8},{10,9... | collective-permute-start | bytes 393224 | tf_op jit(solution)/shard_map/ppermute | solution.py:311
  100.2 28.7 %collective-permute-start.11 = (bf16[512,1024]{1,0:T(8,128)(2,1)}, bf16[512,1024]{1,0:T(8,128)(2,1)S(1)}, u32[]{:S(2)}, u32[]{:S(2)}) collective-permute-start(bf16[512,1024]{1,0:T(8,128)(2,1)} %collective-permute-done.4.refs_0_), channel_id=1, source_target_pairs={{0,1},{1,2},{2,3},{3,0},{4,5},{5,6},{6,7},{7,4},{8,9},{9,10},{10,1... | collective-permute-start | bytes 3145736 | tf_op jit(solution)/shard_map/ppermute | solution.py:311
  103.6 25.6 %collective-permute-start.10 = (bf16[128,192]{1,0:T(8,128)(2,1)S(1)}, bf16[128,192]{1,0:T(8,128)(2,1)S(1)}, u32[]{:S(2)}, u32[]{:S(2)}) collective-permute-start(bf16[128,192]{1,0:T(8,128)(2,1)S(1)} %add_convert_fusion.refs_0_), channel_id=1, source_target_pairs={{0,3},{1,0},{2,1},{3,2},{4,7},{5,4},{6,5},{7,6},{8,11},{9,8},{10,9... | collective-permute-start | bytes 147464 | tf_op jit(solution)/shard_map/ppermute | solution.py:311
  104.7 28.7 %collective-permute-start.9 = (bf16[128,192]{1,0:T(8,128)(2,1)S(1)}, bf16[128,192]{1,0:T(8,128)(2,1)S(1)}, u32[]{:S(2)}, u32[]{:S(2)}) collective-permute-start(bf16[128,192]{1,0:T(8,128)(2,1)S(1)} %add_convert_fusion.refs_0_), channel_id=1, source_target_pairs={{0,2},{1,3},{2,0},{3,1},{4,6},{5,7},{6,4},{7,5},{8,10},{9,11},{10,... | collective-permute-start | bytes 147464 | tf_op jit(solution)/shard_map/ppermute | solution.py:311
  105.2 28.2 %collective-permute-start.8 = (bf16[128,192]{1,0:T(8,128)(2,1)S(1)}, bf16[128,192]{1,0:T(8,128)(2,1)S(1)}, u32[]{:S(2)}, u32[]{:S(2)}) collective-permute-start(bf16[128,192]{1,0:T(8,128)(2,1)S(1)} %add_convert_fusion.refs_0_), channel_id=1, source_target_pairs={{0,1},{1,2},{2,3},{3,0},{4,5},{5,6},{6,7},{7,4},{8,9},{9,10},{10,1... | collective-permute-start | bytes 147464 | tf_op jit(solution)/shard_map/ppermute | solution.py:311
  107.3 3.1 %copy-start.2 = (bf16[4096,6,128]{2,0,1:T(8,128)(2,1)S(1)}, bf16[4096,6,128]{2,0,1:T(8,128)(2,1)}, u32[]{:S(2)}) copy-start(bf16[4096,6,128]{2,0,1:T(8,128)(2,1)} %param.10) | copy-start | bytes 18874372
  110.4 23.0 %copy-start.10 = (f32[512,256]{1,0:T(8,128)S(1)}, f32[512,256]{1,0:T(8,128)}, u32[]{:S(2)}) copy-start(f32[512,256]{1,0:T(8,128)} %pad_maximum_fusion.turn_ref) | copy-start | bytes 1572868
  110.4 23.0 %copy-start.13 = (bf16[24,64,128]{2,1,0:T(8,128)(2,1)S(1)}, bf16[24,64,128]{2,1,0:T(8,128)(2,1)}, u32[]{:S(2)}) copy-start(bf16[24,64,128]{2,1,0:T(8,128)(2,1)} %all-gather) | copy-start | bytes 1179652
  133.4 2.8 %copy-start.3 = (bf16[4096,6,128]{2,0,1:T(8,128)(2,1)S(1)}, bf16[4096,6,128]{2,0,1:T(8,128)(2,1)}, u32[]{:S(2)}) copy-start(bf16[4096,6,128]{2,0,1:T(8,128)(2,1)} %param.10) | copy-start | bytes 18874372
  142.6 15.8 %collective-permute-start.12 = (bf16[512,512]{1,0:T(8,128)(2,1)S(1)}, bf16[512,512]{1,0:T(8,128)(2,1)}, u32[]{:S(2)}, u32[]{:S(2)}) collective-permute-start(bf16[512,512]{1,0:T(8,128)(2,1)S(1)} %attend.1.refs_0_), channel_id=1, source_target_pairs={{0,1},{1,2},{2,3},{3,0},{4,5},{5,6},{6,7},{7,4},{8,9},{9,10},{10,1... | collective-permute-start | bytes 1572872 | tf_op jit(solution)/shard_map/ppermute | solution.py:311
  147.8 10.6 %copy-start.7 = (bf16[1024,512]{1,0:T(8,128)(2,1)S(1)}, bf16[1024,512]{1,0:T(8,128)(2,1)}, u32[]{:S(2)}) copy-start(bf16[1024,512]{1,0:T(8,128)(2,1)} %all-gather.9.cloned.1.call-done) | copy-start | bytes 3145732
  158.4 15.1 %collective-permute-start.13 = (bf16[512,512]{1,0:T(8,128)(2,1)}, bf16[512,512]{1,0:T(8,128)(2,1)}, u32[]{:S(2)}, u32[]{:S(2)}) collective-permute-start(bf16[512,512]{1,0:T(8,128)(2,1)} %collective-permute-done.12.refs_0_), channel_id=1, source_target_pairs={{0,1},{1,2},{2,3},{3,0},{4,5},{5,6},{6,7},{7,4},{8,9},{9,10},{10,1... | collective-permute-start | bytes 1572872 | tf_op jit(solution)/shard_map/ppermute | solution.py:311
  162.9 10.6 %copy-start.17 = (bf16[1,64,1024]{2,1,0:T(8,128)(2,1)S(1)}, bf16[1,64,1024]{2,1,0:T(8,128)(2,1)}, u32[]{:S(2)}) copy-start(bf16[1,64,1024]{2,1,0:T(8,128)(2,1)} %param.15) | copy-start | bytes 393220
  162.9 17.1 %copy-start.5 = (bf16[24,64,1024]{2,1,0:T(8,128)(2,1)S(1)}, bf16[24,64,1024]{2,1,0:T(8,128)(2,1)}, u32[]{:S(2)}) copy-start(bf16[24,64,1024]{2,1,0:T(8,128)(2,1)} %all-gather.11.cloned.1.call-done) | copy-start | bytes 9437188
  173.5 14.1 %collective-permute-start.14 = (bf16[512,512]{1,0:T(8,128)(2,1)}, bf16[512,512]{1,0:T(8,128)(2,1)S(1)}, u32[]{:S(2)}, u32[]{:S(2)}) collective-permute-start(bf16[512,512]{1,0:T(8,128)(2,1)} %collective-permute-done.13.refs_0_), channel_id=1, source_target_pairs={{0,1},{1,2},{2,3},{3,0},{4,5},{5,6},{6,7},{7,4},{8,9},{9,10},{10,1... | collective-permute-start | bytes 1572872 | tf_op jit(solution)/shard_map/ppermute | solution.py:311
  (8 other events, 10.5 us)
Sparse Core Ops, SparseCore 0:
  8.9 22.3 all-gather.6
  33.5 55.4 all-gather.8
  100.3 33.3 all-gather.10

commit v8 on v7

--- a/solution.py
+++ b/solution.py
@@ -205,81 +205,73 @@
     )
 
 
-def output_kernel(groups, begun, last, ids_ref, *refs):
-    attended_refs, w_refs, rest = refs[:groups], refs[groups : 2 * groups], refs[2 * groups :]
-    down_ref, rest = rest[0], rest[1:]
-    begun_refs, rest = rest[:begun], rest[begun:]
+def output_kernel(begun, last, lines, ids_ref, attended_ref, w_ref, down_ref, *refs):
+    begun_refs, rest = refs[:begun], refs[begun:]
     if last:
         table_ref, up_ref, out_ref = rest
     else:
         acc_ref, low_ref = rest
-    count = ids_ref.shape[0] - groups
-    step = pl.program_id(0)
-    down = jnp.concatenate([down_ref[ids_ref[groups + j], 0] for j in range(count)], axis=0)
-    rank = down_ref.shape[2]
-
-    def one(number):
-        w_ref = w_refs[number]
-        if len(w_ref.shape) == 2:
-            weight = w_ref[...]
-        else:
-            weight = jnp.concatenate([w_ref[i, 0] for i in range(w_ref.shape[0])], axis=0)
-        attended = attended_refs[number][...]
-        total = jnp.dot(attended, weight, preferred_element_type=jnp.float32)
-        low = lax.dot_general(
-            attended, down, (((1,), (1,)), ((), ())), preferred_element_type=jnp.float32
-        )
-        if number:
-            total, low = acc_ref[...] + total, low_ref[...] + low
-        elif begun:
-            total, low = begun_refs[0][...] + total, begun_refs[1][...] + low
-        if last:
-            low = low.astype(jnp.bfloat16).astype(jnp.float32)
-            lane = lax.broadcasted_iota(jnp.int32, low.shape, 1)
-            kept = (lane >= table_ref[:, 1:2]) & (lane < table_ref[:, 1:2] + rank)
-            low = jnp.where(kept, low, 0.0).astype(jnp.bfloat16)
-            up = jnp.concatenate([up_ref[ids_ref[groups + j]] for j in range(count)], axis=0)
-            extra = jnp.dot(low, up, preferred_element_type=jnp.float32)
-            out_ref[...] = (total + extra).astype(jnp.bfloat16)
-        else:
-            acc_ref[...] = total
-            low_ref[...] = low
-
-    for number in range(groups):
-        pl.when(step == number)(functools.partial(one, number))
-
-
-def project_out(planes_of, adapters, attended, weights, down, begun, final):
-    groups = len(attended)
-    rows, features = attended[0].shape
-    rank = down.shape[2]
-    columns = weights[0][0].shape[-1]
-    w_arrays, w_specs = [], []
-    for array, turn in weights:
-        w_arrays.append(array)
-        if turn is None:
-            w_specs.append(None)
-        else:
-            w_specs.append(
-                pl.BlockSpec(
-                    (array.shape[0], 1) + array.shape[2:],
-                    lambda step, ids, turn=turn: (0, turn, 0, 0),
-                )
-            )
-    down_spec = pl.BlockSpec(
-        (down.shape[0], 1) + down.shape[2:], lambda step, ids: (0, ids[step], 0, 0)
-    )
+    count = ids_ref.shape[0] - 1
+    attended = attended_ref[...]
+    features = attended.shape[1]
+    if lines:
+        weight = jnp.concatenate([w_ref[i, 0, lines:] for i in range(w_ref.shape[0])], axis=0)
+    else:
+        weight = w_ref[...]
+    downs = []
+    for j in range(count):
+        down = down_ref[ids_ref[1 + j], 0] if lines else down_ref[ids_ref[1 + j]]
+        downs += [down[:, at : at + features] for at in range(0, down.shape[1], features)]
+    down = jnp.concatenate(downs, axis=0)
+    rank = down.shape[0] // count
+    total = jnp.dot(attended, weight, preferred_element_type=jnp.float32)
+    low = lax.dot_general(
+        attended, down, (((1,), (1,)), ((), ())), preferred_element_type=jnp.float32
+    )
+    if begun:
+        total, low = begun_refs[0][...] + total, begun_refs[1][...] + low
+    if last:
+        low = low.astype(jnp.bfloat16).astype(jnp.float32)
+        lane = lax.broadcasted_iota(jnp.int32, low.shape, 1)
+        kept = (lane >= table_ref[:, 1:2]) & (lane < table_ref[:, 1:2] + rank)
+        low = jnp.where(kept, low, 0.0).astype(jnp.bfloat16)
+        up = jnp.concatenate([up_ref[ids_ref[1 + j]] for j in range(count)], axis=0)
+        extra = jnp.dot(low, up, preferred_element_type=jnp.float32)
+        out_ref[...] = (total + extra).astype(jnp.bfloat16)
+    else:
+        acc_ref[...] = total
+        low_ref[...] = low
+
+
+def project_out(ids, rank, attended, weight, down, begun, final, turn=None):
+    rows, features = attended.shape
+    columns = weight.shape[-1]
+    if turn is None:
+        specs, down_rows = [None, None, None], 0
+    else:
+        down_rows = rank * features // columns
+        specs = [
+            None,
+            pl.BlockSpec(
+                (weight.shape[0], 1) + weight.shape[2:], lambda step, ids: (0, turn - 1, 0, 0)
+            ),
+            pl.BlockSpec(
+                (down, 1, down_rows, columns),
+                lambda step, ids: (ids[0], turn - 1, 0, 0),
+            ),
+        ]
+        down = weight
     sums = (
         jax.ShapeDtypeStruct((rows, columns), jnp.float32),
-        jax.ShapeDtypeStruct((rows, adapters.shape[0] * rank), jnp.float32),
+        jax.ShapeDtypeStruct((rows, (ids.shape[0] - 1) * rank), jnp.float32),
     )
     return call(
-        functools.partial(output_kernel, groups, len(begun), bool(final)),
+        functools.partial(output_kernel, len(begun), bool(final), down_rows),
         "project_out",
-        jnp.concatenate([planes_of, adapters]),
-        groups,
-        [None] * groups + w_specs + [down_spec] + [None] * (len(begun) + len(final)),
-        [*attended, *w_arrays, down, *begun, *final],
+        ids,
+        1,
+        specs + [None] * (len(begun) + len(final)),
+        [attended, weight, down, *begun, *final],
         jax.ShapeDtypeStruct((rows, columns), jnp.bfloat16) if final else sums,
     )
 
@@ -314,9 +306,6 @@
     weight = jnp.transpose(query_key_value_weight, (1, 0, 2))
     down_all = lax.all_gather(adapter_down_maps, "dp", axis=0, tiled=True)
     up_all = lax.all_gather(jnp.transpose(adapter_up_maps[0], (1, 0, 2)), "dp", axis=0)
-    out_down = output_down_maps[0].reshape(rank, features)
-    out_downs = lax.all_gather(after(out_down, down_all), ("dp", "tensor"), axis=0)
-    out_downs = out_downs.reshape(pool, planes, rank, features)
 
     requests = request_adapter.shape[1]
     request_ends = jnp.cumsum(lengths[0])
@@ -345,14 +334,23 @@
         output_weight, (line % head_size, line // head_size, 0),
         (share, 1, output_weight.shape[2]),
     )[:, 0]
+    out_down = output_down_maps[0].reshape(rank, features)
+    out_down = jnp.concatenate(jnp.split(out_down, columns // features, axis=0), axis=1)
     sends = [
-        lax.dynamic_slice_in_dim(piece, (here + k) % planes * columns, columns, axis=1)
+        jnp.concatenate(
+            [
+                out_down,
+                lax.dynamic_slice_in_dim(piece, (here + k) % planes * columns, columns, axis=1),
+            ],
+            axis=0,
+        )
         for k in range(1, planes)
     ]
 
     begun = project(planes_of[:1], held[:1], weight)
-    held[1] = after(held[1], begun, up_all, table, turn, own_rows, *sends)
-    lines = [turned(after(send, held[1]), k) for k, send in enumerate(sends, 1)]
+    lines = [turned(send, k) for k, send in enumerate(sends, 1)]
+    held[1] = after(held[1], begun, up_all, table, turn, own_rows, *lines)
+    lines = lax.all_gather(jnp.stack(lines), PLANE, axis=0)
     sums = shrink_partial(adapters, here, planes, table, after(tokens, held[1]), down_all)
     sums = [sums[0]] + [turned(sums[k], k) for k in range(1, planes)]
     shrink = sum(sums[1:], sums[0]).astype(jnp.bfloat16)
@@ -360,28 +358,26 @@
         arrived = held[-1]
         held.append(turned(arrived))
         begun = project(planes_of[step - 1 : step], [arrived], weight, [begun])
-        held[-1] = after(held[-1], begun, *([shrink, *lines] if step == 2 else []))
-    lines = lax.all_gather(jnp.stack([after(line, held[2]) for line in lines]), PLANE, axis=0)
+        held[-1] = after(held[-1], begun, *([shrink] if step == 2 else []))
     shrink = after(shrink, held[2])
     shrink = [shrink] + [turned(shrink, k) for k in range(1, planes)]
+    out_up_all = lax.all_gather(after(output_up_maps, held[2]), "dp", axis=0, tiled=True)
+    own_down = lax.all_gather(after(out_down, held[2]), "dp", axis=0)
+    held[-1] = after(held[-1], out_up_all, own_down)
     attended = [
         attend(planes_of, adapters, table, turn, up_all, shrink, held[-1], weight, begun)
     ]
 
-    out_up_all = lax.all_gather(
-        after(output_up_maps, attended[0]), "dp", axis=0, tiled=True
-    )
+    ids = jnp.concatenate([lax.axis_index("groups")[None], adapters])
     attended.append(turned(attended[0]))
-    sums = project_out(
-        planes_of[:1], adapters, attended[:1], [(own_rows, None)], out_downs, [], []
-    )
+    sums = project_out(ids, rank, attended[0], own_rows, own_down, [], [])
     for step in range(2, planes + 1):
         arrived = after(attended[-1], *sums)
         if step < planes:
             attended.append(turned(arrived))
         sums = project_out(
-            planes_of[step - 1 : step], adapters, [arrived], [(lines, step - 2)], out_downs,
-            list(sums), [] if step < planes else [table, out_up_all],
+            ids, rank, arrived, lines, pool, list(sums),
+            [] if step < planes else [table, out_up_all], step - 1,
         )
     return sums
 

time: 198 us -> 186 us (0.939)
  local copies, waits for them, and re-layouts: 30.2 us -> 19.4 us
  blocking collectives: 14.1 us -> 22 us
  starting transfers between devices: 30 us -> 24.5 us
  other arithmetic: 7.5 us -> 2.88 us
  waiting for transfers between devices: 76 us -> 79.2 us
  Pallas kernels: 25.7 us -> 23.3 us
    ppermute x15, waiting for transfers between devices: 61.9 us -> 78.5 us  [turned(): lax.ppermute(value, 'tensor', [(i, (i + turn) % planes) for i in range(pl...]
    all_gather x1, waiting for transfers between devices: 13.4 us -> 0.01 us  [local(): down_all = lax.all_gather(adapter_down_maps, 'dp', axis=0, tiled=True)]
    unnamed x46 -> x36, local copies, waits for them, and re-layouts: 22.7 us -> 12.7 us
    all_gather x1 -> x2, blocking collectives: 6.5 us -> 13.3 us  [the longest x1 7.27 us: local(): lax.all_gather(after(output_up_maps, held[2]), 'dp', axis=0, tiled=True)]
    ppermute x15, starting transfers between devices: 29.9 us -> 24.5 us  [turned(): lax.ppermute(value, 'tensor', [(i, (i + turn) % planes) for i in range(pl...]
    concatenate x1 -> x2, other arithmetic: 2.68 us -> 0.13 us  [the longest x1 0.08 us: local(): ids = jnp.concatenate([lax.axis_index('groups')[None], adapters])]
    pallas_call x9, Pallas kernels: 25.7 us -> 23.3 us  [call(): pl.pallas_call(kernel, out_shape=out, grid_spec=pltpu.PrefetchScalarGridS...]
  transfers between devices with their start and end apart: 18 -> 17, of which waited for: 9 -> 12; matrix products, arithmetic and copies ran while one was open for 8% -> 5% of each run, Pallas kernels for 12% -> 11%
where the time goes in v8:
time: 186 us; the launch traced here: 185 us
  waiting for transfers between devices  79.2 us (43%)
  starting transfers between devices  24.5 us (13%)
  Pallas kernels  23.3 us (13%)
  blocking collectives  22 us (12%)
  local copies, waits for them, and re-layouts  19.4 us (10%)
  between operations  13.8 us (7%)
  other arithmetic  2.88 us (2%)
    ppermute x15, waiting for transfers between devices, turned(): lax.ppermute(value, 'tensor', [(i, (i + turn) % planes) for i in range(pl...  78.5 us
    ppermute x15, starting transfers between devices, turned(): lax.ppermute(value, 'tensor', [(i, (i + turn) % planes) for i in range(pl...  24.5 us
    pallas_call x9, Pallas kernels, call(): pl.pallas_call(kernel, out_shape=out, grid_spec=pltpu.PrefetchScalarGridS...  23.3 us
    unnamed x36, local copies, waits for them, and re-layouts  12.7 us
    all_gather x1, blocking collectives, local(): lax.all_gather(jnp.transpose(adapter_up_maps[0], (1, 0, 2)), 'dp', axis=0)  8.7 us
    all_gather x1, blocking collectives, local(): lax.all_gather(after(output_up_maps, held[2]), 'dp', axis=0, tiled=True)  7.27 us
    all_gather x1, blocking collectives, local(): own_down = lax.all_gather(after(out_down, held[2]), 'dp', axis=0)  6.03 us
  transfers between devices with their start and end apart: 17, of which 12 were waited for; matrix products, arithmetic and copies ran while one was open for 5% of the time, Pallas kernels for 11%

profile of v8, /device:TPU:0, one launch (start us, length us, event | category | flops | bytes accessed | tf_op | source)
XLA Modules:
  0.0 185.1 jit_solution(16285514782563485718)
XLA Ops:
  7.4 2.8 %fusion.4 = (bf16[64,1,1024]{2,1,0:T(2,128)(2,1)S(1)}, bf16[64,1,1024]{2,1,0:T(2,128)(2,1)S(1)}, bf16[64,1,1024]{2,1,0:T(2,128)(2,1)S(1)}) fusion(bf16[128,4,4096]{2,1,0:T(4,128)(2,1)} %param.11, s32[]{:T(128)S(6)} %select_n.66, s32[]{:T(128)S(6)} %select_n.69, s32[]{:T(128)S(6)} %select_n.78, s32[]{:T(128)S(6)} %select_n.75, s32[]{:T(128)S(6)} %select_n.72), kind=kLoop, calls=%fused_computation.32 | loop fusion | bytes 786452 | tf_op jit(solution)/shard_map/dynamic_slice | solution.py:343
  10.5 3.1 %collective-permute-start.1 = (bf16[96,1024]{1,0:T(8,128)(2,1)S(1)}, bf16[96,1024]{1,0:T(8,128)(2,1)S(1)}, u32[]{:S(2)}, u32[]{:S(2)}) collective-permute-start(bf16[96,1024]{1,0:T(8,128)(2,1)S(1)} %get-tuple-element.52), channel_id=1, source_target_pairs={{0,1},{1,2},{2,3},{3,0},{4,5},{5,6},{6,7},{7,4},{8,9},{9,10},{10,1... | collective-permute-start | bytes 589832 | tf_op jit(solution)/shard_map/ppermute | solution.py:303
  13.6 2.6 %collective-permute-start.2 = (bf16[96,1024]{1,0:T(8,128)(2,1)S(1)}, bf16[96,1024]{1,0:T(8,128)(2,1)S(1)}, u32[]{:S(2)}, u32[]{:S(2)}) collective-permute-start(bf16[96,1024]{1,0:T(8,128)(2,1)S(1)} %get-tuple-element.51), channel_id=1, source_target_pairs={{0,2},{1,3},{2,0},{3,1},{4,6},{5,7},{6,4},{7,5},{8,10},{9,11},{10,... | collective-permute-start | bytes 589832 | tf_op jit(solution)/shard_map/ppermute | solution.py:303
  17.5 4.0 %collective-permute-done.1 = bf16[96,1024]{1,0:T(8,128)(2,1)S(1)} collective-permute-done((bf16[96,1024]{1,0:T(8,128)(2,1)S(1)}, bf16[96,1024]{1,0:T(8,128)(2,1)S(1)}, u32[]{:S(2)}, u32[]{:S(2)}) %collective-permute-start.1) | collective-permute-done | bytes 196640 | tf_op jit(solution)/shard_map/ppermute | solution.py:303
  21.5 7.6 %collective-permute-done.2 = bf16[96,1024]{1,0:T(8,128)(2,1)S(1)} collective-permute-done((bf16[96,1024]{1,0:T(8,128)(2,1)S(1)}, bf16[96,1024]{1,0:T(8,128)(2,1)S(1)}, u32[]{:S(2)}, u32[]{:S(2)}) %collective-permute-start.2) | collective-permute-done | bytes 196640 | tf_op jit(solution)/shard_map/ppermute | solution.py:303
  30.0 4.7 %collective-permute-start = (bf16[512,1024]{1,0:T(8,128)(2,1)S(1)}, bf16[512,1024]{1,0:T(8,128)(2,1)}, u32[]{:S(2)}, u32[]{:S(2)}) collective-permute-start(bf16[512,1024]{1,0:T(8,128)(2,1)S(1)} %copy-done.4), channel_id=1, source_target_pairs={{0,1},{1,2},{2,3},{3,0},{4,5},{5,6},{6,7},{7,4},{8,9},{9,10},{10,1... | collective-permute-start | bytes 3145736 | tf_op jit(solution)/shard_map/ppermute | solution.py:303
  35.0 1.6 dynamic-slice_bitcast_fusion
  38.5 3.1 %copy-done.2 = bf16[4096,6,128]{2,0,1:T(8,128)(2,1)S(1)} copy-done((bf16[4096,6,128]{2,0,1:T(8,128)(2,1)S(1)}, bf16[4096,6,128]{2,0,1:T(8,128)(2,1)}, u32[]{:S(2)}) %copy-start.2) | copy-done | bytes 6291480
  41.6 1.6 project.3.refs_2_
  44.8 8.7 %all-gather = bf16[24,64,128]{2,1,0:T(8,128)(2,1)} all-gather(bf16[6,64,128]{2,1,0:T(8,128)(2,1)S(1)} %bitcast.57), channel_id=2, replica_groups=mesh['groups'=2,'dp'=4,'tensor'=4] {'dp'}, dimensions={0}, use_global_device_ids=true | all-gather | bytes 491520 | tf_op jit(solution)/shard_map/all_gather | solution.py:308
  53.5 4.7 %collective-permute-done.refs_0_ = bf16[512,1024]{1,0:T(8,128)(2,1)} collective-permute-done((bf16[512,1024]{1,0:T(8,128)(2,1)S(1)}, bf16[512,1024]{1,0:T(8,128)(2,1)}, u32[]{:S(2)}, u32[]{:S(2)}) %collective-permute-start) | collective-permute-done | bytes 1048608 | tf_op jit(solution)/shard_map/ppermute | solution.py:303
  58.2 1.8 collective-permute-start.7
  61.6 2.7 %shrink.1 = (f32[128,192]{1,0:T(8,128)S(1)}, f32[128,192]{1,0:T(8,128)S(1)}, f32[128,192]{1,0:T(8,128)S(1)}, f32[128,192]{1,0:T(8,128)S(1)}) custom-call(s32[5]{0:T(128)S(1)} %pad_add_fusion.3.ids_ref, s32[512,2]{1,0:T(8,128)S(1)} %copy.32.table_ref.refs_2_, bf16[512,1024]{1,0:T(8,128)(2,1)S(1)} %copy-done.4, bf16[4,192,1024]{2,1,0:T(8,128)(2,1)S(1)} %copy-done.9), custom_call_target="tpu_custom_call" | custom-call | bytes 7876608 | tf_op jit(solution)/shard_map/shrink/pallas_call | solution.py:26
  64.6 2.3 %collective-permute-start.5 = (f32[128,192]{1,0:T(8,128)S(1)}, f32[128,192]{1,0:T(8,128)S(1)}, u32[]{:S(2)}, u32[]{:S(2)}) collective-permute-start(f32[128,192]{1,0:T(8,128)S(1)} %get-tuple-element.30), channel_id=1, source_target_pairs={{0,2},{1,3},{2,0},{3,1},{4,6},{5,7},{6,4},{7,5},{8,10},{9,11},{10,... | collective-permute-start | bytes 294920 | tf_op jit(solution)/shard_map/ppermute | solution.py:303
  68.1 2.8 %copy-done.3 = bf16[4096,6,128]{2,0,1:T(8,128)(2,1)S(1)} copy-done((bf16[4096,6,128]{2,0,1:T(8,128)(2,1)S(1)}, bf16[4096,6,128]{2,0,1:T(8,128)(2,1)}, u32[]{:S(2)}) %copy-start.3) | copy-done | bytes 6291480
  71.0 2.9 %project.4.refs_2_ = f32[512,768]{1,0:T(8,128)S(1)} custom-call(s32[1]{0:T(128)} %get-tuple-element.59.ids_ref, bf16[512,1024]{1,0:T(8,128)(2,1)} %collective-permute-done.refs_0_, bf16[6,4096,128]{2,1,0:T(8,128)(2,1)S(1)} %bitcast.43, f32[512,768]{1,0:T(8,128)S(1)} %project.3.refs_2_), custom_call_target="tpu_custom_call" | custom-call | bytes 26738688 | tf_op jit(solution)/shard_map/project/pallas_call | solution.py:26
  73.9 15.3 %collective-permute-done.4 = f32[128,192]{1,0:T(8,128)S(1)} collective-permute-done((f32[128,192]{1,0:T(8,128)S(1)}, f32[128,192]{1,0:T(8,128)S(1)}, u32[]{:S(2)}, u32[]{:S(2)}) %collective-permute-start.4) | collective-permute-done | bytes 98336 | tf_op jit(solution)/shard_map/ppermute | solution.py:303
  89.2 2.9 %collective-permute-done.5 = f32[128,192]{1,0:T(8,128)S(1)} collective-permute-done((f32[128,192]{1,0:T(8,128)S(1)}, f32[128,192]{1,0:T(8,128)S(1)}, u32[]{:S(2)}, u32[]{:S(2)}) %collective-permute-start.5) | collective-permute-done | bytes 98336 | tf_op jit(solution)/shard_map/ppermute | solution.py:303
  92.2 3.3 %collective-permute-start.11 = (bf16[512,1024]{1,0:T(8,128)(2,1)}, bf16[512,1024]{1,0:T(8,128)(2,1)S(1)}, u32[]{:S(2)}, u32[]{:S(2)}) collective-permute-start(bf16[512,1024]{1,0:T(8,128)(2,1)} %collective-permute-done.7.refs_0_), channel_id=1, source_target_pairs={{0,1},{1,2},{2,3},{3,0},{4,5},{5,6},{6,7},{7,4},{8,9},{9,10},{10,1... | collective-permute-start | bytes 3145736 | tf_op jit(solution)/shard_map/ppermute | solution.py:303
  97.7 1.7 collective-permute-start.9
  99.4 7.3 %all_gather.27.refs_3_ = bf16[4,64,1024]{2,1,0:T(8,128)(2,1)S(1)} all-gather(bf16[1,64,1024]{2,1,0:T(8,128)(2,1)S(1)} %copy-done.10), channel_id=1, replica_groups=mesh['groups'=2,'dp'=4,'tensor'=4] {'dp'}, dimensions={0}, use_global_device_ids=true | all-gather | bytes 655360 | tf_op jit(solution)/shard_map/all_gather | solution.py:364
  106.6 6.0 %all-gather.1 = bf16[128,1024]{1,0:T(8,128)(2,1)S(1)} all-gather(bf16[32,1024]{1,0:T(8,128)(2,1)S(1)} %bitcast_dynamic-update-slice_fusion), channel_id=3, replica_groups=mesh['groups'=2,'dp'=4,'tensor'=4] {'dp'}, dimensions={0}, use_global_device_ids=true | all-gather | bytes 327680 | tf_op jit(solution)/shard_map/all_gather | solution.py:365
  112.7 3.0 %project.5.refs_6_ = f32[512,768]{1,0:T(8,128)S(1)} custom-call(s32[1]{0:T(128)} %get-tuple-element.58.ids_ref, bf16[512,1024]{1,0:T(8,128)(2,1)} %collective-permute-done.7.refs_0_, bf16[6,4096,128]{2,1,0:T(8,128)(2,1)S(1)} %bitcast.44, f32[512,768]{1,0:T(8,128)S(1)} %project.4.refs_2_), custom_call_target="tpu_custom_call" | custom-call | bytes 26738688 | tf_op jit(solution)/shard_map/project/pallas_call | solution.py:26
  115.6 5.4 %collective-permute-done.11.refs_4_ = bf16[512,1024]{1,0:T(8,128)(2,1)S(1)} collective-permute-done((bf16[512,1024]{1,0:T(8,128)(2,1)}, bf16[512,1024]{1,0:T(8,128)(2,1)S(1)}, u32[]{:S(2)}, u32[]{:S(2)}) %collective-permute-start.11) | collective-permute-done | bytes 1048608 | tf_op jit(solution)/shard_map/ppermute | solution.py:303
  122.8 2.1 %collective-permute-done.9.refs_2_ = bf16[128,192]{1,0:T(8,128)(2,1)S(1)} collective-permute-done((bf16[128,192]{1,0:T(8,128)(2,1)S(1)}, bf16[128,192]{1,0:T(8,128)(2,1)S(1)}, u32[]{:S(2)}, u32[]{:S(2)}) %collective-permute-start.9) | collective-permute-done | bytes 49184 | tf_op jit(solution)/shard_map/ppermute | solution.py:303
  124.9 6.3 %attend.1.attended_ref = bf16[512,512]{1,0:T(8,128)(2,1)S(1)} custom-call(s32[8]{0:T(128)S(1)} %pad_add_fusion.2.ids_ref, s32[512,2]{1,0:T(8,128)S(1)} %copy.32.table_ref.refs_2_, f32[512,256]{1,0:T(8,128)S(1)} %pad_maximum_fusion.1.turn_ref, bf16[4,6,64,128]{3,2,1,0:T(8,128)(2,1)S(1)} %bitcast.49, bf16[128,192]{1,0:T(8,128)(2,1)S(1)} %add_convert_fusion.refs_0_, ...), custom_call_target="tpu_custom_call" | custom-call | bytes 30093312 | tf_op jit(solution)/shard_map/attend/pallas_call | solution.py:26
  134.2 12.8 %collective-permute-done.12.attended_ref = bf16[512,512]{1,0:T(8,128)(2,1)S(1)} collective-permute-done((bf16[512,512]{1,0:T(8,128)(2,1)S(1)}, bf16[512,512]{1,0:T(8,128)(2,1)S(1)}, u32[]{:S(2)}, u32[]{:S(2)}) %collective-permute-start.12) | collective-permute-done | bytes 524320 | tf_op jit(solution)/shard_map/ppermute | solution.py:303
  146.9 2.3 %copy-done = bf16[24,96,1024]{2,1,0:T(8,128)(2,1)S(1)} copy-done((bf16[24,96,1024]{2,1,0:T(8,128)(2,1)S(1)}, bf16[24,96,1024]{2,1,0:T(8,128)(2,1)}, u32[]{:S(2)}) %copy-start) | copy-done | bytes 4718616
  149.3 1.6 copy-done.7
  152.3 9.5 %collective-permute-done.13.attended_ref = bf16[512,512]{1,0:T(8,128)(2,1)S(1)} collective-permute-done((bf16[512,512]{1,0:T(8,128)(2,1)S(1)}, bf16[512,512]{1,0:T(8,128)(2,1)S(1)}, u32[]{:S(2)}, u32[]{:S(2)}) %collective-permute-start.13) | collective-permute-done | bytes 524320 | tf_op jit(solution)/shard_map/ppermute | solution.py:303
  163.1 12.5 %collective-permute-done.14.attended_ref = bf16[512,512]{1,0:T(8,128)(2,1)S(1)} collective-permute-done((bf16[512,512]{1,0:T(8,128)(2,1)S(1)}, bf16[512,512]{1,0:T(8,128)(2,1)S(1)}, u32[]{:S(2)}, u32[]{:S(2)}) %collective-permute-start.14) | collective-permute-done | bytes 524320 | tf_op jit(solution)/shard_map/ppermute | solution.py:303
  175.6 2.6 %project_out.7 = bf16[512,1024]{1,0:T(8,128)(2,1)} custom-call(s32[5]{0:T(128)S(1)} %pad_add_fusion.1.ids_ref, bf16[512,512]{1,0:T(8,128)(2,1)S(1)} %collective-permute-done.14.attended_ref, bf16[8,3,96,1024]{3,2,1,0:T(8,128)(2,1)S(1)} %bitcast.40, bf16[8,3,96,1024]{3,2,1,0:T(8,128)(2,1)S(1)} %bitcast.41, f32[512,1024]{1,0:T(8,128)S(1)} %get-tuple-element.44.refs_0_, ...), custom_call_target="tpu_custom_call" | custom-call | bytes 39333888 | tf_op jit(solution)/shard_map/project_out/pallas_call | solution.py:26
  (80 shorter events, 19.6 us)
Async XLA Ops:
  6.5 3.8 %copy-start.12 = (bf16[1,64,4,128]{3,2,1,0:T(4,128)(2,1)S(1)}, bf16[1,64,4,128]{3,2,1,0:T(4,128)(2,1)}, u32[]{:S(2)}) copy-start(bf16[1,64,4,128]{3,2,1,0:T(4,128)(2,1)} %param.14) | copy-start | bytes 196612
  6.5 53.7 %all-gather.6.cloned.1.call-start = ((), (), s32[]{:S(2)}) async-start(), calls=%async_computation | async-start | bytes 1966080 | tf_op jit(solution)/shard_map/all_gather | solution.py:307
  7.3 139.7 %all-gather.8.cloned.1.call-start = ((), (), s32[]{:S(2)}) async-start(), calls=%async_computation.1 | async-start | bytes 5308416 | tf_op jit(solution)/shard_map/all_gather | solution.py:353
  10.2 19.8 %copy-start.4 = (bf16[512,1024]{1,0:T(8,128)(2,1)S(1)}, bf16[512,1024]{1,0:T(8,128)(2,1)}, u32[]{:S(2)}) copy-start(bf16[512,1024]{1,0:T(8,128)(2,1)} %token_ref) | copy-start | bytes 3145732
  10.2 24.5 %copy-start.13 = (s32[1,4]{1,0:T(1,128)S(1)}, s32[1,4]{1,0:T(1,128)}, u32[]{:S(2)}) copy-start(s32[1,4]{1,0:T(1,128)} %param.17) | copy-start | bytes 52
  10.5 11.0 %collective-permute-start.1 = (bf16[96,1024]{1,0:T(8,128)(2,1)S(1)}, bf16[96,1024]{1,0:T(8,128)(2,1)S(1)}, u32[]{:S(2)}, u32[]{:S(2)}) collective-permute-start(bf16[96,1024]{1,0:T(8,128)(2,1)S(1)} %get-tuple-element.52), channel_id=1, source_target_pairs={{0,1},{1,2},{2,3},{3,0},{4,5},{5,6},{6,7},{7,4},{8,9},{9,10},{10,1... | collective-permute-start | bytes 589832 | tf_op jit(solution)/shard_map/ppermute | solution.py:303
  13.6 15.5 %collective-permute-start.2 = (bf16[96,1024]{1,0:T(8,128)(2,1)S(1)}, bf16[96,1024]{1,0:T(8,128)(2,1)S(1)}, u32[]{:S(2)}, u32[]{:S(2)}) collective-permute-start(bf16[96,1024]{1,0:T(8,128)(2,1)S(1)} %get-tuple-element.51), channel_id=1, source_target_pairs={{0,2},{1,3},{2,0},{3,1},{4,6},{5,7},{6,4},{7,5},{8,10},{9,11},{10,... | collective-permute-start | bytes 589832 | tf_op jit(solution)/shard_map/ppermute | solution.py:303
  16.2 12.9 %collective-permute-start.3 = (bf16[96,1024]{1,0:T(8,128)(2,1)S(1)}, bf16[96,1024]{1,0:T(8,128)(2,1)S(1)}, u32[]{:S(2)}, u32[]{:S(2)}) collective-permute-start(bf16[96,1024]{1,0:T(8,128)(2,1)S(1)} %get-tuple-element.50), channel_id=1, source_target_pairs={{0,3},{1,0},{2,1},{3,2},{4,7},{5,4},{6,5},{7,6},{8,11},{9,8},{10,9... | collective-permute-start | bytes 589832 | tf_op jit(solution)/shard_map/ppermute | solution.py:303
  30.0 28.1 %collective-permute-start = (bf16[512,1024]{1,0:T(8,128)(2,1)S(1)}, bf16[512,1024]{1,0:T(8,128)(2,1)}, u32[]{:S(2)}, u32[]{:S(2)}) collective-permute-start(bf16[512,1024]{1,0:T(8,128)(2,1)S(1)} %copy-done.4), channel_id=1, source_target_pairs={{0,1},{1,2},{2,3},{3,0},{4,5},{5,6},{6,7},{7,4},{8,9},{9,10},{10,1... | collective-permute-start | bytes 3145736 | tf_op jit(solution)/shard_map/ppermute | solution.py:303
  38.5 3.1 %copy-start.2 = (bf16[4096,6,128]{2,0,1:T(8,128)(2,1)S(1)}, bf16[4096,6,128]{2,0,1:T(8,128)(2,1)}, u32[]{:S(2)}) copy-start(bf16[4096,6,128]{2,0,1:T(8,128)(2,1)} %param.10) | copy-start | bytes 18874372
  41.6 1.7 copy-start.14
  43.2 1.5 copy-start.11
  58.2 34.0 %collective-permute-start.7 = (bf16[512,1024]{1,0:T(8,128)(2,1)}, bf16[512,1024]{1,0:T(8,128)(2,1)}, u32[]{:S(2)}, u32[]{:S(2)}) collective-permute-start(bf16[512,1024]{1,0:T(8,128)(2,1)} %collective-permute-done.refs_0_), channel_id=1, source_target_pairs={{0,1},{1,2},{2,3},{3,0},{4,5},{5,6},{6,7},{7,4},{8,9},{9,10},{10,1... | collective-permute-start | bytes 3145736 | tf_op jit(solution)/shard_map/ppermute | solution.py:303
  64.3 25.0 %collective-permute-start.4 = (f32[128,192]{1,0:T(8,128)S(1)}, f32[128,192]{1,0:T(8,128)S(1)}, u32[]{:S(2)}, u32[]{:S(2)}) collective-permute-start(f32[128,192]{1,0:T(8,128)S(1)} %get-tuple-element.29), channel_id=1, source_target_pairs={{0,1},{1,2},{2,3},{3,0},{4,5},{5,6},{6,7},{7,4},{8,9},{9,10},{10,1... | collective-permute-start | bytes 294920 | tf_op jit(solution)/shard_map/ppermute | solution.py:303
  64.6 27.6 %collective-permute-start.5 = (f32[128,192]{1,0:T(8,128)S(1)}, f32[128,192]{1,0:T(8,128)S(1)}, u32[]{:S(2)}, u32[]{:S(2)}) collective-permute-start(f32[128,192]{1,0:T(8,128)S(1)} %get-tuple-element.30), channel_id=1, source_target_pairs={{0,2},{1,3},{2,0},{3,1},{4,6},{5,7},{6,4},{7,5},{8,10},{9,11},{10,... | collective-permute-start | bytes 294920 | tf_op jit(solution)/shard_map/ppermute | solution.py:303
  66.9 25.2 %collective-permute-start.6 = (f32[128,192]{1,0:T(8,128)S(1)}, f32[128,192]{1,0:T(8,128)S(1)}, u32[]{:S(2)}, u32[]{:S(2)}) collective-permute-start(f32[128,192]{1,0:T(8,128)S(1)} %get-tuple-element.31), channel_id=1, source_target_pairs={{0,3},{1,0},{2,1},{3,2},{4,7},{5,4},{6,5},{7,6},{8,11},{9,8},{10,9... | collective-permute-start | bytes 294920 | tf_op jit(solution)/shard_map/ppermute | solution.py:303
  68.1 2.8 %copy-start.3 = (bf16[4096,6,128]{2,0,1:T(8,128)(2,1)S(1)}, bf16[4096,6,128]{2,0,1:T(8,128)(2,1)}, u32[]{:S(2)}) copy-start(bf16[4096,6,128]{2,0,1:T(8,128)(2,1)} %param.10) | copy-start | bytes 18874372
  71.0 28.4 %copy-start.10 = (bf16[1,64,1024]{2,1,0:T(8,128)(2,1)S(1)}, bf16[1,64,1024]{2,1,0:T(8,128)(2,1)}, u32[]{:S(2)}) copy-start(bf16[1,64,1024]{2,1,0:T(8,128)(2,1)} %param.15) | copy-start | bytes 393220
  92.2 28.8 %collective-permute-start.11 = (bf16[512,1024]{1,0:T(8,128)(2,1)}, bf16[512,1024]{1,0:T(8,128)(2,1)S(1)}, u32[]{:S(2)}, u32[]{:S(2)}) collective-permute-start(bf16[512,1024]{1,0:T(8,128)(2,1)} %collective-permute-done.7.refs_0_), channel_id=1, source_target_pairs={{0,1},{1,2},{2,3},{3,0},{4,5},{5,6},{6,7},{7,4},{8,9},{9,10},{10,1... | collective-permute-start | bytes 3145736 | tf_op jit(solution)/shard_map/ppermute | solution.py:303
  95.6 25.8 %collective-permute-start.10 = (bf16[128,192]{1,0:T(8,128)(2,1)S(1)}, bf16[128,192]{1,0:T(8,128)(2,1)S(1)}, u32[]{:S(2)}, u32[]{:S(2)}) collective-permute-start(bf16[128,192]{1,0:T(8,128)(2,1)S(1)} %add_convert_fusion.refs_0_), channel_id=1, source_target_pairs={{0,3},{1,0},{2,1},{3,2},{4,7},{5,4},{6,5},{7,6},{8,11},{9,8},{10,9... | collective-permute-start | bytes 147464 | tf_op jit(solution)/shard_map/ppermute | solution.py:303
  96.8 26.1 %collective-permute-start.8 = (bf16[128,192]{1,0:T(8,128)(2,1)S(1)}, bf16[128,192]{1,0:T(8,128)(2,1)S(1)}, u32[]{:S(2)}, u32[]{:S(2)}) collective-permute-start(bf16[128,192]{1,0:T(8,128)(2,1)S(1)} %add_convert_fusion.refs_0_), channel_id=1, source_target_pairs={{0,1},{1,2},{2,3},{3,0},{4,5},{5,6},{6,7},{7,4},{8,9},{9,10},{10,1... | collective-permute-start | bytes 147464 | tf_op jit(solution)/shard_map/ppermute | solution.py:303
  97.7 27.2 %collective-permute-start.9 = (bf16[128,192]{1,0:T(8,128)(2,1)S(1)}, bf16[128,192]{1,0:T(8,128)(2,1)S(1)}, u32[]{:S(2)}, u32[]{:S(2)}) collective-permute-start(bf16[128,192]{1,0:T(8,128)(2,1)S(1)} %add_convert_fusion.refs_0_), channel_id=1, source_target_pairs={{0,2},{1,3},{2,0},{3,1},{4,6},{5,7},{6,4},{7,5},{8,10},{9,11},{10,... | collective-permute-start | bytes 147464 | tf_op jit(solution)/shard_map/ppermute | solution.py:303
  99.4 25.5 %slice-start = ((s8[6291456]{0:T(1024)(128)(4,1)}), s8[4194304]{0:T(1024)(128)(4,1)S(1)}, s32[]{:S(2)}) async-start(s8[6291456]{0:T(1024)(128)(4,1)} %bitcast.45), calls=%async_computation.2 | async-start | bytes 8388608
  112.7 12.2 %slice-start.1 = ((s8[6291456]{0:T(1024)(128)(4,1)}), s8[2097152]{0:T(1024)(128)(4,1)S(1)}, s32[]{:S(2)}) async-start(s8[6291456]{0:T(1024)(128)(4,1)} %bitcast.45), calls=%async_computation.3 | async-start | bytes 4194304
  112.7 12.2 %copy-start.8 = (bf16[24,64,128]{2,1,0:T(8,128)(2,1)S(1)}, bf16[24,64,128]{2,1,0:T(8,128)(2,1)}, u32[]{:S(2)}) copy-start(bf16[24,64,128]{2,1,0:T(8,128)(2,1)} %all-gather) | copy-start | bytes 1179652
  121.1 10.3 %copy-start.5 = (bf16[4,128,1024]{2,1,0:T(8,128)(2,1)S(1)}, bf16[4,128,1024]{2,1,0:T(8,128)(2,1)}, u32[]{:S(2)}) copy-start(bf16[4,128,1024]{2,1,0:T(8,128)(2,1)} %copy.27) | copy-start | bytes 3145732
  131.2 15.7 %collective-permute-start.12 = (bf16[512,512]{1,0:T(8,128)(2,1)S(1)}, bf16[512,512]{1,0:T(8,128)(2,1)S(1)}, u32[]{:S(2)}, u32[]{:S(2)}) collective-permute-start(bf16[512,512]{1,0:T(8,128)(2,1)S(1)} %attend.1.attended_ref), channel_id=1, source_target_pairs={{0,1},{1,2},{2,3},{3,0},{4,5},{5,6},{6,7},{7,4},{8,9},{9,10},{10,1... | collective-permute-start | bytes 1572872 | tf_op jit(solution)/shard_map/ppermute | solution.py:303
  146.9 14.8 %collective-permute-start.13 = (bf16[512,512]{1,0:T(8,128)(2,1)S(1)}, bf16[512,512]{1,0:T(8,128)(2,1)S(1)}, u32[]{:S(2)}, u32[]{:S(2)}) collective-permute-start(bf16[512,512]{1,0:T(8,128)(2,1)S(1)} %collective-permute-done.12.attended_ref), channel_id=1, source_target_pairs={{0,1},{1,2},{2,3},{3,0},{4,5},{5,6},{6,7},{7,4},{8,9},{9,10},{10,1... | collective-permute-start | bytes 1572872 | tf_op jit(solution)/shard_map/ppermute | solution.py:303
  146.9 2.3 %copy-start = (bf16[24,96,1024]{2,1,0:T(8,128)(2,1)S(1)}, bf16[24,96,1024]{2,1,0:T(8,128)(2,1)}, u32[]{:S(2)}) copy-start(bf16[24,96,1024]{2,1,0:T(8,128)(2,1)} %all-gather.8.cloned.1.call-done) | copy-start | bytes 14155780
  149.3 1.6 copy-start.7
  150.9 10.9 %copy-start.1 = (bf16[24,96,1024]{2,1,0:T(8,128)(2,1)S(1)}, bf16[24,96,1024]{2,1,0:T(8,128)(2,1)}, u32[]{:S(2)}) copy-start(bf16[24,96,1024]{2,1,0:T(8,128)(2,1)} %all-gather.8.cloned.1.call-done) | copy-start | bytes 14155780
  161.7 13.9 %collective-permute-start.14 = (bf16[512,512]{1,0:T(8,128)(2,1)S(1)}, bf16[512,512]{1,0:T(8,128)(2,1)S(1)}, u32[]{:S(2)}, u32[]{:S(2)}) collective-permute-start(bf16[512,512]{1,0:T(8,128)(2,1)S(1)} %collective-permute-done.13.attended_ref), channel_id=1, source_target_pairs={{0,1},{1,2},{2,3},{3,0},{4,5},{5,6},{6,7},{7,4},{8,9},{9,10},{10,1... | collective-permute-start | bytes 1572872 | tf_op jit(solution)/shard_map/ppermute | solution.py:303
  (2 other events, 2.8 us)
Sparse Core Ops, SparseCore 0:
  8.9 22.3 all-gather.5
  33.2 41.0 all-gather.7

commit v9 on v8

--- a/solution.py
+++ b/solution.py
@@ -349,6 +349,7 @@
 
     begun = project(planes_of[:1], held[:1], weight)
     lines = [turned(send, k) for k, send in enumerate(sends, 1)]
+    lines = [after(line, held[1]) for line in lines]
     held[1] = after(held[1], begun, up_all, table, turn, own_rows, *lines)
     lines = lax.all_gather(jnp.stack(lines), PLANE, axis=0)
     sums = shrink_partial(adapters, here, planes, table, after(tokens, held[1]), down_all)

time: 186 us -> 202 us (1.086)
  waiting for transfers between devices: 79.2 us -> 101 us
  starting transfers between devices: 24.5 us -> 18.4 us
    ppermute x15, waiting for transfers between devices: 78.5 us -> 100 us  [turned(): lax.ppermute(value, 'tensor', [(i, (i + turn) % planes) for i in range(pl...]
    ppermute x15, starting transfers between devices: 24.5 us -> 18.4 us  [turned(): lax.ppermute(value, 'tensor', [(i, (i + turn) % planes) for i in range(pl...]
    unnamed x36 -> x34, local copies, waits for them, and re-layouts: 12.7 us -> 12.8 us
  transfers between devices with their start and end apart: 17 -> 17, of which waited for: 12 -> 11; matrix products, arithmetic and copies ran while one was open for 5% -> 5% of each run, Pallas kernels for 11% -> 10%
where the time goes in v9:
time: 202 us; the launch traced here: 201 us
  waiting for transfers between devices  101 us (50%)
  Pallas kernels  23.3 us (12%)
  blocking collectives  21.3 us (11%)
  local copies, waits for them, and re-layouts  20.3 us (10%)
  starting transfers between devices  18.4 us (9%)
  between operations  13.7 us (7%)
  other arithmetic  2.89 us (1%)
    ppermute x15, waiting for transfers between devices, turned(): lax.ppermute(value, 'tensor', [(i, (i + turn) % planes) for i in range(pl...  100 us
    pallas_call x9, Pallas kernels, call(): pl.pallas_call(kernel, out_shape=out, grid_spec=pltpu.PrefetchScalarGridS...  23.3 us
    ppermute x15, starting transfers between devices, turned(): lax.ppermute(value, 'tensor', [(i, (i + turn) % planes) for i in range(pl...  18.4 us
    unnamed x34, local copies, waits for them, and re-layouts  12.8 us
    all_gather x1, blocking collectives, local(): lax.all_gather(jnp.transpose(adapter_up_maps[0], (1, 0, 2)), 'dp', axis=0)  8.3 us
    all_gather x1, blocking collectives, local(): lax.all_gather(after(output_up_maps, held[2]), 'dp', axis=0, tiled=True)  6.97 us
    all_gather x1, blocking collectives, local(): own_down = lax.all_gather(after(out_down, held[2]), 'dp', axis=0)  6.03 us
  transfers between devices with their start and end apart: 17, of which 11 were waited for; matrix products, arithmetic and copies ran while one was open for 5% of the time, Pallas kernels for 10%

profile of v9, /device:TPU:0, one launch (start us, length us, event | category | flops | bytes accessed | tf_op | source)
XLA Modules:
  0.0 201.0 jit_solution(7094561244600976956)
XLA Ops:
  7.3 3.1 %collective-permute-start = (bf16[512,1024]{1,0:T(8,128)(2,1)}, bf16[512,1024]{1,0:T(8,128)(2,1)}, u32[]{:S(2)}, u32[]{:S(2)}) collective-permute-start(bf16[512,1024]{1,0:T(8,128)(2,1)} %token_ref), channel_id=1, source_target_pairs={{0,1},{1,2},{2,3},{3,0},{4,5},{5,6},{6,7},{7,4},{8,9},{9,10},{10,1... | collective-permute-start | bytes 3145736 | tf_op jit(solution)/shard_map/ppermute | solution.py:303
  11.2 2.8 %fusion.4 = (bf16[64,1,1024]{2,1,0:T(2,128)(2,1)S(1)}, bf16[64,1,1024]{2,1,0:T(2,128)(2,1)S(1)}, bf16[64,1,1024]{2,1,0:T(2,128)(2,1)S(1)}) fusion(bf16[128,4,4096]{2,1,0:T(4,128)(2,1)} %param.11, s32[]{:T(128)S(6)} %select_n.66, s32[]{:T(128)S(6)} %select_n.69, s32[]{:T(128)S(6)} %select_n.78, s32[]{:T(128)S(6)} %select_n.75, s32[]{:T(128)S(6)} %select_n.72), kind=kLoop, calls=%fused_computation.32 | loop fusion | bytes 786452 | tf_op jit(solution)/shard_map/dynamic_slice | solution.py:343
  14.3 2.2 %collective-permute-start.3 = (bf16[96,1024]{1,0:T(8,128)(2,1)S(1)}, bf16[96,1024]{1,0:T(8,128)(2,1)S(1)}, u32[]{:S(2)}, u32[]{:S(2)}) collective-permute-start(bf16[96,1024]{1,0:T(8,128)(2,1)S(1)} %get-tuple-element.56), channel_id=1, source_target_pairs={{0,3},{1,0},{2,1},{3,2},{4,7},{5,4},{6,5},{7,6},{8,11},{9,8},{10,9... | collective-permute-start | bytes 589832 | tf_op jit(solution)/shard_map/ppermute | solution.py:303
  17.4 1.6 collective-permute-start.1
  18.9 21.0 %collective-permute-done.3 = bf16[96,1024]{1,0:T(8,128)(2,1)S(1)} collective-permute-done((bf16[96,1024]{1,0:T(8,128)(2,1)S(1)}, bf16[96,1024]{1,0:T(8,128)(2,1)S(1)}, u32[]{:S(2)}, u32[]{:S(2)}) %collective-permute-start.3) | collective-permute-done | bytes 196640 | tf_op jit(solution)/shard_map/ppermute | solution.py:303
  40.0 12.6 %collective-permute-done.2 = bf16[96,1024]{1,0:T(8,128)(2,1)S(1)} collective-permute-done((bf16[96,1024]{1,0:T(8,128)(2,1)S(1)}, bf16[96,1024]{1,0:T(8,128)(2,1)S(1)}, u32[]{:S(2)}, u32[]{:S(2)}) %collective-permute-start.2) | collective-permute-done | bytes 196640 | tf_op jit(solution)/shard_map/ppermute | solution.py:303
  53.8 1.7 dynamic-slice_bitcast_fusion
  57.4 3.2 %copy-done.2 = bf16[4096,6,128]{2,0,1:T(8,128)(2,1)S(1)} copy-done((bf16[4096,6,128]{2,0,1:T(8,128)(2,1)S(1)}, bf16[4096,6,128]{2,0,1:T(8,128)(2,1)}, u32[]{:S(2)}) %copy-start.2) | copy-done | bytes 6291480
  60.6 1.7 project.3.refs_2_
  63.8 8.3 %all-gather = bf16[24,64,128]{2,1,0:T(8,128)(2,1)} all-gather(bf16[6,64,128]{2,1,0:T(8,128)(2,1)S(1)} %bitcast.57), channel_id=2, replica_groups=mesh['groups'=2,'dp'=4,'tensor'=4] {'dp'}, dimensions={0}, use_global_device_ids=true | all-gather | bytes 491520 | tf_op jit(solution)/shard_map/all_gather | solution.py:308
  73.7 2.7 %shrink.1 = (f32[128,192]{1,0:T(8,128)S(1)}, f32[128,192]{1,0:T(8,128)S(1)}, f32[128,192]{1,0:T(8,128)S(1)}, f32[128,192]{1,0:T(8,128)S(1)}) custom-call(s32[5]{0:T(128)S(1)} %pad_add_fusion.3.ids_ref, s32[512,2]{1,0:T(8,128)S(1)} %copy.32.table_ref.refs_2_, bf16[512,1024]{1,0:T(8,128)(2,1)S(1)} %copy-done.4, bf16[4,192,1024]{2,1,0:T(8,128)(2,1)S(1)} %copy-done.9), custom_call_target="tpu_custom_call" | custom-call | bytes 7876608 | tf_op jit(solution)/shard_map/shrink/pallas_call | solution.py:26
  76.4 2.2 %collective-permute-start.4 = (f32[128,192]{1,0:T(8,128)S(1)}, f32[128,192]{1,0:T(8,128)S(1)}, u32[]{:S(2)}, u32[]{:S(2)}) collective-permute-start(f32[128,192]{1,0:T(8,128)S(1)} %get-tuple-element.35), channel_id=1, source_target_pairs={{0,1},{1,2},{2,3},{3,0},{4,5},{5,6},{6,7},{7,4},{8,9},{9,10},{10,1... | collective-permute-start | bytes 294920 | tf_op jit(solution)/shard_map/ppermute | solution.py:303
  78.6 2.3 %collective-permute-start.5 = (f32[128,192]{1,0:T(8,128)S(1)}, f32[128,192]{1,0:T(8,128)S(1)}, u32[]{:S(2)}, u32[]{:S(2)}) collective-permute-start(f32[128,192]{1,0:T(8,128)S(1)} %get-tuple-element.36), channel_id=1, source_target_pairs={{0,2},{1,3},{2,0},{3,1},{4,6},{5,7},{6,4},{7,5},{8,10},{9,11},{10,... | collective-permute-start | bytes 294920 | tf_op jit(solution)/shard_map/ppermute | solution.py:303
  81.0 2.9 %copy-done.3 = bf16[4096,6,128]{2,0,1:T(8,128)(2,1)S(1)} copy-done((bf16[4096,6,128]{2,0,1:T(8,128)(2,1)S(1)}, bf16[4096,6,128]{2,0,1:T(8,128)(2,1)}, u32[]{:S(2)}) %copy-start.3) | copy-done | bytes 6291480
  83.9 2.8 %project.4.refs_2_ = f32[512,768]{1,0:T(8,128)S(1)} custom-call(s32[1]{0:T(128)} %get-tuple-element.65.ids_ref, bf16[512,1024]{1,0:T(8,128)(2,1)} %collective-permute-done.refs_0_, bf16[6,4096,128]{2,1,0:T(8,128)(2,1)S(1)} %bitcast.43, f32[512,768]{1,0:T(8,128)S(1)} %project.3.refs_2_), custom_call_target="tpu_custom_call" | custom-call | bytes 26738688 | tf_op jit(solution)/shard_map/project/pallas_call | solution.py:26
  86.7 16.3 %collective-permute-done.4 = f32[128,192]{1,0:T(8,128)S(1)} collective-permute-done((f32[128,192]{1,0:T(8,128)S(1)}, f32[128,192]{1,0:T(8,128)S(1)}, u32[]{:S(2)}, u32[]{:S(2)}) %collective-permute-start.4) | collective-permute-done | bytes 98336 | tf_op jit(solution)/shard_map/ppermute | solution.py:303
  103.0 5.0 %collective-permute-done.5 = f32[128,192]{1,0:T(8,128)S(1)} collective-permute-done((f32[128,192]{1,0:T(8,128)S(1)}, f32[128,192]{1,0:T(8,128)S(1)}, u32[]{:S(2)}, u32[]{:S(2)}) %collective-permute-start.5) | collective-permute-done | bytes 98336 | tf_op jit(solution)/shard_map/ppermute | solution.py:303
  108.1 3.3 %collective-permute-start.11 = (bf16[512,1024]{1,0:T(8,128)(2,1)}, bf16[512,1024]{1,0:T(8,128)(2,1)S(1)}, u32[]{:S(2)}, u32[]{:S(2)}) collective-permute-start(bf16[512,1024]{1,0:T(8,128)(2,1)} %collective-permute-done.7.refs_0_), channel_id=1, source_target_pairs={{0,1},{1,2},{2,3},{3,0},{4,5},{5,6},{6,7},{7,4},{8,9},{9,10},{10,1... | collective-permute-start | bytes 3145736 | tf_op jit(solution)/shard_map/ppermute | solution.py:303
  112.1 1.5 collective-permute-start.8
  114.2 7.0 %all_gather.27.refs_3_ = bf16[4,64,1024]{2,1,0:T(8,128)(2,1)S(1)} all-gather(bf16[1,64,1024]{2,1,0:T(8,128)(2,1)S(1)} %copy-done.10), channel_id=1, replica_groups=mesh['groups'=2,'dp'=4,'tensor'=4] {'dp'}, dimensions={0}, use_global_device_ids=true | all-gather | bytes 655360 | tf_op jit(solution)/shard_map/all_gather | solution.py:365
  121.1 6.0 %all-gather.1 = bf16[128,1024]{1,0:T(8,128)(2,1)S(1)} all-gather(bf16[32,1024]{1,0:T(8,128)(2,1)S(1)} %bitcast_dynamic-update-slice_fusion), channel_id=3, replica_groups=mesh['groups'=2,'dp'=4,'tensor'=4] {'dp'}, dimensions={0}, use_global_device_ids=true | all-gather | bytes 327680 | tf_op jit(solution)/shard_map/all_gather | solution.py:366
  127.2 3.0 %project.5.refs_6_ = f32[512,768]{1,0:T(8,128)S(1)} custom-call(s32[1]{0:T(128)} %get-tuple-element.64.ids_ref, bf16[512,1024]{1,0:T(8,128)(2,1)} %collective-permute-done.7.refs_0_, bf16[6,4096,128]{2,1,0:T(8,128)(2,1)S(1)} %bitcast.44, f32[512,768]{1,0:T(8,128)S(1)} %project.4.refs_2_), custom_call_target="tpu_custom_call" | custom-call | bytes 26738688 | tf_op jit(solution)/shard_map/project/pallas_call | solution.py:26
  130.1 6.2 %collective-permute-done.11.refs_4_ = bf16[512,1024]{1,0:T(8,128)(2,1)S(1)} collective-permute-done((bf16[512,1024]{1,0:T(8,128)(2,1)}, bf16[512,1024]{1,0:T(8,128)(2,1)S(1)}, u32[]{:S(2)}, u32[]{:S(2)}) %collective-permute-start.11) | collective-permute-done | bytes 1048608 | tf_op jit(solution)/shard_map/ppermute | solution.py:303
  137.3 1.4 collective-permute-done.8.refs_1_
  138.7 2.1 %collective-permute-done.9.refs_2_ = bf16[128,192]{1,0:T(8,128)(2,1)S(1)} collective-permute-done((bf16[128,192]{1,0:T(8,128)(2,1)S(1)}, bf16[128,192]{1,0:T(8,128)(2,1)S(1)}, u32[]{:S(2)}, u32[]{:S(2)}) %collective-permute-start.9) | collective-permute-done | bytes 49184 | tf_op jit(solution)/shard_map/ppermute | solution.py:303
  140.8 6.4 %attend.1.attended_ref = bf16[512,512]{1,0:T(8,128)(2,1)S(1)} custom-call(s32[8]{0:T(128)S(1)} %pad_add_fusion.2.ids_ref, s32[512,2]{1,0:T(8,128)S(1)} %copy.32.table_ref.refs_2_, f32[512,256]{1,0:T(8,128)S(1)} %pad_maximum_fusion.1.turn_ref, bf16[4,6,64,128]{3,2,1,0:T(8,128)(2,1)S(1)} %bitcast.49, bf16[128,192]{1,0:T(8,128)(2,1)S(1)} %add_convert_fusion.refs_0_, ...), custom_call_target="tpu_custom_call" | custom-call | bytes 30093312 | tf_op jit(solution)/shard_map/attend/pallas_call | solution.py:26
  150.1 12.8 %collective-permute-done.12.attended_ref = bf16[512,512]{1,0:T(8,128)(2,1)S(1)} collective-permute-done((bf16[512,512]{1,0:T(8,128)(2,1)S(1)}, bf16[512,512]{1,0:T(8,128)(2,1)S(1)}, u32[]{:S(2)}, u32[]{:S(2)}) %collective-permute-start.12) | collective-permute-done | bytes 524320 | tf_op jit(solution)/shard_map/ppermute | solution.py:303
  162.9 2.3 %copy-done = bf16[24,96,1024]{2,1,0:T(8,128)(2,1)S(1)} copy-done((bf16[24,96,1024]{2,1,0:T(8,128)(2,1)S(1)}, bf16[24,96,1024]{2,1,0:T(8,128)(2,1)}, u32[]{:S(2)}) %copy-start) | copy-done | bytes 4718616
  165.2 1.6 copy-done.7
  168.2 9.5 %collective-permute-done.13.attended_ref = bf16[512,512]{1,0:T(8,128)(2,1)S(1)} collective-permute-done((bf16[512,512]{1,0:T(8,128)(2,1)S(1)}, bf16[512,512]{1,0:T(8,128)(2,1)S(1)}, u32[]{:S(2)}, u32[]{:S(2)}) %collective-permute-start.13) | collective-permute-done | bytes 524320 | tf_op jit(solution)/shard_map/ppermute | solution.py:303
  179.1 12.5 %collective-permute-done.14.attended_ref = bf16[512,512]{1,0:T(8,128)(2,1)S(1)} collective-permute-done((bf16[512,512]{1,0:T(8,128)(2,1)S(1)}, bf16[512,512]{1,0:T(8,128)(2,1)S(1)}, u32[]{:S(2)}, u32[]{:S(2)}) %collective-permute-start.14) | collective-permute-done | bytes 524320 | tf_op jit(solution)/shard_map/ppermute | solution.py:303
  191.6 2.6 %project_out.7 = bf16[512,1024]{1,0:T(8,128)(2,1)} custom-call(s32[5]{0:T(128)S(1)} %pad_add_fusion.1.ids_ref, bf16[512,512]{1,0:T(8,128)(2,1)S(1)} %collective-permute-done.14.attended_ref, bf16[8,3,96,1024]{3,2,1,0:T(8,128)(2,1)S(1)} %bitcast.40, bf16[8,3,96,1024]{3,2,1,0:T(8,128)(2,1)S(1)} %bitcast.41, f32[512,1024]{1,0:T(8,128)S(1)} %get-tuple-element.50.refs_0_, ...), custom_call_target="tpu_custom_call" | custom-call | bytes 39333888 | tf_op jit(solution)/shard_map/project_out/pallas_call | solution.py:26
  (78 shorter events, 16.9 us)
Async XLA Ops:
  6.5 65.8 %all-gather.6.cloned.1.call-start = ((), (), s32[]{:S(2)}) async-start(), calls=%async_computation | async-start | bytes 1966080 | tf_op jit(solution)/shard_map/all_gather | solution.py:307
  7.3 155.6 %all-gather.8.cloned.1.call-start = ((), (), s32[]{:S(2)}) async-start(), calls=%async_computation.1 | async-start | bytes 5308416 | tf_op jit(solution)/shard_map/all_gather | solution.py:354
  7.3 32.7 %collective-permute-start = (bf16[512,1024]{1,0:T(8,128)(2,1)}, bf16[512,1024]{1,0:T(8,128)(2,1)}, u32[]{:S(2)}, u32[]{:S(2)}) collective-permute-start(bf16[512,1024]{1,0:T(8,128)(2,1)} %token_ref), channel_id=1, source_target_pairs={{0,1},{1,2},{2,3},{3,0},{4,5},{5,6},{6,7},{7,4},{8,9},{9,10},{10,1... | collective-permute-start | bytes 3145736 | tf_op jit(solution)/shard_map/ppermute | solution.py:303
  14.0 39.5 %copy-start.12 = (s32[1,4]{1,0:T(1,128)S(1)}, s32[1,4]{1,0:T(1,128)}, u32[]{:S(2)}) copy-start(s32[1,4]{1,0:T(1,128)} %param.17) | copy-start | bytes 52
  14.3 25.7 %collective-permute-start.3 = (bf16[96,1024]{1,0:T(8,128)(2,1)S(1)}, bf16[96,1024]{1,0:T(8,128)(2,1)S(1)}, u32[]{:S(2)}, u32[]{:S(2)}) collective-permute-start(bf16[96,1024]{1,0:T(8,128)(2,1)S(1)} %get-tuple-element.56), channel_id=1, source_target_pairs={{0,3},{1,0},{2,1},{3,2},{4,7},{5,4},{6,5},{7,6},{8,11},{9,8},{10,9... | collective-permute-start | bytes 589832 | tf_op jit(solution)/shard_map/ppermute | solution.py:303
  16.5 36.2 %collective-permute-start.2 = (bf16[96,1024]{1,0:T(8,128)(2,1)S(1)}, bf16[96,1024]{1,0:T(8,128)(2,1)S(1)}, u32[]{:S(2)}, u32[]{:S(2)}) collective-permute-start(bf16[96,1024]{1,0:T(8,128)(2,1)S(1)} %get-tuple-element.57), channel_id=1, source_target_pairs={{0,2},{1,3},{2,0},{3,1},{4,6},{5,7},{6,4},{7,5},{8,10},{9,11},{10,... | collective-permute-start | bytes 589832 | tf_op jit(solution)/shard_map/ppermute | solution.py:303
  17.4 35.3 %collective-permute-start.1 = (bf16[96,1024]{1,0:T(8,128)(2,1)S(1)}, bf16[96,1024]{1,0:T(8,128)(2,1)S(1)}, u32[]{:S(2)}, u32[]{:S(2)}) collective-permute-start(bf16[96,1024]{1,0:T(8,128)(2,1)S(1)} %get-tuple-element.58), channel_id=1, source_target_pairs={{0,1},{1,2},{2,3},{3,0},{4,5},{5,6},{6,7},{7,4},{8,9},{9,10},{10,1... | collective-permute-start | bytes 589832 | tf_op jit(solution)/shard_map/ppermute | solution.py:303
  53.8 3.6 %copy-start.4 = (bf16[512,1024]{1,0:T(8,128)(2,1)S(1)}, bf16[512,1024]{1,0:T(8,128)(2,1)}, u32[]{:S(2)}) copy-start(bf16[512,1024]{1,0:T(8,128)(2,1)} %token_ref) | copy-start | bytes 3145732
  57.4 3.2 %copy-start.2 = (bf16[4096,6,128]{2,0,1:T(8,128)(2,1)S(1)}, bf16[4096,6,128]{2,0,1:T(8,128)(2,1)}, u32[]{:S(2)}) copy-start(bf16[4096,6,128]{2,0,1:T(8,128)(2,1)} %param.10) | copy-start | bytes 18874372
  60.6 1.7 copy-start.13
  62.3 1.5 copy-start.11
  72.1 36.0 %collective-permute-start.7 = (bf16[512,1024]{1,0:T(8,128)(2,1)}, bf16[512,1024]{1,0:T(8,128)(2,1)}, u32[]{:S(2)}, u32[]{:S(2)}) collective-permute-start(bf16[512,1024]{1,0:T(8,128)(2,1)} %collective-permute-done.refs_0_), channel_id=1, source_target_pairs={{0,1},{1,2},{2,3},{3,0},{4,5},{5,6},{6,7},{7,4},{8,9},{9,10},{10,1... | collective-permute-start | bytes 3145736 | tf_op jit(solution)/shard_map/ppermute | solution.py:303
  72.3 1.4 copy-start.9
  76.4 26.6 %collective-permute-start.4 = (f32[128,192]{1,0:T(8,128)S(1)}, f32[128,192]{1,0:T(8,128)S(1)}, u32[]{:S(2)}, u32[]{:S(2)}) collective-permute-start(f32[128,192]{1,0:T(8,128)S(1)} %get-tuple-element.35), channel_id=1, source_target_pairs={{0,1},{1,2},{2,3},{3,0},{4,5},{5,6},{6,7},{7,4},{8,9},{9,10},{10,1... | collective-permute-start | bytes 294920 | tf_op jit(solution)/shard_map/ppermute | solution.py:303
  78.6 29.5 %collective-permute-start.5 = (f32[128,192]{1,0:T(8,128)S(1)}, f32[128,192]{1,0:T(8,128)S(1)}, u32[]{:S(2)}, u32[]{:S(2)}) collective-permute-start(f32[128,192]{1,0:T(8,128)S(1)} %get-tuple-element.36), channel_id=1, source_target_pairs={{0,2},{1,3},{2,0},{3,1},{4,6},{5,7},{6,4},{7,5},{8,10},{9,11},{10,... | collective-permute-start | bytes 294920 | tf_op jit(solution)/shard_map/ppermute | solution.py:303
  80.8 27.2 %collective-permute-start.6 = (f32[128,192]{1,0:T(8,128)S(1)}, f32[128,192]{1,0:T(8,128)S(1)}, u32[]{:S(2)}, u32[]{:S(2)}) collective-permute-start(f32[128,192]{1,0:T(8,128)S(1)} %get-tuple-element.37), channel_id=1, source_target_pairs={{0,3},{1,0},{2,1},{3,2},{4,7},{5,4},{6,5},{7,6},{8,11},{9,8},{10,9... | collective-permute-start | bytes 294920 | tf_op jit(solution)/shard_map/ppermute | solution.py:303
  81.0 2.9 %copy-start.3 = (bf16[4096,6,128]{2,0,1:T(8,128)(2,1)S(1)}, bf16[4096,6,128]{2,0,1:T(8,128)(2,1)}, u32[]{:S(2)}) copy-start(bf16[4096,6,128]{2,0,1:T(8,128)(2,1)} %param.10) | copy-start | bytes 18874372
  83.9 30.3 %copy-start.10 = (bf16[1,64,1024]{2,1,0:T(8,128)(2,1)S(1)}, bf16[1,64,1024]{2,1,0:T(8,128)(2,1)}, u32[]{:S(2)}) copy-start(bf16[1,64,1024]{2,1,0:T(8,128)(2,1)} %param.15) | copy-start | bytes 393220
  108.1 28.2 %collective-permute-start.11 = (bf16[512,1024]{1,0:T(8,128)(2,1)}, bf16[512,1024]{1,0:T(8,128)(2,1)S(1)}, u32[]{:S(2)}, u32[]{:S(2)}) collective-permute-start(bf16[512,1024]{1,0:T(8,128)(2,1)} %collective-permute-done.7.refs_0_), channel_id=1, source_target_pairs={{0,1},{1,2},{2,3},{3,0},{4,5},{5,6},{6,7},{7,4},{8,9},{9,10},{10,1... | collective-permute-start | bytes 3145736 | tf_op jit(solution)/shard_map/ppermute | solution.py:303
  111.5 25.8 %collective-permute-start.10 = (bf16[128,192]{1,0:T(8,128)(2,1)S(1)}, bf16[128,192]{1,0:T(8,128)(2,1)S(1)}, u32[]{:S(2)}, u32[]{:S(2)}) collective-permute-start(bf16[128,192]{1,0:T(8,128)(2,1)S(1)} %add_convert_fusion.refs_0_), channel_id=1, source_target_pairs={{0,3},{1,0},{2,1},{3,2},{4,7},{5,4},{6,5},{7,6},{8,11},{9,8},{10,9... | collective-permute-start | bytes 147464 | tf_op jit(solution)/shard_map/ppermute | solution.py:303
  112.1 26.6 %collective-permute-start.8 = (bf16[128,192]{1,0:T(8,128)(2,1)S(1)}, bf16[128,192]{1,0:T(8,128)(2,1)S(1)}, u32[]{:S(2)}, u32[]{:S(2)}) collective-permute-start(bf16[128,192]{1,0:T(8,128)(2,1)S(1)} %add_convert_fusion.refs_0_), channel_id=1, source_target_pairs={{0,1},{1,2},{2,3},{3,0},{4,5},{5,6},{6,7},{7,4},{8,9},{9,10},{10,1... | collective-permute-start | bytes 147464 | tf_op jit(solution)/shard_map/ppermute | solution.py:303
  113.6 27.2 %collective-permute-start.9 = (bf16[128,192]{1,0:T(8,128)(2,1)S(1)}, bf16[128,192]{1,0:T(8,128)(2,1)S(1)}, u32[]{:S(2)}, u32[]{:S(2)}) collective-permute-start(bf16[128,192]{1,0:T(8,128)(2,1)S(1)} %add_convert_fusion.refs_0_), channel_id=1, source_target_pairs={{0,2},{1,3},{2,0},{3,1},{4,6},{5,7},{6,4},{7,5},{8,10},{9,11},{10,... | collective-permute-start | bytes 147464 | tf_op jit(solution)/shard_map/ppermute | solution.py:303
  114.2 26.6 %slice-start = ((s8[6291456]{0:T(1024)(128)(4,1)}), s8[4194304]{0:T(1024)(128)(4,1)S(1)}, s32[]{:S(2)}) async-start(s8[6291456]{0:T(1024)(128)(4,1)} %bitcast.45), calls=%async_computation.2 | async-start | bytes 8388608
  127.2 13.6 %slice-start.1 = ((s8[6291456]{0:T(1024)(128)(4,1)}), s8[2097152]{0:T(1024)(128)(4,1)S(1)}, s32[]{:S(2)}) async-start(s8[6291456]{0:T(1024)(128)(4,1)} %bitcast.45), calls=%async_computation.3 | async-start | bytes 4194304
  127.2 13.6 %copy-start.8 = (bf16[24,64,128]{2,1,0:T(8,128)(2,1)S(1)}, bf16[24,64,128]{2,1,0:T(8,128)(2,1)}, u32[]{:S(2)}) copy-start(bf16[24,64,128]{2,1,0:T(8,128)(2,1)} %all-gather) | copy-start | bytes 1179652
  136.3 11.0 %copy-start.5 = (bf16[4,128,1024]{2,1,0:T(8,128)(2,1)S(1)}, bf16[4,128,1024]{2,1,0:T(8,128)(2,1)}, u32[]{:S(2)}) copy-start(bf16[4,128,1024]{2,1,0:T(8,128)(2,1)} %copy.27) | copy-start | bytes 3145732
  147.2 15.7 %collective-permute-start.12 = (bf16[512,512]{1,0:T(8,128)(2,1)S(1)}, bf16[512,512]{1,0:T(8,128)(2,1)S(1)}, u32[]{:S(2)}, u32[]{:S(2)}) collective-permute-start(bf16[512,512]{1,0:T(8,128)(2,1)S(1)} %attend.1.attended_ref), channel_id=1, source_target_pairs={{0,1},{1,2},{2,3},{3,0},{4,5},{5,6},{6,7},{7,4},{8,9},{9,10},{10,1... | collective-permute-start | bytes 1572872 | tf_op jit(solution)/shard_map/ppermute | solution.py:303
  162.9 14.8 %collective-permute-start.13 = (bf16[512,512]{1,0:T(8,128)(2,1)S(1)}, bf16[512,512]{1,0:T(8,128)(2,1)S(1)}, u32[]{:S(2)}, u32[]{:S(2)}) collective-permute-start(bf16[512,512]{1,0:T(8,128)(2,1)S(1)} %collective-permute-done.12.attended_ref), channel_id=1, source_target_pairs={{0,1},{1,2},{2,3},{3,0},{4,5},{5,6},{6,7},{7,4},{8,9},{9,10},{10,1... | collective-permute-start | bytes 1572872 | tf_op jit(solution)/shard_map/ppermute | solution.py:303
  162.9 2.3 %copy-start = (bf16[24,96,1024]{2,1,0:T(8,128)(2,1)S(1)}, bf16[24,96,1024]{2,1,0:T(8,128)(2,1)}, u32[]{:S(2)}) copy-start(bf16[24,96,1024]{2,1,0:T(8,128)(2,1)} %all-gather.8.cloned.1.call-done) | copy-start | bytes 14155780
  165.2 1.6 copy-start.7
  166.8 10.9 %copy-start.1 = (bf16[24,96,1024]{2,1,0:T(8,128)(2,1)S(1)}, bf16[24,96,1024]{2,1,0:T(8,128)(2,1)}, u32[]{:S(2)}) copy-start(bf16[24,96,1024]{2,1,0:T(8,128)(2,1)} %all-gather.8.cloned.1.call-done) | copy-start | bytes 14155780
  177.7 13.9 %collective-permute-start.14 = (bf16[512,512]{1,0:T(8,128)(2,1)S(1)}, bf16[512,512]{1,0:T(8,128)(2,1)S(1)}, u32[]{:S(2)}, u32[]{:S(2)}) collective-permute-start(bf16[512,512]{1,0:T(8,128)(2,1)S(1)} %collective-permute-done.13.attended_ref), channel_id=1, source_target_pairs={{0,1},{1,2},{2,3},{3,0},{4,5},{5,6},{6,7},{7,4},{8,9},{9,10},{10,1... | collective-permute-start | bytes 1572872 | tf_op jit(solution)/shard_map/ppermute | solution.py:303
  (1 other events, 1.4 us)
Sparse Core Ops, SparseCore 0:
  8.9 22.3 all-gather.5
  53.7 38.9 all-gather.7

commit v10 on v8

--- a/solution.py
+++ b/solution.py
@@ -59,28 +59,36 @@
         )
 
 
-def shard_spec(weight, depth):
+def shard_spec(weight, depth, number=0):
     slots, _, head_size = weight.shape
-    return pl.BlockSpec((slots, depth, head_size), lambda step, ids: (0, ids[step], 0))
-
-
-def project(ids, tokens, weight, begun=()):
-    rows, depth = tokens[0].shape
+    return pl.BlockSpec((slots, depth, head_size), lambda step, ids: (0, ids[number], 0))
+
+
+def rows_spec(array, rows, part):
+    if array.shape[0] == rows:
+        return None
+    return pl.BlockSpec((rows, array.shape[1]), lambda step, ids: (part, 0))
+
+
+def project(ids, tokens, weight, begun=(), part=0):
+    rows, depth = tokens.shape
     slots, _, head_size = weight.shape
     return call(
-        functools.partial(project_kernel, len(tokens), len(begun)),
+        functools.partial(project_kernel, 1, len(begun)),
         "project",
         ids,
-        len(tokens),
-        [None] * len(tokens) + [shard_spec(weight, depth)] + [None] * len(begun),
-        [*tokens, weight, *begun],
+        1,
+        [None, shard_spec(weight, depth)] + [rows_spec(array, rows, part) for array in begun],
+        [tokens, weight, *begun],
         jax.ShapeDtypeStruct((rows, slots * head_size), jnp.float32),
     )
 
 
-def attend_kernel(planes, ids_ref, table_ref, turn_ref, up_ref, *refs):
+def attend_kernel(planes, earlier, ids_ref, table_ref, turn_ref, up_ref, *refs):
     piece_refs, refs = refs[:planes], refs[planes:]
-    token_ref, w_ref, begun_ref, out_ref, acc_ref, keys_ref, values_ref, shrink_ref = refs
+    token_ref, w_ref, begun_ref, refs = refs[0], refs[1], refs[2], refs[3:]
+    earlier_refs, refs = refs[: 2 * earlier], refs[2 * earlier :]
+    out_ref, keys_ref, values_ref, acc_ref, shrink_ref = refs
     for number, piece_ref in enumerate(piece_refs):
         size = piece_ref.shape[0]
         shrink_ref[pl.ds(pl.multiple_of(ids_ref[number] * size, size), size), :] = piece_ref[...]
@@ -89,77 +97,77 @@
     rank = up_ref.shape[2]
     count = ids_ref.shape[0] - planes
     rows = acc_ref.shape[0]
-    block = min(rows, 256)
+    first_row = earlier_refs[0].shape[0] if earlier else 0
     queries = slots - 2
-    ups = [
-        jnp.concatenate([up_ref[ids_ref[planes + j], index] for j in range(count)], axis=0)
-        for index in range(slots)
-    ]
-    for row in range(0, rows, block):
-        at = slice(row, row + block)
-        lane = lax.broadcasted_iota(jnp.int32, (block, count * rank), 1)
-        kept = (lane >= table_ref[at, 1:2]) & (lane < table_ref[at, 1:2] + rank)
-        lows = []
-        for part in range(3):
-            piece = shrink_ref[at, part * rank : (part + 1) * rank].astype(jnp.float32)
-            piece = jnp.concatenate([piece] * count, axis=1)
-            lows.append(jnp.where(kept, piece, 0.0).astype(jnp.bfloat16))
-
-        def slot(index):
-            low = lows[0 if index < queries else index - queries + 1]
-            extra = jnp.dot(low, ups[index], preferred_element_type=jnp.float32)
-            return acc_ref[at, index * head_size : (index + 1) * head_size] + extra
-
-        def rotated(index):
-            value = slot(index)
-            turned = pltpu.roll(value, head_size // 2, 1)
-            cos, sin = turn_ref[at, :head_size], turn_ref[at, head_size:]
-            return (value * cos + turned * sin).astype(jnp.bfloat16)
-
-        keys_ref[at, :] = rotated(queries)
-        values_ref[at, :] = slot(queries + 1).astype(jnp.bfloat16)
-        key_rows = row + block
-        keys, values = keys_ref[:key_rows], values_ref[:key_rows]
-        key_at = lax.broadcasted_iota(jnp.int32, (block, key_rows), 1)
-        row_at = lax.broadcasted_iota(jnp.int32, (block, key_rows), 0) + row
-        allowed = (key_at >= table_ref[at, 0:1]) & (key_at <= row_at)
-        for index in range(queries):
-            scores = lax.dot_general(
-                rotated(index), keys, (((1,), (1,)), ((), ())),
-                preferred_element_type=jnp.float32,
-            )
-            scores = jnp.where(allowed, scores * (1.0 / math.sqrt(head_size)), -1e30)
-            weights = jnp.exp(scores - jnp.max(scores, axis=1, keepdims=True))
-            scale = 1.0 / jnp.sum(weights, axis=1, keepdims=True)
-            attended = jnp.dot(
-                (weights * scale).astype(jnp.bfloat16), values, preferred_element_type=jnp.float32
-            )
-            out_ref[at, index * head_size : (index + 1) * head_size] = attended.astype(
-                jnp.bfloat16
-            )
-
-
-def attend(planes_of, adapters, table, turn, up, shrink, tokens, weight, begun):
+    lane = lax.broadcasted_iota(jnp.int32, (rows, count * rank), 1)
+    kept = (lane >= table_ref[:, 1:2]) & (lane < table_ref[:, 1:2] + rank)
+    lows = []
+    for part in range(3):
+        piece = shrink_ref[first_row : first_row + rows, part * rank : (part + 1) * rank]
+        piece = jnp.concatenate([piece.astype(jnp.float32)] * count, axis=1)
+        lows.append(jnp.where(kept, piece, 0.0).astype(jnp.bfloat16))
+
+    def slot(index):
+        low = lows[0 if index < queries else index - queries + 1]
+        up = jnp.concatenate([up_ref[ids_ref[planes + j], index] for j in range(count)], axis=0)
+        extra = jnp.dot(low, up, preferred_element_type=jnp.float32)
+        return acc_ref[:, index * head_size : (index + 1) * head_size] + extra
+
+    def rotated(index):
+        value = slot(index)
+        turned = pltpu.roll(value, head_size // 2, 1)
+        return (value * turn_ref[:, :head_size] + turned * turn_ref[:, head_size:]).astype(
+            jnp.bfloat16
+        )
+
+    keys = rotated(queries)
+    values = slot(queries + 1).astype(jnp.bfloat16)
+    keys_ref[...] = keys
+    values_ref[...] = values
+    if earlier:
+        keys = jnp.concatenate([earlier_refs[0][...], keys], axis=0)
+        values = jnp.concatenate([earlier_refs[1][...], values], axis=0)
+    shape = (rows, keys.shape[0])
+    key_at = lax.broadcasted_iota(jnp.int32, shape, 1)
+    row_at = lax.broadcasted_iota(jnp.int32, shape, 0) + first_row
+    allowed = (key_at >= table_ref[:, 0:1]) & (key_at <= row_at)
+    for index in range(queries):
+        scores = lax.dot_general(
+            rotated(index), keys, (((1,), (1,)), ((), ())), preferred_element_type=jnp.float32
+        )
+        scores = jnp.where(allowed, scores * (1.0 / math.sqrt(head_size)), -1e30)
+        weights = jnp.exp(scores - jnp.max(scores, axis=1, keepdims=True))
+        scale = 1.0 / jnp.sum(weights, axis=1, keepdims=True)
+        attended = jnp.dot(
+            (weights * scale).astype(jnp.bfloat16), values, preferred_element_type=jnp.float32
+        )
+        out_ref[:, index * head_size : (index + 1) * head_size] = attended.astype(jnp.bfloat16)
+
+
+def attend(planes_of, adapters, part, table, turn, up, shrink, tokens, weight, begun, earlier):
     rows, depth = tokens.shape
     slots, _, head_size = weight.shape
     planes = len(shrink)
+    arrays = [table, turn, up, *shrink, tokens, weight, begun, *earlier]
+    specs = [None] * len(arrays)
+    for index in (0, 1):
+        specs[index] = rows_spec(arrays[index], rows, part)
+    specs[4 + planes] = shard_spec(weight, depth, planes - 1)
     return call(
-        functools.partial(attend_kernel, planes),
+        functools.partial(attend_kernel, planes, len(earlier) // 2),
         "attend",
         jnp.concatenate([planes_of, adapters]),
         1,
-        [None] * (4 + planes)
-        + [
-            pl.BlockSpec((slots, depth, head_size), lambda step, ids: (0, ids[planes - 1], 0)),
-            None,
-        ],
-        [table, turn, up, *shrink, tokens, weight, begun],
-        jax.ShapeDtypeStruct((rows, (slots - 2) * head_size), jnp.bfloat16),
+        specs,
+        arrays,
+        (
+            jax.ShapeDtypeStruct((rows, (slots - 2) * head_size), jnp.bfloat16),
+            jax.ShapeDtypeStruct((rows, head_size), jnp.bfloat16),
+            jax.ShapeDtypeStruct((rows, head_size), jnp.bfloat16),
+        ),
         [
             pltpu.VMEM((rows, slots * head_size), jnp.float32),
-            pltpu.VMEM((rows, head_size), jnp.bfloat16),
-            pltpu.VMEM((rows, head_size), jnp.bfloat16),
-            pltpu.VMEM((rows, shrink[0].shape[1]), jnp.bfloat16),
+            pltpu.VMEM((planes * shrink[0].shape[0], shrink[0].shape[1]), jnp.bfloat16),
         ],
     )
 
@@ -208,7 +216,7 @@
 def output_kernel(begun, last, lines, ids_ref, attended_ref, w_ref, down_ref, *refs):
     begun_refs, rest = refs[:begun], refs[begun:]
     if last:
-        table_ref, up_ref, out_ref = rest
+        table_ref, up_ref, before_refs, out_ref = rest[0], rest[1], rest[2:-1], rest[-1]
     else:
         acc_ref, low_ref = rest
     count = ids_ref.shape[0] - 1
@@ -237,13 +245,16 @@
         low = jnp.where(kept, low, 0.0).astype(jnp.bfloat16)
         up = jnp.concatenate([up_ref[ids_ref[1 + j]] for j in range(count)], axis=0)
         extra = jnp.dot(low, up, preferred_element_type=jnp.float32)
-        out_ref[...] = (total + extra).astype(jnp.bfloat16)
+        first_row = out_ref.shape[0] - total.shape[0]
+        for before_ref in before_refs:
+            out_ref[:first_row, :] = before_ref[...]
+        out_ref[first_row:, :] = (total + extra).astype(jnp.bfloat16)
     else:
         acc_ref[...] = total
         low_ref[...] = low
 
 
-def project_out(ids, rank, attended, weight, down, begun, final, turn=None):
+def project_out(ids, rank, attended, weight, down, begun, final, turn=None, part=0):
     rows, features = attended.shape
     columns = weight.shape[-1]
     if turn is None:
@@ -270,9 +281,11 @@
         "project_out",
         ids,
         1,
-        specs + [None] * (len(begun) + len(final)),
+        specs + [None] * len(begun) + [rows_spec(table, rows, part) for table in final[:1]]
+        + [None] * len(final[1:]),
         [attended, weight, down, *begun, *final],
-        jax.ShapeDtypeStruct((rows, columns), jnp.bfloat16) if final else sums,
+        jax.ShapeDtypeStruct((rows + sum(item.shape[0] for item in final[2:]), columns), jnp.bfloat16)
+        if final else sums,
     )
 
 
@@ -302,7 +315,9 @@
     def turned(value, turn=1):
         return lax.ppermute(value, "tensor", [(i, (i + turn) % planes) for i in range(planes)])
 
-    held = [tokens, turned(tokens)]
+    half_rows = token_rows // 2
+    held = [[tokens[:half_rows]], [tokens[half_rows:]]]
+    held[0].append(turned(held[0][0]))
     weight = jnp.transpose(query_key_value_weight, (1, 0, 2))
     down_all = lax.all_gather(adapter_down_maps, "dp", axis=0, tiled=True)
     up_all = lax.all_gather(jnp.transpose(adapter_up_maps[0], (1, 0, 2)), "dp", axis=0)
@@ -347,39 +362,68 @@
         for k in range(1, planes)
     ]
 
-    begun = project(planes_of[:1], held[:1], weight)
     lines = [turned(send, k) for k, send in enumerate(sends, 1)]
-    held[1] = after(held[1], begun, up_all, table, turn, own_rows, *lines)
+    begun = project(planes_of[:1], tokens, weight)
+
+    done = lax.optimization_barrier(
+        (held[0][1], held[1][0], lines, begun, table, turn, up_all, own_rows)
+    )
+    held[0][1], held[1][0], lines, begun, table, turn, up_all, own_rows = done
     lines = lax.all_gather(jnp.stack(lines), PLANE, axis=0)
-    sums = shrink_partial(adapters, here, planes, table, after(tokens, held[1]), down_all)
-    sums = [sums[0]] + [turned(sums[k], k) for k in range(1, planes)]
-    shrink = sum(sums[1:], sums[0]).astype(jnp.bfloat16)
+    begun = [begun, begun]
     for step in range(2, planes):
-        arrived = held[-1]
-        held.append(turned(arrived))
-        begun = project(planes_of[step - 1 : step], [arrived], weight, [begun])
-        held[-1] = after(held[-1], begun, *([shrink] if step == 2 else []))
-    shrink = after(shrink, held[2])
-    shrink = [shrink] + [turned(shrink, k) for k in range(1, planes)]
-    out_up_all = lax.all_gather(after(output_up_maps, held[2]), "dp", axis=0, tiled=True)
-    own_down = lax.all_gather(after(out_down, held[2]), "dp", axis=0)
-    held[-1] = after(held[-1], out_up_all, own_down)
-    attended = [
-        attend(planes_of, adapters, table, turn, up_all, shrink, held[-1], weight, begun)
+        for part in range(2):
+            held[part].append(turned(held[part][-1]))
+            number = step - 1 - part
+            if number > 0:
+                begun[part] = project(
+                    planes_of[number : number + 1], held[part][number], weight, [begun[part]], part
+                )
+        if step == 2:
+            sums = shrink_partial(adapters, here, planes, table, after(tokens, held[0][1]), down_all)
+            side = [sums[0]] + [turned(sums[k], k) for k in range(1, planes)]
+        elif step == 3:
+            shrink = sum(side[1:], side[0]).astype(jnp.bfloat16)
+            out_up = after(output_up_maps, held[0][2])
+            own_down = after(out_down, held[0][2])
+            side = [shrink] + [turned(shrink, k) for k in range(1, planes)] + [
+                lax.all_gather(out_up, "dp", axis=0, tiled=True),
+                lax.all_gather(own_down, "dp", axis=0),
+            ]
+        held[0][-1], held[1][-1], begun, side = lax.optimization_barrier(
+            (held[0][-1], held[1][-1], begun, side)
+        )
+    shrink, out_up_all, own_down = side[:planes], side[-2], side[-1]
+    held[1].append(turned(held[1][-1]))
+    begun[1] = project(
+        planes_of[planes - 2 : planes - 1], held[1][planes - 2], weight, [begun[1]], 1
+    )
+
+    ids = jnp.concatenate([lax.axis_index("groups")[None], adapters])
+    attended, earlier = [[], []], ()
+    for part in range(2):
+        made, *earlier = attend(
+            planes_of, adapters, part, table, turn, up_all, shrink, held[part][-1], weight,
+            begun[part], earlier,
+        )
+        attended[part] = [made, turned(made)]
+        earlier = [after(array, attended[part][1]) for array in earlier]
+    sums = [
+        project_out(ids, rank, attended[part][0], own_rows, own_down, [], []) for part in range(2)
     ]
-
-    ids = jnp.concatenate([lax.axis_index("groups")[None], adapters])
-    attended.append(turned(attended[0]))
-    sums = project_out(ids, rank, attended[0], own_rows, own_down, [], [])
+    before = []
     for step in range(2, planes + 1):
-        arrived = after(attended[-1], *sums)
-        if step < planes:
-            attended.append(turned(arrived))
-        sums = project_out(
-            ids, rank, arrived, lines, pool, list(sums),
-            [] if step < planes else [table, out_up_all], step - 1,
-        )
-    return sums
+        for part in range(2):
+            arrived = after(attended[part][-1], *sums[part])
+            if step < planes:
+                attended[part].append(turned(arrived))
+            final = [] if step < planes else [table, out_up_all, *before]
+            sums[part] = project_out(
+                ids, rank, arrived, lines, pool, list(sums[part]), final, step - 1, part
+            )
+            if final:
+                before = [sums[part]]
+    return before[0]
 
 
 def solution(mesh):

time: 186 us -> 180 us (0.968)
  waiting for transfers between devices: 79.2 us -> 60.9 us
  Pallas kernels: 23.3 us -> 29.7 us
  starting transfers between devices: 24.5 us -> 28.8 us
  local copies, waits for them, and re-layouts: 19.4 us -> 21.7 us
  blocking collectives: 22 us -> 20 us
  other arithmetic: 2.88 us -> 4.8 us
    ppermute x15 -> x21, waiting for transfers between devices: 78.5 us -> 60.8 us  [turned(): lax.ppermute(value, 'tensor', [(i, (i + turn) % planes) for i in range(pl...]
    pallas_call x9 -> x16, Pallas kernels: 23.3 us -> 29.7 us  [call(): pl.pallas_call(kernel, out_shape=out, grid_spec=pltpu.PrefetchScalarGridS...]
    ppermute x15 -> x21, starting transfers between devices: 24.5 us -> 28.8 us  [turned(): lax.ppermute(value, 'tensor', [(i, (i + turn) % planes) for i in range(pl...]
    slice x1 -> x2, local copies, waits for them, and re-layouts: 0.65 us -> 2.97 us  [the longest x1 2.31 us: local(): held = [[tokens[:half_rows]], [tokens[half_rows:]]]]
    unnamed x36 -> x34, local copies, waits for them, and re-layouts: 12.7 us -> 12 us
  transfers between devices with their start and end apart: 17 -> 23, of which waited for: 12 -> 12; matrix products, arithmetic and copies ran while one was open for 5% -> 7% of each run, Pallas kernels for 11% -> 15%
where the time goes in v10:
time: 180 us
  waiting for transfers between devices  60.9 us (34%)
  Pallas kernels  29.7 us (16%)
  starting transfers between devices  28.8 us (16%)
  local copies, waits for them, and re-layouts  21.7 us (12%)
  blocking collectives  20 us (11%)
  between operations  13.8 us (8%)
  other arithmetic  4.8 us (3%)
    ppermute x21, waiting for transfers between devices, turned(): lax.ppermute(value, 'tensor', [(i, (i + turn) % planes) for i in range(pl...  60.8 us
    pallas_call x16, Pallas kernels, call(): pl.pallas_call(kernel, out_shape=out, grid_spec=pltpu.PrefetchScalarGridS...  29.7 us
    ppermute x21, starting transfers between devices, turned(): lax.ppermute(value, 'tensor', [(i, (i + turn) % planes) for i in range(pl...  28.8 us
    unnamed x34, local copies, waits for them, and re-layouts  12 us
    all_gather x1, blocking collectives, local(): lax.all_gather(out_up, 'dp', axis=0, tiled=True)  7.16 us
    all_gather x1, blocking collectives, local(): lax.all_gather(jnp.transpose(adapter_up_maps[0], (1, 0, 2)), 'dp', axis=0)  6.91 us
    all_gather x1, blocking collectives, local(): lax.all_gather(own_down, 'dp', axis=0)  5.98 us
  transfers between devices with their start and end apart: 23, of which 12 were waited for; matrix products, arithmetic and copies ran while one was open for 7% of the time, Pallas kernels for 15%

profile of v10, /device:TPU:0, one launch (start us, length us, event | category | flops | bytes accessed | tf_op | source)
XLA Modules:
  0.0 179.8 jit_solution(17866285348120008323)
XLA Ops:
  6.5 2.3 %fusion.5 = (bf16[256,1024]{1,0:T(8,128)(2,1)}, bf16[256,1024]{1,0:T(8,128)(2,1)}) fusion(bf16[512,1024]{1,0:T(8,128)(2,1)} %token_ref), kind=kLoop, calls=%fused_computation.33 | loop fusion | bytes 2097152 | tf_op jit(solution)/shard_map/slice | solution.py:319
  8.8 3.0 %collective-permute-start = (bf16[256,1024]{1,0:T(8,128)(2,1)}, bf16[256,1024]{1,0:T(8,128)(2,1)}, u32[]{:S(2)}, u32[]{:S(2)}) collective-permute-start(bf16[256,1024]{1,0:T(8,128)(2,1)} %get-tuple-element.127), channel_id=1, source_target_pairs={{0,1},{1,2},{2,3},{3,0},{4,5},{5,6},{6,7},{7,4},{8,9},{9,10},{10,1... | collective-permute-start | bytes 1572872 | tf_op jit(solution)/shard_map/ppermute | solution.py:316
  12.9 2.8 %fusion.4 = (bf16[64,1,1024]{2,1,0:T(2,128)(2,1)S(1)}, bf16[64,1,1024]{2,1,0:T(2,128)(2,1)S(1)}, bf16[64,1,1024]{2,1,0:T(2,128)(2,1)S(1)}) fusion(bf16[128,4,4096]{2,1,0:T(4,128)(2,1)} %param.11, s32[]{:T(128)S(6)} %select_n.64, s32[]{:T(128)S(6)} %select_n.67, s32[]{:T(128)S(6)} %select_n.76, s32[]{:T(128)S(6)} %select_n.73, s32[]{:T(128)S(6)} %select_n.70), kind=kLoop, calls=%fused_computation.32 | loop fusion | bytes 786452 | tf_op jit(solution)/shard_map/dynamic_slice | solution.py:358
  19.4 2.9 %collective-permute-start.3 = (bf16[96,1024]{1,0:T(8,128)(2,1)}, bf16[96,1024]{1,0:T(8,128)(2,1)}, u32[]{:S(2)}, u32[]{:S(2)}) collective-permute-start(bf16[96,1024]{1,0:T(8,128)(2,1)} %get-tuple-element.128), channel_id=1, source_target_pairs={{0,3},{1,0},{2,1},{3,2},{4,7},{5,4},{6,5},{7,6},{8,11},{9,8},{10,9... | collective-permute-start | bytes 589832 | tf_op jit(solution)/shard_map/ppermute | solution.py:316
  27.5 2.8 %copy-done.2 = bf16[4096,6,128]{2,0,1:T(8,128)(2,1)S(1)} copy-done((bf16[4096,6,128]{2,0,1:T(8,128)(2,1)S(1)}, bf16[4096,6,128]{2,0,1:T(8,128)(2,1)}, u32[]{:S(2)}) %copy-start.2) | copy-done | bytes 6291480
  32.1 6.9 %all-gather = bf16[24,64,128]{2,1,0:T(8,128)(2,1)} all-gather(bf16[6,64,128]{2,1,0:T(8,128)(2,1)S(1)} %bitcast.66), channel_id=2, replica_groups=mesh['groups'=2,'dp'=4,'tensor'=4] {'dp'}, dimensions={0}, use_global_device_ids=true | all-gather | bytes 491520 | tf_op jit(solution)/shard_map/all_gather | solution.py:323
  41.0 4.6 %collective-permute-start.4 = (bf16[256,1024]{1,0:T(8,128)(2,1)}, bf16[256,1024]{1,0:T(8,128)(2,1)}, u32[]{:S(2)}, u32[]{:S(2)}) collective-permute-start(bf16[256,1024]{1,0:T(8,128)(2,1)} %collective-permute-done.refs_0_), channel_id=1, source_target_pairs={{0,1},{1,2},{2,3},{3,0},{4,5},{5,6},{6,7},{7,4},{8,9},{9,10},{10,1... | collective-permute-start | bytes 1572872 | tf_op jit(solution)/shard_map/ppermute | solution.py:316
  47.4 2.7 %shrink.1 = (f32[128,192]{1,0:T(8,128)S(1)}, f32[128,192]{1,0:T(8,128)S(1)}, f32[128,192]{1,0:T(8,128)S(1)}, f32[128,192]{1,0:T(8,128)S(1)}) custom-call(s32[5]{0:T(128)S(1)} %pad_add_fusion.3.ids_ref, s32[512,2]{1,0:T(8,128)S(1)} %copy.35.table_ref.refs_2_, bf16[512,1024]{1,0:T(8,128)(2,1)S(1)} %copy-done.4, bf16[4,192,1024]{2,1,0:T(8,128)(2,1)S(1)} %copy-done.7), custom_call_target="tpu_custom_call" | custom-call | bytes 7876608 | tf_op jit(solution)/shard_map/shrink/pallas_call | solution.py:26
  50.1 2.1 %collective-permute-start.6 = (f32[128,192]{1,0:T(8,128)S(1)}, f32[128,192]{1,0:T(8,128)S(1)}, u32[]{:S(2)}, u32[]{:S(2)}) collective-permute-start(f32[128,192]{1,0:T(8,128)S(1)} %get-tuple-element.72), channel_id=1, source_target_pairs={{0,1},{1,2},{2,3},{3,0},{4,5},{5,6},{6,7},{7,4},{8,9},{9,10},{10,1... | collective-permute-start | bytes 294920 | tf_op jit(solution)/shard_map/ppermute | solution.py:316
  52.2 2.2 %collective-permute-start.7 = (f32[128,192]{1,0:T(8,128)S(1)}, f32[128,192]{1,0:T(8,128)S(1)}, u32[]{:S(2)}, u32[]{:S(2)}) collective-permute-start(f32[128,192]{1,0:T(8,128)S(1)} %get-tuple-element.73), channel_id=1, source_target_pairs={{0,2},{1,3},{2,0},{3,1},{4,6},{5,7},{6,4},{7,5},{8,10},{9,11},{10,... | collective-permute-start | bytes 294920 | tf_op jit(solution)/shard_map/ppermute | solution.py:316
  54.7 2.8 %copy-done.3 = bf16[4096,6,128]{2,0,1:T(8,128)(2,1)S(1)} copy-done((bf16[4096,6,128]{2,0,1:T(8,128)(2,1)S(1)}, bf16[4096,6,128]{2,0,1:T(8,128)(2,1)}, u32[]{:S(2)}) %copy-start.3) | copy-done | bytes 6291480
  57.5 2.3 %project.6.refs_2_ = f32[256,768]{1,0:T(8,128)S(1)} custom-call(s32[1]{0:T(128)} %get-tuple-element.137.ids_ref, bf16[256,1024]{1,0:T(8,128)(2,1)} %collective-permute-done.refs_0_, bf16[6,4096,128]{2,1,0:T(8,128)(2,1)S(1)} %bitcast.49, f32[512,768]{1,0:T(8,128)S(1)} %project.5.refs_2_), custom_call_target="tpu_custom_call" | custom-call | bytes 25165824 | tf_op jit(solution)/shard_map/project/pallas_call | solution.py:26
  60.1 11.2 %collective-permute-done.5.refs_0_ = bf16[256,1024]{1,0:T(8,128)(2,1)} collective-permute-done((bf16[256,1024]{1,0:T(8,128)(2,1)}, bf16[256,1024]{1,0:T(8,128)(2,1)}, u32[]{:S(2)}, u32[]{:S(2)}) %collective-permute-start.5) | collective-permute-done | bytes 524320 | tf_op jit(solution)/shard_map/ppermute | solution.py:316
  71.2 2.7 %collective-permute-done.6 = f32[128,192]{1,0:T(8,128)S(1)} collective-permute-done((f32[128,192]{1,0:T(8,128)S(1)}, f32[128,192]{1,0:T(8,128)S(1)}, u32[]{:S(2)}, u32[]{:S(2)}) %collective-permute-start.6) | collective-permute-done | bytes 98336 | tf_op jit(solution)/shard_map/ppermute | solution.py:316
  73.9 3.8 %collective-permute-done.7 = f32[128,192]{1,0:T(8,128)S(1)} collective-permute-done((f32[128,192]{1,0:T(8,128)S(1)}, f32[128,192]{1,0:T(8,128)S(1)}, u32[]{:S(2)}, u32[]{:S(2)}) %collective-permute-start.7) | collective-permute-done | bytes 98336 | tf_op jit(solution)/shard_map/ppermute | solution.py:316
  77.8 3.3 %collective-permute-start.9 = (bf16[256,1024]{1,0:T(8,128)(2,1)}, bf16[256,1024]{1,0:T(8,128)(2,1)S(1)}, u32[]{:S(2)}, u32[]{:S(2)}) collective-permute-start(bf16[256,1024]{1,0:T(8,128)(2,1)} %collective-permute-done.4.refs_0_), channel_id=1, source_target_pairs={{0,1},{1,2},{2,3},{3,0},{4,5},{5,6},{6,7},{7,4},{8,9},{9,10},{10,1... | collective-permute-start | bytes 1572872 | tf_op jit(solution)/shard_map/ppermute | solution.py:316
  81.1 2.9 %collective-permute-start.11 = (bf16[128,192]{1,0:T(8,128)(2,1)S(1)}, bf16[128,192]{1,0:T(8,128)(2,1)S(1)}, u32[]{:S(2)}, u32[]{:S(2)}) collective-permute-start(bf16[128,192]{1,0:T(8,128)(2,1)S(1)} %add_convert_fusion.refs_0_), channel_id=1, source_target_pairs={{0,1},{1,2},{2,3},{3,0},{4,5},{5,6},{6,7},{7,4},{8,9},{9,10},{10,1... | collective-permute-start | bytes 147464 | tf_op jit(solution)/shard_map/ppermute | solution.py:316
  86.5 7.2 %all_gather.27.refs_3_ = bf16[4,64,1024]{2,1,0:T(8,128)(2,1)S(1)} all-gather(bf16[1,64,1024]{2,1,0:T(8,128)(2,1)S(1)} %copy-done.10), channel_id=1, replica_groups=mesh['groups'=2,'dp'=4,'tensor'=4] {'dp'}, dimensions={0}, use_global_device_ids=true | all-gather | bytes 655360 | tf_op jit(solution)/shard_map/all_gather | solution.py:390
  93.7 6.0 %all-gather.1 = bf16[128,1024]{1,0:T(8,128)(2,1)S(1)} all-gather(bf16[32,1024]{1,0:T(8,128)(2,1)S(1)} %bitcast_dynamic-update-slice_fusion), channel_id=3, replica_groups=mesh['groups'=2,'dp'=4,'tensor'=4] {'dp'}, dimensions={0}, use_global_device_ids=true | all-gather | bytes 327680 | tf_op jit(solution)/shard_map/all_gather | solution.py:391
  99.6 2.5 %project.8.refs_2_ = f32[256,768]{1,0:T(8,128)S(1)} custom-call(s32[1]{0:T(128)} %get-tuple-element.137.ids_ref, bf16[256,1024]{1,0:T(8,128)(2,1)} %collective-permute-done.5.refs_0_, bf16[6,4096,128]{2,1,0:T(8,128)(2,1)S(1)} %bitcast.50, f32[512,768]{1,0:T(8,128)S(1)} %project.5.refs_2_), custom_call_target="tpu_custom_call" | custom-call | bytes 25165824 | tf_op jit(solution)/shard_map/project/pallas_call | solution.py:26
  102.1 2.3 %project.7.refs_6_ = f32[256,768]{1,0:T(8,128)S(1)} custom-call(s32[1]{0:T(128)} %get-tuple-element.136.ids_ref, bf16[256,1024]{1,0:T(8,128)(2,1)} %collective-permute-done.4.refs_0_, bf16[6,4096,128]{2,1,0:T(8,128)(2,1)S(1)} %bitcast.51, f32[256,768]{1,0:T(8,128)S(1)} %project.6.refs_2_), custom_call_target="tpu_custom_call" | custom-call | bytes 22806528 | tf_op jit(solution)/shard_map/project/pallas_call | solution.py:26
  104.4 4.2 %collective-permute-done.11.refs_1_ = bf16[128,192]{1,0:T(8,128)(2,1)S(1)} collective-permute-done((bf16[128,192]{1,0:T(8,128)(2,1)S(1)}, bf16[128,192]{1,0:T(8,128)(2,1)S(1)}, u32[]{:S(2)}, u32[]{:S(2)}) %collective-permute-start.11) | collective-permute-done | bytes 49184 | tf_op jit(solution)/shard_map/ppermute | solution.py:316
  112.2 3.2 %attend.2 = (bf16[256,512]{1,0:T(8,128)(2,1)S(1)}, bf16[256,128]{1,0:T(8,128)(2,1)S(1)}, bf16[256,128]{1,0:T(8,128)(2,1)S(1)}) custom-call(s32[8]{0:T(128)S(1)} %pad_add_fusion.2.ids_ref, s32[512,2]{1,0:T(8,128)S(1)} %copy.35.table_ref.refs_2_, f32[512,256]{1,0:T(8,128)S(1)} %pad_maximum_fusion.1.turn_ref, bf16[4,6,64,128]{3,2,1,0:T(8,128)(2,1)S(1)} %bitcast.59, ...), custom_call_target="tpu_custom_call" | custom-call | bytes 26161152 | tf_op jit(solution)/shard_map/attend/pallas_call | solution.py:26
  116.9 14.5 %collective-permute-done.15.attended_ref = bf16[256,512]{1,0:T(8,128)(2,1)S(1)} collective-permute-done((bf16[256,512]{1,0:T(8,128)(2,1)S(1)}, bf16[256,512]{1,0:T(8,128)(2,1)S(1)}, u32[]{:S(2)}, u32[]{:S(2)}) %collective-permute-start.15) | collective-permute-done | bytes 262176 | tf_op jit(solution)/shard_map/ppermute | solution.py:316
  131.4 3.9 %attend.3 = (bf16[256,512]{1,0:T(8,128)(2,1)S(1)}, bf16[256,128]{1,0:T(8,128)(2,1)}, bf16[256,128]{1,0:T(8,128)(2,1)}) custom-call(s32[8]{0:T(128)S(1)} %pad_add_fusion.2.ids_ref, s32[512,2]{1,0:T(8,128)S(1)} %copy.35.table_ref.refs_2_, f32[512,256]{1,0:T(8,128)S(1)} %pad_maximum_fusion.1.turn_ref, bf16[4,6,64,128]{3,2,1,0:T(8,128)(2,1)S(1)} %bitcast.60, ...), custom_call_target="tpu_custom_call" | custom-call | bytes 26554368 | tf_op jit(solution)/shard_map/attend/pallas_call | solution.py:26
  136.6 7.8 %collective-permute-done.16.attended_ref = bf16[256,512]{1,0:T(8,128)(2,1)S(1)} collective-permute-done((bf16[256,512]{1,0:T(8,128)(2,1)S(1)}, bf16[256,512]{1,0:T(8,128)(2,1)S(1)}, u32[]{:S(2)}, u32[]{:S(2)}) %collective-permute-start.16) | collective-permute-done | bytes 262176 | tf_op jit(solution)/shard_map/ppermute | solution.py:316
  146.5 2.3 %copy-done = bf16[24,96,1024]{2,1,0:T(8,128)(2,1)S(1)} copy-done((bf16[24,96,1024]{2,1,0:T(8,128)(2,1)S(1)}, bf16[24,96,1024]{2,1,0:T(8,128)(2,1)}, u32[]{:S(2)}) %copy-start) | copy-done | bytes 4718616
  152.5 2.9 %collective-permute-done.17.attended_ref = bf16[256,512]{1,0:T(8,128)(2,1)S(1)} collective-permute-done((bf16[256,512]{1,0:T(8,128)(2,1)S(1)}, bf16[256,512]{1,0:T(8,128)(2,1)S(1)}, u32[]{:S(2)}, u32[]{:S(2)}) %collective-permute-start.17) | collective-permute-done | bytes 262176 | tf_op jit(solution)/shard_map/ppermute | solution.py:316
  155.5 5.6 %collective-permute-done.19.attended_ref = bf16[256,512]{1,0:T(8,128)(2,1)S(1)} collective-permute-done((bf16[256,512]{1,0:T(8,128)(2,1)S(1)}, bf16[256,512]{1,0:T(8,128)(2,1)S(1)}, u32[]{:S(2)}, u32[]{:S(2)}) %collective-permute-start.19) | collective-permute-done | bytes 262176 | tf_op jit(solution)/shard_map/ppermute | solution.py:316
  163.3 3.4 %collective-permute-done.18.attended_ref = bf16[256,512]{1,0:T(8,128)(2,1)S(1)} collective-permute-done((bf16[256,512]{1,0:T(8,128)(2,1)S(1)}, bf16[256,512]{1,0:T(8,128)(2,1)S(1)}, u32[]{:S(2)}, u32[]{:S(2)}) %collective-permute-start.18) | collective-permute-done | bytes 262176 | tf_op jit(solution)/shard_map/ppermute | solution.py:316
  166.6 2.8 %collective-permute-done.20.attended_ref = bf16[256,512]{1,0:T(8,128)(2,1)S(1)} collective-permute-done((bf16[256,512]{1,0:T(8,128)(2,1)S(1)}, bf16[256,512]{1,0:T(8,128)(2,1)S(1)}, u32[]{:S(2)}, u32[]{:S(2)}) %collective-permute-start.20) | collective-permute-done | bytes 262176 | tf_op jit(solution)/shard_map/ppermute | solution.py:316
  170.7 2.3 %project_out.15 = bf16[512,1024]{1,0:T(8,128)(2,1)} custom-call(s32[5]{0:T(128)S(1)} %pad_add_fusion.1.ids_ref, bf16[256,512]{1,0:T(8,128)(2,1)S(1)} %collective-permute-done.18.attended_ref, bf16[8,3,96,1024]{3,2,1,0:T(8,128)(2,1)S(1)} %bitcast.46, bf16[8,3,96,1024]{3,2,1,0:T(8,128)(2,1)S(1)} %bitcast.47, f32[256,1024]{1,0:T(8,128)S(1)} %get-tuple-element.110.refs_0_, ...), custom_call_target="tpu_custom_call" | custom-call | bytes 36188160 | tf_op jit(solution)/shard_map/project_out/pallas_call | solution.py:26
  (98 shorter events, 33.7 us)
Async XLA Ops:
  6.5 15.7 %copy-start.12 = (s32[1,4]{1,0:T(1,128)S(1)}, s32[1,4]{1,0:T(1,128)}, u32[]{:S(2)}) copy-start(s32[1,4]{1,0:T(1,128)} %param.17) | copy-start | bytes 52
  6.5 15.9 %copy-start.13 = (s32[1,4]{1,0:T(1,128)S(1)}, s32[1,4]{1,0:T(1,128)}, u32[]{:S(2)}) copy-start(s32[1,4]{1,0:T(1,128)} %param.16) | copy-start | bytes 52
  6.5 39.5 %all-gather.6.cloned.1.call-start = ((), (), s32[]{:S(2)}) async-start(), calls=%async_computation | async-start | bytes 1966080 | tf_op jit(solution)/shard_map/all_gather | solution.py:322
  8.8 30.1 %collective-permute-start = (bf16[256,1024]{1,0:T(8,128)(2,1)}, bf16[256,1024]{1,0:T(8,128)(2,1)}, u32[]{:S(2)}, u32[]{:S(2)}) collective-permute-start(bf16[256,1024]{1,0:T(8,128)(2,1)} %get-tuple-element.127), channel_id=1, source_target_pairs={{0,1},{1,2},{2,3},{3,0},{4,5},{5,6},{6,7},{7,4},{8,9},{9,10},{10,1... | collective-permute-start | bytes 1572872 | tf_op jit(solution)/shard_map/ppermute | solution.py:316
  11.9 134.6 %all-gather.8.cloned.1.call-start = ((), (), s32[]{:S(2)}) async-start(), calls=%async_computation.1 | async-start | bytes 5308416 | tf_op jit(solution)/shard_map/all_gather | solution.py:372
  15.8 11.8 %copy-start.4 = (bf16[512,1024]{1,0:T(8,128)(2,1)S(1)}, bf16[512,1024]{1,0:T(8,128)(2,1)}, u32[]{:S(2)}) copy-start(bf16[512,1024]{1,0:T(8,128)(2,1)} %token_ref) | copy-start | bytes 3145732
  16.8 22.2 %collective-permute-start.1 = (bf16[96,1024]{1,0:T(8,128)(2,1)}, bf16[96,1024]{1,0:T(8,128)(2,1)}, u32[]{:S(2)}, u32[]{:S(2)}) collective-permute-start(bf16[96,1024]{1,0:T(8,128)(2,1)} %get-tuple-element.130), channel_id=1, source_target_pairs={{0,1},{1,2},{2,3},{3,0},{4,5},{5,6},{6,7},{7,4},{8,9},{9,10},{10,1... | collective-permute-start | bytes 589832 | tf_op jit(solution)/shard_map/ppermute | solution.py:316
  18.3 20.6 %collective-permute-start.2 = (bf16[96,1024]{1,0:T(8,128)(2,1)}, bf16[96,1024]{1,0:T(8,128)(2,1)}, u32[]{:S(2)}, u32[]{:S(2)}) collective-permute-start(bf16[96,1024]{1,0:T(8,128)(2,1)} %get-tuple-element.129), channel_id=1, source_target_pairs={{0,2},{1,3},{2,0},{3,1},{4,6},{5,7},{6,4},{7,5},{8,10},{9,11},{10,... | collective-permute-start | bytes 589832 | tf_op jit(solution)/shard_map/ppermute | solution.py:316
  19.4 19.6 %collective-permute-start.3 = (bf16[96,1024]{1,0:T(8,128)(2,1)}, bf16[96,1024]{1,0:T(8,128)(2,1)}, u32[]{:S(2)}, u32[]{:S(2)}) collective-permute-start(bf16[96,1024]{1,0:T(8,128)(2,1)} %get-tuple-element.128), channel_id=1, source_target_pairs={{0,3},{1,0},{2,1},{3,2},{4,7},{5,4},{6,5},{7,6},{8,11},{9,8},{10,9... | collective-permute-start | bytes 589832 | tf_op jit(solution)/shard_map/ppermute | solution.py:316
  27.5 2.8 %copy-start.2 = (bf16[4096,6,128]{2,0,1:T(8,128)(2,1)S(1)}, bf16[4096,6,128]{2,0,1:T(8,128)(2,1)}, u32[]{:S(2)}) copy-start(bf16[4096,6,128]{2,0,1:T(8,128)(2,1)} %param.10) | copy-start | bytes 18874372
  41.0 19.0 %collective-permute-start.4 = (bf16[256,1024]{1,0:T(8,128)(2,1)}, bf16[256,1024]{1,0:T(8,128)(2,1)}, u32[]{:S(2)}, u32[]{:S(2)}) collective-permute-start(bf16[256,1024]{1,0:T(8,128)(2,1)} %collective-permute-done.refs_0_), channel_id=1, source_target_pairs={{0,1},{1,2},{2,3},{3,0},{4,5},{5,6},{6,7},{7,4},{8,9},{9,10},{10,1... | collective-permute-start | bytes 1572872 | tf_op jit(solution)/shard_map/ppermute | solution.py:316
  45.7 25.6 %collective-permute-start.5 = (bf16[256,1024]{1,0:T(8,128)(2,1)}, bf16[256,1024]{1,0:T(8,128)(2,1)}, u32[]{:S(2)}, u32[]{:S(2)}) collective-permute-start(bf16[256,1024]{1,0:T(8,128)(2,1)} %get-tuple-element.68), channel_id=1, source_target_pairs={{0,1},{1,2},{2,3},{3,0},{4,5},{5,6},{6,7},{7,4},{8,9},{9,10},{10,1... | collective-permute-start | bytes 1572872 | tf_op jit(solution)/shard_map/ppermute | solution.py:316
  50.1 23.9 %collective-permute-start.6 = (f32[128,192]{1,0:T(8,128)S(1)}, f32[128,192]{1,0:T(8,128)S(1)}, u32[]{:S(2)}, u32[]{:S(2)}) collective-permute-start(f32[128,192]{1,0:T(8,128)S(1)} %get-tuple-element.72), channel_id=1, source_target_pairs={{0,1},{1,2},{2,3},{3,0},{4,5},{5,6},{6,7},{7,4},{8,9},{9,10},{10,1... | collective-permute-start | bytes 294920 | tf_op jit(solution)/shard_map/ppermute | solution.py:316
  52.2 25.5 %collective-permute-start.7 = (f32[128,192]{1,0:T(8,128)S(1)}, f32[128,192]{1,0:T(8,128)S(1)}, u32[]{:S(2)}, u32[]{:S(2)}) collective-permute-start(f32[128,192]{1,0:T(8,128)S(1)} %get-tuple-element.73), channel_id=1, source_target_pairs={{0,2},{1,3},{2,0},{3,1},{4,6},{5,7},{6,4},{7,5},{8,10},{9,11},{10,... | collective-permute-start | bytes 294920 | tf_op jit(solution)/shard_map/ppermute | solution.py:316
  54.4 23.3 %collective-permute-start.8 = (f32[128,192]{1,0:T(8,128)S(1)}, f32[128,192]{1,0:T(8,128)S(1)}, u32[]{:S(2)}, u32[]{:S(2)}) collective-permute-start(f32[128,192]{1,0:T(8,128)S(1)} %get-tuple-element.74), channel_id=1, source_target_pairs={{0,3},{1,0},{2,1},{3,2},{4,7},{5,4},{6,5},{7,6},{8,11},{9,8},{10,9... | collective-permute-start | bytes 294920 | tf_op jit(solution)/shard_map/ppermute | solution.py:316
  57.5 29.0 %copy-start.10 = (bf16[1,64,1024]{2,1,0:T(8,128)(2,1)S(1)}, bf16[1,64,1024]{2,1,0:T(8,128)(2,1)}, u32[]{:S(2)}) copy-start(bf16[1,64,1024]{2,1,0:T(8,128)(2,1)} %param.15) | copy-start | bytes 393220
  77.8 32.4 %collective-permute-start.9 = (bf16[256,1024]{1,0:T(8,128)(2,1)}, bf16[256,1024]{1,0:T(8,128)(2,1)S(1)}, u32[]{:S(2)}, u32[]{:S(2)}) collective-permute-start(bf16[256,1024]{1,0:T(8,128)(2,1)} %collective-permute-done.4.refs_0_), channel_id=1, source_target_pairs={{0,1},{1,2},{2,3},{3,0},{4,5},{5,6},{6,7},{7,4},{8,9},{9,10},{10,1... | collective-permute-start | bytes 1572872 | tf_op jit(solution)/shard_map/ppermute | solution.py:316
  81.0 29.2 %collective-permute-start.10 = (bf16[256,1024]{1,0:T(8,128)(2,1)}, bf16[256,1024]{1,0:T(8,128)(2,1)S(1)}, u32[]{:S(2)}, u32[]{:S(2)}) collective-permute-start(bf16[256,1024]{1,0:T(8,128)(2,1)} %collective-permute-done.5.refs_0_), channel_id=1, source_target_pairs={{0,1},{1,2},{2,3},{3,0},{4,5},{5,6},{6,7},{7,4},{8,9},{9,10},{10,1... | collective-permute-start | bytes 1572872 | tf_op jit(solution)/shard_map/ppermute | solution.py:316
  81.1 27.5 %collective-permute-start.11 = (bf16[128,192]{1,0:T(8,128)(2,1)S(1)}, bf16[128,192]{1,0:T(8,128)(2,1)S(1)}, u32[]{:S(2)}, u32[]{:S(2)}) collective-permute-start(bf16[128,192]{1,0:T(8,128)(2,1)S(1)} %add_convert_fusion.refs_0_), channel_id=1, source_target_pairs={{0,1},{1,2},{2,3},{3,0},{4,5},{5,6},{6,7},{7,4},{8,9},{9,10},{10,1... | collective-permute-start | bytes 147464 | tf_op jit(solution)/shard_map/ppermute | solution.py:316
  84.1 26.2 %collective-permute-start.12 = (bf16[128,192]{1,0:T(8,128)(2,1)S(1)}, bf16[128,192]{1,0:T(8,128)(2,1)S(1)}, u32[]{:S(2)}, u32[]{:S(2)}) collective-permute-start(bf16[128,192]{1,0:T(8,128)(2,1)S(1)} %add_convert_fusion.refs_0_), channel_id=1, source_target_pairs={{0,2},{1,3},{2,0},{3,1},{4,6},{5,7},{6,4},{7,5},{8,10},{9,11},{10,... | collective-permute-start | bytes 147464 | tf_op jit(solution)/shard_map/ppermute | solution.py:316
  85.5 24.7 %collective-permute-start.13 = (bf16[128,192]{1,0:T(8,128)(2,1)S(1)}, bf16[128,192]{1,0:T(8,128)(2,1)S(1)}, u32[]{:S(2)}, u32[]{:S(2)}) collective-permute-start(bf16[128,192]{1,0:T(8,128)(2,1)S(1)} %add_convert_fusion.refs_0_), channel_id=1, source_target_pairs={{0,3},{1,0},{2,1},{3,2},{4,7},{5,4},{6,5},{7,6},{8,11},{9,8},{10,9... | collective-permute-start | bytes 147464 | tf_op jit(solution)/shard_map/ppermute | solution.py:316
  93.7 18.5 %slice-start = ((s8[6291456]{0:T(1024)(128)(4,1)}), s8[4194304]{0:T(1024)(128)(4,1)S(1)}, s32[]{:S(2)}) async-start(s8[6291456]{0:T(1024)(128)(4,1)} %bitcast.52), calls=%async_computation.2 | async-start | bytes 8388608
  99.6 12.5 %slice-start.1 = ((s8[6291456]{0:T(1024)(128)(4,1)}), s8[2097152]{0:T(1024)(128)(4,1)S(1)}, s32[]{:S(2)}) async-start(s8[6291456]{0:T(1024)(128)(4,1)} %bitcast.52), calls=%async_computation.3 | async-start | bytes 4194304
  102.1 10.1 %copy-start.6 = (bf16[24,64,128]{2,1,0:T(8,128)(2,1)S(1)}, bf16[24,64,128]{2,1,0:T(8,128)(2,1)}, u32[]{:S(2)}) copy-start(bf16[24,64,128]{2,1,0:T(8,128)(2,1)} %all-gather) | copy-start | bytes 1179652
  110.2 21.2 %collective-permute-start.14 = (bf16[256,1024]{1,0:T(8,128)(2,1)S(1)}, bf16[256,1024]{1,0:T(8,128)(2,1)S(1)}, u32[]{:S(2)}, u32[]{:S(2)}) collective-permute-start(bf16[256,1024]{1,0:T(8,128)(2,1)S(1)} %collective-permute-done.10.refs_0_), channel_id=1, source_target_pairs={{0,1},{1,2},{2,3},{3,0},{4,5},{5,6},{6,7},{7,4},{8,9},{9,10},{10,1... | collective-permute-start | bytes 1572872 | tf_op jit(solution)/shard_map/ppermute | solution.py:316
  115.3 16.1 %collective-permute-start.15 = (bf16[256,512]{1,0:T(8,128)(2,1)S(1)}, bf16[256,512]{1,0:T(8,128)(2,1)S(1)}, u32[]{:S(2)}, u32[]{:S(2)}) collective-permute-start(bf16[256,512]{1,0:T(8,128)(2,1)S(1)} %get-tuple-element.94.attended_ref), channel_id=1, source_target_pairs={{0,1},{1,2},{2,3},{3,0},{4,5},{5,6},{6,7},{7,4},{8,9},{9,10},{10,1... | collective-permute-start | bytes 786440 | tf_op jit(solution)/shard_map/ppermute | solution.py:316
  131.4 4.1 %copy-start.5 = (bf16[4,128,1024]{2,1,0:T(8,128)(2,1)S(1)}, bf16[4,128,1024]{2,1,0:T(8,128)(2,1)}, u32[]{:S(2)}) copy-start(bf16[4,128,1024]{2,1,0:T(8,128)(2,1)} %copy.32) | copy-start | bytes 3145732
  135.3 9.1 %collective-permute-start.16 = (bf16[256,512]{1,0:T(8,128)(2,1)S(1)}, bf16[256,512]{1,0:T(8,128)(2,1)S(1)}, u32[]{:S(2)}, u32[]{:S(2)}) collective-permute-start(bf16[256,512]{1,0:T(8,128)(2,1)S(1)} %get-tuple-element.98.attended_ref), channel_id=1, source_target_pairs={{0,1},{1,2},{2,3},{3,0},{4,5},{5,6},{6,7},{7,4},{8,9},{9,10},{10,1... | collective-permute-start | bytes 786440 | tf_op jit(solution)/shard_map/ppermute | solution.py:316
  144.4 11.0 %collective-permute-start.17 = (bf16[256,512]{1,0:T(8,128)(2,1)S(1)}, bf16[256,512]{1,0:T(8,128)(2,1)S(1)}, u32[]{:S(2)}, u32[]{:S(2)}) collective-permute-start(bf16[256,512]{1,0:T(8,128)(2,1)S(1)} %collective-permute-done.16.attended_ref), channel_id=1, source_target_pairs={{0,1},{1,2},{2,3},{3,0},{4,5},{5,6},{6,7},{7,4},{8,9},{9,10},{10,1... | collective-permute-start | bytes 786440 | tf_op jit(solution)/shard_map/ppermute | solution.py:316
  146.5 14.6 %collective-permute-start.19 = (bf16[256,512]{1,0:T(8,128)(2,1)S(1)}, bf16[256,512]{1,0:T(8,128)(2,1)S(1)}, u32[]{:S(2)}, u32[]{:S(2)}) collective-permute-start(bf16[256,512]{1,0:T(8,128)(2,1)S(1)} %collective-permute-done.15.attended_ref), channel_id=1, source_target_pairs={{0,1},{1,2},{2,3},{3,0},{4,5},{5,6},{6,7},{7,4},{8,9},{9,10},{10,1... | collective-permute-start | bytes 786440 | tf_op jit(solution)/shard_map/ppermute | solution.py:316
  155.5 11.2 %collective-permute-start.18 = (bf16[256,512]{1,0:T(8,128)(2,1)S(1)}, bf16[256,512]{1,0:T(8,128)(2,1)S(1)}, u32[]{:S(2)}, u32[]{:S(2)}) collective-permute-start(bf16[256,512]{1,0:T(8,128)(2,1)S(1)} %collective-permute-done.17.attended_ref), channel_id=1, source_target_pairs={{0,1},{1,2},{2,3},{3,0},{4,5},{5,6},{6,7},{7,4},{8,9},{9,10},{10,1... | collective-permute-start | bytes 786440 | tf_op jit(solution)/shard_map/ppermute | solution.py:316
  161.1 8.3 %collective-permute-start.20 = (bf16[256,512]{1,0:T(8,128)(2,1)S(1)}, bf16[256,512]{1,0:T(8,128)(2,1)S(1)}, u32[]{:S(2)}, u32[]{:S(2)}) collective-permute-start(bf16[256,512]{1,0:T(8,128)(2,1)S(1)} %collective-permute-done.19.attended_ref), channel_id=1, source_target_pairs={{0,1},{1,2},{2,3},{3,0},{4,5},{5,6},{6,7},{7,4},{8,9},{9,10},{10,1... | collective-permute-start | bytes 786440 | tf_op jit(solution)/shard_map/ppermute | solution.py:316
  (7 other events, 14.2 us)
Sparse Core Ops, SparseCore 0:
  12.0 19.8 all-gather.5
  41.2 42.1 all-gather.7

commit v11 on v10

--- a/solution.py
+++ b/solution.py
@@ -362,14 +362,9 @@
         for k in range(1, planes)
     ]
 
+    held[0][1], held[1][0], sends = lax.optimization_barrier((held[0][1], held[1][0], sends))
     lines = [turned(send, k) for k, send in enumerate(sends, 1)]
-    begun = project(planes_of[:1], tokens, weight)
-
-    done = lax.optimization_barrier(
-        (held[0][1], held[1][0], lines, begun, table, turn, up_all, own_rows)
-    )
-    held[0][1], held[1][0], lines, begun, table, turn, up_all, own_rows = done
-    lines = lax.all_gather(jnp.stack(lines), PLANE, axis=0)
+    begun = project(planes_of[:1], after(tokens, held[0][1]), weight)
     begun = [begun, begun]
     for step in range(2, planes):
         for part in range(2):
@@ -382,6 +377,7 @@
         if step == 2:
             sums = shrink_partial(adapters, here, planes, table, after(tokens, held[0][1]), down_all)
             side = [sums[0]] + [turned(sums[k], k) for k in range(1, planes)]
+            side = (side, lines, table, turn, up_all, own_rows)
         elif step == 3:
             shrink = sum(side[1:], side[0]).astype(jnp.bfloat16)
             out_up = after(output_up_maps, held[0][2])
@@ -393,6 +389,9 @@
         held[0][-1], held[1][-1], begun, side = lax.optimization_barrier(
             (held[0][-1], held[1][-1], begun, side)
         )
+        if step == 2:
+            side, lines, table, turn, up_all, own_rows = side
+            lines = lax.all_gather(jnp.stack(lines), PLANE, axis=0)
     shrink, out_up_all, own_down = side[:planes], side[-2], side[-1]
     held[1].append(turned(held[1][-1]))
     begun[1] = project(
@@ -406,8 +405,7 @@
             planes_of, adapters, part, table, turn, up_all, shrink, held[part][-1], weight,
             begun[part], earlier,
         )
-        attended[part] = [made, turned(made)]
-        earlier = [after(array, attended[part][1]) for array in earlier]
+        attended[part] = [made, turned(after(made, *attended[0][1:]))]
     sums = [
         project_out(ids, rank, attended[part][0], own_rows, own_down, [], []) for part in range(2)
     ]
@@ -416,7 +414,8 @@
         for part in range(2):
             arrived = after(attended[part][-1], *sums[part])
             if step < planes:
-                attended[part].append(turned(arrived))
+                ahead = attended[0][step:]
+                attended[part].append(turned(after(arrived, *ahead)))
             final = [] if step < planes else [table, out_up_all, *before]
             sums[part] = project_out(
                 ids, rank, arrived, lines, pool, list(sums[part]), final, step - 1, part

time: 180 us -> 195 us (1.083)
  local copies, waits for them, and re-layouts: 21.7 us -> 42.5 us
  waiting for transfers between devices: 60.9 us -> 41.1 us
  starting transfers between devices: 28.8 us -> 33.9 us
  other arithmetic: 4.8 us -> 8.02 us
  blocking collectives: 20 us -> 23 us
    ppermute x21, waiting for transfers between devices: 60.8 us -> 41.1 us  [turned(): lax.ppermute(value, 'tensor', [(i, (i + turn) % planes) for i in range(pl...]
    unnamed x34 -> x94, local copies, waits for them, and re-layouts: 12 us -> 29.7 us
    ppermute x21, starting transfers between devices: 28.8 us -> 33.9 us  [turned(): lax.ppermute(value, 'tensor', [(i, (i + turn) % planes) for i in range(pl...]
    all_gather x1, blocking collectives: 7.16 us -> 10.2 us  [local(): lax.all_gather(out_up, 'dp', axis=0, tiled=True)]
    transpose x2, local copies, waits for them, and re-layouts: 2.88 us -> 5.3 us  [local(): jnp.transpose(lax.dynamic_slice_in_dim(output_weight, here * columns, col...]
  transfers between devices with their start and end apart: 23 -> 23, of which waited for: 12 -> 8; matrix products, arithmetic and copies ran while one was open for 7% -> 9% of each run, Pallas kernels for 15% -> 15%
where the time goes in v11:
time: 195 us; the launch traced here: 194 us
  local copies, waits for them, and re-layouts  42.5 us (22%)
  waiting for transfers between devices  41.1 us (21%)
  starting transfers between devices  33.9 us (17%)
  Pallas kernels  31 us (16%)
  blocking collectives  23 us (12%)
  between operations  14 us (7%)
  other arithmetic  8.02 us (4%)
    ppermute x21, waiting for transfers between devices, turned(): lax.ppermute(value, 'tensor', [(i, (i + turn) % planes) for i in range(pl...  41.1 us
    ppermute x21, starting transfers between devices, turned(): lax.ppermute(value, 'tensor', [(i, (i + turn) % planes) for i in range(pl...  33.9 us
    pallas_call x16, Pallas kernels, call(): pl.pallas_call(kernel, out_shape=out, grid_spec=pltpu.PrefetchScalarGridS...  31 us
    unnamed x94, local copies, waits for them, and re-layouts  29.7 us
    all_gather x1, blocking collectives, local(): lax.all_gather(out_up, 'dp', axis=0, tiled=True)  10.2 us
    all_gather x1, blocking collectives, local(): lax.all_gather(jnp.transpose(adapter_up_maps[0], (1, 0, 2)), 'dp', axis=0)  6.66 us
    all_gather x1, blocking collectives, local(): lax.all_gather(own_down, 'dp', axis=0)  6.06 us
    transpose x2, local copies, waits for them, and re-layouts, local(): jnp.transpose(lax.dynamic_slice_in_dim(output_weight, here * columns, col...  5.3 us
  transfers between devices with their start and end apart: 23, of which 8 were waited for; matrix products, arithmetic and copies ran while one was open for 9% of the time, Pallas kernels for 15%

profile of v11, /device:TPU:0, one launch (start us, length us, event | category | flops | bytes accessed | tf_op | source)
XLA Modules:
  0.0 193.5 jit_solution(4834458881915393035)
XLA Ops:
  6.5 2.1 %fusion.5 = (bf16[256,1024]{1,0:T(8,128)(2,1)}, bf16[256,1024]{1,0:T(8,128)(2,1)S(1)}) fusion(bf16[512,1024]{1,0:T(8,128)(2,1)} %token_ref), kind=kLoop, calls=%fused_computation.33 | loop fusion | bytes 2097152 | tf_op jit(solution)/shard_map/slice | solution.py:319
  8.7 3.0 %collective-permute-start = (bf16[256,1024]{1,0:T(8,128)(2,1)S(1)}, bf16[256,1024]{1,0:T(8,128)(2,1)}, u32[]{:S(2)}, u32[]{:S(2)}) collective-permute-start(bf16[256,1024]{1,0:T(8,128)(2,1)S(1)} %get-tuple-element.133), channel_id=1, source_target_pairs={{0,1},{1,2},{2,3},{3,0},{4,5},{5,6},{6,7},{7,4},{8,9},{9,10},{10,1... | collective-permute-start | bytes 1572872 | tf_op jit(solution)/shard_map/ppermute | solution.py:316
  15.4 2.8 %fusion.4 = (bf16[64,1,1024]{2,1,0:T(2,128)(2,1)S(1)}, bf16[64,1,1024]{2,1,0:T(2,128)(2,1)S(1)}, bf16[64,1,1024]{2,1,0:T(2,128)(2,1)S(1)}) fusion(bf16[128,4,4096]{2,1,0:T(4,128)(2,1)} %param.11, s32[]{:T(128)S(6)} %select_n.64, s32[]{:T(128)S(6)} %select_n.67, s32[]{:T(128)S(6)} %select_n.76, s32[]{:T(128)S(6)} %select_n.73, s32[]{:T(128)S(6)} %select_n.70), kind=kLoop, calls=%fused_computation.32 | loop fusion | bytes 786452 | tf_op jit(solution)/shard_map/dynamic_slice | solution.py:358
  20.4 5.4 %collective-permute-done.refs_0_ = bf16[256,1024]{1,0:T(8,128)(2,1)} collective-permute-done((bf16[256,1024]{1,0:T(8,128)(2,1)S(1)}, bf16[256,1024]{1,0:T(8,128)(2,1)}, u32[]{:S(2)}, u32[]{:S(2)}) %collective-permute-start) | collective-permute-done | bytes 524320 | tf_op jit(solution)/shard_map/ppermute | solution.py:316
  27.1 2.6 %dynamic-slice_bitcast_fusion = bf16[4,128,1024]{2,0,1:T(4,128)(2,1)} fusion(bf16[128,4,4096]{2,1,0:T(4,128)(2,1)} %param.11, s32[]{:T(128)S(6)} %select_n.78), kind=kLoop, calls=%fused_computation | loop fusion | bytes 2097156 | tf_op jit(solution)/shard_map/transpose | solution.py:343
  32.7 2.9 %collective-permute-start.8 = (bf16[96,1024]{1,0:T(8,128)(2,1)}, bf16[96,1024]{1,0:T(8,128)(2,1)}, u32[]{:S(2)}, u32[]{:S(2)}) collective-permute-start(bf16[96,1024]{1,0:T(8,128)(2,1)} %get-tuple-element.76), channel_id=1, source_target_pairs={{0,3},{1,0},{2,1},{3,2},{4,7},{5,4},{6,5},{7,6},{8,11},{9,8},{10,9... | collective-permute-start | bytes 589832 | tf_op jit(solution)/shard_map/ppermute | solution.py:316
  36.6 2.7 %copy.33 = bf16[4,128,1024]{2,1,0:T(8,128)(2,1)} copy(bf16[4,128,1024]{2,0,1:T(4,128)(2,1)} %dynamic-slice_bitcast_fusion) | data formatting | bytes 2097152 | tf_op jit(solution)/shard_map/transpose | solution.py:343
  39.3 6.7 %all-gather = bf16[24,64,128]{2,1,0:T(8,128)(2,1)S(1)} all-gather(bf16[6,64,128]{2,1,0:T(8,128)(2,1)} %bitcast.68), channel_id=2, replica_groups=mesh['groups'=2,'dp'=4,'tensor'=4] {'dp'}, dimensions={0}, use_global_device_ids=true | all-gather | bytes 491520 | tf_op jit(solution)/shard_map/all_gather | solution.py:323
  48.4 2.7 %shrink.1 = (f32[128,192]{1,0:T(8,128)S(1)}, f32[128,192]{1,0:T(8,128)S(1)}, f32[128,192]{1,0:T(8,128)S(1)}, f32[128,192]{1,0:T(8,128)S(1)}) custom-call(s32[5]{0:T(128)S(1)} %pad_add_fusion.3.ids_ref, s32[512,2]{1,0:T(8,128)S(1)} %copy-done.15, bf16[512,1024]{1,0:T(8,128)(2,1)S(1)} %copy-done.7, bf16[4,192,1024]{2,1,0:T(8,128)(2,1)S(1)} %copy-done.14), custom_call_target="tpu_custom_call" | custom-call | bytes 7876608 | tf_op jit(solution)/shard_map/shrink/pallas_call | solution.py:26
  51.7 6.6 %collective-permute-done.6 = bf16[96,1024]{1,0:T(8,128)(2,1)} collective-permute-done((bf16[96,1024]{1,0:T(8,128)(2,1)}, bf16[96,1024]{1,0:T(8,128)(2,1)}, u32[]{:S(2)}, u32[]{:S(2)}) %collective-permute-start.6) | collective-permute-done | bytes 196640 | tf_op jit(solution)/shard_map/ppermute | solution.py:316
  58.3 4.6 %collective-permute-start.3 = (f32[128,192]{1,0:T(8,128)S(1)}, f32[128,192]{1,0:T(8,128)}, u32[]{:S(2)}, u32[]{:S(2)}) collective-permute-start(f32[128,192]{1,0:T(8,128)S(1)} %get-tuple-element.71), channel_id=1, source_target_pairs={{0,1},{1,2},{2,3},{3,0},{4,5},{5,6},{6,7},{7,4},{8,9},{9,10},{10,1... | collective-permute-start | bytes 294920 | tf_op jit(solution)/shard_map/ppermute | solution.py:316
  62.9 3.5 %collective-permute-done.7 = bf16[96,1024]{1,0:T(8,128)(2,1)} collective-permute-done((bf16[96,1024]{1,0:T(8,128)(2,1)}, bf16[96,1024]{1,0:T(8,128)(2,1)}, u32[]{:S(2)}, u32[]{:S(2)}) %collective-permute-start.7) | collective-permute-done | bytes 196640 | tf_op jit(solution)/shard_map/ppermute | solution.py:316
  66.4 3.7 %collective-permute-start.5 = (f32[128,192]{1,0:T(8,128)S(1)}, f32[128,192]{1,0:T(8,128)S(1)}, u32[]{:S(2)}, u32[]{:S(2)}) collective-permute-start(f32[128,192]{1,0:T(8,128)S(1)} %get-tuple-element.73), channel_id=1, source_target_pairs={{0,3},{1,0},{2,1},{3,2},{4,7},{5,4},{6,5},{7,6},{8,11},{9,8},{10,9... | collective-permute-start | bytes 294920 | tf_op jit(solution)/shard_map/ppermute | solution.py:316
  70.7 2.8 %copy-done.2 = bf16[4096,6,128]{2,0,1:T(8,128)(2,1)S(1)} copy-done((bf16[4096,6,128]{2,0,1:T(8,128)(2,1)S(1)}, bf16[4096,6,128]{2,0,1:T(8,128)(2,1)}, u32[]{:S(2)}) %copy-start.2) | copy-done | bytes 6291480
  75.7 2.3 %project.6.refs_2_ = f32[256,768]{1,0:T(8,128)S(1)} custom-call(s32[1]{0:T(128)} %get-tuple-element.144.ids_ref, bf16[256,1024]{1,0:T(8,128)(2,1)} %collective-permute-done.refs_0_, bf16[6,4096,128]{2,1,0:T(8,128)(2,1)S(1)} %bitcast.51, f32[512,768]{1,0:T(8,128)S(1)} %project.5.refs_2_), custom_call_target="tpu_custom_call" | custom-call | bytes 25165824 | tf_op jit(solution)/shard_map/project/pallas_call | solution.py:26
  83.0 3.9 %collective-permute-start.9 = (bf16[256,1024]{1,0:T(8,128)(2,1)}, bf16[256,1024]{1,0:T(8,128)(2,1)S(1)}, u32[]{:S(2)}, u32[]{:S(2)}) collective-permute-start(bf16[256,1024]{1,0:T(8,128)(2,1)} %collective-permute-done.1.refs_0_), channel_id=1, source_target_pairs={{0,1},{1,2},{2,3},{3,0},{4,5},{5,6},{6,7},{7,4},{8,9},{9,10},{10,1... | collective-permute-start | bytes 1572872 | tf_op jit(solution)/shard_map/ppermute | solution.py:316
  90.1 2.3 %collective-permute-start.12 = (bf16[128,192]{1,0:T(8,128)(2,1)S(1)}, bf16[128,192]{1,0:T(8,128)(2,1)S(1)}, u32[]{:S(2)}, u32[]{:S(2)}) collective-permute-start(bf16[128,192]{1,0:T(8,128)(2,1)S(1)} %add_convert_fusion.refs_0_), channel_id=1, source_target_pairs={{0,2},{1,3},{2,0},{3,1},{4,6},{5,7},{6,4},{7,5},{8,10},{9,11},{10,... | collective-permute-start | bytes 147464 | tf_op jit(solution)/shard_map/ppermute | solution.py:316
  93.9 10.2 %all_gather.27.refs_3_ = bf16[4,64,1024]{2,1,0:T(8,128)(2,1)S(1)} all-gather(bf16[1,64,1024]{2,1,0:T(8,128)(2,1)S(1)} %copy-done.39), channel_id=1, replica_groups=mesh['groups'=2,'dp'=4,'tensor'=4] {'dp'}, dimensions={0}, use_global_device_ids=true | all-gather | bytes 655360 | tf_op jit(solution)/shard_map/all_gather | solution.py:386
  104.1 6.1 %all-gather.1 = bf16[128,1024]{1,0:T(8,128)(2,1)S(1)} all-gather(bf16[32,1024]{1,0:T(8,128)(2,1)} %copy-done.38), channel_id=3, replica_groups=mesh['groups'=2,'dp'=4,'tensor'=4] {'dp'}, dimensions={0}, use_global_device_ids=true | all-gather | bytes 327680 | tf_op jit(solution)/shard_map/all_gather | solution.py:387
  110.2 2.8 %copy-done.3 = bf16[4096,6,128]{2,0,1:T(8,128)(2,1)S(1)} copy-done((bf16[4096,6,128]{2,0,1:T(8,128)(2,1)S(1)}, bf16[4096,6,128]{2,0,1:T(8,128)(2,1)}, u32[]{:S(2)}) %copy-start.3) | copy-done | bytes 6291480
  113.0 2.3 %project.8.refs_2_ = f32[256,768]{1,0:T(8,128)S(1)} custom-call(s32[1]{0:T(128)} %get-tuple-element.144.ids_ref, bf16[256,1024]{1,0:T(8,128)(2,1)} %collective-permute-done.2.refs_0_, bf16[6,4096,128]{2,1,0:T(8,128)(2,1)S(1)} %bitcast.52, f32[512,768]{1,0:T(8,128)S(1)} %copy-done.6), custom_call_target="tpu_custom_call" | custom-call | bytes 25165824 | tf_op jit(solution)/shard_map/project/pallas_call | solution.py:26
  116.1 2.3 %project.7.refs_6_ = f32[256,768]{1,0:T(8,128)S(1)} custom-call(s32[1]{0:T(128)} %get-tuple-element.142.ids_ref, bf16[256,1024]{1,0:T(8,128)(2,1)} %collective-permute-done.1.refs_0_, bf16[6,4096,128]{2,1,0:T(8,128)(2,1)S(1)} %bitcast.53, f32[256,768]{1,0:T(8,128)S(1)} %project.6.refs_2_), custom_call_target="tpu_custom_call" | custom-call | bytes 22806528 | tf_op jit(solution)/shard_map/project/pallas_call | solution.py:26
  123.5 2.9 %copy-done.4 = bf16[4096,6,128]{2,0,1:T(8,128)(2,1)S(1)} copy-done((bf16[4096,6,128]{2,0,1:T(8,128)(2,1)S(1)}, bf16[4096,6,128]{2,0,1:T(8,128)(2,1)}, u32[]{:S(2)}) %copy-start.4) | copy-done | bytes 6291480
  131.9 3.2 %attend.2 = (bf16[256,512]{1,0:T(8,128)(2,1)S(1)}, bf16[256,128]{1,0:T(8,128)(2,1)S(1)}, bf16[256,128]{1,0:T(8,128)(2,1)S(1)}) custom-call(s32[8]{0:T(128)S(1)} %pad_add_fusion.2.ids_ref, s32[512,2]{1,0:T(8,128)S(1)} %copy.35.table_ref.refs_2_, f32[512,256]{1,0:T(8,128)S(1)} %copy-done.9, bf16[4,6,64,128]{3,2,1,0:T(8,128)(2,1)S(1)} %bitcast.61, ...), custom_call_target="tpu_custom_call" | custom-call | bytes 26161152 | tf_op jit(solution)/shard_map/attend/pallas_call | solution.py:26
  137.3 2.6 %project.9.refs_6_ = f32[256,768]{1,0:T(8,128)S(1)} custom-call(s32[1]{0:T(128)} %get-tuple-element.142.ids_ref, bf16[256,1024]{1,0:T(8,128)(2,1)} %collective-permute-done.10.refs_0_, bf16[6,4096,128]{2,1,0:T(8,128)(2,1)S(1)} %bitcast.55, f32[256,768]{1,0:T(8,128)S(1)} %copy-done.11), custom_call_target="tpu_custom_call" | custom-call | bytes 22806528 | tf_op jit(solution)/shard_map/project/pallas_call | solution.py:26
  141.7 3.8 %attend.3 = (bf16[256,512]{1,0:T(8,128)(2,1)S(1)}, bf16[256,128]{1,0:T(8,128)(2,1)}, bf16[256,128]{1,0:T(8,128)(2,1)}) custom-call(s32[8]{0:T(128)S(1)} %pad_add_fusion.2.ids_ref, s32[512,2]{1,0:T(8,128)S(1)} %copy.35.table_ref.refs_2_, f32[512,256]{1,0:T(8,128)S(1)} %copy-done.9, bf16[4,6,64,128]{3,2,1,0:T(8,128)(2,1)S(1)} %bitcast.62, ...), custom_call_target="tpu_custom_call" | custom-call | bytes 26554368 | tf_op jit(solution)/shard_map/attend/pallas_call | solution.py:26
  148.6 8.1 %collective-permute-done.16.attended_ref = bf16[256,512]{1,0:T(8,128)(2,1)S(1)} collective-permute-done((bf16[256,512]{1,0:T(8,128)(2,1)S(1)}, bf16[256,512]{1,0:T(8,128)(2,1)S(1)}, u32[]{:S(2)}, u32[]{:S(2)}) %collective-permute-start.16) | collective-permute-done | bytes 262176 | tf_op jit(solution)/shard_map/ppermute | solution.py:316
  156.7 4.2 %collective-permute-done.17.attended_ref = bf16[256,512]{1,0:T(8,128)(2,1)S(1)} collective-permute-done((bf16[256,512]{1,0:T(8,128)(2,1)S(1)}, bf16[256,512]{1,0:T(8,128)(2,1)S(1)}, u32[]{:S(2)}, u32[]{:S(2)}) %collective-permute-start.17) | collective-permute-done | bytes 262176 | tf_op jit(solution)/shard_map/ppermute | solution.py:316
  160.9 2.3 %copy-done = bf16[24,96,1024]{2,1,0:T(8,128)(2,1)S(1)} copy-done((bf16[24,96,1024]{2,1,0:T(8,128)(2,1)S(1)}, bf16[24,96,1024]{2,1,0:T(8,128)(2,1)}, u32[]{:S(2)}) %copy-start) | copy-done | bytes 4718616
  169.8 6.5 %collective-permute-done.19.attended_ref = bf16[256,512]{1,0:T(8,128)(2,1)S(1)} collective-permute-done((bf16[256,512]{1,0:T(8,128)(2,1)S(1)}, bf16[256,512]{1,0:T(8,128)(2,1)S(1)}, u32[]{:S(2)}, u32[]{:S(2)}) %collective-permute-start.19) | collective-permute-done | bytes 262176 | tf_op jit(solution)/shard_map/ppermute | solution.py:316
  179.7 4.7 %collective-permute-done.20.attended_ref = bf16[256,512]{1,0:T(8,128)(2,1)S(1)} collective-permute-done((bf16[256,512]{1,0:T(8,128)(2,1)S(1)}, bf16[256,512]{1,0:T(8,128)(2,1)S(1)}, u32[]{:S(2)}, u32[]{:S(2)}) %collective-permute-start.20) | collective-permute-done | bytes 262176 | tf_op jit(solution)/shard_map/ppermute | solution.py:316
  184.4 2.3 %project_out.15 = bf16[512,1024]{1,0:T(8,128)(2,1)} custom-call(s32[5]{0:T(128)S(1)} %pad_add_fusion.1.ids_ref, bf16[256,512]{1,0:T(8,128)(2,1)S(1)} %collective-permute-done.20.attended_ref, bf16[8,3,96,1024]{3,2,1,0:T(8,128)(2,1)S(1)} %bitcast.46, bf16[8,3,96,1024]{3,2,1,0:T(8,128)(2,1)S(1)} %bitcast.47, f32[256,1024]{1,0:T(8,128)S(1)} %get-tuple-element.122.refs_0_, ...), custom_call_target="tpu_custom_call" | custom-call | bytes 36188160 | tf_op jit(solution)/shard_map/project_out/pallas_call | solution.py:26
  (160 shorter events, 54.7 us)
Async XLA Ops:
  6.5 39.5 %all-gather.6.cloned.1.call-start = ((), (), s32[]{:S(2)}) async-start(), calls=%async_computation | async-start | bytes 1966080 | tf_op jit(solution)/shard_map/all_gather | solution.py:322
  8.7 17.1 %collective-permute-start = (bf16[256,1024]{1,0:T(8,128)(2,1)S(1)}, bf16[256,1024]{1,0:T(8,128)(2,1)}, u32[]{:S(2)}, u32[]{:S(2)}) collective-permute-start(bf16[256,1024]{1,0:T(8,128)(2,1)S(1)} %get-tuple-element.133), channel_id=1, source_target_pairs={{0,1},{1,2},{2,3},{3,0},{4,5},{5,6},{6,7},{7,4},{8,9},{9,10},{10,1... | collective-permute-start | bytes 1572872 | tf_op jit(solution)/shard_map/ppermute | solution.py:316
  11.7 149.2 %all-gather.8.cloned.1.call-start = ((), (), s32[]{:S(2)}) async-start(), calls=%async_computation.1 | async-start | bytes 5308416 | tf_op jit(solution)/shard_map/all_gather | solution.py:394
  14.4 21.3 %copy-start.38 = (bf16[32,1024]{1,0:T(8,128)(2,1)}, bf16[32,1024]{1,0:T(8,128)(2,1)S(1)}, u32[]{:S(2)}) copy-start(bf16[32,1024]{1,0:T(8,128)(2,1)S(1)} %bitcast_dynamic-update-slice_fusion) | copy-start | bytes 196612
  18.3 27.7 %copy-start.7 = (bf16[512,1024]{1,0:T(8,128)(2,1)S(1)}, bf16[512,1024]{1,0:T(8,128)(2,1)}, u32[]{:S(2)}) copy-start(bf16[512,1024]{1,0:T(8,128)(2,1)} %token_ref) | copy-start | bytes 3145732
  25.7 52.4 %collective-permute-start.1 = (bf16[256,1024]{1,0:T(8,128)(2,1)}, bf16[256,1024]{1,0:T(8,128)(2,1)}, u32[]{:S(2)}, u32[]{:S(2)}) collective-permute-start(bf16[256,1024]{1,0:T(8,128)(2,1)} %collective-permute-done.refs_0_), channel_id=1, source_target_pairs={{0,1},{1,2},{2,3},{3,0},{4,5},{5,6},{6,7},{7,4},{8,9},{9,10},{10,1... | collective-permute-start | bytes 1572872 | tf_op jit(solution)/shard_map/ppermute | solution.py:316
  25.7 52.4 %collective-permute-start.2 = (bf16[256,1024]{1,0:T(8,128)(2,1)}, bf16[256,1024]{1,0:T(8,128)(2,1)}, u32[]{:S(2)}, u32[]{:S(2)}) collective-permute-start(bf16[256,1024]{1,0:T(8,128)(2,1)} %get-tuple-element.68), channel_id=1, source_target_pairs={{0,1},{1,2},{2,3},{3,0},{4,5},{5,6},{6,7},{7,4},{8,9},{9,10},{10,1... | collective-permute-start | bytes 1572872 | tf_op jit(solution)/shard_map/ppermute | solution.py:316
  29.6 28.7 %collective-permute-start.6 = (bf16[96,1024]{1,0:T(8,128)(2,1)}, bf16[96,1024]{1,0:T(8,128)(2,1)}, u32[]{:S(2)}, u32[]{:S(2)}) collective-permute-start(bf16[96,1024]{1,0:T(8,128)(2,1)} %get-tuple-element.74), channel_id=1, source_target_pairs={{0,1},{1,2},{2,3},{3,0},{4,5},{5,6},{6,7},{7,4},{8,9},{9,10},{10,1... | collective-permute-start | bytes 589832 | tf_op jit(solution)/shard_map/ppermute | solution.py:316
  31.2 35.2 %collective-permute-start.7 = (bf16[96,1024]{1,0:T(8,128)(2,1)}, bf16[96,1024]{1,0:T(8,128)(2,1)}, u32[]{:S(2)}, u32[]{:S(2)}) collective-permute-start(bf16[96,1024]{1,0:T(8,128)(2,1)} %get-tuple-element.75), channel_id=1, source_target_pairs={{0,2},{1,3},{2,0},{3,1},{4,6},{5,7},{6,4},{7,5},{8,10},{9,11},{10,... | collective-permute-start | bytes 589832 | tf_op jit(solution)/shard_map/ppermute | solution.py:316
  32.7 33.7 %collective-permute-start.8 = (bf16[96,1024]{1,0:T(8,128)(2,1)}, bf16[96,1024]{1,0:T(8,128)(2,1)}, u32[]{:S(2)}, u32[]{:S(2)}) collective-permute-start(bf16[96,1024]{1,0:T(8,128)(2,1)} %get-tuple-element.76), channel_id=1, source_target_pairs={{0,3},{1,0},{2,1},{3,2},{4,7},{5,4},{6,5},{7,6},{8,11},{9,8},{10,9... | collective-permute-start | bytes 589832 | tf_op jit(solution)/shard_map/ppermute | solution.py:316
  36.6 38.8 %slice-start = ((s8[6291456]{0:T(1024)(128)(4,1)}), s8[2097152]{0:T(1024)(128)(4,1)S(1)}, s32[]{:S(2)}) async-start(s8[6291456]{0:T(1024)(128)(4,1)} %bitcast.49), calls=%async_computation.2 | async-start | bytes 4194304
  58.3 19.8 %collective-permute-start.3 = (f32[128,192]{1,0:T(8,128)S(1)}, f32[128,192]{1,0:T(8,128)}, u32[]{:S(2)}, u32[]{:S(2)}) collective-permute-start(f32[128,192]{1,0:T(8,128)S(1)} %get-tuple-element.71), channel_id=1, source_target_pairs={{0,1},{1,2},{2,3},{3,0},{4,5},{5,6},{6,7},{7,4},{8,9},{9,10},{10,1... | collective-permute-start | bytes 294920 | tf_op jit(solution)/shard_map/ppermute | solution.py:316
  66.4 11.7 %collective-permute-start.4 = (f32[128,192]{1,0:T(8,128)S(1)}, f32[128,192]{1,0:T(8,128)S(1)}, u32[]{:S(2)}, u32[]{:S(2)}) collective-permute-start(f32[128,192]{1,0:T(8,128)S(1)} %get-tuple-element.72), channel_id=1, source_target_pairs={{0,2},{1,3},{2,0},{3,1},{4,6},{5,7},{6,4},{7,5},{8,10},{9,11},{10,... | collective-permute-start | bytes 294920 | tf_op jit(solution)/shard_map/ppermute | solution.py:316
  66.4 13.8 %collective-permute-start.5 = (f32[128,192]{1,0:T(8,128)S(1)}, f32[128,192]{1,0:T(8,128)S(1)}, u32[]{:S(2)}, u32[]{:S(2)}) collective-permute-start(f32[128,192]{1,0:T(8,128)S(1)} %get-tuple-element.73), channel_id=1, source_target_pairs={{0,3},{1,0},{2,1},{3,2},{4,7},{5,4},{6,5},{7,6},{8,11},{9,8},{10,9... | collective-permute-start | bytes 294920 | tf_op jit(solution)/shard_map/ppermute | solution.py:316
  75.7 13.2 %copy-start.37 = (f32[128,192]{1,0:T(8,128)S(1)}, f32[128,192]{1,0:T(8,128)}, u32[]{:S(2)}) copy-start(f32[128,192]{1,0:T(8,128)} %copy-done.36) | copy-start | bytes 294916
  75.7 18.1 %copy-start.39 = (bf16[1,64,1024]{2,1,0:T(8,128)(2,1)S(1)}, bf16[1,64,1024]{2,1,0:T(8,128)(2,1)}, u32[]{:S(2)}) copy-start(bf16[1,64,1024]{2,1,0:T(8,128)(2,1)} %param.15) | copy-start | bytes 393220
  78.1 32.1 %copy-start.6 = (f32[512,768]{1,0:T(8,128)S(1)}, f32[512,768]{1,0:T(8,128)}, u32[]{:S(2)}) copy-start(f32[512,768]{1,0:T(8,128)} %copy-done.5) | copy-start | bytes 4718596
  83.0 38.2 %collective-permute-start.9 = (bf16[256,1024]{1,0:T(8,128)(2,1)}, bf16[256,1024]{1,0:T(8,128)(2,1)S(1)}, u32[]{:S(2)}, u32[]{:S(2)}) collective-permute-start(bf16[256,1024]{1,0:T(8,128)(2,1)} %collective-permute-done.1.refs_0_), channel_id=1, source_target_pairs={{0,1},{1,2},{2,3},{3,0},{4,5},{5,6},{6,7},{7,4},{8,9},{9,10},{10,1... | collective-permute-start | bytes 1572872 | tf_op jit(solution)/shard_map/ppermute | solution.py:316
  86.9 35.1 %collective-permute-start.10 = (bf16[256,1024]{1,0:T(8,128)(2,1)}, bf16[256,1024]{1,0:T(8,128)(2,1)}, u32[]{:S(2)}, u32[]{:S(2)}) collective-permute-start(bf16[256,1024]{1,0:T(8,128)(2,1)} %collective-permute-done.2.refs_0_), channel_id=1, source_target_pairs={{0,1},{1,2},{2,3},{3,0},{4,5},{5,6},{6,7},{7,4},{8,9},{9,10},{10,1... | collective-permute-start | bytes 1572872 | tf_op jit(solution)/shard_map/ppermute | solution.py:316
  90.0 25.3 %copy-start.18 = (bf16[128,192]{1,0:T(8,128)(2,1)}, bf16[128,192]{1,0:T(8,128)(2,1)S(1)}, u32[]{:S(2)}) copy-start(bf16[128,192]{1,0:T(8,128)(2,1)S(1)} %add_convert_fusion.refs_0_) | copy-start | bytes 147460
  90.0 29.3 %collective-permute-start.11 = (bf16[128,192]{1,0:T(8,128)(2,1)S(1)}, bf16[128,192]{1,0:T(8,128)(2,1)S(1)}, u32[]{:S(2)}, u32[]{:S(2)}) collective-permute-start(bf16[128,192]{1,0:T(8,128)(2,1)S(1)} %add_convert_fusion.refs_0_), channel_id=1, source_target_pairs={{0,1},{1,2},{2,3},{3,0},{4,5},{5,6},{6,7},{7,4},{8,9},{9,10},{10,1... | collective-permute-start | bytes 147464 | tf_op jit(solution)/shard_map/ppermute | solution.py:316
  90.1 29.9 %collective-permute-start.12 = (bf16[128,192]{1,0:T(8,128)(2,1)S(1)}, bf16[128,192]{1,0:T(8,128)(2,1)S(1)}, u32[]{:S(2)}, u32[]{:S(2)}) collective-permute-start(bf16[128,192]{1,0:T(8,128)(2,1)S(1)} %add_convert_fusion.refs_0_), channel_id=1, source_target_pairs={{0,2},{1,3},{2,0},{3,1},{4,6},{5,7},{6,4},{7,5},{8,10},{9,11},{10,... | collective-permute-start | bytes 147464 | tf_op jit(solution)/shard_map/ppermute | solution.py:316
  92.4 28.2 %collective-permute-start.13 = (bf16[128,192]{1,0:T(8,128)(2,1)S(1)}, bf16[128,192]{1,0:T(8,128)(2,1)S(1)}, u32[]{:S(2)}, u32[]{:S(2)}) collective-permute-start(bf16[128,192]{1,0:T(8,128)(2,1)S(1)} %add_convert_fusion.refs_0_), channel_id=1, source_target_pairs={{0,3},{1,0},{2,1},{3,2},{4,7},{5,4},{6,5},{7,6},{8,11},{9,8},{10,9... | collective-permute-start | bytes 147464 | tf_op jit(solution)/shard_map/ppermute | solution.py:316
  116.1 7.3 %copy-start.9 = (f32[512,256]{1,0:T(8,128)S(1)}, f32[512,256]{1,0:T(8,128)}, u32[]{:S(2)}) copy-start(f32[512,256]{1,0:T(8,128)} %pad_maximum_fusion.1.turn_ref) | copy-start | bytes 1572868
  122.0 19.6 %collective-permute-start.14 = (bf16[256,1024]{1,0:T(8,128)(2,1)}, bf16[256,1024]{1,0:T(8,128)(2,1)S(1)}, u32[]{:S(2)}, u32[]{:S(2)}) collective-permute-start(bf16[256,1024]{1,0:T(8,128)(2,1)} %collective-permute-done.10.refs_0_), channel_id=1, source_target_pairs={{0,1},{1,2},{2,3},{3,0},{4,5},{5,6},{6,7},{7,4},{8,9},{9,10},{10,1... | collective-permute-start | bytes 1572872 | tf_op jit(solution)/shard_map/ppermute | solution.py:316
  131.9 9.8 %slice-start.2 = ((s8[6291456]{0:T(1024)(128)(4,1)}), s8[4194304]{0:T(1024)(128)(4,1)S(1)}, s32[]{:S(2)}) async-start(s8[6291456]{0:T(1024)(128)(4,1)} %bitcast.56), calls=%async_computation.4 | async-start | bytes 8388608
  135.0 10.5 %collective-permute-start.15 = (bf16[256,512]{1,0:T(8,128)(2,1)S(1)}, bf16[256,512]{1,0:T(8,128)(2,1)S(1)}, u32[]{:S(2)}, u32[]{:S(2)}) collective-permute-start(bf16[256,512]{1,0:T(8,128)(2,1)S(1)} %get-tuple-element.101.attended_ref), channel_id=1, source_target_pairs={{0,1},{1,2},{2,3},{3,0},{4,5},{5,6},{6,7},{7,4},{8,9},{9,10},{10,1... | collective-permute-start | bytes 786440 | tf_op jit(solution)/shard_map/ppermute | solution.py:316
  145.6 11.1 %collective-permute-start.16 = (bf16[256,512]{1,0:T(8,128)(2,1)S(1)}, bf16[256,512]{1,0:T(8,128)(2,1)S(1)}, u32[]{:S(2)}, u32[]{:S(2)}) collective-permute-start(bf16[256,512]{1,0:T(8,128)(2,1)S(1)} %get-tuple-element.102.attended_ref), channel_id=1, source_target_pairs={{0,1},{1,2},{2,3},{3,0},{4,5},{5,6},{6,7},{7,4},{8,9},{9,10},{10,1... | collective-permute-start | bytes 786440 | tf_op jit(solution)/shard_map/ppermute | solution.py:316
  145.7 15.2 %collective-permute-start.17 = (bf16[256,512]{1,0:T(8,128)(2,1)S(1)}, bf16[256,512]{1,0:T(8,128)(2,1)S(1)}, u32[]{:S(2)}, u32[]{:S(2)}) collective-permute-start(bf16[256,512]{1,0:T(8,128)(2,1)S(1)} %collective-permute-done.15.attended_ref), channel_id=1, source_target_pairs={{0,1},{1,2},{2,3},{3,0},{4,5},{5,6},{6,7},{7,4},{8,9},{9,10},{10,1... | collective-permute-start | bytes 786440 | tf_op jit(solution)/shard_map/ppermute | solution.py:316
  160.9 8.9 %collective-permute-start.18 = (bf16[256,512]{1,0:T(8,128)(2,1)S(1)}, bf16[256,512]{1,0:T(8,128)(2,1)S(1)}, u32[]{:S(2)}, u32[]{:S(2)}) collective-permute-start(bf16[256,512]{1,0:T(8,128)(2,1)S(1)} %collective-permute-done.16.attended_ref), channel_id=1, source_target_pairs={{0,1},{1,2},{2,3},{3,0},{4,5},{5,6},{6,7},{7,4},{8,9},{9,10},{10,1... | collective-permute-start | bytes 786440 | tf_op jit(solution)/shard_map/ppermute | solution.py:316
  167.5 8.8 %collective-permute-start.19 = (bf16[256,512]{1,0:T(8,128)(2,1)S(1)}, bf16[256,512]{1,0:T(8,128)(2,1)S(1)}, u32[]{:S(2)}, u32[]{:S(2)}) collective-permute-start(bf16[256,512]{1,0:T(8,128)(2,1)S(1)} %collective-permute-done.17.attended_ref), channel_id=1, source_target_pairs={{0,1},{1,2},{2,3},{3,0},{4,5},{5,6},{6,7},{7,4},{8,9},{9,10},{10,1... | collective-permute-start | bytes 786440 | tf_op jit(solution)/shard_map/ppermute | solution.py:316
  176.3 8.2 %collective-permute-start.20 = (bf16[256,512]{1,0:T(8,128)(2,1)S(1)}, bf16[256,512]{1,0:T(8,128)(2,1)S(1)}, u32[]{:S(2)}, u32[]{:S(2)}) collective-permute-start(bf16[256,512]{1,0:T(8,128)(2,1)S(1)} %collective-permute-done.18.attended_ref), channel_id=1, source_target_pairs={{0,1},{1,2},{2,3},{3,0},{4,5},{5,6},{6,7},{7,4},{8,9},{9,10},{10,1... | collective-permute-start | bytes 786440 | tf_op jit(solution)/shard_map/ppermute | solution.py:316
  (37 other events, 74.8 us)
Sparse Core Ops, SparseCore 0:
  11.8 19.9 all-gather.5
  83.1 43.2 all-gather.7

commit v12 on v10

--- a/solution.py
+++ b/solution.py
@@ -382,18 +382,20 @@
         if step == 2:
             sums = shrink_partial(adapters, here, planes, table, after(tokens, held[0][1]), down_all)
             side = [sums[0]] + [turned(sums[k], k) for k in range(1, planes)]
+            out_up_all = lax.all_gather(
+                after(output_up_maps, held[0][1]), "dp", axis=0, tiled=True
+            )
+            own_down = lax.all_gather(after(out_down, held[0][1]), "dp", axis=0)
+            side = (side, out_up_all, own_down)
         elif step == 3:
             shrink = sum(side[1:], side[0]).astype(jnp.bfloat16)
-            out_up = after(output_up_maps, held[0][2])
-            own_down = after(out_down, held[0][2])
-            side = [shrink] + [turned(shrink, k) for k in range(1, planes)] + [
-                lax.all_gather(out_up, "dp", axis=0, tiled=True),
-                lax.all_gather(own_down, "dp", axis=0),
-            ]
+            side = [shrink] + [turned(shrink, k) for k in range(1, planes)]
         held[0][-1], held[1][-1], begun, side = lax.optimization_barrier(
             (held[0][-1], held[1][-1], begun, side)
         )
-    shrink, out_up_all, own_down = side[:planes], side[-2], side[-1]
+        if step == 2:
+            side, out_up_all, own_down = side
+    shrink = side
     held[1].append(turned(held[1][-1]))
     begun[1] = project(
         planes_of[planes - 2 : planes - 1], held[1][planes - 2], weight, [begun[1]], 1
@@ -406,17 +408,17 @@
             planes_of, adapters, part, table, turn, up_all, shrink, held[part][-1], weight,
             begun[part], earlier,
         )
-        attended[part] = [made, turned(made)]
-        earlier = [after(array, attended[part][1]) for array in earlier]
+        attended[part] = [made, turned(after(made, *attended[0][1:]))]
     sums = [
         project_out(ids, rank, attended[part][0], own_rows, own_down, [], []) for part in range(2)
     ]
     before = []
     for step in range(2, planes + 1):
         for part in range(2):
-            arrived = after(attended[part][-1], *sums[part])
+            arrived = attended[part][-1]
             if step < planes:
-                attended[part].append(turned(arrived))
+                ahead = attended[0][step:]
+                attended[part].append(turned(after(arrived, *ahead)))
             final = [] if step < planes else [table, out_up_all, *before]
             sums[part] = project_out(
                 ids, rank, arrived, lines, pool, list(sums[part]), final, step - 1, part

time: 180 us -> 184 us (1.022)
  waiting for transfers between devices: 60.9 us -> 49.2 us
  local copies, waits for them, and re-layouts: 21.7 us -> 30.8 us
  blocking collectives: 20 us -> 25 us
    ppermute x21, waiting for transfers between devices: 60.8 us -> 49.2 us  [turned(): lax.ppermute(value, 'tensor', [(i, (i + turn) % planes) for i in range(pl...]
    unnamed x34 -> x56, local copies, waits for them, and re-layouts: 12 us -> 21.2 us
    all_gather x2, blocking collectives: 13.1 us -> 18.1 us  [the longest x1 10.6 us: local(): lax.all_gather(after(output_up_maps, held[0][1]), 'dp', axis=0, tiled=True)]
  transfers between devices with their start and end apart: 23 -> 23, of which waited for: 12 -> 8; matrix products, arithmetic and copies ran while one was open for 7% -> 7% of each run, Pallas kernels for 15% -> 15%
where the time goes in v12:
time: 184 us
  waiting for transfers between devices  49.2 us (27%)
  local copies, waits for them, and re-layouts  30.8 us (17%)
  Pallas kernels  30.8 us (17%)
  starting transfers between devices  29 us (16%)
  blocking collectives  25 us (14%)
  between operations  13.9 us (8%)
  other arithmetic  4.86 us (3%)
    ppermute x21, waiting for transfers between devices, turned(): lax.ppermute(value, 'tensor', [(i, (i + turn) % planes) for i in range(pl...  49.2 us
    pallas_call x16, Pallas kernels, call(): pl.pallas_call(kernel, out_shape=out, grid_spec=pltpu.PrefetchScalarGridS...  30.8 us
    ppermute x21, starting transfers between devices, turned(): lax.ppermute(value, 'tensor', [(i, (i + turn) % planes) for i in range(pl...  28.9 us
    unnamed x56, local copies, waits for them, and re-layouts  21.2 us
    all_gather x1, blocking collectives, local(): lax.all_gather(after(output_up_maps, held[0][1]), 'dp', axis=0, tiled=True)  10.6 us
    all_gather x1, blocking collectives, local(): own_down = lax.all_gather(after(out_down, held[0][1]), 'dp', axis=0)  7.49 us
    all_gather x1, blocking collectives, local(): lax.all_gather(jnp.transpose(adapter_up_maps[0], (1, 0, 2)), 'dp', axis=0)  6.91 us
  transfers between devices with their start and end apart: 23, of which 8 were waited for; matrix products, arithmetic and copies ran while one was open for 7% of the time, Pallas kernels for 15%

profile of v12, /device:TPU:0, one launch (start us, length us, event | category | flops | bytes accessed | tf_op | source)
XLA Modules:
  0.0 183.5 jit_solution(10446009187179463443)
XLA Ops:
  6.5 2.3 %fusion.5 = (bf16[256,1024]{1,0:T(8,128)(2,1)}, bf16[256,1024]{1,0:T(8,128)(2,1)}) fusion(bf16[512,1024]{1,0:T(8,128)(2,1)} %token_ref), kind=kLoop, calls=%fused_computation.33 | loop fusion | bytes 2097152 | tf_op jit(solution)/shard_map/slice | solution.py:319
  8.8 3.0 %collective-permute-start = (bf16[256,1024]{1,0:T(8,128)(2,1)}, bf16[256,1024]{1,0:T(8,128)(2,1)}, u32[]{:S(2)}, u32[]{:S(2)}) collective-permute-start(bf16[256,1024]{1,0:T(8,128)(2,1)} %get-tuple-element.117), channel_id=1, source_target_pairs={{0,1},{1,2},{2,3},{3,0},{4,5},{5,6},{6,7},{7,4},{8,9},{9,10},{10,1... | collective-permute-start | bytes 1572872 | tf_op jit(solution)/shard_map/ppermute | solution.py:316
  12.8 2.8 %fusion.4 = (bf16[64,1,1024]{2,1,0:T(2,128)(2,1)S(1)}, bf16[64,1,1024]{2,1,0:T(2,128)(2,1)S(1)}, bf16[64,1,1024]{2,1,0:T(2,128)(2,1)S(1)}) fusion(bf16[128,4,4096]{2,1,0:T(4,128)(2,1)} %param.11, s32[]{:T(128)S(6)} %select_n.64, s32[]{:T(128)S(6)} %select_n.67, s32[]{:T(128)S(6)} %select_n.76, s32[]{:T(128)S(6)} %select_n.73, s32[]{:T(128)S(6)} %select_n.70), kind=kLoop, calls=%fused_computation.32 | loop fusion | bytes 786452 | tf_op jit(solution)/shard_map/dynamic_slice | solution.py:358
  19.4 2.9 %collective-permute-start.3 = (bf16[96,1024]{1,0:T(8,128)(2,1)}, bf16[96,1024]{1,0:T(8,128)(2,1)}, u32[]{:S(2)}, u32[]{:S(2)}) collective-permute-start(bf16[96,1024]{1,0:T(8,128)(2,1)} %get-tuple-element.118), channel_id=1, source_target_pairs={{0,3},{1,0},{2,1},{3,2},{4,7},{5,4},{6,5},{7,6},{8,11},{9,8},{10,9... | collective-permute-start | bytes 589832 | tf_op jit(solution)/shard_map/ppermute | solution.py:316
  27.4 2.8 %copy-done.2 = bf16[4096,6,128]{2,0,1:T(8,128)(2,1)S(1)} copy-done((bf16[4096,6,128]{2,0,1:T(8,128)(2,1)S(1)}, bf16[4096,6,128]{2,0,1:T(8,128)(2,1)}, u32[]{:S(2)}) %copy-start.2) | copy-done | bytes 6291480
  32.0 6.9 %all-gather = bf16[24,64,128]{2,1,0:T(8,128)(2,1)} all-gather(bf16[6,64,128]{2,1,0:T(8,128)(2,1)S(1)} %bitcast.66), channel_id=2, replica_groups=mesh['groups'=2,'dp'=4,'tensor'=4] {'dp'}, dimensions={0}, use_global_device_ids=true | all-gather | bytes 491520 | tf_op jit(solution)/shard_map/all_gather | solution.py:323
  38.9 2.1 %pad_maximum_fusion = bf16[3,96,1024]{2,1,0:T(8,128)(2,1)} fusion(bf16[1,96,1024]{2,1,0:T(8,128)(2,1)} %bitcast.19, bf16[1,96,1024]{2,1,0:T(8,128)(2,1)} %bitcast.18, bf16[1,96,1024]{2,1,0:T(8,128)(2,1)} %bitcast.17), kind=kLoop, calls=%fused_computation.1 | loop fusion | flops 589824 | bytes 1179648 | tf_op jit(solution)/shard_map/stack | solution.py:372
  41.0 4.7 %collective-permute-start.4 = (bf16[256,1024]{1,0:T(8,128)(2,1)}, bf16[256,1024]{1,0:T(8,128)(2,1)}, u32[]{:S(2)}, u32[]{:S(2)}) collective-permute-start(bf16[256,1024]{1,0:T(8,128)(2,1)} %collective-permute-done.refs_0_), channel_id=1, source_target_pairs={{0,1},{1,2},{2,3},{3,0},{4,5},{5,6},{6,7},{7,4},{8,9},{9,10},{10,1... | collective-permute-start | bytes 1572872 | tf_op jit(solution)/shard_map/ppermute | solution.py:316
  46.0 2.8 %copy-done.3 = bf16[4096,6,128]{2,0,1:T(8,128)(2,1)S(1)} copy-done((bf16[4096,6,128]{2,0,1:T(8,128)(2,1)S(1)}, bf16[4096,6,128]{2,0,1:T(8,128)(2,1)}, u32[]{:S(2)}) %copy-start.3) | copy-done | bytes 6291480
  48.8 2.3 %project.6.refs_2_ = f32[256,768]{1,0:T(8,128)S(1)} custom-call(s32[1]{0:T(128)} %get-tuple-element.127.ids_ref, bf16[256,1024]{1,0:T(8,128)(2,1)} %collective-permute-done.refs_0_, bf16[6,4096,128]{2,1,0:T(8,128)(2,1)S(1)} %bitcast.49, f32[512,768]{1,0:T(8,128)S(1)} %project.5.refs_2_), custom_call_target="tpu_custom_call" | custom-call | bytes 25165824 | tf_op jit(solution)/shard_map/project/pallas_call | solution.py:26
  52.0 10.6 %all_gather.27.refs_3_ = bf16[4,64,1024]{2,1,0:T(8,128)(2,1)} all-gather(bf16[1,64,1024]{2,1,0:T(8,128)(2,1)S(1)} %copy-done.21), channel_id=1, replica_groups=mesh['groups'=2,'dp'=4,'tensor'=4] {'dp'}, dimensions={0}, use_global_device_ids=true | all-gather | bytes 655360 | tf_op jit(solution)/shard_map/all_gather | solution.py:385
  64.0 2.7 %shrink.1 = (f32[128,192]{1,0:T(8,128)S(1)}, f32[128,192]{1,0:T(8,128)S(1)}, f32[128,192]{1,0:T(8,128)S(1)}, f32[128,192]{1,0:T(8,128)S(1)}) custom-call(s32[5]{0:T(128)S(1)} %pad_add_fusion.3.ids_ref, s32[512,2]{1,0:T(8,128)S(1)} %copy.35.table_ref.refs_2_, bf16[512,1024]{1,0:T(8,128)(2,1)S(1)} %copy-done.6, bf16[4,192,1024]{2,1,0:T(8,128)(2,1)S(1)} %copy-done.12), custom_call_target="tpu_custom_call" | custom-call | bytes 7876608 | tf_op jit(solution)/shard_map/shrink/pallas_call | solution.py:26
  66.6 2.3 %collective-permute-start.6 = (f32[128,192]{1,0:T(8,128)S(1)}, f32[128,192]{1,0:T(8,128)S(1)}, u32[]{:S(2)}, u32[]{:S(2)}) collective-permute-start(f32[128,192]{1,0:T(8,128)S(1)} %get-tuple-element.67), channel_id=1, source_target_pairs={{0,1},{1,2},{2,3},{3,0},{4,5},{5,6},{6,7},{7,4},{8,9},{9,10},{10,1... | collective-permute-start | bytes 294920 | tf_op jit(solution)/shard_map/ppermute | solution.py:316
  69.0 2.2 %collective-permute-start.7 = (f32[128,192]{1,0:T(8,128)S(1)}, f32[128,192]{1,0:T(8,128)S(1)}, u32[]{:S(2)}, u32[]{:S(2)}) collective-permute-start(f32[128,192]{1,0:T(8,128)S(1)} %get-tuple-element.68), channel_id=1, source_target_pairs={{0,2},{1,3},{2,0},{3,1},{4,6},{5,7},{6,4},{7,5},{8,10},{9,11},{10,... | collective-permute-start | bytes 294920 | tf_op jit(solution)/shard_map/ppermute | solution.py:316
  71.4 7.5 %all-gather.1 = bf16[128,1024]{1,0:T(8,128)(2,1)S(1)} all-gather(bf16[32,1024]{1,0:T(8,128)(2,1)S(1)} %bitcast_dynamic-update-slice_fusion), channel_id=3, replica_groups=mesh['groups'=2,'dp'=4,'tensor'=4] {'dp'}, dimensions={0}, use_global_device_ids=true | all-gather | bytes 327680 | tf_op jit(solution)/shard_map/all_gather | solution.py:388
  80.3 3.3 %collective-permute-start.9 = (bf16[256,1024]{1,0:T(8,128)(2,1)}, bf16[256,1024]{1,0:T(8,128)(2,1)S(1)}, u32[]{:S(2)}, u32[]{:S(2)}) collective-permute-start(bf16[256,1024]{1,0:T(8,128)(2,1)} %collective-permute-done.4.refs_0_), channel_id=1, source_target_pairs={{0,1},{1,2},{2,3},{3,0},{4,5},{5,6},{6,7},{7,4},{8,9},{9,10},{10,1... | collective-permute-start | bytes 1572872 | tf_op jit(solution)/shard_map/ppermute | solution.py:316
  85.0 3.1 %collective-permute-start.12 = (bf16[128,192]{1,0:T(8,128)(2,1)S(1)}, bf16[128,192]{1,0:T(8,128)(2,1)S(1)}, u32[]{:S(2)}, u32[]{:S(2)}) collective-permute-start(bf16[128,192]{1,0:T(8,128)(2,1)S(1)} %add_convert_fusion.refs_0_), channel_id=1, source_target_pairs={{0,2},{1,3},{2,0},{3,1},{4,6},{5,7},{6,4},{7,5},{8,10},{9,11},{10,... | collective-permute-start | bytes 147464 | tf_op jit(solution)/shard_map/ppermute | solution.py:316
  88.1 2.8 %copy-done.4 = bf16[4096,6,128]{2,0,1:T(8,128)(2,1)S(1)} copy-done((bf16[4096,6,128]{2,0,1:T(8,128)(2,1)S(1)}, bf16[4096,6,128]{2,0,1:T(8,128)(2,1)}, u32[]{:S(2)}) %copy-start.4) | copy-done | bytes 6291480
  90.9 2.3 %project.8.refs_2_ = f32[256,768]{1,0:T(8,128)S(1)} custom-call(s32[1]{0:T(128)} %get-tuple-element.127.ids_ref, bf16[256,1024]{1,0:T(8,128)(2,1)} %collective-permute-done.5.refs_0_, bf16[6,4096,128]{2,1,0:T(8,128)(2,1)S(1)} %bitcast.50, f32[512,768]{1,0:T(8,128)S(1)} %project.5.refs_2_), custom_call_target="tpu_custom_call" | custom-call | bytes 25165824 | tf_op jit(solution)/shard_map/project/pallas_call | solution.py:26
  93.2 2.8 %project.7.refs_6_ = f32[256,768]{1,0:T(8,128)S(1)} custom-call(s32[1]{0:T(128)} %get-tuple-element.126.ids_ref, bf16[256,1024]{1,0:T(8,128)(2,1)} %collective-permute-done.4.refs_0_, bf16[6,4096,128]{2,1,0:T(8,128)(2,1)S(1)} %bitcast.51, f32[256,768]{1,0:T(8,128)S(1)} %copy-done.11), custom_call_target="tpu_custom_call" | custom-call | bytes 22806528 | tf_op jit(solution)/shard_map/project/pallas_call | solution.py:26
  96.0 13.9 %collective-permute-done.11.refs_1_ = bf16[128,192]{1,0:T(8,128)(2,1)S(1)} collective-permute-done((bf16[128,192]{1,0:T(8,128)(2,1)S(1)}, bf16[128,192]{1,0:T(8,128)(2,1)S(1)}, u32[]{:S(2)}, u32[]{:S(2)}) %collective-permute-start.11) | collective-permute-done | bytes 49184 | tf_op jit(solution)/shard_map/ppermute | solution.py:316
  111.7 1.9 %collective-permute-start.14 = (bf16[256,1024]{1,0:T(8,128)(2,1)S(1)}, bf16[256,1024]{1,0:T(8,128)(2,1)S(1)}, u32[]{:S(2)}, u32[]{:S(2)}) collective-permute-start(bf16[256,1024]{1,0:T(8,128)(2,1)S(1)} %collective-permute-done.10.refs_0_), channel_id=1, source_target_pairs={{0,1},{1,2},{2,3},{3,0},{4,5},{5,6},{6,7},{7,4},{8,9},{9,10},{10,1... | collective-permute-start | bytes 1572872 | tf_op jit(solution)/shard_map/ppermute | solution.py:316
  113.7 2.8 %copy-done.5 = bf16[4096,6,128]{2,0,1:T(8,128)(2,1)S(1)} copy-done((bf16[4096,6,128]{2,0,1:T(8,128)(2,1)S(1)}, bf16[4096,6,128]{2,0,1:T(8,128)(2,1)}, u32[]{:S(2)}) %copy-start.5) | copy-done | bytes 6291480
  116.4 3.2 %attend.2 = (bf16[256,512]{1,0:T(8,128)(2,1)S(1)}, bf16[256,128]{1,0:T(8,128)(2,1)S(1)}, bf16[256,128]{1,0:T(8,128)(2,1)S(1)}) custom-call(s32[8]{0:T(128)S(1)} %pad_add_fusion.2.ids_ref, s32[512,2]{1,0:T(8,128)S(1)} %copy.35.table_ref.refs_2_, f32[512,256]{1,0:T(8,128)S(1)} %pad_maximum_fusion.1.turn_ref, bf16[4,6,64,128]{3,2,1,0:T(8,128)(2,1)S(1)} %bitcast.59, ...), custom_call_target="tpu_custom_call" | custom-call | bytes 26161152 | tf_op jit(solution)/shard_map/attend/pallas_call | solution.py:26
  121.7 11.2 %collective-permute-done.15.attended_ref = bf16[256,512]{1,0:T(8,128)(2,1)S(1)} collective-permute-done((bf16[256,512]{1,0:T(8,128)(2,1)S(1)}, bf16[256,512]{1,0:T(8,128)(2,1)S(1)}, u32[]{:S(2)}, u32[]{:S(2)}) %collective-permute-start.15) | collective-permute-done | bytes 262176 | tf_op jit(solution)/shard_map/ppermute | solution.py:316
  133.0 3.8 %attend.3 = (bf16[256,512]{1,0:T(8,128)(2,1)S(1)}, bf16[256,128]{1,0:T(8,128)(2,1)}, bf16[256,128]{1,0:T(8,128)(2,1)}) custom-call(s32[8]{0:T(128)S(1)} %pad_add_fusion.2.ids_ref, s32[512,2]{1,0:T(8,128)S(1)} %copy.35.table_ref.refs_2_, f32[512,256]{1,0:T(8,128)S(1)} %pad_maximum_fusion.1.turn_ref, bf16[4,6,64,128]{3,2,1,0:T(8,128)(2,1)S(1)} %bitcast.60, ...), custom_call_target="tpu_custom_call" | custom-call | bytes 26554368 | tf_op jit(solution)/shard_map/attend/pallas_call | solution.py:26
  137.2 6.4 %collective-permute-done.17.attended_ref = bf16[256,512]{1,0:T(8,128)(2,1)S(1)} collective-permute-done((bf16[256,512]{1,0:T(8,128)(2,1)S(1)}, bf16[256,512]{1,0:T(8,128)(2,1)S(1)}, u32[]{:S(2)}, u32[]{:S(2)}) %collective-permute-start.17) | collective-permute-done | bytes 262176 | tf_op jit(solution)/shard_map/ppermute | solution.py:316
  143.6 5.6 %collective-permute-done.16.attended_ref = bf16[256,512]{1,0:T(8,128)(2,1)S(1)} collective-permute-done((bf16[256,512]{1,0:T(8,128)(2,1)S(1)}, bf16[256,512]{1,0:T(8,128)(2,1)S(1)}, u32[]{:S(2)}, u32[]{:S(2)}) %collective-permute-start.16) | collective-permute-done | bytes 262176 | tf_op jit(solution)/shard_map/ppermute | solution.py:316
  150.0 4.9 %collective-permute-done.19.attended_ref = bf16[256,512]{1,0:T(8,128)(2,1)S(1)} collective-permute-done((bf16[256,512]{1,0:T(8,128)(2,1)S(1)}, bf16[256,512]{1,0:T(8,128)(2,1)S(1)}, u32[]{:S(2)}, u32[]{:S(2)}) %collective-permute-start.19) | collective-permute-done | bytes 262176 | tf_op jit(solution)/shard_map/ppermute | solution.py:316
  154.9 4.0 %collective-permute-done.18.attended_ref = bf16[256,512]{1,0:T(8,128)(2,1)S(1)} collective-permute-done((bf16[256,512]{1,0:T(8,128)(2,1)S(1)}, bf16[256,512]{1,0:T(8,128)(2,1)S(1)}, u32[]{:S(2)}, u32[]{:S(2)}) %collective-permute-start.18) | collective-permute-done | bytes 262176 | tf_op jit(solution)/shard_map/ppermute | solution.py:316
  162.4 2.3 %copy-done = bf16[24,96,1024]{2,1,0:T(8,128)(2,1)S(1)} copy-done((bf16[24,96,1024]{2,1,0:T(8,128)(2,1)S(1)}, bf16[24,96,1024]{2,1,0:T(8,128)(2,1)}, u32[]{:S(2)}) %copy-start) | copy-done | bytes 4718616
  173.5 3.2 %project_out.15 = bf16[512,1024]{1,0:T(8,128)(2,1)} custom-call(s32[5]{0:T(128)S(1)} %pad_add_fusion.1.ids_ref, bf16[256,512]{1,0:T(8,128)(2,1)} %collective-permute-done.20.attended_ref, bf16[8,3,96,1024]{3,2,1,0:T(8,128)(2,1)S(1)} %bitcast.46, bf16[8,3,96,1024]{3,2,1,0:T(8,128)(2,1)S(1)} %bitcast.47, f32[256,1024]{1,0:T(8,128)S(1)} %get-tuple-element.104.refs_0_, ...), custom_call_target="tpu_custom_call" | custom-call | bytes 36188160 | tf_op jit(solution)/shard_map/project_out/pallas_call | solution.py:26
  (120 shorter events, 34.4 us)
Async XLA Ops:
  6.5 15.7 %copy-start.23 = (s32[1,4]{1,0:T(1,128)S(1)}, s32[1,4]{1,0:T(1,128)}, u32[]{:S(2)}) copy-start(s32[1,4]{1,0:T(1,128)} %param.17) | copy-start | bytes 52
  6.5 15.9 %copy-start.24 = (s32[1,4]{1,0:T(1,128)S(1)}, s32[1,4]{1,0:T(1,128)}, u32[]{:S(2)}) copy-start(s32[1,4]{1,0:T(1,128)} %param.16) | copy-start | bytes 52
  6.5 56.0 %all-gather.6.cloned.1.call-start = ((), (), s32[]{:S(2)}) async-start(), calls=%async_computation | async-start | bytes 1966080 | tf_op jit(solution)/shard_map/all_gather | solution.py:322
  8.8 30.1 %collective-permute-start = (bf16[256,1024]{1,0:T(8,128)(2,1)}, bf16[256,1024]{1,0:T(8,128)(2,1)}, u32[]{:S(2)}, u32[]{:S(2)}) collective-permute-start(bf16[256,1024]{1,0:T(8,128)(2,1)} %get-tuple-element.117), channel_id=1, source_target_pairs={{0,1},{1,2},{2,3},{3,0},{4,5},{5,6},{6,7},{7,4},{8,9},{9,10},{10,1... | collective-permute-start | bytes 1572872 | tf_op jit(solution)/shard_map/ppermute | solution.py:316
  11.9 150.6 %all-gather.8.cloned.1.call-start = ((), (), s32[]{:S(2)}) async-start(), calls=%async_computation.1 | async-start | bytes 5308416 | tf_op jit(solution)/shard_map/all_gather | solution.py:372
  15.7 11.7 %copy-start.6 = (bf16[512,1024]{1,0:T(8,128)(2,1)S(1)}, bf16[512,1024]{1,0:T(8,128)(2,1)}, u32[]{:S(2)}) copy-start(bf16[512,1024]{1,0:T(8,128)(2,1)} %token_ref) | copy-start | bytes 3145732
  16.7 22.2 %collective-permute-start.1 = (bf16[96,1024]{1,0:T(8,128)(2,1)}, bf16[96,1024]{1,0:T(8,128)(2,1)}, u32[]{:S(2)}, u32[]{:S(2)}) collective-permute-start(bf16[96,1024]{1,0:T(8,128)(2,1)} %get-tuple-element.120), channel_id=1, source_target_pairs={{0,1},{1,2},{2,3},{3,0},{4,5},{5,6},{6,7},{7,4},{8,9},{9,10},{10,1... | collective-permute-start | bytes 589832 | tf_op jit(solution)/shard_map/ppermute | solution.py:316
  18.3 20.6 %collective-permute-start.2 = (bf16[96,1024]{1,0:T(8,128)(2,1)}, bf16[96,1024]{1,0:T(8,128)(2,1)}, u32[]{:S(2)}, u32[]{:S(2)}) collective-permute-start(bf16[96,1024]{1,0:T(8,128)(2,1)} %get-tuple-element.119), channel_id=1, source_target_pairs={{0,2},{1,3},{2,0},{3,1},{4,6},{5,7},{6,4},{7,5},{8,10},{9,11},{10,... | collective-permute-start | bytes 589832 | tf_op jit(solution)/shard_map/ppermute | solution.py:316
  19.4 19.6 %collective-permute-start.3 = (bf16[96,1024]{1,0:T(8,128)(2,1)}, bf16[96,1024]{1,0:T(8,128)(2,1)}, u32[]{:S(2)}, u32[]{:S(2)}) collective-permute-start(bf16[96,1024]{1,0:T(8,128)(2,1)} %get-tuple-element.118), channel_id=1, source_target_pairs={{0,3},{1,0},{2,1},{3,2},{4,7},{5,4},{6,5},{7,6},{8,11},{9,8},{10,9... | collective-permute-start | bytes 589832 | tf_op jit(solution)/shard_map/ppermute | solution.py:316
  41.0 37.9 %collective-permute-start.4 = (bf16[256,1024]{1,0:T(8,128)(2,1)}, bf16[256,1024]{1,0:T(8,128)(2,1)}, u32[]{:S(2)}, u32[]{:S(2)}) collective-permute-start(bf16[256,1024]{1,0:T(8,128)(2,1)} %collective-permute-done.refs_0_), channel_id=1, source_target_pairs={{0,1},{1,2},{2,3},{3,0},{4,5},{5,6},{6,7},{7,4},{8,9},{9,10},{10,1... | collective-permute-start | bytes 1572872 | tf_op jit(solution)/shard_map/ppermute | solution.py:316
  45.7 33.2 %collective-permute-start.5 = (bf16[256,1024]{1,0:T(8,128)(2,1)}, bf16[256,1024]{1,0:T(8,128)(2,1)}, u32[]{:S(2)}, u32[]{:S(2)}) collective-permute-start(bf16[256,1024]{1,0:T(8,128)(2,1)} %get-tuple-element.63), channel_id=1, source_target_pairs={{0,1},{1,2},{2,3},{3,0},{4,5},{5,6},{6,7},{7,4},{8,9},{9,10},{10,1... | collective-permute-start | bytes 1572872 | tf_op jit(solution)/shard_map/ppermute | solution.py:316
  48.8 3.2 %copy-start.21 = (bf16[1,64,1024]{2,1,0:T(8,128)(2,1)S(1)}, bf16[1,64,1024]{2,1,0:T(8,128)(2,1)}, u32[]{:S(2)}) copy-start(bf16[1,64,1024]{2,1,0:T(8,128)(2,1)} %param.15) | copy-start | bytes 393220
  66.6 12.3 %collective-permute-start.6 = (f32[128,192]{1,0:T(8,128)S(1)}, f32[128,192]{1,0:T(8,128)S(1)}, u32[]{:S(2)}, u32[]{:S(2)}) collective-permute-start(f32[128,192]{1,0:T(8,128)S(1)} %get-tuple-element.67), channel_id=1, source_target_pairs={{0,1},{1,2},{2,3},{3,0},{4,5},{5,6},{6,7},{7,4},{8,9},{9,10},{10,1... | collective-permute-start | bytes 294920 | tf_op jit(solution)/shard_map/ppermute | solution.py:316
  69.0 11.3 %collective-permute-start.7 = (f32[128,192]{1,0:T(8,128)S(1)}, f32[128,192]{1,0:T(8,128)S(1)}, u32[]{:S(2)}, u32[]{:S(2)}) collective-permute-start(f32[128,192]{1,0:T(8,128)S(1)} %get-tuple-element.68), channel_id=1, source_target_pairs={{0,2},{1,3},{2,0},{3,1},{4,6},{5,7},{6,4},{7,5},{8,10},{9,11},{10,... | collective-permute-start | bytes 294920 | tf_op jit(solution)/shard_map/ppermute | solution.py:316
  71.2 9.1 %collective-permute-start.8 = (f32[128,192]{1,0:T(8,128)S(1)}, f32[128,192]{1,0:T(8,128)S(1)}, u32[]{:S(2)}, u32[]{:S(2)}) collective-permute-start(f32[128,192]{1,0:T(8,128)S(1)} %get-tuple-element.69), channel_id=1, source_target_pairs={{0,3},{1,0},{2,1},{3,2},{4,7},{5,4},{6,5},{7,6},{8,11},{9,8},{10,9... | collective-permute-start | bytes 294920 | tf_op jit(solution)/shard_map/ppermute | solution.py:316
  80.3 31.4 %collective-permute-start.9 = (bf16[256,1024]{1,0:T(8,128)(2,1)}, bf16[256,1024]{1,0:T(8,128)(2,1)S(1)}, u32[]{:S(2)}, u32[]{:S(2)}) collective-permute-start(bf16[256,1024]{1,0:T(8,128)(2,1)} %collective-permute-done.4.refs_0_), channel_id=1, source_target_pairs={{0,1},{1,2},{2,3},{3,0},{4,5},{5,6},{6,7},{7,4},{8,9},{9,10},{10,1... | collective-permute-start | bytes 1572872 | tf_op jit(solution)/shard_map/ppermute | solution.py:316
  83.6 28.1 %collective-permute-start.10 = (bf16[256,1024]{1,0:T(8,128)(2,1)}, bf16[256,1024]{1,0:T(8,128)(2,1)S(1)}, u32[]{:S(2)}, u32[]{:S(2)}) collective-permute-start(bf16[256,1024]{1,0:T(8,128)(2,1)} %collective-permute-done.5.refs_0_), channel_id=1, source_target_pairs={{0,1},{1,2},{2,3},{3,0},{4,5},{5,6},{6,7},{7,4},{8,9},{9,10},{10,1... | collective-permute-start | bytes 1572872 | tf_op jit(solution)/shard_map/ppermute | solution.py:316
  83.7 26.2 %collective-permute-start.11 = (bf16[128,192]{1,0:T(8,128)(2,1)S(1)}, bf16[128,192]{1,0:T(8,128)(2,1)S(1)}, u32[]{:S(2)}, u32[]{:S(2)}) collective-permute-start(bf16[128,192]{1,0:T(8,128)(2,1)S(1)} %add_convert_fusion.refs_0_), channel_id=1, source_target_pairs={{0,1},{1,2},{2,3},{3,0},{4,5},{5,6},{6,7},{7,4},{8,9},{9,10},{10,1... | collective-permute-start | bytes 147464 | tf_op jit(solution)/shard_map/ppermute | solution.py:316
  85.0 26.7 %collective-permute-start.12 = (bf16[128,192]{1,0:T(8,128)(2,1)S(1)}, bf16[128,192]{1,0:T(8,128)(2,1)S(1)}, u32[]{:S(2)}, u32[]{:S(2)}) collective-permute-start(bf16[128,192]{1,0:T(8,128)(2,1)S(1)} %add_convert_fusion.refs_0_), channel_id=1, source_target_pairs={{0,2},{1,3},{2,0},{3,1},{4,6},{5,7},{6,4},{7,5},{8,10},{9,11},{10,... | collective-permute-start | bytes 147464 | tf_op jit(solution)/shard_map/ppermute | solution.py:316
  88.1 23.6 %collective-permute-start.13 = (bf16[128,192]{1,0:T(8,128)(2,1)S(1)}, bf16[128,192]{1,0:T(8,128)(2,1)S(1)}, u32[]{:S(2)}, u32[]{:S(2)}) collective-permute-start(bf16[128,192]{1,0:T(8,128)(2,1)S(1)} %add_convert_fusion.refs_0_), channel_id=1, source_target_pairs={{0,3},{1,0},{2,1},{3,2},{4,7},{5,4},{6,5},{7,6},{8,11},{9,8},{10,9... | collective-permute-start | bytes 147464 | tf_op jit(solution)/shard_map/ppermute | solution.py:316
  93.2 20.4 %copy-start.9 = (bf16[24,64,128]{2,1,0:T(8,128)(2,1)S(1)}, bf16[24,64,128]{2,1,0:T(8,128)(2,1)}, u32[]{:S(2)}) copy-start(bf16[24,64,128]{2,1,0:T(8,128)(2,1)} %all-gather) | copy-start | bytes 1179652
  93.2 27.2 %slice-start = ((s8[6291456]{0:T(1024)(128)(4,1)}), s8[4194304]{0:T(1024)(128)(4,1)S(1)}, s32[]{:S(2)}) async-start(s8[6291456]{0:T(1024)(128)(4,1)} %bitcast.53), calls=%async_computation.2 | async-start | bytes 8388608
  111.7 21.3 %collective-permute-start.14 = (bf16[256,1024]{1,0:T(8,128)(2,1)S(1)}, bf16[256,1024]{1,0:T(8,128)(2,1)S(1)}, u32[]{:S(2)}, u32[]{:S(2)}) collective-permute-start(bf16[256,1024]{1,0:T(8,128)(2,1)S(1)} %collective-permute-done.10.refs_0_), channel_id=1, source_target_pairs={{0,1},{1,2},{2,3},{3,0},{4,5},{5,6},{6,7},{7,4},{8,9},{9,10},{10,1... | collective-permute-start | bytes 1572872 | tf_op jit(solution)/shard_map/ppermute | solution.py:316
  116.4 4.0 %slice-start.1 = ((s8[6291456]{0:T(1024)(128)(4,1)}), s8[2097152]{0:T(1024)(128)(4,1)S(1)}, s32[]{:S(2)}) async-start(s8[6291456]{0:T(1024)(128)(4,1)} %bitcast.53), calls=%async_computation.3 | async-start | bytes 4194304
  119.6 13.3 %collective-permute-start.15 = (bf16[256,512]{1,0:T(8,128)(2,1)S(1)}, bf16[256,512]{1,0:T(8,128)(2,1)S(1)}, u32[]{:S(2)}, u32[]{:S(2)}) collective-permute-start(bf16[256,512]{1,0:T(8,128)(2,1)S(1)} %get-tuple-element.91.attended_ref), channel_id=1, source_target_pairs={{0,1},{1,2},{2,3},{3,0},{4,5},{5,6},{6,7},{7,4},{8,9},{9,10},{10,1... | collective-permute-start | bytes 786440 | tf_op jit(solution)/shard_map/ppermute | solution.py:316
  132.9 4.0 %copy-start.13 = (bf16[256,512]{1,0:T(8,128)(2,1)}, bf16[256,512]{1,0:T(8,128)(2,1)S(1)}, u32[]{:S(2)}) copy-start(bf16[256,512]{1,0:T(8,128)(2,1)S(1)} %collective-permute-done.15.attended_ref) | copy-start | bytes 786436
  132.9 10.7 %collective-permute-start.17 = (bf16[256,512]{1,0:T(8,128)(2,1)S(1)}, bf16[256,512]{1,0:T(8,128)(2,1)S(1)}, u32[]{:S(2)}, u32[]{:S(2)}) collective-permute-start(bf16[256,512]{1,0:T(8,128)(2,1)S(1)} %collective-permute-done.15.attended_ref), channel_id=1, source_target_pairs={{0,1},{1,2},{2,3},{3,0},{4,5},{5,6},{6,7},{7,4},{8,9},{9,10},{10,1... | collective-permute-start | bytes 786440 | tf_op jit(solution)/shard_map/ppermute | solution.py:316
  133.0 25.9 %copy-start.7 = (bf16[4,128,1024]{2,1,0:T(8,128)(2,1)S(1)}, bf16[4,128,1024]{2,1,0:T(8,128)(2,1)}, u32[]{:S(2)}) copy-start(bf16[4,128,1024]{2,1,0:T(8,128)(2,1)} %copy.32) | copy-start | bytes 3145732
  136.9 12.4 %collective-permute-start.16 = (bf16[256,512]{1,0:T(8,128)(2,1)S(1)}, bf16[256,512]{1,0:T(8,128)(2,1)S(1)}, u32[]{:S(2)}, u32[]{:S(2)}) collective-permute-start(bf16[256,512]{1,0:T(8,128)(2,1)S(1)} %get-tuple-element.92.attended_ref), channel_id=1, source_target_pairs={{0,1},{1,2},{2,3},{3,0},{4,5},{5,6},{6,7},{7,4},{8,9},{9,10},{10,1... | collective-permute-start | bytes 786440 | tf_op jit(solution)/shard_map/ppermute | solution.py:316
  143.6 11.2 %collective-permute-start.19 = (bf16[256,512]{1,0:T(8,128)(2,1)S(1)}, bf16[256,512]{1,0:T(8,128)(2,1)S(1)}, u32[]{:S(2)}, u32[]{:S(2)}) collective-permute-start(bf16[256,512]{1,0:T(8,128)(2,1)S(1)} %collective-permute-done.17.attended_ref), channel_id=1, source_target_pairs={{0,1},{1,2},{2,3},{3,0},{4,5},{5,6},{6,7},{7,4},{8,9},{9,10},{10,1... | collective-permute-start | bytes 786440 | tf_op jit(solution)/shard_map/ppermute | solution.py:316
  149.2 9.6 %collective-permute-start.18 = (bf16[256,512]{1,0:T(8,128)(2,1)S(1)}, bf16[256,512]{1,0:T(8,128)(2,1)S(1)}, u32[]{:S(2)}, u32[]{:S(2)}) collective-permute-start(bf16[256,512]{1,0:T(8,128)(2,1)S(1)} %collective-permute-done.16.attended_ref), channel_id=1, source_target_pairs={{0,1},{1,2},{2,3},{3,0},{4,5},{5,6},{6,7},{7,4},{8,9},{9,10},{10,1... | collective-permute-start | bytes 786440 | tf_op jit(solution)/shard_map/ppermute | solution.py:316
  158.8 14.7 %collective-permute-start.20 = (bf16[256,512]{1,0:T(8,128)(2,1)S(1)}, bf16[256,512]{1,0:T(8,128)(2,1)}, u32[]{:S(2)}, u32[]{:S(2)}) collective-permute-start(bf16[256,512]{1,0:T(8,128)(2,1)S(1)} %collective-permute-done.18.attended_ref), channel_id=1, source_target_pairs={{0,1},{1,2},{2,3},{3,0},{4,5},{5,6},{6,7},{7,4},{8,9},{9,10},{10,1... | collective-permute-start | bytes 786440 | tf_op jit(solution)/shard_map/ppermute | solution.py:316
  (18 other events, 29.4 us)
Sparse Core Ops, SparseCore 0:
  12.0 19.8 all-gather.5
  41.1 45.9 all-gather.7

commit v13 on v12

--- a/solution.py
+++ b/solution.py
@@ -8,7 +8,7 @@
 from jax.experimental.pallas import tpu as pltpu
 from jax.sharding import PartitionSpec as P
 
-VMEM_BYTES = 40 * 1024 * 1024
+VMEM_BYTES = 60 * 1024 * 1024
 PLANE = ("groups", "dp")
 
 
@@ -369,7 +369,6 @@
         (held[0][1], held[1][0], lines, begun, table, turn, up_all, own_rows)
     )
     held[0][1], held[1][0], lines, begun, table, turn, up_all, own_rows = done
-    lines = lax.all_gather(jnp.stack(lines), PLANE, axis=0)
     begun = [begun, begun]
     for step in range(2, planes):
         for part in range(2):
@@ -383,9 +382,11 @@
             sums = shrink_partial(adapters, here, planes, table, after(tokens, held[0][1]), down_all)
             side = [sums[0]] + [turned(sums[k], k) for k in range(1, planes)]
             out_up_all = lax.all_gather(
-                after(output_up_maps, held[0][1]), "dp", axis=0, tiled=True
+                after(output_up_maps, sums[0]), "dp", axis=0, tiled=True
             )
-            own_down = lax.all_gather(after(out_down, held[0][1]), "dp", axis=0)
+            own_down = lax.all_gather(after(out_down, sums[0]), "dp", axis=0)
+            lines = jnp.stack([after(line, sums[0]) for line in lines])
+            lines = lax.all_gather(lines, PLANE, axis=0)
             side = (side, out_up_all, own_down)
         elif step == 3:
             shrink = sum(side[1:], side[0]).astype(jnp.bfloat16)
@@ -417,7 +418,7 @@
         for part in range(2):
             arrived = attended[part][-1]
             if step < planes:
-                ahead = attended[0][step:]
+                ahead = [*attended[0][step:], *sums[part]]
                 attended[part].append(turned(after(arrived, *ahead)))
             final = [] if step < planes else [table, out_up_all, *before]
             sums[part] = project_out(

time: 184 us -> 192 us (1.043)
  Pallas kernels: 30.8 us -> 71.6 us
  local copies, waits for them, and re-layouts: 30.8 us -> 11.1 us
  waiting for transfers between devices: 49.2 us -> 37.1 us
    pallas_call x16, Pallas kernels: 30.8 us -> 71.6 us  [call(): pl.pallas_call(kernel, out_shape=out, grid_spec=pltpu.PrefetchScalarGridS...]
    unnamed x56 -> x50, local copies, waits for them, and re-layouts: 21.2 us -> 1.67 us
    ppermute x21, waiting for transfers between devices: 49.2 us -> 37.1 us  [turned(): lax.ppermute(value, 'tensor', [(i, (i + turn) % planes) for i in range(pl...]
  transfers between devices with their start and end apart: 23 -> 23, of which waited for: 8 -> 8; matrix products, arithmetic and copies ran while one was open for 7% -> 7% of each run, Pallas kernels for 15% -> 32%
where the time goes in v13:
time: 192 us; the launch traced here: 191 us
  Pallas kernels  71.6 us (37%)
  waiting for transfers between devices  37.1 us (19%)
  starting transfers between devices  27.2 us (14%)
  blocking collectives  23.9 us (12%)
  between operations  13.7 us (7%)
  local copies, waits for them, and re-layouts  11.1 us (6%)
  other arithmetic  6.08 us (3%)
    pallas_call x16, Pallas kernels, call(): pl.pallas_call(kernel, out_shape=out, grid_spec=pltpu.PrefetchScalarGridS...  71.6 us
    ppermute x21, waiting for transfers between devices, turned(): lax.ppermute(value, 'tensor', [(i, (i + turn) % planes) for i in range(pl...  37.1 us
    ppermute x21, starting transfers between devices, turned(): lax.ppermute(value, 'tensor', [(i, (i + turn) % planes) for i in range(pl...  27.1 us
    all_gather x1, blocking collectives, local(): lax.all_gather(after(output_up_maps, sums[0]), 'dp', axis=0, tiled=True)  10.7 us
    all_gather x1, blocking collectives, local(): lax.all_gather(jnp.transpose(adapter_up_maps[0], (1, 0, 2)), 'dp', axis=0)  6.91 us
    all_gather x1, blocking collectives, local(): own_down = lax.all_gather(after(out_down, sums[0]), 'dp', axis=0)  6.3 us
  transfers between devices with their start and end apart: 23, of which 8 were waited for; matrix products, arithmetic and copies ran while one was open for 7% of the time, Pallas kernels for 32%

profile of v13, /device:TPU:0, one launch (start us, length us, event | category | flops | bytes accessed | tf_op | source)
XLA Modules:
  0.0 190.8 jit_solution(14958576633843073915)
XLA Ops:
  7.8 3.1 %collective-permute-start = (bf16[256,1024]{1,0:T(8,128)(2,1)S(1)}, bf16[256,1024]{1,0:T(8,128)(2,1)S(1)}, u32[]{:S(2)}, u32[]{:S(2)}) collective-permute-start(bf16[256,1024]{1,0:T(8,128)(2,1)S(1)} %get-tuple-element.127), channel_id=1, source_target_pairs={{0,1},{1,2},{2,3},{3,0},{4,5},{5,6},{6,7},{7,4},{8,9},{9,10},{10,1... | collective-permute-start | bytes 1572872 | tf_op jit(solution)/shard_map/ppermute | solution.py:316
  11.9 2.8 %fusion.4 = (bf16[64,1,1024]{2,1,0:T(2,128)(2,1)S(1)}, bf16[64,1,1024]{2,1,0:T(2,128)(2,1)S(1)}, bf16[64,1,1024]{2,1,0:T(2,128)(2,1)S(1)}) fusion(bf16[128,4,4096]{2,1,0:T(4,128)(2,1)} %param.11, s32[]{:T(128)S(6)} %select_n.64, s32[]{:T(128)S(6)} %select_n.67, s32[]{:T(128)S(6)} %select_n.76, s32[]{:T(128)S(6)} %select_n.73, s32[]{:T(128)S(6)} %select_n.70), kind=kLoop, calls=%fused_computation.32 | loop fusion | bytes 786452 | tf_op jit(solution)/shard_map/dynamic_slice | solution.py:358
  18.3 2.9 %collective-permute-start.3 = (bf16[96,1024]{1,0:T(8,128)(2,1)S(1)}, bf16[96,1024]{1,0:T(8,128)(2,1)S(1)}, u32[]{:S(2)}, u32[]{:S(2)}) collective-permute-start(bf16[96,1024]{1,0:T(8,128)(2,1)S(1)} %get-tuple-element.128), channel_id=1, source_target_pairs={{0,3},{1,0},{2,1},{3,2},{4,7},{5,4},{6,5},{7,6},{8,11},{9,8},{10,9... | collective-permute-start | bytes 589832 | tf_op jit(solution)/shard_map/ppermute | solution.py:316
  27.9 4.6 %project.5.refs_2_ = f32[512,768]{1,0:T(8,128)} custom-call(s32[1]{0:T(128)} %get-tuple-element.138.ids_ref, bf16[512,1024]{1,0:T(8,128)(2,1)} %token_ref, bf16[6,4096,128]{2,1,0:T(8,128)(2,1)} %bitcast.48), custom_call_target="tpu_custom_call" | custom-call | bytes 22020096 | tf_op jit(solution)/shard_map/project/pallas_call | solution.py:26
  32.5 6.9 %all-gather = bf16[24,64,128]{2,1,0:T(8,128)(2,1)} all-gather(bf16[6,64,128]{2,1,0:T(8,128)(2,1)S(1)} %bitcast.67), channel_id=2, replica_groups=mesh['groups'=2,'dp'=4,'tensor'=4] {'dp'}, dimensions={0}, use_global_device_ids=true | all-gather | bytes 491520 | tf_op jit(solution)/shard_map/all_gather | solution.py:323
  40.3 5.5 %shrink.1 = (f32[128,192]{1,0:T(8,128)}, f32[128,192]{1,0:T(8,128)}, f32[128,192]{1,0:T(8,128)}, f32[128,192]{1,0:T(8,128)}) custom-call(s32[5]{0:T(128)} %pad_add_fusion.3.ids_ref, s32[512,2]{1,0:T(8,128)} %copy.35.table_ref.refs_2_, bf16[512,1024]{1,0:T(8,128)(2,1)} %token_ref, bf16[4,192,1024]{2,1,0:T(8,128)(2,1)} %all-gather.6.cloned.1.call-done.down_ref), custom_call_target="tpu_custom_call" | custom-call | bytes 7876608 | tf_op jit(solution)/shard_map/shrink/pallas_call | solution.py:26
  46.8 3.0 %collective-permute-start.4 = (bf16[256,1024]{1,0:T(8,128)(2,1)S(1)}, bf16[256,1024]{1,0:T(8,128)(2,1)S(1)}, u32[]{:S(2)}, u32[]{:S(2)}) collective-permute-start(bf16[256,1024]{1,0:T(8,128)(2,1)S(1)} %collective-permute-done.refs_0_), channel_id=1, source_target_pairs={{0,1},{1,2},{2,3},{3,0},{4,5},{5,6},{6,7},{7,4},{8,9},{9,10},{10,1... | collective-permute-start | bytes 1572872 | tf_op jit(solution)/shard_map/ppermute | solution.py:316
  49.9 4.0 %project.6.refs_2_ = f32[256,768]{1,0:T(8,128)} custom-call(s32[1]{0:T(128)} %get-tuple-element.137.ids_ref, bf16[256,1024]{1,0:T(8,128)(2,1)} %copy-done.1, bf16[6,4096,128]{2,1,0:T(8,128)(2,1)} %bitcast.49, f32[512,768]{1,0:T(8,128)} %project.5.refs_2_), custom_call_target="tpu_custom_call" | custom-call | bytes 25165824 | tf_op jit(solution)/shard_map/project/pallas_call | solution.py:26
  56.0 2.2 %collective-permute-start.7 = (f32[128,192]{1,0:T(8,128)S(1)}, f32[128,192]{1,0:T(8,128)S(1)}, u32[]{:S(2)}, u32[]{:S(2)}) collective-permute-start(f32[128,192]{1,0:T(8,128)S(1)} %copy-done.22), channel_id=1, source_target_pairs={{0,2},{1,3},{2,0},{3,1},{4,6},{5,7},{6,4},{7,5},{8,10},{9,11},{10,... | collective-permute-start | bytes 294920 | tf_op jit(solution)/shard_map/ppermute | solution.py:316
  58.4 10.7 %all_gather.27.refs_3_ = bf16[4,64,1024]{2,1,0:T(8,128)(2,1)} all-gather(bf16[1,64,1024]{2,1,0:T(8,128)(2,1)S(1)} %copy-done.16), channel_id=1, replica_groups=mesh['groups'=2,'dp'=4,'tensor'=4] {'dp'}, dimensions={0}, use_global_device_ids=true | all-gather | bytes 655360 | tf_op jit(solution)/shard_map/all_gather | solution.py:384
  69.2 6.3 %all-gather.1 = bf16[128,1024]{1,0:T(8,128)(2,1)} all-gather(bf16[32,1024]{1,0:T(8,128)(2,1)S(1)} %bitcast_dynamic-update-slice_fusion), channel_id=3, replica_groups=mesh['groups'=2,'dp'=4,'tensor'=4] {'dp'}, dimensions={0}, use_global_device_ids=true | all-gather | bytes 327680 | tf_op jit(solution)/shard_map/all_gather | solution.py:387
  75.5 2.3 %collective-permute-done.6 = f32[128,192]{1,0:T(8,128)S(1)} collective-permute-done((f32[128,192]{1,0:T(8,128)S(1)}, f32[128,192]{1,0:T(8,128)S(1)}, u32[]{:S(2)}, u32[]{:S(2)}) %collective-permute-start.6) | collective-permute-done | bytes 98336 | tf_op jit(solution)/shard_map/ppermute | solution.py:316
  77.7 4.9 %collective-permute-done.7 = f32[128,192]{1,0:T(8,128)S(1)} collective-permute-done((f32[128,192]{1,0:T(8,128)S(1)}, f32[128,192]{1,0:T(8,128)S(1)}, u32[]{:S(2)}, u32[]{:S(2)}) %collective-permute-start.7) | collective-permute-done | bytes 98336 | tf_op jit(solution)/shard_map/ppermute | solution.py:316
  82.6 3.3 %collective-permute-start.9 = (bf16[256,1024]{1,0:T(8,128)(2,1)S(1)}, bf16[256,1024]{1,0:T(8,128)(2,1)S(1)}, u32[]{:S(2)}, u32[]{:S(2)}) collective-permute-start(bf16[256,1024]{1,0:T(8,128)(2,1)S(1)} %collective-permute-done.4.refs_0_), channel_id=1, source_target_pairs={{0,1},{1,2},{2,3},{3,0},{4,5},{5,6},{6,7},{7,4},{8,9},{9,10},{10,1... | collective-permute-start | bytes 1572872 | tf_op jit(solution)/shard_map/ppermute | solution.py:316
  88.0 2.5 %collective-permute-start.12 = (bf16[128,192]{1,0:T(8,128)(2,1)S(1)}, bf16[128,192]{1,0:T(8,128)(2,1)S(1)}, u32[]{:S(2)}, u32[]{:S(2)}) collective-permute-start(bf16[128,192]{1,0:T(8,128)(2,1)S(1)} %add_convert_fusion.refs_0_), channel_id=1, source_target_pairs={{0,2},{1,3},{2,0},{3,1},{4,6},{5,7},{6,4},{7,5},{8,10},{9,11},{10,... | collective-permute-start | bytes 147464 | tf_op jit(solution)/shard_map/ppermute | solution.py:316
  90.4 3.9 %project.8.refs_2_ = f32[256,768]{1,0:T(8,128)} custom-call(s32[1]{0:T(128)} %get-tuple-element.137.ids_ref, bf16[256,1024]{1,0:T(8,128)(2,1)} %copy-done.3, bf16[6,4096,128]{2,1,0:T(8,128)(2,1)} %bitcast.50, f32[512,768]{1,0:T(8,128)} %project.5.refs_2_), custom_call_target="tpu_custom_call" | custom-call | bytes 25165824 | tf_op jit(solution)/shard_map/project/pallas_call | solution.py:26
  94.3 3.9 %project.7.refs_6_ = f32[256,768]{1,0:T(8,128)} custom-call(s32[1]{0:T(128)} %get-tuple-element.136.ids_ref, bf16[256,1024]{1,0:T(8,128)(2,1)} %copy-done.2, bf16[6,4096,128]{2,1,0:T(8,128)(2,1)} %bitcast.51, f32[256,768]{1,0:T(8,128)} %project.6.refs_2_), custom_call_target="tpu_custom_call" | custom-call | bytes 22806528 | tf_op jit(solution)/shard_map/project/pallas_call | solution.py:26
  98.2 14.1 %collective-permute-done.11.refs_1_ = bf16[128,192]{1,0:T(8,128)(2,1)S(1)} collective-permute-done((bf16[128,192]{1,0:T(8,128)(2,1)S(1)}, bf16[128,192]{1,0:T(8,128)(2,1)S(1)}, u32[]{:S(2)}, u32[]{:S(2)}) %collective-permute-start.11) | collective-permute-done | bytes 49184 | tf_op jit(solution)/shard_map/ppermute | solution.py:316
  116.4 6.1 %attend.2 = (bf16[256,512]{1,0:T(8,128)(2,1)}, bf16[256,128]{1,0:T(8,128)(2,1)}, bf16[256,128]{1,0:T(8,128)(2,1)}) custom-call(s32[8]{0:T(128)} %pad_add_fusion.2.ids_ref, s32[512,2]{1,0:T(8,128)} %copy.35.table_ref.refs_2_, f32[512,256]{1,0:T(8,128)} %pad_maximum_fusion.1.turn_ref, bf16[4,6,64,128]{3,2,1,0:T(8,128)(2,1)} %bitcast.57, ...), custom_call_target="tpu_custom_call" | custom-call | bytes 26161152 | tf_op jit(solution)/shard_map/attend/pallas_call | solution.py:26
  123.6 4.0 %project.9.refs_6_ = f32[256,768]{1,0:T(8,128)} custom-call(s32[1]{0:T(128)} %get-tuple-element.136.ids_ref, bf16[256,1024]{1,0:T(8,128)(2,1)} %copy-done.4, bf16[6,4096,128]{2,1,0:T(8,128)(2,1)} %bitcast.53, f32[256,768]{1,0:T(8,128)} %project.8.refs_2_), custom_call_target="tpu_custom_call" | custom-call | bytes 22806528 | tf_op jit(solution)/shard_map/project/pallas_call | solution.py:26
  127.6 3.7 %project_out.8 = (f32[256,1024]{1,0:T(8,128)}, f32[256,256]{1,0:T(8,128)}) custom-call(s32[5]{0:T(128)} %pad_add_fusion.1.ids_ref, bf16[256,512]{1,0:T(8,128)(2,1)} %get-tuple-element.96.attended_ref, bf16[512,1024]{1,0:T(8,128)(2,1)} %bitcast.55, bf16[4,32,1024]{2,1,0:T(8,128)(2,1)} %bitcast.59), custom_call_target="tpu_custom_call" | custom-call | bytes 4718592 | tf_op jit(solution)/shard_map/project_out/pallas_call | solution.py:26
  131.3 3.9 %collective-permute-done.15.attended_ref = bf16[256,512]{1,0:T(8,128)(2,1)S(1)} collective-permute-done((bf16[256,512]{1,0:T(8,128)(2,1)}, bf16[256,512]{1,0:T(8,128)(2,1)S(1)}, u32[]{:S(2)}, u32[]{:S(2)}) %collective-permute-start.15) | collective-permute-done | bytes 262176 | tf_op jit(solution)/shard_map/ppermute | solution.py:316
  136.1 6.8 %attend.3 = (bf16[256,512]{1,0:T(8,128)(2,1)}, bf16[256,128]{1,0:T(8,128)(2,1)}, bf16[256,128]{1,0:T(8,128)(2,1)}) custom-call(s32[8]{0:T(128)} %pad_add_fusion.2.ids_ref, s32[512,2]{1,0:T(8,128)} %copy.35.table_ref.refs_2_, f32[512,256]{1,0:T(8,128)} %pad_maximum_fusion.1.turn_ref, bf16[4,6,64,128]{3,2,1,0:T(8,128)(2,1)} %bitcast.58, ...), custom_call_target="tpu_custom_call" | custom-call | bytes 26554368 | tf_op jit(solution)/shard_map/attend/pallas_call | solution.py:26
  143.2 3.6 %project_out.9 = (f32[256,1024]{1,0:T(8,128)}, f32[256,256]{1,0:T(8,128)}) custom-call(s32[5]{0:T(128)} %pad_add_fusion.1.ids_ref, bf16[256,512]{1,0:T(8,128)(2,1)} %get-tuple-element.97.attended_ref, bf16[512,1024]{1,0:T(8,128)(2,1)} %bitcast.56, bf16[4,32,1024]{2,1,0:T(8,128)(2,1)} %bitcast.60), custom_call_target="tpu_custom_call" | custom-call | bytes 4718592 | tf_op jit(solution)/shard_map/project_out/pallas_call | solution.py:26
  146.8 5.3 %collective-permute-done.16.attended_ref = bf16[256,512]{1,0:T(8,128)(2,1)S(1)} collective-permute-done((bf16[256,512]{1,0:T(8,128)(2,1)}, bf16[256,512]{1,0:T(8,128)(2,1)S(1)}, u32[]{:S(2)}, u32[]{:S(2)}) %collective-permute-start.16) | collective-permute-done | bytes 262176 | tf_op jit(solution)/shard_map/ppermute | solution.py:316
  152.1 4.1 %project_out.10 = (f32[256,1024]{1,0:T(8,128)}, f32[256,256]{1,0:T(8,128)}) custom-call(s32[5]{0:T(128)} %pad_add_fusion.1.ids_ref, bf16[256,512]{1,0:T(8,128)(2,1)} %copy-done.11, bf16[8,3,96,1024]{3,2,1,0:T(8,128)(2,1)} %bitcast.36, bf16[8,3,96,1024]{3,2,1,0:T(8,128)(2,1)} %bitcast.37, f32[256,1024]{1,0:T(8,128)} %get-tuple-element.100.refs_0_, ...), custom_call_target="tpu_custom_call" | custom-call | bytes 33030144 | tf_op jit(solution)/shard_map/project_out/pallas_call | solution.py:26
  156.7 4.1 %project_out.11 = (f32[256,1024]{1,0:T(8,128)}, f32[256,256]{1,0:T(8,128)}) custom-call(s32[5]{0:T(128)} %pad_add_fusion.1.ids_ref, bf16[256,512]{1,0:T(8,128)(2,1)} %copy-done.13, bf16[8,3,96,1024]{3,2,1,0:T(8,128)(2,1)} %bitcast.38, bf16[8,3,96,1024]{3,2,1,0:T(8,128)(2,1)} %bitcast.39, f32[256,1024]{1,0:T(8,128)} %get-tuple-element.103.refs_0_, ...), custom_call_target="tpu_custom_call" | custom-call | bytes 33030144 | tf_op jit(solution)/shard_map/project_out/pallas_call | solution.py:26
  161.8 4.1 %collective-permute-done.19.attended_ref = bf16[256,512]{1,0:T(8,128)(2,1)S(1)} collective-permute-done((bf16[256,512]{1,0:T(8,128)(2,1)S(1)}, bf16[256,512]{1,0:T(8,128)(2,1)S(1)}, u32[]{:S(2)}, u32[]{:S(2)}) %collective-permute-start.19) | collective-permute-done | bytes 262176 | tf_op jit(solution)/shard_map/ppermute | solution.py:316
  165.9 4.2 %project_out.12 = (f32[256,1024]{1,0:T(8,128)}, f32[256,256]{1,0:T(8,128)}) custom-call(s32[5]{0:T(128)} %pad_add_fusion.1.ids_ref, bf16[256,512]{1,0:T(8,128)(2,1)} %copy-done.12, bf16[8,3,96,1024]{3,2,1,0:T(8,128)(2,1)} %bitcast.40, bf16[8,3,96,1024]{3,2,1,0:T(8,128)(2,1)} %bitcast.41, f32[256,1024]{1,0:T(8,128)} %get-tuple-element.115.refs_0_, ...), custom_call_target="tpu_custom_call" | custom-call | bytes 33030144 | tf_op jit(solution)/shard_map/project_out/pallas_call | solution.py:26
  170.1 4.1 %project_out.13 = (f32[256,1024]{1,0:T(8,128)}, f32[256,256]{1,0:T(8,128)}) custom-call(s32[5]{0:T(128)} %pad_add_fusion.1.ids_ref, bf16[256,512]{1,0:T(8,128)(2,1)} %copy-done.10, bf16[8,3,96,1024]{3,2,1,0:T(8,128)(2,1)} %bitcast.42, bf16[8,3,96,1024]{3,2,1,0:T(8,128)(2,1)} %bitcast.43, f32[256,1024]{1,0:T(8,128)} %get-tuple-element.112.refs_0_, ...), custom_call_target="tpu_custom_call" | custom-call | bytes 33030144 | tf_op jit(solution)/shard_map/project_out/pallas_call | solution.py:26
  174.2 4.3 %project_out.14.refs_4_ = bf16[256,1024]{1,0:T(8,128)(2,1)} custom-call(s32[5]{0:T(128)} %pad_add_fusion.1.ids_ref, bf16[256,512]{1,0:T(8,128)(2,1)} %copy-done.14, bf16[8,3,96,1024]{3,2,1,0:T(8,128)(2,1)} %bitcast.44, bf16[8,3,96,1024]{3,2,1,0:T(8,128)(2,1)} %bitcast.45, f32[256,1024]{1,0:T(8,128)} %get-tuple-element.121.refs_0_, ...), custom_call_target="tpu_custom_call" | custom-call | bytes 34615296 | tf_op jit(solution)/shard_map/project_out/pallas_call | solution.py:26
  179.3 4.6 %project_out.15 = bf16[512,1024]{1,0:T(8,128)(2,1)} custom-call(s32[5]{0:T(128)} %pad_add_fusion.1.ids_ref, bf16[256,512]{1,0:T(8,128)(2,1)} %copy-done.15, bf16[8,3,96,1024]{3,2,1,0:T(8,128)(2,1)} %bitcast.46, bf16[8,3,96,1024]{3,2,1,0:T(8,128)(2,1)} %bitcast.47, f32[256,1024]{1,0:T(8,128)} %get-tuple-element.118.refs_0_, ...), custom_call_target="tpu_custom_call" | custom-call | bytes 36188160 | tf_op jit(solution)/shard_map/project_out/pallas_call | solution.py:26
  (113 shorter events, 27.2 us)
Async XLA Ops:
  6.5 14.6 %copy-start.19 = (s32[1,4]{1,0:T(1,128)S(1)}, s32[1,4]{1,0:T(1,128)}, u32[]{:S(2)}) copy-start(s32[1,4]{1,0:T(1,128)} %param.17) | copy-start | bytes 52
  6.5 14.8 %copy-start.20 = (s32[1,4]{1,0:T(1,128)S(1)}, s32[1,4]{1,0:T(1,128)}, u32[]{:S(2)}) copy-start(s32[1,4]{1,0:T(1,128)} %param.16) | copy-start | bytes 52
  6.5 33.8 %all-gather.6.cloned.1.call-start = ((), (), s32[]{:S(2)}) async-start(), calls=%async_computation | async-start | bytes 1966080 | tf_op jit(solution)/shard_map/all_gather | solution.py:322
  7.8 31.6 %collective-permute-start = (bf16[256,1024]{1,0:T(8,128)(2,1)S(1)}, bf16[256,1024]{1,0:T(8,128)(2,1)S(1)}, u32[]{:S(2)}, u32[]{:S(2)}) collective-permute-start(bf16[256,1024]{1,0:T(8,128)(2,1)S(1)} %get-tuple-element.127), channel_id=1, source_target_pairs={{0,1},{1,2},{2,3},{3,0},{4,5},{5,6},{6,7},{7,4},{8,9},{9,10},{10,1... | collective-permute-start | bytes 1572872 | tf_op jit(solution)/shard_map/ppermute | solution.py:316
  10.9 141.1 %all-gather.8.cloned.1.call-start = ((), (), s32[]{:S(2)}) async-start(), calls=%async_computation.1 | async-start | bytes 5308416 | tf_op jit(solution)/shard_map/all_gather | solution.py:389
  15.7 23.7 %collective-permute-start.1 = (bf16[96,1024]{1,0:T(8,128)(2,1)}, bf16[96,1024]{1,0:T(8,128)(2,1)S(1)}, u32[]{:S(2)}, u32[]{:S(2)}) collective-permute-start(bf16[96,1024]{1,0:T(8,128)(2,1)} %get-tuple-element.130), channel_id=1, source_target_pairs={{0,1},{1,2},{2,3},{3,0},{4,5},{5,6},{6,7},{7,4},{8,9},{9,10},{10,1... | collective-permute-start | bytes 589832 | tf_op jit(solution)/shard_map/ppermute | solution.py:316
  17.2 22.1 %collective-permute-start.2 = (bf16[96,1024]{1,0:T(8,128)(2,1)S(1)}, bf16[96,1024]{1,0:T(8,128)(2,1)S(1)}, u32[]{:S(2)}, u32[]{:S(2)}) collective-permute-start(bf16[96,1024]{1,0:T(8,128)(2,1)S(1)} %get-tuple-element.129), channel_id=1, source_target_pairs={{0,2},{1,3},{2,0},{3,1},{4,6},{5,7},{6,4},{7,5},{8,10},{9,11},{10,... | collective-permute-start | bytes 589832 | tf_op jit(solution)/shard_map/ppermute | solution.py:316
  18.3 21.1 %collective-permute-start.3 = (bf16[96,1024]{1,0:T(8,128)(2,1)S(1)}, bf16[96,1024]{1,0:T(8,128)(2,1)S(1)}, u32[]{:S(2)}, u32[]{:S(2)}) collective-permute-start(bf16[96,1024]{1,0:T(8,128)(2,1)S(1)} %get-tuple-element.128), channel_id=1, source_target_pairs={{0,3},{1,0},{2,1},{3,2},{4,7},{5,4},{6,5},{7,6},{8,11},{9,8},{10,9... | collective-permute-start | bytes 589832 | tf_op jit(solution)/shard_map/ppermute | solution.py:316
  39.4 10.5 %copy-start.1 = (bf16[256,1024]{1,0:T(8,128)(2,1)}, bf16[256,1024]{1,0:T(8,128)(2,1)S(1)}, u32[]{:S(2)}) copy-start(bf16[256,1024]{1,0:T(8,128)(2,1)S(1)} %collective-permute-done.refs_0_) | copy-start | bytes 1572868
  46.8 28.6 %collective-permute-start.4 = (bf16[256,1024]{1,0:T(8,128)(2,1)S(1)}, bf16[256,1024]{1,0:T(8,128)(2,1)S(1)}, u32[]{:S(2)}, u32[]{:S(2)}) collective-permute-start(bf16[256,1024]{1,0:T(8,128)(2,1)S(1)} %collective-permute-done.refs_0_), channel_id=1, source_target_pairs={{0,1},{1,2},{2,3},{3,0},{4,5},{5,6},{6,7},{7,4},{8,9},{9,10},{10,1... | collective-permute-start | bytes 1572872 | tf_op jit(solution)/shard_map/ppermute | solution.py:316
  49.8 25.7 %collective-permute-start.5 = (bf16[256,1024]{1,0:T(8,128)(2,1)S(1)}, bf16[256,1024]{1,0:T(8,128)(2,1)S(1)}, u32[]{:S(2)}, u32[]{:S(2)}) collective-permute-start(bf16[256,1024]{1,0:T(8,128)(2,1)S(1)} %get-tuple-element.68), channel_id=1, source_target_pairs={{0,1},{1,2},{2,3},{3,0},{4,5},{5,6},{6,7},{7,4},{8,9},{9,10},{10,1... | collective-permute-start | bytes 1572872 | tf_op jit(solution)/shard_map/ppermute | solution.py:316
  49.9 36.1 %copy-start.17 = (f32[128,192]{1,0:T(8,128)S(1)}, f32[128,192]{1,0:T(8,128)}, u32[]{:S(2)}) copy-start(f32[128,192]{1,0:T(8,128)} %get-tuple-element.81) | copy-start | bytes 294916
  53.9 23.8 %collective-permute-start.6 = (f32[128,192]{1,0:T(8,128)S(1)}, f32[128,192]{1,0:T(8,128)S(1)}, u32[]{:S(2)}, u32[]{:S(2)}) collective-permute-start(f32[128,192]{1,0:T(8,128)S(1)} %copy-done.23), channel_id=1, source_target_pairs={{0,1},{1,2},{2,3},{3,0},{4,5},{5,6},{6,7},{7,4},{8,9},{9,10},{10,1... | collective-permute-start | bytes 294920 | tf_op jit(solution)/shard_map/ppermute | solution.py:316
  56.0 26.7 %collective-permute-start.7 = (f32[128,192]{1,0:T(8,128)S(1)}, f32[128,192]{1,0:T(8,128)S(1)}, u32[]{:S(2)}, u32[]{:S(2)}) collective-permute-start(f32[128,192]{1,0:T(8,128)S(1)} %copy-done.22), channel_id=1, source_target_pairs={{0,2},{1,3},{2,0},{3,1},{4,6},{5,7},{6,4},{7,5},{8,10},{9,11},{10,... | collective-permute-start | bytes 294920 | tf_op jit(solution)/shard_map/ppermute | solution.py:316
  58.2 24.4 %collective-permute-start.8 = (f32[128,192]{1,0:T(8,128)S(1)}, f32[128,192]{1,0:T(8,128)S(1)}, u32[]{:S(2)}, u32[]{:S(2)}) collective-permute-start(f32[128,192]{1,0:T(8,128)S(1)} %copy-done.21), channel_id=1, source_target_pairs={{0,3},{1,0},{2,1},{3,2},{4,7},{5,4},{6,5},{7,6},{8,11},{9,8},{10,9... | collective-permute-start | bytes 294920 | tf_op jit(solution)/shard_map/ppermute | solution.py:316
  75.5 18.8 %copy-start.2 = (bf16[256,1024]{1,0:T(8,128)(2,1)}, bf16[256,1024]{1,0:T(8,128)(2,1)S(1)}, u32[]{:S(2)}) copy-start(bf16[256,1024]{1,0:T(8,128)(2,1)S(1)} %collective-permute-done.4.refs_0_) | copy-start | bytes 1572868
  75.5 15.0 %copy-start.3 = (bf16[256,1024]{1,0:T(8,128)(2,1)}, bf16[256,1024]{1,0:T(8,128)(2,1)S(1)}, u32[]{:S(2)}) copy-start(bf16[256,1024]{1,0:T(8,128)(2,1)S(1)} %collective-permute-done.5.refs_0_) | copy-start | bytes 1572868
  82.6 31.3 %collective-permute-start.9 = (bf16[256,1024]{1,0:T(8,128)(2,1)S(1)}, bf16[256,1024]{1,0:T(8,128)(2,1)S(1)}, u32[]{:S(2)}, u32[]{:S(2)}) collective-permute-start(bf16[256,1024]{1,0:T(8,128)(2,1)S(1)} %collective-permute-done.4.refs_0_), channel_id=1, source_target_pairs={{0,1},{1,2},{2,3},{3,0},{4,5},{5,6},{6,7},{7,4},{8,9},{9,10},{10,1... | collective-permute-start | bytes 1572872 | tf_op jit(solution)/shard_map/ppermute | solution.py:316
  85.9 28.0 %collective-permute-start.10 = (bf16[256,1024]{1,0:T(8,128)(2,1)S(1)}, bf16[256,1024]{1,0:T(8,128)(2,1)S(1)}, u32[]{:S(2)}, u32[]{:S(2)}) collective-permute-start(bf16[256,1024]{1,0:T(8,128)(2,1)S(1)} %collective-permute-done.5.refs_0_), channel_id=1, source_target_pairs={{0,1},{1,2},{2,3},{3,0},{4,5},{5,6},{6,7},{7,4},{8,9},{9,10},{10,1... | collective-permute-start | bytes 1572872 | tf_op jit(solution)/shard_map/ppermute | solution.py:316
  86.0 26.3 %collective-permute-start.11 = (bf16[128,192]{1,0:T(8,128)(2,1)S(1)}, bf16[128,192]{1,0:T(8,128)(2,1)S(1)}, u32[]{:S(2)}, u32[]{:S(2)}) collective-permute-start(bf16[128,192]{1,0:T(8,128)(2,1)S(1)} %add_convert_fusion.refs_0_), channel_id=1, source_target_pairs={{0,1},{1,2},{2,3},{3,0},{4,5},{5,6},{6,7},{7,4},{8,9},{9,10},{10,1... | collective-permute-start | bytes 147464 | tf_op jit(solution)/shard_map/ppermute | solution.py:316
  88.0 25.9 %collective-permute-start.12 = (bf16[128,192]{1,0:T(8,128)(2,1)S(1)}, bf16[128,192]{1,0:T(8,128)(2,1)S(1)}, u32[]{:S(2)}, u32[]{:S(2)}) collective-permute-start(bf16[128,192]{1,0:T(8,128)(2,1)S(1)} %add_convert_fusion.refs_0_), channel_id=1, source_target_pairs={{0,2},{1,3},{2,0},{3,1},{4,6},{5,7},{6,4},{7,5},{8,10},{9,11},{10,... | collective-permute-start | bytes 147464 | tf_op jit(solution)/shard_map/ppermute | solution.py:316
  90.4 23.5 %collective-permute-start.13 = (bf16[128,192]{1,0:T(8,128)(2,1)S(1)}, bf16[128,192]{1,0:T(8,128)(2,1)S(1)}, u32[]{:S(2)}, u32[]{:S(2)}) collective-permute-start(bf16[128,192]{1,0:T(8,128)(2,1)S(1)} %add_convert_fusion.refs_0_), channel_id=1, source_target_pairs={{0,3},{1,0},{2,1},{3,2},{4,7},{5,4},{6,5},{7,6},{8,11},{9,8},{10,9... | collective-permute-start | bytes 147464 | tf_op jit(solution)/shard_map/ppermute | solution.py:316
  113.9 8.6 %copy-start.4 = (bf16[256,1024]{1,0:T(8,128)(2,1)}, bf16[256,1024]{1,0:T(8,128)(2,1)S(1)}, u32[]{:S(2)}) copy-start(bf16[256,1024]{1,0:T(8,128)(2,1)S(1)} %collective-permute-done.10.refs_0_) | copy-start | bytes 1572868
  113.9 21.4 %collective-permute-start.14 = (bf16[256,1024]{1,0:T(8,128)(2,1)S(1)}, bf16[256,1024]{1,0:T(8,128)(2,1)S(1)}, u32[]{:S(2)}, u32[]{:S(2)}) collective-permute-start(bf16[256,1024]{1,0:T(8,128)(2,1)S(1)} %collective-permute-done.10.refs_0_), channel_id=1, source_target_pairs={{0,1},{1,2},{2,3},{3,0},{4,5},{5,6},{6,7},{7,4},{8,9},{9,10},{10,1... | collective-permute-start | bytes 1572872 | tf_op jit(solution)/shard_map/ppermute | solution.py:316
  122.5 12.6 %collective-permute-start.15 = (bf16[256,512]{1,0:T(8,128)(2,1)}, bf16[256,512]{1,0:T(8,128)(2,1)S(1)}, u32[]{:S(2)}, u32[]{:S(2)}) collective-permute-start(bf16[256,512]{1,0:T(8,128)(2,1)} %get-tuple-element.96.attended_ref), channel_id=1, source_target_pairs={{0,1},{1,2},{2,3},{3,0},{4,5},{5,6},{6,7},{7,4},{8,9},{9,10},{10,1... | collective-permute-start | bytes 786440 | tf_op jit(solution)/shard_map/ppermute | solution.py:316
  135.2 16.9 %copy-start.11 = (bf16[256,512]{1,0:T(8,128)(2,1)}, bf16[256,512]{1,0:T(8,128)(2,1)S(1)}, u32[]{:S(2)}) copy-start(bf16[256,512]{1,0:T(8,128)(2,1)S(1)} %collective-permute-done.15.attended_ref) | copy-start | bytes 786436
  135.2 11.7 %collective-permute-start.17 = (bf16[256,512]{1,0:T(8,128)(2,1)S(1)}, bf16[256,512]{1,0:T(8,128)(2,1)S(1)}, u32[]{:S(2)}, u32[]{:S(2)}) collective-permute-start(bf16[256,512]{1,0:T(8,128)(2,1)S(1)} %collective-permute-done.15.attended_ref), channel_id=1, source_target_pairs={{0,1},{1,2},{2,3},{3,0},{4,5},{5,6},{6,7},{7,4},{8,9},{9,10},{10,1... | collective-permute-start | bytes 786440 | tf_op jit(solution)/shard_map/ppermute | solution.py:316
  142.9 9.2 %collective-permute-start.16 = (bf16[256,512]{1,0:T(8,128)(2,1)}, bf16[256,512]{1,0:T(8,128)(2,1)S(1)}, u32[]{:S(2)}, u32[]{:S(2)}) collective-permute-start(bf16[256,512]{1,0:T(8,128)(2,1)} %get-tuple-element.97.attended_ref), channel_id=1, source_target_pairs={{0,1},{1,2},{2,3},{3,0},{4,5},{5,6},{6,7},{7,4},{8,9},{9,10},{10,1... | collective-permute-start | bytes 786440 | tf_op jit(solution)/shard_map/ppermute | solution.py:316
  146.8 9.4 %copy-start.10 = (bf16[256,512]{1,0:T(8,128)(2,1)}, bf16[256,512]{1,0:T(8,128)(2,1)S(1)}, u32[]{:S(2)}) copy-start(bf16[256,512]{1,0:T(8,128)(2,1)S(1)} %collective-permute-done.17.attended_ref) | copy-start | bytes 786436
  152.1 9.7 %collective-permute-start.18 = (bf16[256,512]{1,0:T(8,128)(2,1)S(1)}, bf16[256,512]{1,0:T(8,128)(2,1)S(1)}, u32[]{:S(2)}, u32[]{:S(2)}) collective-permute-start(bf16[256,512]{1,0:T(8,128)(2,1)S(1)} %collective-permute-done.16.attended_ref), channel_id=1, source_target_pairs={{0,1},{1,2},{2,3},{3,0},{4,5},{5,6},{6,7},{7,4},{8,9},{9,10},{10,1... | collective-permute-start | bytes 786440 | tf_op jit(solution)/shard_map/ppermute | solution.py:316
  156.2 9.6 %collective-permute-start.19 = (bf16[256,512]{1,0:T(8,128)(2,1)S(1)}, bf16[256,512]{1,0:T(8,128)(2,1)S(1)}, u32[]{:S(2)}, u32[]{:S(2)}) collective-permute-start(bf16[256,512]{1,0:T(8,128)(2,1)S(1)} %collective-permute-done.17.attended_ref), channel_id=1, source_target_pairs={{0,1},{1,2},{2,3},{3,0},{4,5},{5,6},{6,7},{7,4},{8,9},{9,10},{10,1... | collective-permute-start | bytes 786440 | tf_op jit(solution)/shard_map/ppermute | solution.py:316
  165.9 12.7 %collective-permute-start.20 = (bf16[256,512]{1,0:T(8,128)(2,1)S(1)}, bf16[256,512]{1,0:T(8,128)(2,1)S(1)}, u32[]{:S(2)}, u32[]{:S(2)}) collective-permute-start(bf16[256,512]{1,0:T(8,128)(2,1)S(1)} %collective-permute-done.18.attended_ref), channel_id=1, source_target_pairs={{0,1},{1,2},{2,3},{3,0},{4,5},{5,6},{6,7},{7,4},{8,9},{9,10},{10,1... | collective-permute-start | bytes 786440 | tf_op jit(solution)/shard_map/ppermute | solution.py:316
  (15 other events, 65.7 us)
Sparse Core Ops, SparseCore 0:
  11.1 20.2 all-gather.5
  46.9 43.0 all-gather.7

commit v14 on v12

--- a/solution.py
+++ b/solution.py
@@ -48,20 +48,8 @@
         acc_ref[:, columns] = total if first is None else first[:, columns] + total
 
 
-def project_kernel(shards, begun, ids_ref, *refs):
-    token_refs, w_ref, rest = refs[:shards], refs[shards], refs[shards + 1 :]
-    acc_ref = rest[-1]
-    step = pl.program_id(0)
-    for number, token_ref in enumerate(token_refs):
-        first = acc_ref if number else (rest[0] if begun else None)
-        pl.when(step == number)(
-            functools.partial(accumulate, acc_ref, token_ref, w_ref, first)
-        )
-
-
-def shard_spec(weight, depth, number=0):
-    slots, _, head_size = weight.shape
-    return pl.BlockSpec((slots, depth, head_size), lambda step, ids: (0, ids[number], 0))
+def project_kernel(begun, ids_ref, token_ref, w_ref, *refs):
+    accumulate(refs[-1], token_ref, w_ref, refs[0] if begun else None)
 
 
 def rows_spec(array, rows, part):
@@ -70,17 +58,16 @@
     return pl.BlockSpec((rows, array.shape[1]), lambda step, ids: (part, 0))
 
 
-def project(ids, tokens, weight, begun=(), part=0):
-    rows, depth = tokens.shape
+def project(ids, tokens, weight, begun=()):
     slots, _, head_size = weight.shape
     return call(
-        functools.partial(project_kernel, 1, len(begun)),
+        functools.partial(project_kernel, len(begun)),
         "project",
         ids,
         1,
-        [None, shard_spec(weight, depth)] + [rows_spec(array, rows, part) for array in begun],
+        [None] * (2 + len(begun)),
         [tokens, weight, *begun],
-        jax.ShapeDtypeStruct((rows, slots * head_size), jnp.float32),
+        jax.ShapeDtypeStruct((tokens.shape[0], slots * head_size), jnp.float32),
     )
 
 
@@ -145,14 +132,13 @@
 
 
 def attend(planes_of, adapters, part, table, turn, up, shrink, tokens, weight, begun, earlier):
-    rows, depth = tokens.shape
+    rows = tokens.shape[0] // 2
     slots, _, head_size = weight.shape
     planes = len(shrink)
     arrays = [table, turn, up, *shrink, tokens, weight, begun, *earlier]
     specs = [None] * len(arrays)
-    for index in (0, 1):
+    for index in (0, 1, 3 + planes, 5 + planes):
         specs[index] = rows_spec(arrays[index], rows, part)
-    specs[4 + planes] = shard_spec(weight, depth, planes - 1)
     return call(
         functools.partial(attend_kernel, planes, len(earlier) // 2),
         "attend",
@@ -223,12 +209,12 @@
     attended = attended_ref[...]
     features = attended.shape[1]
     if lines:
-        weight = jnp.concatenate([w_ref[i, 0, lines:] for i in range(w_ref.shape[0])], axis=0)
+        weight = jnp.concatenate([w_ref[i, lines:] for i in range(w_ref.shape[0])], axis=0)
     else:
         weight = w_ref[...]
     downs = []
     for j in range(count):
-        down = down_ref[ids_ref[1 + j], 0] if lines else down_ref[ids_ref[1 + j]]
+        down = down_ref[ids_ref[1 + j]]
         downs += [down[:, at : at + features] for at in range(0, down.shape[1], features)]
     down = jnp.concatenate(downs, axis=0)
     rank = down.shape[0] // count
@@ -254,38 +240,31 @@
         low_ref[...] = low
 
 
-def project_out(ids, rank, attended, weight, down, begun, final, turn=None, part=0):
+def project_out(ids, rank, attended, weight, down, begun, final, part=0):
     rows, features = attended.shape
     columns = weight.shape[-1]
-    if turn is None:
-        specs, down_rows = [None, None, None], 0
+    if len(weight.shape) == 2:
+        down_spec, down_rows = None, 0
     else:
         down_rows = rank * features // columns
-        specs = [
-            None,
-            pl.BlockSpec(
-                (weight.shape[0], 1) + weight.shape[2:], lambda step, ids: (0, turn - 1, 0, 0)
-            ),
-            pl.BlockSpec(
-                (down, 1, down_rows, columns),
-                lambda step, ids: (ids[0], turn - 1, 0, 0),
-            ),
-        ]
+        down_spec = pl.BlockSpec(
+            (down, down_rows, columns), lambda step, ids: (ids[0], 0, 0)
+        )
         down = weight
     sums = (
         jax.ShapeDtypeStruct((rows, columns), jnp.float32),
         jax.ShapeDtypeStruct((rows, (ids.shape[0] - 1) * rank), jnp.float32),
     )
+    all_rows = rows + sum(item.shape[0] for item in final[2:])
     return call(
         functools.partial(output_kernel, len(begun), bool(final), down_rows),
         "project_out",
         ids,
         1,
-        specs + [None] * len(begun) + [rows_spec(table, rows, part) for table in final[:1]]
-        + [None] * len(final[1:]),
+        [None, None, down_spec] + [None] * len(begun)
+        + [rows_spec(table, rows, part) for table in final[:1]] + [None] * len(final[1:]),
         [attended, weight, down, *begun, *final],
-        jax.ShapeDtypeStruct((rows + sum(item.shape[0] for item in final[2:]), columns), jnp.bfloat16)
-        if final else sums,
+        jax.ShapeDtypeStruct((all_rows, columns), jnp.bfloat16) if final else sums,
     )
 
 
@@ -315,9 +294,7 @@
     def turned(value, turn=1):
         return lax.ppermute(value, "tensor", [(i, (i + turn) % planes) for i in range(planes)])
 
-    half_rows = token_rows // 2
-    held = [[tokens[:half_rows]], [tokens[half_rows:]]]
-    held[0].append(turned(held[0][0]))
+    held = [tokens, turned(tokens)]
     weight = jnp.transpose(query_key_value_weight, (1, 0, 2))
     down_all = lax.all_gather(adapter_down_maps, "dp", axis=0, tiled=True)
     up_all = lax.all_gather(jnp.transpose(adapter_up_maps[0], (1, 0, 2)), "dp", axis=0)
@@ -362,51 +339,46 @@
         for k in range(1, planes)
     ]
 
+    def shard(number):
+        start = planes_of[number] * depth
+        return lax.dynamic_slice_in_dim(weight, start, depth, axis=1)
+
     lines = [turned(send, k) for k, send in enumerate(sends, 1)]
-    begun = project(planes_of[:1], tokens, weight)
-
-    done = lax.optimization_barrier(
-        (held[0][1], held[1][0], lines, begun, table, turn, up_all, own_rows)
-    )
-    held[0][1], held[1][0], lines, begun, table, turn, up_all, own_rows = done
+    begun = project(planes_of[:1], tokens, shard(0))
+    done = (held[1], lines, begun, table, turn, up_all, own_rows, shard(1))
+    done = lax.optimization_barrier(done)
+    held[1], lines, begun, table, turn, up_all, own_rows, part_weight = done
     lines = lax.all_gather(jnp.stack(lines), PLANE, axis=0)
-    begun = [begun, begun]
     for step in range(2, planes):
-        for part in range(2):
-            held[part].append(turned(held[part][-1]))
-            number = step - 1 - part
-            if number > 0:
-                begun[part] = project(
-                    planes_of[number : number + 1], held[part][number], weight, [begun[part]], part
-                )
+        arrived = held[-1]
+        held.append(turned(arrived))
+        begun = project(planes_of[step - 1 : step], arrived, part_weight, [begun])
+        side = ()
         if step == 2:
-            sums = shrink_partial(adapters, here, planes, table, after(tokens, held[0][1]), down_all)
-            side = [sums[0]] + [turned(sums[k], k) for k in range(1, planes)]
-            out_up_all = lax.all_gather(
-                after(output_up_maps, held[0][1]), "dp", axis=0, tiled=True
+            sums = shrink_partial(adapters, here, planes, table, after(tokens, arrived), down_all)
+            sums = [sums[0]] + [turned(sums[k], k) for k in range(1, planes)]
+            side = (
+                sums,
+                lax.all_gather(after(output_up_maps, sums[0]), "dp", axis=0, tiled=True),
+                lax.all_gather(after(out_down, sums[0]), "dp", axis=0),
             )
-            own_down = lax.all_gather(after(out_down, held[0][1]), "dp", axis=0)
-            side = (side, out_up_all, own_down)
         elif step == 3:
-            shrink = sum(side[1:], side[0]).astype(jnp.bfloat16)
-            side = [shrink] + [turned(shrink, k) for k in range(1, planes)]
-        held[0][-1], held[1][-1], begun, side = lax.optimization_barrier(
-            (held[0][-1], held[1][-1], begun, side)
-        )
+            shrink = sum(sums[1:], sums[0]).astype(jnp.bfloat16)
+            shrink = [shrink] + [turned(shrink, k) for k in range(1, planes)]
+            side = (shrink, [lines[:, k] for k in range(planes - 1)])
+        done = lax.optimization_barrier((held[-1], begun, shard(step), side))
+        held[-1], begun, part_weight, side = done
         if step == 2:
-            side, out_up_all, own_down = side
-    shrink = side
-    held[1].append(turned(held[1][-1]))
-    begun[1] = project(
-        planes_of[planes - 2 : planes - 1], held[1][planes - 2], weight, [begun[1]], 1
-    )
+            sums, out_up_all, own_down = side
+        elif step == 3:
+            shrink, lines = side
 
     ids = jnp.concatenate([lax.axis_index("groups")[None], adapters])
     attended, earlier = [[], []], ()
     for part in range(2):
         made, *earlier = attend(
-            planes_of, adapters, part, table, turn, up_all, shrink, held[part][-1], weight,
-            begun[part], earlier,
+            planes_of, adapters, part, table, turn, up_all, shrink, held[-1], part_weight,
+            begun, earlier,
         )
         attended[part] = [made, turned(after(made, *attended[0][1:]))]
     sums = [
@@ -417,11 +389,11 @@
         for part in range(2):
             arrived = attended[part][-1]
             if step < planes:
-                ahead = attended[0][step:]
+                ahead = [*attended[0][step:], *sums[part]]
                 attended[part].append(turned(after(arrived, *ahead)))
             final = [] if step < planes else [table, out_up_all, *before]
             sums[part] = project_out(
-                ids, rank, arrived, lines, pool, list(sums[part]), final, step - 1, part
+                ids, rank, arrived, lines[step - 2], pool, list(sums[part]), final, part
             )
             if final:
                 before = [sums[part]]

time: 184 us -> 180 us (0.978)
  local copies, waits for them, and re-layouts: 30.8 us -> 22.3 us
  waiting for transfers between devices: 49.2 us -> 54 us
  between operations: 13.9 us -> 16.3 us
  blocking collectives: 25 us -> 23.1 us
    unnamed x56 -> x34, local copies, waits for them, and re-layouts: 21.2 us -> 5.62 us
    dynamic_slice x0 -> x1, local copies, waits for them, and re-layouts: none -> 5.11 us  [shard(): return lax.dynamic_slice_in_dim(weight, start, depth, axis=1)]
    ppermute x21 -> x18, waiting for transfers between devices: 49.2 us -> 54 us  [turned(): lax.ppermute(value, 'tensor', [(i, (i + turn) % planes) for i in range(pl...]
    squeeze x0 -> x1, local copies, waits for them, and re-layouts: none -> 3.2 us  [local(): side = (shrink, [lines[:, k] for k in range(planes - 1)])]
    slice x2 -> x1, local copies, waits for them, and re-layouts: 2.89 us -> 0.64 us  [shard(): start = planes_of[number] * depth]
    all_gather x2, blocking collectives: 18.1 us -> 16.2 us  [the longest x1 8.11 us: local(): lax.all_gather(after(output_up_maps, sums[0]), 'dp', axis=0, tiled=True)]
    pallas_call x16 -> x14, Pallas kernels: 30.8 us -> 29 us  [call(): pl.pallas_call(kernel, out_shape=out, grid_spec=pltpu.PrefetchScalarGridS...]
    ppermute x21 -> x18, starting transfers between devices: 28.9 us -> 28.8 us  [turned(): lax.ppermute(value, 'tensor', [(i, (i + turn) % planes) for i in range(pl...]
  transfers between devices with their start and end apart: 23 -> 20, of which waited for: 8 -> 10; matrix products, arithmetic and copies ran while one was open for 7% -> 12% of each run, Pallas kernels for 15% -> 13%
where the time goes in v14:
time: 180 us; the launch traced here: 179 us
  waiting for transfers between devices  54 us (30%)
  Pallas kernels  29 us (16%)
  starting transfers between devices  28.9 us (16%)
  blocking collectives  23.1 us (13%)
  local copies, waits for them, and re-layouts  22.3 us (12%)
  between operations  16.3 us (9%)
  other arithmetic  5.53 us (3%)
    ppermute x18, waiting for transfers between devices, turned(): lax.ppermute(value, 'tensor', [(i, (i + turn) % planes) for i in range(pl...  54 us
    pallas_call x14, Pallas kernels, call(): pl.pallas_call(kernel, out_shape=out, grid_spec=pltpu.PrefetchScalarGridS...  29 us
    ppermute x18, starting transfers between devices, turned(): lax.ppermute(value, 'tensor', [(i, (i + turn) % planes) for i in range(pl...  28.8 us
    all_gather x1, blocking collectives, local(): lax.all_gather(after(output_up_maps, sums[0]), 'dp', axis=0, tiled=True)  8.11 us
    all_gather x1, blocking collectives, local(): lax.all_gather(after(out_down, sums[0]), 'dp', axis=0)  8.08 us
    all_gather x1, blocking collectives, local(): lax.all_gather(jnp.transpose(adapter_up_maps[0], (1, 0, 2)), 'dp', axis=0)  6.88 us
    unnamed x34, local copies, waits for them, and re-layouts  5.62 us
    dynamic_slice x1, local copies, waits for them, and re-layouts, shard(): return lax.dynamic_slice_in_dim(weight, start, depth, axis=1)  5.11 us
  transfers between devices with their start and end apart: 20, of which 10 were waited for; matrix products, arithmetic and copies ran while one was open for 12% of the time, Pallas kernels for 13%

profile of v14, /device:TPU:0, one launch (start us, length us, event | category | flops | bytes accessed | tf_op | source)
XLA Modules:
  0.0 179.1 jit_solution(1573894995946794942)
XLA Ops:
  6.5 3.0 %collective-permute-start = (bf16[512,1024]{1,0:T(8,128)(2,1)}, bf16[512,1024]{1,0:T(8,128)(2,1)}, u32[]{:S(2)}, u32[]{:S(2)}) collective-permute-start(bf16[512,1024]{1,0:T(8,128)(2,1)} %token_ref.2), channel_id=1, source_target_pairs={{0,1},{1,2},{2,3},{3,0},{4,5},{5,6},{6,7},{7,4},{8,9},{9,10},{10,1... | collective-permute-start | bytes 3145736 | tf_op jit(solution)/shard_map/ppermute | solution.py:295
  10.6 2.8 %fusion.4 = (bf16[64,1,1024]{2,1,0:T(2,128)(2,1)S(1)}, bf16[64,1,1024]{2,1,0:T(2,128)(2,1)S(1)}, bf16[64,1,1024]{2,1,0:T(2,128)(2,1)S(1)}) fusion(bf16[128,4,4096]{2,1,0:T(4,128)(2,1)} %param.11, s32[]{:T(128)S(6)} %select_n.76, s32[]{:T(128)S(6)} %select_n.79, s32[]{:T(128)S(6)} %select_n.88, s32[]{:T(128)S(6)} %select_n.85, s32[]{:T(128)S(6)} %select_n.82), kind=kLoop, calls=%fused_computation.39 | loop fusion | bytes 786452 | tf_op jit(solution)/shard_map/dynamic_slice | solution.py:335
  16.0 1.7 collective-permute-start.2
  17.7 2.2 %collective-permute-start.3 = (bf16[96,1024]{1,0:T(8,128)(2,1)}, bf16[96,1024]{1,0:T(8,128)(2,1)}, u32[]{:S(2)}, u32[]{:S(2)}) collective-permute-start(bf16[96,1024]{1,0:T(8,128)(2,1)} %get-tuple-element.129), channel_id=1, source_target_pairs={{0,3},{1,0},{2,1},{3,2},{4,7},{5,4},{6,5},{7,6},{8,11},{9,8},{10,9... | collective-permute-start | bytes 589832 | tf_op jit(solution)/shard_map/ppermute | solution.py:295
  21.0 2.6 %dynamic-slice_bitcast_fusion.4 = bf16[4,128,1024]{2,0,1:T(4,128)(2,1)} fusion(bf16[128,4,4096]{2,1,0:T(4,128)(2,1)} %param.11, s32[]{:T(128)S(6)} %select_n.91), kind=kLoop, calls=%fused_computation.7 | loop fusion | bytes 2097156 | tf_op jit(solution)/shard_map/transpose | solution.py:320
  27.0 5.1 %dynamic-slice_bitcast_fusion = (bf16[6,1024,128]{2,1,0:T(8,128)(2,1)S(1)}, bf16[6,1024,128]{2,1,0:T(8,128)(2,1)}, bf16[6,1024,128]{2,1,0:T(8,128)(2,1)S(1)}, bf16[6,1024,128]{2,1,0:T(8,128)(2,1)}) fusion(bf16[4096,6,128]{2,0,1:T(8,128)(2,1)} %param.10, s32[]{:T(128)S(6)} %select_n.94, s32[]{:T(128)S(6)} %select_n.92, s32[]{:T(128)S(6)} %select_n.89, ...), kind=kLoop, calls=%fused_computation.3 | loop fusion | bytes 12582928 | tf_op jit(solution)/shard_map/dynamic_slice | solution.py:344
  36.4 6.9 %all-gather = bf16[24,64,128]{2,1,0:T(8,128)(2,1)} all-gather(bf16[6,64,128]{2,1,0:T(8,128)(2,1)S(1)} %bitcast.70), channel_id=2, replica_groups=mesh['groups'=2,'dp'=4,'tensor'=4] {'dp'}, dimensions={0}, use_global_device_ids=true | all-gather | bytes 491520 | tf_op jit(solution)/shard_map/all_gather | solution.py:300
  43.2 4.6 %collective-permute-done.2 = bf16[96,1024]{1,0:T(8,128)(2,1)} collective-permute-done((bf16[96,1024]{1,0:T(8,128)(2,1)}, bf16[96,1024]{1,0:T(8,128)(2,1)}, u32[]{:S(2)}, u32[]{:S(2)}) %collective-permute-start.2) | collective-permute-done | bytes 196640 | tf_op jit(solution)/shard_map/ppermute | solution.py:295
  47.8 1.9 %pad_maximum_fusion = bf16[3,96,1024]{2,1,0:T(8,128)(2,1)} fusion(bf16[1,96,1024]{2,1,0:T(8,128)(2,1)} %bitcast.26, bf16[1,96,1024]{2,1,0:T(8,128)(2,1)} %bitcast.25, bf16[1,96,1024]{2,1,0:T(8,128)(2,1)S(1)} %bitcast.67), kind=kLoop, calls=%fused_computation.8 | loop fusion | flops 589824 | bytes 1179648 | tf_op jit(solution)/shard_map/stack | solution.py:351
  49.8 4.7 %collective-permute-start.4 = (bf16[512,1024]{1,0:T(8,128)(2,1)}, bf16[512,1024]{1,0:T(8,128)(2,1)}, u32[]{:S(2)}, u32[]{:S(2)}) collective-permute-start(bf16[512,1024]{1,0:T(8,128)(2,1)} %collective-permute-done.token_ref), channel_id=1, source_target_pairs={{0,1},{1,2},{2,3},{3,0},{4,5},{5,6},{6,7},{7,4},{8,9},{9,10},{10,1... | collective-permute-start | bytes 3145736 | tf_op jit(solution)/shard_map/ppermute | solution.py:295
  56.2 2.8 %project.4.refs_0_ = f32[512,768]{1,0:T(8,128)S(1)} custom-call(s32[1]{0:T(128)} %get-tuple-element.139.ids_ref, bf16[512,1024]{1,0:T(8,128)(2,1)} %collective-permute-done.token_ref, bf16[6,1024,128]{2,1,0:T(8,128)(2,1)S(1)} %copy-done.4, f32[512,768]{1,0:T(8,128)S(1)} %project.3.refs_0_), custom_call_target="tpu_custom_call" | custom-call | bytes 12582912 | tf_op jit(solution)/shard_map/project/pallas_call | solution.py:26
  63.0 2.7 %shrink.1 = (f32[128,192]{1,0:T(8,128)S(1)}, f32[128,192]{1,0:T(8,128)S(1)}, f32[128,192]{1,0:T(8,128)S(1)}, f32[128,192]{1,0:T(8,128)S(1)}) custom-call(s32[5]{0:T(128)S(1)} %pad_add_fusion.3.ids_ref, s32[512,2]{1,0:T(8,128)S(1)} %copy.47.table_ref.refs_2_, bf16[512,1024]{1,0:T(8,128)(2,1)S(1)} %copy-done.8, bf16[4,192,1024]{2,1,0:T(8,128)(2,1)S(1)} %copy-done.11), custom_call_target="tpu_custom_call" | custom-call | bytes 7876608 | tf_op jit(solution)/shard_map/shrink/pallas_call | solution.py:26
  67.4 2.8 %collective-permute-start.7 = (f32[128,192]{1,0:T(8,128)S(1)}, f32[128,192]{1,0:T(8,128)S(1)}, u32[]{:S(2)}, u32[]{:S(2)}) collective-permute-start(f32[128,192]{1,0:T(8,128)S(1)} %get-tuple-element.72), channel_id=1, source_target_pairs={{0,3},{1,0},{2,1},{3,2},{4,7},{5,4},{6,5},{7,6},{8,11},{9,8},{10,9... | collective-permute-start | bytes 294920 | tf_op jit(solution)/shard_map/ppermute | solution.py:295
  70.3 8.1 %all_gather.27.refs_3_ = bf16[4,64,1024]{2,1,0:T(8,128)(2,1)} all-gather(bf16[1,64,1024]{2,1,0:T(8,128)(2,1)} %param.15), channel_id=1, replica_groups=mesh['groups'=2,'dp'=4,'tensor'=4] {'dp'}, dimensions={0}, use_global_device_ids=true | all-gather | bytes 655360 | tf_op jit(solution)/shard_map/all_gather | solution.py:362
  78.4 8.1 %all-gather.1 = bf16[128,1024]{1,0:T(8,128)(2,1)} all-gather(bf16[32,1024]{1,0:T(8,128)(2,1)S(1)} %bitcast_dynamic-update-slice_fusion), channel_id=3, replica_groups=mesh['groups'=2,'dp'=4,'tensor'=4] {'dp'}, dimensions={0}, use_global_device_ids=true | all-gather | bytes 327680 | tf_op jit(solution)/shard_map/all_gather | solution.py:363
  86.6 3.3 %collective-permute-start.8 = (bf16[512,1024]{1,0:T(8,128)(2,1)}, bf16[512,1024]{1,0:T(8,128)(2,1)}, u32[]{:S(2)}, u32[]{:S(2)}) collective-permute-start(bf16[512,1024]{1,0:T(8,128)(2,1)} %collective-permute-done.4.token_ref), channel_id=1, source_target_pairs={{0,1},{1,2},{2,3},{3,0},{4,5},{5,6},{6,7},{7,4},{8,9},{9,10},{10,1... | collective-permute-start | bytes 3145736 | tf_op jit(solution)/shard_map/ppermute | solution.py:295
  90.1 2.4 %collective-permute-start.10 = (bf16[128,192]{1,0:T(8,128)(2,1)S(1)}, bf16[128,192]{1,0:T(8,128)(2,1)}, u32[]{:S(2)}, u32[]{:S(2)}) collective-permute-start(bf16[128,192]{1,0:T(8,128)(2,1)S(1)} %add_convert_fusion.refs_0_), channel_id=1, source_target_pairs={{0,2},{1,3},{2,0},{3,1},{4,6},{5,7},{6,4},{7,5},{8,10},{9,11},{10,... | collective-permute-start | bytes 147464 | tf_op jit(solution)/shard_map/ppermute | solution.py:295
  92.5 2.8 %collective-permute-start.11 = (bf16[128,192]{1,0:T(8,128)(2,1)S(1)}, bf16[128,192]{1,0:T(8,128)(2,1)}, u32[]{:S(2)}, u32[]{:S(2)}) collective-permute-start(bf16[128,192]{1,0:T(8,128)(2,1)S(1)} %add_convert_fusion.refs_0_), channel_id=1, source_target_pairs={{0,3},{1,0},{2,1},{3,2},{4,7},{5,4},{6,5},{7,6},{8,11},{9,8},{10,9... | collective-permute-start | bytes 147464 | tf_op jit(solution)/shard_map/ppermute | solution.py:295
  95.3 2.8 %project.5.refs_6_ = f32[512,768]{1,0:T(8,128)S(1)} custom-call(s32[1]{0:T(128)} %get-tuple-element.138.ids_ref, bf16[512,1024]{1,0:T(8,128)(2,1)} %collective-permute-done.4.token_ref, bf16[6,1024,128]{2,1,0:T(8,128)(2,1)S(1)} %copy-done.3, f32[512,768]{1,0:T(8,128)S(1)} %copy-done.2), custom_call_target="tpu_custom_call" | custom-call | bytes 12582912 | tf_op jit(solution)/shard_map/project/pallas_call | solution.py:26
  98.2 3.2 %slice_bitcast_fusion = (bf16[8,96,1024]{2,1,0:T(8,128)(2,1)S(1)}, bf16[8,96,1024]{2,1,0:T(8,128)(2,1)S(1)}, bf16[8,96,1024]{2,1,0:T(8,128)(2,1)S(1)}) fusion(bf16[8,3,96,1024]{3,2,1,0:T(8,128)(2,1)} %bitcast.65), kind=kLoop, calls=%fused_computation | loop fusion | bytes 9437184 | tf_op jit(solution)/shard_map/squeeze | solution.py:368
  101.4 16.0 %collective-permute-done.9.refs_1_ = bf16[128,192]{1,0:T(8,128)(2,1)S(1)} collective-permute-done((bf16[128,192]{1,0:T(8,128)(2,1)S(1)}, bf16[128,192]{1,0:T(8,128)(2,1)S(1)}, u32[]{:S(2)}, u32[]{:S(2)}) %collective-permute-start.9) | collective-permute-done | bytes 49184 | tf_op jit(solution)/shard_map/ppermute | solution.py:295
  117.5 1.7 collective-permute-done.10.refs_2_
  119.2 4.2 %attend.2 = (bf16[256,512]{1,0:T(8,128)(2,1)S(1)}, bf16[256,128]{1,0:T(8,128)(2,1)S(1)}, bf16[256,128]{1,0:T(8,128)(2,1)S(1)}) custom-call(s32[8]{0:T(128)S(1)} %pad_add_fusion.2.ids_ref, s32[512,2]{1,0:T(8,128)S(1)} %copy.47.table_ref.refs_2_, f32[512,256]{1,0:T(8,128)S(1)} %copy-done.6, bf16[4,6,64,128]{3,2,1,0:T(8,128)(2,1)S(1)} %bitcast.61, ...), custom_call_target="tpu_custom_call" | custom-call | bytes 15937536 | tf_op jit(solution)/shard_map/attend/pallas_call | solution.py:26
  123.4 1.9 %collective-permute-start.12 = (bf16[256,512]{1,0:T(8,128)(2,1)S(1)}, bf16[256,512]{1,0:T(8,128)(2,1)S(1)}, u32[]{:S(2)}, u32[]{:S(2)}) collective-permute-start(bf16[256,512]{1,0:T(8,128)(2,1)S(1)} %get-tuple-element.95.attended_ref), channel_id=1, source_target_pairs={{0,1},{1,2},{2,3},{3,0},{4,5},{5,6},{6,7},{7,4},{8,9},{9,10},{10,1... | collective-permute-start | bytes 786440 | tf_op jit(solution)/shard_map/ppermute | solution.py:295
  125.4 4.9 %attend.3 = (bf16[256,512]{1,0:T(8,128)(2,1)S(1)}, bf16[256,128]{1,0:T(8,128)(2,1)}, bf16[256,128]{1,0:T(8,128)(2,1)}) custom-call(s32[8]{0:T(128)S(1)} %pad_add_fusion.2.ids_ref, s32[512,2]{1,0:T(8,128)S(1)} %copy.47.table_ref.refs_2_, f32[512,256]{1,0:T(8,128)S(1)} %copy-done.6, bf16[4,6,64,128]{3,2,1,0:T(8,128)(2,1)S(1)} %bitcast.62, ...), custom_call_target="tpu_custom_call" | custom-call | bytes 16330752 | tf_op jit(solution)/shard_map/attend/pallas_call | solution.py:26
  131.4 2.0 %collective-permute-done.12.attended_ref = bf16[256,512]{1,0:T(8,128)(2,1)S(1)} collective-permute-done((bf16[256,512]{1,0:T(8,128)(2,1)S(1)}, bf16[256,512]{1,0:T(8,128)(2,1)S(1)}, u32[]{:S(2)}, u32[]{:S(2)}) %collective-permute-start.12) | collective-permute-done | bytes 262176 | tf_op jit(solution)/shard_map/ppermute | solution.py:295
  136.0 8.5 %collective-permute-done.13.attended_ref = bf16[256,512]{1,0:T(8,128)(2,1)S(1)} collective-permute-done((bf16[256,512]{1,0:T(8,128)(2,1)S(1)}, bf16[256,512]{1,0:T(8,128)(2,1)S(1)}, u32[]{:S(2)}, u32[]{:S(2)}) %collective-permute-start.13) | collective-permute-done | bytes 262176 | tf_op jit(solution)/shard_map/ppermute | solution.py:295
  144.4 3.6 %collective-permute-done.14.attended_ref = bf16[256,512]{1,0:T(8,128)(2,1)S(1)} collective-permute-done((bf16[256,512]{1,0:T(8,128)(2,1)S(1)}, bf16[256,512]{1,0:T(8,128)(2,1)S(1)}, u32[]{:S(2)}, u32[]{:S(2)}) %collective-permute-start.14) | collective-permute-done | bytes 262176 | tf_op jit(solution)/shard_map/ppermute | solution.py:295
  149.2 9.9 %collective-permute-done.15.attended_ref = bf16[256,512]{1,0:T(8,128)(2,1)S(1)} collective-permute-done((bf16[256,512]{1,0:T(8,128)(2,1)S(1)}, bf16[256,512]{1,0:T(8,128)(2,1)S(1)}, u32[]{:S(2)}, u32[]{:S(2)}) %collective-permute-start.15) | collective-permute-done | bytes 262176 | tf_op jit(solution)/shard_map/ppermute | solution.py:295
  159.0 2.8 %collective-permute-done.16.attended_ref = bf16[256,512]{1,0:T(8,128)(2,1)S(1)} collective-permute-done((bf16[256,512]{1,0:T(8,128)(2,1)S(1)}, bf16[256,512]{1,0:T(8,128)(2,1)S(1)}, u32[]{:S(2)}, u32[]{:S(2)}) %collective-permute-start.16) | collective-permute-done | bytes 262176 | tf_op jit(solution)/shard_map/ppermute | solution.py:295
  165.3 4.7 %collective-permute-done.17.attended_ref = bf16[256,512]{1,0:T(8,128)(2,1)S(1)} collective-permute-done((bf16[256,512]{1,0:T(8,128)(2,1)S(1)}, bf16[256,512]{1,0:T(8,128)(2,1)S(1)}, u32[]{:S(2)}, u32[]{:S(2)}) %collective-permute-start.17) | collective-permute-done | bytes 262176 | tf_op jit(solution)/shard_map/ppermute | solution.py:295
  170.0 2.2 %project_out.15 = bf16[512,1024]{1,0:T(8,128)(2,1)} custom-call(s32[5]{0:T(128)S(1)} %pad_add_fusion.1.ids_ref, bf16[256,512]{1,0:T(8,128)(2,1)S(1)} %collective-permute-done.17.attended_ref, bf16[8,96,1024]{2,1,0:T(8,128)(2,1)S(1)} %get-tuple-element.112.w_ref.down_ref, bf16[8,96,1024]{2,1,0:T(8,128)(2,1)S(1)} %get-tuple-element.112.w_ref.down_ref, ...), custom_call_target="tpu_custom_call" | custom-call | bytes 17313792 | tf_op jit(solution)/shard_map/project_out/pallas_call | solution.py:26
  (90 shorter events, 25.6 us)
Async XLA Ops:
  6.5 53.7 %all-gather.6.cloned.1.call-start = ((), (), s32[]{:S(2)}) async-start(), calls=%async_computation | async-start | bytes 1966080 | tf_op jit(solution)/shard_map/all_gather | solution.py:299
  6.5 41.3 %collective-permute-start = (bf16[512,1024]{1,0:T(8,128)(2,1)}, bf16[512,1024]{1,0:T(8,128)(2,1)}, u32[]{:S(2)}, u32[]{:S(2)}) collective-permute-start(bf16[512,1024]{1,0:T(8,128)(2,1)} %token_ref.2), channel_id=1, source_target_pairs={{0,1},{1,2},{2,3},{3,0},{4,5},{5,6},{6,7},{7,4},{8,9},{9,10},{10,1... | collective-permute-start | bytes 3145736 | tf_op jit(solution)/shard_map/ppermute | solution.py:295
  9.6 88.6 %all-gather.8.cloned.1.call-start = ((), (), s32[]{:S(2)}) async-start(), calls=%async_computation.1 | async-start | bytes 5308416 | tf_op jit(solution)/shard_map/all_gather | solution.py:351
  10.6 9.4 %copy-start.14 = (s32[1,4]{1,0:T(1,128)S(1)}, s32[1,4]{1,0:T(1,128)}, u32[]{:S(2)}) copy-start(s32[1,4]{1,0:T(1,128)} %param.17) | copy-start | bytes 52
  10.6 9.6 %copy-start.15 = (s32[1,4]{1,0:T(1,128)S(1)}, s32[1,4]{1,0:T(1,128)}, u32[]{:S(2)}) copy-start(s32[1,4]{1,0:T(1,128)} %param.16) | copy-start | bytes 52
  14.4 28.8 %collective-permute-start.1 = (bf16[96,1024]{1,0:T(8,128)(2,1)}, bf16[96,1024]{1,0:T(8,128)(2,1)S(1)}, u32[]{:S(2)}, u32[]{:S(2)}) collective-permute-start(bf16[96,1024]{1,0:T(8,128)(2,1)} %get-tuple-element.131), channel_id=1, source_target_pairs={{0,1},{1,2},{2,3},{3,0},{4,5},{5,6},{6,7},{7,4},{8,9},{9,10},{10,1... | collective-permute-start | bytes 589832 | tf_op jit(solution)/shard_map/ppermute | solution.py:295
  16.0 31.8 %collective-permute-start.2 = (bf16[96,1024]{1,0:T(8,128)(2,1)}, bf16[96,1024]{1,0:T(8,128)(2,1)}, u32[]{:S(2)}, u32[]{:S(2)}) collective-permute-start(bf16[96,1024]{1,0:T(8,128)(2,1)} %get-tuple-element.130), channel_id=1, source_target_pairs={{0,2},{1,3},{2,0},{3,1},{4,6},{5,7},{6,4},{7,5},{8,10},{9,11},{10,... | collective-permute-start | bytes 589832 | tf_op jit(solution)/shard_map/ppermute | solution.py:295
  17.7 30.1 %collective-permute-start.3 = (bf16[96,1024]{1,0:T(8,128)(2,1)}, bf16[96,1024]{1,0:T(8,128)(2,1)}, u32[]{:S(2)}, u32[]{:S(2)}) collective-permute-start(bf16[96,1024]{1,0:T(8,128)(2,1)} %get-tuple-element.129), channel_id=1, source_target_pairs={{0,3},{1,0},{2,1},{3,2},{4,7},{5,4},{6,5},{7,6},{8,11},{9,8},{10,9... | collective-permute-start | bytes 589832 | tf_op jit(solution)/shard_map/ppermute | solution.py:295
  33.4 1.6 copy-start.12
  49.8 36.7 %collective-permute-start.4 = (bf16[512,1024]{1,0:T(8,128)(2,1)}, bf16[512,1024]{1,0:T(8,128)(2,1)}, u32[]{:S(2)}, u32[]{:S(2)}) collective-permute-start(bf16[512,1024]{1,0:T(8,128)(2,1)} %collective-permute-done.token_ref), channel_id=1, source_target_pairs={{0,1},{1,2},{2,3},{3,0},{4,5},{5,6},{6,7},{7,4},{8,9},{9,10},{10,1... | collective-permute-start | bytes 3145736 | tf_op jit(solution)/shard_map/ppermute | solution.py:295
  54.8 1.4 copy-start.4
  60.2 1.3 copy-start.8
  61.5 1.4 copy-start.11
  63.0 32.4 %copy-start.2 = (f32[512,768]{1,0:T(8,128)S(1)}, f32[512,768]{1,0:T(8,128)}, u32[]{:S(2)}) copy-start(f32[512,768]{1,0:T(8,128)} %copy-done.1) | copy-start | bytes 4718596
  63.0 32.4 %copy-start.3 = (bf16[6,1024,128]{2,1,0:T(8,128)(2,1)S(1)}, bf16[6,1024,128]{2,1,0:T(8,128)(2,1)}, u32[]{:S(2)}) copy-start(bf16[6,1024,128]{2,1,0:T(8,128)(2,1)} %get-tuple-element.76.w_ref) | copy-start | bytes 4718596
  65.7 20.8 %collective-permute-start.5 = (f32[128,192]{1,0:T(8,128)S(1)}, f32[128,192]{1,0:T(8,128)S(1)}, u32[]{:S(2)}, u32[]{:S(2)}) collective-permute-start(f32[128,192]{1,0:T(8,128)S(1)} %get-tuple-element.70), channel_id=1, source_target_pairs={{0,1},{1,2},{2,3},{3,0},{4,5},{5,6},{6,7},{7,4},{8,9},{9,10},{10,1... | collective-permute-start | bytes 294920 | tf_op jit(solution)/shard_map/ppermute | solution.py:295
  65.7 20.9 %collective-permute-start.6 = (f32[128,192]{1,0:T(8,128)S(1)}, f32[128,192]{1,0:T(8,128)S(1)}, u32[]{:S(2)}, u32[]{:S(2)}) collective-permute-start(f32[128,192]{1,0:T(8,128)S(1)} %get-tuple-element.71), channel_id=1, source_target_pairs={{0,2},{1,3},{2,0},{3,1},{4,6},{5,7},{6,4},{7,5},{8,10},{9,11},{10,... | collective-permute-start | bytes 294920 | tf_op jit(solution)/shard_map/ppermute | solution.py:295
  67.4 19.2 %collective-permute-start.7 = (f32[128,192]{1,0:T(8,128)S(1)}, f32[128,192]{1,0:T(8,128)S(1)}, u32[]{:S(2)}, u32[]{:S(2)}) collective-permute-start(f32[128,192]{1,0:T(8,128)S(1)} %get-tuple-element.72), channel_id=1, source_target_pairs={{0,3},{1,0},{2,1},{3,2},{4,7},{5,4},{6,5},{7,6},{8,11},{9,8},{10,9... | collective-permute-start | bytes 294920 | tf_op jit(solution)/shard_map/ppermute | solution.py:295
  86.6 32.5 %collective-permute-start.8 = (bf16[512,1024]{1,0:T(8,128)(2,1)}, bf16[512,1024]{1,0:T(8,128)(2,1)}, u32[]{:S(2)}, u32[]{:S(2)}) collective-permute-start(bf16[512,1024]{1,0:T(8,128)(2,1)} %collective-permute-done.4.token_ref), channel_id=1, source_target_pairs={{0,1},{1,2},{2,3},{3,0},{4,5},{5,6},{6,7},{7,4},{8,9},{9,10},{10,1... | collective-permute-start | bytes 3145736 | tf_op jit(solution)/shard_map/ppermute | solution.py:295
  90.0 27.5 %collective-permute-start.9 = (bf16[128,192]{1,0:T(8,128)(2,1)S(1)}, bf16[128,192]{1,0:T(8,128)(2,1)S(1)}, u32[]{:S(2)}, u32[]{:S(2)}) collective-permute-start(bf16[128,192]{1,0:T(8,128)(2,1)S(1)} %add_convert_fusion.refs_0_), channel_id=1, source_target_pairs={{0,1},{1,2},{2,3},{3,0},{4,5},{5,6},{6,7},{7,4},{8,9},{9,10},{10,1... | collective-permute-start | bytes 147464 | tf_op jit(solution)/shard_map/ppermute | solution.py:295
  90.1 29.1 %collective-permute-start.10 = (bf16[128,192]{1,0:T(8,128)(2,1)S(1)}, bf16[128,192]{1,0:T(8,128)(2,1)}, u32[]{:S(2)}, u32[]{:S(2)}) collective-permute-start(bf16[128,192]{1,0:T(8,128)(2,1)S(1)} %add_convert_fusion.refs_0_), channel_id=1, source_target_pairs={{0,2},{1,3},{2,0},{3,1},{4,6},{5,7},{6,4},{7,5},{8,10},{9,11},{10,... | collective-permute-start | bytes 147464 | tf_op jit(solution)/shard_map/ppermute | solution.py:295
  92.5 26.7 %collective-permute-start.11 = (bf16[128,192]{1,0:T(8,128)(2,1)S(1)}, bf16[128,192]{1,0:T(8,128)(2,1)}, u32[]{:S(2)}, u32[]{:S(2)}) collective-permute-start(bf16[128,192]{1,0:T(8,128)(2,1)S(1)} %add_convert_fusion.refs_0_), channel_id=1, source_target_pairs={{0,3},{1,0},{2,1},{3,2},{4,7},{5,4},{6,5},{7,6},{8,11},{9,8},{10,9... | collective-permute-start | bytes 147464 | tf_op jit(solution)/shard_map/ppermute | solution.py:295
  98.2 21.0 %copy-start.6 = (f32[512,256]{1,0:T(8,128)S(1)}, f32[512,256]{1,0:T(8,128)}, u32[]{:S(2)}) copy-start(f32[512,256]{1,0:T(8,128)} %pad_maximum_fusion.1.turn_ref) | copy-start | bytes 1572868
  98.2 21.0 %copy-start.9 = (bf16[24,64,128]{2,1,0:T(8,128)(2,1)S(1)}, bf16[24,64,128]{2,1,0:T(8,128)(2,1)}, u32[]{:S(2)}) copy-start(bf16[24,64,128]{2,1,0:T(8,128)(2,1)} %all-gather) | copy-start | bytes 1179652
  123.4 10.0 %collective-permute-start.12 = (bf16[256,512]{1,0:T(8,128)(2,1)S(1)}, bf16[256,512]{1,0:T(8,128)(2,1)S(1)}, u32[]{:S(2)}, u32[]{:S(2)}) collective-permute-start(bf16[256,512]{1,0:T(8,128)(2,1)S(1)} %get-tuple-element.95.attended_ref), channel_id=1, source_target_pairs={{0,1},{1,2},{2,3},{3,0},{4,5},{5,6},{6,7},{7,4},{8,9},{9,10},{10,1... | collective-permute-start | bytes 786440 | tf_op jit(solution)/shard_map/ppermute | solution.py:295
  125.4 4.9 %copy-start = (bf16[4,128,1024]{2,1,0:T(8,128)(2,1)S(1)}, bf16[4,128,1024]{2,1,0:T(8,128)(2,1)}, u32[]{:S(2)}) copy-start(bf16[4,128,1024]{2,1,0:T(8,128)(2,1)} %copy.41) | copy-start | bytes 3145732
  125.4 4.9 %copy-start.10 = (bf16[128,1024]{1,0:T(8,128)(2,1)S(1)}, bf16[128,1024]{1,0:T(8,128)(2,1)}, u32[]{:S(2)}) copy-start(bf16[128,1024]{1,0:T(8,128)(2,1)} %all-gather.1) | copy-start | bytes 786436
  133.4 11.0 %collective-permute-start.13 = (bf16[256,512]{1,0:T(8,128)(2,1)S(1)}, bf16[256,512]{1,0:T(8,128)(2,1)S(1)}, u32[]{:S(2)}, u32[]{:S(2)}) collective-permute-start(bf16[256,512]{1,0:T(8,128)(2,1)S(1)} %get-tuple-element.96.attended_ref), channel_id=1, source_target_pairs={{0,1},{1,2},{2,3},{3,0},{4,5},{5,6},{6,7},{7,4},{8,9},{9,10},{10,1... | collective-permute-start | bytes 786440 | tf_op jit(solution)/shard_map/ppermute | solution.py:295
  133.5 14.5 %collective-permute-start.14 = (bf16[256,512]{1,0:T(8,128)(2,1)S(1)}, bf16[256,512]{1,0:T(8,128)(2,1)S(1)}, u32[]{:S(2)}, u32[]{:S(2)}) collective-permute-start(bf16[256,512]{1,0:T(8,128)(2,1)S(1)} %collective-permute-done.12.attended_ref), channel_id=1, source_target_pairs={{0,1},{1,2},{2,3},{3,0},{4,5},{5,6},{6,7},{7,4},{8,9},{9,10},{10,1... | collective-permute-start | bytes 786440 | tf_op jit(solution)/shard_map/ppermute | solution.py:295
  148.1 11.0 %collective-permute-start.15 = (bf16[256,512]{1,0:T(8,128)(2,1)S(1)}, bf16[256,512]{1,0:T(8,128)(2,1)S(1)}, u32[]{:S(2)}, u32[]{:S(2)}) collective-permute-start(bf16[256,512]{1,0:T(8,128)(2,1)S(1)} %collective-permute-done.13.attended_ref), channel_id=1, source_target_pairs={{0,1},{1,2},{2,3},{3,0},{4,5},{5,6},{6,7},{7,4},{8,9},{9,10},{10,1... | collective-permute-start | bytes 786440 | tf_op jit(solution)/shard_map/ppermute | solution.py:295
  148.1 13.8 %collective-permute-start.16 = (bf16[256,512]{1,0:T(8,128)(2,1)S(1)}, bf16[256,512]{1,0:T(8,128)(2,1)S(1)}, u32[]{:S(2)}, u32[]{:S(2)}) collective-permute-start(bf16[256,512]{1,0:T(8,128)(2,1)S(1)} %collective-permute-done.14.attended_ref), channel_id=1, source_target_pairs={{0,1},{1,2},{2,3},{3,0},{4,5},{5,6},{6,7},{7,4},{8,9},{9,10},{10,1... | collective-permute-start | bytes 786440 | tf_op jit(solution)/shard_map/ppermute | solution.py:295
  161.8 8.2 %collective-permute-start.17 = (bf16[256,512]{1,0:T(8,128)(2,1)S(1)}, bf16[256,512]{1,0:T(8,128)(2,1)S(1)}, u32[]{:S(2)}, u32[]{:S(2)}) collective-permute-start(bf16[256,512]{1,0:T(8,128)(2,1)S(1)} %collective-permute-done.15.attended_ref), channel_id=1, source_target_pairs={{0,1},{1,2},{2,3},{3,0},{4,5},{5,6},{6,7},{7,4},{8,9},{9,10},{10,1... | collective-permute-start | bytes 786440 | tf_op jit(solution)/shard_map/ppermute | solution.py:295
  (4 other events, 4.9 us)
Sparse Core Ops, SparseCore 0:
  9.7 21.5 all-gather.5
  49.9 43.4 all-gather.7

commit v15 on v14

--- a/solution.py
+++ b/solution.py
@@ -58,12 +58,12 @@
     return pl.BlockSpec((rows, array.shape[1]), lambda step, ids: (part, 0))
 
 
-def project(ids, tokens, weight, begun=()):
+def project(tokens, weight, begun=()):
     slots, _, head_size = weight.shape
     return call(
         functools.partial(project_kernel, len(begun)),
         "project",
-        ids,
+        jnp.zeros(1),
         1,
         [None] * (2 + len(begun)),
         [tokens, weight, *begun],
@@ -132,7 +132,7 @@
 
 
 def attend(planes_of, adapters, part, table, turn, up, shrink, tokens, weight, begun, earlier):
-    rows = tokens.shape[0] // 2
+    rows = tokens.shape[0]
     slots, _, head_size = weight.shape
     planes = len(shrink)
     arrays = [table, turn, up, *shrink, tokens, weight, begun, *earlier]
@@ -294,7 +294,6 @@
     def turned(value, turn=1):
         return lax.ppermute(value, "tensor", [(i, (i + turn) % planes) for i in range(planes)])
 
-    held = [tokens, turned(tokens)]
     weight = jnp.transpose(query_key_value_weight, (1, 0, 2))
     down_all = lax.all_gather(adapter_down_maps, "dp", axis=0, tiled=True)
     up_all = lax.all_gather(jnp.transpose(adapter_up_maps[0], (1, 0, 2)), "dp", axis=0)
@@ -339,64 +338,71 @@
         for k in range(1, planes)
     ]
 
-    def shard(number):
-        start = planes_of[number] * depth
+    def shard(plane):
+        start = (plane + planes) % planes * depth
         return lax.dynamic_slice_in_dim(weight, start, depth, axis=1)
 
-    lines = [turned(send, k) for k, send in enumerate(sends, 1)]
-    begun = project(planes_of[:1], tokens, shard(0))
-    done = (held[1], lines, begun, table, turn, up_all, own_rows, shard(1))
-    done = lax.optimization_barrier(done)
-    held[1], lines, begun, table, turn, up_all, own_rows, part_weight = done
-    lines = lax.all_gather(jnp.stack(lines), PLANE, axis=0)
-    for step in range(2, planes):
-        arrived = held[-1]
-        held.append(turned(arrived))
-        begun = project(planes_of[step - 1 : step], arrived, part_weight, [begun])
+    opposite = planes // 2
+    half_rows = token_rows // 2
+    right, left, begun, weights = [tokens], [tokens], [], [shard(here)]
+    for step in range(1, opposite + 1):
+        if step < opposite:
+            moved = (turned(right[-1]), turned(left[-1], planes - 1))
+            ahead = (here - step, here + step)
+        else:
+            moved = (turned(right[-1][:half_rows]), turned(left[-1][half_rows:], planes - 1))
+            ahead = (here - step,)
+        for tokens_of, weight_of in zip((right[-1], left[-1]), weights):
+            begun = [project(tokens_of, weight_of, begun)]
         side = ()
-        if step == 2:
-            sums = shrink_partial(adapters, here, planes, table, after(tokens, arrived), down_all)
+        if step == 1:
+            lines = [turned(send, k) for k, send in enumerate(sends, 1)]
+            sums = shrink_partial(adapters, here, planes, table, tokens, down_all)
             sums = [sums[0]] + [turned(sums[k], k) for k in range(1, planes)]
-            side = (
-                sums,
-                lax.all_gather(after(output_up_maps, sums[0]), "dp", axis=0, tiled=True),
-                lax.all_gather(after(out_down, sums[0]), "dp", axis=0),
-            )
-        elif step == 3:
+            out_up_all = lax.all_gather(after(output_up_maps, sums[0]), "dp", axis=0, tiled=True)
+            own_down = lax.all_gather(after(out_down, sums[0]), "dp", axis=0)
+            side = (lines, sums, out_up_all, own_down, table, turn, up_all, own_rows)
+        elif step == 2:
             shrink = sum(sums[1:], sums[0]).astype(jnp.bfloat16)
-            shrink = [shrink] + [turned(shrink, k) for k in range(1, planes)]
-            side = (shrink, [lines[:, k] for k in range(planes - 1)])
-        done = lax.optimization_barrier((held[-1], begun, shard(step), side))
-        held[-1], begun, part_weight, side = done
-        if step == 2:
-            sums, out_up_all, own_down = side
-        elif step == 3:
-            shrink, lines = side
+            side = [shrink] + [turned(shrink, k) for k in range(1, planes)]
+        weights = [shard(plane) for plane in ahead]
+        moved, begun, weights, side = lax.optimization_barrier((moved, begun, weights, side))
+        if step == 1:
+            lines, sums, out_up_all, own_down, table, turn, up_all, own_rows = side
+            lines = lax.all_gather(jnp.stack(lines), PLANE, axis=0)
+        elif step == 2:
+            shrink = side
+        right.append(moved[0])
+        left.append(moved[1])
 
     ids = jnp.concatenate([lax.axis_index("groups")[None], adapters])
-    attended, earlier = [[], []], ()
+    made, earlier = [], ()
     for part in range(2):
-        made, *earlier = attend(
-            planes_of, adapters, part, table, turn, up_all, shrink, held[-1], part_weight,
-            begun, earlier,
-        )
-        attended[part] = [made, turned(after(made, *attended[0][1:]))]
-    sums = [
-        project_out(ids, rank, attended[part][0], own_rows, own_down, [], []) for part in range(2)
-    ]
-    before = []
-    for step in range(2, planes + 1):
+        own, *earlier = attend(
+            planes_of, adapters, part, table, turn, up_all, shrink, moved[part], weights[0],
+            begun[0], earlier,
+        )
+        made.append([(own,)])
+        for step in range(1, opposite):
+            source = made[part][-1]
+            made[part].append((turned(source[0]), turned(source[-1], planes - 1)))
+        source = made[part][-1][part]
+        made[part].append((turned(source, (1, planes - 1)[part]),))
+    lines = [lines[:, k] for k in range(planes - 1)]
+    sums, before = [(), ()], []
+    for step in range(opposite + 1):
         for part in range(2):
-            arrived = attended[part][-1]
-            if step < planes:
-                ahead = [*attended[0][step:], *sums[part]]
-                attended[part].append(turned(after(arrived, *ahead)))
-            final = [] if step < planes else [table, out_up_all, *before]
-            sums[part] = project_out(
-                ids, rank, arrived, lines[step - 2], pool, list(sums[part]), final, part
-            )
-            if final:
-                before = [sums[part]]
+            arrived = made[part][step]
+            for way, array in enumerate(arrived):
+                last = step == opposite
+                turn_of = (step, planes - step)[way]
+                sums[part] = project_out(
+                    ids, rank, array, lines[turn_of - 1] if step else own_rows,
+                    pool if step else own_down, list(sums[part]),
+                    [table, out_up_all, *before] if last else [], part,
+                )
+                if last:
+                    before = [sums[part]]
     return before[0]
 
 

time: 180 us -> 183 us (1.017)
  local copies, waits for them, and re-layouts: 22.3 us -> 31.4 us
  Pallas kernels: 29 us -> 34.4 us
  waiting for transfers between devices: 54 us -> 49 us
  blocking collectives: 23.1 us -> 20.6 us
  between operations: 16.3 us -> 13.9 us
    unnamed x34 -> x54, local copies, waits for them, and re-layouts: 5.62 us -> 11.3 us
    pallas_call x14, Pallas kernels: 29 us -> 34.4 us  [call(): pl.pallas_call(kernel, out_shape=out, grid_spec=pltpu.PrefetchScalarGridS...]
    ppermute x18 -> x19, waiting for transfers between devices: 54 us -> 48.9 us  [turned(): lax.ppermute(value, 'tensor', [(i, (i + turn) % planes) for i in range(pl...]
    slice x1 -> x2, local copies, waits for them, and re-layouts: 0.64 us -> 3.81 us  [the longest x1 1.92 us: local(): right[-1][:half_rows]]
    all_gather x1, blocking collectives: 8.08 us -> 6.24 us  [local(): own_down = lax.all_gather(after(out_down, sums[0]), 'dp', axis=0)]
    ppermute x18 -> x19, starting transfers between devices: 28.8 us -> 27.5 us  [turned(): lax.ppermute(value, 'tensor', [(i, (i + turn) % planes) for i in range(pl...]
  transfers between devices with their start and end apart: 20 -> 21, of which waited for: 10 -> 8; matrix products, arithmetic and copies ran while one was open for 12% -> 13% of each run, Pallas kernels for 13% -> 18%
where the time goes in v15:
time: 183 us; the launch traced here: 182 us
  waiting for transfers between devices  49 us (27%)
  Pallas kernels  34.4 us (19%)
  local copies, waits for them, and re-layouts  31.4 us (17%)
  starting transfers between devices  27.5 us (15%)
  blocking collectives  20.6 us (11%)
  between operations  13.9 us (8%)
  other arithmetic  5.61 us (3%)
    ppermute x19, waiting for transfers between devices, turned(): lax.ppermute(value, 'tensor', [(i, (i + turn) % planes) for i in range(pl...  48.9 us
    pallas_call x14, Pallas kernels, call(): pl.pallas_call(kernel, out_shape=out, grid_spec=pltpu.PrefetchScalarGridS...  34.4 us
    ppermute x19, starting transfers between devices, turned(): lax.ppermute(value, 'tensor', [(i, (i + turn) % planes) for i in range(pl...  27.5 us
    unnamed x54, local copies, waits for them, and re-layouts  11.3 us
    all_gather x1, blocking collectives, local(): lax.all_gather(after(output_up_maps, sums[0]), 'dp', axis=0, tiled=True)  7.49 us
    all_gather x1, blocking collectives, local(): lax.all_gather(jnp.transpose(adapter_up_maps[0], (1, 0, 2)), 'dp', axis=0)  6.88 us
    all_gather x1, blocking collectives, local(): own_down = lax.all_gather(after(out_down, sums[0]), 'dp', axis=0)  6.24 us
    dynamic_slice x1, local copies, waits for them, and re-layouts, shard(): return lax.dynamic_slice_in_dim(weight, start, depth, axis=1)  5.15 us
  transfers between devices with their start and end apart: 21, of which 8 were waited for; matrix products, arithmetic and copies ran while one was open for 13% of the time, Pallas kernels for 18%

profile of v15, /device:TPU:0, one launch (start us, length us, event | category | flops | bytes accessed | tf_op | source)
XLA Modules:
  0.0 182.5 jit_solution(9120208543448324690)
XLA Ops:
  6.5 5.0 %collective-permute-start.1 = (bf16[512,1024]{1,0:T(8,128)(2,1)}, bf16[512,1024]{1,0:T(8,128)(2,1)}, u32[]{:S(2)}, u32[]{:S(2)}) collective-permute-start(bf16[512,1024]{1,0:T(8,128)(2,1)} %token_ref.3), channel_id=1, source_target_pairs={{0,3},{1,0},{2,1},{3,2},{4,7},{5,4},{6,5},{7,6},{8,11},{9,8},{10,9... | collective-permute-start | bytes 3145736 | tf_op jit(solution)/shard_map/ppermute | solution.py:295
  12.6 2.8 %fusion.4 = (bf16[64,1,1024]{2,1,0:T(2,128)(2,1)S(1)}, bf16[64,1,1024]{2,1,0:T(2,128)(2,1)S(1)}, bf16[64,1,1024]{2,1,0:T(2,128)(2,1)S(1)}) fusion(bf16[128,4,4096]{2,1,0:T(4,128)(2,1)} %param.11, s32[]{:T(128)S(6)} %select_n.90, s32[]{:T(128)S(6)} %select_n.93, s32[]{:T(128)S(6)} %select_n.100, s32[]{:T(128)S(6)} %select_n.99, s32[]{:T(128)S(6)} %select_n.96), kind=kLoop, calls=%fused_computation.39 | loop fusion | bytes 786452 | tf_op jit(solution)/shard_map/dynamic_slice | solution.py:334
  16.5 3.8 %collective-permute-start.4 = (bf16[96,1024]{1,0:T(8,128)(2,1)}, bf16[96,1024]{1,0:T(8,128)(2,1)}, u32[]{:S(2)}, u32[]{:S(2)}) collective-permute-start(bf16[96,1024]{1,0:T(8,128)(2,1)} %get-tuple-element.111), channel_id=1, source_target_pairs={{0,3},{1,0},{2,1},{3,2},{4,7},{5,4},{6,5},{7,6},{8,11},{9,8},{10,9... | collective-permute-start | bytes 589832 | tf_op jit(solution)/shard_map/ppermute | solution.py:295
  21.3 2.6 %dynamic-slice_bitcast_fusion.4 = bf16[4,128,1024]{2,0,1:T(4,128)(2,1)} fusion(bf16[128,4,4096]{2,1,0:T(4,128)(2,1)} %param.11, s32[]{:T(128)S(6)} %select_n.102), kind=kLoop, calls=%fused_computation.7 | loop fusion | bytes 2097156 | tf_op jit(solution)/shard_map/transpose | solution.py:319
  23.8 5.2 %dynamic-slice_bitcast_fusion = (bf16[6,1024,128]{2,1,0:T(8,128)(2,1)S(1)}, bf16[6,1024,128]{2,1,0:T(8,128)(2,1)}, bf16[6,1024,128]{2,1,0:T(8,128)(2,1)}, bf16[6,1024,128]{2,1,0:T(8,128)(2,1)}) fusion(bf16[4096,6,128]{2,0,1:T(8,128)(2,1)} %param.10, s32[]{:T(128)S(6)} %select_n.98, s32[]{:T(128)S(6)} %select_n.85, s32[]{:T(128)S(6)} %select_n.83, s32[]{:T(128)S(6)} %select_n.87), kind=kLoop, calls=%fused_computation.3 | loop fusion | bytes 12582928 | tf_op jit(solution)/shard_map/dynamic_slice | solution.py:343
  36.5 6.9 %all-gather.1 = bf16[24,64,128]{2,1,0:T(8,128)(2,1)} all-gather(bf16[6,64,128]{2,1,0:T(8,128)(2,1)S(1)} %bitcast.65), channel_id=3, replica_groups=mesh['groups'=2,'dp'=4,'tensor'=4] {'dp'}, dimensions={0}, use_global_device_ids=true | all-gather | bytes 491520 | tf_op jit(solution)/shard_map/all_gather | solution.py:299
  46.0 2.7 %shrink.1 = (f32[128,192]{1,0:T(8,128)S(1)}, f32[128,192]{1,0:T(8,128)S(1)}, f32[128,192]{1,0:T(8,128)S(1)}, f32[128,192]{1,0:T(8,128)S(1)}) custom-call(s32[5]{0:T(128)S(1)} %pad_add_fusion.3.ids_ref, s32[512,2]{1,0:T(8,128)S(1)} %copy.40.table_ref, bf16[512,1024]{1,0:T(8,128)(2,1)S(1)} %copy-done.7, bf16[4,192,1024]{2,1,0:T(8,128)(2,1)S(1)} %copy-done.10), custom_call_target="tpu_custom_call" | custom-call | bytes 7876608 | tf_op jit(solution)/shard_map/shrink/pallas_call | solution.py:26
  49.3 7.5 %all_gather.25.refs_3_ = bf16[4,64,1024]{2,1,0:T(8,128)(2,1)S(1)} all-gather(bf16[1,64,1024]{2,1,0:T(8,128)(2,1)} %param.15), channel_id=1, replica_groups=mesh['groups'=2,'dp'=4,'tensor'=4] {'dp'}, dimensions={0}, use_global_device_ids=true | all-gather | bytes 655360 | tf_op jit(solution)/shard_map/all_gather | solution.py:362
  56.8 5.4 %collective-permute-done.4 = bf16[96,1024]{1,0:T(8,128)(2,1)} collective-permute-done((bf16[96,1024]{1,0:T(8,128)(2,1)}, bf16[96,1024]{1,0:T(8,128)(2,1)}, u32[]{:S(2)}, u32[]{:S(2)}) %collective-permute-start.4) | collective-permute-done | bytes 196640 | tf_op jit(solution)/shard_map/ppermute | solution.py:295
  63.8 15.4 %collective-permute-done.3 = bf16[96,1024]{1,0:T(8,128)(2,1)} collective-permute-done((bf16[96,1024]{1,0:T(8,128)(2,1)}, bf16[96,1024]{1,0:T(8,128)(2,1)}, u32[]{:S(2)}, u32[]{:S(2)}) %collective-permute-start.3) | collective-permute-done | bytes 196640 | tf_op jit(solution)/shard_map/ppermute | solution.py:295
  79.2 6.2 %all-gather = bf16[128,1024]{1,0:T(8,128)(2,1)} all-gather(bf16[32,1024]{1,0:T(8,128)(2,1)S(1)} %bitcast_dynamic-update-slice_fusion), channel_id=2, replica_groups=mesh['groups'=2,'dp'=4,'tensor'=4] {'dp'}, dimensions={0}, use_global_device_ids=true | all-gather | bytes 327680 | tf_op jit(solution)/shard_map/all_gather | solution.py:363
  87.0 2.0 %pad_maximum_fusion = bf16[3,96,1024]{2,1,0:T(8,128)(2,1)} fusion(bf16[1,96,1024]{2,1,0:T(8,128)(2,1)} %bitcast.22, bf16[1,96,1024]{2,1,0:T(8,128)(2,1)} %bitcast.21, bf16[1,96,1024]{2,1,0:T(8,128)(2,1)} %bitcast.20), kind=kLoop, calls=%fused_computation.8 | loop fusion | flops 589824 | bytes 1179648 | tf_op jit(solution)/shard_map/stack | solution.py:372
  92.9 3.5 %collective-permute-start.9 = (bf16[256,1024]{1,0:T(8,128)(2,1)}, bf16[256,1024]{1,0:T(8,128)(2,1)}, u32[]{:S(2)}, u32[]{:S(2)}) collective-permute-start(bf16[256,1024]{1,0:T(8,128)(2,1)} %slice.22), channel_id=1, source_target_pairs={{0,3},{1,0},{2,1},{3,2},{4,7},{5,4},{6,5},{7,6},{8,11},{9,8},{10,9... | collective-permute-start | bytes 1572872 | tf_op jit(solution)/shard_map/ppermute | solution.py:295
  96.5 3.9 %collective-permute-start.12 = (bf16[128,192]{1,0:T(8,128)(2,1)S(1)}, bf16[128,192]{1,0:T(8,128)(2,1)S(1)}, u32[]{:S(2)}, u32[]{:S(2)}) collective-permute-start(bf16[128,192]{1,0:T(8,128)(2,1)S(1)} %add_convert_fusion.refs_0_), channel_id=1, source_target_pairs={{0,3},{1,0},{2,1},{3,2},{4,7},{5,4},{6,5},{7,6},{8,11},{9,8},{10,9... | collective-permute-start | bytes 147464 | tf_op jit(solution)/shard_map/ppermute | solution.py:295
  104.0 2.3 %project.4.refs_0_ = f32[512,768]{1,0:T(8,128)S(1)} custom-call(s32[1]{0:T(128)} %constant.146.clone.1.ids_ref, bf16[512,1024]{1,0:T(8,128)(2,1)} %collective-permute-done.token_ref, bf16[6,1024,128]{2,1,0:T(8,128)(2,1)S(1)} %copy-done.4, f32[512,768]{1,0:T(8,128)S(1)} %copy-done.1), custom_call_target="tpu_custom_call" | custom-call | bytes 12582912 | tf_op jit(solution)/shard_map/project/pallas_call | solution.py:26
  106.4 2.3 %project.5.refs_6_ = f32[512,768]{1,0:T(8,128)S(1)} custom-call(s32[1]{0:T(128)} %constant.146.clone.1.ids_ref, bf16[512,1024]{1,0:T(8,128)(2,1)} %collective-permute-done.1.token_ref, bf16[6,1024,128]{2,1,0:T(8,128)(2,1)S(1)} %copy-done.3, f32[512,768]{1,0:T(8,128)S(1)} %project.4.refs_0_), custom_call_target="tpu_custom_call" | custom-call | bytes 12582912 | tf_op jit(solution)/shard_map/project/pallas_call | solution.py:26
  108.7 12.8 %collective-permute-done.12.refs_3_ = bf16[128,192]{1,0:T(8,128)(2,1)S(1)} collective-permute-done((bf16[128,192]{1,0:T(8,128)(2,1)S(1)}, bf16[128,192]{1,0:T(8,128)(2,1)S(1)}, u32[]{:S(2)}, u32[]{:S(2)}) %collective-permute-start.12) | collective-permute-done | bytes 49184 | tf_op jit(solution)/shard_map/ppermute | solution.py:295
  121.5 3.3 %collective-permute-done.11.refs_2_ = bf16[128,192]{1,0:T(8,128)(2,1)} collective-permute-done((bf16[128,192]{1,0:T(8,128)(2,1)S(1)}, bf16[128,192]{1,0:T(8,128)(2,1)}, u32[]{:S(2)}, u32[]{:S(2)}) %collective-permute-start.11) | collective-permute-done | bytes 49184 | tf_op jit(solution)/shard_map/ppermute | solution.py:295
  124.8 4.9 %attend.2 = (bf16[256,512]{1,0:T(8,128)(2,1)}, bf16[256,128]{1,0:T(8,128)(2,1)S(1)}, bf16[256,128]{1,0:T(8,128)(2,1)S(1)}) custom-call(s32[8]{0:T(128)S(1)} %pad_add_fusion.2.ids_ref, s32[512,2]{1,0:T(8,128)S(1)} %copy.44.table_ref.refs_2_, f32[512,256]{1,0:T(8,128)S(1)} %copy-done.5, bf16[4,6,64,128]{3,2,1,0:T(8,128)(2,1)S(1)} %bitcast.57, ...), custom_call_target="tpu_custom_call" | custom-call | bytes 14364672 | tf_op jit(solution)/shard_map/attend/pallas_call | solution.py:26
  129.8 5.6 %attend.3 = (bf16[256,512]{1,0:T(8,128)(2,1)}, bf16[256,128]{1,0:T(8,128)(2,1)}, bf16[256,128]{1,0:T(8,128)(2,1)}) custom-call(s32[8]{0:T(128)S(1)} %pad_add_fusion.2.ids_ref, s32[512,2]{1,0:T(8,128)S(1)} %copy.44.table_ref.refs_2_, f32[512,256]{1,0:T(8,128)S(1)} %copy-done.5, bf16[4,6,64,128]{3,2,1,0:T(8,128)(2,1)S(1)} %bitcast.58, ...), custom_call_target="tpu_custom_call" | custom-call | bytes 14757888 | tf_op jit(solution)/shard_map/attend/pallas_call | solution.py:26
  139.0 2.3 %collective-permute-start.18 = (bf16[256,512]{1,0:T(8,128)(2,1)}, bf16[256,512]{1,0:T(8,128)(2,1)}, u32[]{:S(2)}, u32[]{:S(2)}) collective-permute-start(bf16[256,512]{1,0:T(8,128)(2,1)} %get-tuple-element.94.attended_ref), channel_id=1, source_target_pairs={{0,3},{1,0},{2,1},{3,2},{4,7},{5,4},{6,5},{7,6},{8,11},{9,8},{10,9... | collective-permute-start | bytes 786440 | tf_op jit(solution)/shard_map/ppermute | solution.py:295
  141.3 2.0 %project_out.8 = (f32[256,1024]{1,0:T(8,128)S(1)}, f32[256,256]{1,0:T(8,128)S(1)}) custom-call(s32[5]{0:T(128)S(1)} %pad_add_fusion.1.ids_ref, bf16[256,512]{1,0:T(8,128)(2,1)} %get-tuple-element.81.attended_ref, bf16[512,1024]{1,0:T(8,128)(2,1)S(1)} %bitcast.55, bf16[4,32,1024]{2,1,0:T(8,128)(2,1)S(1)} %bitcast.59), custom_call_target="tpu_custom_call" | custom-call | bytes 4718592 | tf_op jit(solution)/shard_map/project_out/pallas_call | solution.py:26
  143.3 2.0 %project_out.11 = (f32[256,1024]{1,0:T(8,128)S(1)}, f32[256,256]{1,0:T(8,128)S(1)}) custom-call(s32[5]{0:T(128)S(1)} %pad_add_fusion.1.ids_ref, bf16[256,512]{1,0:T(8,128)(2,1)} %get-tuple-element.94.attended_ref, bf16[512,1024]{1,0:T(8,128)(2,1)S(1)} %bitcast.56, bf16[4,32,1024]{2,1,0:T(8,128)(2,1)S(1)} %bitcast.60), custom_call_target="tpu_custom_call" | custom-call | bytes 4718592 | tf_op jit(solution)/shard_map/project_out/pallas_call | solution.py:26
  146.3 8.5 %collective-permute-done.13.attended_ref = bf16[256,512]{1,0:T(8,128)(2,1)} collective-permute-done((bf16[256,512]{1,0:T(8,128)(2,1)}, bf16[256,512]{1,0:T(8,128)(2,1)}, u32[]{:S(2)}, u32[]{:S(2)}) %collective-permute-start.13) | collective-permute-done | bytes 262176 | tf_op jit(solution)/shard_map/ppermute | solution.py:295
  154.8 2.6 %collective-permute-start.17 = (bf16[256,512]{1,0:T(8,128)(2,1)}, bf16[256,512]{1,0:T(8,128)(2,1)S(1)}, u32[]{:S(2)}, u32[]{:S(2)}) collective-permute-start(bf16[256,512]{1,0:T(8,128)(2,1)} %collective-permute-done.16.attended_ref), channel_id=1, source_target_pairs={{0,1},{1,2},{2,3},{3,0},{4,5},{5,6},{6,7},{7,4},{8,9},{9,10},{10,1... | collective-permute-start | bytes 786440 | tf_op jit(solution)/shard_map/ppermute | solution.py:295
  157.4 3.0 %slice_bitcast_fusion = (bf16[8,96,1024]{2,1,0:T(8,128)(2,1)S(1)}, bf16[8,96,1024]{2,1,0:T(8,128)(2,1)S(1)}, bf16[8,96,1024]{2,1,0:T(8,128)(2,1)S(1)}) fusion(bf16[8,3,96,1024]{3,2,1,0:T(8,128)(2,1)} %bitcast.61), kind=kLoop, calls=%fused_computation | loop fusion | bytes 9437184 | tf_op jit(solution)/shard_map/squeeze | solution.py:391
  161.4 2.0 %project_out.12 = (f32[256,1024]{1,0:T(8,128)S(1)}, f32[256,256]{1,0:T(8,128)S(1)}) custom-call(s32[5]{0:T(128)S(1)} %pad_add_fusion.1.ids_ref, bf16[256,512]{1,0:T(8,128)(2,1)} %collective-permute-done.16.attended_ref, bf16[8,96,1024]{2,1,0:T(8,128)(2,1)S(1)} %get-tuple-element.105.w_ref.down_ref, ...), custom_call_target="tpu_custom_call" | custom-call | bytes 14155776 | tf_op jit(solution)/shard_map/project_out/pallas_call | solution.py:26
  163.4 2.0 %project_out.9 = (f32[256,1024]{1,0:T(8,128)S(1)}, f32[256,256]{1,0:T(8,128)S(1)}) custom-call(s32[5]{0:T(128)S(1)} %pad_add_fusion.1.ids_ref, bf16[256,512]{1,0:T(8,128)(2,1)} %collective-permute-done.15.attended_ref, bf16[8,96,1024]{2,1,0:T(8,128)(2,1)S(1)} %get-tuple-element.105.w_ref.down_ref, ...), custom_call_target="tpu_custom_call" | custom-call | bytes 14155776 | tf_op jit(solution)/shard_map/project_out/pallas_call | solution.py:26
  165.4 2.0 %project_out.10 = (f32[256,1024]{1,0:T(8,128)S(1)}, f32[256,256]{1,0:T(8,128)S(1)}) custom-call(s32[5]{0:T(128)S(1)} %pad_add_fusion.1.ids_ref, bf16[256,512]{1,0:T(8,128)(2,1)} %collective-permute-done.13.attended_ref, bf16[8,96,1024]{2,1,0:T(8,128)(2,1)S(1)} %get-tuple-element.106.w_ref.down_ref, ...), custom_call_target="tpu_custom_call" | custom-call | bytes 14155776 | tf_op jit(solution)/shard_map/project_out/pallas_call | solution.py:26
  167.5 2.0 %project_out.13 = (f32[256,1024]{1,0:T(8,128)S(1)}, f32[256,256]{1,0:T(8,128)S(1)}) custom-call(s32[5]{0:T(128)S(1)} %pad_add_fusion.1.ids_ref, bf16[256,512]{1,0:T(8,128)(2,1)} %collective-permute-done.18.attended_ref, bf16[8,96,1024]{2,1,0:T(8,128)(2,1)S(1)} %get-tuple-element.106.w_ref.down_ref, ...), custom_call_target="tpu_custom_call" | custom-call | bytes 14155776 | tf_op jit(solution)/shard_map/project_out/pallas_call | solution.py:26
  169.5 2.6 %collective-permute-done.17.attended_ref = bf16[256,512]{1,0:T(8,128)(2,1)S(1)} collective-permute-done((bf16[256,512]{1,0:T(8,128)(2,1)}, bf16[256,512]{1,0:T(8,128)(2,1)S(1)}, u32[]{:S(2)}, u32[]{:S(2)}) %collective-permute-start.17) | collective-permute-done | bytes 262176 | tf_op jit(solution)/shard_map/ppermute | solution.py:295
  173.4 2.3 %project_out.15 = bf16[512,1024]{1,0:T(8,128)(2,1)} custom-call(s32[5]{0:T(128)S(1)} %pad_add_fusion.1.ids_ref, bf16[256,512]{1,0:T(8,128)(2,1)S(1)} %collective-permute-done.14.attended_ref, bf16[8,96,1024]{2,1,0:T(8,128)(2,1)S(1)} %get-tuple-element.107.w_ref.down_ref, bf16[8,96,1024]{2,1,0:T(8,128)(2,1)S(1)} %get-tuple-element.107.w_ref.down_ref, ...), custom_call_target="tpu_custom_call" | custom-call | bytes 17313792 | tf_op jit(solution)/shard_map/project_out/pallas_call | solution.py:26
  (114 shorter events, 31.2 us)
Async XLA Ops:
  6.5 36.8 %all-gather.6.cloned.1.call-start = ((), (), s32[]{:S(2)}) async-start(), calls=%async_computation | async-start | bytes 1966080 | tf_op jit(solution)/shard_map/all_gather | solution.py:298
  6.5 78.9 %collective-permute-start.1 = (bf16[512,1024]{1,0:T(8,128)(2,1)}, bf16[512,1024]{1,0:T(8,128)(2,1)}, u32[]{:S(2)}, u32[]{:S(2)}) collective-permute-start(bf16[512,1024]{1,0:T(8,128)(2,1)} %token_ref.3), channel_id=1, source_target_pairs={{0,3},{1,0},{2,1},{3,2},{4,7},{5,4},{6,5},{7,6},{8,11},{9,8},{10,9... | collective-permute-start | bytes 3145736 | tf_op jit(solution)/shard_map/ppermute | solution.py:295
  11.6 73.8 %collective-permute-start = (bf16[512,1024]{1,0:T(8,128)(2,1)}, bf16[512,1024]{1,0:T(8,128)(2,1)}, u32[]{:S(2)}, u32[]{:S(2)}) collective-permute-start(bf16[512,1024]{1,0:T(8,128)(2,1)} %token_ref.3), channel_id=1, source_target_pairs={{0,1},{1,2},{2,3},{3,0},{4,5},{5,6},{6,7},{7,4},{8,9},{9,10},{10,1... | collective-permute-start | bytes 3145736 | tf_op jit(solution)/shard_map/ppermute | solution.py:295
  11.6 145.8 %all-gather.8.cloned.1.call-start = ((), (), s32[]{:S(2)}) async-start(), calls=%async_computation.1 | async-start | bytes 5308416 | tf_op jit(solution)/shard_map/all_gather | solution.py:372
  15.4 5.5 %copy-start.24 = (s32[1,4]{1,0:T(1,128)S(1)}, s32[1,4]{1,0:T(1,128)}, u32[]{:S(2)}) copy-start(s32[1,4]{1,0:T(1,128)} %param.17) | copy-start | bytes 52
  15.4 5.6 %copy-start.25 = (s32[1,4]{1,0:T(1,128)S(1)}, s32[1,4]{1,0:T(1,128)}, u32[]{:S(2)}) copy-start(s32[1,4]{1,0:T(1,128)} %param.16) | copy-start | bytes 52
  16.5 45.7 %collective-permute-start.4 = (bf16[96,1024]{1,0:T(8,128)(2,1)}, bf16[96,1024]{1,0:T(8,128)(2,1)}, u32[]{:S(2)}, u32[]{:S(2)}) collective-permute-start(bf16[96,1024]{1,0:T(8,128)(2,1)} %get-tuple-element.111), channel_id=1, source_target_pairs={{0,3},{1,0},{2,1},{3,2},{4,7},{5,4},{6,5},{7,6},{8,11},{9,8},{10,9... | collective-permute-start | bytes 589832 | tf_op jit(solution)/shard_map/ppermute | solution.py:295
  20.3 58.9 %collective-permute-start.3 = (bf16[96,1024]{1,0:T(8,128)(2,1)}, bf16[96,1024]{1,0:T(8,128)(2,1)}, u32[]{:S(2)}, u32[]{:S(2)}) collective-permute-start(bf16[96,1024]{1,0:T(8,128)(2,1)} %get-tuple-element.112), channel_id=1, source_target_pairs={{0,2},{1,3},{2,0},{3,1},{4,6},{5,7},{6,4},{7,5},{8,10},{9,11},{10,... | collective-permute-start | bytes 589832 | tf_op jit(solution)/shard_map/ppermute | solution.py:295
  20.3 58.9 %collective-permute-start.2 = (bf16[96,1024]{1,0:T(8,128)(2,1)}, bf16[96,1024]{1,0:T(8,128)(2,1)}, u32[]{:S(2)}, u32[]{:S(2)}) collective-permute-start(bf16[96,1024]{1,0:T(8,128)(2,1)} %get-tuple-element.113), channel_id=1, source_target_pairs={{0,1},{1,2},{2,3},{3,0},{4,5},{5,6},{6,7},{7,4},{8,9},{9,10},{10,1... | collective-permute-start | bytes 589832 | tf_op jit(solution)/shard_map/ppermute | solution.py:295
  62.2 23.2 %collective-permute-start.5 = (f32[128,192]{1,0:T(8,128)S(1)}, f32[128,192]{1,0:T(8,128)S(1)}, u32[]{:S(2)}, u32[]{:S(2)}) collective-permute-start(f32[128,192]{1,0:T(8,128)S(1)} %get-tuple-element.54), channel_id=1, source_target_pairs={{0,1},{1,2},{2,3},{3,0},{4,5},{5,6},{6,7},{7,4},{8,9},{9,10},{10,1... | collective-permute-start | bytes 294920 | tf_op jit(solution)/shard_map/ppermute | solution.py:295
  79.2 6.8 %collective-permute-start.6 = (f32[128,192]{1,0:T(8,128)S(1)}, f32[128,192]{1,0:T(8,128)S(1)}, u32[]{:S(2)}, u32[]{:S(2)}) collective-permute-start(f32[128,192]{1,0:T(8,128)S(1)} %get-tuple-element.55), channel_id=1, source_target_pairs={{0,2},{1,3},{2,0},{3,1},{4,6},{5,7},{6,4},{7,5},{8,10},{9,11},{10,... | collective-permute-start | bytes 294920 | tf_op jit(solution)/shard_map/ppermute | solution.py:295
  79.2 7.2 %collective-permute-start.7 = (f32[128,192]{1,0:T(8,128)S(1)}, f32[128,192]{1,0:T(8,128)S(1)}, u32[]{:S(2)}, u32[]{:S(2)}) collective-permute-start(f32[128,192]{1,0:T(8,128)S(1)} %get-tuple-element.56), channel_id=1, source_target_pairs={{0,3},{1,0},{2,1},{3,2},{4,7},{5,4},{6,5},{7,6},{8,11},{9,8},{10,9... | collective-permute-start | bytes 294920 | tf_op jit(solution)/shard_map/ppermute | solution.py:295
  89.0 7.4 %copy-start.18 = (f32[128,192]{1,0:T(8,128)S(1)}, f32[128,192]{1,0:T(8,128)}, u32[]{:S(2)}) copy-start(f32[128,192]{1,0:T(8,128)} %copy-done.17) | copy-start | bytes 294916
  89.0 7.4 %copy-start.20 = (f32[128,192]{1,0:T(8,128)S(1)}, f32[128,192]{1,0:T(8,128)}, u32[]{:S(2)}) copy-start(f32[128,192]{1,0:T(8,128)} %copy-done.19) | copy-start | bytes 294916
  89.1 7.4 %copy-start.22 = (f32[128,192]{1,0:T(8,128)S(1)}, f32[128,192]{1,0:T(8,128)}, u32[]{:S(2)}) copy-start(f32[128,192]{1,0:T(8,128)} %copy-done.21) | copy-start | bytes 294916
  92.9 31.9 %collective-permute-start.9 = (bf16[256,1024]{1,0:T(8,128)(2,1)}, bf16[256,1024]{1,0:T(8,128)(2,1)}, u32[]{:S(2)}, u32[]{:S(2)}) collective-permute-start(bf16[256,1024]{1,0:T(8,128)(2,1)} %slice.22), channel_id=1, source_target_pairs={{0,3},{1,0},{2,1},{3,2},{4,7},{5,4},{6,5},{7,6},{8,11},{9,8},{10,9... | collective-permute-start | bytes 1572872 | tf_op jit(solution)/shard_map/ppermute | solution.py:295
  96.4 28.4 %collective-permute-start.8 = (bf16[256,1024]{1,0:T(8,128)(2,1)}, bf16[256,1024]{1,0:T(8,128)(2,1)}, u32[]{:S(2)}, u32[]{:S(2)}) collective-permute-start(bf16[256,1024]{1,0:T(8,128)(2,1)} %slice.21), channel_id=1, source_target_pairs={{0,1},{1,2},{2,3},{3,0},{4,5},{5,6},{6,7},{7,4},{8,9},{9,10},{10,1... | collective-permute-start | bytes 1572872 | tf_op jit(solution)/shard_map/ppermute | solution.py:295
  96.5 25.1 %collective-permute-start.12 = (bf16[128,192]{1,0:T(8,128)(2,1)S(1)}, bf16[128,192]{1,0:T(8,128)(2,1)S(1)}, u32[]{:S(2)}, u32[]{:S(2)}) collective-permute-start(bf16[128,192]{1,0:T(8,128)(2,1)S(1)} %add_convert_fusion.refs_0_), channel_id=1, source_target_pairs={{0,3},{1,0},{2,1},{3,2},{4,7},{5,4},{6,5},{7,6},{8,11},{9,8},{10,9... | collective-permute-start | bytes 147464 | tf_op jit(solution)/shard_map/ppermute | solution.py:295
  100.3 24.5 %collective-permute-start.11 = (bf16[128,192]{1,0:T(8,128)(2,1)S(1)}, bf16[128,192]{1,0:T(8,128)(2,1)}, u32[]{:S(2)}, u32[]{:S(2)}) collective-permute-start(bf16[128,192]{1,0:T(8,128)(2,1)S(1)} %add_convert_fusion.refs_0_), channel_id=1, source_target_pairs={{0,2},{1,3},{2,0},{3,1},{4,6},{5,7},{6,4},{7,5},{8,10},{9,11},{10,... | collective-permute-start | bytes 147464 | tf_op jit(solution)/shard_map/ppermute | solution.py:295
  100.3 24.5 %collective-permute-start.10 = (bf16[128,192]{1,0:T(8,128)(2,1)S(1)}, bf16[128,192]{1,0:T(8,128)(2,1)}, u32[]{:S(2)}, u32[]{:S(2)}) collective-permute-start(bf16[128,192]{1,0:T(8,128)(2,1)S(1)} %add_convert_fusion.refs_0_), channel_id=1, source_target_pairs={{0,1},{1,2},{2,3},{3,0},{4,5},{5,6},{6,7},{7,4},{8,9},{9,10},{10,1... | collective-permute-start | bytes 147464 | tf_op jit(solution)/shard_map/ppermute | solution.py:295
  106.4 18.4 %copy-start.5 = (f32[512,256]{1,0:T(8,128)S(1)}, f32[512,256]{1,0:T(8,128)}, u32[]{:S(2)}) copy-start(f32[512,256]{1,0:T(8,128)} %pad_maximum_fusion.1.turn_ref) | copy-start | bytes 1572868
  106.4 18.4 %copy-start.8 = (bf16[24,64,128]{2,1,0:T(8,128)(2,1)S(1)}, bf16[24,64,128]{2,1,0:T(8,128)(2,1)}, u32[]{:S(2)}) copy-start(bf16[24,64,128]{2,1,0:T(8,128)(2,1)} %all-gather.1) | copy-start | bytes 1179652
  129.8 11.6 %copy-start.9 = (bf16[128,1024]{1,0:T(8,128)(2,1)S(1)}, bf16[128,1024]{1,0:T(8,128)(2,1)}, u32[]{:S(2)}) copy-start(bf16[128,1024]{1,0:T(8,128)(2,1)} %all-gather) | copy-start | bytes 786436
  135.4 19.5 %collective-permute-start.13 = (bf16[256,512]{1,0:T(8,128)(2,1)}, bf16[256,512]{1,0:T(8,128)(2,1)}, u32[]{:S(2)}, u32[]{:S(2)}) collective-permute-start(bf16[256,512]{1,0:T(8,128)(2,1)} %get-tuple-element.81.attended_ref), channel_id=1, source_target_pairs={{0,3},{1,0},{2,1},{3,2},{4,7},{5,4},{6,5},{7,6},{8,11},{9,8},{10,9... | collective-permute-start | bytes 786440 | tf_op jit(solution)/shard_map/ppermute | solution.py:295
  136.9 18.0 %collective-permute-start.16 = (bf16[256,512]{1,0:T(8,128)(2,1)}, bf16[256,512]{1,0:T(8,128)(2,1)}, u32[]{:S(2)}, u32[]{:S(2)}) collective-permute-start(bf16[256,512]{1,0:T(8,128)(2,1)} %get-tuple-element.94.attended_ref), channel_id=1, source_target_pairs={{0,1},{1,2},{2,3},{3,0},{4,5},{5,6},{6,7},{7,4},{8,9},{9,10},{10,1... | collective-permute-start | bytes 786440 | tf_op jit(solution)/shard_map/ppermute | solution.py:295
  137.5 25.9 %collective-permute-start.15 = (bf16[256,512]{1,0:T(8,128)(2,1)}, bf16[256,512]{1,0:T(8,128)(2,1)}, u32[]{:S(2)}, u32[]{:S(2)}) collective-permute-start(bf16[256,512]{1,0:T(8,128)(2,1)} %get-tuple-element.81.attended_ref), channel_id=1, source_target_pairs={{0,1},{1,2},{2,3},{3,0},{4,5},{5,6},{6,7},{7,4},{8,9},{9,10},{10,1... | collective-permute-start | bytes 786440 | tf_op jit(solution)/shard_map/ppermute | solution.py:295
  139.0 28.4 %collective-permute-start.18 = (bf16[256,512]{1,0:T(8,128)(2,1)}, bf16[256,512]{1,0:T(8,128)(2,1)}, u32[]{:S(2)}, u32[]{:S(2)}) collective-permute-start(bf16[256,512]{1,0:T(8,128)(2,1)} %get-tuple-element.94.attended_ref), channel_id=1, source_target_pairs={{0,3},{1,0},{2,1},{3,2},{4,7},{5,4},{6,5},{7,6},{8,11},{9,8},{10,9... | collective-permute-start | bytes 786440 | tf_op jit(solution)/shard_map/ppermute | solution.py:295
  143.3 17.0 %copy-start.13 = (f32[256,256]{1,0:T(8,128)}, f32[256,256]{1,0:T(8,128)S(1)}, u32[]{:S(2)}) copy-start(f32[256,256]{1,0:T(8,128)S(1)} %get-tuple-element.88.refs_1_) | copy-start | bytes 786436
  146.3 14.1 %copy-start.15 = (f32[256,256]{1,0:T(8,128)}, f32[256,256]{1,0:T(8,128)S(1)}, u32[]{:S(2)}) copy-start(f32[256,256]{1,0:T(8,128)S(1)} %get-tuple-element.96.refs_1_) | copy-start | bytes 786436
  154.8 18.5 %collective-permute-start.14 = (bf16[256,512]{1,0:T(8,128)(2,1)}, bf16[256,512]{1,0:T(8,128)(2,1)S(1)}, u32[]{:S(2)}, u32[]{:S(2)}) collective-permute-start(bf16[256,512]{1,0:T(8,128)(2,1)} %collective-permute-done.13.attended_ref), channel_id=1, source_target_pairs={{0,3},{1,0},{2,1},{3,2},{4,7},{5,4},{6,5},{7,6},{8,11},{9,8},{10,9... | collective-permute-start | bytes 786440 | tf_op jit(solution)/shard_map/ppermute | solution.py:295
  154.8 17.2 %collective-permute-start.17 = (bf16[256,512]{1,0:T(8,128)(2,1)}, bf16[256,512]{1,0:T(8,128)(2,1)S(1)}, u32[]{:S(2)}, u32[]{:S(2)}) collective-permute-start(bf16[256,512]{1,0:T(8,128)(2,1)} %collective-permute-done.16.attended_ref), channel_id=1, source_target_pairs={{0,1},{1,2},{2,3},{3,0},{4,5},{5,6},{6,7},{7,4},{8,9},{9,10},{10,1... | collective-permute-start | bytes 786440 | tf_op jit(solution)/shard_map/ppermute | solution.py:295
  157.4 3.0 %copy-start.12 = (f32[256,1024]{1,0:T(8,128)S(1)}, f32[256,1024]{1,0:T(8,128)}, u32[]{:S(2)}) copy-start(f32[256,1024]{1,0:T(8,128)} %copy-done.11) | copy-start | bytes 3145732
  (15 other events, 20.0 us)
Sparse Core Ops, SparseCore 0:
  11.7 21.1 all-gather.5
  89.2 40.0 all-gather.7

commit v16 on v15

--- a/solution.py
+++ b/solution.py
@@ -132,7 +132,7 @@
 
 
 def attend(planes_of, adapters, part, table, turn, up, shrink, tokens, weight, begun, earlier):
-    rows = tokens.shape[0]
+    rows = tokens.shape[0] // 2
     slots, _, head_size = weight.shape
     planes = len(shrink)
     arrays = [table, turn, up, *shrink, tokens, weight, begun, *earlier]
@@ -343,14 +343,13 @@
         return lax.dynamic_slice_in_dim(weight, start, depth, axis=1)
 
     opposite = planes // 2
-    half_rows = token_rows // 2
     right, left, begun, weights = [tokens], [tokens], [], [shard(here)]
     for step in range(1, opposite + 1):
         if step < opposite:
             moved = (turned(right[-1]), turned(left[-1], planes - 1))
             ahead = (here - step, here + step)
         else:
-            moved = (turned(right[-1][:half_rows]), turned(left[-1][half_rows:], planes - 1))
+            moved = (turned(right[-1]),)
             ahead = (here - step,)
         for tokens_of, weight_of in zip((right[-1], left[-1]), weights):
             begun = [project(tokens_of, weight_of, begun)]
@@ -361,7 +360,7 @@
             sums = [sums[0]] + [turned(sums[k], k) for k in range(1, planes)]
             out_up_all = lax.all_gather(after(output_up_maps, sums[0]), "dp", axis=0, tiled=True)
             own_down = lax.all_gather(after(out_down, sums[0]), "dp", axis=0)
-            side = (lines, sums, out_up_all, own_down, table, turn, up_all, own_rows)
+            side = (jnp.stack(lines), sums, out_up_all, own_down, table, turn, up_all, own_rows)
         elif step == 2:
             shrink = sum(sums[1:], sums[0]).astype(jnp.bfloat16)
             side = [shrink] + [turned(shrink, k) for k in range(1, planes)]
@@ -369,26 +368,29 @@
         moved, begun, weights, side = lax.optimization_barrier((moved, begun, weights, side))
         if step == 1:
             lines, sums, out_up_all, own_down, table, turn, up_all, own_rows = side
-            lines = lax.all_gather(jnp.stack(lines), PLANE, axis=0)
+            lines = lax.all_gather(lines, PLANE, axis=0)
         elif step == 2:
             shrink = side
         right.append(moved[0])
-        left.append(moved[1])
+        left.append(moved[-1])
 
     ids = jnp.concatenate([lax.axis_index("groups")[None], adapters])
+    lines = [lines[:, k] for k in range(planes - 1)]
     made, earlier = [], ()
     for part in range(2):
         own, *earlier = attend(
-            planes_of, adapters, part, table, turn, up_all, shrink, moved[part], weights[0],
+            planes_of, adapters, part, table, turn, up_all, shrink, right[-1], weights[0],
             begun[0], earlier,
         )
+        first = [*made[0][1], *lines] if part else []
         made.append([(own,)])
         for step in range(1, opposite):
             source = made[part][-1]
-            made[part].append((turned(source[0]), turned(source[-1], planes - 1)))
-        source = made[part][-1][part]
-        made[part].append((turned(source, (1, planes - 1)[part]),))
-    lines = [lines[:, k] for k in range(planes - 1)]
+            made[part].append(
+                (turned(source[0]), turned(after(source[-1], *first), planes - 1))
+            )
+            first = []
+        made[part].append((turned(made[part][-1][part], (1, planes - 1)[part]),))
     sums, before = [(), ()], []
     for step in range(opposite + 1):
         for part in range(2):

time: 183 us -> 192 us (1.049)
  waiting for transfers between devices: 49 us -> 69.5 us
  starting transfers between devices: 27.5 us -> 23.2 us
  local copies, waits for them, and re-layouts: 31.4 us -> 27.2 us
  Pallas kernels: 34.4 us -> 30.8 us
    ppermute x19 -> x18, waiting for transfers between devices: 48.9 us -> 69.5 us  [turned(): lax.ppermute(value, 'tensor', [(i, (i + turn) % planes) for i in range(pl...]
    ppermute x19 -> x18, starting transfers between devices: 27.5 us -> 23.2 us  [turned(): lax.ppermute(value, 'tensor', [(i, (i + turn) % planes) for i in range(pl...]
    slice x2 -> x0, local copies, waits for them, and re-layouts: 3.81 us -> none  [the longest x1 1.92 us: local(): right[-1][:half_rows]]
    pallas_call x14, Pallas kernels: 34.4 us -> 30.8 us  [call(): pl.pallas_call(kernel, out_shape=out, grid_spec=pltpu.PrefetchScalarGridS...]
    unnamed x54 -> x42, local copies, waits for them, and re-layouts: 11.3 us -> 10.7 us
  transfers between devices with their start and end apart: 21 -> 20, of which waited for: 8 -> 6; matrix products, arithmetic and copies ran while one was open for 13% -> 12% of each run, Pallas kernels for 18% -> 15%
where the time goes in v16:
time: 192 us
  waiting for transfers between devices  69.5 us (36%)
  Pallas kernels  30.8 us (16%)
  local copies, waits for them, and re-layouts  27.2 us (14%)
  starting transfers between devices  23.2 us (12%)
  blocking collectives  20.5 us (11%)
  between operations  13.9 us (7%)
  other arithmetic  6.39 us (3%)
    ppermute x18, waiting for transfers between devices, turned(): lax.ppermute(value, 'tensor', [(i, (i + turn) % planes) for i in range(pl...  69.5 us
    pallas_call x14, Pallas kernels, call(): pl.pallas_call(kernel, out_shape=out, grid_spec=pltpu.PrefetchScalarGridS...  30.8 us
    ppermute x18, starting transfers between devices, turned(): lax.ppermute(value, 'tensor', [(i, (i + turn) % planes) for i in range(pl...  23.2 us
    unnamed x42, local copies, waits for them, and re-layouts  10.7 us
    all_gather x1, blocking collectives, local(): lax.all_gather(after(output_up_maps, sums[0]), 'dp', axis=0, tiled=True)  7.37 us
    all_gather x1, blocking collectives, local(): lax.all_gather(jnp.transpose(adapter_up_maps[0], (1, 0, 2)), 'dp', axis=0)  6.88 us
    all_gather x1, blocking collectives, local(): own_down = lax.all_gather(after(out_down, sums[0]), 'dp', axis=0)  6.3 us
    dynamic_slice x1, local copies, waits for them, and re-layouts, shard(): return lax.dynamic_slice_in_dim(weight, start, depth, axis=1)  5.15 us
  transfers between devices with their start and end apart: 20, of which 6 were waited for; matrix products, arithmetic and copies ran while one was open for 12% of the time, Pallas kernels for 15%

profile of v16, /device:TPU:0, one launch (start us, length us, event | category | flops | bytes accessed | tf_op | source)
XLA Modules:
  0.0 191.6 jit_solution(9398635972390478161)
XLA Ops:
  6.5 3.0 %collective-permute-start = (bf16[512,1024]{1,0:T(8,128)(2,1)}, bf16[512,1024]{1,0:T(8,128)(2,1)}, u32[]{:S(2)}, u32[]{:S(2)}) collective-permute-start(bf16[512,1024]{1,0:T(8,128)(2,1)} %token_ref.3), channel_id=1, source_target_pairs={{0,1},{1,2},{2,3},{3,0},{4,5},{5,6},{6,7},{7,4},{8,9},{9,10},{10,1... | collective-permute-start | bytes 3145736 | tf_op jit(solution)/shard_map/ppermute | solution.py:295
  9.6 2.0 %collective-permute-start.1 = (bf16[512,1024]{1,0:T(8,128)(2,1)}, bf16[512,1024]{1,0:T(8,128)(2,1)}, u32[]{:S(2)}, u32[]{:S(2)}) collective-permute-start(bf16[512,1024]{1,0:T(8,128)(2,1)} %token_ref.3), channel_id=1, source_target_pairs={{0,3},{1,0},{2,1},{3,2},{4,7},{5,4},{6,5},{7,6},{8,11},{9,8},{10,9... | collective-permute-start | bytes 3145736 | tf_op jit(solution)/shard_map/ppermute | solution.py:295
  12.6 2.8 %fusion.4 = (bf16[64,1,1024]{2,1,0:T(2,128)(2,1)S(1)}, bf16[64,1,1024]{2,1,0:T(2,128)(2,1)S(1)}, bf16[64,1,1024]{2,1,0:T(2,128)(2,1)S(1)}) fusion(bf16[128,4,4096]{2,1,0:T(4,128)(2,1)} %param.11, s32[]{:T(128)S(6)} %select_n.90, s32[]{:T(128)S(6)} %select_n.93, s32[]{:T(128)S(6)} %select_n.96, s32[]{:T(128)S(6)} %select_n.99, s32[]{:T(128)S(6)} %select_n.100), kind=kLoop, calls=%fused_computation.39 | loop fusion | bytes 786452 | tf_op jit(solution)/shard_map/dynamic_slice | solution.py:334
  16.4 2.0 %collective-permute-start.4 = (bf16[96,1024]{1,0:T(8,128)(2,1)}, bf16[96,1024]{1,0:T(8,128)(2,1)S(1)}, u32[]{:S(2)}, u32[]{:S(2)}) collective-permute-start(bf16[96,1024]{1,0:T(8,128)(2,1)} %get-tuple-element.109), channel_id=1, source_target_pairs={{0,3},{1,0},{2,1},{3,2},{4,7},{5,4},{6,5},{7,6},{8,11},{9,8},{10,9... | collective-permute-start | bytes 589832 | tf_op jit(solution)/shard_map/ppermute | solution.py:295
  19.9 2.6 %dynamic-slice_bitcast_fusion.4 = bf16[4,128,1024]{2,0,1:T(4,128)(2,1)} fusion(bf16[128,4,4096]{2,1,0:T(4,128)(2,1)} %param.11, s32[]{:T(128)S(6)} %select_n.102), kind=kLoop, calls=%fused_computation.7 | loop fusion | bytes 2097156 | tf_op jit(solution)/shard_map/transpose | solution.py:319
  24.5 5.1 %dynamic-slice_bitcast_fusion = (bf16[6,1024,128]{2,1,0:T(8,128)(2,1)S(1)}, bf16[6,1024,128]{2,1,0:T(8,128)(2,1)}, bf16[6,1024,128]{2,1,0:T(8,128)(2,1)}, bf16[6,1024,128]{2,1,0:T(8,128)(2,1)}) fusion(bf16[4096,6,128]{2,0,1:T(8,128)(2,1)} %param.10, s32[]{:T(128)S(6)} %select_n.98, s32[]{:T(128)S(6)} %select_n.85, s32[]{:T(128)S(6)} %select_n.83, s32[]{:T(128)S(6)} %select_n.87), kind=kLoop, calls=%fused_computation.3 | loop fusion | bytes 12582928 | tf_op jit(solution)/shard_map/dynamic_slice | solution.py:343
  35.0 6.9 %all-gather.1 = bf16[24,64,128]{2,1,0:T(8,128)(2,1)} all-gather(bf16[6,64,128]{2,1,0:T(8,128)(2,1)S(1)} %bitcast.66), channel_id=3, replica_groups=mesh['groups'=2,'dp'=4,'tensor'=4] {'dp'}, dimensions={0}, use_global_device_ids=true | all-gather | bytes 491520 | tf_op jit(solution)/shard_map/all_gather | solution.py:299
  41.9 19.2 %collective-permute-done.4 = bf16[96,1024]{1,0:T(8,128)(2,1)S(1)} collective-permute-done((bf16[96,1024]{1,0:T(8,128)(2,1)}, bf16[96,1024]{1,0:T(8,128)(2,1)S(1)}, u32[]{:S(2)}, u32[]{:S(2)}) %collective-permute-start.4) | collective-permute-done | bytes 196640 | tf_op jit(solution)/shard_map/ppermute | solution.py:295
  61.1 13.3 %collective-permute-done.3 = bf16[96,1024]{1,0:T(8,128)(2,1)} collective-permute-done((bf16[96,1024]{1,0:T(8,128)(2,1)}, bf16[96,1024]{1,0:T(8,128)(2,1)}, u32[]{:S(2)}, u32[]{:S(2)}) %collective-permute-start.3) | collective-permute-done | bytes 196640 | tf_op jit(solution)/shard_map/ppermute | solution.py:295
  74.4 1.9 pad_maximum_fusion
  78.9 2.6 %shrink.1 = (f32[128,192]{1,0:T(8,128)S(1)}, f32[128,192]{1,0:T(8,128)S(1)}, f32[128,192]{1,0:T(8,128)S(1)}, f32[128,192]{1,0:T(8,128)S(1)}) custom-call(s32[5]{0:T(128)S(1)} %pad_add_fusion.3.ids_ref, s32[512,2]{1,0:T(8,128)S(1)} %copy.40.table_ref, bf16[512,1024]{1,0:T(8,128)(2,1)S(1)} %copy-done.7, bf16[4,192,1024]{2,1,0:T(8,128)(2,1)S(1)} %copy-done.10), custom_call_target="tpu_custom_call" | custom-call | bytes 7876608 | tf_op jit(solution)/shard_map/shrink/pallas_call | solution.py:26
  83.0 3.1 %collective-permute-start.7 = (f32[128,192]{1,0:T(8,128)S(1)}, f32[128,192]{1,0:T(8,128)S(1)}, u32[]{:S(2)}, u32[]{:S(2)}) collective-permute-start(f32[128,192]{1,0:T(8,128)S(1)} %get-tuple-element.54), channel_id=1, source_target_pairs={{0,3},{1,0},{2,1},{3,2},{4,7},{5,4},{6,5},{7,6},{8,11},{9,8},{10,9... | collective-permute-start | bytes 294920 | tf_op jit(solution)/shard_map/ppermute | solution.py:295
  86.0 7.4 %all_gather.25.refs_3_ = bf16[4,64,1024]{2,1,0:T(8,128)(2,1)S(1)} all-gather(bf16[1,64,1024]{2,1,0:T(8,128)(2,1)} %param.15), channel_id=1, replica_groups=mesh['groups'=2,'dp'=4,'tensor'=4] {'dp'}, dimensions={0}, use_global_device_ids=true | all-gather | bytes 655360 | tf_op jit(solution)/shard_map/all_gather | solution.py:361
  93.4 6.3 %all-gather = bf16[128,1024]{1,0:T(8,128)(2,1)} all-gather(bf16[32,1024]{1,0:T(8,128)(2,1)S(1)} %bitcast_dynamic-update-slice_fusion), channel_id=2, replica_groups=mesh['groups'=2,'dp'=4,'tensor'=4] {'dp'}, dimensions={0}, use_global_device_ids=true | all-gather | bytes 327680 | tf_op jit(solution)/shard_map/all_gather | solution.py:362
  102.7 2.1 %collective-permute-start.9 = (bf16[128,192]{1,0:T(8,128)(2,1)S(1)}, bf16[128,192]{1,0:T(8,128)(2,1)S(1)}, u32[]{:S(2)}, u32[]{:S(2)}) collective-permute-start(bf16[128,192]{1,0:T(8,128)(2,1)S(1)} %add_convert_fusion.refs_0_), channel_id=1, source_target_pairs={{0,1},{1,2},{2,3},{3,0},{4,5},{5,6},{6,7},{7,4},{8,9},{9,10},{10,1... | collective-permute-start | bytes 147464 | tf_op jit(solution)/shard_map/ppermute | solution.py:295
  104.8 1.8 collective-permute-start.10
  110.3 2.3 %project.4.refs_0_ = f32[512,768]{1,0:T(8,128)S(1)} custom-call(s32[1]{0:T(128)} %constant.146.clone.1.ids_ref, bf16[512,1024]{1,0:T(8,128)(2,1)} %collective-permute-done.token_ref, bf16[6,1024,128]{2,1,0:T(8,128)(2,1)S(1)} %copy-done.4, f32[512,768]{1,0:T(8,128)S(1)} %copy-done.1), custom_call_target="tpu_custom_call" | custom-call | bytes 12582912 | tf_op jit(solution)/shard_map/project/pallas_call | solution.py:26
  112.7 2.3 %project.5.refs_6_ = f32[512,768]{1,0:T(8,128)S(1)} custom-call(s32[1]{0:T(128)} %constant.146.clone.1.ids_ref, bf16[512,1024]{1,0:T(8,128)(2,1)} %collective-permute-done.1.token_ref, bf16[6,1024,128]{2,1,0:T(8,128)(2,1)S(1)} %copy-done.3, f32[512,768]{1,0:T(8,128)S(1)} %project.4.refs_0_), custom_call_target="tpu_custom_call" | custom-call | bytes 12582912 | tf_op jit(solution)/shard_map/project/pallas_call | solution.py:26
  115.0 15.7 %collective-permute-done.9.refs_1_ = bf16[128,192]{1,0:T(8,128)(2,1)S(1)} collective-permute-done((bf16[128,192]{1,0:T(8,128)(2,1)S(1)}, bf16[128,192]{1,0:T(8,128)(2,1)S(1)}, u32[]{:S(2)}, u32[]{:S(2)}) %collective-permute-start.9) | collective-permute-done | bytes 49184 | tf_op jit(solution)/shard_map/ppermute | solution.py:295
  130.7 2.3 %collective-permute-done.10.refs_2_ = bf16[128,192]{1,0:T(8,128)(2,1)} collective-permute-done((bf16[128,192]{1,0:T(8,128)(2,1)S(1)}, bf16[128,192]{1,0:T(8,128)(2,1)}, u32[]{:S(2)}, u32[]{:S(2)}) %collective-permute-start.10) | collective-permute-done | bytes 49184 | tf_op jit(solution)/shard_map/ppermute | solution.py:295
  133.0 4.9 %attend.2 = (bf16[256,512]{1,0:T(8,128)(2,1)}, bf16[256,128]{1,0:T(8,128)(2,1)S(1)}, bf16[256,128]{1,0:T(8,128)(2,1)S(1)}) custom-call(s32[8]{0:T(128)S(1)} %pad_add_fusion.2.ids_ref, s32[512,2]{1,0:T(8,128)S(1)} %copy.44.table_ref.refs_2_, f32[512,256]{1,0:T(8,128)S(1)} %copy-done.5, bf16[4,6,64,128]{3,2,1,0:T(8,128)(2,1)S(1)} %bitcast.57, ...), custom_call_target="tpu_custom_call" | custom-call | bytes 15937536 | tf_op jit(solution)/shard_map/attend/pallas_call | solution.py:26
  137.9 1.9 collective-permute-start.12
  139.8 2.0 %collective-permute-start.13 = (bf16[256,512]{1,0:T(8,128)(2,1)}, bf16[256,512]{1,0:T(8,128)(2,1)}, u32[]{:S(2)}, u32[]{:S(2)}) collective-permute-start(bf16[256,512]{1,0:T(8,128)(2,1)} %get-tuple-element.79.attended_ref), channel_id=1, source_target_pairs={{0,3},{1,0},{2,1},{3,2},{4,7},{5,4},{6,5},{7,6},{8,11},{9,8},{10,9... | collective-permute-start | bytes 786440 | tf_op jit(solution)/shard_map/ppermute | solution.py:295
  141.7 4.9 %attend.3 = (bf16[256,512]{1,0:T(8,128)(2,1)S(1)}, bf16[256,128]{1,0:T(8,128)(2,1)}, bf16[256,128]{1,0:T(8,128)(2,1)}) custom-call(s32[8]{0:T(128)S(1)} %pad_add_fusion.2.ids_ref, s32[512,2]{1,0:T(8,128)S(1)} %copy.44.table_ref.refs_2_, f32[512,256]{1,0:T(8,128)S(1)} %copy-done.5, bf16[4,6,64,128]{3,2,1,0:T(8,128)(2,1)S(1)} %bitcast.58, ...), custom_call_target="tpu_custom_call" | custom-call | bytes 16330752 | tf_op jit(solution)/shard_map/attend/pallas_call | solution.py:26
  147.3 3.2 %slice_bitcast_fusion = (bf16[8,96,1024]{2,1,0:T(8,128)(2,1)S(1)}, bf16[8,96,1024]{2,1,0:T(8,128)(2,1)S(1)}, bf16[8,96,1024]{2,1,0:T(8,128)(2,1)S(1)}) fusion(bf16[8,3,96,1024]{3,2,1,0:T(8,128)(2,1)} %bitcast.61), kind=kLoop, calls=%fused_computation | loop fusion | bytes 9437184 | tf_op jit(solution)/shard_map/squeeze | solution.py:378
  150.5 3.1 %collective-permute-done.13.attended_ref = bf16[256,512]{1,0:T(8,128)(2,1)} collective-permute-done((bf16[256,512]{1,0:T(8,128)(2,1)}, bf16[256,512]{1,0:T(8,128)(2,1)}, u32[]{:S(2)}, u32[]{:S(2)}) %collective-permute-start.13) | collective-permute-done | bytes 262176 | tf_op jit(solution)/shard_map/ppermute | solution.py:295
  153.7 2.1 %collective-permute-start.14 = (bf16[256,512]{1,0:T(8,128)(2,1)S(1)}, bf16[256,512]{1,0:T(8,128)(2,1)S(1)}, u32[]{:S(2)}, u32[]{:S(2)}) collective-permute-start(bf16[256,512]{1,0:T(8,128)(2,1)S(1)} %copy-done.12), channel_id=1, source_target_pairs={{0,3},{1,0},{2,1},{3,2},{4,7},{5,4},{6,5},{7,6},{8,11},{9,8},{10,9... | collective-permute-start | bytes 786440 | tf_op jit(solution)/shard_map/ppermute | solution.py:295
  156.0 15.8 %collective-permute-done.14.attended_ref = bf16[256,512]{1,0:T(8,128)(2,1)S(1)} collective-permute-done((bf16[256,512]{1,0:T(8,128)(2,1)S(1)}, bf16[256,512]{1,0:T(8,128)(2,1)S(1)}, u32[]{:S(2)}, u32[]{:S(2)}) %collective-permute-start.14) | collective-permute-done | bytes 262176 | tf_op jit(solution)/shard_map/ppermute | solution.py:295
  172.9 2.0 %project_out.11 = (f32[256,1024]{1,0:T(8,128)S(1)}, f32[256,256]{1,0:T(8,128)S(1)}) custom-call(s32[5]{0:T(128)S(1)} %pad_add_fusion.1.ids_ref, bf16[256,512]{1,0:T(8,128)(2,1)} %get-tuple-element.79.attended_ref, bf16[512,1024]{1,0:T(8,128)(2,1)S(1)} %bitcast.56, bf16[4,32,1024]{2,1,0:T(8,128)(2,1)S(1)} %bitcast.60), custom_call_target="tpu_custom_call" | custom-call | bytes 4718592 | tf_op jit(solution)/shard_map/project_out/pallas_call | solution.py:26
  174.9 2.0 %project_out.12 = (f32[256,1024]{1,0:T(8,128)S(1)}, f32[256,256]{1,0:T(8,128)S(1)}) custom-call(s32[5]{0:T(128)S(1)} %pad_add_fusion.1.ids_ref, bf16[256,512]{1,0:T(8,128)(2,1)} %collective-permute-done.12.attended_ref, bf16[8,96,1024]{2,1,0:T(8,128)(2,1)S(1)} %get-tuple-element.103.w_ref.down_ref, ...), custom_call_target="tpu_custom_call" | custom-call | bytes 14155776 | tf_op jit(solution)/shard_map/project_out/pallas_call | solution.py:26
  177.0 2.0 %project_out.13 = (f32[256,1024]{1,0:T(8,128)S(1)}, f32[256,256]{1,0:T(8,128)S(1)}) custom-call(s32[5]{0:T(128)S(1)} %pad_add_fusion.1.ids_ref, bf16[256,512]{1,0:T(8,128)(2,1)} %collective-permute-done.13.attended_ref, bf16[8,96,1024]{2,1,0:T(8,128)(2,1)S(1)} %get-tuple-element.101.w_ref.down_ref, ...), custom_call_target="tpu_custom_call" | custom-call | bytes 14155776 | tf_op jit(solution)/shard_map/project_out/pallas_call | solution.py:26
  182.5 2.2 %project_out.15 = bf16[512,1024]{1,0:T(8,128)(2,1)} custom-call(s32[5]{0:T(128)S(1)} %pad_add_fusion.1.ids_ref, bf16[256,512]{1,0:T(8,128)(2,1)S(1)} %collective-permute-done.15.attended_ref, bf16[8,96,1024]{2,1,0:T(8,128)(2,1)S(1)} %get-tuple-element.102.w_ref.down_ref, bf16[8,96,1024]{2,1,0:T(8,128)(2,1)S(1)} %get-tuple-element.102.w_ref.down_ref, ...), custom_call_target="tpu_custom_call" | custom-call | bytes 17313792 | tf_op jit(solution)/shard_map/project_out/pallas_call | solution.py:26
  (98 shorter events, 26.9 us)
Async XLA Ops:
  6.5 69.8 %all-gather.6.cloned.1.call-start = ((), (), s32[]{:S(2)}) async-start(), calls=%async_computation | async-start | bytes 1966080 | tf_op jit(solution)/shard_map/all_gather | solution.py:298
  6.5 93.2 %collective-permute-start = (bf16[512,1024]{1,0:T(8,128)(2,1)}, bf16[512,1024]{1,0:T(8,128)(2,1)}, u32[]{:S(2)}, u32[]{:S(2)}) collective-permute-start(bf16[512,1024]{1,0:T(8,128)(2,1)} %token_ref.3), channel_id=1, source_target_pairs={{0,1},{1,2},{2,3},{3,0},{4,5},{5,6},{6,7},{7,4},{8,9},{9,10},{10,1... | collective-permute-start | bytes 3145736 | tf_op jit(solution)/shard_map/ppermute | solution.py:295
  9.6 90.2 %collective-permute-start.1 = (bf16[512,1024]{1,0:T(8,128)(2,1)}, bf16[512,1024]{1,0:T(8,128)(2,1)}, u32[]{:S(2)}, u32[]{:S(2)}) collective-permute-start(bf16[512,1024]{1,0:T(8,128)(2,1)} %token_ref.3), channel_id=1, source_target_pairs={{0,3},{1,0},{2,1},{3,2},{4,7},{5,4},{6,5},{7,6},{8,11},{9,8},{10,9... | collective-permute-start | bytes 3145736 | tf_op jit(solution)/shard_map/ppermute | solution.py:295
  11.6 135.7 %all-gather.8.cloned.1.call-start = ((), (), s32[]{:S(2)}) async-start(), calls=%async_computation.1 | async-start | bytes 5308416 | tf_op jit(solution)/shard_map/all_gather | solution.py:371
  15.4 4.0 %copy-start.18 = (s32[1,4]{1,0:T(1,128)S(1)}, s32[1,4]{1,0:T(1,128)}, u32[]{:S(2)}) copy-start(s32[1,4]{1,0:T(1,128)} %param.17) | copy-start | bytes 52
  15.4 4.2 %copy-start.19 = (s32[1,4]{1,0:T(1,128)S(1)}, s32[1,4]{1,0:T(1,128)}, u32[]{:S(2)}) copy-start(s32[1,4]{1,0:T(1,128)} %param.16) | copy-start | bytes 52
  16.4 44.6 %collective-permute-start.4 = (bf16[96,1024]{1,0:T(8,128)(2,1)}, bf16[96,1024]{1,0:T(8,128)(2,1)S(1)}, u32[]{:S(2)}, u32[]{:S(2)}) collective-permute-start(bf16[96,1024]{1,0:T(8,128)(2,1)} %get-tuple-element.109), channel_id=1, source_target_pairs={{0,3},{1,0},{2,1},{3,2},{4,7},{5,4},{6,5},{7,6},{8,11},{9,8},{10,9... | collective-permute-start | bytes 589832 | tf_op jit(solution)/shard_map/ppermute | solution.py:295
  18.5 55.9 %collective-permute-start.3 = (bf16[96,1024]{1,0:T(8,128)(2,1)}, bf16[96,1024]{1,0:T(8,128)(2,1)}, u32[]{:S(2)}, u32[]{:S(2)}) collective-permute-start(bf16[96,1024]{1,0:T(8,128)(2,1)} %get-tuple-element.108), channel_id=1, source_target_pairs={{0,2},{1,3},{2,0},{3,1},{4,6},{5,7},{6,4},{7,5},{8,10},{9,11},{10,... | collective-permute-start | bytes 589832 | tf_op jit(solution)/shard_map/ppermute | solution.py:295
  18.5 55.9 %collective-permute-start.2 = (bf16[96,1024]{1,0:T(8,128)(2,1)S(1)}, bf16[96,1024]{1,0:T(8,128)(2,1)}, u32[]{:S(2)}, u32[]{:S(2)}) collective-permute-start(bf16[96,1024]{1,0:T(8,128)(2,1)S(1)} %get-tuple-element.107), channel_id=1, source_target_pairs={{0,1},{1,2},{2,3},{3,0},{4,5},{5,6},{6,7},{7,4},{8,9},{9,10},{10,1... | collective-permute-start | bytes 589832 | tf_op jit(solution)/shard_map/ppermute | solution.py:295
  29.9 1.7 copy-start.2
  32.8 2.2 %copy-start.17 = (bf16[1,64,6,128]{3,1,2,0:T(8,128)(2,1)S(1)}, bf16[1,64,6,128]{3,1,2,0:T(8,128)(2,1)}, u32[]{:S(2)}) copy-start(bf16[1,64,6,128]{3,1,2,0:T(8,128)(2,1)} %param.13) | copy-start | bytes 294916
  77.5 1.4 copy-start.10
  82.2 19.5 %copy-start.14 = (f32[128,192]{1,0:T(8,128)S(1)}, f32[128,192]{1,0:T(8,128)}, u32[]{:S(2)}) copy-start(f32[128,192]{1,0:T(8,128)} %copy-done.13) | copy-start | bytes 294916
  82.2 17.5 %collective-permute-start.5 = (f32[128,192]{1,0:T(8,128)S(1)}, f32[128,192]{1,0:T(8,128)S(1)}, u32[]{:S(2)}, u32[]{:S(2)}) collective-permute-start(f32[128,192]{1,0:T(8,128)S(1)} %get-tuple-element.52), channel_id=1, source_target_pairs={{0,1},{1,2},{2,3},{3,0},{4,5},{5,6},{6,7},{7,4},{8,9},{9,10},{10,1... | collective-permute-start | bytes 294920 | tf_op jit(solution)/shard_map/ppermute | solution.py:295
  82.2 17.5 %collective-permute-start.6 = (f32[128,192]{1,0:T(8,128)S(1)}, f32[128,192]{1,0:T(8,128)S(1)}, u32[]{:S(2)}, u32[]{:S(2)}) collective-permute-start(f32[128,192]{1,0:T(8,128)S(1)} %get-tuple-element.53), channel_id=1, source_target_pairs={{0,2},{1,3},{2,0},{3,1},{4,6},{5,7},{6,4},{7,5},{8,10},{9,11},{10,... | collective-permute-start | bytes 294920 | tf_op jit(solution)/shard_map/ppermute | solution.py:295
  83.0 16.8 %collective-permute-start.7 = (f32[128,192]{1,0:T(8,128)S(1)}, f32[128,192]{1,0:T(8,128)S(1)}, u32[]{:S(2)}, u32[]{:S(2)}) collective-permute-start(f32[128,192]{1,0:T(8,128)S(1)} %get-tuple-element.54), channel_id=1, source_target_pairs={{0,3},{1,0},{2,1},{3,2},{4,7},{5,4},{6,5},{7,6},{8,11},{9,8},{10,9... | collective-permute-start | bytes 294920 | tf_op jit(solution)/shard_map/ppermute | solution.py:295
  101.1 31.9 %collective-permute-start.8 = (bf16[512,1024]{1,0:T(8,128)(2,1)}, bf16[512,1024]{1,0:T(8,128)(2,1)}, u32[]{:S(2)}, u32[]{:S(2)}) collective-permute-start(bf16[512,1024]{1,0:T(8,128)(2,1)} %collective-permute-done.token_ref), channel_id=1, source_target_pairs={{0,1},{1,2},{2,3},{3,0},{4,5},{5,6},{6,7},{7,4},{8,9},{9,10},{10,1... | collective-permute-start | bytes 3145736 | tf_op jit(solution)/shard_map/ppermute | solution.py:295
  102.7 28.0 %collective-permute-start.9 = (bf16[128,192]{1,0:T(8,128)(2,1)S(1)}, bf16[128,192]{1,0:T(8,128)(2,1)S(1)}, u32[]{:S(2)}, u32[]{:S(2)}) collective-permute-start(bf16[128,192]{1,0:T(8,128)(2,1)S(1)} %add_convert_fusion.refs_0_), channel_id=1, source_target_pairs={{0,1},{1,2},{2,3},{3,0},{4,5},{5,6},{6,7},{7,4},{8,9},{9,10},{10,1... | collective-permute-start | bytes 147464 | tf_op jit(solution)/shard_map/ppermute | solution.py:295
  104.8 28.2 %collective-permute-start.10 = (bf16[128,192]{1,0:T(8,128)(2,1)S(1)}, bf16[128,192]{1,0:T(8,128)(2,1)}, u32[]{:S(2)}, u32[]{:S(2)}) collective-permute-start(bf16[128,192]{1,0:T(8,128)(2,1)S(1)} %add_convert_fusion.refs_0_), channel_id=1, source_target_pairs={{0,2},{1,3},{2,0},{3,1},{4,6},{5,7},{6,4},{7,5},{8,10},{9,11},{10,... | collective-permute-start | bytes 147464 | tf_op jit(solution)/shard_map/ppermute | solution.py:295
  106.6 26.4 %collective-permute-start.11 = (bf16[128,192]{1,0:T(8,128)(2,1)S(1)}, bf16[128,192]{1,0:T(8,128)(2,1)}, u32[]{:S(2)}, u32[]{:S(2)}) collective-permute-start(bf16[128,192]{1,0:T(8,128)(2,1)S(1)} %add_convert_fusion.refs_0_), channel_id=1, source_target_pairs={{0,3},{1,0},{2,1},{3,2},{4,7},{5,4},{6,5},{7,6},{8,11},{9,8},{10,9... | collective-permute-start | bytes 147464 | tf_op jit(solution)/shard_map/ppermute | solution.py:295
  107.4 1.5 copy-start.1
  110.3 2.3 %copy-start.3 = (bf16[6,1024,128]{2,1,0:T(8,128)(2,1)S(1)}, bf16[6,1024,128]{2,1,0:T(8,128)(2,1)}, u32[]{:S(2)}) copy-start(bf16[6,1024,128]{2,1,0:T(8,128)(2,1)} %get-tuple-element.62.w_ref) | copy-start | bytes 4718596
  112.7 20.3 %copy-start.5 = (f32[512,256]{1,0:T(8,128)S(1)}, f32[512,256]{1,0:T(8,128)}, u32[]{:S(2)}) copy-start(f32[512,256]{1,0:T(8,128)} %pad_maximum_fusion.1.turn_ref) | copy-start | bytes 1572868
  112.7 20.3 %copy-start.8 = (bf16[24,64,128]{2,1,0:T(8,128)(2,1)S(1)}, bf16[24,64,128]{2,1,0:T(8,128)(2,1)}, u32[]{:S(2)}) copy-start(bf16[24,64,128]{2,1,0:T(8,128)(2,1)} %all-gather.1) | copy-start | bytes 1179652
  137.9 12.6 %collective-permute-start.12 = (bf16[256,512]{1,0:T(8,128)(2,1)}, bf16[256,512]{1,0:T(8,128)(2,1)}, u32[]{:S(2)}, u32[]{:S(2)}) collective-permute-start(bf16[256,512]{1,0:T(8,128)(2,1)} %get-tuple-element.79.attended_ref), channel_id=1, source_target_pairs={{0,1},{1,2},{2,3},{3,0},{4,5},{5,6},{6,7},{7,4},{8,9},{9,10},{10,1... | collective-permute-start | bytes 786440 | tf_op jit(solution)/shard_map/ppermute | solution.py:295
  139.8 13.9 %collective-permute-start.13 = (bf16[256,512]{1,0:T(8,128)(2,1)}, bf16[256,512]{1,0:T(8,128)(2,1)}, u32[]{:S(2)}, u32[]{:S(2)}) collective-permute-start(bf16[256,512]{1,0:T(8,128)(2,1)} %get-tuple-element.79.attended_ref), channel_id=1, source_target_pairs={{0,3},{1,0},{2,1},{3,2},{4,7},{5,4},{6,5},{7,6},{8,11},{9,8},{10,9... | collective-permute-start | bytes 786440 | tf_op jit(solution)/shard_map/ppermute | solution.py:295
  147.3 6.3 %copy-start.12 = (bf16[256,512]{1,0:T(8,128)(2,1)S(1)}, bf16[256,512]{1,0:T(8,128)(2,1)}, u32[]{:S(2)}) copy-start(bf16[256,512]{1,0:T(8,128)(2,1)} %copy-done.11) | copy-start | bytes 786436
  147.3 24.5 %copy-start.9 = (bf16[128,1024]{1,0:T(8,128)(2,1)S(1)}, bf16[128,1024]{1,0:T(8,128)(2,1)}, u32[]{:S(2)}) copy-start(bf16[128,1024]{1,0:T(8,128)(2,1)} %all-gather) | copy-start | bytes 786436
  153.7 18.1 %collective-permute-start.14 = (bf16[256,512]{1,0:T(8,128)(2,1)S(1)}, bf16[256,512]{1,0:T(8,128)(2,1)S(1)}, u32[]{:S(2)}, u32[]{:S(2)}) collective-permute-start(bf16[256,512]{1,0:T(8,128)(2,1)S(1)} %copy-done.12), channel_id=1, source_target_pairs={{0,3},{1,0},{2,1},{3,2},{4,7},{5,4},{6,5},{7,6},{8,11},{9,8},{10,9... | collective-permute-start | bytes 786440 | tf_op jit(solution)/shard_map/ppermute | solution.py:295
  155.7 23.3 %collective-permute-start.16 = (bf16[256,512]{1,0:T(8,128)(2,1)S(1)}, bf16[256,512]{1,0:T(8,128)(2,1)S(1)}, u32[]{:S(2)}, u32[]{:S(2)}) collective-permute-start(bf16[256,512]{1,0:T(8,128)(2,1)S(1)} %copy-done.12), channel_id=1, source_target_pairs={{0,1},{1,2},{2,3},{3,0},{4,5},{5,6},{6,7},{7,4},{8,9},{9,10},{10,1... | collective-permute-start | bytes 786440 | tf_op jit(solution)/shard_map/ppermute | solution.py:295
  155.7 24.3 %collective-permute-start.17 = (bf16[256,512]{1,0:T(8,128)(2,1)}, bf16[256,512]{1,0:T(8,128)(2,1)S(1)}, u32[]{:S(2)}, u32[]{:S(2)}) collective-permute-start(bf16[256,512]{1,0:T(8,128)(2,1)} %collective-permute-done.12.attended_ref), channel_id=1, source_target_pairs={{0,1},{1,2},{2,3},{3,0},{4,5},{5,6},{6,7},{7,4},{8,9},{9,10},{10,1... | collective-permute-start | bytes 786440 | tf_op jit(solution)/shard_map/ppermute | solution.py:295
  171.8 10.7 %collective-permute-start.15 = (bf16[256,512]{1,0:T(8,128)(2,1)S(1)}, bf16[256,512]{1,0:T(8,128)(2,1)S(1)}, u32[]{:S(2)}, u32[]{:S(2)}) collective-permute-start(bf16[256,512]{1,0:T(8,128)(2,1)S(1)} %collective-permute-done.14.attended_ref), channel_id=1, source_target_pairs={{0,3},{1,0},{2,1},{3,2},{4,7},{5,4},{6,5},{7,6},{8,11},{9,8},{10,9... | collective-permute-start | bytes 786440 | tf_op jit(solution)/shard_map/ppermute | solution.py:295
  (8 other events, 7.7 us)
Sparse Core Ops, SparseCore 0:
  11.7 19.5 all-gather.5
  101.2 37.9 all-gather.7

commit v17 on v14

--- a/solution.py
+++ b/solution.py
@@ -77,8 +77,12 @@
     earlier_refs, refs = refs[: 2 * earlier], refs[2 * earlier :]
     out_ref, keys_ref, values_ref, acc_ref, shrink_ref = refs
     for number, piece_ref in enumerate(piece_refs):
-        size = piece_ref.shape[0]
-        shrink_ref[pl.ds(pl.multiple_of(ids_ref[number] * size, size), size), :] = piece_ref[...]
+        width = piece_ref.shape[1]
+        size = piece_ref.shape[0] * 2 // 3
+        start = pl.multiple_of(ids_ref[number] * size, size)
+        shrink_ref[pl.ds(start, size), :width] = piece_ref[:size, :]
+        shrink_ref[pl.ds(start, size // 2), width:] = piece_ref[size:, : width // 2]
+        shrink_ref[pl.ds(start + size // 2, size // 2), width:] = piece_ref[size:, width // 2 :]
     accumulate(acc_ref, token_ref, w_ref, begun_ref)
     slots, _, head_size = w_ref.shape
     rank = up_ref.shape[2]
@@ -153,7 +157,9 @@
         ),
         [
             pltpu.VMEM((rows, slots * head_size), jnp.float32),
-            pltpu.VMEM((planes * shrink[0].shape[0], shrink[0].shape[1]), jnp.bfloat16),
+            pltpu.VMEM(
+                (planes * shrink[0].shape[0] * 2 // 3, shrink[0].shape[1] * 3 // 2), jnp.bfloat16
+            ),
         ],
     )
 
@@ -179,9 +185,13 @@
     @pl.when(step == count - 1)
     def _():
         for turn, out_ref in enumerate(out_refs):
-            rows = out_ref.shape[0]
+            rows = out_ref.shape[0] * 2 // 3
             plane = lax.rem(ids_ref[count] + turn, planes)
-            out_ref[...] = acc_ref[pl.ds(pl.multiple_of(plane * rows, rows), rows), :]
+            piece = acc_ref[pl.ds(pl.multiple_of(plane * rows, rows), rows), :]
+            out_ref[:rows, :] = piece[:, : 2 * rank]
+            out_ref[rows:, :] = jnp.concatenate(
+                [piece[: rows // 2, 2 * rank :], piece[rows // 2 :, 2 * rank :]], axis=1
+            )
 
 
 def shrink_partial(adapters, here, planes, table, tokens, down):
@@ -194,7 +204,7 @@
         adapters.shape[0],
         [None, None, pl.BlockSpec((1, width, depth), lambda step, ids: (ids[step], 0, 0))],
         [table, tokens, down],
-        (jax.ShapeDtypeStruct((rows // planes, width), jnp.float32),) * planes,
+        (jax.ShapeDtypeStruct((rows // planes * 3 // 2, width * 2 // 3), jnp.float32),) * planes,
         [pltpu.VMEM((rows, width), jnp.float32)],
     )
 
@@ -345,9 +355,10 @@
 
     lines = [turned(send, k) for k, send in enumerate(sends, 1)]
     begun = project(planes_of[:1], tokens, shard(0))
-    done = (held[1], lines, begun, table, turn, up_all, own_rows, shard(1))
+    sums = shrink_partial(adapters, here, planes, table, tokens, down_all)
+    done = (held[1], lines, begun, table, turn, up_all, own_rows, shard(1), sums)
     done = lax.optimization_barrier(done)
-    held[1], lines, begun, table, turn, up_all, own_rows, part_weight = done
+    held[1], lines, begun, table, turn, up_all, own_rows, part_weight, sums = done
     lines = lax.all_gather(jnp.stack(lines), PLANE, axis=0)
     for step in range(2, planes):
         arrived = held[-1]
@@ -355,7 +366,6 @@
         begun = project(planes_of[step - 1 : step], arrived, part_weight, [begun])
         side = ()
         if step == 2:
-            sums = shrink_partial(adapters, here, planes, table, after(tokens, arrived), down_all)
             sums = [sums[0]] + [turned(sums[k], k) for k in range(1, planes)]
             side = (
                 sums,

time: 180 us -> 181 us (level)
  starting transfers between devices: 28.9 us -> 21.2 us
  local copies, waits for them, and re-layouts: 22.3 us -> 29.5 us
    ppermute x18, starting transfers between devices: 28.8 us -> 21.2 us  [turned(): lax.ppermute(value, 'tensor', [(i, (i + turn) % planes) for i in range(pl...]
    unnamed x34 -> x58, local copies, waits for them, and re-layouts: 5.62 us -> 12.9 us
where the time goes in v17:
time: 181 us; the launch traced here: 180 us
  waiting for transfers between devices  54.8 us (30%)
  local copies, waits for them, and re-layouts  29.5 us (16%)
  Pallas kernels  29.1 us (16%)
  blocking collectives  21.7 us (12%)
  starting transfers between devices  21.2 us (12%)
  between operations  16.5 us (9%)
  other arithmetic  7.09 us (4%)
    ppermute x18, waiting for transfers between devices, turned(): lax.ppermute(value, 'tensor', [(i, (i + turn) % planes) for i in range(pl...  54.7 us
    pallas_call x14, Pallas kernels, call(): pl.pallas_call(kernel, out_shape=out, grid_spec=pltpu.PrefetchScalarGridS...  29.1 us
    ppermute x18, starting transfers between devices, turned(): lax.ppermute(value, 'tensor', [(i, (i + turn) % planes) for i in range(pl...  21.2 us
    unnamed x58, local copies, waits for them, and re-layouts  12.9 us
    all_gather x1, blocking collectives, local(): lax.all_gather(after(output_up_maps, sums[0]), 'dp', axis=0, tiled=True)  8.55 us
    all_gather x1, blocking collectives, local(): lax.all_gather(jnp.transpose(adapter_up_maps[0], (1, 0, 2)), 'dp', axis=0)  6.89 us
    all_gather x1, blocking collectives, local(): lax.all_gather(after(out_down, sums[0]), 'dp', axis=0)  6.3 us
    dynamic_slice x1, local copies, waits for them, and re-layouts, shard(): return lax.dynamic_slice_in_dim(weight, start, depth, axis=1)  5.13 us
  transfers between devices with their start and end apart: 20, of which 10 were waited for; matrix products, arithmetic and copies ran while one was open for 12% of the time, Pallas kernels for 13%

profile of v17, /device:TPU:0, one launch (start us, length us, event | category | flops | bytes accessed | tf_op | source)
XLA Modules:
  0.0 180.0 jit_solution(10303163167750125222)
XLA Ops:
  6.5 3.0 %collective-permute-start = (bf16[512,1024]{1,0:T(8,128)(2,1)}, bf16[512,1024]{1,0:T(8,128)(2,1)}, u32[]{:S(2)}, u32[]{:S(2)}) collective-permute-start(bf16[512,1024]{1,0:T(8,128)(2,1)} %token_ref.3), channel_id=1, source_target_pairs={{0,1},{1,2},{2,3},{3,0},{4,5},{5,6},{6,7},{7,4},{8,9},{9,10},{10,1... | collective-permute-start | bytes 3145736 | tf_op jit(solution)/shard_map/ppermute | solution.py:305
  10.6 2.8 %fusion.4 = (bf16[64,1,1024]{2,1,0:T(2,128)(2,1)S(1)}, bf16[64,1,1024]{2,1,0:T(2,128)(2,1)S(1)}, bf16[64,1,1024]{2,1,0:T(2,128)(2,1)S(1)}) fusion(bf16[128,4,4096]{2,1,0:T(4,128)(2,1)} %param.11, s32[]{:T(128)S(6)} %select_n.76, s32[]{:T(128)S(6)} %select_n.79, s32[]{:T(128)S(6)} %select_n.88, s32[]{:T(128)S(6)} %select_n.85, s32[]{:T(128)S(6)} %select_n.82), kind=kLoop, calls=%fused_computation.39 | loop fusion | bytes 786452 | tf_op jit(solution)/shard_map/dynamic_slice | solution.py:345
  14.5 1.6 collective-permute-start.1
  16.0 1.7 collective-permute-start.2
  17.8 2.2 %collective-permute-start.3 = (bf16[96,1024]{1,0:T(8,128)(2,1)}, bf16[96,1024]{1,0:T(8,128)(2,1)}, u32[]{:S(2)}, u32[]{:S(2)}) collective-permute-start(bf16[96,1024]{1,0:T(8,128)(2,1)} %get-tuple-element.135), channel_id=1, source_target_pairs={{0,3},{1,0},{2,1},{3,2},{4,7},{5,4},{6,5},{7,6},{8,11},{9,8},{10,9... | collective-permute-start | bytes 589832 | tf_op jit(solution)/shard_map/ppermute | solution.py:305
  25.7 2.6 %dynamic-slice_bitcast_fusion.4 = bf16[4,128,1024]{2,0,1:T(4,128)(2,1)} fusion(bf16[128,4,4096]{2,1,0:T(4,128)(2,1)} %param.11, s32[]{:T(128)S(6)} %select_n.91), kind=kLoop, calls=%fused_computation.7 | loop fusion | bytes 2097156 | tf_op jit(solution)/shard_map/transpose | solution.py:330
  28.3 5.1 %dynamic-slice_bitcast_fusion = (bf16[6,1024,128]{2,1,0:T(8,128)(2,1)S(1)}, bf16[6,1024,128]{2,1,0:T(8,128)(2,1)}, bf16[6,1024,128]{2,1,0:T(8,128)(2,1)}, bf16[6,1024,128]{2,1,0:T(8,128)(2,1)}) fusion(bf16[4096,6,128]{2,0,1:T(8,128)(2,1)} %param.10, s32[]{:T(128)S(6)} %select_n.94, s32[]{:T(128)S(6)} %select_n.92, s32[]{:T(128)S(6)} %select_n.89, s32[]{:T(128)S(6)} %select_n.93), kind=kLoop, calls=%fused_computation.3 | loop fusion | bytes 12582928 | tf_op jit(solution)/shard_map/dynamic_slice | solution.py:354
  36.3 1.8 project.3.refs_0_
  39.4 6.9 %all-gather = bf16[24,64,128]{2,1,0:T(8,128)(2,1)} all-gather(bf16[6,64,128]{2,1,0:T(8,128)(2,1)S(1)} %bitcast.69), channel_id=2, replica_groups=mesh['groups'=2,'dp'=4,'tensor'=4] {'dp'}, dimensions={0}, use_global_device_ids=true | all-gather | bytes 491520 | tf_op jit(solution)/shard_map/all_gather | solution.py:310
  48.9 2.7 %shrink.1 = (f32[192,128]{1,0:T(8,128)S(1)}, f32[192,128]{1,0:T(8,128)S(1)}, f32[192,128]{1,0:T(8,128)S(1)}, f32[192,128]{1,0:T(8,128)S(1)}) custom-call(s32[5]{0:T(128)S(1)} %pad_add_fusion.3.ids_ref, s32[512,2]{1,0:T(8,128)S(1)} %copy.42.table_ref, bf16[512,1024]{1,0:T(8,128)(2,1)S(1)} %copy-done.9, bf16[4,192,1024]{2,1,0:T(8,128)(2,1)S(1)} %copy-done.12), custom_call_target="tpu_custom_call" | custom-call | bytes 7876608 | tf_op jit(solution)/shard_map/shrink/pallas_call | solution.py:26
  53.6 2.1 %pad_maximum_fusion = bf16[3,96,1024]{2,1,0:T(8,128)(2,1)} fusion(bf16[1,96,1024]{2,1,0:T(8,128)(2,1)} %bitcast.26, bf16[1,96,1024]{2,1,0:T(8,128)(2,1)} %bitcast.25, bf16[1,96,1024]{2,1,0:T(8,128)(2,1)} %bitcast.24), kind=kLoop, calls=%fused_computation.8 | loop fusion | flops 589824 | bytes 1179648 | tf_op jit(solution)/shard_map/stack | solution.py:362
  56.7 3.5 %collective-permute-start.6 = (f32[192,128]{1,0:T(8,128)S(1)}, f32[192,128]{1,0:T(8,128)}, u32[]{:S(2)}, u32[]{:S(2)}) collective-permute-start(f32[192,128]{1,0:T(8,128)S(1)} %copy-done.17), channel_id=1, source_target_pairs={{0,2},{1,3},{2,0},{3,1},{4,6},{5,7},{6,4},{7,5},{8,10},{9,11},{10,... | collective-permute-start | bytes 294920 | tf_op jit(solution)/shard_map/ppermute | solution.py:305
  61.7 2.9 %project.4.refs_0_ = f32[512,768]{1,0:T(8,128)S(1)} custom-call(s32[1]{0:T(128)} %get-tuple-element.145.ids_ref, bf16[512,1024]{1,0:T(8,128)(2,1)} %collective-permute-done.token_ref, bf16[6,1024,128]{2,1,0:T(8,128)(2,1)S(1)} %copy-done.5, f32[512,768]{1,0:T(8,128)S(1)} %project.3.refs_0_), custom_call_target="tpu_custom_call" | custom-call | bytes 12582912 | tf_op jit(solution)/shard_map/project/pallas_call | solution.py:26
  65.9 8.6 %all_gather.27.refs_3_ = bf16[4,64,1024]{2,1,0:T(8,128)(2,1)} all-gather(bf16[1,64,1024]{2,1,0:T(8,128)(2,1)S(1)} %copy-done.23), channel_id=1, replica_groups=mesh['groups'=2,'dp'=4,'tensor'=4] {'dp'}, dimensions={0}, use_global_device_ids=true | all-gather | bytes 655360 | tf_op jit(solution)/shard_map/all_gather | solution.py:372
  74.4 6.3 %all-gather.1 = bf16[128,1024]{1,0:T(8,128)(2,1)} all-gather(bf16[32,1024]{1,0:T(8,128)(2,1)S(1)} %copy-done.22), channel_id=3, replica_groups=mesh['groups'=2,'dp'=4,'tensor'=4] {'dp'}, dimensions={0}, use_global_device_ids=true | all-gather | bytes 327680 | tf_op jit(solution)/shard_map/all_gather | solution.py:373
  80.7 5.3 %collective-permute-done.5 = f32[192,128]{1,0:T(8,128)} collective-permute-done((f32[192,128]{1,0:T(8,128)S(1)}, f32[192,128]{1,0:T(8,128)}, u32[]{:S(2)}, u32[]{:S(2)}) %collective-permute-start.5) | collective-permute-done | bytes 98336 | tf_op jit(solution)/shard_map/ppermute | solution.py:305
  86.1 3.6 %collective-permute-done.6 = f32[192,128]{1,0:T(8,128)} collective-permute-done((f32[192,128]{1,0:T(8,128)S(1)}, f32[192,128]{1,0:T(8,128)}, u32[]{:S(2)}, u32[]{:S(2)}) %collective-permute-start.6) | collective-permute-done | bytes 98336 | tf_op jit(solution)/shard_map/ppermute | solution.py:305
  89.7 2.5 %collective-permute-start.8 = (bf16[512,1024]{1,0:T(8,128)(2,1)}, bf16[512,1024]{1,0:T(8,128)(2,1)}, u32[]{:S(2)}, u32[]{:S(2)}) collective-permute-start(bf16[512,1024]{1,0:T(8,128)(2,1)} %collective-permute-done.4.token_ref), channel_id=1, source_target_pairs={{0,1},{1,2},{2,3},{3,0},{4,5},{5,6},{6,7},{7,4},{8,9},{9,10},{10,1... | collective-permute-start | bytes 3145736 | tf_op jit(solution)/shard_map/ppermute | solution.py:305
  95.9 1.9 %collective-permute-start.11 = (bf16[192,128]{1,0:T(8,128)(2,1)S(1)}, bf16[192,128]{1,0:T(8,128)(2,1)}, u32[]{:S(2)}, u32[]{:S(2)}) collective-permute-start(bf16[192,128]{1,0:T(8,128)(2,1)S(1)} %add_convert_fusion.refs_0_), channel_id=1, source_target_pairs={{0,3},{1,0},{2,1},{3,2},{4,7},{5,4},{6,5},{7,6},{8,11},{9,8},{10,9... | collective-permute-start | bytes 147464 | tf_op jit(solution)/shard_map/ppermute | solution.py:305
  100.6 2.8 %project.5.refs_6_ = f32[512,768]{1,0:T(8,128)S(1)} custom-call(s32[1]{0:T(128)} %get-tuple-element.144.ids_ref, bf16[512,1024]{1,0:T(8,128)(2,1)} %collective-permute-done.4.token_ref, bf16[6,1024,128]{2,1,0:T(8,128)(2,1)S(1)} %copy-done.4, f32[512,768]{1,0:T(8,128)S(1)} %copy-done.2), custom_call_target="tpu_custom_call" | custom-call | bytes 12582912 | tf_op jit(solution)/shard_map/project/pallas_call | solution.py:26
  103.5 2.9 %slice_bitcast_fusion = (bf16[8,96,1024]{2,1,0:T(8,128)(2,1)S(1)}, bf16[8,96,1024]{2,1,0:T(8,128)(2,1)S(1)}, bf16[8,96,1024]{2,1,0:T(8,128)(2,1)S(1)}) fusion(bf16[8,3,96,1024]{3,2,1,0:T(8,128)(2,1)} %bitcast.65), kind=kLoop, calls=%fused_computation | loop fusion | bytes 9437184 | tf_op jit(solution)/shard_map/squeeze | solution.py:378
  106.4 12.6 %collective-permute-done.9.refs_1_ = bf16[192,128]{1,0:T(8,128)(2,1)S(1)} collective-permute-done((bf16[192,128]{1,0:T(8,128)(2,1)S(1)}, bf16[192,128]{1,0:T(8,128)(2,1)S(1)}, u32[]{:S(2)}, u32[]{:S(2)}) %collective-permute-start.9) | collective-permute-done | bytes 49184 | tf_op jit(solution)/shard_map/ppermute | solution.py:305
  120.1 4.2 %attend.2 = (bf16[256,512]{1,0:T(8,128)(2,1)S(1)}, bf16[256,128]{1,0:T(8,128)(2,1)S(1)}, bf16[256,128]{1,0:T(8,128)(2,1)S(1)}) custom-call(s32[8]{0:T(128)S(1)} %copy-done.13, s32[512,2]{1,0:T(8,128)S(1)} %copy.47.table_ref.refs_2_, f32[512,256]{1,0:T(8,128)S(1)} %copy-done.7, bf16[4,6,64,128]{3,2,1,0:T(8,128)(2,1)S(1)} %bitcast.61, ...), custom_call_target="tpu_custom_call" | custom-call | bytes 15937536 | tf_op jit(solution)/shard_map/attend/pallas_call | solution.py:26
  124.3 1.7 collective-permute-start.12
  126.0 4.9 %attend.3 = (bf16[256,512]{1,0:T(8,128)(2,1)S(1)}, bf16[256,128]{1,0:T(8,128)(2,1)}, bf16[256,128]{1,0:T(8,128)(2,1)}) custom-call(s32[8]{0:T(128)S(1)} %copy-done.13, s32[512,2]{1,0:T(8,128)S(1)} %copy.47.table_ref.refs_2_, f32[512,256]{1,0:T(8,128)S(1)} %copy-done.7, bf16[4,6,64,128]{3,2,1,0:T(8,128)(2,1)S(1)} %bitcast.62, ...), custom_call_target="tpu_custom_call" | custom-call | bytes 16330752 | tf_op jit(solution)/shard_map/attend/pallas_call | solution.py:26
  132.0 2.3 %collective-permute-done.12.attended_ref = bf16[256,512]{1,0:T(8,128)(2,1)S(1)} collective-permute-done((bf16[256,512]{1,0:T(8,128)(2,1)S(1)}, bf16[256,512]{1,0:T(8,128)(2,1)S(1)}, u32[]{:S(2)}, u32[]{:S(2)}) %collective-permute-start.12) | collective-permute-done | bytes 262176 | tf_op jit(solution)/shard_map/ppermute | solution.py:305
  136.6 8.7 %collective-permute-done.13.attended_ref = bf16[256,512]{1,0:T(8,128)(2,1)S(1)} collective-permute-done((bf16[256,512]{1,0:T(8,128)(2,1)S(1)}, bf16[256,512]{1,0:T(8,128)(2,1)S(1)}, u32[]{:S(2)}, u32[]{:S(2)}) %collective-permute-start.13) | collective-permute-done | bytes 262176 | tf_op jit(solution)/shard_map/ppermute | solution.py:305
  145.3 3.7 %collective-permute-done.14.attended_ref = bf16[256,512]{1,0:T(8,128)(2,1)S(1)} collective-permute-done((bf16[256,512]{1,0:T(8,128)(2,1)S(1)}, bf16[256,512]{1,0:T(8,128)(2,1)S(1)}, u32[]{:S(2)}, u32[]{:S(2)}) %collective-permute-start.14) | collective-permute-done | bytes 262176 | tf_op jit(solution)/shard_map/ppermute | solution.py:305
  150.0 9.9 %collective-permute-done.15.attended_ref = bf16[256,512]{1,0:T(8,128)(2,1)S(1)} collective-permute-done((bf16[256,512]{1,0:T(8,128)(2,1)S(1)}, bf16[256,512]{1,0:T(8,128)(2,1)S(1)}, u32[]{:S(2)}, u32[]{:S(2)}) %collective-permute-start.15) | collective-permute-done | bytes 262176 | tf_op jit(solution)/shard_map/ppermute | solution.py:305
  159.9 2.8 %collective-permute-done.16.attended_ref = bf16[256,512]{1,0:T(8,128)(2,1)S(1)} collective-permute-done((bf16[256,512]{1,0:T(8,128)(2,1)S(1)}, bf16[256,512]{1,0:T(8,128)(2,1)S(1)}, u32[]{:S(2)}, u32[]{:S(2)}) %collective-permute-start.16) | collective-permute-done | bytes 262176 | tf_op jit(solution)/shard_map/ppermute | solution.py:305
  166.2 4.7 %collective-permute-done.17.attended_ref = bf16[256,512]{1,0:T(8,128)(2,1)S(1)} collective-permute-done((bf16[256,512]{1,0:T(8,128)(2,1)S(1)}, bf16[256,512]{1,0:T(8,128)(2,1)S(1)}, u32[]{:S(2)}, u32[]{:S(2)}) %collective-permute-start.17) | collective-permute-done | bytes 262176 | tf_op jit(solution)/shard_map/ppermute | solution.py:305
  170.9 2.2 %project_out.15 = bf16[512,1024]{1,0:T(8,128)(2,1)} custom-call(s32[5]{0:T(128)S(1)} %pad_add_fusion.1.ids_ref, bf16[256,512]{1,0:T(8,128)(2,1)S(1)} %collective-permute-done.17.attended_ref, bf16[8,96,1024]{2,1,0:T(8,128)(2,1)S(1)} %get-tuple-element.118.w_ref.down_ref, bf16[8,96,1024]{2,1,0:T(8,128)(2,1)S(1)} %get-tuple-element.118.w_ref.down_ref, ...), custom_call_target="tpu_custom_call" | custom-call | bytes 17313792 | tf_op jit(solution)/shard_map/project_out/pallas_call | solution.py:26
  (115 shorter events, 33.1 us)
Async XLA Ops:
  6.5 39.7 %all-gather.6.cloned.1.call-start = ((), (), s32[]{:S(2)}) async-start(), calls=%async_computation | async-start | bytes 1966080 | tf_op jit(solution)/shard_map/all_gather | solution.py:309
  6.5 47.0 %collective-permute-start = (bf16[512,1024]{1,0:T(8,128)(2,1)}, bf16[512,1024]{1,0:T(8,128)(2,1)}, u32[]{:S(2)}, u32[]{:S(2)}) collective-permute-start(bf16[512,1024]{1,0:T(8,128)(2,1)} %token_ref.3), channel_id=1, source_target_pairs={{0,1},{1,2},{2,3},{3,0},{4,5},{5,6},{6,7},{7,4},{8,9},{9,10},{10,1... | collective-permute-start | bytes 3145736 | tf_op jit(solution)/shard_map/ppermute | solution.py:305
  9.6 93.9 %all-gather.8.cloned.1.call-start = ((), (), s32[]{:S(2)}) async-start(), calls=%async_computation.1 | async-start | bytes 5308416 | tf_op jit(solution)/shard_map/all_gather | solution.py:362
  10.6 9.4 %copy-start.26 = (s32[1,4]{1,0:T(1,128)S(1)}, s32[1,4]{1,0:T(1,128)}, u32[]{:S(2)}) copy-start(s32[1,4]{1,0:T(1,128)} %param.17) | copy-start | bytes 52
  10.6 9.6 %copy-start.27 = (s32[1,4]{1,0:T(1,128)S(1)}, s32[1,4]{1,0:T(1,128)}, u32[]{:S(2)}) copy-start(s32[1,4]{1,0:T(1,128)} %param.16) | copy-start | bytes 52
  13.5 12.2 %copy-start.21 = (bf16[32,1024]{1,0:T(8,128)(2,1)}, bf16[32,1024]{1,0:T(8,128)(2,1)S(1)}, u32[]{:S(2)}) copy-start(bf16[32,1024]{1,0:T(8,128)(2,1)S(1)} %bitcast_dynamic-update-slice_fusion) | copy-start | bytes 196612
  14.5 39.1 %collective-permute-start.1 = (bf16[96,1024]{1,0:T(8,128)(2,1)}, bf16[96,1024]{1,0:T(8,128)(2,1)}, u32[]{:S(2)}, u32[]{:S(2)}) collective-permute-start(bf16[96,1024]{1,0:T(8,128)(2,1)} %get-tuple-element.137), channel_id=1, source_target_pairs={{0,1},{1,2},{2,3},{3,0},{4,5},{5,6},{6,7},{7,4},{8,9},{9,10},{10,1... | collective-permute-start | bytes 589832 | tf_op jit(solution)/shard_map/ppermute | solution.py:305
  16.0 37.5 %collective-permute-start.2 = (bf16[96,1024]{1,0:T(8,128)(2,1)}, bf16[96,1024]{1,0:T(8,128)(2,1)}, u32[]{:S(2)}, u32[]{:S(2)}) collective-permute-start(bf16[96,1024]{1,0:T(8,128)(2,1)} %get-tuple-element.136), channel_id=1, source_target_pairs={{0,2},{1,3},{2,0},{3,1},{4,6},{5,7},{6,4},{7,5},{8,10},{9,11},{10,... | collective-permute-start | bytes 589832 | tf_op jit(solution)/shard_map/ppermute | solution.py:305
  17.8 35.8 %collective-permute-start.3 = (bf16[96,1024]{1,0:T(8,128)(2,1)}, bf16[96,1024]{1,0:T(8,128)(2,1)}, u32[]{:S(2)}, u32[]{:S(2)}) collective-permute-start(bf16[96,1024]{1,0:T(8,128)(2,1)} %get-tuple-element.135), channel_id=1, source_target_pairs={{0,3},{1,0},{2,1},{3,2},{4,7},{5,4},{6,5},{7,6},{8,11},{9,8},{10,9... | collective-permute-start | bytes 589832 | tf_op jit(solution)/shard_map/ppermute | solution.py:305
  53.6 3.1 %copy-start.17 = (f32[192,128]{1,0:T(8,128)S(1)}, f32[192,128]{1,0:T(8,128)}, u32[]{:S(2)}) copy-start(f32[192,128]{1,0:T(8,128)} %copy-done.16) | copy-start | bytes 294916
  53.6 6.6 %copy-start.15 = (f32[192,128]{1,0:T(8,128)S(1)}, f32[192,128]{1,0:T(8,128)}, u32[]{:S(2)}) copy-start(f32[192,128]{1,0:T(8,128)} %copy-done.14) | copy-start | bytes 294916
  55.7 34.0 %collective-permute-start.4 = (bf16[512,1024]{1,0:T(8,128)(2,1)}, bf16[512,1024]{1,0:T(8,128)(2,1)}, u32[]{:S(2)}, u32[]{:S(2)}) collective-permute-start(bf16[512,1024]{1,0:T(8,128)(2,1)} %collective-permute-done.token_ref), channel_id=1, source_target_pairs={{0,1},{1,2},{2,3},{3,0},{4,5},{5,6},{6,7},{7,4},{8,9},{9,10},{10,1... | collective-permute-start | bytes 3145736 | tf_op jit(solution)/shard_map/ppermute | solution.py:305
  55.8 30.3 %collective-permute-start.5 = (f32[192,128]{1,0:T(8,128)S(1)}, f32[192,128]{1,0:T(8,128)}, u32[]{:S(2)}, u32[]{:S(2)}) collective-permute-start(f32[192,128]{1,0:T(8,128)S(1)} %copy-done.19), channel_id=1, source_target_pairs={{0,1},{1,2},{2,3},{3,0},{4,5},{5,6},{6,7},{7,4},{8,9},{9,10},{10,1... | collective-permute-start | bytes 294920 | tf_op jit(solution)/shard_map/ppermute | solution.py:305
  56.7 33.1 %collective-permute-start.6 = (f32[192,128]{1,0:T(8,128)S(1)}, f32[192,128]{1,0:T(8,128)}, u32[]{:S(2)}, u32[]{:S(2)}) collective-permute-start(f32[192,128]{1,0:T(8,128)S(1)} %copy-done.17), channel_id=1, source_target_pairs={{0,2},{1,3},{2,0},{3,1},{4,6},{5,7},{6,4},{7,5},{8,10},{9,11},{10,... | collective-permute-start | bytes 294920 | tf_op jit(solution)/shard_map/ppermute | solution.py:305
  60.1 29.6 %collective-permute-start.7 = (f32[192,128]{1,0:T(8,128)S(1)}, f32[192,128]{1,0:T(8,128)S(1)}, u32[]{:S(2)}, u32[]{:S(2)}) collective-permute-start(f32[192,128]{1,0:T(8,128)S(1)} %copy-done.15), channel_id=1, source_target_pairs={{0,3},{1,0},{2,1},{3,2},{4,7},{5,4},{6,5},{7,6},{8,11},{9,8},{10,9... | collective-permute-start | bytes 294920 | tf_op jit(solution)/shard_map/ppermute | solution.py:305
  61.7 4.2 %copy-start.23 = (bf16[1,64,1024]{2,1,0:T(8,128)(2,1)S(1)}, bf16[1,64,1024]{2,1,0:T(8,128)(2,1)}, u32[]{:S(2)}) copy-start(bf16[1,64,1024]{2,1,0:T(8,128)(2,1)} %param.15) | copy-start | bytes 393220
  61.7 12.7 %copy-start.22 = (bf16[32,1024]{1,0:T(8,128)(2,1)S(1)}, bf16[32,1024]{1,0:T(8,128)(2,1)}, u32[]{:S(2)}) copy-start(bf16[32,1024]{1,0:T(8,128)(2,1)} %copy-done.21) | copy-start | bytes 196612
  89.7 30.4 %collective-permute-start.8 = (bf16[512,1024]{1,0:T(8,128)(2,1)}, bf16[512,1024]{1,0:T(8,128)(2,1)}, u32[]{:S(2)}, u32[]{:S(2)}) collective-permute-start(bf16[512,1024]{1,0:T(8,128)(2,1)} %collective-permute-done.4.token_ref), channel_id=1, source_target_pairs={{0,1},{1,2},{2,3},{3,0},{4,5},{5,6},{6,7},{7,4},{8,9},{9,10},{10,1... | collective-permute-start | bytes 3145736 | tf_op jit(solution)/shard_map/ppermute | solution.py:305
  93.9 25.1 %collective-permute-start.9 = (bf16[192,128]{1,0:T(8,128)(2,1)S(1)}, bf16[192,128]{1,0:T(8,128)(2,1)S(1)}, u32[]{:S(2)}, u32[]{:S(2)}) collective-permute-start(bf16[192,128]{1,0:T(8,128)(2,1)S(1)} %add_convert_fusion.refs_0_), channel_id=1, source_target_pairs={{0,1},{1,2},{2,3},{3,0},{4,5},{5,6},{6,7},{7,4},{8,9},{9,10},{10,1... | collective-permute-start | bytes 147464 | tf_op jit(solution)/shard_map/ppermute | solution.py:305
  94.6 25.5 %collective-permute-start.10 = (bf16[192,128]{1,0:T(8,128)(2,1)S(1)}, bf16[192,128]{1,0:T(8,128)(2,1)S(1)}, u32[]{:S(2)}, u32[]{:S(2)}) collective-permute-start(bf16[192,128]{1,0:T(8,128)(2,1)S(1)} %add_convert_fusion.refs_0_), channel_id=1, source_target_pairs={{0,2},{1,3},{2,0},{3,1},{4,6},{5,7},{6,4},{7,5},{8,10},{9,11},{10,... | collective-permute-start | bytes 147464 | tf_op jit(solution)/shard_map/ppermute | solution.py:305
  95.9 24.1 %collective-permute-start.11 = (bf16[192,128]{1,0:T(8,128)(2,1)S(1)}, bf16[192,128]{1,0:T(8,128)(2,1)}, u32[]{:S(2)}, u32[]{:S(2)}) collective-permute-start(bf16[192,128]{1,0:T(8,128)(2,1)S(1)} %add_convert_fusion.refs_0_), channel_id=1, source_target_pairs={{0,3},{1,0},{2,1},{3,2},{4,7},{5,4},{6,5},{7,6},{8,11},{9,8},{10,9... | collective-permute-start | bytes 147464 | tf_op jit(solution)/shard_map/ppermute | solution.py:305
  103.5 16.6 %copy-start.7 = (f32[512,256]{1,0:T(8,128)S(1)}, f32[512,256]{1,0:T(8,128)}, u32[]{:S(2)}) copy-start(f32[512,256]{1,0:T(8,128)} %pad_maximum_fusion.1.turn_ref) | copy-start | bytes 1572868
  103.5 16.6 %copy-start.10 = (bf16[24,64,128]{2,1,0:T(8,128)(2,1)S(1)}, bf16[24,64,128]{2,1,0:T(8,128)(2,1)}, u32[]{:S(2)}) copy-start(bf16[24,64,128]{2,1,0:T(8,128)(2,1)} %all-gather) | copy-start | bytes 1179652
  103.5 16.6 %copy-start.13 = (s32[8]{0:T(128)S(1)}, s32[8]{0:T(128)}, u32[]{:S(2)}) copy-start(s32[8]{0:T(128)} %pad_add_fusion.2.ids_ref) | copy-start | bytes 100
  124.3 10.0 %collective-permute-start.12 = (bf16[256,512]{1,0:T(8,128)(2,1)S(1)}, bf16[256,512]{1,0:T(8,128)(2,1)S(1)}, u32[]{:S(2)}, u32[]{:S(2)}) collective-permute-start(bf16[256,512]{1,0:T(8,128)(2,1)S(1)} %get-tuple-element.101.attended_ref), channel_id=1, source_target_pairs={{0,1},{1,2},{2,3},{3,0},{4,5},{5,6},{6,7},{7,4},{8,9},{9,10},{10,1... | collective-permute-start | bytes 786440 | tf_op jit(solution)/shard_map/ppermute | solution.py:305
  126.0 4.9 %copy-start = (bf16[4,128,1024]{2,1,0:T(8,128)(2,1)S(1)}, bf16[4,128,1024]{2,1,0:T(8,128)(2,1)}, u32[]{:S(2)}) copy-start(bf16[4,128,1024]{2,1,0:T(8,128)(2,1)} %copy.41) | copy-start | bytes 3145732
  126.0 4.9 %copy-start.11 = (bf16[128,1024]{1,0:T(8,128)(2,1)S(1)}, bf16[128,1024]{1,0:T(8,128)(2,1)}, u32[]{:S(2)}) copy-start(bf16[128,1024]{1,0:T(8,128)(2,1)} %all-gather.1) | copy-start | bytes 786436
  134.3 11.0 %collective-permute-start.13 = (bf16[256,512]{1,0:T(8,128)(2,1)S(1)}, bf16[256,512]{1,0:T(8,128)(2,1)S(1)}, u32[]{:S(2)}, u32[]{:S(2)}) collective-permute-start(bf16[256,512]{1,0:T(8,128)(2,1)S(1)} %get-tuple-element.102.attended_ref), channel_id=1, source_target_pairs={{0,1},{1,2},{2,3},{3,0},{4,5},{5,6},{6,7},{7,4},{8,9},{9,10},{10,1... | collective-permute-start | bytes 786440 | tf_op jit(solution)/shard_map/ppermute | solution.py:305
  134.3 14.7 %collective-permute-start.14 = (bf16[256,512]{1,0:T(8,128)(2,1)S(1)}, bf16[256,512]{1,0:T(8,128)(2,1)S(1)}, u32[]{:S(2)}, u32[]{:S(2)}) collective-permute-start(bf16[256,512]{1,0:T(8,128)(2,1)S(1)} %collective-permute-done.12.attended_ref), channel_id=1, source_target_pairs={{0,1},{1,2},{2,3},{3,0},{4,5},{5,6},{6,7},{7,4},{8,9},{9,10},{10,1... | collective-permute-start | bytes 786440 | tf_op jit(solution)/shard_map/ppermute | solution.py:305
  149.0 11.0 %collective-permute-start.15 = (bf16[256,512]{1,0:T(8,128)(2,1)S(1)}, bf16[256,512]{1,0:T(8,128)(2,1)S(1)}, u32[]{:S(2)}, u32[]{:S(2)}) collective-permute-start(bf16[256,512]{1,0:T(8,128)(2,1)S(1)} %collective-permute-done.13.attended_ref), channel_id=1, source_target_pairs={{0,1},{1,2},{2,3},{3,0},{4,5},{5,6},{6,7},{7,4},{8,9},{9,10},{10,1... | collective-permute-start | bytes 786440 | tf_op jit(solution)/shard_map/ppermute | solution.py:305
  149.0 13.8 %collective-permute-start.16 = (bf16[256,512]{1,0:T(8,128)(2,1)S(1)}, bf16[256,512]{1,0:T(8,128)(2,1)S(1)}, u32[]{:S(2)}, u32[]{:S(2)}) collective-permute-start(bf16[256,512]{1,0:T(8,128)(2,1)S(1)} %collective-permute-done.14.attended_ref), channel_id=1, source_target_pairs={{0,1},{1,2},{2,3},{3,0},{4,5},{5,6},{6,7},{7,4},{8,9},{9,10},{10,1... | collective-permute-start | bytes 786440 | tf_op jit(solution)/shard_map/ppermute | solution.py:305
  162.7 8.2 %collective-permute-start.17 = (bf16[256,512]{1,0:T(8,128)(2,1)S(1)}, bf16[256,512]{1,0:T(8,128)(2,1)S(1)}, u32[]{:S(2)}, u32[]{:S(2)}) collective-permute-start(bf16[256,512]{1,0:T(8,128)(2,1)S(1)} %collective-permute-done.15.attended_ref), channel_id=1, source_target_pairs={{0,1},{1,2},{2,3},{3,0},{4,5},{5,6},{6,7},{7,4},{8,9},{9,10},{10,1... | collective-permute-start | bytes 786440 | tf_op jit(solution)/shard_map/ppermute | solution.py:305
  (16 other events, 21.6 us)
Sparse Core Ops, SparseCore 0:
  9.7 21.5 all-gather.5
  55.8 39.2 all-gather.7

commit v18 on v17

--- a/solution.py
+++ b/solution.py
@@ -48,8 +48,14 @@
         acc_ref[:, columns] = total if first is None else first[:, columns] + total
 
 
-def project_kernel(begun, ids_ref, token_ref, w_ref, *refs):
-    accumulate(refs[-1], token_ref, w_ref, refs[0] if begun else None)
+def project_kernel(parts, begun, ids_ref, *refs):
+    w_ref, acc_ref = refs[parts], refs[-1]
+    row = 0
+    for token_ref in refs[:parts]:
+        rows = pl.ds(row, token_ref.shape[0])
+        first = refs[parts + 1].at[rows] if begun else None
+        accumulate(acc_ref.at[rows], token_ref, w_ref, first)
+        row += token_ref.shape[0]
 
 
 def rows_spec(array, rows, part):
@@ -58,16 +64,17 @@
     return pl.BlockSpec((rows, array.shape[1]), lambda step, ids: (part, 0))
 
 
-def project(ids, tokens, weight, begun=()):
+def project(tokens, weight, begun=()):
     slots, _, head_size = weight.shape
+    rows = sum(part.shape[0] for part in tokens)
     return call(
-        functools.partial(project_kernel, len(begun)),
+        functools.partial(project_kernel, len(tokens), len(begun)),
         "project",
-        ids,
+        jnp.zeros(1),
         1,
-        [None] * (2 + len(begun)),
-        [tokens, weight, *begun],
-        jax.ShapeDtypeStruct((tokens.shape[0], slots * head_size), jnp.float32),
+        [None] * (len(tokens) + 1 + len(begun)),
+        [*tokens, weight, *begun],
+        jax.ShapeDtypeStruct((rows, slots * head_size), jnp.float32),
     )
 
 
@@ -136,7 +143,7 @@
 
 
 def attend(planes_of, adapters, part, table, turn, up, shrink, tokens, weight, begun, earlier):
-    rows = tokens.shape[0] // 2
+    rows = tokens.shape[0]
     slots, _, head_size = weight.shape
     planes = len(shrink)
     arrays = [table, turn, up, *shrink, tokens, weight, begun, *earlier]
@@ -304,7 +311,6 @@
     def turned(value, turn=1):
         return lax.ppermute(value, "tensor", [(i, (i + turn) % planes) for i in range(planes)])
 
-    held = [tokens, turned(tokens)]
     weight = jnp.transpose(query_key_value_weight, (1, 0, 2))
     down_all = lax.all_gather(adapter_down_maps, "dp", axis=0, tiled=True)
     up_all = lax.all_gather(jnp.transpose(adapter_up_maps[0], (1, 0, 2)), "dp", axis=0)
@@ -353,20 +359,24 @@
         start = planes_of[number] * depth
         return lax.dynamic_slice_in_dim(weight, start, depth, axis=1)
 
+    half_rows = token_rows // 2
+    arrived = [tokens[:half_rows], tokens[half_rows:]]
+    moved = [turned(half) for half in arrived]
     lines = [turned(send, k) for k, send in enumerate(sends, 1)]
-    begun = project(planes_of[:1], tokens, shard(0))
+    begun = project(arrived, shard(0))
     sums = shrink_partial(adapters, here, planes, table, tokens, down_all)
-    done = (held[1], lines, begun, table, turn, up_all, own_rows, shard(1), sums)
+    done = (moved, lines, begun, table, turn, up_all, own_rows, shard(1), sums)
     done = lax.optimization_barrier(done)
-    held[1], lines, begun, table, turn, up_all, own_rows, part_weight, sums = done
-    lines = lax.all_gather(jnp.stack(lines), PLANE, axis=0)
+    moved, lines, begun, table, turn, up_all, own_rows, part_weight, sums = done
     for step in range(2, planes):
-        arrived = held[-1]
-        held.append(turned(arrived))
-        begun = project(planes_of[step - 1 : step], arrived, part_weight, [begun])
+        arrived = moved
+        last = step == planes - 1
+        moved = [turned(arrived[0]), arrived[1] if last else turned(arrived[1])]
+        begun = project(arrived, part_weight, [begun])
         side = ()
         if step == 2:
             sums = [sums[0]] + [turned(sums[k], k) for k in range(1, planes)]
+            lines = lax.all_gather(jnp.stack(lines), PLANE, axis=0)
             side = (
                 sums,
                 lax.all_gather(after(output_up_maps, sums[0]), "dp", axis=0, tiled=True),
@@ -376,18 +386,19 @@
             shrink = sum(sums[1:], sums[0]).astype(jnp.bfloat16)
             shrink = [shrink] + [turned(shrink, k) for k in range(1, planes)]
             side = (shrink, [lines[:, k] for k in range(planes - 1)])
-        done = lax.optimization_barrier((held[-1], begun, shard(step), side))
-        held[-1], begun, part_weight, side = done
+        done = lax.optimization_barrier((moved, begun, shard(step), side))
+        moved, begun, part_weight, side = done
         if step == 2:
             sums, out_up_all, own_down = side
         elif step == 3:
             shrink, lines = side
+    moved[1] = turned(moved[1])
 
     ids = jnp.concatenate([lax.axis_index("groups")[None], adapters])
     attended, earlier = [[], []], ()
     for part in range(2):
         made, *earlier = attend(
-            planes_of, adapters, part, table, turn, up_all, shrink, held[-1], part_weight,
+            planes_of, adapters, part, table, turn, up_all, shrink, moved[part], part_weight,
             begun, earlier,
         )
         attended[part] = [made, turned(after(made, *attended[0][1:]))]

time: 181 us -> 176 us (0.972)
  waiting for transfers between devices: 54.8 us -> 42.6 us
  local copies, waits for them, and re-layouts: 29.5 us -> 33.1 us
  starting transfers between devices: 21.2 us -> 24.3 us
  blocking collectives: 21.7 us -> 24.2 us
    ppermute x18 -> x21, waiting for transfers between devices: 54.7 us -> 42.6 us  [turned(): lax.ppermute(value, 'tensor', [(i, (i + turn) % planes) for i in range(pl...]
    ppermute x18 -> x21, starting transfers between devices: 21.2 us -> 24.2 us  [turned(): lax.ppermute(value, 'tensor', [(i, (i + turn) % planes) for i in range(pl...]
    slice x0 -> x1, local copies, waits for them, and re-layouts: none -> 2.34 us  [local(): arrived = [tokens[:half_rows], tokens[half_rows:]]]
    all_gather x1, blocking collectives: 8.55 us -> 10.8 us  [local(): lax.all_gather(after(output_up_maps, sums[0]), 'dp', axis=0, tiled=True)]
    unnamed x58 -> x74, local copies, waits for them, and re-layouts: 12.9 us -> 13.8 us
  transfers between devices with their start and end apart: 20 -> 23, of which waited for: 10 -> 10; matrix products, arithmetic and copies ran while one was open for 12% -> 12% of each run, Pallas kernels for 13% -> 15%
where the time goes in v18:
time: 176 us
  waiting for transfers between devices  42.6 us (24%)
  local copies, waits for them, and re-layouts  33.1 us (19%)
  Pallas kernels  28.7 us (16%)
  starting transfers between devices  24.3 us (14%)
  blocking collectives  24.2 us (14%)
  between operations  16.5 us (9%)
  other arithmetic  6.24 us (4%)
    ppermute x21, waiting for transfers between devices, turned(): lax.ppermute(value, 'tensor', [(i, (i + turn) % planes) for i in range(pl...  42.6 us
    pallas_call x14, Pallas kernels, call(): pl.pallas_call(kernel, out_shape=out, grid_spec=pltpu.PrefetchScalarGridS...  28.7 us
    ppermute x21, starting transfers between devices, turned(): lax.ppermute(value, 'tensor', [(i, (i + turn) % planes) for i in range(pl...  24.2 us
    unnamed x74, local copies, waits for them, and re-layouts  13.8 us
    all_gather x1, blocking collectives, local(): lax.all_gather(after(output_up_maps, sums[0]), 'dp', axis=0, tiled=True)  10.8 us
    all_gather x1, blocking collectives, local(): lax.all_gather(jnp.transpose(adapter_up_maps[0], (1, 0, 2)), 'dp', axis=0)  7.08 us
    all_gather x1, blocking collectives, local(): lax.all_gather(after(out_down, sums[0]), 'dp', axis=0)  6.3 us
    dynamic_slice x1, local copies, waits for them, and re-layouts, shard(): return lax.dynamic_slice_in_dim(weight, start, depth, axis=1)  5.17 us
  transfers between devices with their start and end apart: 23, of which 10 were waited for; matrix products, arithmetic and copies ran while one was open for 12% of the time, Pallas kernels for 15%

profile of v18, /device:TPU:0, one launch (start us, length us, event | category | flops | bytes accessed | tf_op | source)
XLA Modules:
  0.0 175.6 jit_solution(12124830141074962490)
XLA Ops:
  6.5 2.3 %fusion.5 = (bf16[256,1024]{1,0:T(8,128)(2,1)}, bf16[256,1024]{1,0:T(8,128)(2,1)}) fusion(bf16[512,1024]{1,0:T(8,128)(2,1)} %token_ref.1), kind=kLoop, calls=%fused_computation.40 | loop fusion | bytes 2097152 | tf_op jit(solution)/shard_map/slice | solution.py:363
  8.9 3.0 %collective-permute-start = (bf16[256,1024]{1,0:T(8,128)(2,1)}, bf16[256,1024]{1,0:T(8,128)(2,1)}, u32[]{:S(2)}, u32[]{:S(2)}) collective-permute-start(bf16[256,1024]{1,0:T(8,128)(2,1)} %get-tuple-element.142.refs_0_), channel_id=1, source_target_pairs={{0,1},{1,2},{2,3},{3,0},{4,5},{5,6},{6,7},{7,4},{8,9},{9,10},{10,1... | collective-permute-start | bytes 1572872 | tf_op jit(solution)/shard_map/ppermute | solution.py:312
  13.7 2.8 %fusion.4 = (bf16[64,1,1024]{2,1,0:T(2,128)(2,1)S(1)}, bf16[64,1,1024]{2,1,0:T(2,128)(2,1)S(1)}, bf16[64,1,1024]{2,1,0:T(2,128)(2,1)S(1)}) fusion(bf16[128,4,4096]{2,1,0:T(4,128)(2,1)} %param.11, s32[]{:T(128)S(6)} %select_n.76, s32[]{:T(128)S(6)} %select_n.79, s32[]{:T(128)S(6)} %select_n.88, s32[]{:T(128)S(6)} %select_n.85, s32[]{:T(128)S(6)} %select_n.82), kind=kLoop, calls=%fused_computation.39 | loop fusion | bytes 786452 | tf_op jit(solution)/shard_map/dynamic_slice | solution.py:351
  27.9 1.6 dynamic-slice_bitcast_fusion.4
  29.5 5.2 %dynamic-slice_bitcast_fusion = (bf16[6,1024,128]{2,1,0:T(8,128)(2,1)}, bf16[6,1024,128]{2,1,0:T(8,128)(2,1)}, bf16[6,1024,128]{2,1,0:T(8,128)(2,1)S(1)}, bf16[6,1024,128]{2,1,0:T(8,128)(2,1)}) fusion(bf16[4096,6,128]{2,0,1:T(8,128)(2,1)} %param.10, s32[]{:T(128)S(6)} %select_n.94, s32[]{:T(128)S(6)} %select_n.92, s32[]{:T(128)S(6)} %select_n.89, s32[]{:T(128)S(6)} %select_n.93), kind=kLoop, calls=%fused_computation.3 | loop fusion | bytes 12582928 | tf_op jit(solution)/shard_map/dynamic_slice | solution.py:360
  36.2 2.2 %project.3.refs_3_ = f32[512,768]{1,0:T(8,128)S(1)} custom-call(s32[1]{0:T(128)} %constant.140.clone.1.ids_ref, bf16[256,1024]{1,0:T(8,128)(2,1)} %get-tuple-element.142.refs_0_, bf16[256,1024]{1,0:T(8,128)(2,1)} %get-tuple-element.141.refs_1_, bf16[6,1024,128]{2,1,0:T(8,128)(2,1)S(1)} %get-tuple-element.133.refs_2_), custom_call_target="tpu_custom_call" | custom-call | bytes 7864320 | tf_op jit(solution)/shard_map/project/pallas_call | solution.py:26
  38.4 7.1 %all-gather = bf16[24,64,128]{2,1,0:T(8,128)(2,1)} all-gather(bf16[6,64,128]{2,1,0:T(8,128)(2,1)S(1)} %bitcast.69), channel_id=2, replica_groups=mesh['groups'=2,'dp'=4,'tensor'=4] {'dp'}, dimensions={0}, use_global_device_ids=true | all-gather | bytes 491520 | tf_op jit(solution)/shard_map/all_gather | solution.py:316
  48.1 2.7 %shrink.1 = (f32[192,128]{1,0:T(8,128)S(1)}, f32[192,128]{1,0:T(8,128)S(1)}, f32[192,128]{1,0:T(8,128)S(1)}, f32[192,128]{1,0:T(8,128)S(1)}) custom-call(s32[5]{0:T(128)S(1)} %pad_add_fusion.3.ids_ref, s32[512,2]{1,0:T(8,128)S(1)} %copy.42.table_ref, bf16[512,1024]{1,0:T(8,128)(2,1)S(1)} %copy-done.12, bf16[4,192,1024]{2,1,0:T(8,128)(2,1)S(1)} %copy-done.16), custom_call_target="tpu_custom_call" | custom-call | bytes 7876608 | tf_op jit(solution)/shard_map/shrink/pallas_call | solution.py:26
  52.9 2.1 %pad_maximum_fusion = bf16[3,96,1024]{2,1,0:T(8,128)(2,1)} fusion(bf16[1,96,1024]{2,1,0:T(8,128)(2,1)} %bitcast.26, bf16[1,96,1024]{2,1,0:T(8,128)(2,1)} %bitcast.25, bf16[1,96,1024]{2,1,0:T(8,128)(2,1)} %bitcast.24), kind=kLoop, calls=%fused_computation.8 | loop fusion | flops 589824 | bytes 1179648 | tf_op jit(solution)/shard_map/stack | solution.py:379
  55.1 1.9 %collective-permute-start.5 = (bf16[256,1024]{1,0:T(8,128)(2,1)}, bf16[256,1024]{1,0:T(8,128)(2,1)}, u32[]{:S(2)}, u32[]{:S(2)}) collective-permute-start(bf16[256,1024]{1,0:T(8,128)(2,1)} %collective-permute-done.refs_0_), channel_id=1, source_target_pairs={{0,1},{1,2},{2,3},{3,0},{4,5},{5,6},{6,7},{7,4},{8,9},{9,10},{10,1... | collective-permute-start | bytes 1572872 | tf_op jit(solution)/shard_map/ppermute | solution.py:312
  57.4 1.8 %collective-permute-start.7 = (f32[192,128]{1,0:T(8,128)}, f32[192,128]{1,0:T(8,128)S(1)}, u32[]{:S(2)}, u32[]{:S(2)}) collective-permute-start(f32[192,128]{1,0:T(8,128)} %copy-done.25), channel_id=1, source_target_pairs={{0,1},{1,2},{2,3},{3,0},{4,5},{5,6},{6,7},{7,4},{8,9},{9,10},{10,1... | collective-permute-start | bytes 294920 | tf_op jit(solution)/shard_map/ppermute | solution.py:312
  59.1 2.2 %collective-permute-start.8 = (f32[192,128]{1,0:T(8,128)S(1)}, f32[192,128]{1,0:T(8,128)S(1)}, u32[]{:S(2)}, u32[]{:S(2)}) collective-permute-start(f32[192,128]{1,0:T(8,128)S(1)} %copy-done.24), channel_id=1, source_target_pairs={{0,2},{1,3},{2,0},{3,1},{4,6},{5,7},{6,4},{7,5},{8,10},{9,11},{10,... | collective-permute-start | bytes 294920 | tf_op jit(solution)/shard_map/ppermute | solution.py:312
  62.4 2.4 %project.4.refs_3_ = f32[512,768]{1,0:T(8,128)S(1)} custom-call(s32[1]{0:T(128)} %constant.140.clone.1.ids_ref, bf16[256,1024]{1,0:T(8,128)(2,1)} %collective-permute-done.refs_0_, bf16[256,1024]{1,0:T(8,128)(2,1)} %collective-permute-done.1.refs_1_, bf16[6,1024,128]{2,1,0:T(8,128)(2,1)S(1)} %copy-done.8, f32[512,768]{1,0:T(8,128)S(1)} %project.3.refs_3_), custom_call_target="tpu_custom_call" | custom-call | bytes 12582912 | tf_op jit(solution)/shard_map/project/pallas_call | solution.py:26
  64.8 10.8 %all_gather.27.refs_3_ = bf16[4,64,1024]{2,1,0:T(8,128)(2,1)} all-gather(bf16[1,64,1024]{2,1,0:T(8,128)(2,1)S(1)} %copy-done.28), channel_id=1, replica_groups=mesh['groups'=2,'dp'=4,'tensor'=4] {'dp'}, dimensions={0}, use_global_device_ids=true | all-gather | bytes 655360 | tf_op jit(solution)/shard_map/all_gather | solution.py:382
  75.6 6.3 %all-gather.1 = bf16[128,1024]{1,0:T(8,128)(2,1)} all-gather(bf16[32,1024]{1,0:T(8,128)(2,1)S(1)} %copy-done.27), channel_id=3, replica_groups=mesh['groups'=2,'dp'=4,'tensor'=4] {'dp'}, dimensions={0}, use_global_device_ids=true | all-gather | bytes 327680 | tf_op jit(solution)/shard_map/all_gather | solution.py:383
  81.9 3.4 %collective-permute-done.7 = f32[192,128]{1,0:T(8,128)S(1)} collective-permute-done((f32[192,128]{1,0:T(8,128)}, f32[192,128]{1,0:T(8,128)S(1)}, u32[]{:S(2)}, u32[]{:S(2)}) %collective-permute-start.7) | collective-permute-done | bytes 98336 | tf_op jit(solution)/shard_map/ppermute | solution.py:312
  85.3 3.6 %collective-permute-done.8 = f32[192,128]{1,0:T(8,128)S(1)} collective-permute-done((f32[192,128]{1,0:T(8,128)S(1)}, f32[192,128]{1,0:T(8,128)S(1)}, u32[]{:S(2)}, u32[]{:S(2)}) %collective-permute-start.8) | collective-permute-done | bytes 98336 | tf_op jit(solution)/shard_map/ppermute | solution.py:312
  89.0 2.6 %collective-permute-start.10 = (bf16[256,1024]{1,0:T(8,128)(2,1)}, bf16[256,1024]{1,0:T(8,128)(2,1)}, u32[]{:S(2)}, u32[]{:S(2)}) collective-permute-start(bf16[256,1024]{1,0:T(8,128)(2,1)} %collective-permute-done.5.refs_0_), channel_id=1, source_target_pairs={{0,1},{1,2},{2,3},{3,0},{4,5},{5,6},{6,7},{7,4},{8,9},{9,10},{10,1... | collective-permute-start | bytes 1572872 | tf_op jit(solution)/shard_map/ppermute | solution.py:312
  91.7 1.9 %collective-permute-start.12 = (bf16[192,128]{1,0:T(8,128)(2,1)S(1)}, bf16[192,128]{1,0:T(8,128)(2,1)S(1)}, u32[]{:S(2)}, u32[]{:S(2)}) collective-permute-start(bf16[192,128]{1,0:T(8,128)(2,1)S(1)} %add_convert_fusion.refs_0_), channel_id=1, source_target_pairs={{0,2},{1,3},{2,0},{3,1},{4,6},{5,7},{6,4},{7,5},{8,10},{9,11},{10,... | collective-permute-start | bytes 147464 | tf_op jit(solution)/shard_map/ppermute | solution.py:312
  93.5 2.0 %collective-permute-start.13 = (bf16[192,128]{1,0:T(8,128)(2,1)S(1)}, bf16[192,128]{1,0:T(8,128)(2,1)S(1)}, u32[]{:S(2)}, u32[]{:S(2)}) collective-permute-start(bf16[192,128]{1,0:T(8,128)(2,1)S(1)} %add_convert_fusion.refs_0_), channel_id=1, source_target_pairs={{0,3},{1,0},{2,1},{3,2},{4,7},{5,4},{6,5},{7,6},{8,11},{9,8},{10,9... | collective-permute-start | bytes 147464 | tf_op jit(solution)/shard_map/ppermute | solution.py:312
  95.5 2.2 %project.5.refs_6_ = f32[512,768]{1,0:T(8,128)S(1)} custom-call(s32[1]{0:T(128)} %constant.140.clone.1.ids_ref, bf16[256,1024]{1,0:T(8,128)(2,1)} %collective-permute-done.5.refs_0_, bf16[256,1024]{1,0:T(8,128)(2,1)} %collective-permute-done.6.refs_1_, bf16[6,1024,128]{2,1,0:T(8,128)(2,1)S(1)} %copy-done.7, f32[512,768]{1,0:T(8,128)S(1)} %project.4.refs_3_), custom_call_target="tpu_custom_call" | custom-call | bytes 12582912 | tf_op jit(solution)/shard_map/project/pallas_call | solution.py:26
  98.8 4.4 %slice_bitcast_fusion = (bf16[8,96,1024]{2,1,0:T(8,128)(2,1)}, bf16[8,96,1024]{2,1,0:T(8,128)(2,1)S(1)}, bf16[8,96,1024]{2,1,0:T(8,128)(2,1)S(1)}) fusion(bf16[8,3,96,1024]{3,2,1,0:T(8,128)(2,1)} %bitcast.65), kind=kLoop, calls=%fused_computation | loop fusion | bytes 9437184 | tf_op jit(solution)/shard_map/squeeze | solution.py:388
  103.2 3.8 %collective-permute-done.11.refs_1_ = bf16[192,128]{1,0:T(8,128)(2,1)S(1)} collective-permute-done((bf16[192,128]{1,0:T(8,128)(2,1)S(1)}, bf16[192,128]{1,0:T(8,128)(2,1)S(1)}, u32[]{:S(2)}, u32[]{:S(2)}) %collective-permute-start.11) | collective-permute-done | bytes 49184 | tf_op jit(solution)/shard_map/ppermute | solution.py:312
  118.0 4.4 %attend.2 = (bf16[256,512]{1,0:T(8,128)(2,1)S(1)}, bf16[256,128]{1,0:T(8,128)(2,1)S(1)}, bf16[256,128]{1,0:T(8,128)(2,1)S(1)}) custom-call(s32[8]{0:T(128)S(1)} %copy-done.20, s32[512,2]{1,0:T(8,128)S(1)} %copy.47.table_ref.refs_2_, f32[512,256]{1,0:T(8,128)S(1)} %copy-done.10, bf16[4,6,64,128]{3,2,1,0:T(8,128)(2,1)S(1)} %bitcast.61, ...), custom_call_target="tpu_custom_call" | custom-call | bytes 14364672 | tf_op jit(solution)/shard_map/attend/pallas_call | solution.py:26
  123.8 8.4 %collective-permute-done.15.attended_ref = bf16[256,512]{1,0:T(8,128)(2,1)S(1)} collective-permute-done((bf16[256,512]{1,0:T(8,128)(2,1)S(1)}, bf16[256,512]{1,0:T(8,128)(2,1)S(1)}, u32[]{:S(2)}, u32[]{:S(2)}) %collective-permute-start.15) | collective-permute-done | bytes 262176 | tf_op jit(solution)/shard_map/ppermute | solution.py:312
  132.3 4.9 %attend.3 = (bf16[256,512]{1,0:T(8,128)(2,1)S(1)}, bf16[256,128]{1,0:T(8,128)(2,1)}, bf16[256,128]{1,0:T(8,128)(2,1)}) custom-call(s32[8]{0:T(128)S(1)} %copy-done.20, s32[512,2]{1,0:T(8,128)S(1)} %copy.47.table_ref.refs_2_, f32[512,256]{1,0:T(8,128)S(1)} %copy-done.11, bf16[4,6,64,128]{3,2,1,0:T(8,128)(2,1)S(1)} %bitcast.62, ...), custom_call_target="tpu_custom_call" | custom-call | bytes 14757888 | tf_op jit(solution)/shard_map/attend/pallas_call | solution.py:26
  139.4 2.3 %collective-permute-done.17.attended_ref = bf16[256,512]{1,0:T(8,128)(2,1)S(1)} collective-permute-done((bf16[256,512]{1,0:T(8,128)(2,1)S(1)}, bf16[256,512]{1,0:T(8,128)(2,1)S(1)}, u32[]{:S(2)}, u32[]{:S(2)}) %collective-permute-start.17) | collective-permute-done | bytes 262176 | tf_op jit(solution)/shard_map/ppermute | solution.py:312
  141.7 6.6 %collective-permute-done.16.attended_ref = bf16[256,512]{1,0:T(8,128)(2,1)S(1)} collective-permute-done((bf16[256,512]{1,0:T(8,128)(2,1)S(1)}, bf16[256,512]{1,0:T(8,128)(2,1)S(1)}, u32[]{:S(2)}, u32[]{:S(2)}) %collective-permute-start.16) | collective-permute-done | bytes 262176 | tf_op jit(solution)/shard_map/ppermute | solution.py:312
  149.3 4.5 %collective-permute-done.19.attended_ref = bf16[256,512]{1,0:T(8,128)(2,1)S(1)} collective-permute-done((bf16[256,512]{1,0:T(8,128)(2,1)S(1)}, bf16[256,512]{1,0:T(8,128)(2,1)S(1)}, u32[]{:S(2)}, u32[]{:S(2)}) %collective-permute-start.19) | collective-permute-done | bytes 262176 | tf_op jit(solution)/shard_map/ppermute | solution.py:312
  153.9 4.1 %collective-permute-done.18.attended_ref = bf16[256,512]{1,0:T(8,128)(2,1)S(1)} collective-permute-done((bf16[256,512]{1,0:T(8,128)(2,1)S(1)}, bf16[256,512]{1,0:T(8,128)(2,1)S(1)}, u32[]{:S(2)}, u32[]{:S(2)}) %collective-permute-start.18) | collective-permute-done | bytes 262176 | tf_op jit(solution)/shard_map/ppermute | solution.py:312
  161.8 4.7 %collective-permute-done.20.attended_ref = bf16[256,512]{1,0:T(8,128)(2,1)S(1)} collective-permute-done((bf16[256,512]{1,0:T(8,128)(2,1)S(1)}, bf16[256,512]{1,0:T(8,128)(2,1)S(1)}, u32[]{:S(2)}, u32[]{:S(2)}) %collective-permute-start.20) | collective-permute-done | bytes 262176 | tf_op jit(solution)/shard_map/ppermute | solution.py:312
  166.5 2.3 %project_out.15 = bf16[512,1024]{1,0:T(8,128)(2,1)} custom-call(s32[5]{0:T(128)S(1)} %pad_add_fusion.1.ids_ref, bf16[256,512]{1,0:T(8,128)(2,1)S(1)} %collective-permute-done.20.attended_ref, bf16[8,96,1024]{2,1,0:T(8,128)(2,1)S(1)} %copy-done, bf16[8,96,1024]{2,1,0:T(8,128)(2,1)S(1)} %copy-done, f32[256,1024]{1,0:T(8,128)S(1)} %get-tuple-element.126.refs_0_, ...), custom_call_target="tpu_custom_call" | custom-call | bytes 17313792 | tf_op jit(solution)/shard_map/project_out/pallas_call | solution.py:26
  (138 shorter events, 38.6 us)
Async XLA Ops:
  6.5 39.0 %all-gather.6.cloned.1.call-start = ((), (), s32[]{:S(2)}) async-start(), calls=%async_computation | async-start | bytes 1966080 | tf_op jit(solution)/shard_map/all_gather | solution.py:315
  8.9 44.0 %collective-permute-start = (bf16[256,1024]{1,0:T(8,128)(2,1)}, bf16[256,1024]{1,0:T(8,128)(2,1)}, u32[]{:S(2)}, u32[]{:S(2)}) collective-permute-start(bf16[256,1024]{1,0:T(8,128)(2,1)} %get-tuple-element.142.refs_0_), channel_id=1, source_target_pairs={{0,1},{1,2},{2,3},{3,0},{4,5},{5,6},{6,7},{7,4},{8,9},{9,10},{10,1... | collective-permute-start | bytes 1572872 | tf_op jit(solution)/shard_map/ppermute | solution.py:312
  11.9 41.0 %collective-permute-start.1 = (bf16[256,1024]{1,0:T(8,128)(2,1)}, bf16[256,1024]{1,0:T(8,128)(2,1)}, u32[]{:S(2)}, u32[]{:S(2)}) collective-permute-start(bf16[256,1024]{1,0:T(8,128)(2,1)} %get-tuple-element.141.refs_1_), channel_id=1, source_target_pairs={{0,1},{1,2},{2,3},{3,0},{4,5},{5,6},{6,7},{7,4},{8,9},{9,10},{10,1... | collective-permute-start | bytes 1572872 | tf_op jit(solution)/shard_map/ppermute | solution.py:312
  13.5 85.3 %all-gather.8.cloned.1.call-start = ((), (), s32[]{:S(2)}) async-start(), calls=%async_computation.1 | async-start | bytes 5308416 | tf_op jit(solution)/shard_map/all_gather | solution.py:379
  16.7 10.1 %copy-start.26 = (bf16[32,1024]{1,0:T(8,128)(2,1)}, bf16[32,1024]{1,0:T(8,128)(2,1)S(1)}, u32[]{:S(2)}) copy-start(bf16[32,1024]{1,0:T(8,128)(2,1)S(1)} %bitcast_dynamic-update-slice_fusion) | copy-start | bytes 196612
  17.6 35.2 %collective-permute-start.2 = (bf16[96,1024]{1,0:T(8,128)(2,1)}, bf16[96,1024]{1,0:T(8,128)(2,1)}, u32[]{:S(2)}, u32[]{:S(2)}) collective-permute-start(bf16[96,1024]{1,0:T(8,128)(2,1)} %get-tuple-element.145), channel_id=1, source_target_pairs={{0,1},{1,2},{2,3},{3,0},{4,5},{5,6},{6,7},{7,4},{8,9},{9,10},{10,1... | collective-permute-start | bytes 589832 | tf_op jit(solution)/shard_map/ppermute | solution.py:312
  19.2 33.6 %collective-permute-start.3 = (bf16[96,1024]{1,0:T(8,128)(2,1)}, bf16[96,1024]{1,0:T(8,128)(2,1)}, u32[]{:S(2)}, u32[]{:S(2)}) collective-permute-start(bf16[96,1024]{1,0:T(8,128)(2,1)} %get-tuple-element.144), channel_id=1, source_target_pairs={{0,2},{1,3},{2,0},{3,1},{4,6},{5,7},{6,4},{7,5},{8,10},{9,11},{10,... | collective-permute-start | bytes 589832 | tf_op jit(solution)/shard_map/ppermute | solution.py:312
  20.5 32.4 %collective-permute-start.4 = (bf16[96,1024]{1,0:T(8,128)(2,1)}, bf16[96,1024]{1,0:T(8,128)(2,1)}, u32[]{:S(2)}, u32[]{:S(2)}) collective-permute-start(bf16[96,1024]{1,0:T(8,128)(2,1)} %get-tuple-element.143), channel_id=1, source_target_pairs={{0,3},{1,0},{2,1},{3,2},{4,7},{5,4},{6,5},{7,6},{8,11},{9,8},{10,9... | collective-permute-start | bytes 589832 | tf_op jit(solution)/shard_map/ppermute | solution.py:312
  55.0 20.6 %copy-start.27 = (bf16[32,1024]{1,0:T(8,128)(2,1)S(1)}, bf16[32,1024]{1,0:T(8,128)(2,1)}, u32[]{:S(2)}) copy-start(bf16[32,1024]{1,0:T(8,128)(2,1)} %copy-done.26) | copy-start | bytes 196612
  55.1 33.9 %collective-permute-start.5 = (bf16[256,1024]{1,0:T(8,128)(2,1)}, bf16[256,1024]{1,0:T(8,128)(2,1)}, u32[]{:S(2)}, u32[]{:S(2)}) collective-permute-start(bf16[256,1024]{1,0:T(8,128)(2,1)} %collective-permute-done.refs_0_), channel_id=1, source_target_pairs={{0,1},{1,2},{2,3},{3,0},{4,5},{5,6},{6,7},{7,4},{8,9},{9,10},{10,1... | collective-permute-start | bytes 1572872 | tf_op jit(solution)/shard_map/ppermute | solution.py:312
  57.0 32.0 %collective-permute-start.6 = (bf16[256,1024]{1,0:T(8,128)(2,1)}, bf16[256,1024]{1,0:T(8,128)(2,1)}, u32[]{:S(2)}, u32[]{:S(2)}) collective-permute-start(bf16[256,1024]{1,0:T(8,128)(2,1)} %collective-permute-done.1.refs_1_), channel_id=1, source_target_pairs={{0,1},{1,2},{2,3},{3,0},{4,5},{5,6},{6,7},{7,4},{8,9},{9,10},{10,1... | collective-permute-start | bytes 1572872 | tf_op jit(solution)/shard_map/ppermute | solution.py:312
  57.4 28.0 %collective-permute-start.7 = (f32[192,128]{1,0:T(8,128)}, f32[192,128]{1,0:T(8,128)S(1)}, u32[]{:S(2)}, u32[]{:S(2)}) collective-permute-start(f32[192,128]{1,0:T(8,128)} %copy-done.25), channel_id=1, source_target_pairs={{0,1},{1,2},{2,3},{3,0},{4,5},{5,6},{6,7},{7,4},{8,9},{9,10},{10,1... | collective-permute-start | bytes 294920 | tf_op jit(solution)/shard_map/ppermute | solution.py:312
  59.1 29.9 %collective-permute-start.8 = (f32[192,128]{1,0:T(8,128)S(1)}, f32[192,128]{1,0:T(8,128)S(1)}, u32[]{:S(2)}, u32[]{:S(2)}) collective-permute-start(f32[192,128]{1,0:T(8,128)S(1)} %copy-done.24), channel_id=1, source_target_pairs={{0,2},{1,3},{2,0},{3,1},{4,6},{5,7},{6,4},{7,5},{8,10},{9,11},{10,... | collective-permute-start | bytes 294920 | tf_op jit(solution)/shard_map/ppermute | solution.py:312
  61.4 27.6 %collective-permute-start.9 = (f32[192,128]{1,0:T(8,128)S(1)}, f32[192,128]{1,0:T(8,128)S(1)}, u32[]{:S(2)}, u32[]{:S(2)}) collective-permute-start(f32[192,128]{1,0:T(8,128)S(1)} %copy-done.22), channel_id=1, source_target_pairs={{0,3},{1,0},{2,1},{3,2},{4,7},{5,4},{6,5},{7,6},{8,11},{9,8},{10,9... | collective-permute-start | bytes 294920 | tf_op jit(solution)/shard_map/ppermute | solution.py:312
  62.4 33.0 %copy-start.7 = (bf16[6,1024,128]{2,1,0:T(8,128)(2,1)S(1)}, bf16[6,1024,128]{2,1,0:T(8,128)(2,1)}, u32[]{:S(2)}) copy-start(bf16[6,1024,128]{2,1,0:T(8,128)(2,1)} %get-tuple-element.87.refs_2_) | copy-start | bytes 4718596
  89.0 19.7 %collective-permute-start.10 = (bf16[256,1024]{1,0:T(8,128)(2,1)}, bf16[256,1024]{1,0:T(8,128)(2,1)}, u32[]{:S(2)}, u32[]{:S(2)}) collective-permute-start(bf16[256,1024]{1,0:T(8,128)(2,1)} %collective-permute-done.5.refs_0_), channel_id=1, source_target_pairs={{0,1},{1,2},{2,3},{3,0},{4,5},{5,6},{6,7},{7,4},{8,9},{9,10},{10,1... | collective-permute-start | bytes 1572872 | tf_op jit(solution)/shard_map/ppermute | solution.py:312
  91.6 15.5 %collective-permute-start.11 = (bf16[192,128]{1,0:T(8,128)(2,1)S(1)}, bf16[192,128]{1,0:T(8,128)(2,1)S(1)}, u32[]{:S(2)}, u32[]{:S(2)}) collective-permute-start(bf16[192,128]{1,0:T(8,128)(2,1)S(1)} %add_convert_fusion.refs_0_), channel_id=1, source_target_pairs={{0,1},{1,2},{2,3},{3,0},{4,5},{5,6},{6,7},{7,4},{8,9},{9,10},{10,1... | collective-permute-start | bytes 147464 | tf_op jit(solution)/shard_map/ppermute | solution.py:312
  91.7 16.4 %collective-permute-start.12 = (bf16[192,128]{1,0:T(8,128)(2,1)S(1)}, bf16[192,128]{1,0:T(8,128)(2,1)S(1)}, u32[]{:S(2)}, u32[]{:S(2)}) collective-permute-start(bf16[192,128]{1,0:T(8,128)(2,1)S(1)} %add_convert_fusion.refs_0_), channel_id=1, source_target_pairs={{0,2},{1,3},{2,0},{3,1},{4,6},{5,7},{6,4},{7,5},{8,10},{9,11},{10,... | collective-permute-start | bytes 147464 | tf_op jit(solution)/shard_map/ppermute | solution.py:312
  93.5 14.6 %collective-permute-start.13 = (bf16[192,128]{1,0:T(8,128)(2,1)S(1)}, bf16[192,128]{1,0:T(8,128)(2,1)S(1)}, u32[]{:S(2)}, u32[]{:S(2)}) collective-permute-start(bf16[192,128]{1,0:T(8,128)(2,1)S(1)} %add_convert_fusion.refs_0_), channel_id=1, source_target_pairs={{0,3},{1,0},{2,1},{3,2},{4,7},{5,4},{6,5},{7,6},{8,11},{9,8},{10,9... | collective-permute-start | bytes 147464 | tf_op jit(solution)/shard_map/ppermute | solution.py:312
  98.8 11.4 %copy-start.33 = (s32[4]{0:T(128)S(1)}, s32[4]{0:T(128)}, u32[]{:S(2)}) copy-start(s32[4]{0:T(128)} %copy-done.32) | copy-start | bytes 52
  108.7 23.5 %collective-permute-start.14 = (bf16[256,1024]{1,0:T(8,128)(2,1)}, bf16[256,1024]{1,0:T(8,128)(2,1)}, u32[]{:S(2)}, u32[]{:S(2)}) collective-permute-start(bf16[256,1024]{1,0:T(8,128)(2,1)} %collective-permute-done.6.refs_1_), channel_id=1, source_target_pairs={{0,1},{1,2},{2,3},{3,0},{4,5},{5,6},{6,7},{7,4},{8,9},{9,10},{10,1... | collective-permute-start | bytes 1572872 | tf_op jit(solution)/shard_map/ppermute | solution.py:312
  118.0 14.3 %copy-start.5 = (bf16[6,1024,128]{2,1,0:T(8,128)(2,1)S(1)}, bf16[6,1024,128]{2,1,0:T(8,128)(2,1)}, u32[]{:S(2)}) copy-start(bf16[6,1024,128]{2,1,0:T(8,128)(2,1)} %get-tuple-element.101.refs_5_) | copy-start | bytes 4718596
  118.0 14.3 %copy-start.11 = (f32[512,256]{1,0:T(8,128)S(1)}, f32[512,256]{1,0:T(8,128)}, u32[]{:S(2)}) copy-start(f32[512,256]{1,0:T(8,128)} %pad_maximum_fusion.1.turn_ref) | copy-start | bytes 1572868
  118.0 14.3 %copy-start.14 = (bf16[24,64,128]{2,1,0:T(8,128)(2,1)S(1)}, bf16[24,64,128]{2,1,0:T(8,128)(2,1)}, u32[]{:S(2)}) copy-start(bf16[24,64,128]{2,1,0:T(8,128)(2,1)} %all-gather) | copy-start | bytes 1179652
  118.0 14.3 %copy-start.19 = (bf16[192,128]{1,0:T(8,128)(2,1)S(1)}, bf16[192,128]{1,0:T(8,128)(2,1)}, u32[]{:S(2)}) copy-start(bf16[192,128]{1,0:T(8,128)(2,1)} %copy-done.17) | copy-start | bytes 147460
  122.4 9.9 %copy-start.3 = (f32[512,768]{1,0:T(8,128)S(1)}, f32[512,768]{1,0:T(8,128)}, u32[]{:S(2)}) copy-start(f32[512,768]{1,0:T(8,128)} %copy-done.1) | copy-start | bytes 4718596
  122.5 9.8 %collective-permute-start.15 = (bf16[256,512]{1,0:T(8,128)(2,1)S(1)}, bf16[256,512]{1,0:T(8,128)(2,1)S(1)}, u32[]{:S(2)}, u32[]{:S(2)}) collective-permute-start(bf16[256,512]{1,0:T(8,128)(2,1)S(1)} %get-tuple-element.107.attended_ref), channel_id=1, source_target_pairs={{0,1},{1,2},{2,3},{3,0},{4,5},{5,6},{6,7},{7,4},{8,9},{9,10},{10,1... | collective-permute-start | bytes 786440 | tf_op jit(solution)/shard_map/ppermute | solution.py:312
  132.2 9.4 %collective-permute-start.17 = (bf16[256,512]{1,0:T(8,128)(2,1)S(1)}, bf16[256,512]{1,0:T(8,128)(2,1)S(1)}, u32[]{:S(2)}, u32[]{:S(2)}) collective-permute-start(bf16[256,512]{1,0:T(8,128)(2,1)S(1)} %collective-permute-done.15.attended_ref), channel_id=1, source_target_pairs={{0,1},{1,2},{2,3},{3,0},{4,5},{5,6},{6,7},{7,4},{8,9},{9,10},{10,1... | collective-permute-start | bytes 786440 | tf_op jit(solution)/shard_map/ppermute | solution.py:312
  137.2 11.1 %collective-permute-start.16 = (bf16[256,512]{1,0:T(8,128)(2,1)S(1)}, bf16[256,512]{1,0:T(8,128)(2,1)S(1)}, u32[]{:S(2)}, u32[]{:S(2)}) collective-permute-start(bf16[256,512]{1,0:T(8,128)(2,1)S(1)} %get-tuple-element.108.attended_ref), channel_id=1, source_target_pairs={{0,1},{1,2},{2,3},{3,0},{4,5},{5,6},{6,7},{7,4},{8,9},{9,10},{10,1... | collective-permute-start | bytes 786440 | tf_op jit(solution)/shard_map/ppermute | solution.py:312
  141.7 12.2 %collective-permute-start.19 = (bf16[256,512]{1,0:T(8,128)(2,1)S(1)}, bf16[256,512]{1,0:T(8,128)(2,1)S(1)}, u32[]{:S(2)}, u32[]{:S(2)}) collective-permute-start(bf16[256,512]{1,0:T(8,128)(2,1)S(1)} %collective-permute-done.17.attended_ref), channel_id=1, source_target_pairs={{0,1},{1,2},{2,3},{3,0},{4,5},{5,6},{6,7},{7,4},{8,9},{9,10},{10,1... | collective-permute-start | bytes 786440 | tf_op jit(solution)/shard_map/ppermute | solution.py:312
  148.3 9.7 %collective-permute-start.18 = (bf16[256,512]{1,0:T(8,128)(2,1)S(1)}, bf16[256,512]{1,0:T(8,128)(2,1)S(1)}, u32[]{:S(2)}, u32[]{:S(2)}) collective-permute-start(bf16[256,512]{1,0:T(8,128)(2,1)S(1)} %collective-permute-done.16.attended_ref), channel_id=1, source_target_pairs={{0,1},{1,2},{2,3},{3,0},{4,5},{5,6},{6,7},{7,4},{8,9},{9,10},{10,1... | collective-permute-start | bytes 786440 | tf_op jit(solution)/shard_map/ppermute | solution.py:312
  158.0 8.6 %collective-permute-start.20 = (bf16[256,512]{1,0:T(8,128)(2,1)S(1)}, bf16[256,512]{1,0:T(8,128)(2,1)S(1)}, u32[]{:S(2)}, u32[]{:S(2)}) collective-permute-start(bf16[256,512]{1,0:T(8,128)(2,1)S(1)} %collective-permute-done.18.attended_ref), channel_id=1, source_target_pairs={{0,1},{1,2},{2,3},{3,0},{4,5},{5,6},{6,7},{7,4},{8,9},{9,10},{10,1... | collective-permute-start | bytes 786440 | tf_op jit(solution)/shard_map/ppermute | solution.py:312
  (27 other events, 96.1 us)
Sparse Core Ops, SparseCore 0:
  13.6 19.5 all-gather.5
  55.2 41.9 all-gather.7

commit v19 on v18

--- a/solution.py
+++ b/solution.py
@@ -386,13 +386,16 @@
             shrink = sum(sums[1:], sums[0]).astype(jnp.bfloat16)
             shrink = [shrink] + [turned(shrink, k) for k in range(1, planes)]
             side = (shrink, [lines[:, k] for k in range(planes - 1)])
+        if step == 3:
+            shrink, lines = side
+        if last:
+            part_weight = shard(step)
+            moved[1] = turned(after(moved[1], moved[0], *lines))
+            break
         done = lax.optimization_barrier((moved, begun, shard(step), side))
         moved, begun, part_weight, side = done
         if step == 2:
             sums, out_up_all, own_down = side
-        elif step == 3:
-            shrink, lines = side
-    moved[1] = turned(moved[1])
 
     ids = jnp.concatenate([lax.axis_index("groups")[None], adapters])
     attended, earlier = [[], []], ()

time: 176 us -> 180 us (1.023)
  waiting for transfers between devices: 42.6 us -> 49.5 us
  local copies, waits for them, and re-layouts: 33.1 us -> 28.3 us
  starting transfers between devices: 24.3 us -> 27.2 us
    all_gather x1, waiting for transfers between devices: 0.01 us -> 6.54 us  [local(): lines = lax.all_gather(jnp.stack(lines), PLANE, axis=0)]
    unnamed x74 -> x70, local copies, waits for them, and re-layouts: 13.8 us -> 10.2 us
    ppermute x21, starting transfers between devices: 24.2 us -> 27.2 us  [turned(): lax.ppermute(value, 'tensor', [(i, (i + turn) % planes) for i in range(pl...]
  transfers between devices with their start and end apart: 23 -> 23, of which waited for: 10 -> 14; matrix products, arithmetic and copies ran while one was open for 12% -> 10% of each run, Pallas kernels for 15% -> 15%
where the time goes in v19:
time: 180 us
  waiting for transfers between devices  49.5 us (28%)
  Pallas kernels  28.6 us (16%)
  local copies, waits for them, and re-layouts  28.3 us (16%)
  starting transfers between devices  27.2 us (15%)
  blocking collectives  23.9 us (13%)
  between operations  16.3 us (9%)
  other arithmetic  6.13 us (3%)
    ppermute x21, waiting for transfers between devices, turned(): lax.ppermute(value, 'tensor', [(i, (i + turn) % planes) for i in range(pl...  42.9 us
    pallas_call x14, Pallas kernels, call(): pl.pallas_call(kernel, out_shape=out, grid_spec=pltpu.PrefetchScalarGridS...  28.6 us
    ppermute x21, starting transfers between devices, turned(): lax.ppermute(value, 'tensor', [(i, (i + turn) % planes) for i in range(pl...  27.2 us
    all_gather x1, blocking collectives, local(): lax.all_gather(after(output_up_maps, sums[0]), 'dp', axis=0, tiled=True)  10.5 us
    unnamed x70, local copies, waits for them, and re-layouts  10.2 us
    all_gather x1, blocking collectives, local(): lax.all_gather(jnp.transpose(adapter_up_maps[0], (1, 0, 2)), 'dp', axis=0)  7.06 us
    all_gather x1, waiting for transfers between devices, local(): lines = lax.all_gather(jnp.stack(lines), PLANE, axis=0)  6.54 us
    all_gather x1, blocking collectives, local(): lax.all_gather(after(out_down, sums[0]), 'dp', axis=0)  6.3 us
  transfers between devices with their start and end apart: 23, of which 14 were waited for; matrix products, arithmetic and copies ran while one was open for 10% of the time, Pallas kernels for 15%

profile of v19, /device:TPU:0, one launch (start us, length us, event | category | flops | bytes accessed | tf_op | source)
XLA Modules:
  0.0 179.9 jit_solution(18279771079315101128)
XLA Ops:
  6.5 2.9 %fusion.4 = (bf16[64,1,1024]{2,1,0:T(2,128)(2,1)S(1)}, bf16[64,1,1024]{2,1,0:T(2,128)(2,1)S(1)}, bf16[64,1,1024]{2,1,0:T(2,128)(2,1)S(1)}) fusion(bf16[128,4,4096]{2,1,0:T(4,128)(2,1)} %param.11, s32[]{:T(128)S(6)} %select_n.76, s32[]{:T(128)S(6)} %select_n.79, s32[]{:T(128)S(6)} %select_n.88, s32[]{:T(128)S(6)} %select_n.85, s32[]{:T(128)S(6)} %select_n.82), kind=kLoop, calls=%fused_computation.39 | loop fusion | bytes 786452 | tf_op jit(solution)/shard_map/dynamic_slice | solution.py:351
  10.5 3.0 %collective-permute-start.2 = (bf16[96,1024]{1,0:T(8,128)(2,1)}, bf16[96,1024]{1,0:T(8,128)(2,1)}, u32[]{:S(2)}, u32[]{:S(2)}) collective-permute-start(bf16[96,1024]{1,0:T(8,128)(2,1)} %get-tuple-element.125), channel_id=1, source_target_pairs={{0,1},{1,2},{2,3},{3,0},{4,5},{5,6},{6,7},{7,4},{8,9},{9,10},{10,1... | collective-permute-start | bytes 589832 | tf_op jit(solution)/shard_map/ppermute | solution.py:312
  13.5 2.6 %collective-permute-start.3 = (bf16[96,1024]{1,0:T(8,128)(2,1)}, bf16[96,1024]{1,0:T(8,128)(2,1)}, u32[]{:S(2)}, u32[]{:S(2)}) collective-permute-start(bf16[96,1024]{1,0:T(8,128)(2,1)} %get-tuple-element.124), channel_id=1, source_target_pairs={{0,2},{1,3},{2,0},{3,1},{4,6},{5,7},{6,4},{7,5},{8,10},{9,11},{10,... | collective-permute-start | bytes 589832 | tf_op jit(solution)/shard_map/ppermute | solution.py:312
  25.5 1.6 dynamic-slice_bitcast_fusion.4
  27.0 5.2 %dynamic-slice_bitcast_fusion = (bf16[6,1024,128]{2,1,0:T(8,128)(2,1)}, bf16[6,1024,128]{2,1,0:T(8,128)(2,1)}, bf16[6,1024,128]{2,1,0:T(8,128)(2,1)S(1)}, bf16[6,1024,128]{2,1,0:T(8,128)(2,1)}) fusion(bf16[4096,6,128]{2,0,1:T(8,128)(2,1)} %param.10, s32[]{:T(128)S(6)} %select_n.94, s32[]{:T(128)S(6)} %select_n.92, s32[]{:T(128)S(6)} %select_n.89, s32[]{:T(128)S(6)} %select_n.93), kind=kLoop, calls=%fused_computation.3 | loop fusion | bytes 12582928 | tf_op jit(solution)/shard_map/dynamic_slice | solution.py:360
  33.8 2.2 %project.3.refs_3_ = f32[512,768]{1,0:T(8,128)S(1)} custom-call(s32[1]{0:T(128)} %constant.140.clone.1.ids_ref, bf16[256,1024]{1,0:T(8,128)(2,1)} %get-tuple-element.122.refs_0_, bf16[256,1024]{1,0:T(8,128)(2,1)} %get-tuple-element.121.refs_1_, bf16[6,1024,128]{2,1,0:T(8,128)(2,1)S(1)} %get-tuple-element.113.refs_2_), custom_call_target="tpu_custom_call" | custom-call | bytes 7864320 | tf_op jit(solution)/shard_map/project/pallas_call | solution.py:26
  36.0 7.1 %all-gather = bf16[24,64,128]{2,1,0:T(8,128)(2,1)} all-gather(bf16[6,64,128]{2,1,0:T(8,128)(2,1)S(1)} %bitcast.69), channel_id=2, replica_groups=mesh['groups'=2,'dp'=4,'tensor'=4] {'dp'}, dimensions={0}, use_global_device_ids=true | all-gather | bytes 491520 | tf_op jit(solution)/shard_map/all_gather | solution.py:316
  45.7 2.7 %shrink.1 = (f32[192,128]{1,0:T(8,128)S(1)}, f32[192,128]{1,0:T(8,128)S(1)}, f32[192,128]{1,0:T(8,128)S(1)}, f32[192,128]{1,0:T(8,128)S(1)}) custom-call(s32[5]{0:T(128)S(1)} %pad_add_fusion.3.ids_ref, s32[512,2]{1,0:T(8,128)S(1)} %copy.42.table_ref, bf16[512,1024]{1,0:T(8,128)(2,1)S(1)} %copy-done.10, bf16[4,192,1024]{2,1,0:T(8,128)(2,1)S(1)} %copy-done.13), custom_call_target="tpu_custom_call" | custom-call | bytes 7876608 | tf_op jit(solution)/shard_map/shrink/pallas_call | solution.py:26
  51.8 2.1 %pad_maximum_fusion = bf16[3,96,1024]{2,1,0:T(8,128)(2,1)} fusion(bf16[1,96,1024]{2,1,0:T(8,128)(2,1)} %bitcast.24, bf16[1,96,1024]{2,1,0:T(8,128)(2,1)} %bitcast.23, bf16[1,96,1024]{2,1,0:T(8,128)(2,1)} %bitcast.22), kind=kLoop, calls=%fused_computation.8 | loop fusion | flops 589824 | bytes 1179648 | tf_op jit(solution)/shard_map/stack | solution.py:379
  54.0 4.7 %collective-permute-start.5 = (bf16[256,1024]{1,0:T(8,128)(2,1)}, bf16[256,1024]{1,0:T(8,128)(2,1)}, u32[]{:S(2)}, u32[]{:S(2)}) collective-permute-start(bf16[256,1024]{1,0:T(8,128)(2,1)} %collective-permute-done.refs_0_), channel_id=1, source_target_pairs={{0,1},{1,2},{2,3},{3,0},{4,5},{5,6},{6,7},{7,4},{8,9},{9,10},{10,1... | collective-permute-start | bytes 1572872 | tf_op jit(solution)/shard_map/ppermute | solution.py:312
  59.4 3.6 %collective-permute-start.8 = (f32[192,128]{1,0:T(8,128)S(1)}, f32[192,128]{1,0:T(8,128)S(1)}, u32[]{:S(2)}, u32[]{:S(2)}) collective-permute-start(f32[192,128]{1,0:T(8,128)S(1)} %copy-done.18), channel_id=1, source_target_pairs={{0,2},{1,3},{2,0},{3,1},{4,6},{5,7},{6,4},{7,5},{8,10},{9,11},{10,... | collective-permute-start | bytes 294920 | tf_op jit(solution)/shard_map/ppermute | solution.py:312
  63.3 2.3 %project.4.refs_3_ = f32[512,768]{1,0:T(8,128)S(1)} custom-call(s32[1]{0:T(128)} %constant.140.clone.1.ids_ref, bf16[256,1024]{1,0:T(8,128)(2,1)} %collective-permute-done.refs_0_, bf16[256,1024]{1,0:T(8,128)(2,1)} %collective-permute-done.1.refs_1_, bf16[6,1024,128]{2,1,0:T(8,128)(2,1)S(1)} %copy-done.6, f32[512,768]{1,0:T(8,128)S(1)} %project.3.refs_3_), custom_call_target="tpu_custom_call" | custom-call | bytes 12582912 | tf_op jit(solution)/shard_map/project/pallas_call | solution.py:26
  66.7 10.5 %all_gather.27.refs_3_ = bf16[4,64,1024]{2,1,0:T(8,128)(2,1)} all-gather(bf16[1,64,1024]{2,1,0:T(8,128)(2,1)S(1)} %copy-done.22), channel_id=1, replica_groups=mesh['groups'=2,'dp'=4,'tensor'=4] {'dp'}, dimensions={0}, use_global_device_ids=true | all-gather | bytes 655360 | tf_op jit(solution)/shard_map/all_gather | solution.py:382
  77.2 6.3 %all-gather.1 = bf16[128,1024]{1,0:T(8,128)(2,1)} all-gather(bf16[32,1024]{1,0:T(8,128)(2,1)S(1)} %copy-done.21), channel_id=3, replica_groups=mesh['groups'=2,'dp'=4,'tensor'=4] {'dp'}, dimensions={0}, use_global_device_ids=true | all-gather | bytes 327680 | tf_op jit(solution)/shard_map/all_gather | solution.py:383
  84.6 2.2 %collective-permute-done.8 = f32[192,128]{1,0:T(8,128)S(1)} collective-permute-done((f32[192,128]{1,0:T(8,128)S(1)}, f32[192,128]{1,0:T(8,128)S(1)}, u32[]{:S(2)}, u32[]{:S(2)}) %collective-permute-start.8) | collective-permute-done | bytes 98336 | tf_op jit(solution)/shard_map/ppermute | solution.py:312
  88.5 3.0 %collective-permute-start.13 = (bf16[256,1024]{1,0:T(8,128)(2,1)}, bf16[256,1024]{1,0:T(8,128)(2,1)}, u32[]{:S(2)}, u32[]{:S(2)}) collective-permute-start(bf16[256,1024]{1,0:T(8,128)(2,1)} %collective-permute-done.5.refs_0_), channel_id=1, source_target_pairs={{0,1},{1,2},{2,3},{3,0},{4,5},{5,6},{6,7},{7,4},{8,9},{9,10},{10,1... | collective-permute-start | bytes 1572872 | tf_op jit(solution)/shard_map/ppermute | solution.py:312
  91.4 6.5 %all-gather.8.cloned.1.call-done = bf16[24,96,1024]{2,1,0:T(8,128)(2,1)} async-done(((bf16[3,96,1024]{2,1,0:T(8,128)(2,1)}), bf16[24,96,1024]{2,1,0:T(8,128)(2,1)}) %all-gather.8.cloned.1.call-update) | async-done | bytes 4718608 | tf_op jit(solution)/shard_map/all_gather | solution.py:379
  98.0 4.4 %slice_bitcast_fusion = (bf16[8,96,1024]{2,1,0:T(8,128)(2,1)}, bf16[8,96,1024]{2,1,0:T(8,128)(2,1)S(1)}, bf16[8,96,1024]{2,1,0:T(8,128)(2,1)S(1)}) fusion(bf16[8,3,96,1024]{3,2,1,0:T(8,128)(2,1)} %bitcast.65), kind=kLoop, calls=%fused_computation | loop fusion | bytes 9437184 | tf_op jit(solution)/shard_map/squeeze | solution.py:388
  102.4 1.9 %collective-permute-done.13.refs_4_ = bf16[256,1024]{1,0:T(8,128)(2,1)} collective-permute-done((bf16[256,1024]{1,0:T(8,128)(2,1)}, bf16[256,1024]{1,0:T(8,128)(2,1)}, u32[]{:S(2)}, u32[]{:S(2)}) %collective-permute-start.13) | collective-permute-done | bytes 524320 | tf_op jit(solution)/shard_map/ppermute | solution.py:312
  105.5 3.3 %collective-permute-start.11 = (bf16[192,128]{1,0:T(8,128)(2,1)S(1)}, bf16[192,128]{1,0:T(8,128)(2,1)S(1)}, u32[]{:S(2)}, u32[]{:S(2)}) collective-permute-start(bf16[192,128]{1,0:T(8,128)(2,1)S(1)} %add_convert_fusion.refs_0_), channel_id=1, source_target_pairs={{0,2},{1,3},{2,0},{3,1},{4,6},{5,7},{6,4},{7,5},{8,10},{9,11},{10,... | collective-permute-start | bytes 147464 | tf_op jit(solution)/shard_map/ppermute | solution.py:312
  113.9 2.4 %project.5.refs_6_ = f32[512,768]{1,0:T(8,128)S(1)} custom-call(s32[1]{0:T(128)} %constant.140.clone.1.ids_ref, bf16[256,1024]{1,0:T(8,128)(2,1)} %collective-permute-done.5.refs_0_, bf16[256,1024]{1,0:T(8,128)(2,1)} %collective-permute-done.6.refs_1_, bf16[6,1024,128]{2,1,0:T(8,128)(2,1)S(1)} %copy-done.5, f32[512,768]{1,0:T(8,128)S(1)} %copy-done.4), custom_call_target="tpu_custom_call" | custom-call | bytes 12582912 | tf_op jit(solution)/shard_map/project/pallas_call | solution.py:26
  116.3 4.5 %collective-permute-done.10.refs_1_ = bf16[192,128]{1,0:T(8,128)(2,1)S(1)} collective-permute-done((bf16[192,128]{1,0:T(8,128)(2,1)S(1)}, bf16[192,128]{1,0:T(8,128)(2,1)S(1)}, u32[]{:S(2)}, u32[]{:S(2)}) %collective-permute-start.10) | collective-permute-done | bytes 49184 | tf_op jit(solution)/shard_map/ppermute | solution.py:312
  121.9 4.2 %attend.2 = (bf16[256,512]{1,0:T(8,128)(2,1)S(1)}, bf16[256,128]{1,0:T(8,128)(2,1)S(1)}, bf16[256,128]{1,0:T(8,128)(2,1)S(1)}) custom-call(s32[8]{0:T(128)S(1)} %copy-done.14, s32[512,2]{1,0:T(8,128)S(1)} %copy.47.table_ref.refs_2_, f32[512,256]{1,0:T(8,128)S(1)} %copy-done.8, bf16[4,6,64,128]{3,2,1,0:T(8,128)(2,1)S(1)} %bitcast.61, ...), custom_call_target="tpu_custom_call" | custom-call | bytes 14364672 | tf_op jit(solution)/shard_map/attend/pallas_call | solution.py:26
  126.1 1.7 collective-permute-start.15
  128.9 7.2 %collective-permute-done.15.attended_ref = bf16[256,512]{1,0:T(8,128)(2,1)S(1)} collective-permute-done((bf16[256,512]{1,0:T(8,128)(2,1)S(1)}, bf16[256,512]{1,0:T(8,128)(2,1)S(1)}, u32[]{:S(2)}, u32[]{:S(2)}) %collective-permute-start.15) | collective-permute-done | bytes 262176 | tf_op jit(solution)/shard_map/ppermute | solution.py:312
  136.1 4.9 %attend.3 = (bf16[256,512]{1,0:T(8,128)(2,1)S(1)}, bf16[256,128]{1,0:T(8,128)(2,1)}, bf16[256,128]{1,0:T(8,128)(2,1)}) custom-call(s32[8]{0:T(128)S(1)} %copy-done.14, s32[512,2]{1,0:T(8,128)S(1)} %copy.47.table_ref.refs_2_, f32[512,256]{1,0:T(8,128)S(1)} %copy-done.8, bf16[4,6,64,128]{3,2,1,0:T(8,128)(2,1)S(1)} %bitcast.62, ...), custom_call_target="tpu_custom_call" | custom-call | bytes 14757888 | tf_op jit(solution)/shard_map/attend/pallas_call | solution.py:26
  142.2 3.5 %collective-permute-done.17.attended_ref = bf16[256,512]{1,0:T(8,128)(2,1)S(1)} collective-permute-done((bf16[256,512]{1,0:T(8,128)(2,1)S(1)}, bf16[256,512]{1,0:T(8,128)(2,1)S(1)}, u32[]{:S(2)}, u32[]{:S(2)}) %collective-permute-start.17) | collective-permute-done | bytes 262176 | tf_op jit(solution)/shard_map/ppermute | solution.py:312
  146.8 5.2 %collective-permute-done.16.attended_ref = bf16[256,512]{1,0:T(8,128)(2,1)S(1)} collective-permute-done((bf16[256,512]{1,0:T(8,128)(2,1)S(1)}, bf16[256,512]{1,0:T(8,128)(2,1)S(1)}, u32[]{:S(2)}, u32[]{:S(2)}) %collective-permute-start.16) | collective-permute-done | bytes 262176 | tf_op jit(solution)/shard_map/ppermute | solution.py:312
  153.1 4.5 %collective-permute-done.19.attended_ref = bf16[256,512]{1,0:T(8,128)(2,1)S(1)} collective-permute-done((bf16[256,512]{1,0:T(8,128)(2,1)S(1)}, bf16[256,512]{1,0:T(8,128)(2,1)S(1)}, u32[]{:S(2)}, u32[]{:S(2)}) %collective-permute-start.19) | collective-permute-done | bytes 262176 | tf_op jit(solution)/shard_map/ppermute | solution.py:312
  157.6 4.3 %collective-permute-done.18.attended_ref = bf16[256,512]{1,0:T(8,128)(2,1)S(1)} collective-permute-done((bf16[256,512]{1,0:T(8,128)(2,1)S(1)}, bf16[256,512]{1,0:T(8,128)(2,1)S(1)}, u32[]{:S(2)}, u32[]{:S(2)}) %collective-permute-start.18) | collective-permute-done | bytes 262176 | tf_op jit(solution)/shard_map/ppermute | solution.py:312
  165.8 5.0 %collective-permute-done.20.attended_ref = bf16[256,512]{1,0:T(8,128)(2,1)S(1)} collective-permute-done((bf16[256,512]{1,0:T(8,128)(2,1)S(1)}, bf16[256,512]{1,0:T(8,128)(2,1)S(1)}, u32[]{:S(2)}, u32[]{:S(2)}) %collective-permute-start.20) | collective-permute-done | bytes 262176 | tf_op jit(solution)/shard_map/ppermute | solution.py:312
  170.8 2.3 %project_out.15 = bf16[512,1024]{1,0:T(8,128)(2,1)} custom-call(s32[5]{0:T(128)S(1)} %pad_add_fusion.1.ids_ref, bf16[256,512]{1,0:T(8,128)(2,1)S(1)} %collective-permute-done.20.attended_ref, bf16[8,96,1024]{2,1,0:T(8,128)(2,1)S(1)} %copy-done, bf16[8,96,1024]{2,1,0:T(8,128)(2,1)S(1)} %copy-done, f32[256,1024]{1,0:T(8,128)S(1)} %get-tuple-element.106.refs_0_, ...), custom_call_target="tpu_custom_call" | custom-call | bytes 17313792 | tf_op jit(solution)/shard_map/project_out/pallas_call | solution.py:26
  (134 shorter events, 36.0 us)
Async XLA Ops:
  6.5 36.5 %all-gather.6.cloned.1.call-start = ((), (), s32[]{:S(2)}) async-start(), calls=%async_computation | async-start | bytes 1966080 | tf_op jit(solution)/shard_map/all_gather | solution.py:315
  9.6 13.3 %copy-start.32 = (s32[1,4]{1,0:T(1,128)S(1)}, s32[1,4]{1,0:T(1,128)}, u32[]{:S(2)}) copy-start(s32[1,4]{1,0:T(1,128)} %param.17) | copy-start | bytes 52
  9.6 13.5 %copy-start.33 = (s32[1,4]{1,0:T(1,128)S(1)}, s32[1,4]{1,0:T(1,128)}, u32[]{:S(2)}) copy-start(s32[1,4]{1,0:T(1,128)} %param.16) | copy-start | bytes 52
  10.5 39.9 %collective-permute-start.2 = (bf16[96,1024]{1,0:T(8,128)(2,1)}, bf16[96,1024]{1,0:T(8,128)(2,1)}, u32[]{:S(2)}, u32[]{:S(2)}) collective-permute-start(bf16[96,1024]{1,0:T(8,128)(2,1)} %get-tuple-element.125), channel_id=1, source_target_pairs={{0,1},{1,2},{2,3},{3,0},{4,5},{5,6},{6,7},{7,4},{8,9},{9,10},{10,1... | collective-permute-start | bytes 589832 | tf_op jit(solution)/shard_map/ppermute | solution.py:312
  13.5 36.9 %collective-permute-start.3 = (bf16[96,1024]{1,0:T(8,128)(2,1)}, bf16[96,1024]{1,0:T(8,128)(2,1)}, u32[]{:S(2)}, u32[]{:S(2)}) collective-permute-start(bf16[96,1024]{1,0:T(8,128)(2,1)} %get-tuple-element.124), channel_id=1, source_target_pairs={{0,2},{1,3},{2,0},{3,1},{4,6},{5,7},{6,4},{7,5},{8,10},{9,11},{10,... | collective-permute-start | bytes 589832 | tf_op jit(solution)/shard_map/ppermute | solution.py:312
  16.1 34.3 %collective-permute-start.4 = (bf16[96,1024]{1,0:T(8,128)(2,1)}, bf16[96,1024]{1,0:T(8,128)(2,1)}, u32[]{:S(2)}, u32[]{:S(2)}) collective-permute-start(bf16[96,1024]{1,0:T(8,128)(2,1)} %get-tuple-element.123), channel_id=1, source_target_pairs={{0,3},{1,0},{2,1},{3,2},{4,7},{5,4},{6,5},{7,6},{8,11},{9,8},{10,9... | collective-permute-start | bytes 589832 | tf_op jit(solution)/shard_map/ppermute | solution.py:312
  17.5 80.5 %all-gather.8.cloned.1.call-start = ((), (), s32[]{:S(2)}) async-start(), calls=%async_computation.1 | async-start | bytes 5308416 | tf_op jit(solution)/shard_map/all_gather | solution.py:379
  18.6 31.8 %collective-permute-start = (bf16[256,1024]{1,0:T(8,128)(2,1)}, bf16[256,1024]{1,0:T(8,128)(2,1)}, u32[]{:S(2)}, u32[]{:S(2)}) collective-permute-start(bf16[256,1024]{1,0:T(8,128)(2,1)} %get-tuple-element.122.refs_0_), channel_id=1, source_target_pairs={{0,1},{1,2},{2,3},{3,0},{4,5},{5,6},{6,7},{7,4},{8,9},{9,10},{10,1... | collective-permute-start | bytes 1572872 | tf_op jit(solution)/shard_map/ppermute | solution.py:312
  19.3 32.5 %collective-permute-start.1 = (bf16[256,1024]{1,0:T(8,128)(2,1)}, bf16[256,1024]{1,0:T(8,128)(2,1)}, u32[]{:S(2)}, u32[]{:S(2)}) collective-permute-start(bf16[256,1024]{1,0:T(8,128)(2,1)} %get-tuple-element.121.refs_1_), channel_id=1, source_target_pairs={{0,1},{1,2},{2,3},{3,0},{4,5},{5,6},{6,7},{7,4},{8,9},{9,10},{10,1... | collective-permute-start | bytes 1572872 | tf_op jit(solution)/shard_map/ppermute | solution.py:312
  23.3 9.0 %copy-start.29 = (s32[512,2]{0,1:T(2,128)}, s32[512,2]{0,1:T(2,128)S(1)}, u32[]{:S(2)}) copy-start(s32[512,2]{0,1:T(2,128)S(1)} %select_reduce_fusion) | copy-start | bytes 12292
  50.4 12.9 %copy-start.6 = (bf16[6,1024,128]{2,1,0:T(8,128)(2,1)S(1)}, bf16[6,1024,128]{2,1,0:T(8,128)(2,1)}, u32[]{:S(2)}) copy-start(bf16[6,1024,128]{2,1,0:T(8,128)(2,1)} %get-tuple-element.67.refs_2_) | copy-start | bytes 4718596
  50.4 9.1 %copy-start.18 = (f32[192,128]{1,0:T(8,128)S(1)}, f32[192,128]{1,0:T(8,128)}, u32[]{:S(2)}) copy-start(f32[192,128]{1,0:T(8,128)} %copy-done.17) | copy-start | bytes 294916
  50.4 12.7 %copy-start.16 = (f32[192,128]{1,0:T(8,128)S(1)}, f32[192,128]{1,0:T(8,128)}, u32[]{:S(2)}) copy-start(f32[192,128]{1,0:T(8,128)} %copy-done.15) | copy-start | bytes 294916
  53.9 12.7 %copy-start.22 = (bf16[1,64,1024]{2,1,0:T(8,128)(2,1)S(1)}, bf16[1,64,1024]{2,1,0:T(8,128)(2,1)}, u32[]{:S(2)}) copy-start(bf16[1,64,1024]{2,1,0:T(8,128)(2,1)} %param.15) | copy-start | bytes 393220
  54.0 23.2 %copy-start.21 = (bf16[32,1024]{1,0:T(8,128)(2,1)S(1)}, bf16[32,1024]{1,0:T(8,128)(2,1)}, u32[]{:S(2)}) copy-start(bf16[32,1024]{1,0:T(8,128)(2,1)} %copy-done.20) | copy-start | bytes 196612
  54.0 33.9 %collective-permute-start.5 = (bf16[256,1024]{1,0:T(8,128)(2,1)}, bf16[256,1024]{1,0:T(8,128)(2,1)}, u32[]{:S(2)}, u32[]{:S(2)}) collective-permute-start(bf16[256,1024]{1,0:T(8,128)(2,1)} %collective-permute-done.refs_0_), channel_id=1, source_target_pairs={{0,1},{1,2},{2,3},{3,0},{4,5},{5,6},{6,7},{7,4},{8,9},{9,10},{10,1... | collective-permute-start | bytes 1572872 | tf_op jit(solution)/shard_map/ppermute | solution.py:312
  58.7 29.8 %collective-permute-start.6 = (bf16[256,1024]{1,0:T(8,128)(2,1)}, bf16[256,1024]{1,0:T(8,128)(2,1)}, u32[]{:S(2)}, u32[]{:S(2)}) collective-permute-start(bf16[256,1024]{1,0:T(8,128)(2,1)} %collective-permute-done.1.refs_1_), channel_id=1, source_target_pairs={{0,1},{1,2},{2,3},{3,0},{4,5},{5,6},{6,7},{7,4},{8,9},{9,10},{10,1... | collective-permute-start | bytes 1572872 | tf_op jit(solution)/shard_map/ppermute | solution.py:312
  59.4 25.2 %collective-permute-start.7 = (f32[192,128]{1,0:T(8,128)}, f32[192,128]{1,0:T(8,128)S(1)}, u32[]{:S(2)}, u32[]{:S(2)}) collective-permute-start(f32[192,128]{1,0:T(8,128)} %copy-done.19), channel_id=1, source_target_pairs={{0,1},{1,2},{2,3},{3,0},{4,5},{5,6},{6,7},{7,4},{8,9},{9,10},{10,1... | collective-permute-start | bytes 294920 | tf_op jit(solution)/shard_map/ppermute | solution.py:312
  59.4 27.3 %collective-permute-start.8 = (f32[192,128]{1,0:T(8,128)S(1)}, f32[192,128]{1,0:T(8,128)S(1)}, u32[]{:S(2)}, u32[]{:S(2)}) collective-permute-start(f32[192,128]{1,0:T(8,128)S(1)} %copy-done.18), channel_id=1, source_target_pairs={{0,2},{1,3},{2,0},{3,1},{4,6},{5,7},{6,4},{7,5},{8,10},{9,11},{10,... | collective-permute-start | bytes 294920 | tf_op jit(solution)/shard_map/ppermute | solution.py:312
  63.0 24.8 %collective-permute-start.9 = (f32[192,128]{1,0:T(8,128)S(1)}, f32[192,128]{1,0:T(8,128)S(1)}, u32[]{:S(2)}, u32[]{:S(2)}) collective-permute-start(f32[192,128]{1,0:T(8,128)S(1)} %copy-done.16), channel_id=1, source_target_pairs={{0,3},{1,0},{2,1},{3,2},{4,7},{5,4},{6,5},{7,6},{8,11},{9,8},{10,9... | collective-permute-start | bytes 294920 | tf_op jit(solution)/shard_map/ppermute | solution.py:312
  88.5 15.9 %collective-permute-start.13 = (bf16[256,1024]{1,0:T(8,128)(2,1)}, bf16[256,1024]{1,0:T(8,128)(2,1)}, u32[]{:S(2)}, u32[]{:S(2)}) collective-permute-start(bf16[256,1024]{1,0:T(8,128)(2,1)} %collective-permute-done.5.refs_0_), channel_id=1, source_target_pairs={{0,1},{1,2},{2,3},{3,0},{4,5},{5,6},{6,7},{7,4},{8,9},{9,10},{10,1... | collective-permute-start | bytes 1572872 | tf_op jit(solution)/shard_map/ppermute | solution.py:312
  98.0 11.7 %copy-start.31 = (s32[4]{0:T(128)S(1)}, s32[4]{0:T(128)}, u32[]{:S(2)}) copy-start(s32[4]{0:T(128)} %copy-done.30) | copy-start | bytes 52
  104.3 31.7 %collective-permute-start.14 = (bf16[256,1024]{1,0:T(8,128)(2,1)}, bf16[256,1024]{1,0:T(8,128)(2,1)}, u32[]{:S(2)}, u32[]{:S(2)}) collective-permute-start(bf16[256,1024]{1,0:T(8,128)(2,1)} %collective-permute-done.6.refs_1_), channel_id=1, source_target_pairs={{0,1},{1,2},{2,3},{3,0},{4,5},{5,6},{6,7},{7,4},{8,9},{9,10},{10,1... | collective-permute-start | bytes 1572872 | tf_op jit(solution)/shard_map/ppermute | solution.py:312
  104.4 16.4 %collective-permute-start.10 = (bf16[192,128]{1,0:T(8,128)(2,1)S(1)}, bf16[192,128]{1,0:T(8,128)(2,1)S(1)}, u32[]{:S(2)}, u32[]{:S(2)}) collective-permute-start(bf16[192,128]{1,0:T(8,128)(2,1)S(1)} %add_convert_fusion.refs_0_), channel_id=1, source_target_pairs={{0,1},{1,2},{2,3},{3,0},{4,5},{5,6},{6,7},{7,4},{8,9},{9,10},{10,1... | collective-permute-start | bytes 147464 | tf_op jit(solution)/shard_map/ppermute | solution.py:312
  105.5 16.3 %collective-permute-start.11 = (bf16[192,128]{1,0:T(8,128)(2,1)S(1)}, bf16[192,128]{1,0:T(8,128)(2,1)S(1)}, u32[]{:S(2)}, u32[]{:S(2)}) collective-permute-start(bf16[192,128]{1,0:T(8,128)(2,1)S(1)} %add_convert_fusion.refs_0_), channel_id=1, source_target_pairs={{0,2},{1,3},{2,0},{3,1},{4,6},{5,7},{6,4},{7,5},{8,10},{9,11},{10,... | collective-permute-start | bytes 147464 | tf_op jit(solution)/shard_map/ppermute | solution.py:312
  108.8 13.0 %collective-permute-start.12 = (bf16[192,128]{1,0:T(8,128)(2,1)S(1)}, bf16[192,128]{1,0:T(8,128)(2,1)}, u32[]{:S(2)}, u32[]{:S(2)}) collective-permute-start(bf16[192,128]{1,0:T(8,128)(2,1)S(1)} %add_convert_fusion.refs_0_), channel_id=1, source_target_pairs={{0,3},{1,0},{2,1},{3,2},{4,7},{5,4},{6,5},{7,6},{8,11},{9,8},{10,9... | collective-permute-start | bytes 147464 | tf_op jit(solution)/shard_map/ppermute | solution.py:312
  126.1 10.0 %collective-permute-start.15 = (bf16[256,512]{1,0:T(8,128)(2,1)S(1)}, bf16[256,512]{1,0:T(8,128)(2,1)S(1)}, u32[]{:S(2)}, u32[]{:S(2)}) collective-permute-start(bf16[256,512]{1,0:T(8,128)(2,1)S(1)} %get-tuple-element.90.attended_ref), channel_id=1, source_target_pairs={{0,1},{1,2},{2,3},{3,0},{4,5},{5,6},{6,7},{7,4},{8,9},{9,10},{10,1... | collective-permute-start | bytes 786440 | tf_op jit(solution)/shard_map/ppermute | solution.py:312
  136.0 9.7 %collective-permute-start.17 = (bf16[256,512]{1,0:T(8,128)(2,1)S(1)}, bf16[256,512]{1,0:T(8,128)(2,1)S(1)}, u32[]{:S(2)}, u32[]{:S(2)}) collective-permute-start(bf16[256,512]{1,0:T(8,128)(2,1)S(1)} %collective-permute-done.15.attended_ref), channel_id=1, source_target_pairs={{0,1},{1,2},{2,3},{3,0},{4,5},{5,6},{6,7},{7,4},{8,9},{9,10},{10,1... | collective-permute-start | bytes 786440 | tf_op jit(solution)/shard_map/ppermute | solution.py:312
  140.9 11.1 %collective-permute-start.16 = (bf16[256,512]{1,0:T(8,128)(2,1)S(1)}, bf16[256,512]{1,0:T(8,128)(2,1)S(1)}, u32[]{:S(2)}, u32[]{:S(2)}) collective-permute-start(bf16[256,512]{1,0:T(8,128)(2,1)S(1)} %get-tuple-element.91.attended_ref), channel_id=1, source_target_pairs={{0,1},{1,2},{2,3},{3,0},{4,5},{5,6},{6,7},{7,4},{8,9},{9,10},{10,1... | collective-permute-start | bytes 786440 | tf_op jit(solution)/shard_map/ppermute | solution.py:312
  145.7 11.9 %collective-permute-start.19 = (bf16[256,512]{1,0:T(8,128)(2,1)S(1)}, bf16[256,512]{1,0:T(8,128)(2,1)S(1)}, u32[]{:S(2)}, u32[]{:S(2)}) collective-permute-start(bf16[256,512]{1,0:T(8,128)(2,1)S(1)} %collective-permute-done.17.attended_ref), channel_id=1, source_target_pairs={{0,1},{1,2},{2,3},{3,0},{4,5},{5,6},{6,7},{7,4},{8,9},{9,10},{10,1... | collective-permute-start | bytes 786440 | tf_op jit(solution)/shard_map/ppermute | solution.py:312
  152.0 9.9 %collective-permute-start.18 = (bf16[256,512]{1,0:T(8,128)(2,1)S(1)}, bf16[256,512]{1,0:T(8,128)(2,1)S(1)}, u32[]{:S(2)}, u32[]{:S(2)}) collective-permute-start(bf16[256,512]{1,0:T(8,128)(2,1)S(1)} %collective-permute-done.16.attended_ref), channel_id=1, source_target_pairs={{0,1},{1,2},{2,3},{3,0},{4,5},{5,6},{6,7},{7,4},{8,9},{9,10},{10,1... | collective-permute-start | bytes 786440 | tf_op jit(solution)/shard_map/ppermute | solution.py:312
  162.0 8.8 %collective-permute-start.20 = (bf16[256,512]{1,0:T(8,128)(2,1)S(1)}, bf16[256,512]{1,0:T(8,128)(2,1)S(1)}, u32[]{:S(2)}, u32[]{:S(2)}) collective-permute-start(bf16[256,512]{1,0:T(8,128)(2,1)S(1)} %collective-permute-done.18.attended_ref), channel_id=1, source_target_pairs={{0,1},{1,2},{2,3},{3,0},{4,5},{5,6},{6,7},{7,4},{8,9},{9,10},{10,1... | collective-permute-start | bytes 786440 | tf_op jit(solution)/shard_map/ppermute | solution.py:312
  (25 other events, 84.3 us)
Sparse Core Ops, SparseCore 0:
  17.6 17.9 all-gather.5
  54.1 43.8 all-gather.7

commit v20 on v19

--- a/solution.py
+++ b/solution.py
@@ -390,7 +390,7 @@
             shrink, lines = side
         if last:
             part_weight = shard(step)
-            moved[1] = turned(after(moved[1], moved[0], *lines))
+            moved[1] = turned(after(moved[1], moved[0], *shrink))
             break
         done = lax.optimization_barrier((moved, begun, shard(step), side))
         moved, begun, part_weight, side = done
@@ -404,7 +404,8 @@
             planes_of, adapters, part, table, turn, up_all, shrink, moved[part], part_weight,
             begun, earlier,
         )
-        attended[part] = [made, turned(after(made, *attended[0][1:]))]
+        ahead = [attended[0][1], *lines] if part else []
+        attended[part] = [made, turned(after(made, *ahead))]
     sums = [
         project_out(ids, rank, attended[part][0], own_rows, own_down, [], []) for part in range(2)
     ]

time: 180 us -> 180 us (level)
  local copies, waits for them, and re-layouts: 28.3 us -> 36.8 us
  waiting for transfers between devices: 49.5 us -> 43 us
  blocking collectives: 23.9 us -> 20.8 us
    unnamed x70 -> x82, local copies, waits for them, and re-layouts: 10.2 us -> 17.8 us
    all_gather x1, waiting for transfers between devices: 6.54 us -> 0.01 us  [local(): lines = lax.all_gather(jnp.stack(lines), PLANE, axis=0)]
    all_gather x1, blocking collectives: 10.5 us -> 6.96 us  [local(): lax.all_gather(after(output_up_maps, sums[0]), 'dp', axis=0, tiled=True)]
  transfers between devices with their start and end apart: 23 -> 23, of which waited for: 14 -> 9; matrix products, arithmetic and copies ran while one was open for 10% -> 12% of each run, Pallas kernels for 15% -> 15%
where the time goes in v20:
time: 180 us; the launch traced here: 179 us
  waiting for transfers between devices  43 us (24%)
  local copies, waits for them, and re-layouts  36.8 us (20%)
  Pallas kernels  29.5 us (16%)
  starting transfers between devices  25.7 us (14%)
  blocking collectives  20.8 us (12%)
  between operations  16.5 us (9%)
  other arithmetic  6.82 us (4%)
    ppermute x21, waiting for transfers between devices, turned(): lax.ppermute(value, 'tensor', [(i, (i + turn) % planes) for i in range(pl...  43 us
    pallas_call x14, Pallas kernels, call(): pl.pallas_call(kernel, out_shape=out, grid_spec=pltpu.PrefetchScalarGridS...  29.5 us
    ppermute x21, starting transfers between devices, turned(): lax.ppermute(value, 'tensor', [(i, (i + turn) % planes) for i in range(pl...  25.7 us
    unnamed x82, local copies, waits for them, and re-layouts  17.8 us
    all_gather x1, blocking collectives, local(): lax.all_gather(jnp.transpose(adapter_up_maps[0], (1, 0, 2)), 'dp', axis=0)  7.06 us
    all_gather x1, blocking collectives, local(): lax.all_gather(after(output_up_maps, sums[0]), 'dp', axis=0, tiled=True)  6.96 us
    all_gather x1, blocking collectives, local(): lax.all_gather(after(out_down, sums[0]), 'dp', axis=0)  6.76 us
    dynamic_slice x1, local copies, waits for them, and re-layouts, shard(): return lax.dynamic_slice_in_dim(weight, start, depth, axis=1)  5.12 us
  transfers between devices with their start and end apart: 23, of which 9 were waited for; matrix products, arithmetic and copies ran while one was open for 12% of the time, Pallas kernels for 15%

profile of v20, /device:TPU:0, one launch (start us, length us, event | category | flops | bytes accessed | tf_op | source)
XLA Modules:
  0.0 179.2 jit_solution(4068969655742093542)
XLA Ops:
  6.5 2.1 %fusion.5 = (bf16[256,1024]{1,0:T(8,128)(2,1)S(1)}, bf16[256,1024]{1,0:T(8,128)(2,1)}) fusion(bf16[512,1024]{1,0:T(8,128)(2,1)} %token_ref.1), kind=kLoop, calls=%fused_computation.40 | loop fusion | bytes 2097152 | tf_op jit(solution)/shard_map/slice | solution.py:363
  8.6 3.0 %collective-permute-start = (bf16[256,1024]{1,0:T(8,128)(2,1)}, bf16[256,1024]{1,0:T(8,128)(2,1)}, u32[]{:S(2)}, u32[]{:S(2)}) collective-permute-start(bf16[256,1024]{1,0:T(8,128)(2,1)} %get-tuple-element.122.refs_0_), channel_id=1, source_target_pairs={{0,1},{1,2},{2,3},{3,0},{4,5},{5,6},{6,7},{7,4},{8,9},{9,10},{10,1... | collective-permute-start | bytes 1572872 | tf_op jit(solution)/shard_map/ppermute | solution.py:312
  13.5 2.8 %fusion.4 = (bf16[64,1,1024]{2,1,0:T(2,128)(2,1)S(1)}, bf16[64,1,1024]{2,1,0:T(2,128)(2,1)S(1)}, bf16[64,1,1024]{2,1,0:T(2,128)(2,1)S(1)}) fusion(bf16[128,4,4096]{2,1,0:T(4,128)(2,1)} %param.11, s32[]{:T(128)S(6)} %select_n.76, s32[]{:T(128)S(6)} %select_n.79, s32[]{:T(128)S(6)} %select_n.88, s32[]{:T(128)S(6)} %select_n.85, s32[]{:T(128)S(6)} %select_n.82), kind=kLoop, calls=%fused_computation.39 | loop fusion | bytes 786452 | tf_op jit(solution)/shard_map/dynamic_slice | solution.py:351
  27.5 2.6 %dynamic-slice_bitcast_fusion.4 = bf16[4,128,1024]{2,0,1:T(4,128)(2,1)} fusion(bf16[128,4,4096]{2,1,0:T(4,128)(2,1)} %param.11, s32[]{:T(128)S(6)} %select_n.91), kind=kLoop, calls=%fused_computation.7 | loop fusion | bytes 2097156 | tf_op jit(solution)/shard_map/transpose | solution.py:336
  30.1 5.1 %dynamic-slice_bitcast_fusion = (bf16[6,1024,128]{2,1,0:T(8,128)(2,1)S(1)}, bf16[6,1024,128]{2,1,0:T(8,128)(2,1)}, bf16[6,1024,128]{2,1,0:T(8,128)(2,1)}, bf16[6,1024,128]{2,1,0:T(8,128)(2,1)}) fusion(bf16[4096,6,128]{2,0,1:T(8,128)(2,1)} %param.10, s32[]{:T(128)S(6)} %select_n.94, s32[]{:T(128)S(6)} %select_n.92, s32[]{:T(128)S(6)} %select_n.89, s32[]{:T(128)S(6)} %select_n.93), kind=kLoop, calls=%fused_computation.3 | loop fusion | bytes 12582928 | tf_op jit(solution)/shard_map/dynamic_slice | solution.py:360
  37.1 2.0 %project.3.refs_3_ = f32[512,768]{1,0:T(8,128)S(1)} custom-call(s32[1]{0:T(128)} %constant.140.clone.1.ids_ref, bf16[256,1024]{1,0:T(8,128)(2,1)} %get-tuple-element.122.refs_0_, bf16[256,1024]{1,0:T(8,128)(2,1)S(1)} %get-tuple-element.121.refs_1_, bf16[6,1024,128]{2,1,0:T(8,128)(2,1)S(1)} %copy-done.4), custom_call_target="tpu_custom_call" | custom-call | bytes 7864320 | tf_op jit(solution)/shard_map/project/pallas_call | solution.py:26
  40.4 7.1 %all-gather = bf16[24,64,128]{2,1,0:T(8,128)(2,1)} all-gather(bf16[6,64,128]{2,1,0:T(8,128)(2,1)S(1)} %bitcast.69), channel_id=2, replica_groups=mesh['groups'=2,'dp'=4,'tensor'=4] {'dp'}, dimensions={0}, use_global_device_ids=true | all-gather | bytes 491520 | tf_op jit(solution)/shard_map/all_gather | solution.py:316
  50.1 3.4 %shrink.1 = (f32[192,128]{1,0:T(8,128)S(1)}, f32[192,128]{1,0:T(8,128)}, f32[192,128]{1,0:T(8,128)S(1)}, f32[192,128]{1,0:T(8,128)S(1)}) custom-call(s32[5]{0:T(128)S(1)} %pad_add_fusion.3.ids_ref, s32[512,2]{1,0:T(8,128)S(1)} %copy.42.table_ref, bf16[512,1024]{1,0:T(8,128)(2,1)S(1)} %copy-done.8, bf16[4,192,1024]{2,1,0:T(8,128)(2,1)S(1)} %copy-done.12), custom_call_target="tpu_custom_call" | custom-call | bytes 7876608 | tf_op jit(solution)/shard_map/shrink/pallas_call | solution.py:26
  54.1 2.0 %pad_maximum_fusion = bf16[3,96,1024]{2,1,0:T(8,128)(2,1)} fusion(bf16[1,96,1024]{2,1,0:T(8,128)(2,1)} %bitcast.26, bf16[1,96,1024]{2,1,0:T(8,128)(2,1)} %bitcast.25, bf16[1,96,1024]{2,1,0:T(8,128)(2,1)} %bitcast.24), kind=kLoop, calls=%fused_computation.8 | loop fusion | flops 589824 | bytes 1179648 | tf_op jit(solution)/shard_map/stack | solution.py:379
  59.2 2.2 %collective-permute-start.8 = (f32[192,128]{1,0:T(8,128)S(1)}, f32[192,128]{1,0:T(8,128)S(1)}, u32[]{:S(2)}, u32[]{:S(2)}) collective-permute-start(f32[192,128]{1,0:T(8,128)S(1)} %copy-done.31), channel_id=1, source_target_pairs={{0,2},{1,3},{2,0},{3,1},{4,6},{5,7},{6,4},{7,5},{8,10},{9,11},{10,... | collective-permute-start | bytes 294920 | tf_op jit(solution)/shard_map/ppermute | solution.py:312
  61.3 2.2 %collective-permute-start.9 = (f32[192,128]{1,0:T(8,128)S(1)}, f32[192,128]{1,0:T(8,128)S(1)}, u32[]{:S(2)}, u32[]{:S(2)}) collective-permute-start(f32[192,128]{1,0:T(8,128)S(1)} %copy-done.29), channel_id=1, source_target_pairs={{0,3},{1,0},{2,1},{3,2},{4,7},{5,4},{6,5},{7,6},{8,11},{9,8},{10,9... | collective-permute-start | bytes 294920 | tf_op jit(solution)/shard_map/ppermute | solution.py:312
  66.5 2.2 %project.4.refs_3_ = f32[512,768]{1,0:T(8,128)S(1)} custom-call(s32[1]{0:T(128)} %constant.140.clone.1.ids_ref, bf16[256,1024]{1,0:T(8,128)(2,1)} %collective-permute-done.refs_0_, bf16[256,1024]{1,0:T(8,128)(2,1)} %collective-permute-done.1.refs_1_, bf16[6,1024,128]{2,1,0:T(8,128)(2,1)S(1)} %copy-done.6, f32[512,768]{1,0:T(8,128)S(1)} %copy-done.1), custom_call_target="tpu_custom_call" | custom-call | bytes 12582912 | tf_op jit(solution)/shard_map/project/pallas_call | solution.py:26
  69.9 7.0 %all_gather.27.refs_3_ = bf16[4,64,1024]{2,1,0:T(8,128)(2,1)S(1)} all-gather(bf16[1,64,1024]{2,1,0:T(8,128)(2,1)} %param.15), channel_id=1, replica_groups=mesh['groups'=2,'dp'=4,'tensor'=4] {'dp'}, dimensions={0}, use_global_device_ids=true | all-gather | bytes 655360 | tf_op jit(solution)/shard_map/all_gather | solution.py:382
  76.9 6.8 %all-gather.1 = bf16[128,1024]{1,0:T(8,128)(2,1)} all-gather(bf16[32,1024]{1,0:T(8,128)(2,1)S(1)} %copy-done.33), channel_id=3, replica_groups=mesh['groups'=2,'dp'=4,'tensor'=4] {'dp'}, dimensions={0}, use_global_device_ids=true | all-gather | bytes 327680 | tf_op jit(solution)/shard_map/all_gather | solution.py:383
  83.6 2.8 %collective-permute-done.7 = f32[192,128]{1,0:T(8,128)S(1)} collective-permute-done((f32[192,128]{1,0:T(8,128)}, f32[192,128]{1,0:T(8,128)S(1)}, u32[]{:S(2)}, u32[]{:S(2)}) %collective-permute-start.7) | collective-permute-done | bytes 98336 | tf_op jit(solution)/shard_map/ppermute | solution.py:312
  86.4 3.6 %collective-permute-done.8 = f32[192,128]{1,0:T(8,128)S(1)} collective-permute-done((f32[192,128]{1,0:T(8,128)S(1)}, f32[192,128]{1,0:T(8,128)S(1)}, u32[]{:S(2)}, u32[]{:S(2)}) %collective-permute-start.8) | collective-permute-done | bytes 98336 | tf_op jit(solution)/shard_map/ppermute | solution.py:312
  90.1 2.6 %collective-permute-start.13 = (bf16[256,1024]{1,0:T(8,128)(2,1)S(1)}, bf16[256,1024]{1,0:T(8,128)(2,1)S(1)}, u32[]{:S(2)}, u32[]{:S(2)}) collective-permute-start(bf16[256,1024]{1,0:T(8,128)(2,1)S(1)} %collective-permute-done.5.refs_0_), channel_id=1, source_target_pairs={{0,1},{1,2},{2,3},{3,0},{4,5},{5,6},{6,7},{7,4},{8,9},{9,10},{10,1... | collective-permute-start | bytes 1572872 | tf_op jit(solution)/shard_map/ppermute | solution.py:312
  93.6 1.9 %collective-permute-start.11 = (bf16[192,128]{1,0:T(8,128)(2,1)S(1)}, bf16[192,128]{1,0:T(8,128)(2,1)S(1)}, u32[]{:S(2)}, u32[]{:S(2)}) collective-permute-start(bf16[192,128]{1,0:T(8,128)(2,1)S(1)} %add_convert_fusion.refs_0_), channel_id=1, source_target_pairs={{0,2},{1,3},{2,0},{3,1},{4,6},{5,7},{6,4},{7,5},{8,10},{9,11},{10,... | collective-permute-start | bytes 147464 | tf_op jit(solution)/shard_map/ppermute | solution.py:312
  95.4 2.0 %collective-permute-start.12 = (bf16[192,128]{1,0:T(8,128)(2,1)S(1)}, bf16[192,128]{1,0:T(8,128)(2,1)S(1)}, u32[]{:S(2)}, u32[]{:S(2)}) collective-permute-start(bf16[192,128]{1,0:T(8,128)(2,1)S(1)} %add_convert_fusion.refs_0_), channel_id=1, source_target_pairs={{0,3},{1,0},{2,1},{3,2},{4,7},{5,4},{6,5},{7,6},{8,11},{9,8},{10,9... | collective-permute-start | bytes 147464 | tf_op jit(solution)/shard_map/ppermute | solution.py:312
  97.4 10.6 %collective-permute-done.10.refs_1_ = bf16[192,128]{1,0:T(8,128)(2,1)S(1)} collective-permute-done((bf16[192,128]{1,0:T(8,128)(2,1)S(1)}, bf16[192,128]{1,0:T(8,128)(2,1)S(1)}, u32[]{:S(2)}, u32[]{:S(2)}) %collective-permute-start.10) | collective-permute-done | bytes 49184 | tf_op jit(solution)/shard_map/ppermute | solution.py:312
  117.9 2.1 %project.5.refs_6_ = f32[512,768]{1,0:T(8,128)S(1)} custom-call(s32[1]{0:T(128)} %constant.140.clone.1.ids_ref, bf16[256,1024]{1,0:T(8,128)(2,1)S(1)} %copy-done.16, bf16[256,1024]{1,0:T(8,128)(2,1)} %collective-permute-done.6.refs_1_, bf16[6,1024,128]{2,1,0:T(8,128)(2,1)S(1)} %copy-done.5, f32[512,768]{1,0:T(8,128)S(1)} %copy-done.3), custom_call_target="tpu_custom_call" | custom-call | bytes 12582912 | tf_op jit(solution)/shard_map/project/pallas_call | solution.py:26
  120.1 3.1 %attend.2 = (bf16[256,512]{1,0:T(8,128)(2,1)S(1)}, bf16[256,128]{1,0:T(8,128)(2,1)S(1)}, bf16[256,128]{1,0:T(8,128)(2,1)S(1)}) custom-call(s32[8]{0:T(128)S(1)} %copy-done.27, s32[512,2]{1,0:T(8,128)S(1)} %copy.44.table_ref.refs_2_, f32[512,256]{1,0:T(8,128)S(1)} %copy-done.7, bf16[4,6,64,128]{3,2,1,0:T(8,128)(2,1)S(1)} %bitcast.61, ...), custom_call_target="tpu_custom_call" | custom-call | bytes 14364672 | tf_op jit(solution)/shard_map/attend/pallas_call | solution.py:26
  126.3 6.8 %collective-permute-done.15.attended_ref = bf16[256,512]{1,0:T(8,128)(2,1)} collective-permute-done((bf16[256,512]{1,0:T(8,128)(2,1)S(1)}, bf16[256,512]{1,0:T(8,128)(2,1)}, u32[]{:S(2)}, u32[]{:S(2)}) %collective-permute-start.15) | collective-permute-done | bytes 262176 | tf_op jit(solution)/shard_map/ppermute | solution.py:312
  133.1 4.8 %attend.3 = (bf16[256,512]{1,0:T(8,128)(2,1)S(1)}, bf16[256,128]{1,0:T(8,128)(2,1)}, bf16[256,128]{1,0:T(8,128)(2,1)}) custom-call(s32[8]{0:T(128)S(1)} %copy-done.27, s32[512,2]{1,0:T(8,128)S(1)} %copy.44.table_ref.refs_2_, f32[512,256]{1,0:T(8,128)S(1)} %copy-done.7, bf16[4,6,64,128]{3,2,1,0:T(8,128)(2,1)S(1)} %bitcast.62, ...), custom_call_target="tpu_custom_call" | custom-call | bytes 14757888 | tf_op jit(solution)/shard_map/attend/pallas_call | solution.py:26
  138.7 3.0 %slice_bitcast_fusion = (bf16[8,96,1024]{2,1,0:T(8,128)(2,1)S(1)}, bf16[8,96,1024]{2,1,0:T(8,128)(2,1)S(1)}, bf16[8,96,1024]{2,1,0:T(8,128)(2,1)S(1)}) fusion(bf16[8,3,96,1024]{3,2,1,0:T(8,128)(2,1)} %bitcast.65), kind=kLoop, calls=%fused_computation | loop fusion | bytes 9437184 | tf_op jit(solution)/shard_map/squeeze | solution.py:388
  143.0 2.0 %project_out.10 = (f32[256,1024]{1,0:T(8,128)S(1)}, f32[256,256]{1,0:T(8,128)S(1)}) custom-call(s32[5]{0:T(128)S(1)} %copy-done.26, bf16[256,512]{1,0:T(8,128)(2,1)} %collective-permute-done.15.attended_ref, bf16[8,96,1024]{2,1,0:T(8,128)(2,1)S(1)} %get-tuple-element.117.w_ref.down_ref, bf16[8,96,1024]{2,1,0:T(8,128)(2,1)S(1)} %get-tuple-element.117.w_ref.down_ref, ...), custom_call_target="tpu_custom_call" | custom-call | bytes 14155776 | tf_op jit(solution)/shard_map/project_out/pallas_call | solution.py:26
  146.5 6.2 %collective-permute-done.16.attended_ref = bf16[256,512]{1,0:T(8,128)(2,1)S(1)} collective-permute-done((bf16[256,512]{1,0:T(8,128)(2,1)S(1)}, bf16[256,512]{1,0:T(8,128)(2,1)S(1)}, u32[]{:S(2)}, u32[]{:S(2)}) %collective-permute-start.16) | collective-permute-done | bytes 262176 | tf_op jit(solution)/shard_map/ppermute | solution.py:312
  153.8 4.5 %collective-permute-done.19.attended_ref = bf16[256,512]{1,0:T(8,128)(2,1)S(1)} collective-permute-done((bf16[256,512]{1,0:T(8,128)(2,1)}, bf16[256,512]{1,0:T(8,128)(2,1)S(1)}, u32[]{:S(2)}, u32[]{:S(2)}) %collective-permute-start.19) | collective-permute-done | bytes 262176 | tf_op jit(solution)/shard_map/ppermute | solution.py:312
  158.4 3.5 %collective-permute-done.18.attended_ref = bf16[256,512]{1,0:T(8,128)(2,1)S(1)} collective-permute-done((bf16[256,512]{1,0:T(8,128)(2,1)S(1)}, bf16[256,512]{1,0:T(8,128)(2,1)S(1)}, u32[]{:S(2)}, u32[]{:S(2)}) %collective-permute-start.18) | collective-permute-done | bytes 262176 | tf_op jit(solution)/shard_map/ppermute | solution.py:312
  161.9 2.0 %project_out.13 = (f32[256,1024]{1,0:T(8,128)S(1)}, f32[256,256]{1,0:T(8,128)S(1)}) custom-call(s32[5]{0:T(128)S(1)} %copy-done.26, bf16[256,512]{1,0:T(8,128)(2,1)} %collective-permute-done.17.attended_ref, bf16[8,96,1024]{2,1,0:T(8,128)(2,1)S(1)} %get-tuple-element.116.w_ref.down_ref, bf16[8,96,1024]{2,1,0:T(8,128)(2,1)S(1)} %get-tuple-element.116.w_ref.down_ref, ...), custom_call_target="tpu_custom_call" | custom-call | bytes 14155776 | tf_op jit(solution)/shard_map/project_out/pallas_call | solution.py:26
  166.3 3.8 %collective-permute-done.20.attended_ref = bf16[256,512]{1,0:T(8,128)(2,1)S(1)} collective-permute-done((bf16[256,512]{1,0:T(8,128)(2,1)S(1)}, bf16[256,512]{1,0:T(8,128)(2,1)S(1)}, u32[]{:S(2)}, u32[]{:S(2)}) %collective-permute-start.20) | collective-permute-done | bytes 262176 | tf_op jit(solution)/shard_map/ppermute | solution.py:312
  170.1 2.3 %project_out.15 = bf16[512,1024]{1,0:T(8,128)(2,1)} custom-call(s32[5]{0:T(128)S(1)} %copy-done.26, bf16[256,512]{1,0:T(8,128)(2,1)S(1)} %collective-permute-done.20.attended_ref, bf16[8,96,1024]{2,1,0:T(8,128)(2,1)S(1)} %get-tuple-element.115.w_ref.down_ref, bf16[8,96,1024]{2,1,0:T(8,128)(2,1)S(1)} %get-tuple-element.115.w_ref.down_ref, ...), custom_call_target="tpu_custom_call" | custom-call | bytes 17313792 | tf_op jit(solution)/shard_map/project_out/pallas_call | solution.py:26
  (146 shorter events, 44.6 us)
Async XLA Ops:
  6.5 6.8 %copy-start.35 = (bf16[1,64,4,128]{3,2,1,0:T(4,128)(2,1)S(1)}, bf16[1,64,4,128]{3,2,1,0:T(4,128)(2,1)}, u32[]{:S(2)}) copy-start(bf16[1,64,4,128]{3,2,1,0:T(4,128)(2,1)} %param.14) | copy-start | bytes 196612
  6.5 40.9 %all-gather.6.cloned.1.call-start = ((), (), s32[]{:S(2)}) async-start(), calls=%async_computation | async-start | bytes 1966080 | tf_op jit(solution)/shard_map/all_gather | solution.py:315
  8.6 44.8 %collective-permute-start = (bf16[256,1024]{1,0:T(8,128)(2,1)}, bf16[256,1024]{1,0:T(8,128)(2,1)}, u32[]{:S(2)}, u32[]{:S(2)}) collective-permute-start(bf16[256,1024]{1,0:T(8,128)(2,1)} %get-tuple-element.122.refs_0_), channel_id=1, source_target_pairs={{0,1},{1,2},{2,3},{3,0},{4,5},{5,6},{6,7},{7,4},{8,9},{9,10},{10,1... | collective-permute-start | bytes 1572872 | tf_op jit(solution)/shard_map/ppermute | solution.py:312
  11.7 41.8 %collective-permute-start.1 = (bf16[256,1024]{1,0:T(8,128)(2,1)S(1)}, bf16[256,1024]{1,0:T(8,128)(2,1)}, u32[]{:S(2)}, u32[]{:S(2)}) collective-permute-start(bf16[256,1024]{1,0:T(8,128)(2,1)S(1)} %get-tuple-element.121.refs_1_), channel_id=1, source_target_pairs={{0,1},{1,2},{2,3},{3,0},{4,5},{5,6},{6,7},{7,4},{8,9},{9,10},{10,1... | collective-permute-start | bytes 1572872 | tf_op jit(solution)/shard_map/ppermute | solution.py:312
  13.3 125.4 %all-gather.8.cloned.1.call-start = ((), (), s32[]{:S(2)}) async-start(), calls=%async_computation.1 | async-start | bytes 5308416 | tf_op jit(solution)/shard_map/all_gather | solution.py:379
  16.3 8.7 %copy-start.38 = (s32[1,4]{1,0:T(1,128)S(1)}, s32[1,4]{1,0:T(1,128)}, u32[]{:S(2)}) copy-start(s32[1,4]{1,0:T(1,128)} %param.17) | copy-start | bytes 52
  16.3 8.9 %copy-start.39 = (s32[1,4]{1,0:T(1,128)S(1)}, s32[1,4]{1,0:T(1,128)}, u32[]{:S(2)}) copy-start(s32[1,4]{1,0:T(1,128)} %param.16) | copy-start | bytes 52
  16.4 11.1 %copy-start.32 = (bf16[32,1024]{1,0:T(8,128)(2,1)}, bf16[32,1024]{1,0:T(8,128)(2,1)S(1)}, u32[]{:S(2)}) copy-start(bf16[32,1024]{1,0:T(8,128)(2,1)S(1)} %bitcast_dynamic-update-slice_fusion) | copy-start | bytes 196612
  17.4 36.0 %collective-permute-start.2 = (bf16[96,1024]{1,0:T(8,128)(2,1)}, bf16[96,1024]{1,0:T(8,128)(2,1)}, u32[]{:S(2)}, u32[]{:S(2)}) collective-permute-start(bf16[96,1024]{1,0:T(8,128)(2,1)} %get-tuple-element.125), channel_id=1, source_target_pairs={{0,1},{1,2},{2,3},{3,0},{4,5},{5,6},{6,7},{7,4},{8,9},{9,10},{10,1... | collective-permute-start | bytes 589832 | tf_op jit(solution)/shard_map/ppermute | solution.py:312
  19.0 34.5 %collective-permute-start.3 = (bf16[96,1024]{1,0:T(8,128)(2,1)}, bf16[96,1024]{1,0:T(8,128)(2,1)}, u32[]{:S(2)}, u32[]{:S(2)}) collective-permute-start(bf16[96,1024]{1,0:T(8,128)(2,1)} %get-tuple-element.124), channel_id=1, source_target_pairs={{0,2},{1,3},{2,0},{3,1},{4,6},{5,7},{6,4},{7,5},{8,10},{9,11},{10,... | collective-permute-start | bytes 589832 | tf_op jit(solution)/shard_map/ppermute | solution.py:312
  20.2 33.2 %collective-permute-start.4 = (bf16[96,1024]{1,0:T(8,128)(2,1)}, bf16[96,1024]{1,0:T(8,128)(2,1)}, u32[]{:S(2)}, u32[]{:S(2)}) collective-permute-start(bf16[96,1024]{1,0:T(8,128)(2,1)} %get-tuple-element.123), channel_id=1, source_target_pairs={{0,3},{1,0},{2,1},{3,2},{4,7},{5,4},{6,5},{7,6},{8,11},{9,8},{10,9... | collective-permute-start | bytes 589832 | tf_op jit(solution)/shard_map/ppermute | solution.py:312
  25.4 9.9 %copy-start.36 = (s32[512,2]{0,1:T(2,128)}, s32[512,2]{0,1:T(2,128)S(1)}, u32[]{:S(2)}) copy-start(s32[512,2]{0,1:T(2,128)S(1)} %select_reduce_fusion) | copy-start | bytes 12292
  54.1 7.2 %copy-start.29 = (f32[192,128]{1,0:T(8,128)S(1)}, f32[192,128]{1,0:T(8,128)}, u32[]{:S(2)}) copy-start(f32[192,128]{1,0:T(8,128)} %copy-done.28) | copy-start | bytes 294916
  54.1 5.1 %copy-start.31 = (f32[192,128]{1,0:T(8,128)S(1)}, f32[192,128]{1,0:T(8,128)}, u32[]{:S(2)}) copy-start(f32[192,128]{1,0:T(8,128)} %copy-done.30) | copy-start | bytes 294916
  56.1 20.7 %copy-start.33 = (bf16[32,1024]{1,0:T(8,128)(2,1)S(1)}, bf16[32,1024]{1,0:T(8,128)(2,1)}, u32[]{:S(2)}) copy-start(bf16[32,1024]{1,0:T(8,128)(2,1)} %copy-done.32) | copy-start | bytes 196612
  56.2 33.9 %collective-permute-start.5 = (bf16[256,1024]{1,0:T(8,128)(2,1)}, bf16[256,1024]{1,0:T(8,128)(2,1)S(1)}, u32[]{:S(2)}, u32[]{:S(2)}) collective-permute-start(bf16[256,1024]{1,0:T(8,128)(2,1)} %collective-permute-done.refs_0_), channel_id=1, source_target_pairs={{0,1},{1,2},{2,3},{3,0},{4,5},{5,6},{6,7},{7,4},{8,9},{9,10},{10,1... | collective-permute-start | bytes 1572872 | tf_op jit(solution)/shard_map/ppermute | solution.py:312
  56.9 33.1 %collective-permute-start.6 = (bf16[256,1024]{1,0:T(8,128)(2,1)}, bf16[256,1024]{1,0:T(8,128)(2,1)}, u32[]{:S(2)}, u32[]{:S(2)}) collective-permute-start(bf16[256,1024]{1,0:T(8,128)(2,1)} %collective-permute-done.1.refs_1_), channel_id=1, source_target_pairs={{0,1},{1,2},{2,3},{3,0},{4,5},{5,6},{6,7},{7,4},{8,9},{9,10},{10,1... | collective-permute-start | bytes 1572872 | tf_op jit(solution)/shard_map/ppermute | solution.py:312
  58.5 28.0 %collective-permute-start.7 = (f32[192,128]{1,0:T(8,128)}, f32[192,128]{1,0:T(8,128)S(1)}, u32[]{:S(2)}, u32[]{:S(2)}) collective-permute-start(f32[192,128]{1,0:T(8,128)} %get-tuple-element.70), channel_id=1, source_target_pairs={{0,1},{1,2},{2,3},{3,0},{4,5},{5,6},{6,7},{7,4},{8,9},{9,10},{10,1... | collective-permute-start | bytes 294920 | tf_op jit(solution)/shard_map/ppermute | solution.py:312
  59.2 30.9 %collective-permute-start.8 = (f32[192,128]{1,0:T(8,128)S(1)}, f32[192,128]{1,0:T(8,128)S(1)}, u32[]{:S(2)}, u32[]{:S(2)}) collective-permute-start(f32[192,128]{1,0:T(8,128)S(1)} %copy-done.31), channel_id=1, source_target_pairs={{0,2},{1,3},{2,0},{3,1},{4,6},{5,7},{6,4},{7,5},{8,10},{9,11},{10,... | collective-permute-start | bytes 294920 | tf_op jit(solution)/shard_map/ppermute | solution.py:312
  61.3 28.7 %collective-permute-start.9 = (f32[192,128]{1,0:T(8,128)S(1)}, f32[192,128]{1,0:T(8,128)S(1)}, u32[]{:S(2)}, u32[]{:S(2)}) collective-permute-start(f32[192,128]{1,0:T(8,128)S(1)} %copy-done.29), channel_id=1, source_target_pairs={{0,3},{1,0},{2,1},{3,2},{4,7},{5,4},{6,5},{7,6},{8,11},{9,8},{10,9... | collective-permute-start | bytes 294920 | tf_op jit(solution)/shard_map/ppermute | solution.py:312
  90.1 19.5 %collective-permute-start.13 = (bf16[256,1024]{1,0:T(8,128)(2,1)S(1)}, bf16[256,1024]{1,0:T(8,128)(2,1)S(1)}, u32[]{:S(2)}, u32[]{:S(2)}) collective-permute-start(bf16[256,1024]{1,0:T(8,128)(2,1)S(1)} %collective-permute-done.5.refs_0_), channel_id=1, source_target_pairs={{0,1},{1,2},{2,3},{3,0},{4,5},{5,6},{6,7},{7,4},{8,9},{9,10},{10,1... | collective-permute-start | bytes 1572872 | tf_op jit(solution)/shard_map/ppermute | solution.py:312
  93.5 14.4 %collective-permute-start.10 = (bf16[192,128]{1,0:T(8,128)(2,1)S(1)}, bf16[192,128]{1,0:T(8,128)(2,1)S(1)}, u32[]{:S(2)}, u32[]{:S(2)}) collective-permute-start(bf16[192,128]{1,0:T(8,128)(2,1)S(1)} %add_convert_fusion.refs_0_), channel_id=1, source_target_pairs={{0,1},{1,2},{2,3},{3,0},{4,5},{5,6},{6,7},{7,4},{8,9},{9,10},{10,1... | collective-permute-start | bytes 147464 | tf_op jit(solution)/shard_map/ppermute | solution.py:312
  93.6 15.4 %collective-permute-start.11 = (bf16[192,128]{1,0:T(8,128)(2,1)S(1)}, bf16[192,128]{1,0:T(8,128)(2,1)S(1)}, u32[]{:S(2)}, u32[]{:S(2)}) collective-permute-start(bf16[192,128]{1,0:T(8,128)(2,1)S(1)} %add_convert_fusion.refs_0_), channel_id=1, source_target_pairs={{0,2},{1,3},{2,0},{3,1},{4,6},{5,7},{6,4},{7,5},{8,10},{9,11},{10,... | collective-permute-start | bytes 147464 | tf_op jit(solution)/shard_map/ppermute | solution.py:312
  95.4 13.6 %collective-permute-start.12 = (bf16[192,128]{1,0:T(8,128)(2,1)S(1)}, bf16[192,128]{1,0:T(8,128)(2,1)S(1)}, u32[]{:S(2)}, u32[]{:S(2)}) collective-permute-start(bf16[192,128]{1,0:T(8,128)(2,1)S(1)} %add_convert_fusion.refs_0_), channel_id=1, source_target_pairs={{0,3},{1,0},{2,1},{3,2},{4,7},{5,4},{6,5},{7,6},{8,11},{9,8},{10,9... | collective-permute-start | bytes 147464 | tf_op jit(solution)/shard_map/ppermute | solution.py:312
  110.4 22.7 %collective-permute-start.14 = (bf16[256,1024]{1,0:T(8,128)(2,1)}, bf16[256,1024]{1,0:T(8,128)(2,1)}, u32[]{:S(2)}, u32[]{:S(2)}) collective-permute-start(bf16[256,1024]{1,0:T(8,128)(2,1)} %collective-permute-done.6.refs_1_), channel_id=1, source_target_pairs={{0,1},{1,2},{2,3},{3,0},{4,5},{5,6},{6,7},{7,4},{8,9},{9,10},{10,1... | collective-permute-start | bytes 1572872 | tf_op jit(solution)/shard_map/ppermute | solution.py:312
  123.2 9.9 %collective-permute-start.15 = (bf16[256,512]{1,0:T(8,128)(2,1)S(1)}, bf16[256,512]{1,0:T(8,128)(2,1)}, u32[]{:S(2)}, u32[]{:S(2)}) collective-permute-start(bf16[256,512]{1,0:T(8,128)(2,1)S(1)} %get-tuple-element.87.attended_ref), channel_id=1, source_target_pairs={{0,1},{1,2},{2,3},{3,0},{4,5},{5,6},{6,7},{7,4},{8,9},{9,10},{10,1... | collective-permute-start | bytes 786440 | tf_op jit(solution)/shard_map/ppermute | solution.py:312
  123.5 9.6 %copy-start.25 = (s32[5]{0:T(128)}, s32[5]{0:T(128)S(1)}, u32[]{:S(2)}) copy-start(s32[5]{0:T(128)S(1)} %pad_add_fusion.1.ids_ref) | copy-start | bytes 64
  133.1 11.9 %collective-permute-start.17 = (bf16[256,512]{1,0:T(8,128)(2,1)}, bf16[256,512]{1,0:T(8,128)(2,1)}, u32[]{:S(2)}, u32[]{:S(2)}) collective-permute-start(bf16[256,512]{1,0:T(8,128)(2,1)} %collective-permute-done.15.attended_ref), channel_id=1, source_target_pairs={{0,1},{1,2},{2,3},{3,0},{4,5},{5,6},{6,7},{7,4},{8,9},{9,10},{10,1... | collective-permute-start | bytes 786440 | tf_op jit(solution)/shard_map/ppermute | solution.py:312
  141.8 11.0 %collective-permute-start.16 = (bf16[256,512]{1,0:T(8,128)(2,1)S(1)}, bf16[256,512]{1,0:T(8,128)(2,1)S(1)}, u32[]{:S(2)}, u32[]{:S(2)}) collective-permute-start(bf16[256,512]{1,0:T(8,128)(2,1)S(1)} %copy-done.22), channel_id=1, source_target_pairs={{0,1},{1,2},{2,3},{3,0},{4,5},{5,6},{6,7},{7,4},{8,9},{9,10},{10,1... | collective-permute-start | bytes 786440 | tf_op jit(solution)/shard_map/ppermute | solution.py:312
  145.0 13.3 %collective-permute-start.19 = (bf16[256,512]{1,0:T(8,128)(2,1)}, bf16[256,512]{1,0:T(8,128)(2,1)S(1)}, u32[]{:S(2)}, u32[]{:S(2)}) collective-permute-start(bf16[256,512]{1,0:T(8,128)(2,1)} %collective-permute-done.17.attended_ref), channel_id=1, source_target_pairs={{0,1},{1,2},{2,3},{3,0},{4,5},{5,6},{6,7},{7,4},{8,9},{9,10},{10,1... | collective-permute-start | bytes 786440 | tf_op jit(solution)/shard_map/ppermute | solution.py:312
  152.7 9.2 %collective-permute-start.18 = (bf16[256,512]{1,0:T(8,128)(2,1)S(1)}, bf16[256,512]{1,0:T(8,128)(2,1)S(1)}, u32[]{:S(2)}, u32[]{:S(2)}) collective-permute-start(bf16[256,512]{1,0:T(8,128)(2,1)S(1)} %collective-permute-done.16.attended_ref), channel_id=1, source_target_pairs={{0,1},{1,2},{2,3},{3,0},{4,5},{5,6},{6,7},{7,4},{8,9},{9,10},{10,1... | collective-permute-start | bytes 786440 | tf_op jit(solution)/shard_map/ppermute | solution.py:312
  161.9 8.2 %collective-permute-start.20 = (bf16[256,512]{1,0:T(8,128)(2,1)S(1)}, bf16[256,512]{1,0:T(8,128)(2,1)S(1)}, u32[]{:S(2)}, u32[]{:S(2)}) collective-permute-start(bf16[256,512]{1,0:T(8,128)(2,1)S(1)} %collective-permute-done.18.attended_ref), channel_id=1, source_target_pairs={{0,1},{1,2},{2,3},{3,0},{4,5},{5,6},{6,7},{7,4},{8,9},{9,10},{10,1... | collective-permute-start | bytes 786440 | tf_op jit(solution)/shard_map/ppermute | solution.py:312
  (31 other events, 49.5 us)
Sparse Core Ops, SparseCore 0:
  13.4 19.5 all-gather.5
  56.3 39.7 all-gather.7

commit v21 on v19

--- a/solution.py
+++ b/solution.py
@@ -390,7 +390,7 @@
             shrink, lines = side
         if last:
             part_weight = shard(step)
-            moved[1] = turned(after(moved[1], moved[0], *lines))
+            moved[1] = turned(after(moved[1], moved[0], begun, *shrink, *lines))
             break
         done = lax.optimization_barrier((moved, begun, shard(step), side))
         moved, begun, part_weight, side = done

time: 180 us -> 176 us (0.978)
  waiting for transfers between devices: 49.5 us -> 42.6 us
  local copies, waits for them, and re-layouts: 28.3 us -> 33.1 us
  starting transfers between devices: 27.2 us -> 24.3 us
    all_gather x1, waiting for transfers between devices: 6.54 us -> 0.01 us  [local(): lines = lax.all_gather(jnp.stack(lines), PLANE, axis=0)]
    unnamed x70 -> x74, local copies, waits for them, and re-layouts: 10.2 us -> 13.8 us
    ppermute x21, starting transfers between devices: 27.2 us -> 24.2 us  [turned(): lax.ppermute(value, 'tensor', [(i, (i + turn) % planes) for i in range(pl...]
  transfers between devices with their start and end apart: 23 -> 23, of which waited for: 14 -> 10; matrix products, arithmetic and copies ran while one was open for 10% -> 12% of each run, Pallas kernels for 15% -> 15%
where the time goes in v21:
time: 176 us
  waiting for transfers between devices  42.6 us (24%)
  local copies, waits for them, and re-layouts  33.1 us (19%)
  Pallas kernels  28.7 us (16%)
  starting transfers between devices  24.3 us (14%)
  blocking collectives  24.2 us (14%)
  between operations  16.5 us (9%)
  other arithmetic  6.24 us (4%)
    ppermute x21, waiting for transfers between devices, turned(): lax.ppermute(value, 'tensor', [(i, (i + turn) % planes) for i in range(pl...  42.6 us
    pallas_call x14, Pallas kernels, call(): pl.pallas_call(kernel, out_shape=out, grid_spec=pltpu.PrefetchScalarGridS...  28.7 us
    ppermute x21, starting transfers between devices, turned(): lax.ppermute(value, 'tensor', [(i, (i + turn) % planes) for i in range(pl...  24.2 us
    unnamed x74, local copies, waits for them, and re-layouts  13.8 us
    all_gather x1, blocking collectives, local(): lax.all_gather(after(output_up_maps, sums[0]), 'dp', axis=0, tiled=True)  10.8 us
    all_gather x1, blocking collectives, local(): lax.all_gather(jnp.transpose(adapter_up_maps[0], (1, 0, 2)), 'dp', axis=0)  7.08 us
    all_gather x1, blocking collectives, local(): lax.all_gather(after(out_down, sums[0]), 'dp', axis=0)  6.3 us
    dynamic_slice x1, local copies, waits for them, and re-layouts, shard(): return lax.dynamic_slice_in_dim(weight, start, depth, axis=1)  5.17 us
  transfers between devices with their start and end apart: 23, of which 10 were waited for; matrix products, arithmetic and copies ran while one was open for 12% of the time, Pallas kernels for 15%

profile of v21, /device:TPU:0, one launch (start us, length us, event | category | flops | bytes accessed | tf_op | source)
XLA Modules:
  0.0 175.6 jit_solution(4687905560434135036)
XLA Ops:
  6.5 2.3 %fusion.5 = (bf16[256,1024]{1,0:T(8,128)(2,1)}, bf16[256,1024]{1,0:T(8,128)(2,1)}) fusion(bf16[512,1024]{1,0:T(8,128)(2,1)} %token_ref.1), kind=kLoop, calls=%fused_computation.40 | loop fusion | bytes 2097152 | tf_op jit(solution)/shard_map/slice | solution.py:363
  8.9 3.0 %collective-permute-start = (bf16[256,1024]{1,0:T(8,128)(2,1)}, bf16[256,1024]{1,0:T(8,128)(2,1)}, u32[]{:S(2)}, u32[]{:S(2)}) collective-permute-start(bf16[256,1024]{1,0:T(8,128)(2,1)} %get-tuple-element.122.refs_0_), channel_id=1, source_target_pairs={{0,1},{1,2},{2,3},{3,0},{4,5},{5,6},{6,7},{7,4},{8,9},{9,10},{10,1... | collective-permute-start | bytes 1572872 | tf_op jit(solution)/shard_map/ppermute | solution.py:312
  13.7 2.8 %fusion.4 = (bf16[64,1,1024]{2,1,0:T(2,128)(2,1)S(1)}, bf16[64,1,1024]{2,1,0:T(2,128)(2,1)S(1)}, bf16[64,1,1024]{2,1,0:T(2,128)(2,1)S(1)}) fusion(bf16[128,4,4096]{2,1,0:T(4,128)(2,1)} %param.11, s32[]{:T(128)S(6)} %select_n.76, s32[]{:T(128)S(6)} %select_n.79, s32[]{:T(128)S(6)} %select_n.88, s32[]{:T(128)S(6)} %select_n.85, s32[]{:T(128)S(6)} %select_n.82), kind=kLoop, calls=%fused_computation.39 | loop fusion | bytes 786452 | tf_op jit(solution)/shard_map/dynamic_slice | solution.py:351
  27.9 1.6 dynamic-slice_bitcast_fusion.4
  29.5 5.2 %dynamic-slice_bitcast_fusion = (bf16[6,1024,128]{2,1,0:T(8,128)(2,1)}, bf16[6,1024,128]{2,1,0:T(8,128)(2,1)}, bf16[6,1024,128]{2,1,0:T(8,128)(2,1)S(1)}, bf16[6,1024,128]{2,1,0:T(8,128)(2,1)}) fusion(bf16[4096,6,128]{2,0,1:T(8,128)(2,1)} %param.10, s32[]{:T(128)S(6)} %select_n.94, s32[]{:T(128)S(6)} %select_n.92, s32[]{:T(128)S(6)} %select_n.89, s32[]{:T(128)S(6)} %select_n.93), kind=kLoop, calls=%fused_computation.3 | loop fusion | bytes 12582928 | tf_op jit(solution)/shard_map/dynamic_slice | solution.py:360
  36.2 2.2 %project.3.refs_3_ = f32[512,768]{1,0:T(8,128)S(1)} custom-call(s32[1]{0:T(128)} %constant.140.clone.1.ids_ref, bf16[256,1024]{1,0:T(8,128)(2,1)} %get-tuple-element.122.refs_0_, bf16[256,1024]{1,0:T(8,128)(2,1)} %get-tuple-element.121.refs_1_, bf16[6,1024,128]{2,1,0:T(8,128)(2,1)S(1)} %get-tuple-element.113.refs_2_), custom_call_target="tpu_custom_call" | custom-call | bytes 7864320 | tf_op jit(solution)/shard_map/project/pallas_call | solution.py:26
  38.4 7.1 %all-gather = bf16[24,64,128]{2,1,0:T(8,128)(2,1)} all-gather(bf16[6,64,128]{2,1,0:T(8,128)(2,1)S(1)} %bitcast.69), channel_id=2, replica_groups=mesh['groups'=2,'dp'=4,'tensor'=4] {'dp'}, dimensions={0}, use_global_device_ids=true | all-gather | bytes 491520 | tf_op jit(solution)/shard_map/all_gather | solution.py:316
  48.1 2.7 %shrink.1 = (f32[192,128]{1,0:T(8,128)S(1)}, f32[192,128]{1,0:T(8,128)S(1)}, f32[192,128]{1,0:T(8,128)S(1)}, f32[192,128]{1,0:T(8,128)S(1)}) custom-call(s32[5]{0:T(128)S(1)} %pad_add_fusion.3.ids_ref, s32[512,2]{1,0:T(8,128)S(1)} %copy.42.table_ref, bf16[512,1024]{1,0:T(8,128)(2,1)S(1)} %copy-done.12, bf16[4,192,1024]{2,1,0:T(8,128)(2,1)S(1)} %copy-done.16), custom_call_target="tpu_custom_call" | custom-call | bytes 7876608 | tf_op jit(solution)/shard_map/shrink/pallas_call | solution.py:26
  52.9 2.1 %pad_maximum_fusion = bf16[3,96,1024]{2,1,0:T(8,128)(2,1)} fusion(bf16[1,96,1024]{2,1,0:T(8,128)(2,1)} %bitcast.24, bf16[1,96,1024]{2,1,0:T(8,128)(2,1)} %bitcast.23, bf16[1,96,1024]{2,1,0:T(8,128)(2,1)} %bitcast.22), kind=kLoop, calls=%fused_computation.8 | loop fusion | flops 589824 | bytes 1179648 | tf_op jit(solution)/shard_map/stack | solution.py:379
  55.1 1.9 %collective-permute-start.5 = (bf16[256,1024]{1,0:T(8,128)(2,1)}, bf16[256,1024]{1,0:T(8,128)(2,1)}, u32[]{:S(2)}, u32[]{:S(2)}) collective-permute-start(bf16[256,1024]{1,0:T(8,128)(2,1)} %collective-permute-done.refs_0_), channel_id=1, source_target_pairs={{0,1},{1,2},{2,3},{3,0},{4,5},{5,6},{6,7},{7,4},{8,9},{9,10},{10,1... | collective-permute-start | bytes 1572872 | tf_op jit(solution)/shard_map/ppermute | solution.py:312
  57.4 1.8 %collective-permute-start.7 = (f32[192,128]{1,0:T(8,128)}, f32[192,128]{1,0:T(8,128)S(1)}, u32[]{:S(2)}, u32[]{:S(2)}) collective-permute-start(f32[192,128]{1,0:T(8,128)} %copy-done.25), channel_id=1, source_target_pairs={{0,1},{1,2},{2,3},{3,0},{4,5},{5,6},{6,7},{7,4},{8,9},{9,10},{10,1... | collective-permute-start | bytes 294920 | tf_op jit(solution)/shard_map/ppermute | solution.py:312
  59.1 2.2 %collective-permute-start.8 = (f32[192,128]{1,0:T(8,128)S(1)}, f32[192,128]{1,0:T(8,128)S(1)}, u32[]{:S(2)}, u32[]{:S(2)}) collective-permute-start(f32[192,128]{1,0:T(8,128)S(1)} %copy-done.24), channel_id=1, source_target_pairs={{0,2},{1,3},{2,0},{3,1},{4,6},{5,7},{6,4},{7,5},{8,10},{9,11},{10,... | collective-permute-start | bytes 294920 | tf_op jit(solution)/shard_map/ppermute | solution.py:312
  62.4 2.4 %project.4.refs_3_ = f32[512,768]{1,0:T(8,128)S(1)} custom-call(s32[1]{0:T(128)} %constant.140.clone.1.ids_ref, bf16[256,1024]{1,0:T(8,128)(2,1)} %collective-permute-done.refs_0_, bf16[256,1024]{1,0:T(8,128)(2,1)} %collective-permute-done.1.refs_1_, bf16[6,1024,128]{2,1,0:T(8,128)(2,1)S(1)} %copy-done.8, f32[512,768]{1,0:T(8,128)S(1)} %project.3.refs_3_), custom_call_target="tpu_custom_call" | custom-call | bytes 12582912 | tf_op jit(solution)/shard_map/project/pallas_call | solution.py:26
  64.8 10.8 %all_gather.27.refs_3_ = bf16[4,64,1024]{2,1,0:T(8,128)(2,1)} all-gather(bf16[1,64,1024]{2,1,0:T(8,128)(2,1)S(1)} %copy-done.28), channel_id=1, replica_groups=mesh['groups'=2,'dp'=4,'tensor'=4] {'dp'}, dimensions={0}, use_global_device_ids=true | all-gather | bytes 655360 | tf_op jit(solution)/shard_map/all_gather | solution.py:382
  75.6 6.3 %all-gather.1 = bf16[128,1024]{1,0:T(8,128)(2,1)} all-gather(bf16[32,1024]{1,0:T(8,128)(2,1)S(1)} %copy-done.27), channel_id=3, replica_groups=mesh['groups'=2,'dp'=4,'tensor'=4] {'dp'}, dimensions={0}, use_global_device_ids=true | all-gather | bytes 327680 | tf_op jit(solution)/shard_map/all_gather | solution.py:383
  81.9 3.4 %collective-permute-done.7 = f32[192,128]{1,0:T(8,128)S(1)} collective-permute-done((f32[192,128]{1,0:T(8,128)}, f32[192,128]{1,0:T(8,128)S(1)}, u32[]{:S(2)}, u32[]{:S(2)}) %collective-permute-start.7) | collective-permute-done | bytes 98336 | tf_op jit(solution)/shard_map/ppermute | solution.py:312
  85.3 3.6 %collective-permute-done.8 = f32[192,128]{1,0:T(8,128)S(1)} collective-permute-done((f32[192,128]{1,0:T(8,128)S(1)}, f32[192,128]{1,0:T(8,128)S(1)}, u32[]{:S(2)}, u32[]{:S(2)}) %collective-permute-start.8) | collective-permute-done | bytes 98336 | tf_op jit(solution)/shard_map/ppermute | solution.py:312
  89.0 2.6 %collective-permute-start.13 = (bf16[256,1024]{1,0:T(8,128)(2,1)}, bf16[256,1024]{1,0:T(8,128)(2,1)}, u32[]{:S(2)}, u32[]{:S(2)}) collective-permute-start(bf16[256,1024]{1,0:T(8,128)(2,1)} %collective-permute-done.5.refs_0_), channel_id=1, source_target_pairs={{0,1},{1,2},{2,3},{3,0},{4,5},{5,6},{6,7},{7,4},{8,9},{9,10},{10,1... | collective-permute-start | bytes 1572872 | tf_op jit(solution)/shard_map/ppermute | solution.py:312
  91.7 1.9 %collective-permute-start.11 = (bf16[192,128]{1,0:T(8,128)(2,1)S(1)}, bf16[192,128]{1,0:T(8,128)(2,1)S(1)}, u32[]{:S(2)}, u32[]{:S(2)}) collective-permute-start(bf16[192,128]{1,0:T(8,128)(2,1)S(1)} %add_convert_fusion.refs_0_), channel_id=1, source_target_pairs={{0,2},{1,3},{2,0},{3,1},{4,6},{5,7},{6,4},{7,5},{8,10},{9,11},{10,... | collective-permute-start | bytes 147464 | tf_op jit(solution)/shard_map/ppermute | solution.py:312
  93.5 2.0 %collective-permute-start.12 = (bf16[192,128]{1,0:T(8,128)(2,1)S(1)}, bf16[192,128]{1,0:T(8,128)(2,1)S(1)}, u32[]{:S(2)}, u32[]{:S(2)}) collective-permute-start(bf16[192,128]{1,0:T(8,128)(2,1)S(1)} %add_convert_fusion.refs_0_), channel_id=1, source_target_pairs={{0,3},{1,0},{2,1},{3,2},{4,7},{5,4},{6,5},{7,6},{8,11},{9,8},{10,9... | collective-permute-start | bytes 147464 | tf_op jit(solution)/shard_map/ppermute | solution.py:312
  95.5 2.2 %project.5.refs_6_ = f32[512,768]{1,0:T(8,128)S(1)} custom-call(s32[1]{0:T(128)} %constant.140.clone.1.ids_ref, bf16[256,1024]{1,0:T(8,128)(2,1)} %collective-permute-done.5.refs_0_, bf16[256,1024]{1,0:T(8,128)(2,1)} %collective-permute-done.6.refs_1_, bf16[6,1024,128]{2,1,0:T(8,128)(2,1)S(1)} %copy-done.7, f32[512,768]{1,0:T(8,128)S(1)} %project.4.refs_3_), custom_call_target="tpu_custom_call" | custom-call | bytes 12582912 | tf_op jit(solution)/shard_map/project/pallas_call | solution.py:26
  98.8 4.4 %slice_bitcast_fusion = (bf16[8,96,1024]{2,1,0:T(8,128)(2,1)}, bf16[8,96,1024]{2,1,0:T(8,128)(2,1)S(1)}, bf16[8,96,1024]{2,1,0:T(8,128)(2,1)S(1)}) fusion(bf16[8,3,96,1024]{3,2,1,0:T(8,128)(2,1)} %bitcast.65), kind=kLoop, calls=%fused_computation | loop fusion | bytes 9437184 | tf_op jit(solution)/shard_map/squeeze | solution.py:388
  103.2 3.8 %collective-permute-done.10.refs_1_ = bf16[192,128]{1,0:T(8,128)(2,1)S(1)} collective-permute-done((bf16[192,128]{1,0:T(8,128)(2,1)S(1)}, bf16[192,128]{1,0:T(8,128)(2,1)S(1)}, u32[]{:S(2)}, u32[]{:S(2)}) %collective-permute-start.10) | collective-permute-done | bytes 49184 | tf_op jit(solution)/shard_map/ppermute | solution.py:312
  118.0 4.4 %attend.2 = (bf16[256,512]{1,0:T(8,128)(2,1)S(1)}, bf16[256,128]{1,0:T(8,128)(2,1)S(1)}, bf16[256,128]{1,0:T(8,128)(2,1)S(1)}) custom-call(s32[8]{0:T(128)S(1)} %copy-done.20, s32[512,2]{1,0:T(8,128)S(1)} %copy.47.table_ref.refs_2_, f32[512,256]{1,0:T(8,128)S(1)} %copy-done.10, bf16[4,6,64,128]{3,2,1,0:T(8,128)(2,1)S(1)} %bitcast.61, ...), custom_call_target="tpu_custom_call" | custom-call | bytes 14364672 | tf_op jit(solution)/shard_map/attend/pallas_call | solution.py:26
  123.8 8.4 %collective-permute-done.15.attended_ref = bf16[256,512]{1,0:T(8,128)(2,1)S(1)} collective-permute-done((bf16[256,512]{1,0:T(8,128)(2,1)S(1)}, bf16[256,512]{1,0:T(8,128)(2,1)S(1)}, u32[]{:S(2)}, u32[]{:S(2)}) %collective-permute-start.15) | collective-permute-done | bytes 262176 | tf_op jit(solution)/shard_map/ppermute | solution.py:312
  132.3 4.9 %attend.3 = (bf16[256,512]{1,0:T(8,128)(2,1)S(1)}, bf16[256,128]{1,0:T(8,128)(2,1)}, bf16[256,128]{1,0:T(8,128)(2,1)}) custom-call(s32[8]{0:T(128)S(1)} %copy-done.20, s32[512,2]{1,0:T(8,128)S(1)} %copy.47.table_ref.refs_2_, f32[512,256]{1,0:T(8,128)S(1)} %copy-done.11, bf16[4,6,64,128]{3,2,1,0:T(8,128)(2,1)S(1)} %bitcast.62, ...), custom_call_target="tpu_custom_call" | custom-call | bytes 14757888 | tf_op jit(solution)/shard_map/attend/pallas_call | solution.py:26
  138.3 3.4 %collective-permute-done.17.attended_ref = bf16[256,512]{1,0:T(8,128)(2,1)S(1)} collective-permute-done((bf16[256,512]{1,0:T(8,128)(2,1)S(1)}, bf16[256,512]{1,0:T(8,128)(2,1)S(1)}, u32[]{:S(2)}, u32[]{:S(2)}) %collective-permute-start.17) | collective-permute-done | bytes 262176 | tf_op jit(solution)/shard_map/ppermute | solution.py:312
  142.8 5.5 %collective-permute-done.16.attended_ref = bf16[256,512]{1,0:T(8,128)(2,1)S(1)} collective-permute-done((bf16[256,512]{1,0:T(8,128)(2,1)S(1)}, bf16[256,512]{1,0:T(8,128)(2,1)S(1)}, u32[]{:S(2)}, u32[]{:S(2)}) %collective-permute-start.16) | collective-permute-done | bytes 262176 | tf_op jit(solution)/shard_map/ppermute | solution.py:312
  149.3 4.5 %collective-permute-done.19.attended_ref = bf16[256,512]{1,0:T(8,128)(2,1)S(1)} collective-permute-done((bf16[256,512]{1,0:T(8,128)(2,1)S(1)}, bf16[256,512]{1,0:T(8,128)(2,1)S(1)}, u32[]{:S(2)}, u32[]{:S(2)}) %collective-permute-start.19) | collective-permute-done | bytes 262176 | tf_op jit(solution)/shard_map/ppermute | solution.py:312
  153.9 4.1 %collective-permute-done.18.attended_ref = bf16[256,512]{1,0:T(8,128)(2,1)S(1)} collective-permute-done((bf16[256,512]{1,0:T(8,128)(2,1)S(1)}, bf16[256,512]{1,0:T(8,128)(2,1)S(1)}, u32[]{:S(2)}, u32[]{:S(2)}) %collective-permute-start.18) | collective-permute-done | bytes 262176 | tf_op jit(solution)/shard_map/ppermute | solution.py:312
  161.8 4.7 %collective-permute-done.20.attended_ref = bf16[256,512]{1,0:T(8,128)(2,1)S(1)} collective-permute-done((bf16[256,512]{1,0:T(8,128)(2,1)S(1)}, bf16[256,512]{1,0:T(8,128)(2,1)S(1)}, u32[]{:S(2)}, u32[]{:S(2)}) %collective-permute-start.20) | collective-permute-done | bytes 262176 | tf_op jit(solution)/shard_map/ppermute | solution.py:312
  166.5 2.3 %project_out.15 = bf16[512,1024]{1,0:T(8,128)(2,1)} custom-call(s32[5]{0:T(128)S(1)} %pad_add_fusion.1.ids_ref, bf16[256,512]{1,0:T(8,128)(2,1)S(1)} %collective-permute-done.20.attended_ref, bf16[8,96,1024]{2,1,0:T(8,128)(2,1)S(1)} %copy-done, bf16[8,96,1024]{2,1,0:T(8,128)(2,1)S(1)} %copy-done, f32[256,1024]{1,0:T(8,128)S(1)} %get-tuple-element.106.refs_0_, ...), custom_call_target="tpu_custom_call" | custom-call | bytes 17313792 | tf_op jit(solution)/shard_map/project_out/pallas_call | solution.py:26
  (138 shorter events, 38.6 us)
Async XLA Ops:
  6.5 39.0 %all-gather.6.cloned.1.call-start = ((), (), s32[]{:S(2)}) async-start(), calls=%async_computation | async-start | bytes 1966080 | tf_op jit(solution)/shard_map/all_gather | solution.py:315
  8.9 44.0 %collective-permute-start = (bf16[256,1024]{1,0:T(8,128)(2,1)}, bf16[256,1024]{1,0:T(8,128)(2,1)}, u32[]{:S(2)}, u32[]{:S(2)}) collective-permute-start(bf16[256,1024]{1,0:T(8,128)(2,1)} %get-tuple-element.122.refs_0_), channel_id=1, source_target_pairs={{0,1},{1,2},{2,3},{3,0},{4,5},{5,6},{6,7},{7,4},{8,9},{9,10},{10,1... | collective-permute-start | bytes 1572872 | tf_op jit(solution)/shard_map/ppermute | solution.py:312
  11.9 41.0 %collective-permute-start.1 = (bf16[256,1024]{1,0:T(8,128)(2,1)}, bf16[256,1024]{1,0:T(8,128)(2,1)}, u32[]{:S(2)}, u32[]{:S(2)}) collective-permute-start(bf16[256,1024]{1,0:T(8,128)(2,1)} %get-tuple-element.121.refs_1_), channel_id=1, source_target_pairs={{0,1},{1,2},{2,3},{3,0},{4,5},{5,6},{6,7},{7,4},{8,9},{9,10},{10,1... | collective-permute-start | bytes 1572872 | tf_op jit(solution)/shard_map/ppermute | solution.py:312
  13.5 85.3 %all-gather.8.cloned.1.call-start = ((), (), s32[]{:S(2)}) async-start(), calls=%async_computation.1 | async-start | bytes 5308416 | tf_op jit(solution)/shard_map/all_gather | solution.py:379
  16.7 10.1 %copy-start.26 = (bf16[32,1024]{1,0:T(8,128)(2,1)}, bf16[32,1024]{1,0:T(8,128)(2,1)S(1)}, u32[]{:S(2)}) copy-start(bf16[32,1024]{1,0:T(8,128)(2,1)S(1)} %bitcast_dynamic-update-slice_fusion) | copy-start | bytes 196612
  17.6 35.2 %collective-permute-start.2 = (bf16[96,1024]{1,0:T(8,128)(2,1)}, bf16[96,1024]{1,0:T(8,128)(2,1)}, u32[]{:S(2)}, u32[]{:S(2)}) collective-permute-start(bf16[96,1024]{1,0:T(8,128)(2,1)} %get-tuple-element.125), channel_id=1, source_target_pairs={{0,1},{1,2},{2,3},{3,0},{4,5},{5,6},{6,7},{7,4},{8,9},{9,10},{10,1... | collective-permute-start | bytes 589832 | tf_op jit(solution)/shard_map/ppermute | solution.py:312
  19.2 33.6 %collective-permute-start.3 = (bf16[96,1024]{1,0:T(8,128)(2,1)}, bf16[96,1024]{1,0:T(8,128)(2,1)}, u32[]{:S(2)}, u32[]{:S(2)}) collective-permute-start(bf16[96,1024]{1,0:T(8,128)(2,1)} %get-tuple-element.124), channel_id=1, source_target_pairs={{0,2},{1,3},{2,0},{3,1},{4,6},{5,7},{6,4},{7,5},{8,10},{9,11},{10,... | collective-permute-start | bytes 589832 | tf_op jit(solution)/shard_map/ppermute | solution.py:312
  20.5 32.4 %collective-permute-start.4 = (bf16[96,1024]{1,0:T(8,128)(2,1)}, bf16[96,1024]{1,0:T(8,128)(2,1)}, u32[]{:S(2)}, u32[]{:S(2)}) collective-permute-start(bf16[96,1024]{1,0:T(8,128)(2,1)} %get-tuple-element.123), channel_id=1, source_target_pairs={{0,3},{1,0},{2,1},{3,2},{4,7},{5,4},{6,5},{7,6},{8,11},{9,8},{10,9... | collective-permute-start | bytes 589832 | tf_op jit(solution)/shard_map/ppermute | solution.py:312
  55.0 20.6 %copy-start.27 = (bf16[32,1024]{1,0:T(8,128)(2,1)S(1)}, bf16[32,1024]{1,0:T(8,128)(2,1)}, u32[]{:S(2)}) copy-start(bf16[32,1024]{1,0:T(8,128)(2,1)} %copy-done.26) | copy-start | bytes 196612
  55.1 33.9 %collective-permute-start.5 = (bf16[256,1024]{1,0:T(8,128)(2,1)}, bf16[256,1024]{1,0:T(8,128)(2,1)}, u32[]{:S(2)}, u32[]{:S(2)}) collective-permute-start(bf16[256,1024]{1,0:T(8,128)(2,1)} %collective-permute-done.refs_0_), channel_id=1, source_target_pairs={{0,1},{1,2},{2,3},{3,0},{4,5},{5,6},{6,7},{7,4},{8,9},{9,10},{10,1... | collective-permute-start | bytes 1572872 | tf_op jit(solution)/shard_map/ppermute | solution.py:312
  57.0 32.0 %collective-permute-start.6 = (bf16[256,1024]{1,0:T(8,128)(2,1)}, bf16[256,1024]{1,0:T(8,128)(2,1)}, u32[]{:S(2)}, u32[]{:S(2)}) collective-permute-start(bf16[256,1024]{1,0:T(8,128)(2,1)} %collective-permute-done.1.refs_1_), channel_id=1, source_target_pairs={{0,1},{1,2},{2,3},{3,0},{4,5},{5,6},{6,7},{7,4},{8,9},{9,10},{10,1... | collective-permute-start | bytes 1572872 | tf_op jit(solution)/shard_map/ppermute | solution.py:312
  57.4 28.0 %collective-permute-start.7 = (f32[192,128]{1,0:T(8,128)}, f32[192,128]{1,0:T(8,128)S(1)}, u32[]{:S(2)}, u32[]{:S(2)}) collective-permute-start(f32[192,128]{1,0:T(8,128)} %copy-done.25), channel_id=1, source_target_pairs={{0,1},{1,2},{2,3},{3,0},{4,5},{5,6},{6,7},{7,4},{8,9},{9,10},{10,1... | collective-permute-start | bytes 294920 | tf_op jit(solution)/shard_map/ppermute | solution.py:312
  59.1 29.9 %collective-permute-start.8 = (f32[192,128]{1,0:T(8,128)S(1)}, f32[192,128]{1,0:T(8,128)S(1)}, u32[]{:S(2)}, u32[]{:S(2)}) collective-permute-start(f32[192,128]{1,0:T(8,128)S(1)} %copy-done.24), channel_id=1, source_target_pairs={{0,2},{1,3},{2,0},{3,1},{4,6},{5,7},{6,4},{7,5},{8,10},{9,11},{10,... | collective-permute-start | bytes 294920 | tf_op jit(solution)/shard_map/ppermute | solution.py:312
  61.4 27.6 %collective-permute-start.9 = (f32[192,128]{1,0:T(8,128)S(1)}, f32[192,128]{1,0:T(8,128)S(1)}, u32[]{:S(2)}, u32[]{:S(2)}) collective-permute-start(f32[192,128]{1,0:T(8,128)S(1)} %copy-done.22), channel_id=1, source_target_pairs={{0,3},{1,0},{2,1},{3,2},{4,7},{5,4},{6,5},{7,6},{8,11},{9,8},{10,9... | collective-permute-start | bytes 294920 | tf_op jit(solution)/shard_map/ppermute | solution.py:312
  62.4 33.0 %copy-start.7 = (bf16[6,1024,128]{2,1,0:T(8,128)(2,1)S(1)}, bf16[6,1024,128]{2,1,0:T(8,128)(2,1)}, u32[]{:S(2)}) copy-start(bf16[6,1024,128]{2,1,0:T(8,128)(2,1)} %get-tuple-element.81.refs_2_) | copy-start | bytes 4718596
  89.0 19.7 %collective-permute-start.13 = (bf16[256,1024]{1,0:T(8,128)(2,1)}, bf16[256,1024]{1,0:T(8,128)(2,1)}, u32[]{:S(2)}, u32[]{:S(2)}) collective-permute-start(bf16[256,1024]{1,0:T(8,128)(2,1)} %collective-permute-done.5.refs_0_), channel_id=1, source_target_pairs={{0,1},{1,2},{2,3},{3,0},{4,5},{5,6},{6,7},{7,4},{8,9},{9,10},{10,1... | collective-permute-start | bytes 1572872 | tf_op jit(solution)/shard_map/ppermute | solution.py:312
  91.6 15.5 %collective-permute-start.10 = (bf16[192,128]{1,0:T(8,128)(2,1)S(1)}, bf16[192,128]{1,0:T(8,128)(2,1)S(1)}, u32[]{:S(2)}, u32[]{:S(2)}) collective-permute-start(bf16[192,128]{1,0:T(8,128)(2,1)S(1)} %add_convert_fusion.refs_0_), channel_id=1, source_target_pairs={{0,1},{1,2},{2,3},{3,0},{4,5},{5,6},{6,7},{7,4},{8,9},{9,10},{10,1... | collective-permute-start | bytes 147464 | tf_op jit(solution)/shard_map/ppermute | solution.py:312
  91.7 16.4 %collective-permute-start.11 = (bf16[192,128]{1,0:T(8,128)(2,1)S(1)}, bf16[192,128]{1,0:T(8,128)(2,1)S(1)}, u32[]{:S(2)}, u32[]{:S(2)}) collective-permute-start(bf16[192,128]{1,0:T(8,128)(2,1)S(1)} %add_convert_fusion.refs_0_), channel_id=1, source_target_pairs={{0,2},{1,3},{2,0},{3,1},{4,6},{5,7},{6,4},{7,5},{8,10},{9,11},{10,... | collective-permute-start | bytes 147464 | tf_op jit(solution)/shard_map/ppermute | solution.py:312
  93.5 14.6 %collective-permute-start.12 = (bf16[192,128]{1,0:T(8,128)(2,1)S(1)}, bf16[192,128]{1,0:T(8,128)(2,1)S(1)}, u32[]{:S(2)}, u32[]{:S(2)}) collective-permute-start(bf16[192,128]{1,0:T(8,128)(2,1)S(1)} %add_convert_fusion.refs_0_), channel_id=1, source_target_pairs={{0,3},{1,0},{2,1},{3,2},{4,7},{5,4},{6,5},{7,6},{8,11},{9,8},{10,9... | collective-permute-start | bytes 147464 | tf_op jit(solution)/shard_map/ppermute | solution.py:312
  98.8 11.4 %copy-start.33 = (s32[4]{0:T(128)S(1)}, s32[4]{0:T(128)}, u32[]{:S(2)}) copy-start(s32[4]{0:T(128)} %copy-done.32) | copy-start | bytes 52
  108.7 23.5 %collective-permute-start.14 = (bf16[256,1024]{1,0:T(8,128)(2,1)}, bf16[256,1024]{1,0:T(8,128)(2,1)}, u32[]{:S(2)}, u32[]{:S(2)}) collective-permute-start(bf16[256,1024]{1,0:T(8,128)(2,1)} %collective-permute-done.6.refs_1_), channel_id=1, source_target_pairs={{0,1},{1,2},{2,3},{3,0},{4,5},{5,6},{6,7},{7,4},{8,9},{9,10},{10,1... | collective-permute-start | bytes 1572872 | tf_op jit(solution)/shard_map/ppermute | solution.py:312
  118.0 14.3 %copy-start.5 = (bf16[6,1024,128]{2,1,0:T(8,128)(2,1)S(1)}, bf16[6,1024,128]{2,1,0:T(8,128)(2,1)}, u32[]{:S(2)}) copy-start(bf16[6,1024,128]{2,1,0:T(8,128)(2,1)} %get-tuple-element.111.refs_5_) | copy-start | bytes 4718596
  118.0 14.3 %copy-start.11 = (f32[512,256]{1,0:T(8,128)S(1)}, f32[512,256]{1,0:T(8,128)}, u32[]{:S(2)}) copy-start(f32[512,256]{1,0:T(8,128)} %pad_maximum_fusion.1.turn_ref) | copy-start | bytes 1572868
  118.0 14.3 %copy-start.14 = (bf16[24,64,128]{2,1,0:T(8,128)(2,1)S(1)}, bf16[24,64,128]{2,1,0:T(8,128)(2,1)}, u32[]{:S(2)}) copy-start(bf16[24,64,128]{2,1,0:T(8,128)(2,1)} %all-gather) | copy-start | bytes 1179652
  118.0 14.3 %copy-start.19 = (bf16[192,128]{1,0:T(8,128)(2,1)S(1)}, bf16[192,128]{1,0:T(8,128)(2,1)}, u32[]{:S(2)}) copy-start(bf16[192,128]{1,0:T(8,128)(2,1)} %copy-done.17) | copy-start | bytes 147460
  122.4 9.9 %copy-start.3 = (f32[512,768]{1,0:T(8,128)S(1)}, f32[512,768]{1,0:T(8,128)}, u32[]{:S(2)}) copy-start(f32[512,768]{1,0:T(8,128)} %copy-done.1) | copy-start | bytes 4718596
  122.5 9.8 %collective-permute-start.15 = (bf16[256,512]{1,0:T(8,128)(2,1)S(1)}, bf16[256,512]{1,0:T(8,128)(2,1)S(1)}, u32[]{:S(2)}, u32[]{:S(2)}) collective-permute-start(bf16[256,512]{1,0:T(8,128)(2,1)S(1)} %get-tuple-element.90.attended_ref), channel_id=1, source_target_pairs={{0,1},{1,2},{2,3},{3,0},{4,5},{5,6},{6,7},{7,4},{8,9},{9,10},{10,1... | collective-permute-start | bytes 786440 | tf_op jit(solution)/shard_map/ppermute | solution.py:312
  132.2 9.4 %collective-permute-start.17 = (bf16[256,512]{1,0:T(8,128)(2,1)S(1)}, bf16[256,512]{1,0:T(8,128)(2,1)S(1)}, u32[]{:S(2)}, u32[]{:S(2)}) collective-permute-start(bf16[256,512]{1,0:T(8,128)(2,1)S(1)} %collective-permute-done.15.attended_ref), channel_id=1, source_target_pairs={{0,1},{1,2},{2,3},{3,0},{4,5},{5,6},{6,7},{7,4},{8,9},{9,10},{10,1... | collective-permute-start | bytes 786440 | tf_op jit(solution)/shard_map/ppermute | solution.py:312
  137.2 11.1 %collective-permute-start.16 = (bf16[256,512]{1,0:T(8,128)(2,1)S(1)}, bf16[256,512]{1,0:T(8,128)(2,1)S(1)}, u32[]{:S(2)}, u32[]{:S(2)}) collective-permute-start(bf16[256,512]{1,0:T(8,128)(2,1)S(1)} %get-tuple-element.91.attended_ref), channel_id=1, source_target_pairs={{0,1},{1,2},{2,3},{3,0},{4,5},{5,6},{6,7},{7,4},{8,9},{9,10},{10,1... | collective-permute-start | bytes 786440 | tf_op jit(solution)/shard_map/ppermute | solution.py:312
  141.7 12.2 %collective-permute-start.19 = (bf16[256,512]{1,0:T(8,128)(2,1)S(1)}, bf16[256,512]{1,0:T(8,128)(2,1)S(1)}, u32[]{:S(2)}, u32[]{:S(2)}) collective-permute-start(bf16[256,512]{1,0:T(8,128)(2,1)S(1)} %collective-permute-done.17.attended_ref), channel_id=1, source_target_pairs={{0,1},{1,2},{2,3},{3,0},{4,5},{5,6},{6,7},{7,4},{8,9},{9,10},{10,1... | collective-permute-start | bytes 786440 | tf_op jit(solution)/shard_map/ppermute | solution.py:312
  148.3 9.7 %collective-permute-start.18 = (bf16[256,512]{1,0:T(8,128)(2,1)S(1)}, bf16[256,512]{1,0:T(8,128)(2,1)S(1)}, u32[]{:S(2)}, u32[]{:S(2)}) collective-permute-start(bf16[256,512]{1,0:T(8,128)(2,1)S(1)} %collective-permute-done.16.attended_ref), channel_id=1, source_target_pairs={{0,1},{1,2},{2,3},{3,0},{4,5},{5,6},{6,7},{7,4},{8,9},{9,10},{10,1... | collective-permute-start | bytes 786440 | tf_op jit(solution)/shard_map/ppermute | solution.py:312
  158.0 8.6 %collective-permute-start.20 = (bf16[256,512]{1,0:T(8,128)(2,1)S(1)}, bf16[256,512]{1,0:T(8,128)(2,1)S(1)}, u32[]{:S(2)}, u32[]{:S(2)}) collective-permute-start(bf16[256,512]{1,0:T(8,128)(2,1)S(1)} %collective-permute-done.18.attended_ref), channel_id=1, source_target_pairs={{0,1},{1,2},{2,3},{3,0},{4,5},{5,6},{6,7},{7,4},{8,9},{9,10},{10,1... | collective-permute-start | bytes 786440 | tf_op jit(solution)/shard_map/ppermute | solution.py:312
  (27 other events, 96.1 us)
Sparse Core Ops, SparseCore 0:
  13.6 19.5 all-gather.5
  55.2 41.9 all-gather.7

commit v22 on v18

--- a/solution.py
+++ b/solution.py
@@ -21,7 +21,7 @@
     return pl.BlockSpec(shape, lambda step, ids: (0,) * len(shape))
 
 
-def call(kernel, name, ids, grid, specs, arrays, out, scratch=()):
+def call(kernel, name, ids, grid, specs, arrays, out, scratch=(), grant=VMEM_BYTES):
     total = sum(array.size * array.dtype.itemsize for array in arrays)
     return pl.pallas_call(
         kernel,
@@ -33,7 +33,7 @@
             out_specs=[fixed(item) for item in out] if isinstance(out, tuple) else fixed(out),
             scratch_shapes=list(scratch),
         ),
-        compiler_params=pltpu.CompilerParams(vmem_limit_bytes=VMEM_BYTES),
+        compiler_params=pltpu.CompilerParams(vmem_limit_bytes=grant),
         cost_estimate=pl.CostEstimate(flops=0, bytes_accessed=3 * total, transcendentals=0),
         name=name,
     )(ids.astype(jnp.int32), *arrays)
@@ -168,6 +168,7 @@
                 (planes * shrink[0].shape[0] * 2 // 3, shrink[0].shape[1] * 3 // 2), jnp.bfloat16
             ),
         ],
+        VMEM_BYTES if earlier else 60 * 1024 * 1024,
     )
 
 

time: 176 us -> 179 us (1.017)
    unnamed x74 -> x80, local copies, waits for them, and re-layouts: 13.8 us -> 15 us
  transfers between devices with their start and end apart: 23 -> 23, of which waited for: 10 -> 9; matrix products, arithmetic and copies ran while one was open for 12% -> 12% of each run, Pallas kernels for 15% -> 16%
where the time goes in v22:
time: 179 us; the launch traced here: 178 us
  waiting for transfers between devices  41.2 us (23%)
  local copies, waits for them, and re-layouts  34.4 us (19%)
  Pallas kernels  30.4 us (17%)
  starting transfers between devices  25.2 us (14%)
  blocking collectives  24.2 us (14%)
  between operations  16.6 us (9%)
  other arithmetic  6.22 us (3%)
    ppermute x21, waiting for transfers between devices, turned(): lax.ppermute(value, 'tensor', [(i, (i + turn) % planes) for i in range(pl...  41.2 us
    pallas_call x14, Pallas kernels, call(): pl.pallas_call(kernel, out_shape=out, grid_spec=pltpu.PrefetchScalarGridS...  30.4 us
    ppermute x21, starting transfers between devices, turned(): lax.ppermute(value, 'tensor', [(i, (i + turn) % planes) for i in range(pl...  25.2 us
    unnamed x80, local copies, waits for them, and re-layouts  15 us
    all_gather x1, blocking collectives, local(): lax.all_gather(after(output_up_maps, sums[0]), 'dp', axis=0, tiled=True)  10.7 us
    all_gather x1, blocking collectives, local(): lax.all_gather(jnp.transpose(adapter_up_maps[0], (1, 0, 2)), 'dp', axis=0)  7.12 us
    all_gather x1, blocking collectives, local(): lax.all_gather(after(out_down, sums[0]), 'dp', axis=0)  6.3 us
    dynamic_slice x1, local copies, waits for them, and re-layouts, shard(): return lax.dynamic_slice_in_dim(weight, start, depth, axis=1)  5.17 us
  transfers between devices with their start and end apart: 23, of which 9 were waited for; matrix products, arithmetic and copies ran while one was open for 12% of the time, Pallas kernels for 16%

profile of v22, /device:TPU:0, one launch (start us, length us, event | category | flops | bytes accessed | tf_op | source)
XLA Modules:
  0.0 178.2 jit_solution(3996915188845043995)
XLA Ops:
  6.5 2.3 %fusion.5 = (bf16[256,1024]{1,0:T(8,128)(2,1)}, bf16[256,1024]{1,0:T(8,128)(2,1)}) fusion(bf16[512,1024]{1,0:T(8,128)(2,1)} %token_ref.1), kind=kLoop, calls=%fused_computation.40 | loop fusion | bytes 2097152 | tf_op jit(solution)/shard_map/slice | solution.py:364
  8.8 3.0 %collective-permute-start = (bf16[256,1024]{1,0:T(8,128)(2,1)}, bf16[256,1024]{1,0:T(8,128)(2,1)}, u32[]{:S(2)}, u32[]{:S(2)}) collective-permute-start(bf16[256,1024]{1,0:T(8,128)(2,1)} %get-tuple-element.142.refs_0_), channel_id=1, source_target_pairs={{0,1},{1,2},{2,3},{3,0},{4,5},{5,6},{6,7},{7,4},{8,9},{9,10},{10,1... | collective-permute-start | bytes 1572872 | tf_op jit(solution)/shard_map/ppermute | solution.py:313
  11.9 1.6 collective-permute-start.1
  13.7 2.8 %fusion.4 = (bf16[64,1,1024]{2,1,0:T(2,128)(2,1)S(1)}, bf16[64,1,1024]{2,1,0:T(2,128)(2,1)S(1)}, bf16[64,1,1024]{2,1,0:T(2,128)(2,1)S(1)}) fusion(bf16[128,4,4096]{2,1,0:T(4,128)(2,1)} %param.11, s32[]{:T(128)S(6)} %select_n.76, s32[]{:T(128)S(6)} %select_n.79, s32[]{:T(128)S(6)} %select_n.88, s32[]{:T(128)S(6)} %select_n.85, s32[]{:T(128)S(6)} %select_n.82), kind=kLoop, calls=%fused_computation.39 | loop fusion | bytes 786452 | tf_op jit(solution)/shard_map/dynamic_slice | solution.py:352
  27.3 1.6 dynamic-slice_bitcast_fusion.4
  28.9 5.2 %dynamic-slice_bitcast_fusion = (bf16[6,1024,128]{2,1,0:T(8,128)(2,1)}, bf16[6,1024,128]{2,1,0:T(8,128)(2,1)}, bf16[6,1024,128]{2,1,0:T(8,128)(2,1)S(1)}, bf16[6,1024,128]{2,1,0:T(8,128)(2,1)}) fusion(bf16[4096,6,128]{2,0,1:T(8,128)(2,1)} %param.10, s32[]{:T(128)S(6)} %select_n.94, s32[]{:T(128)S(6)} %select_n.92, s32[]{:T(128)S(6)} %select_n.89, s32[]{:T(128)S(6)} %select_n.93), kind=kLoop, calls=%fused_computation.3 | loop fusion | bytes 12582928 | tf_op jit(solution)/shard_map/dynamic_slice | solution.py:361
  35.6 2.2 %project.3.refs_3_ = f32[512,768]{1,0:T(8,128)S(1)} custom-call(s32[1]{0:T(128)} %constant.140.clone.1.ids_ref, bf16[256,1024]{1,0:T(8,128)(2,1)} %get-tuple-element.142.refs_0_, bf16[256,1024]{1,0:T(8,128)(2,1)} %get-tuple-element.141.refs_1_, bf16[6,1024,128]{2,1,0:T(8,128)(2,1)S(1)} %get-tuple-element.133.refs_2_), custom_call_target="tpu_custom_call" | custom-call | bytes 7864320 | tf_op jit(solution)/shard_map/project/pallas_call | solution.py:26
  37.8 7.1 %all-gather = bf16[24,64,128]{2,1,0:T(8,128)(2,1)} all-gather(bf16[6,64,128]{2,1,0:T(8,128)(2,1)S(1)} %bitcast.69), channel_id=2, replica_groups=mesh['groups'=2,'dp'=4,'tensor'=4] {'dp'}, dimensions={0}, use_global_device_ids=true | all-gather | bytes 491520 | tf_op jit(solution)/shard_map/all_gather | solution.py:317
  47.6 2.7 %shrink.1 = (f32[192,128]{1,0:T(8,128)S(1)}, f32[192,128]{1,0:T(8,128)S(1)}, f32[192,128]{1,0:T(8,128)S(1)}, f32[192,128]{1,0:T(8,128)S(1)}) custom-call(s32[5]{0:T(128)S(1)} %pad_add_fusion.3.ids_ref, s32[512,2]{1,0:T(8,128)S(1)} %copy.42.table_ref, bf16[512,1024]{1,0:T(8,128)(2,1)S(1)} %copy-done.11, bf16[4,192,1024]{2,1,0:T(8,128)(2,1)S(1)} %copy-done.14), custom_call_target="tpu_custom_call" | custom-call | bytes 7876608 | tf_op jit(solution)/shard_map/shrink/pallas_call | solution.py:26
  52.3 2.1 %pad_maximum_fusion = bf16[3,96,1024]{2,1,0:T(8,128)(2,1)} fusion(bf16[1,96,1024]{2,1,0:T(8,128)(2,1)} %bitcast.26, bf16[1,96,1024]{2,1,0:T(8,128)(2,1)} %bitcast.25, bf16[1,96,1024]{2,1,0:T(8,128)(2,1)} %bitcast.24), kind=kLoop, calls=%fused_computation.8 | loop fusion | flops 589824 | bytes 1179648 | tf_op jit(solution)/shard_map/stack | solution.py:380
  54.4 2.5 %collective-permute-start.5 = (bf16[256,1024]{1,0:T(8,128)(2,1)}, bf16[256,1024]{1,0:T(8,128)(2,1)}, u32[]{:S(2)}, u32[]{:S(2)}) collective-permute-start(bf16[256,1024]{1,0:T(8,128)(2,1)} %collective-permute-done.refs_0_), channel_id=1, source_target_pairs={{0,1},{1,2},{2,3},{3,0},{4,5},{5,6},{6,7},{7,4},{8,9},{9,10},{10,1... | collective-permute-start | bytes 1572872 | tf_op jit(solution)/shard_map/ppermute | solution.py:313
  57.0 2.1 %collective-permute-start.7 = (f32[192,128]{1,0:T(8,128)}, f32[192,128]{1,0:T(8,128)S(1)}, u32[]{:S(2)}, u32[]{:S(2)}) collective-permute-start(f32[192,128]{1,0:T(8,128)} %copy-done.31), channel_id=1, source_target_pairs={{0,1},{1,2},{2,3},{3,0},{4,5},{5,6},{6,7},{7,4},{8,9},{9,10},{10,1... | collective-permute-start | bytes 294920 | tf_op jit(solution)/shard_map/ppermute | solution.py:313
  59.1 2.2 %collective-permute-start.8 = (f32[192,128]{1,0:T(8,128)S(1)}, f32[192,128]{1,0:T(8,128)S(1)}, u32[]{:S(2)}, u32[]{:S(2)}) collective-permute-start(f32[192,128]{1,0:T(8,128)S(1)} %copy-done.30), channel_id=1, source_target_pairs={{0,2},{1,3},{2,0},{3,1},{4,6},{5,7},{6,4},{7,5},{8,10},{9,11},{10,... | collective-permute-start | bytes 294920 | tf_op jit(solution)/shard_map/ppermute | solution.py:313
  61.8 2.4 %project.4.refs_3_ = f32[512,768]{1,0:T(8,128)S(1)} custom-call(s32[1]{0:T(128)} %constant.140.clone.1.ids_ref, bf16[256,1024]{1,0:T(8,128)(2,1)} %collective-permute-done.refs_0_, bf16[256,1024]{1,0:T(8,128)(2,1)} %collective-permute-done.1.refs_1_, bf16[6,1024,128]{2,1,0:T(8,128)(2,1)S(1)} %copy-done.8, f32[512,768]{1,0:T(8,128)S(1)} %project.3.refs_3_), custom_call_target="tpu_custom_call" | custom-call | bytes 12582912 | tf_op jit(solution)/shard_map/project/pallas_call | solution.py:26
  64.2 10.7 %all_gather.27.refs_3_ = bf16[4,64,1024]{2,1,0:T(8,128)(2,1)} all-gather(bf16[1,64,1024]{2,1,0:T(8,128)(2,1)S(1)} %copy-done.34), channel_id=1, replica_groups=mesh['groups'=2,'dp'=4,'tensor'=4] {'dp'}, dimensions={0}, use_global_device_ids=true | all-gather | bytes 655360 | tf_op jit(solution)/shard_map/all_gather | solution.py:383
  74.9 6.3 %all-gather.1 = bf16[128,1024]{1,0:T(8,128)(2,1)} all-gather(bf16[32,1024]{1,0:T(8,128)(2,1)S(1)} %copy-done.33), channel_id=3, replica_groups=mesh['groups'=2,'dp'=4,'tensor'=4] {'dp'}, dimensions={0}, use_global_device_ids=true | all-gather | bytes 327680 | tf_op jit(solution)/shard_map/all_gather | solution.py:384
  81.3 3.5 %collective-permute-done.7 = f32[192,128]{1,0:T(8,128)S(1)} collective-permute-done((f32[192,128]{1,0:T(8,128)}, f32[192,128]{1,0:T(8,128)S(1)}, u32[]{:S(2)}, u32[]{:S(2)}) %collective-permute-start.7) | collective-permute-done | bytes 98336 | tf_op jit(solution)/shard_map/ppermute | solution.py:313
  84.7 3.6 %collective-permute-done.8 = f32[192,128]{1,0:T(8,128)S(1)} collective-permute-done((f32[192,128]{1,0:T(8,128)S(1)}, f32[192,128]{1,0:T(8,128)S(1)}, u32[]{:S(2)}, u32[]{:S(2)}) %collective-permute-start.8) | collective-permute-done | bytes 98336 | tf_op jit(solution)/shard_map/ppermute | solution.py:313
  88.4 2.6 %collective-permute-start.10 = (bf16[256,1024]{1,0:T(8,128)(2,1)}, bf16[256,1024]{1,0:T(8,128)(2,1)}, u32[]{:S(2)}, u32[]{:S(2)}) collective-permute-start(bf16[256,1024]{1,0:T(8,128)(2,1)} %collective-permute-done.5.refs_0_), channel_id=1, source_target_pairs={{0,1},{1,2},{2,3},{3,0},{4,5},{5,6},{6,7},{7,4},{8,9},{9,10},{10,1... | collective-permute-start | bytes 1572872 | tf_op jit(solution)/shard_map/ppermute | solution.py:313
  91.1 1.9 %collective-permute-start.12 = (bf16[192,128]{1,0:T(8,128)(2,1)S(1)}, bf16[192,128]{1,0:T(8,128)(2,1)S(1)}, u32[]{:S(2)}, u32[]{:S(2)}) collective-permute-start(bf16[192,128]{1,0:T(8,128)(2,1)S(1)} %add_convert_fusion.refs_0_), channel_id=1, source_target_pairs={{0,2},{1,3},{2,0},{3,1},{4,6},{5,7},{6,4},{7,5},{8,10},{9,11},{10,... | collective-permute-start | bytes 147464 | tf_op jit(solution)/shard_map/ppermute | solution.py:313
  92.9 2.0 %collective-permute-start.13 = (bf16[192,128]{1,0:T(8,128)(2,1)S(1)}, bf16[192,128]{1,0:T(8,128)(2,1)S(1)}, u32[]{:S(2)}, u32[]{:S(2)}) collective-permute-start(bf16[192,128]{1,0:T(8,128)(2,1)S(1)} %add_convert_fusion.refs_0_), channel_id=1, source_target_pairs={{0,3},{1,0},{2,1},{3,2},{4,7},{5,4},{6,5},{7,6},{8,11},{9,8},{10,9... | collective-permute-start | bytes 147464 | tf_op jit(solution)/shard_map/ppermute | solution.py:313
  94.9 2.2 %project.5.refs_6_ = f32[512,768]{1,0:T(8,128)S(1)} custom-call(s32[1]{0:T(128)} %constant.140.clone.1.ids_ref, bf16[256,1024]{1,0:T(8,128)(2,1)} %collective-permute-done.5.refs_0_, bf16[256,1024]{1,0:T(8,128)(2,1)} %collective-permute-done.6.refs_1_, bf16[6,1024,128]{2,1,0:T(8,128)(2,1)S(1)} %copy-done.7, f32[512,768]{1,0:T(8,128)S(1)} %project.4.refs_3_), custom_call_target="tpu_custom_call" | custom-call | bytes 12582912 | tf_op jit(solution)/shard_map/project/pallas_call | solution.py:26
  98.3 4.4 %slice_bitcast_fusion = (bf16[8,96,1024]{2,1,0:T(8,128)(2,1)}, bf16[8,96,1024]{2,1,0:T(8,128)(2,1)S(1)}, bf16[8,96,1024]{2,1,0:T(8,128)(2,1)S(1)}) fusion(bf16[8,3,96,1024]{3,2,1,0:T(8,128)(2,1)} %bitcast.65), kind=kLoop, calls=%fused_computation | loop fusion | bytes 9437184 | tf_op jit(solution)/shard_map/squeeze | solution.py:389
  102.7 3.7 %collective-permute-done.11.refs_1_ = bf16[192,128]{1,0:T(8,128)(2,1)S(1)} collective-permute-done((bf16[192,128]{1,0:T(8,128)(2,1)S(1)}, bf16[192,128]{1,0:T(8,128)(2,1)S(1)}, u32[]{:S(2)}, u32[]{:S(2)}) %collective-permute-start.11) | collective-permute-done | bytes 49184 | tf_op jit(solution)/shard_map/ppermute | solution.py:313
  110.5 6.1 %attend.2 = (bf16[256,512]{1,0:T(8,128)(2,1)}, bf16[256,128]{1,0:T(8,128)(2,1)}, bf16[256,128]{1,0:T(8,128)(2,1)}) custom-call(s32[8]{0:T(128)} %pad_add_fusion.2.ids_ref, s32[512,2]{1,0:T(8,128)} %copy.47.table_ref.refs_2_, f32[512,256]{1,0:T(8,128)} %pad_maximum_fusion.1.turn_ref, bf16[4,6,64,128]{3,2,1,0:T(8,128)(2,1)} %bitcast.61, ...), custom_call_target="tpu_custom_call" | custom-call | bytes 14364672 | tf_op jit(solution)/shard_map/attend/pallas_call | solution.py:26
  120.4 8.7 %collective-permute-done.15.attended_ref = bf16[256,512]{1,0:T(8,128)(2,1)S(1)} collective-permute-done((bf16[256,512]{1,0:T(8,128)(2,1)}, bf16[256,512]{1,0:T(8,128)(2,1)S(1)}, u32[]{:S(2)}, u32[]{:S(2)}) %collective-permute-start.15) | collective-permute-done | bytes 262176 | tf_op jit(solution)/shard_map/ppermute | solution.py:313
  135.7 4.8 %attend.3 = (bf16[256,512]{1,0:T(8,128)(2,1)S(1)}, bf16[256,128]{1,0:T(8,128)(2,1)}, bf16[256,128]{1,0:T(8,128)(2,1)}) custom-call(s32[8]{0:T(128)S(1)} %copy-done.26, s32[512,2]{1,0:T(8,128)S(1)} %copy-done.6, f32[512,256]{1,0:T(8,128)S(1)} %copy-done.10, bf16[4,6,64,128]{3,2,1,0:T(8,128)(2,1)S(1)} %bitcast.62, bf16[192,128]{1,0:T(8,128)(2,1)S(1)} %copy-done.16, ...), custom_call_target="tpu_custom_call" | custom-call | bytes 14757888 | tf_op jit(solution)/shard_map/attend/pallas_call | solution.py:26
  143.6 8.0 %collective-permute-done.16.attended_ref = bf16[256,512]{1,0:T(8,128)(2,1)S(1)} collective-permute-done((bf16[256,512]{1,0:T(8,128)(2,1)S(1)}, bf16[256,512]{1,0:T(8,128)(2,1)S(1)}, u32[]{:S(2)}, u32[]{:S(2)}) %collective-permute-start.16) | collective-permute-done | bytes 262176 | tf_op jit(solution)/shard_map/ppermute | solution.py:313
  152.7 4.5 %collective-permute-done.19.attended_ref = bf16[256,512]{1,0:T(8,128)(2,1)S(1)} collective-permute-done((bf16[256,512]{1,0:T(8,128)(2,1)S(1)}, bf16[256,512]{1,0:T(8,128)(2,1)S(1)}, u32[]{:S(2)}, u32[]{:S(2)}) %collective-permute-start.19) | collective-permute-done | bytes 262176 | tf_op jit(solution)/shard_map/ppermute | solution.py:313
  157.2 3.7 %collective-permute-done.18.attended_ref = bf16[256,512]{1,0:T(8,128)(2,1)S(1)} collective-permute-done((bf16[256,512]{1,0:T(8,128)(2,1)S(1)}, bf16[256,512]{1,0:T(8,128)(2,1)S(1)}, u32[]{:S(2)}, u32[]{:S(2)}) %collective-permute-start.18) | collective-permute-done | bytes 262176 | tf_op jit(solution)/shard_map/ppermute | solution.py:313
  164.8 4.3 %collective-permute-done.20.attended_ref = bf16[256,512]{1,0:T(8,128)(2,1)S(1)} collective-permute-done((bf16[256,512]{1,0:T(8,128)(2,1)S(1)}, bf16[256,512]{1,0:T(8,128)(2,1)S(1)}, u32[]{:S(2)}, u32[]{:S(2)}) %collective-permute-start.20) | collective-permute-done | bytes 262176 | tf_op jit(solution)/shard_map/ppermute | solution.py:313
  169.1 2.3 %project_out.15 = bf16[512,1024]{1,0:T(8,128)(2,1)} custom-call(s32[5]{0:T(128)S(1)} %pad_add_fusion.1.ids_ref, bf16[256,512]{1,0:T(8,128)(2,1)S(1)} %collective-permute-done.20.attended_ref, bf16[8,96,1024]{2,1,0:T(8,128)(2,1)S(1)} %copy-done, bf16[8,96,1024]{2,1,0:T(8,128)(2,1)S(1)} %copy-done, f32[256,1024]{1,0:T(8,128)S(1)} %get-tuple-element.126.refs_0_, ...), custom_call_target="tpu_custom_call" | custom-call | bytes 17313792 | tf_op jit(solution)/shard_map/project_out/pallas_call | solution.py:26
  (144 shorter events, 38.4 us)
Async XLA Ops:
  6.5 38.4 %all-gather.6.cloned.1.call-start = ((), (), s32[]{:S(2)}) async-start(), calls=%async_computation | async-start | bytes 1966080 | tf_op jit(solution)/shard_map/all_gather | solution.py:316
  8.8 43.4 %collective-permute-start = (bf16[256,1024]{1,0:T(8,128)(2,1)}, bf16[256,1024]{1,0:T(8,128)(2,1)}, u32[]{:S(2)}, u32[]{:S(2)}) collective-permute-start(bf16[256,1024]{1,0:T(8,128)(2,1)} %get-tuple-element.142.refs_0_), channel_id=1, source_target_pairs={{0,1},{1,2},{2,3},{3,0},{4,5},{5,6},{6,7},{7,4},{8,9},{9,10},{10,1... | collective-permute-start | bytes 1572872 | tf_op jit(solution)/shard_map/ppermute | solution.py:313
  11.9 40.4 %collective-permute-start.1 = (bf16[256,1024]{1,0:T(8,128)(2,1)}, bf16[256,1024]{1,0:T(8,128)(2,1)}, u32[]{:S(2)}, u32[]{:S(2)}) collective-permute-start(bf16[256,1024]{1,0:T(8,128)(2,1)} %get-tuple-element.141.refs_1_), channel_id=1, source_target_pairs={{0,1},{1,2},{2,3},{3,0},{4,5},{5,6},{6,7},{7,4},{8,9},{9,10},{10,1... | collective-permute-start | bytes 1572872 | tf_op jit(solution)/shard_map/ppermute | solution.py:313
  13.5 84.9 %all-gather.8.cloned.1.call-start = ((), (), s32[]{:S(2)}) async-start(), calls=%async_computation.1 | async-start | bytes 5308416 | tf_op jit(solution)/shard_map/all_gather | solution.py:380
  16.6 9.6 %copy-start.32 = (bf16[32,1024]{1,0:T(8,128)(2,1)}, bf16[32,1024]{1,0:T(8,128)(2,1)S(1)}, u32[]{:S(2)}) copy-start(bf16[32,1024]{1,0:T(8,128)(2,1)S(1)} %bitcast_dynamic-update-slice_fusion) | copy-start | bytes 196612
  17.6 34.7 %collective-permute-start.2 = (bf16[96,1024]{1,0:T(8,128)(2,1)}, bf16[96,1024]{1,0:T(8,128)(2,1)}, u32[]{:S(2)}, u32[]{:S(2)}) collective-permute-start(bf16[96,1024]{1,0:T(8,128)(2,1)} %get-tuple-element.145), channel_id=1, source_target_pairs={{0,1},{1,2},{2,3},{3,0},{4,5},{5,6},{6,7},{7,4},{8,9},{9,10},{10,1... | collective-permute-start | bytes 589832 | tf_op jit(solution)/shard_map/ppermute | solution.py:313
  19.1 33.1 %collective-permute-start.3 = (bf16[96,1024]{1,0:T(8,128)(2,1)}, bf16[96,1024]{1,0:T(8,128)(2,1)}, u32[]{:S(2)}, u32[]{:S(2)}) collective-permute-start(bf16[96,1024]{1,0:T(8,128)(2,1)} %get-tuple-element.144), channel_id=1, source_target_pairs={{0,2},{1,3},{2,0},{3,1},{4,6},{5,7},{6,4},{7,5},{8,10},{9,11},{10,... | collective-permute-start | bytes 589832 | tf_op jit(solution)/shard_map/ppermute | solution.py:313
  20.4 31.8 %collective-permute-start.4 = (bf16[96,1024]{1,0:T(8,128)(2,1)}, bf16[96,1024]{1,0:T(8,128)(2,1)}, u32[]{:S(2)}, u32[]{:S(2)}) collective-permute-start(bf16[96,1024]{1,0:T(8,128)(2,1)} %get-tuple-element.143), channel_id=1, source_target_pairs={{0,3},{1,0},{2,1},{3,2},{4,7},{5,4},{6,5},{7,6},{8,11},{9,8},{10,9... | collective-permute-start | bytes 589832 | tf_op jit(solution)/shard_map/ppermute | solution.py:313
  54.4 9.8 %copy-start.34 = (bf16[1,64,1024]{2,1,0:T(8,128)(2,1)S(1)}, bf16[1,64,1024]{2,1,0:T(8,128)(2,1)}, u32[]{:S(2)}) copy-start(bf16[1,64,1024]{2,1,0:T(8,128)(2,1)} %param.15) | copy-start | bytes 393220
  54.4 20.5 %copy-start.33 = (bf16[32,1024]{1,0:T(8,128)(2,1)S(1)}, bf16[32,1024]{1,0:T(8,128)(2,1)}, u32[]{:S(2)}) copy-start(bf16[32,1024]{1,0:T(8,128)(2,1)} %copy-done.32) | copy-start | bytes 196612
  54.4 33.9 %collective-permute-start.5 = (bf16[256,1024]{1,0:T(8,128)(2,1)}, bf16[256,1024]{1,0:T(8,128)(2,1)}, u32[]{:S(2)}, u32[]{:S(2)}) collective-permute-start(bf16[256,1024]{1,0:T(8,128)(2,1)} %collective-permute-done.refs_0_), channel_id=1, source_target_pairs={{0,1},{1,2},{2,3},{3,0},{4,5},{5,6},{6,7},{7,4},{8,9},{9,10},{10,1... | collective-permute-start | bytes 1572872 | tf_op jit(solution)/shard_map/ppermute | solution.py:313
  56.9 31.5 %collective-permute-start.6 = (bf16[256,1024]{1,0:T(8,128)(2,1)}, bf16[256,1024]{1,0:T(8,128)(2,1)}, u32[]{:S(2)}, u32[]{:S(2)}) collective-permute-start(bf16[256,1024]{1,0:T(8,128)(2,1)} %collective-permute-done.1.refs_1_), channel_id=1, source_target_pairs={{0,1},{1,2},{2,3},{3,0},{4,5},{5,6},{6,7},{7,4},{8,9},{9,10},{10,1... | collective-permute-start | bytes 1572872 | tf_op jit(solution)/shard_map/ppermute | solution.py:313
  57.0 27.7 %collective-permute-start.7 = (f32[192,128]{1,0:T(8,128)}, f32[192,128]{1,0:T(8,128)S(1)}, u32[]{:S(2)}, u32[]{:S(2)}) collective-permute-start(f32[192,128]{1,0:T(8,128)} %copy-done.31), channel_id=1, source_target_pairs={{0,1},{1,2},{2,3},{3,0},{4,5},{5,6},{6,7},{7,4},{8,9},{9,10},{10,1... | collective-permute-start | bytes 294920 | tf_op jit(solution)/shard_map/ppermute | solution.py:313
  59.1 29.3 %collective-permute-start.8 = (f32[192,128]{1,0:T(8,128)S(1)}, f32[192,128]{1,0:T(8,128)S(1)}, u32[]{:S(2)}, u32[]{:S(2)}) collective-permute-start(f32[192,128]{1,0:T(8,128)S(1)} %copy-done.30), channel_id=1, source_target_pairs={{0,2},{1,3},{2,0},{3,1},{4,6},{5,7},{6,4},{7,5},{8,10},{9,11},{10,... | collective-permute-start | bytes 294920 | tf_op jit(solution)/shard_map/ppermute | solution.py:313
  61.3 27.1 %collective-permute-start.9 = (f32[192,128]{1,0:T(8,128)S(1)}, f32[192,128]{1,0:T(8,128)S(1)}, u32[]{:S(2)}, u32[]{:S(2)}) collective-permute-start(f32[192,128]{1,0:T(8,128)S(1)} %copy-done.28), channel_id=1, source_target_pairs={{0,3},{1,0},{2,1},{3,2},{4,7},{5,4},{6,5},{7,6},{8,11},{9,8},{10,9... | collective-permute-start | bytes 294920 | tf_op jit(solution)/shard_map/ppermute | solution.py:313
  61.8 33.1 %copy-start.7 = (bf16[6,1024,128]{2,1,0:T(8,128)(2,1)S(1)}, bf16[6,1024,128]{2,1,0:T(8,128)(2,1)}, u32[]{:S(2)}) copy-start(bf16[6,1024,128]{2,1,0:T(8,128)(2,1)} %get-tuple-element.87.refs_2_) | copy-start | bytes 4718596
  88.4 19.1 %collective-permute-start.10 = (bf16[256,1024]{1,0:T(8,128)(2,1)}, bf16[256,1024]{1,0:T(8,128)(2,1)}, u32[]{:S(2)}, u32[]{:S(2)}) collective-permute-start(bf16[256,1024]{1,0:T(8,128)(2,1)} %collective-permute-done.5.refs_0_), channel_id=1, source_target_pairs={{0,1},{1,2},{2,3},{3,0},{4,5},{5,6},{6,7},{7,4},{8,9},{9,10},{10,1... | collective-permute-start | bytes 1572872 | tf_op jit(solution)/shard_map/ppermute | solution.py:313
  91.0 15.4 %collective-permute-start.11 = (bf16[192,128]{1,0:T(8,128)(2,1)S(1)}, bf16[192,128]{1,0:T(8,128)(2,1)S(1)}, u32[]{:S(2)}, u32[]{:S(2)}) collective-permute-start(bf16[192,128]{1,0:T(8,128)(2,1)S(1)} %add_convert_fusion.refs_0_), channel_id=1, source_target_pairs={{0,1},{1,2},{2,3},{3,0},{4,5},{5,6},{6,7},{7,4},{8,9},{9,10},{10,1... | collective-permute-start | bytes 147464 | tf_op jit(solution)/shard_map/ppermute | solution.py:313
  91.1 16.4 %collective-permute-start.12 = (bf16[192,128]{1,0:T(8,128)(2,1)S(1)}, bf16[192,128]{1,0:T(8,128)(2,1)S(1)}, u32[]{:S(2)}, u32[]{:S(2)}) collective-permute-start(bf16[192,128]{1,0:T(8,128)(2,1)S(1)} %add_convert_fusion.refs_0_), channel_id=1, source_target_pairs={{0,2},{1,3},{2,0},{3,1},{4,6},{5,7},{6,4},{7,5},{8,10},{9,11},{10,... | collective-permute-start | bytes 147464 | tf_op jit(solution)/shard_map/ppermute | solution.py:313
  92.9 14.6 %collective-permute-start.13 = (bf16[192,128]{1,0:T(8,128)(2,1)S(1)}, bf16[192,128]{1,0:T(8,128)(2,1)S(1)}, u32[]{:S(2)}, u32[]{:S(2)}) collective-permute-start(bf16[192,128]{1,0:T(8,128)(2,1)S(1)} %add_convert_fusion.refs_0_), channel_id=1, source_target_pairs={{0,3},{1,0},{2,1},{3,2},{4,7},{5,4},{6,5},{7,6},{8,11},{9,8},{10,9... | collective-permute-start | bytes 147464 | tf_op jit(solution)/shard_map/ppermute | solution.py:313
  107.5 21.6 %collective-permute-start.14 = (bf16[256,1024]{1,0:T(8,128)(2,1)}, bf16[256,1024]{1,0:T(8,128)(2,1)}, u32[]{:S(2)}, u32[]{:S(2)}) collective-permute-start(bf16[256,1024]{1,0:T(8,128)(2,1)} %collective-permute-done.6.refs_1_), channel_id=1, source_target_pairs={{0,1},{1,2},{2,3},{3,0},{4,5},{5,6},{6,7},{7,4},{8,9},{9,10},{10,1... | collective-permute-start | bytes 1572872 | tf_op jit(solution)/shard_map/ppermute | solution.py:313
  110.5 18.6 %copy-start.6 = (s32[512,2]{1,0:T(8,128)S(1)}, s32[512,2]{1,0:T(8,128)}, u32[]{:S(2)}) copy-start(s32[512,2]{1,0:T(8,128)} %copy.47.table_ref.refs_2_) | copy-start | bytes 12292
  110.5 18.6 %copy-start.12 = (bf16[24,64,128]{2,1,0:T(8,128)(2,1)S(1)}, bf16[24,64,128]{2,1,0:T(8,128)(2,1)}, u32[]{:S(2)}) copy-start(bf16[24,64,128]{2,1,0:T(8,128)(2,1)} %all-gather) | copy-start | bytes 1179652
  110.5 18.6 %copy-start.16 = (bf16[192,128]{1,0:T(8,128)(2,1)S(1)}, bf16[192,128]{1,0:T(8,128)(2,1)}, u32[]{:S(2)}) copy-start(bf16[192,128]{1,0:T(8,128)(2,1)} %copy-done.15) | copy-start | bytes 147460
  110.5 18.6 %copy-start.26 = (s32[8]{0:T(128)S(1)}, s32[8]{0:T(128)}, u32[]{:S(2)}) copy-start(s32[8]{0:T(128)} %pad_add_fusion.2.ids_ref) | copy-start | bytes 100
  116.7 12.5 %copy-start.2 = (f32[512,768]{1,0:T(8,128)S(1)}, f32[512,768]{1,0:T(8,128)}, u32[]{:S(2)}) copy-start(f32[512,768]{1,0:T(8,128)} %copy-done.1) | copy-start | bytes 4718596
  116.7 12.4 %collective-permute-start.15 = (bf16[256,512]{1,0:T(8,128)(2,1)}, bf16[256,512]{1,0:T(8,128)(2,1)S(1)}, u32[]{:S(2)}, u32[]{:S(2)}) collective-permute-start(bf16[256,512]{1,0:T(8,128)(2,1)} %get-tuple-element.107.attended_ref), channel_id=1, source_target_pairs={{0,1},{1,2},{2,3},{3,0},{4,5},{5,6},{6,7},{7,4},{8,9},{9,10},{10,1... | collective-permute-start | bytes 786440 | tf_op jit(solution)/shard_map/ppermute | solution.py:313
  129.1 13.7 %collective-permute-start.17 = (bf16[256,512]{1,0:T(8,128)(2,1)S(1)}, bf16[256,512]{1,0:T(8,128)(2,1)S(1)}, u32[]{:S(2)}, u32[]{:S(2)}) collective-permute-start(bf16[256,512]{1,0:T(8,128)(2,1)S(1)} %collective-permute-done.15.attended_ref), channel_id=1, source_target_pairs={{0,1},{1,2},{2,3},{3,0},{4,5},{5,6},{6,7},{7,4},{8,9},{9,10},{10,1... | collective-permute-start | bytes 786440 | tf_op jit(solution)/shard_map/ppermute | solution.py:313
  140.5 11.1 %collective-permute-start.16 = (bf16[256,512]{1,0:T(8,128)(2,1)S(1)}, bf16[256,512]{1,0:T(8,128)(2,1)S(1)}, u32[]{:S(2)}, u32[]{:S(2)}) collective-permute-start(bf16[256,512]{1,0:T(8,128)(2,1)S(1)} %get-tuple-element.108.attended_ref), channel_id=1, source_target_pairs={{0,1},{1,2},{2,3},{3,0},{4,5},{5,6},{6,7},{7,4},{8,9},{9,10},{10,1... | collective-permute-start | bytes 786440 | tf_op jit(solution)/shard_map/ppermute | solution.py:313
  142.8 14.4 %collective-permute-start.19 = (bf16[256,512]{1,0:T(8,128)(2,1)S(1)}, bf16[256,512]{1,0:T(8,128)(2,1)S(1)}, u32[]{:S(2)}, u32[]{:S(2)}) collective-permute-start(bf16[256,512]{1,0:T(8,128)(2,1)S(1)} %collective-permute-done.17.attended_ref), channel_id=1, source_target_pairs={{0,1},{1,2},{2,3},{3,0},{4,5},{5,6},{6,7},{7,4},{8,9},{9,10},{10,1... | collective-permute-start | bytes 786440 | tf_op jit(solution)/shard_map/ppermute | solution.py:313
  151.6 9.3 %collective-permute-start.18 = (bf16[256,512]{1,0:T(8,128)(2,1)S(1)}, bf16[256,512]{1,0:T(8,128)(2,1)S(1)}, u32[]{:S(2)}, u32[]{:S(2)}) collective-permute-start(bf16[256,512]{1,0:T(8,128)(2,1)S(1)} %collective-permute-done.16.attended_ref), channel_id=1, source_target_pairs={{0,1},{1,2},{2,3},{3,0},{4,5},{5,6},{6,7},{7,4},{8,9},{9,10},{10,1... | collective-permute-start | bytes 786440 | tf_op jit(solution)/shard_map/ppermute | solution.py:313
  160.9 8.2 %collective-permute-start.20 = (bf16[256,512]{1,0:T(8,128)(2,1)S(1)}, bf16[256,512]{1,0:T(8,128)(2,1)S(1)}, u32[]{:S(2)}, u32[]{:S(2)}) collective-permute-start(bf16[256,512]{1,0:T(8,128)(2,1)S(1)} %collective-permute-done.18.attended_ref), channel_id=1, source_target_pairs={{0,1},{1,2},{2,3},{3,0},{4,5},{5,6},{6,7},{7,4},{8,9},{9,10},{10,1... | collective-permute-start | bytes 786440 | tf_op jit(solution)/shard_map/ppermute | solution.py:313
  (30 other events, 90.6 us)
Sparse Core Ops, SparseCore 0:
  13.6 19.5 all-gather.5
  54.5 42.5 all-gather.7
